TPU v7x, 32 devices: a whole 2x2x4 slice. The times are simulated.
32 devices in a mesh: expert: 16 (over z, y, core), etp: 2 (over x).
Axes of the slice: x: 2, y: 2, z: 4, core: 2. Of those that a mesh axis runs over, the one named last changes fastest.
Arguments:
- tokens: bfloat16 [2048, 2048], P('expert', 'etp'), may hold values from -6 to 6
- out_grad: bfloat16 [2048, 2048], P('expert', 'etp'), may hold values from -12 to 12
- routes: int32 [2048, 8], P('expert'), may hold values from 0 to 15, all different within a row; in each aligned block of 128 rows (0 to 127, 128 to 255, ...) at most 72 rows name the same one
- combine: float32 [2048, 8], P('expert'), may hold values from 0.02 to 0.5
- w_gate: bfloat16 [16, 768, 2048], P('expert', 'etp'), may hold values from -0.125 to 0.125
- w_up: bfloat16 [16, 768, 2048], P('expert', 'etp'), may hold values from -0.125 to 0.125
- w_down: bfloat16 [16, 768, 2048], P('expert', 'etp'), may hold values from -0.21875 to 0.21875
Outputs:
- grad_tokens: bfloat16 [2048, 2048], P('expert', 'etp')
- grad_gate: bfloat16 [16, 768, 2048], P('expert', 'etp')
- grad_up: bfloat16 [16, 768, 2048], P('expert', 'etp')
- grad_down: bfloat16 [16, 768, 2048], P('expert', 'etp')
Inputs may be any that keep to these rules, and one draw needn't show every extreme that they name: `routes`: each row names 8 different experts. Within each aligned block of 128 rows (the rows of one index of expert) no expert is named by more than 72 rows, and in some block one expert is named by exactly 72 rows.
All inputs are finite; a program needn't handle non-finite values.
Results may differ from a plain program's by a relative error of at most 0.0064.
Values may be sent and summed in bfloat16 or wider, within the bound.
No kernel may reach another device: no remote copies, remote signals or barrier semaphores. Data moves between devices by JAX's collectives and lax.ppermute only.
A program may use at most 128 MiB of HBM per device.

v0:
```python
import jax
import jax.numpy as jnp
from jax import lax
from jax.sharding import PartitionSpec as P


def pack_rows(token_rows, grad_rows, token_of, scale, is_live):
    mask = is_live[:, None].astype(token_rows.dtype)
    inputs_sent = token_rows[token_of] * mask
    grads_sent = (scale[:, None] * grad_rows[token_of].astype(jnp.float32)).astype(jnp.bfloat16)
    return (inputs_sent, grads_sent)


def pair_positions(routed_flat, experts):
    pair_total = routed_flat.shape[0]
    span = 128
    groups = pair_total // span
    labels = jnp.arange(experts, dtype=jnp.int32)
    one_hot = (routed_flat[:, None] == labels[None, :]).astype(jnp.bfloat16)
    grouped = one_hot.reshape(groups, span, experts)
    row_ids = jnp.arange(span, dtype=jnp.int32)
    lower = (row_ids[None, :] < row_ids[:, None]).astype(jnp.bfloat16)
    within = jnp.einsum("ij,bje->bie", lower, grouped, preferred_element_type=jnp.float32)
    group_sums = jnp.sum(grouped.astype(jnp.float32), axis=1)
    group_before = jnp.cumsum(group_sums, axis=0) - group_sums
    earlier = within + group_before[:, None, :]
    counted = jnp.sum(earlier * grouped.astype(jnp.float32), axis=2)
    return counted.reshape(pair_total).astype(jnp.int32)


def body(tokens, out_grad, routes, combine, w_gate, w_up, w_down):
    experts = lax.axis_size("expert")
    tok_rows = tokens.shape[0]
    col_width = tokens.shape[1]
    choose_count = routes.shape[1]
    per_pair = tok_rows * choose_count // experts
    capacity = per_pair + per_pair // 8
    routed_flat = routes.reshape(-1)
    pair_total = routed_flat.shape[0]
    position = pair_positions(routed_flat, experts)
    target = routed_flat * capacity + position
    anchor = jnp.full((experts * capacity,), pair_total, jnp.int32)
    anchor = anchor.at[target].set(jnp.arange(pair_total, dtype=jnp.int32))
    is_live = anchor < pair_total
    safe_anchor = jnp.minimum(anchor, pair_total - 1)
    token_of = safe_anchor // choose_count
    scale = combine.reshape(-1)[safe_anchor] * is_live.astype(jnp.float32)
    full_tokens, full_grads = (
        lax.all_gather(tokens, "etp", axis=1, tiled=True),
        lax.all_gather(out_grad, "etp", axis=1, tiled=True),
    )
    inputs_sent, grads_sent = pack_rows(full_tokens, full_grads, token_of, scale, is_live)
    rows_x, rows_g = (
        lax.all_to_all(inputs_sent, "expert", split_axis=0, concat_axis=0, tiled=True),
        lax.all_to_all(grads_sent, "expert", split_axis=0, concat_axis=0, tiled=True),
    )
    gate_w = w_gate[0]
    up_w = w_up[0]
    down_w = w_down[0]
    contract_last = (((1,), (1,)), ((), ()))
    contract_first = (((0,), (0,)), ((), ()))
    gate = lax.dot_general(rows_x, gate_w, contract_last, preferred_element_type=jnp.float32)
    up = lax.dot_general(rows_x, up_w, contract_last, preferred_element_type=jnp.float32)
    hidden_grad = lax.dot_general(rows_g, down_w, contract_last, preferred_element_type=jnp.float32)
    sigma = jax.nn.sigmoid(gate)
    silu = gate * sigma
    acts = (silu * up).astype(jnp.bfloat16)
    grad_down = lax.dot_general(acts, rows_g, contract_first, preferred_element_type=jnp.float32)
    gate_term = (hidden_grad * up * sigma * (1.0 + gate * (1.0 - sigma))).astype(jnp.bfloat16)
    up_term = (hidden_grad * silu).astype(jnp.bfloat16)
    grad_gate = lax.dot_general(
        gate_term, rows_x, contract_first, preferred_element_type=jnp.float32
    )
    grad_up = lax.dot_general(up_term, rows_x, contract_first, preferred_element_type=jnp.float32)
    swapped_gate, swapped_up = (
        lax.all_to_all(gate_w, "etp", split_axis=1, concat_axis=0, tiled=True),
        lax.all_to_all(up_w, "etp", split_axis=1, concat_axis=0, tiled=True),
    )
    running = jnp.dot(
        lax.all_gather(gate_term, "etp", axis=1, tiled=True),
        swapped_gate,
        preferred_element_type=jnp.float32,
    )
    slot_grads = running + jnp.dot(
        lax.all_gather(up_term, "etp", axis=1, tiled=True),
        swapped_up,
        preferred_element_type=jnp.float32,
    )
    slot_grads = slot_grads.astype(jnp.bfloat16)
    returned = lax.all_to_all(slot_grads, "expert", split_axis=0, concat_axis=0, tiled=True)
    picked = returned[target].astype(jnp.float32).reshape(tok_rows, choose_count, col_width)
    grad_tokens = jnp.sum(picked, axis=1).astype(jnp.bfloat16)
    return (
        grad_tokens,
        grad_gate.astype(jnp.bfloat16)[None],
        grad_up.astype(jnp.bfloat16)[None],
        grad_down.astype(jnp.bfloat16)[None],
    )


def solution(mesh):
    placed = (
        P("expert", "etp"),
        P("expert", "etp"),
        P("expert", None),
        P("expert", None),
        P("expert", "etp", None),
        P("expert", "etp", None),
        P("expert", "etp", None),
    )
    return jax.shard_map(
        body,
        mesh=mesh,
        in_specs=placed,
        out_specs=(
            P("expert", "etp"),
            P("expert", "etp", None),
            P("expert", "etp", None),
            P("expert", "etp", None),
        ),
        check_vma=False,
    )
```

profile of v0, /device:TPU:0, one launch (start us, length us, event | category | flops | bytes accessed | tf_op | source)
XLA Modules:
  0.0 423.3 jit_solution(16665255436099908871)
XLA Ops:
  7.2 0.8 broadcast_multiply_fusion.1
  8.0 0.8 copy.15
  8.8 0.1 copy.14
  8.9 0.1 mul.69
  9.0 0.8 copy.16
  9.8 0.1 reshape.109
  9.9 0.1 eq.17
  9.9 0.1 convert_reduce_fusion
  10.1 0.2 fusion.13
  10.3 4.3 %scatter_custom_fusion = s32[1152]{0:T(1024)S(1)} fusion(s32[1024]{0:T(1024)S(1)} %bitcast.63, s32[1024]{0:T(1024)S(1)} %iota.21, s32[]{:T(128)} %constant.13.clone.1), kind=kCustom, calls=%fused_computation.51 | custom fusion | bytes 4612 | tf_op jit(solution)/shard_map/scatter | solution.py:43
  14.7 4.6 %gather_fusion = f32[1152]{0:T(1024)S(1)} fusion(f32[1024]{0:T(1024)S(1)} %reshape.109, s32[2048]{0:T(1024)S(1)} %pad_clamp_fusion.1), kind=kCustom, calls=%fused_computation | custom fusion | bytes 13824 | tf_op jit(solution)/shard_map/gather | solution.py:47
  19.3 0.1 reshape.111
  19.4 9.9 %all_gather.13 = bf16[128,2048]{1,0:T(8,128)(2,1)S(1)} all-gather(bf16[128,1024]{1,0:T(8,128)(2,1)S(1)} %copy-done.9), channel_id=1, replica_groups=mesh['expert'=16,'etp'=2] {'etp'}, dimensions={1}, use_global_device_ids=true | all-gather | bytes 786432 | tf_op jit(solution)/shard_map/all_gather | solution.py:49
  29.3 5.9 %gather_fusion.2 = bf16[1152,2048]{1,0:T(8,128)(2,1)} fusion(bf16[128,2048]{1,0:T(8,128)(2,1)S(1)} %all_gather.13, s32[2048]{0:T(1024)S(1)} %pad_clamp_fusion), kind=kCustom, calls=%fused_computation.2 | custom fusion | bytes 9441792 | tf_op jit(solution)/shard_map/gather | solution.py:9
  35.2 4.9 %broadcast_multiply_fusion = bf16[16,72,2048]{2,1,0:T(8,128)(2,1)} fusion(bf16[16,72,2048]{2,1,0:T(8,128)(2,1)} %bitcast.56, bf16[16,72]{1,0:T(8,128)(2,1)S(1)} %reshape.111), kind=kLoop, calls=%fused_computation.14 | loop fusion | flops 2359296 | bytes 9439488 | tf_op jit(solution)/shard_map/mul | solution.py:9
  40.1 6.4 %all-to-all-start.1 = ((bf16[16,72,2048]{2,1,0:T(8,128)(2,1)}), bf16[16,72,2048]{2,1,0:T(8,128)(2,1)}, u32[]{:S(2)}, u32[]{:S(2)}) async-start(bf16[16,72,2048]{2,1,0:T(8,128)(2,1)} %broadcast_multiply_fusion), calls=%async_computation.1 | async-start | bytes 9437184 | tf_op jit(solution)/shard_map/all_to_all | solution.py:54
  46.5 0.1 mul.72
  46.6 9.3 %all_gather.12 = bf16[128,2048]{1,0:T(8,128)(2,1)S(1)} all-gather(bf16[128,1024]{1,0:T(8,128)(2,1)S(1)} %copy-done.10), channel_id=1, replica_groups=mesh['expert'=16,'etp'=2] {'etp'}, dimensions={1}, use_global_device_ids=true | all-gather | bytes 786432 | tf_op jit(solution)/shard_map/all_gather | solution.py:50
  55.8 5.9 %gather_fusion.1 = bf16[1152,2048]{1,0:T(8,128)(2,1)} fusion(bf16[128,2048]{1,0:T(8,128)(2,1)S(1)} %all_gather.12, s32[2048]{0:T(1024)S(1)} %pad_clamp_fusion), kind=kCustom, calls=%fused_computation.1 | custom fusion | bytes 9441792 | tf_op jit(solution)/shard_map/gather | solution.py:10
  61.7 5.4 %fusion = bf16[16,72,2048]{2,1,0:T(8,128)(2,1)} fusion(bf16[16,72,2048]{2,1,0:T(8,128)(2,1)} %bitcast.57, f32[16,72]{1,0:T(8,128)S(1)} %mul.72), kind=kLoop, calls=%fused_computation.6 | loop fusion | flops 7077888 | bytes 9441792 | tf_op jit(solution)/shard_map/convert_element_type | solution.py:10
  67.2 66.1 %all-to-all-done.1 = bf16[16,72,2048]{2,1,0:T(8,128)(2,1)} async-done(((bf16[16,72,2048]{2,1,0:T(8,128)(2,1)}), bf16[16,72,2048]{2,1,0:T(8,128)(2,1)}, u32[]{:S(2)}, u32[]{:S(2)}) %all-to-all-start.1) | async-done | bytes 4718624 | tf_op jit(solution)/shard_map/all_to_all | solution.py:54
  133.3 21.8 %all-to-all-start = ((bf16[16,72,2048]{2,1,0:T(8,128)(2,1)}), bf16[16,72,2048]{2,1,0:T(8,128)(2,1)}, u32[]{:S(2)}, u32[]{:S(2)}) async-start(bf16[16,72,2048]{2,1,0:T(8,128)(2,1)} %fusion), calls=%async_computation | async-start | bytes 9437184 | tf_op jit(solution)/shard_map/all_to_all | solution.py:55
  155.1 0.2 all-gather.3.cloned.1.call-start
  155.3 6.3 %fusion.5 = f32[1152,384]{1,0:T(8,128)} fusion(bf16[1152,2048]{1,0:T(8,128)(2,1)} %bitcast.8, bf16[1,384,2048]{2,1,0:T(8,128)(2,1)S(1)} %copy-done.2), kind=kOutput, calls=%fused_computation.21 | convolution fusion | flops 1811939328 | bytes 8060928 | tf_op jit(solution)/shard_map/dot_general | solution.py:62
  161.7 6.2 %fusion.7 = f32[1152,384]{1,0:T(8,128)} fusion(bf16[1152,2048]{1,0:T(8,128)(2,1)} %bitcast.8, bf16[1,384,2048]{2,1,0:T(8,128)(2,1)S(1)} %copy-done.3), kind=kOutput, calls=%fused_computation.23 | convolution fusion | flops 1811939328 | bytes 8060928 | tf_op jit(solution)/shard_map/dot_general | solution.py:63
  167.8 74.1 %all-to-all-done = bf16[16,72,2048]{2,1,0:T(8,128)(2,1)} async-done(((bf16[16,72,2048]{2,1,0:T(8,128)(2,1)}), bf16[16,72,2048]{2,1,0:T(8,128)(2,1)}, u32[]{:S(2)}, u32[]{:S(2)}) %all-to-all-start) | async-done | bytes 4718624 | tf_op jit(solution)/shard_map/all_to_all | solution.py:55
  241.9 7.9 %multiply_convert_fusion.1 = (bf16[1152,384]{1,0:T(8,128)(2,1)}, bf16[1152,384]{1,0:T(8,128)(2,1)}) fusion(f32[1152,384]{1,0:T(8,128)} %fusion.5, f32[1152,384]{1,0:T(8,128)} %fusion.7, bf16[1152,2048]{1,0:T(8,128)(2,1)} %bitcast.5, bf16[1,384,2048]{2,1,0:T(8,128)(2,1)S(1)} %copy-done), kind=kOutput, calls=%fused_computation.17 | convolution fusion | flops 1817690112 | bytes 11599872 | tf_op jit(solution)/shard_map/dot_general | solution.py:64
  249.8 0.0 all-gather.3.cloned.1.call-update
  249.8 1.6 copy.17
  251.4 3.8 all-to-all-start.2
  255.2 0.0 all-gather.5.cloned.1.call-start
  255.2 0.7 all-gather.5.cloned.1.call-update
  255.9 1.6 copy.19
  257.5 18.1 %all-to-all-done.2 = bf16[384,2,1024]{0,2,1:T(8,128)(2,1)S(1)} async-done(((bf16[384,2,1024]{0,2,1:T(8,128)(2,1)}), bf16[384,2,1024]{0,2,1:T(8,128)(2,1)S(1)}, u32[]{:S(2)}, u32[]{:S(2)}) %all-to-all-start.2) | async-done | bytes 1572896 | tf_op jit(solution)/shard_map/all_to_all | solution.py:76
  275.6 3.7 all-to-all-start.3
  279.3 1.6 copy.18
  280.9 32.1 %all-to-all-done.3 = bf16[384,2,1024]{0,2,1:T(8,128)(2,1)S(1)} async-done(((bf16[384,2,1024]{0,2,1:T(8,128)(2,1)}), bf16[384,2,1024]{0,2,1:T(8,128)(2,1)S(1)}, u32[]{:S(2)}, u32[]{:S(2)}) %all-to-all-start.3) | async-done | bytes 1572896 | tf_op jit(solution)/shard_map/all_to_all | solution.py:77
  313.0 1.6 copy.20
  314.7 5.9 %fusion.24 = f32[1152,1024]{1,0:T(8,128)} fusion(bf16[1152,768]{1,0:T(8,128)(2,1)} %all-gather.3.cloned.1.call-done, bf16[768,1024]{1,0:T(8,128)(2,1)S(1)} %bitcast.61), kind=kOutput, calls=%fused_computation.56 | convolution fusion | flops 1811939328 | bytes 8060928 | tf_op jit(solution)/shard_map/dot_general | solution.py:79
  320.5 21.5 %all-gather.5.cloned.1.call-done = bf16[1152,768]{1,0:T(8,128)(2,1)} async-done(((bf16[1152,384]{1,0:T(8,128)(2,1)}), bf16[1152,768]{1,0:T(8,128)(2,1)}) %all-gather.5.cloned.1.call-update) | async-done | bytes 1769488 | tf_op jit(solution)/shard_map/all_gather | solution.py:85
  342.0 6.3 %add_convert_fusion = bf16[1152,1024]{1,0:T(8,128)(2,1)} fusion(f32[1152,1024]{1,0:T(8,128)} %fusion.24, bf16[1152,768]{1,0:T(8,128)(2,1)} %all-gather.5.cloned.1.call-done, bf16[768,1024]{1,0:T(8,128)(2,1)S(1)} %bitcast.62), kind=kOutput, calls=%fused_computation.7 | convolution fusion | flops 1814298624 | bytes 10420224 | tf_op jit(solution)/shard_map/dot_general | solution.py:84
  348.3 10.6 %all-to-all-start.4 = ((bf16[16,72,1024]{2,1,0:T(8,128)(2,1)}), bf16[16,72,1024]{2,1,0:T(8,128)(2,1)}, u32[]{:S(2)}, u32[]{:S(2)}) async-start(bf16[16,72,1024]{2,1,0:T(8,128)(2,1)} %bitcast.60), calls=%async_computation.4 | async-start | bytes 4718592 | tf_op jit(solution)/shard_map/all_to_all | solution.py:90
  359.0 5.8 %fusion.2 = bf16[1,384,2048]{2,1,0:T(8,128)(2,1)} fusion(bf16[1152,384]{1,0:T(8,128)(2,1)S(1)} %copy-done.8, bf16[1152,2048]{1,0:T(8,128)(2,1)} %bitcast.8), kind=kOutput, calls=%fused_computation.12 | convolution fusion | flops 1812725760 | bytes 7176192 | tf_op jit(solution)/shard_map/dot_general | solution.py:74
  364.8 5.9 %fusion.1 = bf16[1,384,2048]{2,1,0:T(8,128)(2,1)} fusion(bf16[1152,384]{1,0:T(8,128)(2,1)S(1)} %copy-done.7, bf16[1152,2048]{1,0:T(8,128)(2,1)} %bitcast.8), kind=kOutput, calls=%fused_computation.11 | convolution fusion | flops 1812725760 | bytes 7176192 | tf_op jit(solution)/shard_map/dot_general | solution.py:71
  370.6 5.9 %fusion.3 = bf16[1,384,2048]{2,1,0:T(8,128)(2,1)} fusion(bf16[1152,2048]{1,0:T(8,128)(2,1)} %bitcast.5, f32[1152,384]{1,0:T(8,128)S(1)} %copy-done.12, f32[1152,384]{1,0:T(8,128)S(1)} %copy-done.11), kind=kOutput, calls=%fused_computation.13 | convolution fusion | flops 1815379968 | bytes 9830400 | tf_op jit(solution)/shard_map/dot_general | solution.py:68
  376.5 28.2 %all-to-all-done.4 = bf16[16,72,1024]{2,1,0:T(8,128)(2,1)} async-done(((bf16[16,72,1024]{2,1,0:T(8,128)(2,1)}), bf16[16,72,1024]{2,1,0:T(8,128)(2,1)}, u32[]{:S(2)}, u32[]{:S(2)}) %all-to-all-start.4) | async-done | bytes 2359328 | tf_op jit(solution)/shard_map/all_to_all | solution.py:90
  404.7 8.1 %gather_fusion.3 = bf16[1024,1024]{1,0:T(8,128)(2,1)} fusion(bf16[1152,1024]{1,0:T(8,128)(2,1)} %bitcast.18, s32[1024]{0:T(1024)S(1)} %broadcast_clamp_fusion), kind=kCustom, calls=%fused_computation.3 | custom fusion | bytes 4198400 | tf_op jit(solution)/shard_map/gather | solution.py:91
  412.8 3.7 bitcast_reduce_fusion
  (38 shorter events, 0.2 us)
Async XLA Ops:
  7.2 234.7 %copy-start = (bf16[1,384,2048]{2,1,0:T(8,128)(2,1)S(1)}, bf16[1,384,2048]{2,1,0:T(8,128)(2,1)}, u32[]{:S(2)}) copy-start(bf16[1,384,2048]{2,1,0:T(8,128)(2,1)} %param.13) | copy-start | bytes 4718596
  14.7 4.7 %copy-start.9 = (bf16[128,1024]{1,0:T(8,128)(2,1)S(1)}, bf16[128,1024]{1,0:T(8,128)(2,1)}, u32[]{:S(2)}) copy-start(bf16[128,1024]{1,0:T(8,128)(2,1)} %param.7) | copy-start | bytes 786436
  40.1 6.5 %copy-start.10 = (bf16[128,1024]{1,0:T(8,128)(2,1)S(1)}, bf16[128,1024]{1,0:T(8,128)(2,1)}, u32[]{:S(2)}) copy-start(bf16[128,1024]{1,0:T(8,128)(2,1)} %param.8) | copy-start | bytes 786436
  40.1 93.2 %all-to-all-start.1 = ((bf16[16,72,2048]{2,1,0:T(8,128)(2,1)}), bf16[16,72,2048]{2,1,0:T(8,128)(2,1)}, u32[]{:S(2)}, u32[]{:S(2)}) async-start(bf16[16,72,2048]{2,1,0:T(8,128)(2,1)} %broadcast_multiply_fusion), calls=%async_computation.1 | async-start | bytes 9437184 | tf_op jit(solution)/shard_map/all_to_all | solution.py:54
  67.2 88.2 %copy-start.2 = (bf16[1,384,2048]{2,1,0:T(8,128)(2,1)S(1)}, bf16[1,384,2048]{2,1,0:T(8,128)(2,1)}, u32[]{:S(2)}) copy-start(bf16[1,384,2048]{2,1,0:T(8,128)(2,1)} %param.11) | copy-start | bytes 4718596
  133.3 108.6 %all-to-all-start = ((bf16[16,72,2048]{2,1,0:T(8,128)(2,1)}), bf16[16,72,2048]{2,1,0:T(8,128)(2,1)}, u32[]{:S(2)}, u32[]{:S(2)}) async-start(bf16[16,72,2048]{2,1,0:T(8,128)(2,1)} %fusion), calls=%async_computation | async-start | bytes 9437184 | tf_op jit(solution)/shard_map/all_to_all | solution.py:55
  155.1 159.6 %all-gather.3.cloned.1.call-start = ((), (), s32[]{:S(2)}) async-start(), calls=%async_computation.5 | async-start | bytes 2654208 | tf_op jit(solution)/shard_map/all_gather | solution.py:80
  155.3 6.3 %copy-start.3 = (bf16[1,384,2048]{2,1,0:T(8,128)(2,1)S(1)}, bf16[1,384,2048]{2,1,0:T(8,128)(2,1)}, u32[]{:S(2)}) copy-start(bf16[1,384,2048]{2,1,0:T(8,128)(2,1)} %param.12) | copy-start | bytes 4718596
  251.4 4.6 %copy-start.4 = (bf16[1,384,2048]{2,1,0:T(8,128)(2,1)S(1)}, bf16[1,384,2048]{2,1,0:T(8,128)(2,1)}, u32[]{:S(2)}) copy-start(bf16[1,384,2048]{2,1,0:T(8,128)(2,1)} %param.12) | copy-start | bytes 4718596
  251.4 24.2 %all-to-all-start.2 = ((bf16[384,2,1024]{0,2,1:T(8,128)(2,1)}), bf16[384,2,1024]{0,2,1:T(8,128)(2,1)S(1)}, u32[]{:S(2)}, u32[]{:S(2)}) async-start(bf16[384,2,1024]{0,2,1:T(8,128)(2,1)} %bitcast.11), calls=%async_computation.2 | async-start | bytes 3145728 | tf_op jit(solution)/shard_map/all_to_all | solution.py:76
  255.2 86.9 %all-gather.5.cloned.1.call-start = ((), (), s32[]{:S(2)}) async-start(), calls=%async_computation.6 | async-start | bytes 2654208 | tf_op jit(solution)/shard_map/all_gather | solution.py:85
  275.6 37.5 %all-to-all-start.3 = ((bf16[384,2,1024]{0,2,1:T(8,128)(2,1)}), bf16[384,2,1024]{0,2,1:T(8,128)(2,1)S(1)}, u32[]{:S(2)}, u32[]{:S(2)}) async-start(bf16[384,2,1024]{0,2,1:T(8,128)(2,1)} %bitcast.14), calls=%async_computation.3 | async-start | bytes 3145728 | tf_op jit(solution)/shard_map/all_to_all | solution.py:77
  280.9 33.8 %copy-start.5 = (bf16[2,384,1024]{2,1,0:T(8,128)(2,1)S(1)}, bf16[2,384,1024]{2,1,0:T(8,128)(2,1)}, u32[]{:S(2)}) copy-start(bf16[2,384,1024]{2,1,0:T(8,128)(2,1)} %copy.18) | copy-start | bytes 4718596
  314.7 27.4 %copy-start.6 = (bf16[2,384,1024]{2,1,0:T(8,128)(2,1)S(1)}, bf16[2,384,1024]{2,1,0:T(8,128)(2,1)}, u32[]{:S(2)}) copy-start(bf16[2,384,1024]{2,1,0:T(8,128)(2,1)} %copy.20) | copy-start | bytes 4718596
  348.3 10.6 %copy-start.8 = (bf16[1152,384]{1,0:T(8,128)(2,1)S(1)}, bf16[1152,384]{1,0:T(8,128)(2,1)}, u32[]{:S(2)}) copy-start(bf16[1152,384]{1,0:T(8,128)(2,1)} %get-tuple-element.6) | copy-start | bytes 2654212
  348.3 56.3 %all-to-all-start.4 = ((bf16[16,72,1024]{2,1,0:T(8,128)(2,1)}), bf16[16,72,1024]{2,1,0:T(8,128)(2,1)}, u32[]{:S(2)}, u32[]{:S(2)}) async-start(bf16[16,72,1024]{2,1,0:T(8,128)(2,1)} %bitcast.60), calls=%async_computation.4 | async-start | bytes 4718592 | tf_op jit(solution)/shard_map/all_to_all | solution.py:90
  359.0 5.8 %copy-start.7 = (bf16[1152,384]{1,0:T(8,128)(2,1)S(1)}, bf16[1152,384]{1,0:T(8,128)(2,1)}, u32[]{:S(2)}) copy-start(bf16[1152,384]{1,0:T(8,128)(2,1)} %get-tuple-element.7) | copy-start | bytes 2654212
  364.8 5.9 %copy-start.11 = (f32[1152,384]{1,0:T(8,128)S(1)}, f32[1152,384]{1,0:T(8,128)}, u32[]{:S(2)}) copy-start(f32[1152,384]{1,0:T(8,128)} %fusion.5) | copy-start | bytes 5308420
  364.8 5.9 %copy-start.12 = (f32[1152,384]{1,0:T(8,128)S(1)}, f32[1152,384]{1,0:T(8,128)}, u32[]{:S(2)}) copy-start(f32[1152,384]{1,0:T(8,128)} %fusion.7) | copy-start | bytes 5308420
  404.7 11.9 %copy-start.1 = (bf16[1,384,2048]{2,1,0:T(8,128)(2,1)S(1)}, bf16[1,384,2048]{2,1,0:T(8,128)(2,1)}, u32[]{:S(2)}) copy-start(bf16[1,384,2048]{2,1,0:T(8,128)(2,1)} %param.13) | copy-start | bytes 4718596
Sparse Core Ops, SparseCore 0:
  249.9 60.5 all-gather.2
  312.7 29.3 all-gather.4
where the time goes:
time: 431 us; the launch traced here: 423 us
  waiting for transfers between devices  241 us (56%)
  matrix products  50.2 us (12%)
  starting transfers between devices  46.5 us (11%)
  local copies, waits for them, and re-layouts  37.4 us (9%)
  blocking collectives  19.2 us (4%)
  other arithmetic  15 us (3%)
  between operations  14.3 us (3%)
    all_to_all x1, waiting for transfers between devices, body(): lax.all_to_all(grads_sent, 'expert', split_axis=0, concat_axis=0, tiled=T...  74.1 us
    all_to_all x1, waiting for transfers between devices, body(): lax.all_to_all(inputs_sent, 'expert', split_axis=0, concat_axis=0, tiled=...  66.1 us
    all_to_all x1, waiting for transfers between devices, body(): lax.all_to_all(up_w, 'etp', split_axis=1, concat_axis=0, tiled=True)  32.1 us
    all_to_all x1, waiting for transfers between devices, body(): lax.all_to_all(slot_grads, 'expert', split_axis=0, concat_axis=0, tiled=T...  28.2 us
    all_to_all x1, starting transfers between devices, body(): lax.all_to_all(grads_sent, 'expert', split_axis=0, concat_axis=0, tiled=T...  21.8 us
    all_gather x1, waiting for transfers between devices, body(): lax.all_gather(up_term, 'etp', axis=1, tiled=True)  21.5 us
    all_to_all x1, waiting for transfers between devices, body(): lax.all_to_all(gate_w, 'etp', split_axis=1, concat_axis=0, tiled=True)  18.1 us
    all_to_all x1, starting transfers between devices, body(): lax.all_to_all(slot_grads, 'expert', split_axis=0, concat_axis=0, tiled=T...  10.6 us
  transfers between devices with their start and end apart: 7, of which 6 were waited for; matrix products, arithmetic and copies ran while one was open for 13% of the time, Pallas kernels for 0%

commit v1 on v0

--- a/solution.py
+++ b/solution.py
@@ -1,7 +1,14 @@
+import functools
+
 import jax
 import jax.numpy as jnp
 from jax import lax
+from jax.experimental import pallas as pl
+from jax.experimental.pallas import tpu as pltpu
 from jax.sharding import PartitionSpec as P
+
+CONTRACT_LAST = (((1,), (1,)), ((), ()))
+CONTRACT_FIRST = (((0,), (0,)), ((), ()))
 
 
 def pack_rows(token_rows, grad_rows, token_of, scale, is_live):
@@ -28,7 +35,7 @@
     return counted.reshape(pair_total).astype(jnp.int32)
 
 
-def body(tokens, out_grad, routes, combine, w_gate, w_up, w_down):
+def exchange_body(tokens, out_grad, routes, combine, w_gate, w_up, w_down):
     experts = lax.axis_size("expert")
     tok_rows = tokens.shape[0]
     col_width = tokens.shape[1]
@@ -57,21 +64,19 @@
     gate_w = w_gate[0]
     up_w = w_up[0]
     down_w = w_down[0]
-    contract_last = (((1,), (1,)), ((), ()))
-    contract_first = (((0,), (0,)), ((), ()))
-    gate = lax.dot_general(rows_x, gate_w, contract_last, preferred_element_type=jnp.float32)
-    up = lax.dot_general(rows_x, up_w, contract_last, preferred_element_type=jnp.float32)
-    hidden_grad = lax.dot_general(rows_g, down_w, contract_last, preferred_element_type=jnp.float32)
+    gate = lax.dot_general(rows_x, gate_w, CONTRACT_LAST, preferred_element_type=jnp.float32)
+    up = lax.dot_general(rows_x, up_w, CONTRACT_LAST, preferred_element_type=jnp.float32)
+    hidden_grad = lax.dot_general(rows_g, down_w, CONTRACT_LAST, preferred_element_type=jnp.float32)
     sigma = jax.nn.sigmoid(gate)
     silu = gate * sigma
     acts = (silu * up).astype(jnp.bfloat16)
-    grad_down = lax.dot_general(acts, rows_g, contract_first, preferred_element_type=jnp.float32)
+    grad_down = lax.dot_general(acts, rows_g, CONTRACT_FIRST, preferred_element_type=jnp.float32)
     gate_term = (hidden_grad * up * sigma * (1.0 + gate * (1.0 - sigma))).astype(jnp.bfloat16)
     up_term = (hidden_grad * silu).astype(jnp.bfloat16)
     grad_gate = lax.dot_general(
-        gate_term, rows_x, contract_first, preferred_element_type=jnp.float32
-    )
-    grad_up = lax.dot_general(up_term, rows_x, contract_first, preferred_element_type=jnp.float32)
+        gate_term, rows_x, CONTRACT_FIRST, preferred_element_type=jnp.float32
+    )
+    grad_up = lax.dot_general(up_term, rows_x, CONTRACT_FIRST, preferred_element_type=jnp.float32)
     swapped_gate, swapped_up = (
         lax.all_to_all(gate_w, "etp", split_axis=1, concat_axis=0, tiled=True),
         lax.all_to_all(up_w, "etp", split_axis=1, concat_axis=0, tiled=True),
@@ -98,7 +103,148 @@
     )
 
 
+def expert_kernel(me_ref, info_ref, x_ref, g_ref, wg_ref, wu_ref, wd_ref,
+                  part_ref, rx_ref, rg_ref, act_ref, gt_ref, ut_ref):
+    me = me_ref[0]
+    blocks, halves, rows, width = x_ref.shape
+    top = info_ref.shape[1] // 2
+    span = blocks * rows
+    slots = rx_ref.shape[0]
+    named, weights = [], []
+    for b in range(blocks):
+        hit = info_ref[b, :top, :] == me.astype(jnp.float32)
+        named.append(jnp.sum(hit.astype(jnp.float32), axis=0, keepdims=True))
+        weights.append(jnp.sum(jnp.where(hit, info_ref[b, top:, :], 0.0), axis=0, keepdims=True))
+    named = jnp.concatenate(named, axis=1)
+    weights = jnp.concatenate(weights, axis=1)
+    earlier = (
+        lax.broadcasted_iota(jnp.int32, (span, span), 0)
+        < lax.broadcasted_iota(jnp.int32, (span, span), 1)
+    ).astype(jnp.bfloat16)
+    counted = jnp.dot(
+        jnp.broadcast_to(named, (16, span)).astype(jnp.bfloat16),
+        earlier,
+        preferred_element_type=jnp.float32,
+    )[:1]
+    slot_of = jnp.where(named > 0.0, counted.astype(jnp.int32), -1)
+    chosen = slot_of == lax.broadcasted_iota(jnp.int32, (slots, span), 0)
+    pick = chosen.astype(jnp.bfloat16)
+    scale = jnp.sum(jnp.where(chosen, weights, 0.0), axis=1, keepdims=True)
+
+    gate = up = hidden_grad = 0.0
+    for h in range(halves):
+        cols = slice(h * width, (h + 1) * width)
+        x = x_ref[:, h].reshape(span, width)
+        rx = jnp.dot(pick, x, preferred_element_type=jnp.float32).astype(jnp.bfloat16)
+        rx_ref[:, cols] = rx
+        gate += lax.dot_general(rx, wg_ref[:, cols], CONTRACT_LAST, preferred_element_type=jnp.float32)
+        up += lax.dot_general(rx, wu_ref[:, cols], CONTRACT_LAST, preferred_element_type=jnp.float32)
+        g = g_ref[:, h].reshape(span, width)
+        rg = (scale * jnp.dot(pick, g, preferred_element_type=jnp.float32)).astype(jnp.bfloat16)
+        rg_ref[:, cols] = rg
+        hidden_grad += lax.dot_general(rg, wd_ref[:, cols], CONTRACT_LAST, preferred_element_type=jnp.float32)
+
+    sigma = 1.0 / (1.0 + jnp.exp(-gate))
+    silu = gate * sigma
+    act_ref[...] = (silu * up).astype(jnp.bfloat16)
+    gate_term = (hidden_grad * up * sigma * (1.0 + gate * (1.0 - sigma))).astype(jnp.bfloat16)
+    up_term = (hidden_grad * silu).astype(jnp.bfloat16)
+    gt_ref[...] = gate_term
+    ut_ref[...] = up_term
+    for h in range(halves):
+        cols = slice(h * width, (h + 1) * width)
+        slot = jnp.dot(gate_term, wg_ref[:, cols], preferred_element_type=jnp.float32)
+        slot += jnp.dot(up_term, wu_ref[:, cols], preferred_element_type=jnp.float32)
+        back = lax.dot_general(
+            pick, slot.astype(jnp.bfloat16), CONTRACT_FIRST, preferred_element_type=jnp.float32
+        )
+        part_ref[:, h] = back.astype(jnp.bfloat16).reshape(blocks, rows, width)
+
+
+def run_experts(me, info, x, g, gate_w, up_w, down_w, per_step, slots):
+    blocks, halves, rows, width = x.shape
+    hidden, features = gate_w.shape
+    steps = blocks // per_step
+    flops = 2 * steps * slots * features * (hidden * 5 + per_step * rows * 3)
+    moved = 2 * (x.size * 3 + 3 * gate_w.size + steps * slots * (2 * features + 3 * hidden))
+    whole = pl.BlockSpec((hidden, features), lambda i, me: (0, 0))
+    token_blocks = pl.BlockSpec((per_step, halves, rows, width), lambda i, me: (i, 0, 0, 0))
+    return pl.pallas_call(
+        expert_kernel,
+        grid_spec=pltpu.PrefetchScalarGridSpec(
+            num_scalar_prefetch=1,
+            grid=(steps,),
+            in_specs=[
+                pl.BlockSpec((per_step,) + info.shape[1:], lambda i, me: (i, 0, 0)),
+                token_blocks,
+                token_blocks,
+                whole,
+                whole,
+                whole,
+            ],
+            out_specs=[
+                token_blocks,
+                pl.BlockSpec((slots, features), lambda i, me: (i, 0)),
+                pl.BlockSpec((slots, features), lambda i, me: (i, 0)),
+                pl.BlockSpec((slots, hidden), lambda i, me: (i, 0)),
+                pl.BlockSpec((slots, hidden), lambda i, me: (i, 0)),
+                pl.BlockSpec((slots, hidden), lambda i, me: (i, 0)),
+            ],
+        ),
+        out_shape=[
+            jax.ShapeDtypeStruct(x.shape, jnp.bfloat16),
+            jax.ShapeDtypeStruct((steps * slots, features), jnp.bfloat16),
+            jax.ShapeDtypeStruct((steps * slots, features), jnp.bfloat16),
+            jax.ShapeDtypeStruct((steps * slots, hidden), jnp.bfloat16),
+            jax.ShapeDtypeStruct((steps * slots, hidden), jnp.bfloat16),
+            jax.ShapeDtypeStruct((steps * slots, hidden), jnp.bfloat16),
+        ],
+        compiler_params=pltpu.CompilerParams(vmem_limit_bytes=56 * 1024 * 1024),
+        cost_estimate=pl.CostEstimate(flops=flops, bytes_accessed=moved, transcendentals=steps * slots * hidden),
+        name="experts",
+    )(me, info, x, g, gate_w, up_w, down_w)
+
+
+def gather_body(per_step, tokens, out_grad, routes, combine, w_gate, w_up, w_down):
+    experts = lax.axis_size("expert")
+    halves = lax.axis_size("etp")
+    rows, width = tokens.shape
+    top = routes.shape[1]
+    per_pair = rows * top // experts
+    capacity = per_pair + per_pair // 8
+    slots = -(-per_step * capacity // 16) * 16
+    me = lax.axis_index("expert").astype(jnp.int32).reshape(1)
+    info = jnp.concatenate([routes.astype(jnp.float32), combine], axis=1).T
+    info = lax.all_gather(info, "expert", axis=0)
+    x = lax.all_gather(tokens, ("expert", "etp"), axis=0).reshape(experts, halves, rows, width)
+    g = lax.all_gather(out_grad, ("expert", "etp"), axis=0).reshape(experts, halves, rows, width)
+    part, rows_x, rows_g, acts, gate_term, up_term = run_experts(
+        me, info, x, g, w_gate[0], w_up[0], w_down[0], per_step, slots
+    )
+    part = part.reshape(experts * halves * rows, width)
+    grad_tokens = lax.psum_scatter(part, ("expert", "etp"), scatter_dimension=0, tiled=True)
+    grad_down = lax.dot_general(acts, rows_g, CONTRACT_FIRST, preferred_element_type=jnp.float32)
+    grad_gate = lax.dot_general(gate_term, rows_x, CONTRACT_FIRST, preferred_element_type=jnp.float32)
+    grad_up = lax.dot_general(up_term, rows_x, CONTRACT_FIRST, preferred_element_type=jnp.float32)
+    return (
+        grad_tokens,
+        grad_gate.astype(jnp.bfloat16)[None],
+        grad_up.astype(jnp.bfloat16)[None],
+        grad_down.astype(jnp.bfloat16)[None],
+    )
+
+
 def solution(mesh):
+    experts = mesh.shape["expert"]
+
+    def body(tokens, out_grad, routes, combine, w_gate, w_up, w_down):
+        rows, top = routes.shape
+        if top * 4 >= experts and experts % 4 == 0:
+            run = functools.partial(gather_body, experts // 4)
+        else:
+            run = exchange_body
+        return run(tokens, out_grad, routes, combine, w_gate, w_up, w_down)
+
     placed = (
         P("expert", "etp"),
         P("expert", "etp"),

time: 431 us -> 388 us (0.900); the launches traced: 423 us -> 388 us
  waiting for transfers between devices: 241 us -> 305 us
  starting transfers between devices: 46.5 us -> 0.11 us
  matrix products: 50.2 us -> 12.7 us
  local copies, waits for them, and re-layouts: 37.4 us -> 1.15 us
  Pallas kernels: 0 us -> 29.2 us
  other arithmetic: 15 us -> 1.38 us
  blocking collectives: 19.2 us -> 24.8 us
    all_to_all x5 -> x0, waiting for transfers between devices: 219 us -> none  [the longest x1 74.1 us: body(): lax.all_to_all(grads_sent, 'expert', split_axis=0, concat_axis=0, tiled=T...]
    reduce_scatter x0 -> x1, waiting for transfers between devices: none -> 168 us  [gather_body(): lax.psum_scatter(part, ('expert', 'etp'), scatter_dimension=0, tiled=True)]
    all_gather x2, waiting for transfers between devices: 21.5 us -> 135 us  [the longest x1 78.9 us: gather_body(): lax.all_gather(out_grad, ('expert', 'etp'), axis=0)]
    all_to_all x5 -> x0, starting transfers between devices: 46.3 us -> none  [the longest x1 21.8 us: body(): lax.all_to_all(grads_sent, 'expert', split_axis=0, concat_axis=0, tiled=T...]
    dot_general x9 -> x3, matrix products: 50.2 us -> 12.7 us  [the longest x1 5.86 us: gather_body(): lax.dot_general(gate_term, rows_x, CONTRACT_FIRST, preferred_element_type...]
    pallas_call x0 -> x1, Pallas kernels: none -> 29.2 us  [run_experts(): pl.pallas_call(expert_kernel, grid_spec=pltpu.PrefetchScalarGridSpec(num_...]
    gather x4 -> x0, local copies, waits for them, and re-layouts: 24.5 us -> none  [the longest x1 8.12 us: body(): returned[target].astype(jnp.float32)]
    mul x4 -> x0, other arithmetic: 5.69 us -> none  [the longest x2 4.88 us: pack_rows(): inputs_sent = token_rows[token_of] * mask]
  transfers between devices with their start and end apart: 7 -> 3, of which waited for: 6 -> 3; matrix products, arithmetic and copies ran while one was open for 13% -> 4% of each run, Pallas kernels for 0% -> 0%
where the time goes in v1:
time: 388 us
  waiting for transfers between devices  305 us (79%)
  Pallas kernels  29.2 us (8%)
  blocking collectives  24.8 us (6%)
  between operations  13.8 us (4%)
  matrix products  12.7 us (3%)
    reduce_scatter x1, waiting for transfers between devices, gather_body(): lax.psum_scatter(part, ('expert', 'etp'), scatter_dimension=0, tiled=True)  168 us
    all_gather x1, waiting for transfers between devices, gather_body(): lax.all_gather(out_grad, ('expert', 'etp'), axis=0)  78.9 us
    all_gather x1, waiting for transfers between devices, gather_body(): lax.all_gather(tokens, ('expert', 'etp'), axis=0)  56.2 us
    pallas_call x1, Pallas kernels, run_experts(): pl.pallas_call(expert_kernel, grid_spec=pltpu.PrefetchScalarGridSpec(num_...  29.2 us
    all_gather x1, blocking collectives, gather_body(): info = lax.all_gather(info, 'expert', axis=0)  24.8 us
  transfers between devices with their start and end apart: 3, of which 3 were waited for; matrix products, arithmetic and copies ran while one was open for 4% of the time, Pallas kernels for 0%

profile of v1, /device:TPU:0, one launch (start us, length us, event | category | flops | bytes accessed | tf_op | source)
XLA Modules:
  0.0 387.7 jit_solution(3665759999195523569)
XLA Ops:
  7.2 0.0 all-gather.6.cloned.1.call-start
  7.2 0.7 all-gather.6.cloned.1.call-update
  7.9 0.0 all-gather.8.cloned.1.call-start
  7.9 0.7 all-gather.8.cloned.1.call-update
  8.6 0.0 reduce-scatter.2.cloned.1.call-start
  8.7 0.7 convert_element_type.12
  9.4 0.7 maximum_bitcast_fusion
  10.1 24.8 %all-gather = f32[256,128]{1,0:T(8,128)} all-gather(f32[16,128]{1,0:T(8,128)S(1)} %maximum_bitcast_fusion), channel_id=2, replica_groups=mesh['expert'=16,'etp'=2] {'expert'}, dimensions={0}, use_global_device_ids=true | all-gather | bytes 139264 | tf_op jit(solution)/shard_map/all_gather | solution.py:218
  34.9 56.2 %all-gather.6.cloned.1.call-done = bf16[4096,1024]{1,0:T(8,128)(2,1)} async-done(((bf16[128,1024]{1,0:T(8,128)(2,1)}), bf16[4096,1024]{1,0:T(8,128)(2,1)}) %all-gather.6.cloned.1.call-update) | async-done | bytes 8388624 | tf_op jit(solution)/shard_map/all_gather | solution.py:219
  91.1 78.9 %all-gather.8.cloned.1.call-done = bf16[4096,1024]{1,0:T(8,128)(2,1)} async-done(((bf16[128,1024]{1,0:T(8,128)(2,1)}), bf16[4096,1024]{1,0:T(8,128)(2,1)}) %all-gather.8.cloned.1.call-update) | async-done | bytes 8388624 | tf_op jit(solution)/shard_map/all_gather | solution.py:220
  170.0 29.2 %experts.1 = (bf16[16,2,128,1024]{3,2,1,0:T(8,128)(2,1)}, bf16[1152,2048]{1,0:T(8,128)(2,1)}, bf16[1152,2048]{1,0:T(8,128)(2,1)}, bf16[1152,384]{1,0:T(8,128)(2,...) custom-call(s32[1]{0:T(128)} %bitcast.me_ref, f32[16,16,128]{2,1,0:T(8,128)} %bitcast.23, ...), custom_call_target="tpu_custom_call" | custom-call | flops 16307453952 | bytes 41975808 | tf_op jit(solution)/shard_map/experts/pallas_call | solution.py:172
  199.2 0.0 copy-start.2
  199.2 0.0 slice-start.2
  199.2 0.0 reduce-scatter.2.cloned.1.call-update
  199.3 1.1 copy-done.2
  200.4 0.0 slice-start.3
  200.4 0.0 copy-start.1
  200.4 0.0 slice-start
  200.4 5.9 %fusion = bf16[1,384,2048]{2,1,0:T(8,128)(2,1)} fusion(bf16[1152,384]{1,0:T(8,128)(2,1)S(1)} %copy-done.2, bf16[1152,2048]{1,0:T(8,128)(2,1)} %get-tuple-element.12), kind=kOutput, calls=%fused_computation.3 | convolution fusion | flops 1812725760 | bytes 7176192 | tf_op jit(solution)/shard_map/dot_general | solution.py:227
  206.3 0.0 slice-done.2
  206.3 0.0 slice-done.3
  206.3 0.0 copy-done.1
  206.3 0.0 slice-start.1
  206.3 0.0 copy-start
  206.3 3.4 fusion.1
  209.7 0.0 slice-done
  209.7 0.0 slice-done.1
  209.7 0.0 copy-done
  209.7 3.4 fusion.2
  213.1 168.1 %reduce-scatter.2.cloned.1.call-done = bf16[128,1024]{1,0:T(8,128)(2,1)} async-done(((bf16[4096,1024]{1,0:T(8,128)(2,1)}), bf16[128,1024]{1,0:T(8,128)(2,1)}) %reduce-scatter.2.cloned.1.call-update) | async-done | bytes 262160 | tf_op jit(solution)/shard_map/reduce_scatter | solution.py:225
  (2 shorter events, 0.0 us)
Async XLA Ops:
  7.2 84.0 %all-gather.6.cloned.1.call-start = ((), (), s32[]{:S(2)}) async-start(), calls=%async_computation.2 | async-start | bytes 8650752 | tf_op jit(solution)/shard_map/all_gather | solution.py:219
  7.9 162.1 %all-gather.8.cloned.1.call-start = ((), (), s32[]{:S(2)}) async-start(), calls=%async_computation.3 | async-start | bytes 8650752 | tf_op jit(solution)/shard_map/all_gather | solution.py:220
  8.6 372.5 %reduce-scatter.2.cloned.1.call-start = ((), (), s32[]{:S(2)}) async-start(), calls=%async_computation.1 | async-start | bytes 8650752 | tf_op jit(solution)/shard_map/reduce_scatter | solution.py:225
  199.2 1.2 copy-start.2
  199.2 7.0 %slice-start.2 = ((s8[4718592]{0:T(1024)(128)(4,1)}), s8[524288]{0:T(1024)(128)(4,1)S(1)}, s32[]{:S(2)}) async-start(s8[4718592]{0:T(1024)(128)(4,1)} %bitcast.31), calls=%async_computation.6 | async-start | bytes 1048576
  200.4 5.9 %slice-start.3 = ((s8[4718592]{0:T(1024)(128)(4,1)}), s8[4194304]{0:T(1024)(128)(4,1)S(1)}, s32[]{:S(2)}) async-start(s8[4718592]{0:T(1024)(128)(4,1)} %bitcast.31), calls=%async_computation.7 | async-start | bytes 8388608
  200.4 5.9 %copy-start.1 = (bf16[1152,384]{1,0:T(8,128)(2,1)S(1)}, bf16[1152,384]{1,0:T(8,128)(2,1)}, u32[]{:S(2)}) copy-start(bf16[1152,384]{1,0:T(8,128)(2,1)} %get-tuple-element.13) | copy-start | bytes 2654212
  200.4 9.3 %slice-start = ((s8[4718592]{0:T(1024)(128)(4,1)}), s8[4194304]{0:T(1024)(128)(4,1)S(1)}, s32[]{:S(2)}) async-start(s8[4718592]{0:T(1024)(128)(4,1)} %bitcast.29), calls=%async_computation.4 | async-start | bytes 8388608
  206.3 3.4 slice-start.1
  206.3 3.4 copy-start
Sparse Core Ops, SparseCore 0:
  11.0 80.0 all-gather.5
  94.1 75.8 all-gather.7
  199.4 181.7 reduce-scatter.1

commit v2 on v1

--- a/solution.py
+++ b/solution.py
@@ -9,6 +9,7 @@
 
 CONTRACT_LAST = (((1,), (1,)), ((), ()))
 CONTRACT_FIRST = (((0,), (0,)), ((), ()))
+INFO_ROWS = 16
 
 
 def pack_rows(token_rows, grad_rows, token_of, scale, is_live):
@@ -103,18 +104,53 @@
     )
 
 
-def expert_kernel(me_ref, info_ref, x_ref, g_ref, wg_ref, wu_ref, wd_ref,
-                  part_ref, rx_ref, rg_ref, act_ref, gt_ref, ut_ref):
-    me = me_ref[0]
-    blocks, halves, rows, width = x_ref.shape
-    top = info_ref.shape[1] // 2
+def pack_kernel(tokens_ref, grads_ref, routes_ref, combine_ref, out_ref):
+    rows = tokens_ref.shape[0]
+    out_ref[:rows] = tokens_ref[...]
+    out_ref[rows:2 * rows] = grads_ref[...]
+    top = routes_ref.shape[1]
+    routes = routes_ref[...].astype(jnp.float32).T
+    weights = combine_ref[...].T
+    high = weights.astype(jnp.bfloat16).astype(jnp.float32)
+    middle = (weights - high).astype(jnp.bfloat16).astype(jnp.float32)
+    low = weights - high - middle
+    blank = jnp.zeros((INFO_ROWS - 4, rows), jnp.float32)
+    for k in range(top):
+        own = slice(k, k + 1)
+        column = jnp.concatenate([routes[own], high[own], middle[own], low[own], blank], axis=0)
+        out_ref[2 * rows:, k * rows:(k + 1) * rows] = column.astype(jnp.bfloat16)
+
+
+def pack_share(tokens, out_grad, routes, combine):
+    rows, width = tokens.shape
+    return pl.pallas_call(
+        pack_kernel,
+        out_shape=jax.ShapeDtypeStruct((2 * rows + INFO_ROWS, width), jnp.bfloat16),
+        name="pack",
+    )(tokens, out_grad, routes, combine)
+
+
+def expert_kernel(chained, top, rows, place_ref, *refs):
+    shares, refs = refs[:8], refs[8:]
+    wg_ref, wu_ref, wd_ref = refs[:3]
+    refs = refs[3 + (5 if chained else 0):]
+    near_ref, far_ref, rx_ref, rg_ref, act_ref, gt_ref, ut_ref = refs
+    me = place_ref[0].astype(jnp.float32)
+    own_half = place_ref[1]
+    width = shares[0].shape[1]
+    blocks = 4
     span = blocks * rows
     slots = rx_ref.shape[0]
     named, weights = [], []
     for b in range(blocks):
-        hit = info_ref[b, :top, :] == me.astype(jnp.float32)
-        named.append(jnp.sum(hit.astype(jnp.float32), axis=0, keepdims=True))
-        weights.append(jnp.sum(jnp.where(hit, info_ref[b, top:, :], 0.0), axis=0, keepdims=True))
+        hits, weight = 0.0, 0.0
+        for k in range(top):
+            info = shares[2 * b][2 * rows:, k * rows:(k + 1) * rows].astype(jnp.float32)
+            hit = info[0:1] == me
+            hits += hit.astype(jnp.float32)
+            weight += jnp.where(hit, info[1:2] + info[2:3] + info[3:4], 0.0)
+        named.append(hits)
+        weights.append(weight)
     named = jnp.concatenate(named, axis=1)
     weights = jnp.concatenate(weights, axis=1)
     earlier = (
@@ -132,14 +168,15 @@
     scale = jnp.sum(jnp.where(chosen, weights, 0.0), axis=1, keepdims=True)
 
     gate = up = hidden_grad = 0.0
-    for h in range(halves):
-        cols = slice(h * width, (h + 1) * width)
-        x = x_ref[:, h].reshape(span, width)
+    for h in range(2):
+        start = pl.multiple_of((own_half if h == 0 else 1 - own_half) * width, width)
+        cols = pl.ds(start, width)
+        x = jnp.concatenate([shares[2 * b + h][:rows] for b in range(blocks)], axis=0)
         rx = jnp.dot(pick, x, preferred_element_type=jnp.float32).astype(jnp.bfloat16)
         rx_ref[:, cols] = rx
         gate += lax.dot_general(rx, wg_ref[:, cols], CONTRACT_LAST, preferred_element_type=jnp.float32)
         up += lax.dot_general(rx, wu_ref[:, cols], CONTRACT_LAST, preferred_element_type=jnp.float32)
-        g = g_ref[:, h].reshape(span, width)
+        g = jnp.concatenate([shares[2 * b + h][rows:2 * rows] for b in range(blocks)], axis=0)
         rg = (scale * jnp.dot(pick, g, preferred_element_type=jnp.float32)).astype(jnp.bfloat16)
         rg_ref[:, cols] = rg
         hidden_grad += lax.dot_general(rg, wd_ref[:, cols], CONTRACT_LAST, preferred_element_type=jnp.float32)
@@ -151,78 +188,108 @@
     up_term = (hidden_grad * silu).astype(jnp.bfloat16)
     gt_ref[...] = gate_term
     ut_ref[...] = up_term
-    for h in range(halves):
-        cols = slice(h * width, (h + 1) * width)
+    for h in range(2):
+        start = pl.multiple_of((own_half if h == 0 else 1 - own_half) * width, width)
+        cols = pl.ds(start, width)
         slot = jnp.dot(gate_term, wg_ref[:, cols], preferred_element_type=jnp.float32)
         slot += jnp.dot(up_term, wu_ref[:, cols], preferred_element_type=jnp.float32)
         back = lax.dot_general(
             pick, slot.astype(jnp.bfloat16), CONTRACT_FIRST, preferred_element_type=jnp.float32
-        )
-        part_ref[:, h] = back.astype(jnp.bfloat16).reshape(blocks, rows, width)
-
-
-def run_experts(me, info, x, g, gate_w, up_w, down_w, per_step, slots):
-    blocks, halves, rows, width = x.shape
-    hidden, features = gate_w.shape
-    steps = blocks // per_step
-    flops = 2 * steps * slots * features * (hidden * 5 + per_step * rows * 3)
-    moved = 2 * (x.size * 3 + 3 * gate_w.size + steps * slots * (2 * features + 3 * hidden))
-    whole = pl.BlockSpec((hidden, features), lambda i, me: (0, 0))
-    token_blocks = pl.BlockSpec((per_step, halves, rows, width), lambda i, me: (i, 0, 0, 0))
+        ).astype(jnp.bfloat16)
+        for b in range(blocks):
+            target = near_ref if b < 2 else far_ref
+            target[b % 2, h] = back[b * rows:(b + 1) * rows]
+
+
+def run_experts(index, chunks, place, shares, weights, kept, top, rows, slots):
+    width = shares[0].shape[1]
+    hidden, features = weights[0].shape
+    vmem = pl.BlockSpec(memory_space=pltpu.VMEM)
+    part = jax.ShapeDtypeStruct((2, 2, rows, width), jnp.bfloat16)
+    wide = jax.ShapeDtypeStruct((chunks * slots, features), jnp.bfloat16)
+    narrow = jax.ShapeDtypeStruct((chunks * slots, hidden), jnp.bfloat16)
+    wide_block = pl.BlockSpec((slots, features), lambda i: (index, 0))
+    narrow_block = pl.BlockSpec((slots, hidden), lambda i: (index, 0))
+    part_block = pl.BlockSpec(part.shape, lambda i: (0, 0, 0, 0))
+    first_kept = 1 + len(shares) + 3
     return pl.pallas_call(
-        expert_kernel,
-        grid_spec=pltpu.PrefetchScalarGridSpec(
-            num_scalar_prefetch=1,
-            grid=(steps,),
-            in_specs=[
-                pl.BlockSpec((per_step,) + info.shape[1:], lambda i, me: (i, 0, 0)),
-                token_blocks,
-                token_blocks,
-                whole,
-                whole,
-                whole,
-            ],
-            out_specs=[
-                token_blocks,
-                pl.BlockSpec((slots, features), lambda i, me: (i, 0)),
-                pl.BlockSpec((slots, features), lambda i, me: (i, 0)),
-                pl.BlockSpec((slots, hidden), lambda i, me: (i, 0)),
-                pl.BlockSpec((slots, hidden), lambda i, me: (i, 0)),
-                pl.BlockSpec((slots, hidden), lambda i, me: (i, 0)),
-            ],
+        functools.partial(expert_kernel, kept is not None, top, rows),
+        grid=(1,),
+        in_specs=[pl.BlockSpec(memory_space=pltpu.SMEM)]
+        + [pl.BlockSpec(s.shape, lambda i: (0, 0)) for s in shares]
+        + [pl.BlockSpec((hidden, features), lambda i: (0, 0))] * 3
+        + [pl.BlockSpec(memory_space=pl.ANY)] * (0 if kept is None else 5),
+        out_specs=[part_block] * 2 + [wide_block] * 2 + [narrow_block] * 3,
+        out_shape=[part, part, wide, wide, narrow, narrow, narrow],
+        input_output_aliases={} if kept is None else {first_kept + i: 2 + i for i in range(5)},
+        compiler_params=pltpu.CompilerParams(vmem_limit_bytes=56 * 1024 * 1024),
+        cost_estimate=pl.CostEstimate(
+            flops=2 * slots * features * (hidden * 5 + 4 * rows * 3),
+            bytes_accessed=2 * (8 * shares[0].size + 3 * hidden * features + slots * (2 * features + 3 * hidden)),
+            transcendentals=slots * hidden,
         ),
-        out_shape=[
-            jax.ShapeDtypeStruct(x.shape, jnp.bfloat16),
-            jax.ShapeDtypeStruct((steps * slots, features), jnp.bfloat16),
-            jax.ShapeDtypeStruct((steps * slots, features), jnp.bfloat16),
-            jax.ShapeDtypeStruct((steps * slots, hidden), jnp.bfloat16),
-            jax.ShapeDtypeStruct((steps * slots, hidden), jnp.bfloat16),
-            jax.ShapeDtypeStruct((steps * slots, hidden), jnp.bfloat16),
-        ],
-        compiler_params=pltpu.CompilerParams(vmem_limit_bytes=56 * 1024 * 1024),
-        cost_estimate=pl.CostEstimate(flops=flops, bytes_accessed=moved, transcendentals=steps * slots * hidden),
         name="experts",
-    )(me, info, x, g, gate_w, up_w, down_w)
-
-
-def gather_body(per_step, tokens, out_grad, routes, combine, w_gate, w_up, w_down):
+    )(place, *shares, *weights, *(kept or ()))
+
+
+def ring_order(length):
+    return list(range(0, min(1, length))) + list(range(1, length, 2)) + list(range(2, length, 2))[::-1]
+
+
+def gather_body(tokens, out_grad, routes, combine, w_gate, w_up, w_down):
     experts = lax.axis_size("expert")
-    halves = lax.axis_size("etp")
+    chunks = experts // 4
     rows, width = tokens.shape
     top = routes.shape[1]
     per_pair = rows * top // experts
     capacity = per_pair + per_pair // 8
-    slots = -(-per_step * capacity // 16) * 16
-    me = lax.axis_index("expert").astype(jnp.int32).reshape(1)
-    info = jnp.concatenate([routes.astype(jnp.float32), combine], axis=1).T
-    info = lax.all_gather(info, "expert", axis=0)
-    x = lax.all_gather(tokens, ("expert", "etp"), axis=0).reshape(experts, halves, rows, width)
-    g = lax.all_gather(out_grad, ("expert", "etp"), axis=0).reshape(experts, halves, rows, width)
-    part, rows_x, rows_g, acts, gate_term, up_term = run_experts(
-        me, info, x, g, w_gate[0], w_up[0], w_down[0], per_step, slots
-    )
-    part = part.reshape(experts * halves * rows, width)
-    grad_tokens = lax.psum_scatter(part, ("expert", "etp"), scatter_dimension=0, tiled=True)
+    slots = -(-4 * capacity // 16) * 16
+    order = ring_order(chunks)
+    ahead = [
+        (order[i] * 4 + r, order[(i + 1) % chunks] * 4 + r) for i in range(chunks) for r in range(4)
+    ]
+
+    def to_ring(value):
+        return lax.ppermute(value, "expert", ahead)
+
+    def to_side(value):
+        return lax.ppermute(value, "expert", [(e, e ^ 2) for e in range(experts)])
+
+    def to_core(value):
+        return lax.ppermute(value, "expert", [(e, e ^ 1) for e in range(experts)])
+
+    def to_half(value):
+        return lax.ppermute(value, "etp", [(0, 1), (1, 0)])
+
+    place = jnp.stack([lax.axis_index("expert"), lax.axis_index("etp")]).astype(jnp.int32)
+    weights = (w_gate[0], w_up[0], w_down[0])
+    share = pack_share(tokens, out_grad, routes, combine)
+    kept = None
+    running = None
+    for c in range(chunks):
+        if c > 0:
+            share = to_ring(share)
+        across, aside = to_half(share), to_side(share)
+        both = to_half(aside) if c % 2 == 0 else to_side(across)
+        near = [share, across, aside, both]
+        far = [to_core(s) for s in near]
+        near_part, far_part, *kept = run_experts(
+            c, chunks, place, near + far, weights, kept, top, rows, slots
+        )
+        mine = near_part.astype(jnp.float32) + to_core(far_part).astype(jnp.float32)
+        if c % 2 == 0:
+            mine = mine[0] + to_side(mine[1].astype(jnp.bfloat16)).astype(jnp.float32)
+            mine = mine[0] + to_half(mine[1].astype(jnp.bfloat16)).astype(jnp.float32)
+        else:
+            mine = mine[:, 0] + to_half(mine[:, 1].astype(jnp.bfloat16)).astype(jnp.float32)
+            mine = mine[0] + to_side(mine[1].astype(jnp.bfloat16)).astype(jnp.float32)
+        if c == 0:
+            own = mine
+        else:
+            running = mine if c == 1 else mine + running.astype(jnp.float32)
+            running = to_ring(running.astype(jnp.bfloat16))
+    grad_tokens = (own if running is None else own + running.astype(jnp.float32)).astype(jnp.bfloat16)
+    rows_x, rows_g, acts, gate_term, up_term = kept
     grad_down = lax.dot_general(acts, rows_g, CONTRACT_FIRST, preferred_element_type=jnp.float32)
     grad_gate = lax.dot_general(gate_term, rows_x, CONTRACT_FIRST, preferred_element_type=jnp.float32)
     grad_up = lax.dot_general(up_term, rows_x, CONTRACT_FIRST, preferred_element_type=jnp.float32)
@@ -238,11 +305,10 @@
     experts = mesh.shape["expert"]
 
     def body(tokens, out_grad, routes, combine, w_gate, w_up, w_down):
-        rows, top = routes.shape
-        if top * 4 >= experts and experts % 4 == 0:
-            run = functools.partial(gather_body, experts // 4)
-        else:
-            run = exchange_body
+        rows, width = tokens.shape
+        top = routes.shape[1]
+        gathers = top * 4 >= experts and experts % 4 == 0 and mesh.shape["etp"] == 2
+        run = gather_body if gathers and top * rows <= width else exchange_body
         return run(tokens, out_grad, routes, combine, w_gate, w_up, w_down)
 
     placed = (

time: 388 us -> 190 us (0.49)
  waiting for transfers between devices: 305 us -> 77.6 us
  starting transfers between devices: 0.11 us -> 43.7 us
  blocking collectives: 24.8 us -> 0 us
  Pallas kernels: 29.2 us -> 47.3 us
  between operations: 13.8 us -> 1.01 us
  local copies, waits for them, and re-layouts: 1.15 us -> 6.49 us
    reduce_scatter x1 -> x0, waiting for transfers between devices: 168 us -> none  [gather_body(): lax.psum_scatter(part, ('expert', 'etp'), scatter_dimension=0, tiled=True)]
    all_gather x2 -> x0, waiting for transfers between devices: 135 us -> none  [the longest x1 78.9 us: gather_body(): lax.all_gather(out_grad, ('expert', 'etp'), axis=0)]
    ppermute x0 -> x46, waiting for transfers between devices: none -> 77.6 us  [the longest x10 38.8 us: to_half(): return lax.ppermute(value, 'etp', [(0, 1), (1, 0)])]
    ppermute x0 -> x46, starting transfers between devices: none -> 43.7 us  [the longest x10 14.2 us: to_side(): return lax.ppermute(value, 'expert', [(e, e ^ 2) for e in range(experts)])]
    all_gather x1 -> x0, blocking collectives: 24.8 us -> none  [gather_body(): info = lax.all_gather(info, 'expert', axis=0)]
    pallas_call x1 -> x5, Pallas kernels: 29.2 us -> 47.3 us  [the longest x4 45.4 us: run_experts(): pl.pallas_call(functools.partial(expert_kernel, kept is not None, top, ro...]
  transfers between devices with their start and end apart: 3 -> 46, of which waited for: 3 -> 14; matrix products, arithmetic and copies ran while one was open for 4% -> 8% of each run, Pallas kernels for 0% -> 24%
where the time goes in v2:
time: 190 us
  waiting for transfers between devices  77.6 us (41%)
  Pallas kernels  47.3 us (25%)
  starting transfers between devices  43.7 us (23%)
  matrix products  10.2 us (5%)
  local copies, waits for them, and re-layouts  6.49 us (3%)
  other arithmetic  3.8 us (2%)
    pallas_call x4, Pallas kernels, run_experts(): pl.pallas_call(functools.partial(expert_kernel, kept is not None, top, ro...  45.4 us
    ppermute x10, waiting for transfers between devices, to_half(): return lax.ppermute(value, 'etp', [(0, 1), (1, 0)])  38.8 us
    ppermute x10, waiting for transfers between devices, to_side(): return lax.ppermute(value, 'expert', [(e, e ^ 2) for e in range(experts)])  32.9 us
    ppermute x10, starting transfers between devices, to_side(): return lax.ppermute(value, 'expert', [(e, e ^ 2) for e in range(experts)])  14.2 us
    ppermute x6, starting transfers between devices, to_ring(): return lax.ppermute(value, 'expert', ahead)  13 us
    ppermute x10, starting transfers between devices, to_half(): return lax.ppermute(value, 'etp', [(0, 1), (1, 0)])  12.3 us
    ppermute x6, waiting for transfers between devices, to_ring(): return lax.ppermute(value, 'expert', ahead)  5.97 us
    unnamed x56, local copies, waits for them, and re-layouts  4.7 us
  transfers between devices with their start and end apart: 46, of which 14 were waited for; matrix products, arithmetic and copies ran while one was open for 8% of the time, Pallas kernels for 24%

profile of v2, /device:TPU:0, one launch (start us, length us, event | category | flops | bytes accessed | tf_op | source)
XLA Modules:
  0.0 190.2 jit_solution(1852241880343112233)
XLA Ops:
  0.6 1.4 copy.26.routes_ref
  2.0 1.4 copy.27.combine_ref
  3.5 1.9 %pack.1.refs_0_ = bf16[272,1024]{1,0:T(8,128)(2,1)} custom-call(bf16[128,1024]{1,0:T(8,128)(2,1)} %tokens_ref.1, bf16[128,1024]{1,0:T(8,128)(2,1)} %grads_ref.1, s32[128,8]{1,0:T(8,128)} %copy.26.routes_ref, f32[128,8]{1,0:T(8,128)} %copy.27.combine_ref), custom_call_target="tpu_custom_call" | custom-call | tf_op jit(solution)/shard_map/pack/pallas_call | solution.py:126
  5.4 3.0 %collective-permute-start.1 = (bf16[272,1024]{1,0:T(8,128)(2,1)}, bf16[272,1024]{1,0:T(8,128)(2,1)S(1)}, u32[]{:S(2)}, u32[]{:S(2)}) collective-permute-start(bf16[272,1024]{1,0:T(8,128)(2,1)} %pack.1.refs_0_), channel_id=1, source_target_pairs={{0,4},{2,6},{4,0},{6,2},{8,12},{10,14},{12,8},{14,10},{16,20},{18,... | collective-permute-start | bytes 1671176 | tf_op jit(solution)/shard_map/ppermute | solution.py:256
  8.3 1.5 collective-permute-start
  9.8 1.6 collective-permute-start.10
  11.4 9.8 %collective-permute-done.1.refs_2_ = bf16[272,1024]{1,0:T(8,128)(2,1)S(1)} collective-permute-done((bf16[272,1024]{1,0:T(8,128)(2,1)}, bf16[272,1024]{1,0:T(8,128)(2,1)S(1)}, u32[]{:S(2)}, u32[]{:S(2)}) %collective-permute-start.1) | collective-permute-done | bytes 557088 | tf_op jit(solution)/shard_map/ppermute | solution.py:256
  21.2 1.7 collective-permute-start.2
  23.4 1.4 collective-permute-done.10.refs_0_
  26.1 10.6 %collective-permute-done.2.refs_3_ = bf16[272,1024]{1,0:T(8,128)(2,1)S(1)} collective-permute-done((bf16[272,1024]{1,0:T(8,128)(2,1)S(1)}, bf16[272,1024]{1,0:T(8,128)(2,1)S(1)}, u32[]{:S(2)}, u32[]{:S(2)}) %collective-permute-start.2) | collective-permute-done | bytes 557088 | tf_op jit(solution)/shard_map/ppermute | solution.py:262
  36.8 1.9 collective-permute-start.11
  38.8 8.1 %collective-permute-done.27.refs_1_ = bf16[272,1024]{1,0:T(8,128)(2,1)S(1)} collective-permute-done((bf16[272,1024]{1,0:T(8,128)(2,1)S(1)}, bf16[272,1024]{1,0:T(8,128)(2,1)S(1)}, u32[]{:S(2)}, u32[]{:S(2)}) %collective-permute-start.27) | collective-permute-done | bytes 557088 | tf_op jit(solution)/shard_map/ppermute | solution.py:262
  46.9 1.4 collective-permute-start.29
  49.7 3.2 %collective-permute-done.11.refs_0_ = bf16[272,1024]{1,0:T(8,128)(2,1)S(1)} collective-permute-done((bf16[272,1024]{1,0:T(8,128)(2,1)S(1)}, bf16[272,1024]{1,0:T(8,128)(2,1)S(1)}, u32[]{:S(2)}, u32[]{:S(2)}) %collective-permute-start.11) | collective-permute-done | bytes 557088 | tf_op jit(solution)/shard_map/ppermute | solution.py:253
  52.9 1.6 collective-permute-start.21
  55.0 1.5 collective-permute-start.20
  56.5 6.1 %collective-permute-done.29.refs_3_ = bf16[272,1024]{1,0:T(8,128)(2,1)} collective-permute-done((bf16[272,1024]{1,0:T(8,128)(2,1)S(1)}, bf16[272,1024]{1,0:T(8,128)(2,1)}, u32[]{:S(2)}, u32[]{:S(2)}) %collective-permute-start.29) | collective-permute-done | bytes 557088 | tf_op jit(solution)/shard_map/ppermute | solution.py:256
  62.6 1.5 collective-permute-start.12
  64.1 11.3 %experts.4 = (bf16[2,2,128,1024]{3,2,1,0:T(8,128)(2,1)}, bf16[2,2,128,1024]{3,2,1,0:T(8,128)(2,1)}, bf16[1152,2048]{1,0:T(8,128)(2,1)}, bf16[1152,2048]{1,0:T(8,...) custom-call(s32[2]{0:T(128)} %pad_add_fusion.place_ref, ...), custom_call_target="tpu_custom_call" | custom-call | flops 4076863488 | bytes 12197888 | tf_op jit(solution)/shard_map/experts/pallas_call | solution.py:215
  76.1 1.5 collective-permute-start.22
  78.7 11.3 %experts.5 = (bf16[2,2,128,1024]{3,2,1,0:T(8,128)(2,1)}, bf16[2,2,128,1024]{3,2,1,0:T(8,128)(2,1)}, bf16[1152,2048]{1,0:T(8,128)(2,1)}, bf16[1152,2048]{1,0:T(8,...) custom-call(s32[2]{0:T(128)} %pad_add_fusion.place_ref, ...), custom_call_target="tpu_custom_call", output_to_operand_aliasing={{2}: (12, {}), {3}: (13, {}), {4}: (14, {}), {5}: (15, {}),... | custom-call | flops 4076863488 | bytes 12197888 | tf_op jit(solution)/shard_map/experts/pallas_call | solution.py:215
  90.0 1.4 copy.30
  92.0 1.5 collective-permute-start.14
  93.5 9.7 %collective-permute-done.13.refs_1_ = bf16[272,1024]{1,0:T(8,128)(2,1)} collective-permute-done((bf16[272,1024]{1,0:T(8,128)(2,1)S(1)}, bf16[272,1024]{1,0:T(8,128)(2,1)}, u32[]{:S(2)}, u32[]{:S(2)}) %collective-permute-start.13) | collective-permute-done | bytes 557088 | tf_op jit(solution)/shard_map/ppermute | solution.py:262
  103.2 1.5 collective-permute-start.15
  105.4 1.7 collective-permute-done.14.refs_2_
  108.0 11.5 %experts.6 = (bf16[2,2,128,1024]{3,2,1,0:T(8,128)(2,1)}, bf16[2,2,128,1024]{3,2,1,0:T(8,128)(2,1)}, bf16[1152,2048]{1,0:T(8,128)(2,1)}, bf16[1152,2048]{1,0:T(8,...) custom-call(s32[2]{0:T(128)} %pad_add_fusion.place_ref, ...), custom_call_target="tpu_custom_call", output_to_operand_aliasing={{2}: (12, {}), {3}: (13, {}), {4}: (14, {}), {5}: (15, {}),... | custom-call | flops 4076863488 | bytes 12197888 | tf_op jit(solution)/shard_map/experts/pallas_call | solution.py:215
  120.7 1.4 collective-permute-start.41
  122.2 1.6 collective-permute-start.8
  123.8 11.3 %experts.7 = (bf16[2,2,128,1024]{3,2,1,0:T(8,128)(2,1)}, bf16[2,2,128,1024]{3,2,1,0:T(8,128)(2,1)}, bf16[1152,2048]{1,0:T(8,128)(2,1)}, bf16[1152,2048]{1,0:T(8,...) custom-call(s32[2]{0:T(128)} %pad_add_fusion.place_ref, ...), custom_call_target="tpu_custom_call", output_to_operand_aliasing={{2}: (12, {}), {3}: (13, {}), {4}: (14, {}), {5}: (15, {}),... | custom-call | flops 4076863488 | bytes 12197888 | tf_op jit(solution)/shard_map/experts/pallas_call | solution.py:215
  135.4 1.6 collective-permute-start.42
  138.3 1.4 collective-permute-start.9
  139.7 4.9 %collective-permute-done.42 = bf16[128,1024]{1,0:T(8,128)(2,1)S(1)} collective-permute-done((bf16[128,1024]{1,0:T(8,128)(2,1)S(1)}, bf16[128,1024]{1,0:T(8,128)(2,1)S(1)}, u32[]{:S(2)}, u32[]{:S(2)}) %collective-permute-start.42) | collective-permute-done | bytes 262176 | tf_op jit(solution)/shard_map/ppermute | solution.py:256
  144.7 2.9 %collective-permute-start.43 = (bf16[128,1024]{1,0:T(8,128)(2,1)S(1)}, bf16[128,1024]{1,0:T(8,128)(2,1)S(1)}, u32[]{:S(2)}, u32[]{:S(2)}) collective-permute-start(bf16[128,1024]{1,0:T(8,128)(2,1)S(1)} %fusion.12), channel_id=1, source_target_pairs={{0,8},{2,10},{4,12},{6,14},{8,24},{10,26},{12,28},{14,30},{24,16},... | collective-permute-start | bytes 786440 | tf_op jit(solution)/shard_map/ppermute | solution.py:253
  147.6 7.8 %collective-permute-done.38 = bf16[2,128,1024]{2,1,0:T(8,128)(2,1)S(1)} collective-permute-done((bf16[2,128,1024]{2,1,0:T(8,128)(2,1)S(1)}, bf16[2,128,1024]{2,1,0:T(8,128)(2,1)S(1)}, u32[]{:S(2)}, u32[]{:S(2)}) %collective-permute-start.38) | collective-permute-done | bytes 524320 | tf_op jit(solution)/shard_map/ppermute | solution.py:256
  155.6 1.1 collective-permute-start.39
  157.2 1.0 collective-permute-start.35
  158.2 3.4 %fusion.1 = bf16[1,384,2048]{2,1,0:T(8,128)(2,1)} fusion(bf16[1152,384]{1,0:T(8,128)(2,1)S(1)} %copy-done.2, bf16[1152,2048]{1,0:T(8,128)(2,1)S(1)} %bitcast.82), kind=kOutput, calls=%fused_computation.4 | convolution fusion | flops 1812725760 | bytes 7176192 | tf_op jit(solution)/shard_map/dot_general | solution.py:295
  161.6 3.2 %collective-permute-done.39 = bf16[128,1024]{1,0:T(8,128)(2,1)S(1)} collective-permute-done((bf16[128,1024]{1,0:T(8,128)(2,1)S(1)}, bf16[128,1024]{1,0:T(8,128)(2,1)S(1)}, u32[]{:S(2)}, u32[]{:S(2)}) %collective-permute-start.39) | collective-permute-done | bytes 262176 | tf_op jit(solution)/shard_map/ppermute | solution.py:262
  165.0 2.6 %collective-permute-start.44 = (bf16[128,1024]{1,0:T(8,128)(2,1)S(1)}, bf16[128,1024]{1,0:T(8,128)(2,1)S(1)}, u32[]{:S(2)}, u32[]{:S(2)}) collective-permute-start(bf16[128,1024]{1,0:T(8,128)(2,1)S(1)} %fusion.15), channel_id=1, source_target_pairs={{0,8},{2,10},{4,12},{6,14},{8,24},{10,26},{12,28},{14,30},{24,16},... | collective-permute-start | bytes 786440 | tf_op jit(solution)/shard_map/ppermute | solution.py:253
  167.6 7.1 %collective-permute-done.35 = bf16[2,128,1024]{2,1,0:T(8,128)(2,1)S(1)} collective-permute-done((bf16[2,128,1024]{2,1,0:T(8,128)(2,1)S(1)}, bf16[2,128,1024]{2,1,0:T(8,128)(2,1)S(1)}, u32[]{:S(2)}, u32[]{:S(2)}) %collective-permute-start.35) | collective-permute-done | bytes 524320 | tf_op jit(solution)/shard_map/ppermute | solution.py:262
  174.9 1.0 collective-permute-start.36
  175.9 3.4 %fusion = bf16[1,384,2048]{2,1,0:T(8,128)(2,1)} fusion(bf16[1152,384]{1,0:T(8,128)(2,1)S(1)} %copy-done.1, bf16[1152,2048]{1,0:T(8,128)(2,1)S(1)} %bitcast.82), kind=kOutput, calls=%fused_computation.3 | convolution fusion | flops 1812725760 | bytes 7176192 | tf_op jit(solution)/shard_map/dot_general | solution.py:294
  179.3 2.6 %collective-permute-done.36 = bf16[128,1024]{1,0:T(8,128)(2,1)S(1)} collective-permute-done((bf16[128,1024]{1,0:T(8,128)(2,1)S(1)}, bf16[128,1024]{1,0:T(8,128)(2,1)S(1)}, u32[]{:S(2)}, u32[]{:S(2)}) %collective-permute-start.36) | collective-permute-done | bytes 262176 | tf_op jit(solution)/shard_map/ppermute | solution.py:256
  182.1 2.5 %collective-permute-start.45 = (bf16[128,1024]{1,0:T(8,128)(2,1)S(1)}, bf16[128,1024]{1,0:T(8,128)(2,1)S(1)}, u32[]{:S(2)}, u32[]{:S(2)}) collective-permute-start(bf16[128,1024]{1,0:T(8,128)(2,1)S(1)} %fusion.18), channel_id=1, source_target_pairs={{0,8},{2,10},{4,12},{6,14},{8,24},{10,26},{12,28},{14,30},{24,16},... | collective-permute-start | bytes 786440 | tf_op jit(solution)/shard_map/ppermute | solution.py:253
  184.5 3.4 %fusion.2 = bf16[1,384,2048]{2,1,0:T(8,128)(2,1)} fusion(bf16[1152,384]{1,0:T(8,128)(2,1)S(1)} %copy-done, bf16[1152,2048]{1,0:T(8,128)(2,1)S(1)} %bitcast.84), kind=kOutput, calls=%fused_computation.5 | convolution fusion | flops 1812725760 | bytes 7176192 | tf_op jit(solution)/shard_map/dot_general | solution.py:293
  188.0 1.4 collective-permute-done.45
  189.4 0.8 fusion.21
  (132 shorter events, 11.7 us)
Async XLA Ops:
  5.4 15.8 %collective-permute-start.1 = (bf16[272,1024]{1,0:T(8,128)(2,1)}, bf16[272,1024]{1,0:T(8,128)(2,1)S(1)}, u32[]{:S(2)}, u32[]{:S(2)}) collective-permute-start(bf16[272,1024]{1,0:T(8,128)(2,1)} %pack.1.refs_0_), channel_id=1, source_target_pairs={{0,4},{2,6},{4,0},{6,2},{8,12},{10,14},{12,8},{14,10},{16,20},{18,... | collective-permute-start | bytes 1671176 | tf_op jit(solution)/shard_map/ppermute | solution.py:256
  8.3 14.6 %collective-permute-start = (bf16[272,1024]{1,0:T(8,128)(2,1)}, bf16[272,1024]{1,0:T(8,128)(2,1)S(1)}, u32[]{:S(2)}, u32[]{:S(2)}) collective-permute-start(bf16[272,1024]{1,0:T(8,128)(2,1)} %pack.1.refs_0_), channel_id=1, source_target_pairs={{0,1},{1,0},{2,3},{3,2},{4,5},{5,4},{6,7},{7,6},{8,9},{9,8},{10,11... | collective-permute-start | bytes 1671176 | tf_op jit(solution)/shard_map/ppermute | solution.py:262
  9.8 14.9 %collective-permute-start.10 = (bf16[272,1024]{1,0:T(8,128)(2,1)}, bf16[272,1024]{1,0:T(8,128)(2,1)S(1)}, u32[]{:S(2)}, u32[]{:S(2)}) collective-permute-start(bf16[272,1024]{1,0:T(8,128)(2,1)} %pack.1.refs_0_), channel_id=1, source_target_pairs={{0,8},{2,10},{4,12},{6,14},{8,24},{10,26},{12,28},{14,30},{24,16},... | collective-permute-start | bytes 1671176 | tf_op jit(solution)/shard_map/ppermute | solution.py:253
  11.4 13.9 %collective-permute-start.3 = (bf16[272,1024]{1,0:T(8,128)(2,1)}, bf16[272,1024]{1,0:T(8,128)(2,1)S(1)}, u32[]{:S(2)}, u32[]{:S(2)}) collective-permute-start(bf16[272,1024]{1,0:T(8,128)(2,1)} %pack.1.refs_0_), channel_id=1, source_target_pairs={{0,2},{2,0},{4,6},{6,4},{8,10},{10,8},{12,14},{14,12},{16,18},{18,... | collective-permute-start | bytes 1671176 | tf_op jit(solution)/shard_map/ppermute | solution.py:259
  21.2 28.5 %copy-start.17 = (bf16[272,1024]{1,0:T(8,128)(2,1)}, bf16[272,1024]{1,0:T(8,128)(2,1)S(1)}, u32[]{:S(2)}) copy-start(bf16[272,1024]{1,0:T(8,128)(2,1)S(1)} %collective-permute-done.1.refs_2_) | copy-start | bytes 1671172
  21.2 15.6 %collective-permute-start.2 = (bf16[272,1024]{1,0:T(8,128)(2,1)S(1)}, bf16[272,1024]{1,0:T(8,128)(2,1)S(1)}, u32[]{:S(2)}, u32[]{:S(2)}) collective-permute-start(bf16[272,1024]{1,0:T(8,128)(2,1)S(1)} %collective-permute-done.1.refs_2_), channel_id=1, source_target_pairs={{0,1},{1,0},{2,3},{3,2},{4,5},{5,4},{6,7},{7,6},{8,9},{9,8},{10,11... | collective-permute-start | bytes 1671176 | tf_op jit(solution)/shard_map/ppermute | solution.py:262
  22.9 13.9 %collective-permute-start.5 = (bf16[272,1024]{1,0:T(8,128)(2,1)S(1)}, bf16[272,1024]{1,0:T(8,128)(2,1)}, u32[]{:S(2)}, u32[]{:S(2)}) collective-permute-start(bf16[272,1024]{1,0:T(8,128)(2,1)S(1)} %collective-permute-done.1.refs_2_), channel_id=1, source_target_pairs={{0,2},{2,0},{4,6},{6,4},{8,10},{10,8},{12,14},{14,12},{16,18},{18,... | collective-permute-start | bytes 1671176 | tf_op jit(solution)/shard_map/ppermute | solution.py:259
  22.9 15.7 %collective-permute-start.4 = (bf16[272,1024]{1,0:T(8,128)(2,1)S(1)}, bf16[272,1024]{1,0:T(8,128)(2,1)S(1)}, u32[]{:S(2)}, u32[]{:S(2)}) collective-permute-start(bf16[272,1024]{1,0:T(8,128)(2,1)S(1)} %collective-permute-done.refs_1_), channel_id=1, source_target_pairs={{0,2},{2,0},{4,6},{6,4},{8,10},{10,8},{12,14},{14,12},{16,18},{18,... | collective-permute-start | bytes 1671176 | tf_op jit(solution)/shard_map/ppermute | solution.py:259
  24.8 50.6 %copy-start.9 = (bf16[272,1024]{1,0:T(8,128)(2,1)}, bf16[272,1024]{1,0:T(8,128)(2,1)S(1)}, u32[]{:S(2)}) copy-start(bf16[272,1024]{1,0:T(8,128)(2,1)S(1)} %collective-permute-done.10.refs_0_) | copy-start | bytes 1671172
  24.8 22.2 %collective-permute-start.27 = (bf16[272,1024]{1,0:T(8,128)(2,1)S(1)}, bf16[272,1024]{1,0:T(8,128)(2,1)S(1)}, u32[]{:S(2)}, u32[]{:S(2)}) collective-permute-start(bf16[272,1024]{1,0:T(8,128)(2,1)S(1)} %collective-permute-done.10.refs_0_), channel_id=1, source_target_pairs={{0,1},{1,0},{2,3},{3,2},{4,5},{5,4},{6,7},{7,6},{8,9},{9,8},{10,11... | collective-permute-start | bytes 1671176 | tf_op jit(solution)/shard_map/ppermute | solution.py:262
  25.3 23.0 %collective-permute-start.28 = (bf16[272,1024]{1,0:T(8,128)(2,1)S(1)}, bf16[272,1024]{1,0:T(8,128)(2,1)}, u32[]{:S(2)}, u32[]{:S(2)}) collective-permute-start(bf16[272,1024]{1,0:T(8,128)(2,1)S(1)} %collective-permute-done.10.refs_0_), channel_id=1, source_target_pairs={{0,4},{2,6},{4,0},{6,2},{8,12},{10,14},{12,8},{14,10},{16,20},{18,... | collective-permute-start | bytes 1671176 | tf_op jit(solution)/shard_map/ppermute | solution.py:256
  36.7 11.6 %collective-permute-start.30 = (bf16[272,1024]{1,0:T(8,128)(2,1)S(1)}, bf16[272,1024]{1,0:T(8,128)(2,1)S(1)}, u32[]{:S(2)}, u32[]{:S(2)}) collective-permute-start(bf16[272,1024]{1,0:T(8,128)(2,1)S(1)} %collective-permute-done.10.refs_0_), channel_id=1, source_target_pairs={{0,2},{2,0},{4,6},{6,4},{8,10},{10,8},{12,14},{14,12},{16,18},{18,... | collective-permute-start | bytes 1671176 | tf_op jit(solution)/shard_map/ppermute | solution.py:259
  36.8 16.1 %collective-permute-start.11 = (bf16[272,1024]{1,0:T(8,128)(2,1)S(1)}, bf16[272,1024]{1,0:T(8,128)(2,1)S(1)}, u32[]{:S(2)}, u32[]{:S(2)}) collective-permute-start(bf16[272,1024]{1,0:T(8,128)(2,1)S(1)} %collective-permute-done.10.refs_0_), channel_id=1, source_target_pairs={{0,8},{2,10},{4,12},{6,14},{8,24},{10,26},{12,28},{14,30},{24,16},... | collective-permute-start | bytes 1671176 | tf_op jit(solution)/shard_map/ppermute | solution.py:253
  38.6 16.4 %collective-permute-start.6 = (bf16[272,1024]{1,0:T(8,128)(2,1)S(1)}, bf16[272,1024]{1,0:T(8,128)(2,1)S(1)}, u32[]{:S(2)}, u32[]{:S(2)}) collective-permute-start(bf16[272,1024]{1,0:T(8,128)(2,1)S(1)} %collective-permute-done.2.refs_3_), channel_id=1, source_target_pairs={{0,2},{2,0},{4,6},{6,4},{8,10},{10,8},{12,14},{14,12},{16,18},{18,... | collective-permute-start | bytes 1671176 | tf_op jit(solution)/shard_map/ppermute | solution.py:259
  46.9 15.7 %collective-permute-start.29 = (bf16[272,1024]{1,0:T(8,128)(2,1)S(1)}, bf16[272,1024]{1,0:T(8,128)(2,1)}, u32[]{:S(2)}, u32[]{:S(2)}) collective-permute-start(bf16[272,1024]{1,0:T(8,128)(2,1)S(1)} %collective-permute-done.27.refs_1_), channel_id=1, source_target_pairs={{0,4},{2,6},{4,0},{6,2},{8,12},{10,14},{12,8},{14,10},{16,20},{18,... | collective-permute-start | bytes 1671176 | tf_op jit(solution)/shard_map/ppermute | solution.py:256
  48.4 15.7 %collective-permute-start.31 = (bf16[272,1024]{1,0:T(8,128)(2,1)S(1)}, bf16[272,1024]{1,0:T(8,128)(2,1)}, u32[]{:S(2)}, u32[]{:S(2)}) collective-permute-start(bf16[272,1024]{1,0:T(8,128)(2,1)S(1)} %collective-permute-done.27.refs_1_), channel_id=1, source_target_pairs={{0,2},{2,0},{4,6},{6,4},{8,10},{10,8},{12,14},{14,12},{16,18},{18,... | collective-permute-start | bytes 1671176 | tf_op jit(solution)/shard_map/ppermute | solution.py:259
  49.2 26.2 %collective-permute-start.32 = (bf16[272,1024]{1,0:T(8,128)(2,1)}, bf16[272,1024]{1,0:T(8,128)(2,1)}, u32[]{:S(2)}, u32[]{:S(2)}) collective-permute-start(bf16[272,1024]{1,0:T(8,128)(2,1)} %collective-permute-done.28.refs_2_), channel_id=1, source_target_pairs={{0,2},{2,0},{4,6},{6,4},{8,10},{10,8},{12,14},{14,12},{16,18},{18,... | collective-permute-start | bytes 1671176 | tf_op jit(solution)/shard_map/ppermute | solution.py:259
  52.9 23.1 %collective-permute-start.21 = (bf16[272,1024]{1,0:T(8,128)(2,1)S(1)}, bf16[272,1024]{1,0:T(8,128)(2,1)S(1)}, u32[]{:S(2)}, u32[]{:S(2)}) collective-permute-start(bf16[272,1024]{1,0:T(8,128)(2,1)S(1)} %collective-permute-done.11.refs_0_), channel_id=1, source_target_pairs={{0,4},{2,6},{4,0},{6,2},{8,12},{10,14},{12,8},{14,10},{16,20},{18,... | collective-permute-start | bytes 1671176 | tf_op jit(solution)/shard_map/ppermute | solution.py:256
  55.0 21.1 %collective-permute-start.20 = (bf16[272,1024]{1,0:T(8,128)(2,1)S(1)}, bf16[272,1024]{1,0:T(8,128)(2,1)}, u32[]{:S(2)}, u32[]{:S(2)}) collective-permute-start(bf16[272,1024]{1,0:T(8,128)(2,1)S(1)} %collective-permute-done.11.refs_0_), channel_id=1, source_target_pairs={{0,1},{1,0},{2,3},{3,2},{4,5},{5,4},{6,7},{7,6},{8,9},{9,8},{10,11... | collective-permute-start | bytes 1671176 | tf_op jit(solution)/shard_map/ppermute | solution.py:262
  62.6 15.0 %collective-permute-start.12 = (bf16[272,1024]{1,0:T(8,128)(2,1)S(1)}, bf16[272,1024]{1,0:T(8,128)(2,1)S(1)}, u32[]{:S(2)}, u32[]{:S(2)}) collective-permute-start(bf16[272,1024]{1,0:T(8,128)(2,1)S(1)} %collective-permute-done.11.refs_0_), channel_id=1, source_target_pairs={{0,8},{2,10},{4,12},{6,14},{8,24},{10,26},{12,28},{14,30},{24,16},... | collective-permute-start | bytes 1671176 | tf_op jit(solution)/shard_map/ppermute | solution.py:253
  64.1 13.7 %collective-permute-start.33 = (bf16[272,1024]{1,0:T(8,128)(2,1)}, bf16[272,1024]{1,0:T(8,128)(2,1)S(1)}, u32[]{:S(2)}, u32[]{:S(2)}) collective-permute-start(bf16[272,1024]{1,0:T(8,128)(2,1)} %collective-permute-done.29.refs_3_), channel_id=1, source_target_pairs={{0,2},{2,0},{4,6},{6,4},{8,10},{10,8},{12,14},{14,12},{16,18},{18,... | collective-permute-start | bytes 1671176 | tf_op jit(solution)/shard_map/ppermute | solution.py:259
  75.4 27.7 %collective-permute-start.7 = (bf16[2,2,128,1024]{3,2,1,0:T(8,128)(2,1)}, bf16[2,2,128,1024]{3,2,1,0:T(8,128)(2,1)S(1)}, u32[]{:S(2)}, u32[]{:S(2)}) collective-permute-start(bf16[2,2,128,1024]{3,2,1,0:T(8,128)(2,1)} %get-tuple-element.33), channel_id=1, source_target_pairs={{0,2},{2,0},{4,6},{6,4},{8,10},{10,8},{12,14},{14,12},{16,18},{18,... | collective-permute-start | bytes 3145736 | tf_op jit(solution)/shard_map/ppermute | solution.py:259
  76.0 15.4 %collective-permute-start.23 = (bf16[272,1024]{1,0:T(8,128)(2,1)S(1)}, bf16[272,1024]{1,0:T(8,128)(2,1)}, u32[]{:S(2)}, u32[]{:S(2)}) collective-permute-start(bf16[272,1024]{1,0:T(8,128)(2,1)S(1)} %collective-permute-done.11.refs_0_), channel_id=1, source_target_pairs={{0,2},{2,0},{4,6},{6,4},{8,10},{10,8},{12,14},{14,12},{16,18},{18,... | collective-permute-start | bytes 1671176 | tf_op jit(solution)/shard_map/ppermute | solution.py:259
  76.1 15.6 %collective-permute-start.22 = (bf16[272,1024]{1,0:T(8,128)(2,1)S(1)}, bf16[272,1024]{1,0:T(8,128)(2,1)}, u32[]{:S(2)}, u32[]{:S(2)}) collective-permute-start(bf16[272,1024]{1,0:T(8,128)(2,1)S(1)} %collective-permute-done.21.refs_2_), channel_id=1, source_target_pairs={{0,1},{1,0},{2,3},{3,2},{4,5},{5,4},{6,7},{7,6},{8,9},{9,8},{10,11... | collective-permute-start | bytes 1671176 | tf_op jit(solution)/shard_map/ppermute | solution.py:262
  77.6 14.3 %collective-permute-start.25 = (bf16[272,1024]{1,0:T(8,128)(2,1)S(1)}, bf16[272,1024]{1,0:T(8,128)(2,1)S(1)}, u32[]{:S(2)}, u32[]{:S(2)}) collective-permute-start(bf16[272,1024]{1,0:T(8,128)(2,1)S(1)} %collective-permute-done.21.refs_2_), channel_id=1, source_target_pairs={{0,2},{2,0},{4,6},{6,4},{8,10},{10,8},{12,14},{14,12},{16,18},{18,... | collective-permute-start | bytes 1671176 | tf_op jit(solution)/shard_map/ppermute | solution.py:259
  77.8 25.4 %collective-permute-start.13 = (bf16[272,1024]{1,0:T(8,128)(2,1)S(1)}, bf16[272,1024]{1,0:T(8,128)(2,1)}, u32[]{:S(2)}, u32[]{:S(2)}) collective-permute-start(bf16[272,1024]{1,0:T(8,128)(2,1)S(1)} %collective-permute-done.12.refs_0_), channel_id=1, source_target_pairs={{0,1},{1,0},{2,3},{3,2},{4,5},{5,4},{6,7},{7,6},{8,9},{9,8},{10,11... | collective-permute-start | bytes 1671176 | tf_op jit(solution)/shard_map/ppermute | solution.py:262
  91.4 28.7 %collective-permute-start.40 = (bf16[2,2,128,1024]{3,2,0,1:T(8,128)(2,1)S(1)}, bf16[2,2,128,1024]{3,2,0,1:T(8,128)(2,1)S(1)}, u32[]{:S(2)}, u32[]{:S(2)}) collective-permute-start(bf16[2,2,128,1024]{3,2,0,1:T(8,128)(2,1)S(1)} %copy.30), channel_id=1, source_target_pairs={{0,2},{2,0},{4,6},{6,4},{8,10},{10,8},{12,14},{14,12},{16,18},{18,... | collective-permute-start | bytes 3145736 | tf_op jit(solution)/shard_map/ppermute | solution.py:259
  91.7 13.3 %collective-permute-start.24 = (bf16[272,1024]{1,0:T(8,128)(2,1)}, bf16[272,1024]{1,0:T(8,128)(2,1)S(1)}, u32[]{:S(2)}, u32[]{:S(2)}) collective-permute-start(bf16[272,1024]{1,0:T(8,128)(2,1)} %collective-permute-done.20.refs_1_), channel_id=1, source_target_pairs={{0,2},{2,0},{4,6},{6,4},{8,10},{10,8},{12,14},{14,12},{16,18},{18,... | collective-permute-start | bytes 1671176 | tf_op jit(solution)/shard_map/ppermute | solution.py:259
  92.0 15.2 %collective-permute-start.14 = (bf16[272,1024]{1,0:T(8,128)(2,1)S(1)}, bf16[272,1024]{1,0:T(8,128)(2,1)}, u32[]{:S(2)}, u32[]{:S(2)}) collective-permute-start(bf16[272,1024]{1,0:T(8,128)(2,1)S(1)} %collective-permute-done.12.refs_0_), channel_id=1, source_target_pairs={{0,4},{2,6},{4,0},{6,2},{8,12},{10,14},{12,8},{14,10},{16,20},{18,... | collective-permute-start | bytes 1671176 | tf_op jit(solution)/shard_map/ppermute | solution.py:256
  103.1 4.0 %collective-permute-start.26 = (bf16[272,1024]{1,0:T(8,128)(2,1)}, bf16[272,1024]{1,0:T(8,128)(2,1)S(1)}, u32[]{:S(2)}, u32[]{:S(2)}) collective-permute-start(bf16[272,1024]{1,0:T(8,128)(2,1)} %collective-permute-done.22.refs_3_), channel_id=1, source_target_pairs={{0,2},{2,0},{4,6},{6,4},{8,10},{10,8},{12,14},{14,12},{16,18},{18,... | collective-permute-start | bytes 1671176 | tf_op jit(solution)/shard_map/ppermute | solution.py:259
  103.2 16.4 %collective-permute-start.15 = (bf16[272,1024]{1,0:T(8,128)(2,1)}, bf16[272,1024]{1,0:T(8,128)(2,1)}, u32[]{:S(2)}, u32[]{:S(2)}) collective-permute-start(bf16[272,1024]{1,0:T(8,128)(2,1)} %collective-permute-done.13.refs_1_), channel_id=1, source_target_pairs={{0,4},{2,6},{4,0},{6,2},{8,12},{10,14},{12,8},{14,10},{16,20},{18,... | collective-permute-start | bytes 1671176 | tf_op jit(solution)/shard_map/ppermute | solution.py:256
  105.1 15.6 %collective-permute-start.16 = (bf16[272,1024]{1,0:T(8,128)(2,1)S(1)}, bf16[272,1024]{1,0:T(8,128)(2,1)}, u32[]{:S(2)}, u32[]{:S(2)}) collective-permute-start(bf16[272,1024]{1,0:T(8,128)(2,1)S(1)} %collective-permute-done.12.refs_0_), channel_id=1, source_target_pairs={{0,2},{2,0},{4,6},{6,4},{8,10},{10,8},{12,14},{14,12},{16,18},{18,... | collective-permute-start | bytes 1671176 | tf_op jit(solution)/shard_map/ppermute | solution.py:259
  107.1 15.0 %collective-permute-start.17 = (bf16[272,1024]{1,0:T(8,128)(2,1)}, bf16[272,1024]{1,0:T(8,128)(2,1)}, u32[]{:S(2)}, u32[]{:S(2)}) collective-permute-start(bf16[272,1024]{1,0:T(8,128)(2,1)} %collective-permute-done.13.refs_1_), channel_id=1, source_target_pairs={{0,2},{2,0},{4,6},{6,4},{8,10},{10,8},{12,14},{14,12},{16,18},{18,... | collective-permute-start | bytes 1671176 | tf_op jit(solution)/shard_map/ppermute | solution.py:259
  107.1 16.6 %collective-permute-start.18 = (bf16[272,1024]{1,0:T(8,128)(2,1)}, bf16[272,1024]{1,0:T(8,128)(2,1)}, u32[]{:S(2)}, u32[]{:S(2)}) collective-permute-start(bf16[272,1024]{1,0:T(8,128)(2,1)} %collective-permute-done.14.refs_2_), channel_id=1, source_target_pairs={{0,2},{2,0},{4,6},{6,4},{8,10},{10,8},{12,14},{14,12},{16,18},{18,... | collective-permute-start | bytes 1671176 | tf_op jit(solution)/shard_map/ppermute | solution.py:259
  119.5 17.5 %collective-permute-start.37 = (bf16[2,2,128,1024]{3,2,1,0:T(8,128)(2,1)}, bf16[2,2,128,1024]{3,2,1,0:T(8,128)(2,1)S(1)}, u32[]{:S(2)}, u32[]{:S(2)}) collective-permute-start(bf16[2,2,128,1024]{3,2,1,0:T(8,128)(2,1)} %get-tuple-element.52), channel_id=1, source_target_pairs={{0,2},{2,0},{4,6},{6,4},{8,10},{10,8},{12,14},{14,12},{16,18},{18,... | collective-permute-start | bytes 3145736 | tf_op jit(solution)/shard_map/ppermute | solution.py:259
  120.1 3.7 %collective-permute-start.19 = (bf16[272,1024]{1,0:T(8,128)(2,1)}, bf16[272,1024]{1,0:T(8,128)(2,1)}, u32[]{:S(2)}, u32[]{:S(2)}) collective-permute-start(bf16[272,1024]{1,0:T(8,128)(2,1)} %collective-permute-done.15.refs_3_), channel_id=1, source_target_pairs={{0,2},{2,0},{4,6},{6,4},{8,10},{10,8},{12,14},{14,12},{16,18},{18,... | collective-permute-start | bytes 1671176 | tf_op jit(solution)/shard_map/ppermute | solution.py:259
  120.7 14.6 %collective-permute-start.41 = (bf16[2,128,1024]{2,1,0:T(8,128)(2,1)S(1)}, bf16[2,128,1024]{2,1,0:T(8,128)(2,1)S(1)}, u32[]{:S(2)}, u32[]{:S(2)}) collective-permute-start(bf16[2,128,1024]{2,1,0:T(8,128)(2,1)S(1)} %fusion.10), channel_id=1, source_target_pairs={{0,1},{1,0},{2,3},{3,2},{4,5},{5,4},{6,7},{7,6},{8,9},{9,8},{10,11... | collective-permute-start | bytes 1572872 | tf_op jit(solution)/shard_map/ppermute | solution.py:262
  122.2 15.9 %collective-permute-start.8 = (bf16[2,128,1024]{2,1,0:T(8,128)(2,1)S(1)}, bf16[2,128,1024]{2,1,0:T(8,128)(2,1)S(1)}, u32[]{:S(2)}, u32[]{:S(2)}) collective-permute-start(bf16[2,128,1024]{2,1,0:T(8,128)(2,1)S(1)} %fusion.7), channel_id=1, source_target_pairs={{0,4},{2,6},{4,0},{6,2},{8,12},{10,14},{12,8},{14,10},{16,20},{18,... | collective-permute-start | bytes 1572872 | tf_op jit(solution)/shard_map/ppermute | solution.py:256
  135.1 21.6 %collective-permute-start.34 = (bf16[2,2,128,1024]{3,2,1,0:T(8,128)(2,1)}, bf16[2,2,128,1024]{3,2,1,0:T(8,128)(2,1)S(1)}, u32[]{:S(2)}, u32[]{:S(2)}) collective-permute-start(bf16[2,2,128,1024]{3,2,1,0:T(8,128)(2,1)} %get-tuple-element.50), channel_id=1, source_target_pairs={{0,2},{2,0},{4,6},{6,4},{8,10},{10,8},{12,14},{14,12},{16,18},{18,... | collective-permute-start | bytes 3145736 | tf_op jit(solution)/shard_map/ppermute | solution.py:259
  135.4 9.2 %collective-permute-start.42 = (bf16[128,1024]{1,0:T(8,128)(2,1)S(1)}, bf16[128,1024]{1,0:T(8,128)(2,1)S(1)}, u32[]{:S(2)}, u32[]{:S(2)}) collective-permute-start(bf16[128,1024]{1,0:T(8,128)(2,1)S(1)} %fusion.25), channel_id=1, source_target_pairs={{0,4},{2,6},{4,0},{6,2},{8,12},{10,14},{12,8},{14,10},{16,20},{18,... | collective-permute-start | bytes 786440 | tf_op jit(solution)/shard_map/ppermute | solution.py:256
  137.5 17.9 %collective-permute-start.38 = (bf16[2,128,1024]{2,1,0:T(8,128)(2,1)S(1)}, bf16[2,128,1024]{2,1,0:T(8,128)(2,1)S(1)}, u32[]{:S(2)}, u32[]{:S(2)}) collective-permute-start(bf16[2,128,1024]{2,1,0:T(8,128)(2,1)S(1)} %fusion.9), channel_id=1, source_target_pairs={{0,4},{2,6},{4,0},{6,2},{8,12},{10,14},{12,8},{14,10},{16,20},{18,... | collective-permute-start | bytes 1572872 | tf_op jit(solution)/shard_map/ppermute | solution.py:256
  138.3 49.7 %collective-permute-start.9 = (bf16[128,1024]{1,0:T(8,128)(2,1)S(1)}, bf16[128,1024]{1,0:T(8,128)(2,1)S(1)}, u32[]{:S(2)}, u32[]{:S(2)}) collective-permute-start(bf16[128,1024]{1,0:T(8,128)(2,1)S(1)} %fusion.22), channel_id=1, source_target_pairs={{0,1},{1,0},{2,3},{3,2},{4,5},{5,4},{6,7},{7,6},{8,9},{9,8},{10,11... | collective-permute-start | bytes 786440 | tf_op jit(solution)/shard_map/ppermute | solution.py:262
  144.7 17.0 %collective-permute-start.43 = (bf16[128,1024]{1,0:T(8,128)(2,1)S(1)}, bf16[128,1024]{1,0:T(8,128)(2,1)S(1)}, u32[]{:S(2)}, u32[]{:S(2)}) collective-permute-start(bf16[128,1024]{1,0:T(8,128)(2,1)S(1)} %fusion.12), channel_id=1, source_target_pairs={{0,8},{2,10},{4,12},{6,14},{8,24},{10,26},{12,28},{14,30},{24,16},... | collective-permute-start | bytes 786440 | tf_op jit(solution)/shard_map/ppermute | solution.py:253
  155.6 9.3 %collective-permute-start.39 = (bf16[128,1024]{1,0:T(8,128)(2,1)S(1)}, bf16[128,1024]{1,0:T(8,128)(2,1)S(1)}, u32[]{:S(2)}, u32[]{:S(2)}) collective-permute-start(bf16[128,1024]{1,0:T(8,128)(2,1)S(1)} %fusion.24), channel_id=1, source_target_pairs={{0,1},{1,0},{2,3},{3,2},{4,5},{5,4},{6,7},{7,6},{8,9},{9,8},{10,11... | collective-permute-start | bytes 786440 | tf_op jit(solution)/shard_map/ppermute | solution.py:262
  157.2 17.5 %collective-permute-start.35 = (bf16[2,128,1024]{2,1,0:T(8,128)(2,1)S(1)}, bf16[2,128,1024]{2,1,0:T(8,128)(2,1)S(1)}, u32[]{:S(2)}, u32[]{:S(2)}) collective-permute-start(bf16[2,128,1024]{2,1,0:T(8,128)(2,1)S(1)} %fusion.8), channel_id=1, source_target_pairs={{0,1},{1,0},{2,3},{3,2},{4,5},{5,4},{6,7},{7,6},{8,9},{9,8},{10,11... | collective-permute-start | bytes 1572872 | tf_op jit(solution)/shard_map/ppermute | solution.py:262
  165.0 14.4 %collective-permute-start.44 = (bf16[128,1024]{1,0:T(8,128)(2,1)S(1)}, bf16[128,1024]{1,0:T(8,128)(2,1)S(1)}, u32[]{:S(2)}, u32[]{:S(2)}) collective-permute-start(bf16[128,1024]{1,0:T(8,128)(2,1)S(1)} %fusion.15), channel_id=1, source_target_pairs={{0,8},{2,10},{4,12},{6,14},{8,24},{10,26},{12,28},{14,30},{24,16},... | collective-permute-start | bytes 786440 | tf_op jit(solution)/shard_map/ppermute | solution.py:253
  174.9 7.0 %collective-permute-start.36 = (bf16[128,1024]{1,0:T(8,128)(2,1)S(1)}, bf16[128,1024]{1,0:T(8,128)(2,1)S(1)}, u32[]{:S(2)}, u32[]{:S(2)}) collective-permute-start(bf16[128,1024]{1,0:T(8,128)(2,1)S(1)} %fusion.23), channel_id=1, source_target_pairs={{0,4},{2,6},{4,0},{6,2},{8,12},{10,14},{12,8},{14,10},{16,20},{18,... | collective-permute-start | bytes 786440 | tf_op jit(solution)/shard_map/ppermute | solution.py:256
  182.1 7.3 %collective-permute-start.45 = (bf16[128,1024]{1,0:T(8,128)(2,1)S(1)}, bf16[128,1024]{1,0:T(8,128)(2,1)S(1)}, u32[]{:S(2)}, u32[]{:S(2)}) collective-permute-start(bf16[128,1024]{1,0:T(8,128)(2,1)S(1)} %fusion.18), channel_id=1, source_target_pairs={{0,8},{2,10},{4,12},{6,14},{8,24},{10,26},{12,28},{14,30},{24,16},... | collective-permute-start | bytes 786440 | tf_op jit(solution)/shard_map/ppermute | solution.py:253
  (25 other events, 294.7 us)

commit v3 on v2

--- a/solution.py
+++ b/solution.py
@@ -104,127 +104,206 @@
     )
 
 
-def pack_kernel(tokens_ref, grads_ref, routes_ref, combine_ref, out_ref):
+def pack_kernel(tokens_ref, grads_ref, routes_ref, combine_ref, out_ref, info_ref, sems):
     rows = tokens_ref.shape[0]
-    out_ref[:rows] = tokens_ref[...]
-    out_ref[rows:2 * rows] = grads_ref[...]
-    top = routes_ref.shape[1]
-    routes = routes_ref[...].astype(jnp.float32).T
-    weights = combine_ref[...].T
+    moves = [
+        pltpu.make_async_copy(tokens_ref, out_ref.at[pl.ds(0, rows)], sems.at[0]),
+        pltpu.make_async_copy(grads_ref, out_ref.at[pl.ds(rows, rows)], sems.at[1]),
+        pltpu.make_async_copy(info_ref, out_ref.at[pl.ds(2 * rows, INFO_ROWS)], sems.at[2]),
+    ]
+    moves[0].start()
+    moves[1].start()
+    top = routes_ref.shape[0]
+    routes = routes_ref[...].astype(jnp.float32)
+    weights = combine_ref[...]
     high = weights.astype(jnp.bfloat16).astype(jnp.float32)
     middle = (weights - high).astype(jnp.bfloat16).astype(jnp.float32)
     low = weights - high - middle
     blank = jnp.zeros((INFO_ROWS - 4, rows), jnp.float32)
+    info_ref[...] = jnp.zeros(info_ref.shape, info_ref.dtype)
     for k in range(top):
         own = slice(k, k + 1)
         column = jnp.concatenate([routes[own], high[own], middle[own], low[own], blank], axis=0)
-        out_ref[2 * rows:, k * rows:(k + 1) * rows] = column.astype(jnp.bfloat16)
+        info_ref[:, k * rows:(k + 1) * rows] = column.astype(jnp.bfloat16)
+    moves[2].start()
+    for move in moves:
+        move.wait()
 
 
 def pack_share(tokens, out_grad, routes, combine):
     rows, width = tokens.shape
+    anywhere = pl.BlockSpec(memory_space=pl.ANY)
+    vmem = pl.BlockSpec(memory_space=pltpu.VMEM)
     return pl.pallas_call(
         pack_kernel,
+        in_specs=[anywhere, anywhere, vmem, vmem],
+        out_specs=anywhere,
         out_shape=jax.ShapeDtypeStruct((2 * rows + INFO_ROWS, width), jnp.bfloat16),
+        scratch_shapes=[pltpu.VMEM((INFO_ROWS, width), jnp.bfloat16), pltpu.SemaphoreType.DMA((3,))],
+        cost_estimate=pl.CostEstimate(flops=0, bytes_accessed=8 * rows * width, transcendentals=0),
         name="pack",
-    )(tokens, out_grad, routes, combine)
-
-
-def expert_kernel(chained, top, rows, place_ref, *refs):
-    shares, refs = refs[:8], refs[8:]
-    wg_ref, wu_ref, wd_ref = refs[:3]
-    refs = refs[3 + (5 if chained else 0):]
-    near_ref, far_ref, rx_ref, rg_ref, act_ref, gt_ref, ut_ref = refs
+    )(tokens, out_grad, routes.T, combine.T)
+
+
+def expert_kernel(index, chained, top, place_ref, *refs):
+    shares, weight_refs = refs[:8], refs[8:11]
+    refs = refs[11 + (5 if chained else 0):]
+    near_ref, far_ref = refs[:2]
+    kept_refs = refs[2:7]
+    x_buf, g_buf, info_buf, wg_ref, wu_ref, wd_ref, rx_ref, rg_ref, act_ref, gt_ref, ut_ref, slot_ref, back_ref = refs[7:20]
+    in_sems, weight_sems, kept_sems, out_sems = refs[20:]
     me = place_ref[0].astype(jnp.float32)
     own_half = place_ref[1]
-    width = shares[0].shape[1]
-    blocks = 4
-    span = blocks * rows
+    core = place_ref[2]
+    other = 1 - core
+    halves, blocks, rows, width = x_buf.shape
     slots = rx_ref.shape[0]
-    named, weights = [], []
-    for b in range(blocks):
-        hits, weight = 0.0, 0.0
-        for k in range(top):
-            info = shares[2 * b][2 * rows:, k * rows:(k + 1) * rows].astype(jnp.float32)
-            hit = info[0:1] == me
-            hits += hit.astype(jnp.float32)
-            weight += jnp.where(hit, info[1:2] + info[2:3] + info[3:4], 0.0)
-        named.append(hits)
-        weights.append(weight)
-    named = jnp.concatenate(named, axis=1)
-    weights = jnp.concatenate(weights, axis=1)
+    pairs = blocks // 2
+    pair_slots = slots // pairs
+
+    spots = [(0, 0), (core, other), (other, core), (1, 1),
+             (0, 2), (other, 2 + core), (core, 2 + other), (1, 3)]
+    info_moves = [
+        pltpu.make_async_copy(
+            shares[s].at[pl.ds(2 * rows, INFO_ROWS)], info_buf.at[b], in_sems.at[16 + b]
+        )
+        for b, s in enumerate((0, 3, 4, 7))
+    ]
+    x_moves = [
+        pltpu.make_async_copy(shares[s].at[pl.ds(0, rows)], x_buf.at[spots[s]], in_sems.at[s])
+        for s in range(8)
+    ]
+    g_moves = [
+        pltpu.make_async_copy(shares[s].at[pl.ds(rows, rows)], g_buf.at[spots[s]], in_sems.at[8 + s])
+        for s in range(8)
+    ]
+    weight_moves = [
+        pltpu.make_async_copy(source, target, weight_sems.at[i])
+        for i, (source, target) in enumerate(zip(weight_refs, (wg_ref, wu_ref, wd_ref)))
+    ]
+    kept_moves = [
+        pltpu.make_async_copy(
+            source, target.at[pl.ds(index * slots, slots)], kept_sems.at[i]
+        )
+        for i, (source, target) in enumerate(zip((rx_ref, rg_ref, act_ref, gt_ref, ut_ref), kept_refs))
+    ]
+    out_moves = [
+        pltpu.make_async_copy(
+            back_ref.at[spots[s]], (near_ref if s < 4 else far_ref).at[s % 4], out_sems.at[s]
+        )
+        for s in range(8)
+    ]
+    for move in info_moves + x_moves + weight_moves[:2] + g_moves + weight_moves[2:]:
+        move.start()
+
+    for move in info_moves:
+        move.wait()
     earlier = (
-        lax.broadcasted_iota(jnp.int32, (span, span), 0)
-        < lax.broadcasted_iota(jnp.int32, (span, span), 1)
+        lax.broadcasted_iota(jnp.int32, (2 * rows, 2 * rows), 0)
+        < lax.broadcasted_iota(jnp.int32, (2 * rows, 2 * rows), 1)
     ).astype(jnp.bfloat16)
-    counted = jnp.dot(
-        jnp.broadcast_to(named, (16, span)).astype(jnp.bfloat16),
-        earlier,
-        preferred_element_type=jnp.float32,
-    )[:1]
-    slot_of = jnp.where(named > 0.0, counted.astype(jnp.int32), -1)
-    chosen = slot_of == lax.broadcasted_iota(jnp.int32, (slots, span), 0)
-    pick = chosen.astype(jnp.bfloat16)
-    scale = jnp.sum(jnp.where(chosen, weights, 0.0), axis=1, keepdims=True)
-
-    gate = up = hidden_grad = 0.0
-    for h in range(2):
-        start = pl.multiple_of((own_half if h == 0 else 1 - own_half) * width, width)
-        cols = pl.ds(start, width)
-        x = jnp.concatenate([shares[2 * b + h][:rows] for b in range(blocks)], axis=0)
-        rx = jnp.dot(pick, x, preferred_element_type=jnp.float32).astype(jnp.bfloat16)
-        rx_ref[:, cols] = rx
-        gate += lax.dot_general(rx, wg_ref[:, cols], CONTRACT_LAST, preferred_element_type=jnp.float32)
-        up += lax.dot_general(rx, wu_ref[:, cols], CONTRACT_LAST, preferred_element_type=jnp.float32)
-        g = jnp.concatenate([shares[2 * b + h][rows:2 * rows] for b in range(blocks)], axis=0)
-        rg = (scale * jnp.dot(pick, g, preferred_element_type=jnp.float32)).astype(jnp.bfloat16)
-        rg_ref[:, cols] = rg
-        hidden_grad += lax.dot_general(rg, wd_ref[:, cols], CONTRACT_LAST, preferred_element_type=jnp.float32)
-
+    picks, scales = [], []
+    for p in range(pairs):
+        named, weights = [], []
+        for b in (2 * p, 2 * p + 1):
+            hits, weight = 0.0, 0.0
+            for k in range(top):
+                info = info_buf[b, :, k * rows:(k + 1) * rows].astype(jnp.float32)
+                hit = info[0:1] == me
+                hits += hit.astype(jnp.float32)
+                weight += jnp.where(hit, info[1:2] + info[2:3] + info[3:4], 0.0)
+            named.append(hits)
+            weights.append(weight)
+        named = jnp.concatenate(named, axis=1)
+        weights = jnp.concatenate(weights, axis=1)
+        counted = jnp.dot(
+            jnp.broadcast_to(named, (16, 2 * rows)).astype(jnp.bfloat16),
+            earlier,
+            preferred_element_type=jnp.float32,
+        )[:1]
+        slot_of = jnp.where(named > 0.0, counted.astype(jnp.int32), -1)
+        chosen = slot_of == lax.broadcasted_iota(jnp.int32, (pair_slots, 2 * rows), 0)
+        picks.append(chosen.astype(jnp.bfloat16))
+        scales.append(jnp.sum(jnp.where(chosen, weights, 0.0), axis=1, keepdims=True))
+
+    def columns(h):
+        return pl.ds(pl.multiple_of((own_half if h == 0 else 1 - own_half) * width, width), width)
+
+    def slot_rows(p):
+        return slice(p * pair_slots, (p + 1) * pair_slots)
+
+    for move in x_moves:
+        move.wait()
+    for h in range(halves):
+        for p in range(pairs):
+            x = x_buf[h, 2 * p:2 * p + 2].reshape(2 * rows, width)
+            picked = jnp.dot(picks[p], x, preferred_element_type=jnp.float32)
+            rx_ref[slot_rows(p), columns(h)] = picked.astype(jnp.bfloat16)
+    kept_moves[0].start()
+    weight_moves[0].wait()
+    gate = lax.dot_general(rx_ref[...], wg_ref[...], CONTRACT_LAST, preferred_element_type=jnp.float32)
+    weight_moves[1].wait()
+    up = lax.dot_general(rx_ref[...], wu_ref[...], CONTRACT_LAST, preferred_element_type=jnp.float32)
     sigma = 1.0 / (1.0 + jnp.exp(-gate))
     silu = gate * sigma
     act_ref[...] = (silu * up).astype(jnp.bfloat16)
-    gate_term = (hidden_grad * up * sigma * (1.0 + gate * (1.0 - sigma))).astype(jnp.bfloat16)
-    up_term = (hidden_grad * silu).astype(jnp.bfloat16)
-    gt_ref[...] = gate_term
-    ut_ref[...] = up_term
-    for h in range(2):
-        start = pl.multiple_of((own_half if h == 0 else 1 - own_half) * width, width)
-        cols = pl.ds(start, width)
-        slot = jnp.dot(gate_term, wg_ref[:, cols], preferred_element_type=jnp.float32)
-        slot += jnp.dot(up_term, wu_ref[:, cols], preferred_element_type=jnp.float32)
-        back = lax.dot_general(
-            pick, slot.astype(jnp.bfloat16), CONTRACT_FIRST, preferred_element_type=jnp.float32
-        ).astype(jnp.bfloat16)
-        for b in range(blocks):
-            target = near_ref if b < 2 else far_ref
-            target[b % 2, h] = back[b * rows:(b + 1) * rows]
+    kept_moves[2].start()
+
+    for move in g_moves:
+        move.wait()
+    for h in range(halves):
+        for p in range(pairs):
+            g = g_buf[h, 2 * p:2 * p + 2].reshape(2 * rows, width)
+            picked = jnp.dot(picks[p], g, preferred_element_type=jnp.float32)
+            rg_ref[slot_rows(p), columns(h)] = (scales[p] * picked).astype(jnp.bfloat16)
+    kept_moves[1].start()
+    weight_moves[2].wait()
+    hidden_grad = lax.dot_general(rg_ref[...], wd_ref[...], CONTRACT_LAST, preferred_element_type=jnp.float32)
+    gt_ref[...] = (hidden_grad * up * sigma * (1.0 + gate * (1.0 - sigma))).astype(jnp.bfloat16)
+    ut_ref[...] = (hidden_grad * silu).astype(jnp.bfloat16)
+    kept_moves[3].start()
+    kept_moves[4].start()
+
+    slot = jnp.dot(gt_ref[...], wg_ref[...], preferred_element_type=jnp.float32)
+    slot += jnp.dot(ut_ref[...], wu_ref[...], preferred_element_type=jnp.float32)
+    slot_ref[...] = slot.astype(jnp.bfloat16)
+    for p in reversed(range(pairs)):
+        for h in range(halves):
+            back = lax.dot_general(
+                picks[p], slot_ref[slot_rows(p), columns(h)], CONTRACT_FIRST,
+                preferred_element_type=jnp.float32,
+            )
+            back_ref[h, 2 * p:2 * p + 2] = back.astype(jnp.bfloat16).reshape(2, rows, width)
+        for s in range(4 * p, 4 * p + 4):
+            out_moves[s].start()
+    for move in kept_moves + out_moves:
+        move.wait()
 
 
 def run_experts(index, chunks, place, shares, weights, kept, top, rows, slots):
     width = shares[0].shape[1]
     hidden, features = weights[0].shape
-    vmem = pl.BlockSpec(memory_space=pltpu.VMEM)
-    part = jax.ShapeDtypeStruct((2, 2, rows, width), jnp.bfloat16)
+    anywhere = pl.BlockSpec(memory_space=pl.ANY)
+    part = jax.ShapeDtypeStruct((4, rows, width), jnp.bfloat16)
     wide = jax.ShapeDtypeStruct((chunks * slots, features), jnp.bfloat16)
     narrow = jax.ShapeDtypeStruct((chunks * slots, hidden), jnp.bfloat16)
-    wide_block = pl.BlockSpec((slots, features), lambda i: (index, 0))
-    narrow_block = pl.BlockSpec((slots, hidden), lambda i: (index, 0))
-    part_block = pl.BlockSpec(part.shape, lambda i: (0, 0, 0, 0))
+    held = pltpu.VMEM((2, 4, rows, width), jnp.bfloat16)
     first_kept = 1 + len(shares) + 3
     return pl.pallas_call(
-        functools.partial(expert_kernel, kept is not None, top, rows),
-        grid=(1,),
-        in_specs=[pl.BlockSpec(memory_space=pltpu.SMEM)]
-        + [pl.BlockSpec(s.shape, lambda i: (0, 0)) for s in shares]
-        + [pl.BlockSpec((hidden, features), lambda i: (0, 0))] * 3
-        + [pl.BlockSpec(memory_space=pl.ANY)] * (0 if kept is None else 5),
-        out_specs=[part_block] * 2 + [wide_block] * 2 + [narrow_block] * 3,
+        functools.partial(expert_kernel, index, kept is not None, top),
+        in_specs=[pl.BlockSpec(memory_space=pltpu.SMEM)] + [anywhere] * (11 if kept is None else 16),
+        out_specs=[anywhere] * 7,
         out_shape=[part, part, wide, wide, narrow, narrow, narrow],
+        scratch_shapes=[held, held, pltpu.VMEM((4, INFO_ROWS, width), jnp.bfloat16)]
+        + [pltpu.VMEM((hidden, features), jnp.bfloat16)] * 3
+        + [pltpu.VMEM((slots, features), jnp.bfloat16)] * 2
+        + [pltpu.VMEM((slots, hidden), jnp.bfloat16)] * 3
+        + [pltpu.VMEM((slots, features), jnp.bfloat16), held]
+        + [pltpu.SemaphoreType.DMA((n,)) for n in (20, 3, 5, 8)],
         input_output_aliases={} if kept is None else {first_kept + i: 2 + i for i in range(5)},
-        compiler_params=pltpu.CompilerParams(vmem_limit_bytes=56 * 1024 * 1024),
+        compiler_params=pltpu.CompilerParams(vmem_limit_bytes=32 * 1024 * 1024),
         cost_estimate=pl.CostEstimate(
-            flops=2 * slots * features * (hidden * 5 + 4 * rows * 3),
+            flops=2 * slots * features * (hidden * 5 + 2 * rows * 3),
             bytes_accessed=2 * (8 * shares[0].size + 3 * hidden * features + slots * (2 * features + 3 * hidden)),
             transcendentals=slots * hidden,
         ),
@@ -243,46 +322,49 @@
     top = routes.shape[1]
     per_pair = rows * top // experts
     capacity = per_pair + per_pair // 8
-    slots = -(-4 * capacity // 16) * 16
+    slots = 2 * (-(-2 * capacity // 16) * 16)
     order = ring_order(chunks)
-    ahead = [
-        (order[i] * 4 + r, order[(i + 1) % chunks] * 4 + r) for i in range(chunks) for r in range(4)
-    ]
+    after = {order[i]: order[(i + 1) % chunks] for i in range(chunks)}
+    devices = [(e, h) for e in range(experts) for h in range(2)]
+
+    def permute(value, target):
+        pairs = [(e * 2 + h, target(e, h)[0] * 2 + target(e, h)[1]) for e, h in devices]
+        return lax.ppermute(value, ("expert", "etp"), pairs)
 
     def to_ring(value):
-        return lax.ppermute(value, "expert", ahead)
-
-    def to_side(value):
-        return lax.ppermute(value, "expert", [(e, e ^ 2) for e in range(experts)])
+        return permute(value, lambda e, h: (after[e // 4] * 4 + e % 4, h))
 
     def to_core(value):
-        return lax.ppermute(value, "expert", [(e, e ^ 1) for e in range(experts)])
-
-    def to_half(value):
-        return lax.ppermute(value, "etp", [(0, 1), (1, 0)])
-
-    place = jnp.stack([lax.axis_index("expert"), lax.axis_index("etp")]).astype(jnp.int32)
+        return permute(value, lambda e, h: (e ^ 1, h))
+
+    def to_first(value):
+        return permute(value, lambda e, h: (e, h ^ 1) if e % 2 else (e ^ 2, h))
+
+    def to_second(value):
+        return permute(value, lambda e, h: (e ^ 2, h) if e % 2 else (e, h ^ 1))
+
+    me = lax.axis_index("expert")
+    place = jnp.stack([me, lax.axis_index("etp"), me % 2]).astype(jnp.int32)
     weights = (w_gate[0], w_up[0], w_down[0])
     share = pack_share(tokens, out_grad, routes, combine)
     kept = None
     running = None
     for c in range(chunks):
-        if c > 0:
-            share = to_ring(share)
-        across, aside = to_half(share), to_side(share)
-        both = to_half(aside) if c % 2 == 0 else to_side(across)
-        near = [share, across, aside, both]
+        first, second = to_first(share), to_second(share)
+        if c + 1 < chunks:
+            following = to_ring(share)
+            first, second, following = lax.optimization_barrier((first, second, following))
+        else:
+            following = None
+        near = [share, first, second, to_second(first)]
         far = [to_core(s) for s in near]
+        share = following
         near_part, far_part, *kept = run_experts(
             c, chunks, place, near + far, weights, kept, top, rows, slots
         )
         mine = near_part.astype(jnp.float32) + to_core(far_part).astype(jnp.float32)
-        if c % 2 == 0:
-            mine = mine[0] + to_side(mine[1].astype(jnp.bfloat16)).astype(jnp.float32)
-            mine = mine[0] + to_half(mine[1].astype(jnp.bfloat16)).astype(jnp.float32)
-        else:
-            mine = mine[:, 0] + to_half(mine[:, 1].astype(jnp.bfloat16)).astype(jnp.float32)
-            mine = mine[0] + to_side(mine[1].astype(jnp.bfloat16)).astype(jnp.float32)
+        mine = mine[:2] + to_second(mine[2:].astype(jnp.bfloat16)).astype(jnp.float32)
+        mine = mine[0] + to_first(mine[1].astype(jnp.bfloat16)).astype(jnp.float32)
         if c == 0:
             own = mine
         else:

time: 190 us -> 182 us (0.958)
  waiting for transfers between devices: 77.6 us -> 64.4 us
  starting transfers between devices: 43.7 us -> 32.3 us
  local copies, waits for them, and re-layouts: 6.49 us -> 15 us
  Pallas kernels: 47.3 us -> 54.6 us
    ppermute x46, waiting for transfers between devices: 77.6 us -> 64.4 us  [permute(): return lax.ppermute(value, ('expert', 'etp'), pairs)]
    ppermute x46, starting transfers between devices: 43.7 us -> 32.3 us  [permute(): return lax.ppermute(value, ('expert', 'etp'), pairs)]
    unnamed x56 -> x34, local copies, waits for them, and re-layouts: 4.7 us -> 14.6 us
    pallas_call x5, Pallas kernels: 47.3 us -> 54.6 us  [the longest x4 36.9 us: run_experts(): pl.pallas_call(functools.partial(expert_kernel, index, kept is not None,...]
  transfers between devices with their start and end apart: 46 -> 46, of which waited for: 14 -> 15; matrix products, arithmetic and copies ran while one was open for 8% -> 7% of each run, Pallas kernels for 24% -> 20%
where the time goes in v3:
time: 182 us; the launch traced here: 181 us
  waiting for transfers between devices  64.4 us (35%)
  Pallas kernels  54.6 us (30%)
  starting transfers between devices  32.3 us (18%)
  local copies, waits for them, and re-layouts  15 us (8%)
  matrix products  10.3 us (6%)
  other arithmetic  3.39 us (2%)
    ppermute x46, waiting for transfers between devices, permute(): return lax.ppermute(value, ('expert', 'etp'), pairs)  64.4 us
    pallas_call x4, Pallas kernels, run_experts(): pl.pallas_call(functools.partial(expert_kernel, index, kept is not None,...  36.9 us
    ppermute x46, starting transfers between devices, permute(): return lax.ppermute(value, ('expert', 'etp'), pairs)  32.3 us
    pallas_call x1, Pallas kernels, pack_share(): pl.pallas_call(pack_kernel, in_specs=[anywhere, anywhere, vmem, vmem], ou...  17.7 us
    unnamed x34, local copies, waits for them, and re-layouts  14.6 us
  transfers between devices with their start and end apart: 46, of which 15 were waited for; matrix products, arithmetic and copies ran while one was open for 7% of the time, Pallas kernels for 20%

profile of v3, /device:TPU:0, one launch (start us, length us, event | category | flops | bytes accessed | tf_op | source)
XLA Modules:
  0.0 181.0 jit_solution(13364703256997317847)
XLA Ops:
  0.6 17.7 %pack.1.refs_0_ = bf16[272,1024]{1,0:T(8,128)(2,1)} custom-call(bf16[128,1024]{1,0:T(8,128)(2,1)} %tokens_ref.1, bf16[128,1024]{1,0:T(8,128)(2,1)} %grads_ref.1, s32[8,128]{1,0:T(8,128)} %bitcast.72, f32[8,128]{1,0:T(8,128)} %bitcast.73), custom_call_target="tpu_custom_call" | custom-call | bytes 1048576 | tf_op jit(solution)/shard_map/pack/pallas_call | solution.py:137
  18.4 3.0 %collective-permute-start = (bf16[272,1024]{1,0:T(8,128)(2,1)}, bf16[272,1024]{1,0:T(8,128)(2,1)S(1)}, u32[]{:S(2)}, u32[]{:S(2)}) collective-permute-start(bf16[272,1024]{1,0:T(8,128)(2,1)} %pack.1.refs_0_), channel_id=1, source_target_pairs={{0,4},{1,5},{2,3},{3,2},{4,0},{5,1},{6,7},{7,6},{8,12},{9,13},{10,... | collective-permute-start | bytes 1671176 | tf_op jit(solution)/shard_map/ppermute | solution.py:332
  21.4 1.5 collective-permute-start.1
  22.9 1.6 collective-permute-start.2
  24.5 10.2 %collective-permute-done.refs_1_ = bf16[272,1024]{1,0:T(8,128)(2,1)S(1)} collective-permute-done((bf16[272,1024]{1,0:T(8,128)(2,1)}, bf16[272,1024]{1,0:T(8,128)(2,1)S(1)}, u32[]{:S(2)}, u32[]{:S(2)}) %collective-permute-start) | collective-permute-done | bytes 557088 | tf_op jit(solution)/shard_map/ppermute | solution.py:332
  34.6 3.2 %collective-permute-done.2.refs_0_ = bf16[272,1024]{1,0:T(8,128)(2,1)S(1)} collective-permute-done((bf16[272,1024]{1,0:T(8,128)(2,1)}, bf16[272,1024]{1,0:T(8,128)(2,1)S(1)}, u32[]{:S(2)}, u32[]{:S(2)}) %collective-permute-start.2) | collective-permute-done | bytes 557088 | tf_op jit(solution)/shard_map/ppermute | solution.py:332
  38.8 0.9 collective-permute-start.13
  39.7 1.5 collective-permute-start.3
  41.2 12.2 %collective-permute-done.11.refs_1_ = bf16[272,1024]{1,0:T(8,128)(2,1)S(1)} collective-permute-done((bf16[272,1024]{1,0:T(8,128)(2,1)S(1)}, bf16[272,1024]{1,0:T(8,128)(2,1)S(1)}, u32[]{:S(2)}, u32[]{:S(2)}) %collective-permute-start.11) | collective-permute-done | bytes 557088 | tf_op jit(solution)/shard_map/ppermute | solution.py:332
  57.2 1.6 collective-permute-start.15
  59.7 0.9 collective-permute-start.16
  60.5 0.8 copy-done.13
  61.3 9.7 %collective-permute-done.29.refs_3_ = bf16[272,1024]{1,0:T(8,128)(2,1)} collective-permute-done((bf16[272,1024]{1,0:T(8,128)(2,1)S(1)}, bf16[272,1024]{1,0:T(8,128)(2,1)}, u32[]{:S(2)}, u32[]{:S(2)}) %collective-permute-start.29) | collective-permute-done | bytes 557088 | tf_op jit(solution)/shard_map/ppermute | solution.py:332
  71.0 1.4 collective-permute-done.14.refs_1_
  72.4 4.6 %collective-permute-done.15.refs_2_ = bf16[272,1024]{1,0:T(8,128)(2,1)S(1)} collective-permute-done((bf16[272,1024]{1,0:T(8,128)(2,1)S(1)}, bf16[272,1024]{1,0:T(8,128)(2,1)S(1)}, u32[]{:S(2)}, u32[]{:S(2)}) %collective-permute-start.15) | collective-permute-done | bytes 557088 | tf_op jit(solution)/shard_map/ppermute | solution.py:332
  78.1 1.4 copy-done
  79.6 1.4 copy-done.2
  81.0 1.4 copy-done.3
  82.4 1.1 copy-done.4
  83.4 1.1 copy-done.6
  84.5 1.1 copy-done.8
  85.5 1.1 copy-done.10
  86.6 1.1 copy-done.12
  87.6 1.1 copy-done.14
  88.7 9.4 %experts.4 = (bf16[4,128,1024]{2,1,0:T(8,128)(2,1)S(1)}, bf16[4,128,1024]{2,1,0:T(8,128)(2,1)}, bf16[1152,2048]{1,0:T(8,128)(2,1)S(1)}, bf16[1152,2048]{1,0:T(8,...) custom-call(s32[3]{0:T(128)S(1)} %pad_add_fusion.place_ref, ...), custom_call_target="tpu_custom_call" | custom-call | flops 3170893824 | bytes 12197888 | tf_op jit(solution)/shard_map/experts/pallas_call | solution.py:292
  98.7 1.3 collective-permute-start.17
  100.0 9.4 %experts.5 = (bf16[4,128,1024]{2,1,0:T(8,128)(2,1)S(1)}, bf16[4,128,1024]{2,1,0:T(8,128)(2,1)S(1)}, bf16[1152,2048]{1,0:T(8,128)(2,1)S(1)}, bf16[1152,2048]{1,0:...) custom-call(s32[3]{0:T(128)S(1)} %pad_add_fusion.place_ref, ...), custom_call_target="tpu_custom_call", output_to_operand_aliasing={{2}: (12, {}), {3}: (13, {}), {4}: (14, {}), {5}: (15, {}),... | custom-call | flops 3170893824 | bytes 12197888 | tf_op jit(solution)/shard_map/experts/pallas_call | solution.py:292
  110.9 1.2 collective-permute-start.19
  112.1 1.6 collective-permute-done.28.refs_7_
  113.9 9.1 %experts.6 = (bf16[4,128,1024]{2,1,0:T(8,128)(2,1)S(1)}, bf16[4,128,1024]{2,1,0:T(8,128)(2,1)S(1)}, bf16[1152,2048]{1,0:T(8,128)(2,1)S(1)}, bf16[1152,2048]{1,0:...) custom-call(s32[3]{0:T(128)S(1)} %pad_add_fusion.place_ref, ...), custom_call_target="tpu_custom_call", output_to_operand_aliasing={{2}: (12, {}), {3}: (13, {}), {4}: (14, {}), {5}: (15, {}),... | custom-call | flops 3170893824 | bytes 12197888 | tf_op jit(solution)/shard_map/experts/pallas_call | solution.py:292
  123.5 2.1 %collective-permute-done.19.refs_3_ = bf16[272,1024]{1,0:T(8,128)(2,1)S(1)} collective-permute-done((bf16[272,1024]{1,0:T(8,128)(2,1)S(1)}, bf16[272,1024]{1,0:T(8,128)(2,1)S(1)}, u32[]{:S(2)}, u32[]{:S(2)}) %collective-permute-start.19) | collective-permute-done | bytes 557088 | tf_op jit(solution)/shard_map/ppermute | solution.py:332
  126.7 0.9 collective-permute-start.41
  128.1 1.3 collective-permute-start.9
  129.4 8.9 %experts.7 = (bf16[4,128,1024]{2,1,0:T(8,128)(2,1)S(1)}, bf16[4,128,1024]{2,1,0:T(8,128)(2,1)S(1)}, bf16[1152,2048]{1,0:T(8,128)(2,1)S(1)}, bf16[1152,2048]{1,0:...) custom-call(s32[3]{0:T(128)S(1)} %pad_add_fusion.place_ref, ...), custom_call_target="tpu_custom_call", output_to_operand_aliasing={{2}: (12, {}), {3}: (13, {}), {4}: (14, {}), {5}: (15, {}),... | custom-call | flops 3170893824 | bytes 12197888 | tf_op jit(solution)/shard_map/experts/pallas_call | solution.py:292
  139.9 1.6 collective-permute-start.38
  142.6 4.7 %collective-permute-done.42 = bf16[128,1024]{1,0:T(8,128)(2,1)S(1)} collective-permute-done((bf16[128,1024]{1,0:T(8,128)(2,1)S(1)}, bf16[128,1024]{1,0:T(8,128)(2,1)S(1)}, u32[]{:S(2)}, u32[]{:S(2)}) %collective-permute-start.42) | collective-permute-done | bytes 262176 | tf_op jit(solution)/shard_map/ppermute | solution.py:332
  147.4 1.2 collective-permute-start.43
  148.6 4.4 %collective-permute-done.38 = bf16[2,128,1024]{2,1,0:T(8,128)(2,1)S(1)} collective-permute-done((bf16[2,128,1024]{2,1,0:T(8,128)(2,1)S(1)}, bf16[2,128,1024]{2,1,0:T(8,128)(2,1)S(1)}, u32[]{:S(2)}, u32[]{:S(2)}) %collective-permute-start.38) | collective-permute-done | bytes 524320 | tf_op jit(solution)/shard_map/ppermute | solution.py:332
  154.5 1.6 collective-permute-start.35
  156.1 3.4 %fusion.1 = bf16[1,384,2048]{2,1,0:T(8,128)(2,1)} fusion(bf16[1152,384]{1,0:T(8,128)(2,1)S(1)} %get-tuple-element.75, bf16[1152,2048]{1,0:T(8,128)(2,1)S(1)} %get-tuple-element.74), kind=kOutput, calls=%fused_computation.4 | convolution fusion | flops 1812725760 | bytes 7176192 | tf_op jit(solution)/shard_map/dot_general | solution.py:377
  159.6 2.3 %collective-permute-done.39 = bf16[128,1024]{1,0:T(8,128)(2,1)S(1)} collective-permute-done((bf16[128,1024]{1,0:T(8,128)(2,1)S(1)}, bf16[128,1024]{1,0:T(8,128)(2,1)S(1)}, u32[]{:S(2)}, u32[]{:S(2)}) %collective-permute-start.39) | collective-permute-done | bytes 262176 | tf_op jit(solution)/shard_map/ppermute | solution.py:332
  162.0 0.9 collective-permute-start.44
  162.9 2.0 %collective-permute-done.35 = bf16[2,128,1024]{2,1,0:T(8,128)(2,1)S(1)} collective-permute-done((bf16[2,128,1024]{2,1,0:T(8,128)(2,1)S(1)}, bf16[2,128,1024]{2,1,0:T(8,128)(2,1)S(1)}, u32[]{:S(2)}, u32[]{:S(2)}) %collective-permute-start.35) | collective-permute-done | bytes 524320 | tf_op jit(solution)/shard_map/ppermute | solution.py:332
  166.0 3.4 %fusion = bf16[1,384,2048]{2,1,0:T(8,128)(2,1)} fusion(bf16[1152,384]{1,0:T(8,128)(2,1)S(1)} %get-tuple-element.73, bf16[1152,2048]{1,0:T(8,128)(2,1)S(1)} %get-tuple-element.74), kind=kOutput, calls=%fused_computation.3 | convolution fusion | flops 1812725760 | bytes 7176192 | tf_op jit(solution)/shard_map/dot_general | solution.py:376
  169.8 1.8 %collective-permute-done.36 = bf16[128,1024]{1,0:T(8,128)(2,1)S(1)} collective-permute-done((bf16[128,1024]{1,0:T(8,128)(2,1)S(1)}, bf16[128,1024]{1,0:T(8,128)(2,1)S(1)}, u32[]{:S(2)}, u32[]{:S(2)}) %collective-permute-start.36) | collective-permute-done | bytes 262176 | tf_op jit(solution)/shard_map/ppermute | solution.py:332
  171.7 1.3 collective-permute-start.45
  173.0 3.4 %fusion.2 = bf16[1,384,2048]{2,1,0:T(8,128)(2,1)} fusion(bf16[1152,384]{1,0:T(8,128)(2,1)S(1)} %get-tuple-element.76, bf16[1152,2048]{1,0:T(8,128)(2,1)S(1)} %bitcast.71), kind=kOutput, calls=%fused_computation.5 | convolution fusion | flops 1812725760 | bytes 7176192 | tf_op jit(solution)/shard_map/dot_general | solution.py:375
  176.4 3.8 %collective-permute-done.45 = bf16[128,1024]{1,0:T(8,128)(2,1)S(1)} collective-permute-done((bf16[128,1024]{1,0:T(8,128)(2,1)S(1)}, bf16[128,1024]{1,0:T(8,128)(2,1)S(1)}, u32[]{:S(2)}, u32[]{:S(2)}) %collective-permute-start.45) | collective-permute-done | bytes 262176 | tf_op jit(solution)/shard_map/ppermute | solution.py:332
  (108 shorter events, 17.5 us)
Async XLA Ops:
  18.4 16.3 %collective-permute-start = (bf16[272,1024]{1,0:T(8,128)(2,1)}, bf16[272,1024]{1,0:T(8,128)(2,1)S(1)}, u32[]{:S(2)}, u32[]{:S(2)}) collective-permute-start(bf16[272,1024]{1,0:T(8,128)(2,1)} %pack.1.refs_0_), channel_id=1, source_target_pairs={{0,4},{1,5},{2,3},{3,2},{4,0},{5,1},{6,7},{7,6},{8,12},{9,13},{10,... | collective-permute-start | bytes 1671176 | tf_op jit(solution)/shard_map/ppermute | solution.py:332
  21.4 13.3 %collective-permute-start.1 = (bf16[272,1024]{1,0:T(8,128)(2,1)}, bf16[272,1024]{1,0:T(8,128)(2,1)S(1)}, u32[]{:S(2)}, u32[]{:S(2)}) collective-permute-start(bf16[272,1024]{1,0:T(8,128)(2,1)} %pack.1.refs_0_), channel_id=1, source_target_pairs={{0,1},{1,0},{2,6},{3,7},{4,5},{5,4},{6,2},{7,3},{8,9},{9,8},{10,14... | collective-permute-start | bytes 1671176 | tf_op jit(solution)/shard_map/ppermute | solution.py:332
  22.9 14.9 %collective-permute-start.2 = (bf16[272,1024]{1,0:T(8,128)(2,1)}, bf16[272,1024]{1,0:T(8,128)(2,1)S(1)}, u32[]{:S(2)}, u32[]{:S(2)}) collective-permute-start(bf16[272,1024]{1,0:T(8,128)(2,1)} %pack.1.refs_0_), channel_id=1, source_target_pairs={{0,8},{1,9},{2,10},{3,11},{4,12},{5,13},{6,14},{7,15},{8,24},{9,25... | collective-permute-start | bytes 1671176 | tf_op jit(solution)/shard_map/ppermute | solution.py:332
  37.8 15.6 %collective-permute-start.11 = (bf16[272,1024]{1,0:T(8,128)(2,1)S(1)}, bf16[272,1024]{1,0:T(8,128)(2,1)S(1)}, u32[]{:S(2)}, u32[]{:S(2)}) collective-permute-start(bf16[272,1024]{1,0:T(8,128)(2,1)S(1)} %collective-permute-done.2.refs_0_), channel_id=1, source_target_pairs={{0,4},{1,5},{2,3},{3,2},{4,0},{5,1},{6,7},{7,6},{8,12},{9,13},{10,... | collective-permute-start | bytes 1671176 | tf_op jit(solution)/shard_map/ppermute | solution.py:332
  38.3 15.9 %collective-permute-start.12 = (bf16[272,1024]{1,0:T(8,128)(2,1)S(1)}, bf16[272,1024]{1,0:T(8,128)(2,1)}, u32[]{:S(2)}, u32[]{:S(2)}) collective-permute-start(bf16[272,1024]{1,0:T(8,128)(2,1)S(1)} %collective-permute-done.2.refs_0_), channel_id=1, source_target_pairs={{0,1},{1,0},{2,6},{3,7},{4,5},{5,4},{6,2},{7,3},{8,9},{9,8},{10,14... | collective-permute-start | bytes 1671176 | tf_op jit(solution)/shard_map/ppermute | solution.py:332
  38.8 16.7 %collective-permute-start.13 = (bf16[272,1024]{1,0:T(8,128)(2,1)S(1)}, bf16[272,1024]{1,0:T(8,128)(2,1)S(1)}, u32[]{:S(2)}, u32[]{:S(2)}) collective-permute-start(bf16[272,1024]{1,0:T(8,128)(2,1)S(1)} %collective-permute-done.2.refs_0_), channel_id=1, source_target_pairs={{0,8},{1,9},{2,10},{3,11},{4,12},{5,13},{6,14},{7,15},{8,24},{9,25... | collective-permute-start | bytes 1671176 | tf_op jit(solution)/shard_map/ppermute | solution.py:332
  39.7 16.3 %collective-permute-start.4 = (bf16[272,1024]{1,0:T(8,128)(2,1)}, bf16[272,1024]{1,0:T(8,128)(2,1)S(1)}, u32[]{:S(2)}, u32[]{:S(2)}) collective-permute-start(bf16[272,1024]{1,0:T(8,128)(2,1)} %pack.1.refs_0_), channel_id=1, source_target_pairs={{0,2},{1,3},{2,0},{3,1},{4,6},{5,7},{6,4},{7,5},{8,10},{9,11},{10,... | collective-permute-start | bytes 1671176 | tf_op jit(solution)/shard_map/ppermute | solution.py:332
  39.7 17.5 %collective-permute-start.3 = (bf16[272,1024]{1,0:T(8,128)(2,1)S(1)}, bf16[272,1024]{1,0:T(8,128)(2,1)}, u32[]{:S(2)}, u32[]{:S(2)}) collective-permute-start(bf16[272,1024]{1,0:T(8,128)(2,1)S(1)} %collective-permute-done.refs_1_), channel_id=1, source_target_pairs={{0,1},{1,0},{2,6},{3,7},{4,5},{5,4},{6,2},{7,3},{8,9},{9,8},{10,14... | collective-permute-start | bytes 1671176 | tf_op jit(solution)/shard_map/ppermute | solution.py:332
  53.4 5.5 %collective-permute-start.5 = (bf16[272,1024]{1,0:T(8,128)(2,1)S(1)}, bf16[272,1024]{1,0:T(8,128)(2,1)S(1)}, u32[]{:S(2)}, u32[]{:S(2)}) collective-permute-start(bf16[272,1024]{1,0:T(8,128)(2,1)S(1)} %collective-permute-done.refs_1_), channel_id=1, source_target_pairs={{0,2},{1,3},{2,0},{3,1},{4,6},{5,7},{6,4},{7,5},{8,10},{9,11},{10,... | collective-permute-start | bytes 1671176 | tf_op jit(solution)/shard_map/ppermute | solution.py:332
  54.2 6.3 %collective-permute-start.6 = (bf16[272,1024]{1,0:T(8,128)(2,1)S(1)}, bf16[272,1024]{1,0:T(8,128)(2,1)S(1)}, u32[]{:S(2)}, u32[]{:S(2)}) collective-permute-start(bf16[272,1024]{1,0:T(8,128)(2,1)S(1)} %collective-permute-done.1.refs_2_), channel_id=1, source_target_pairs={{0,2},{1,3},{2,0},{3,1},{4,6},{5,7},{6,4},{7,5},{8,10},{9,11},{10,... | collective-permute-start | bytes 1671176 | tf_op jit(solution)/shard_map/ppermute | solution.py:332
  55.5 15.5 %collective-permute-start.29 = (bf16[272,1024]{1,0:T(8,128)(2,1)S(1)}, bf16[272,1024]{1,0:T(8,128)(2,1)}, u32[]{:S(2)}, u32[]{:S(2)}) collective-permute-start(bf16[272,1024]{1,0:T(8,128)(2,1)S(1)} %collective-permute-done.11.refs_1_), channel_id=1, source_target_pairs={{0,1},{1,0},{2,6},{3,7},{4,5},{5,4},{6,2},{7,3},{8,9},{9,8},{10,14... | collective-permute-start | bytes 1671176 | tf_op jit(solution)/shard_map/ppermute | solution.py:332
  56.8 15.6 %collective-permute-start.14 = (bf16[272,1024]{1,0:T(8,128)(2,1)S(1)}, bf16[272,1024]{1,0:T(8,128)(2,1)S(1)}, u32[]{:S(2)}, u32[]{:S(2)}) collective-permute-start(bf16[272,1024]{1,0:T(8,128)(2,1)S(1)} %collective-permute-done.13.refs_0_), channel_id=1, source_target_pairs={{0,4},{1,5},{2,3},{3,2},{4,0},{5,1},{6,7},{7,6},{8,12},{9,13},{10,... | collective-permute-start | bytes 1671176 | tf_op jit(solution)/shard_map/ppermute | solution.py:332
  57.2 19.7 %collective-permute-start.15 = (bf16[272,1024]{1,0:T(8,128)(2,1)S(1)}, bf16[272,1024]{1,0:T(8,128)(2,1)S(1)}, u32[]{:S(2)}, u32[]{:S(2)}) collective-permute-start(bf16[272,1024]{1,0:T(8,128)(2,1)S(1)} %collective-permute-done.13.refs_0_), channel_id=1, source_target_pairs={{0,1},{1,0},{2,6},{3,7},{4,5},{5,4},{6,2},{7,3},{8,9},{9,8},{10,14... | collective-permute-start | bytes 1671176 | tf_op jit(solution)/shard_map/ppermute | solution.py:332
  59.7 17.3 %collective-permute-start.16 = (bf16[272,1024]{1,0:T(8,128)(2,1)S(1)}, bf16[272,1024]{1,0:T(8,128)(2,1)S(1)}, u32[]{:S(2)}, u32[]{:S(2)}) collective-permute-start(bf16[272,1024]{1,0:T(8,128)(2,1)S(1)} %collective-permute-done.13.refs_0_), channel_id=1, source_target_pairs={{0,8},{1,9},{2,10},{3,11},{4,12},{5,13},{6,14},{7,15},{8,24},{9,25... | collective-permute-start | bytes 1671176 | tf_op jit(solution)/shard_map/ppermute | solution.py:332
  61.3 16.2 %collective-permute-start.30 = (bf16[272,1024]{1,0:T(8,128)(2,1)S(1)}, bf16[272,1024]{1,0:T(8,128)(2,1)}, u32[]{:S(2)}, u32[]{:S(2)}) collective-permute-start(bf16[272,1024]{1,0:T(8,128)(2,1)S(1)} %collective-permute-done.2.refs_0_), channel_id=1, source_target_pairs={{0,2},{1,3},{2,0},{3,1},{4,6},{5,7},{6,4},{7,5},{8,10},{9,11},{10,... | collective-permute-start | bytes 1671176 | tf_op jit(solution)/shard_map/ppermute | solution.py:332
  71.0 6.6 %collective-permute-start.7 = (bf16[272,1024]{1,0:T(8,128)(2,1)}, bf16[272,1024]{1,0:T(8,128)(2,1)}, u32[]{:S(2)}, u32[]{:S(2)}) collective-permute-start(bf16[272,1024]{1,0:T(8,128)(2,1)} %collective-permute-done.3.refs_3_), channel_id=1, source_target_pairs={{0,2},{1,3},{2,0},{3,1},{4,6},{5,7},{6,4},{7,5},{8,10},{9,11},{10,... | collective-permute-start | bytes 1671176 | tf_op jit(solution)/shard_map/ppermute | solution.py:332
  72.4 25.7 %collective-permute-start.31 = (bf16[272,1024]{1,0:T(8,128)(2,1)S(1)}, bf16[272,1024]{1,0:T(8,128)(2,1)}, u32[]{:S(2)}, u32[]{:S(2)}) collective-permute-start(bf16[272,1024]{1,0:T(8,128)(2,1)S(1)} %collective-permute-done.11.refs_1_), channel_id=1, source_target_pairs={{0,2},{1,3},{2,0},{3,1},{4,6},{5,7},{6,4},{7,5},{8,10},{9,11},{10,... | collective-permute-start | bytes 1671176 | tf_op jit(solution)/shard_map/ppermute | solution.py:332
  77.0 21.4 %collective-permute-start.32 = (bf16[272,1024]{1,0:T(8,128)(2,1)}, bf16[272,1024]{1,0:T(8,128)(2,1)}, u32[]{:S(2)}, u32[]{:S(2)}) collective-permute-start(bf16[272,1024]{1,0:T(8,128)(2,1)} %collective-permute-done.12.refs_2_), channel_id=1, source_target_pairs={{0,2},{1,3},{2,0},{3,1},{4,6},{5,7},{6,4},{7,5},{8,10},{9,11},{10,... | collective-permute-start | bytes 1671176 | tf_op jit(solution)/shard_map/ppermute | solution.py:332
  77.0 21.7 %collective-permute-start.33 = (bf16[272,1024]{1,0:T(8,128)(2,1)}, bf16[272,1024]{1,0:T(8,128)(2,1)}, u32[]{:S(2)}, u32[]{:S(2)}) collective-permute-start(bf16[272,1024]{1,0:T(8,128)(2,1)} %collective-permute-done.29.refs_3_), channel_id=1, source_target_pairs={{0,2},{1,3},{2,0},{3,1},{4,6},{5,7},{6,4},{7,5},{8,10},{9,11},{10,... | collective-permute-start | bytes 1671176 | tf_op jit(solution)/shard_map/ppermute | solution.py:332
  77.6 31.9 %collective-permute-start.25 = (bf16[272,1024]{1,0:T(8,128)(2,1)S(1)}, bf16[272,1024]{1,0:T(8,128)(2,1)S(1)}, u32[]{:S(2)}, u32[]{:S(2)}) collective-permute-start(bf16[272,1024]{1,0:T(8,128)(2,1)S(1)} %collective-permute-done.13.refs_0_), channel_id=1, source_target_pairs={{0,2},{1,3},{2,0},{3,1},{4,6},{5,7},{6,4},{7,5},{8,10},{9,11},{10,... | collective-permute-start | bytes 1671176 | tf_op jit(solution)/shard_map/ppermute | solution.py:332
  77.6 32.0 %collective-permute-start.24 = (bf16[272,1024]{1,0:T(8,128)(2,1)S(1)}, bf16[272,1024]{1,0:T(8,128)(2,1)S(1)}, u32[]{:S(2)}, u32[]{:S(2)}) collective-permute-start(bf16[272,1024]{1,0:T(8,128)(2,1)S(1)} %collective-permute-done.14.refs_1_), channel_id=1, source_target_pairs={{0,1},{1,0},{2,6},{3,7},{4,5},{5,4},{6,2},{7,3},{8,9},{9,8},{10,14... | collective-permute-start | bytes 1671176 | tf_op jit(solution)/shard_map/ppermute | solution.py:332
  88.7 11.3 %copy-start.1 = (bf16[1,384,2048]{2,1,0:T(8,128)(2,1)S(1)}, bf16[1,384,2048]{2,1,0:T(8,128)(2,1)}, u32[]{:S(2)}) copy-start(bf16[1,384,2048]{2,1,0:T(8,128)(2,1)} %param.11) | copy-start | bytes 4718596
  98.1 11.9 %collective-permute-start.26 = (bf16[272,1024]{1,0:T(8,128)(2,1)S(1)}, bf16[272,1024]{1,0:T(8,128)(2,1)S(1)}, u32[]{:S(2)}, u32[]{:S(2)}) collective-permute-start(bf16[272,1024]{1,0:T(8,128)(2,1)S(1)} %collective-permute-done.14.refs_1_), channel_id=1, source_target_pairs={{0,2},{1,3},{2,0},{3,1},{4,6},{5,7},{6,4},{7,5},{8,10},{9,11},{10,... | collective-permute-start | bytes 1671176 | tf_op jit(solution)/shard_map/ppermute | solution.py:332
  98.4 11.7 %collective-permute-start.27 = (bf16[272,1024]{1,0:T(8,128)(2,1)S(1)}, bf16[272,1024]{1,0:T(8,128)(2,1)S(1)}, u32[]{:S(2)}, u32[]{:S(2)}) collective-permute-start(bf16[272,1024]{1,0:T(8,128)(2,1)S(1)} %collective-permute-done.15.refs_2_), channel_id=1, source_target_pairs={{0,2},{1,3},{2,0},{3,1},{4,6},{5,7},{6,4},{7,5},{8,10},{9,11},{10,... | collective-permute-start | bytes 1671176 | tf_op jit(solution)/shard_map/ppermute | solution.py:332
  98.7 12.2 %collective-permute-start.17 = (bf16[272,1024]{1,0:T(8,128)(2,1)S(1)}, bf16[272,1024]{1,0:T(8,128)(2,1)S(1)}, u32[]{:S(2)}, u32[]{:S(2)}) collective-permute-start(bf16[272,1024]{1,0:T(8,128)(2,1)S(1)} %collective-permute-done.16.refs_0_), channel_id=1, source_target_pairs={{0,4},{1,5},{2,3},{3,2},{4,0},{5,1},{6,7},{7,6},{8,12},{9,13},{10,... | collective-permute-start | bytes 1671176 | tf_op jit(solution)/shard_map/ppermute | solution.py:332
  109.4 16.2 %collective-permute-start.40 = (bf16[4,128,1024]{2,1,0:T(8,128)(2,1)S(1)}, bf16[4,128,1024]{2,1,0:T(8,128)(2,1)S(1)}, u32[]{:S(2)}, u32[]{:S(2)}) collective-permute-start(bf16[4,128,1024]{2,1,0:T(8,128)(2,1)S(1)} %get-tuple-element.72), channel_id=1, source_target_pairs={{0,2},{1,3},{2,0},{3,1},{4,6},{5,7},{6,4},{7,5},{8,10},{9,11},{10,... | collective-permute-start | bytes 3145736 | tf_op jit(solution)/shard_map/ppermute | solution.py:332
  109.6 4.2 %collective-permute-start.28 = (bf16[272,1024]{1,0:T(8,128)(2,1)S(1)}, bf16[272,1024]{1,0:T(8,128)(2,1)S(1)}, u32[]{:S(2)}, u32[]{:S(2)}) collective-permute-start(bf16[272,1024]{1,0:T(8,128)(2,1)S(1)} %collective-permute-done.24.refs_3_), channel_id=1, source_target_pairs={{0,2},{1,3},{2,0},{3,1},{4,6},{5,7},{6,4},{7,5},{8,10},{9,11},{10,... | collective-permute-start | bytes 1671176 | tf_op jit(solution)/shard_map/ppermute | solution.py:332
  110.0 16.7 %collective-permute-start.8 = (bf16[4,128,1024]{2,1,0:T(8,128)(2,1)}, bf16[4,128,1024]{2,1,0:T(8,128)(2,1)S(1)}, u32[]{:S(2)}, u32[]{:S(2)}) collective-permute-start(bf16[4,128,1024]{2,1,0:T(8,128)(2,1)} %get-tuple-element.44), channel_id=1, source_target_pairs={{0,2},{1,3},{2,0},{3,1},{4,6},{5,7},{6,4},{7,5},{8,10},{9,11},{10,... | collective-permute-start | bytes 3145736 | tf_op jit(solution)/shard_map/ppermute | solution.py:332
  110.1 12.9 %collective-permute-start.18 = (bf16[272,1024]{1,0:T(8,128)(2,1)S(1)}, bf16[272,1024]{1,0:T(8,128)(2,1)S(1)}, u32[]{:S(2)}, u32[]{:S(2)}) collective-permute-start(bf16[272,1024]{1,0:T(8,128)(2,1)S(1)} %collective-permute-done.16.refs_0_), channel_id=1, source_target_pairs={{0,1},{1,0},{2,6},{3,7},{4,5},{5,4},{6,2},{7,3},{8,9},{9,8},{10,14... | collective-permute-start | bytes 1671176 | tf_op jit(solution)/shard_map/ppermute | solution.py:332
  110.9 14.7 %collective-permute-start.19 = (bf16[272,1024]{1,0:T(8,128)(2,1)S(1)}, bf16[272,1024]{1,0:T(8,128)(2,1)S(1)}, u32[]{:S(2)}, u32[]{:S(2)}) collective-permute-start(bf16[272,1024]{1,0:T(8,128)(2,1)S(1)} %collective-permute-done.17.refs_1_), channel_id=1, source_target_pairs={{0,1},{1,0},{2,6},{3,7},{4,5},{5,4},{6,2},{7,3},{8,9},{9,8},{10,14... | collective-permute-start | bytes 1671176 | tf_op jit(solution)/shard_map/ppermute | solution.py:332
  113.8 12.9 %collective-permute-start.20 = (bf16[272,1024]{1,0:T(8,128)(2,1)S(1)}, bf16[272,1024]{1,0:T(8,128)(2,1)S(1)}, u32[]{:S(2)}, u32[]{:S(2)}) collective-permute-start(bf16[272,1024]{1,0:T(8,128)(2,1)S(1)} %collective-permute-done.16.refs_0_), channel_id=1, source_target_pairs={{0,2},{1,3},{2,0},{3,1},{4,6},{5,7},{6,4},{7,5},{8,10},{9,11},{10,... | collective-permute-start | bytes 1671176 | tf_op jit(solution)/shard_map/ppermute | solution.py:332
  123.0 5.0 %collective-permute-start.21 = (bf16[272,1024]{1,0:T(8,128)(2,1)S(1)}, bf16[272,1024]{1,0:T(8,128)(2,1)S(1)}, u32[]{:S(2)}, u32[]{:S(2)}) collective-permute-start(bf16[272,1024]{1,0:T(8,128)(2,1)S(1)} %collective-permute-done.17.refs_1_), channel_id=1, source_target_pairs={{0,2},{1,3},{2,0},{3,1},{4,6},{5,7},{6,4},{7,5},{8,10},{9,11},{10,... | collective-permute-start | bytes 1671176 | tf_op jit(solution)/shard_map/ppermute | solution.py:332
  125.6 3.7 %collective-permute-start.22 = (bf16[272,1024]{1,0:T(8,128)(2,1)S(1)}, bf16[272,1024]{1,0:T(8,128)(2,1)S(1)}, u32[]{:S(2)}, u32[]{:S(2)}) collective-permute-start(bf16[272,1024]{1,0:T(8,128)(2,1)S(1)} %collective-permute-done.18.refs_2_), channel_id=1, source_target_pairs={{0,2},{1,3},{2,0},{3,1},{4,6},{5,7},{6,4},{7,5},{8,10},{9,11},{10,... | collective-permute-start | bytes 1671176 | tf_op jit(solution)/shard_map/ppermute | solution.py:332
  125.6 3.7 %collective-permute-start.23 = (bf16[272,1024]{1,0:T(8,128)(2,1)S(1)}, bf16[272,1024]{1,0:T(8,128)(2,1)S(1)}, u32[]{:S(2)}, u32[]{:S(2)}) collective-permute-start(bf16[272,1024]{1,0:T(8,128)(2,1)S(1)} %collective-permute-done.19.refs_3_), channel_id=1, source_target_pairs={{0,2},{1,3},{2,0},{3,1},{4,6},{5,7},{6,4},{7,5},{8,10},{9,11},{10,... | collective-permute-start | bytes 1671176 | tf_op jit(solution)/shard_map/ppermute | solution.py:332
  126.6 12.8 %collective-permute-start.37 = (bf16[4,128,1024]{2,1,0:T(8,128)(2,1)S(1)}, bf16[4,128,1024]{2,1,0:T(8,128)(2,1)S(1)}, u32[]{:S(2)}, u32[]{:S(2)}) collective-permute-start(bf16[4,128,1024]{2,1,0:T(8,128)(2,1)S(1)} %get-tuple-element.70), channel_id=1, source_target_pairs={{0,2},{1,3},{2,0},{3,1},{4,6},{5,7},{6,4},{7,5},{8,10},{9,11},{10,... | collective-permute-start | bytes 3145736 | tf_op jit(solution)/shard_map/ppermute | solution.py:332
  126.7 11.7 %collective-permute-start.41 = (bf16[2,128,1024]{2,1,0:T(8,128)(2,1)S(1)}, bf16[2,128,1024]{2,1,0:T(8,128)(2,1)S(1)}, u32[]{:S(2)}, u32[]{:S(2)}) collective-permute-start(bf16[2,128,1024]{2,1,0:T(8,128)(2,1)S(1)} %slice.134), channel_id=1, source_target_pairs={{0,1},{1,0},{2,6},{3,7},{4,5},{5,4},{6,2},{7,3},{8,9},{9,8},{10,14... | collective-permute-start | bytes 1572872 | tf_op jit(solution)/shard_map/ppermute | solution.py:332
  128.1 13.5 %collective-permute-start.9 = (bf16[2,128,1024]{2,1,0:T(8,128)(2,1)S(1)}, bf16[2,128,1024]{2,1,0:T(8,128)(2,1)S(1)}, u32[]{:S(2)}, u32[]{:S(2)}) collective-permute-start(bf16[2,128,1024]{2,1,0:T(8,128)(2,1)S(1)} %slice.137), channel_id=1, source_target_pairs={{0,1},{1,0},{2,6},{3,7},{4,5},{5,4},{6,2},{7,3},{8,9},{9,8},{10,14... | collective-permute-start | bytes 1572872 | tf_op jit(solution)/shard_map/ppermute | solution.py:332
  138.3 15.7 %collective-permute-start.34 = (bf16[4,128,1024]{2,1,0:T(8,128)(2,1)S(1)}, bf16[4,128,1024]{2,1,0:T(8,128)(2,1)S(1)}, u32[]{:S(2)}, u32[]{:S(2)}) collective-permute-start(bf16[4,128,1024]{2,1,0:T(8,128)(2,1)S(1)} %get-tuple-element.68), channel_id=1, source_target_pairs={{0,2},{1,3},{2,0},{3,1},{4,6},{5,7},{6,4},{7,5},{8,10},{9,11},{10,... | collective-permute-start | bytes 3145736 | tf_op jit(solution)/shard_map/ppermute | solution.py:332
  138.6 8.7 %collective-permute-start.42 = (bf16[128,1024]{1,0:T(8,128)(2,1)S(1)}, bf16[128,1024]{1,0:T(8,128)(2,1)S(1)}, u32[]{:S(2)}, u32[]{:S(2)}) collective-permute-start(bf16[128,1024]{1,0:T(8,128)(2,1)S(1)} %fusion.17), channel_id=1, source_target_pairs={{0,4},{1,5},{2,3},{3,2},{4,0},{5,1},{6,7},{7,6},{8,12},{9,13},{10,... | collective-permute-start | bytes 786440 | tf_op jit(solution)/shard_map/ppermute | solution.py:332
  139.9 13.1 %collective-permute-start.38 = (bf16[2,128,1024]{2,1,0:T(8,128)(2,1)S(1)}, bf16[2,128,1024]{2,1,0:T(8,128)(2,1)S(1)}, u32[]{:S(2)}, u32[]{:S(2)}) collective-permute-start(bf16[2,128,1024]{2,1,0:T(8,128)(2,1)S(1)} %slice.135), channel_id=1, source_target_pairs={{0,1},{1,0},{2,6},{3,7},{4,5},{5,4},{6,2},{7,3},{8,9},{9,8},{10,14... | collective-permute-start | bytes 1572872 | tf_op jit(solution)/shard_map/ppermute | solution.py:332
  141.8 34.6 %collective-permute-start.10 = (bf16[128,1024]{1,0:T(8,128)(2,1)S(1)}, bf16[128,1024]{1,0:T(8,128)(2,1)S(1)}, u32[]{:S(2)}, u32[]{:S(2)}) collective-permute-start(bf16[128,1024]{1,0:T(8,128)(2,1)S(1)} %fusion.14), channel_id=1, source_target_pairs={{0,4},{1,5},{2,3},{3,2},{4,0},{5,1},{6,7},{7,6},{8,12},{9,13},{10,... | collective-permute-start | bytes 786440 | tf_op jit(solution)/shard_map/ppermute | solution.py:332
  147.4 12.1 %collective-permute-start.43 = (bf16[128,1024]{1,0:T(8,128)(2,1)S(1)}, bf16[128,1024]{1,0:T(8,128)(2,1)S(1)}, u32[]{:S(2)}, u32[]{:S(2)}) collective-permute-start(bf16[128,1024]{1,0:T(8,128)(2,1)S(1)} %fusion.4), channel_id=1, source_target_pairs={{0,8},{1,9},{2,10},{3,11},{4,12},{5,13},{6,14},{7,15},{8,24},{9,25... | collective-permute-start | bytes 786440 | tf_op jit(solution)/shard_map/ppermute | solution.py:332
  153.2 8.6 %collective-permute-start.39 = (bf16[128,1024]{1,0:T(8,128)(2,1)S(1)}, bf16[128,1024]{1,0:T(8,128)(2,1)S(1)}, u32[]{:S(2)}, u32[]{:S(2)}) collective-permute-start(bf16[128,1024]{1,0:T(8,128)(2,1)S(1)} %fusion.16), channel_id=1, source_target_pairs={{0,4},{1,5},{2,3},{3,2},{4,0},{5,1},{6,7},{7,6},{8,12},{9,13},{10,... | collective-permute-start | bytes 786440 | tf_op jit(solution)/shard_map/ppermute | solution.py:332
  154.5 10.4 %collective-permute-start.35 = (bf16[2,128,1024]{2,1,0:T(8,128)(2,1)S(1)}, bf16[2,128,1024]{2,1,0:T(8,128)(2,1)S(1)}, u32[]{:S(2)}, u32[]{:S(2)}) collective-permute-start(bf16[2,128,1024]{2,1,0:T(8,128)(2,1)S(1)} %slice.136), channel_id=1, source_target_pairs={{0,1},{1,0},{2,6},{3,7},{4,5},{5,4},{6,2},{7,3},{8,9},{9,8},{10,14... | collective-permute-start | bytes 1572872 | tf_op jit(solution)/shard_map/ppermute | solution.py:332
  162.0 7.8 %collective-permute-start.44 = (bf16[128,1024]{1,0:T(8,128)(2,1)S(1)}, bf16[128,1024]{1,0:T(8,128)(2,1)S(1)}, u32[]{:S(2)}, u32[]{:S(2)}) collective-permute-start(bf16[128,1024]{1,0:T(8,128)(2,1)S(1)} %fusion.7), channel_id=1, source_target_pairs={{0,8},{1,9},{2,10},{3,11},{4,12},{5,13},{6,14},{7,15},{8,24},{9,25... | collective-permute-start | bytes 786440 | tf_op jit(solution)/shard_map/ppermute | solution.py:332
  165.1 7.9 %slice-start = ((s8[4718592]{0:T(1024)(128)(4,1)}), s8[4194304]{0:T(1024)(128)(4,1)S(1)}, s32[]{:S(2)}) async-start(s8[4718592]{0:T(1024)(128)(4,1)} %bitcast.70), calls=%async_computation | async-start | bytes 8388608
  165.2 6.4 %collective-permute-start.36 = (bf16[128,1024]{1,0:T(8,128)(2,1)S(1)}, bf16[128,1024]{1,0:T(8,128)(2,1)S(1)}, u32[]{:S(2)}, u32[]{:S(2)}) collective-permute-start(bf16[128,1024]{1,0:T(8,128)(2,1)S(1)} %fusion.15), channel_id=1, source_target_pairs={{0,4},{1,5},{2,3},{3,2},{4,0},{5,1},{6,7},{7,6},{8,12},{9,13},{10,... | collective-permute-start | bytes 786440 | tf_op jit(solution)/shard_map/ppermute | solution.py:332
  171.7 8.5 %collective-permute-start.45 = (bf16[128,1024]{1,0:T(8,128)(2,1)S(1)}, bf16[128,1024]{1,0:T(8,128)(2,1)S(1)}, u32[]{:S(2)}, u32[]{:S(2)}) collective-permute-start(bf16[128,1024]{1,0:T(8,128)(2,1)S(1)} %fusion.10), channel_id=1, source_target_pairs={{0,8},{1,9},{2,10},{3,11},{4,12},{5,13},{6,14},{7,15},{8,24},{9,25... | collective-permute-start | bytes 786440 | tf_op jit(solution)/shard_map/ppermute | solution.py:332
  (15 other events, 21.6 us)

commit v4 on v3

--- a/solution.py
+++ b/solution.py
@@ -10,6 +10,7 @@
 CONTRACT_LAST = (((1,), (1,)), ((), ()))
 CONTRACT_FIRST = (((0,), (0,)), ((), ()))
 INFO_ROWS = 16
+VMEM_LIMIT = 24 * 1024 * 1024
 
 
 def pack_rows(token_rows, grad_rows, token_of, scale, is_live):
@@ -104,15 +105,10 @@
     )
 
 
-def pack_kernel(tokens_ref, grads_ref, routes_ref, combine_ref, out_ref, info_ref, sems):
+def pack_kernel(tokens_ref, grads_ref, routes_ref, combine_ref, out_ref):
     rows = tokens_ref.shape[0]
-    moves = [
-        pltpu.make_async_copy(tokens_ref, out_ref.at[pl.ds(0, rows)], sems.at[0]),
-        pltpu.make_async_copy(grads_ref, out_ref.at[pl.ds(rows, rows)], sems.at[1]),
-        pltpu.make_async_copy(info_ref, out_ref.at[pl.ds(2 * rows, INFO_ROWS)], sems.at[2]),
-    ]
-    moves[0].start()
-    moves[1].start()
+    out_ref[:rows] = tokens_ref[...]
+    out_ref[rows:2 * rows] = grads_ref[...]
     top = routes_ref.shape[0]
     routes = routes_ref[...].astype(jnp.float32)
     weights = combine_ref[...]
@@ -120,95 +116,72 @@
     middle = (weights - high).astype(jnp.bfloat16).astype(jnp.float32)
     low = weights - high - middle
     blank = jnp.zeros((INFO_ROWS - 4, rows), jnp.float32)
-    info_ref[...] = jnp.zeros(info_ref.shape, info_ref.dtype)
     for k in range(top):
         own = slice(k, k + 1)
         column = jnp.concatenate([routes[own], high[own], middle[own], low[own], blank], axis=0)
-        info_ref[:, k * rows:(k + 1) * rows] = column.astype(jnp.bfloat16)
-    moves[2].start()
-    for move in moves:
-        move.wait()
+        out_ref[2 * rows:, k * rows:(k + 1) * rows] = column.astype(jnp.bfloat16)
 
 
 def pack_share(tokens, out_grad, routes, combine):
     rows, width = tokens.shape
-    anywhere = pl.BlockSpec(memory_space=pl.ANY)
     vmem = pl.BlockSpec(memory_space=pltpu.VMEM)
     return pl.pallas_call(
         pack_kernel,
-        in_specs=[anywhere, anywhere, vmem, vmem],
-        out_specs=anywhere,
+        in_specs=[vmem] * 4,
+        out_specs=vmem,
         out_shape=jax.ShapeDtypeStruct((2 * rows + INFO_ROWS, width), jnp.bfloat16),
-        scratch_shapes=[pltpu.VMEM((INFO_ROWS, width), jnp.bfloat16), pltpu.SemaphoreType.DMA((3,))],
         cost_estimate=pl.CostEstimate(flops=0, bytes_accessed=8 * rows * width, transcendentals=0),
         name="pack",
     )(tokens, out_grad, routes.T, combine.T)
 
 
-def expert_kernel(index, chained, top, place_ref, *refs):
-    shares, weight_refs = refs[:8], refs[8:11]
-    refs = refs[11 + (5 if chained else 0):]
+def expert_kernel(index, chained, top, rows, place_ref, *refs):
+    pair_refs = refs[:4]
+    wg_ref, wu_ref, wd_ref = refs[4:7]
+    refs = refs[7 + (5 if chained else 0):]
     near_ref, far_ref = refs[:2]
     kept_refs = refs[2:7]
-    x_buf, g_buf, info_buf, wg_ref, wu_ref, wd_ref, rx_ref, rg_ref, act_ref, gt_ref, ut_ref, slot_ref, back_ref = refs[7:20]
-    in_sems, weight_sems, kept_sems, out_sems = refs[20:]
+    rx_ref, rg_ref, act_ref, gt_ref, ut_ref, slot_ref, sems = refs[7:]
     me = place_ref[0].astype(jnp.float32)
     own_half = place_ref[1]
     core = place_ref[2]
-    other = 1 - core
-    halves, blocks, rows, width = x_buf.shape
     slots = rx_ref.shape[0]
-    pairs = blocks // 2
-    pair_slots = slots // pairs
-
-    spots = [(0, 0), (core, other), (other, core), (1, 1),
-             (0, 2), (other, 2 + core), (core, 2 + other), (1, 3)]
-    info_moves = [
-        pltpu.make_async_copy(
-            shares[s].at[pl.ds(2 * rows, INFO_ROWS)], info_buf.at[b], in_sems.at[16 + b]
-        )
-        for b, s in enumerate((0, 3, 4, 7))
-    ]
-    x_moves = [
-        pltpu.make_async_copy(shares[s].at[pl.ds(0, rows)], x_buf.at[spots[s]], in_sems.at[s])
-        for s in range(8)
-    ]
-    g_moves = [
-        pltpu.make_async_copy(shares[s].at[pl.ds(rows, rows)], g_buf.at[spots[s]], in_sems.at[8 + s])
-        for s in range(8)
-    ]
-    weight_moves = [
-        pltpu.make_async_copy(source, target, weight_sems.at[i])
-        for i, (source, target) in enumerate(zip(weight_refs, (wg_ref, wu_ref, wd_ref)))
-    ]
+    width = near_ref.shape[2]
+    pair_slots = slots // 2
     kept_moves = [
-        pltpu.make_async_copy(
-            source, target.at[pl.ds(index * slots, slots)], kept_sems.at[i]
-        )
+        pltpu.make_async_copy(source, target.at[pl.ds(index * slots, slots)], sems.at[i])
         for i, (source, target) in enumerate(zip((rx_ref, rg_ref, act_ref, gt_ref, ut_ref), kept_refs))
     ]
-    out_moves = [
-        pltpu.make_async_copy(
-            back_ref.at[spots[s]], (near_ref if s < 4 else far_ref).at[s % 4], out_sems.at[s]
-        )
-        for s in range(8)
-    ]
-    for move in info_moves + x_moves + weight_moves[:2] + g_moves + weight_moves[2:]:
-        move.start()
-
-    for move in info_moves:
-        move.wait()
+
+    def columns(h):
+        return pl.ds(pl.multiple_of((own_half if h == 0 else 1 - own_half) * width, width), width)
+
+    def slot_rows(p):
+        return slice(p * pair_slots, (p + 1) * pair_slots)
+
+    def swapped(p):
+        return core == 1 if p == 0 else core == 0
+
+    def gathered(p, h, part):
+        here = pl.ds(part * rows, rows)
+        first, second = pair_refs[2 * p], pair_refs[2 * p + 1]
+        if h == 0:
+            inner = jnp.where(swapped(p), second[0, here], first[1, here])
+            return jnp.concatenate([first[0, here], inner], axis=0)
+        inner = jnp.where(swapped(p), first[1, here], second[0, here])
+        return jnp.concatenate([inner, second[1, here]], axis=0)
+
     earlier = (
         lax.broadcasted_iota(jnp.int32, (2 * rows, 2 * rows), 0)
         < lax.broadcasted_iota(jnp.int32, (2 * rows, 2 * rows), 1)
     ).astype(jnp.bfloat16)
     picks, scales = [], []
-    for p in range(pairs):
+    for p in range(2):
         named, weights = [], []
-        for b in (2 * p, 2 * p + 1):
+        for pair_ref, s in ((pair_refs[2 * p], 0), (pair_refs[2 * p + 1], 1)):
             hits, weight = 0.0, 0.0
             for k in range(top):
-                info = info_buf[b, :, k * rows:(k + 1) * rows].astype(jnp.float32)
+                info = pair_ref[s, pl.ds(2 * rows, INFO_ROWS), k * rows:(k + 1) * rows].astype(jnp.float32)
                 hit = info[0:1] == me
                 hits += hit.astype(jnp.float32)
                 weight += jnp.where(hit, info[1:2] + info[2:3] + info[3:4], 0.0)
@@ -226,89 +199,72 @@
         picks.append(chosen.astype(jnp.bfloat16))
         scales.append(jnp.sum(jnp.where(chosen, weights, 0.0), axis=1, keepdims=True))
 
-    def columns(h):
-        return pl.ds(pl.multiple_of((own_half if h == 0 else 1 - own_half) * width, width), width)
-
-    def slot_rows(p):
-        return slice(p * pair_slots, (p + 1) * pair_slots)
-
-    for move in x_moves:
-        move.wait()
-    for h in range(halves):
-        for p in range(pairs):
-            x = x_buf[h, 2 * p:2 * p + 2].reshape(2 * rows, width)
-            picked = jnp.dot(picks[p], x, preferred_element_type=jnp.float32)
+    for h in range(2):
+        for p in range(2):
+            picked = jnp.dot(picks[p], gathered(p, h, 0), preferred_element_type=jnp.float32)
             rx_ref[slot_rows(p), columns(h)] = picked.astype(jnp.bfloat16)
     kept_moves[0].start()
-    weight_moves[0].wait()
+    for h in range(2):
+        for p in range(2):
+            picked = jnp.dot(picks[p], gathered(p, h, 1), preferred_element_type=jnp.float32)
+            rg_ref[slot_rows(p), columns(h)] = (scales[p] * picked).astype(jnp.bfloat16)
+    kept_moves[1].start()
     gate = lax.dot_general(rx_ref[...], wg_ref[...], CONTRACT_LAST, preferred_element_type=jnp.float32)
-    weight_moves[1].wait()
     up = lax.dot_general(rx_ref[...], wu_ref[...], CONTRACT_LAST, preferred_element_type=jnp.float32)
+    hidden_grad = lax.dot_general(rg_ref[...], wd_ref[...], CONTRACT_LAST, preferred_element_type=jnp.float32)
     sigma = 1.0 / (1.0 + jnp.exp(-gate))
     silu = gate * sigma
     act_ref[...] = (silu * up).astype(jnp.bfloat16)
-    kept_moves[2].start()
-
-    for move in g_moves:
-        move.wait()
-    for h in range(halves):
-        for p in range(pairs):
-            g = g_buf[h, 2 * p:2 * p + 2].reshape(2 * rows, width)
-            picked = jnp.dot(picks[p], g, preferred_element_type=jnp.float32)
-            rg_ref[slot_rows(p), columns(h)] = (scales[p] * picked).astype(jnp.bfloat16)
-    kept_moves[1].start()
-    weight_moves[2].wait()
-    hidden_grad = lax.dot_general(rg_ref[...], wd_ref[...], CONTRACT_LAST, preferred_element_type=jnp.float32)
     gt_ref[...] = (hidden_grad * up * sigma * (1.0 + gate * (1.0 - sigma))).astype(jnp.bfloat16)
     ut_ref[...] = (hidden_grad * silu).astype(jnp.bfloat16)
-    kept_moves[3].start()
-    kept_moves[4].start()
+    for move in kept_moves[2:]:
+        move.start()
 
     slot = jnp.dot(gt_ref[...], wg_ref[...], preferred_element_type=jnp.float32)
     slot += jnp.dot(ut_ref[...], wu_ref[...], preferred_element_type=jnp.float32)
     slot_ref[...] = slot.astype(jnp.bfloat16)
-    for p in reversed(range(pairs)):
-        for h in range(halves):
+    for p, out_ref in enumerate((near_ref, far_ref)):
+        backs = []
+        for h in range(2):
             back = lax.dot_general(
                 picks[p], slot_ref[slot_rows(p), columns(h)], CONTRACT_FIRST,
                 preferred_element_type=jnp.float32,
-            )
-            back_ref[h, 2 * p:2 * p + 2] = back.astype(jnp.bfloat16).reshape(2, rows, width)
-        for s in range(4 * p, 4 * p + 4):
-            out_moves[s].start()
-    for move in kept_moves + out_moves:
+            ).astype(jnp.bfloat16)
+            backs.append(back)
+        out_ref[0] = backs[0][:rows]
+        out_ref[1] = jnp.where(swapped(p), backs[1][:rows], backs[0][rows:])
+        out_ref[2] = jnp.where(swapped(p), backs[0][rows:], backs[1][:rows])
+        out_ref[3] = backs[1][rows:]
+    for move in kept_moves:
         move.wait()
 
 
-def run_experts(index, chunks, place, shares, weights, kept, top, rows, slots):
-    width = shares[0].shape[1]
+def run_experts(index, chunks, place, pairs, weights, kept, top, rows, slots):
+    width = pairs[0].shape[2]
     hidden, features = weights[0].shape
     anywhere = pl.BlockSpec(memory_space=pl.ANY)
+    vmem = pl.BlockSpec(memory_space=pltpu.VMEM)
     part = jax.ShapeDtypeStruct((4, rows, width), jnp.bfloat16)
     wide = jax.ShapeDtypeStruct((chunks * slots, features), jnp.bfloat16)
     narrow = jax.ShapeDtypeStruct((chunks * slots, hidden), jnp.bfloat16)
-    held = pltpu.VMEM((2, 4, rows, width), jnp.bfloat16)
-    first_kept = 1 + len(shares) + 3
+    first_kept = 1 + len(pairs) + 3
     return pl.pallas_call(
-        functools.partial(expert_kernel, index, kept is not None, top),
-        in_specs=[pl.BlockSpec(memory_space=pltpu.SMEM)] + [anywhere] * (11 if kept is None else 16),
-        out_specs=[anywhere] * 7,
+        functools.partial(expert_kernel, index, kept is not None, top, rows),
+        in_specs=[pl.BlockSpec(memory_space=pltpu.SMEM)] + [vmem] * 7 + [anywhere] * (0 if kept is None else 5),
+        out_specs=[vmem] * 2 + [anywhere] * 5,
         out_shape=[part, part, wide, wide, narrow, narrow, narrow],
-        scratch_shapes=[held, held, pltpu.VMEM((4, INFO_ROWS, width), jnp.bfloat16)]
-        + [pltpu.VMEM((hidden, features), jnp.bfloat16)] * 3
-        + [pltpu.VMEM((slots, features), jnp.bfloat16)] * 2
+        scratch_shapes=[pltpu.VMEM((slots, features), jnp.bfloat16)] * 2
         + [pltpu.VMEM((slots, hidden), jnp.bfloat16)] * 3
-        + [pltpu.VMEM((slots, features), jnp.bfloat16), held]
-        + [pltpu.SemaphoreType.DMA((n,)) for n in (20, 3, 5, 8)],
+        + [pltpu.VMEM((slots, features), jnp.bfloat16), pltpu.SemaphoreType.DMA((5,))],
         input_output_aliases={} if kept is None else {first_kept + i: 2 + i for i in range(5)},
-        compiler_params=pltpu.CompilerParams(vmem_limit_bytes=32 * 1024 * 1024),
+        compiler_params=pltpu.CompilerParams(vmem_limit_bytes=VMEM_LIMIT),
         cost_estimate=pl.CostEstimate(
             flops=2 * slots * features * (hidden * 5 + 2 * rows * 3),
-            bytes_accessed=2 * (8 * shares[0].size + 3 * hidden * features + slots * (2 * features + 3 * hidden)),
+            bytes_accessed=2 * (4 * pairs[0].size + 3 * hidden * features + slots * (2 * features + 3 * hidden)),
             transcendentals=slots * hidden,
         ),
         name="experts",
-    )(place, *shares, *weights, *(kept or ()))
+    )(place, *pairs, *weights, *(kept or ()))
 
 
 def ring_order(length):
@@ -347,29 +303,43 @@
     place = jnp.stack([me, lax.axis_index("etp"), me % 2]).astype(jnp.int32)
     weights = (w_gate[0], w_up[0], w_down[0])
     share = pack_share(tokens, out_grad, routes, combine)
+    together = lax.optimization_barrier
     kept = None
-    running = None
+    sums, sends, running = [], [], None
+    first, second, following = together((to_first(share), to_second(share), to_ring(share)))
+    pair, share = jnp.stack([share, first]), following
     for c in range(chunks):
-        first, second = to_first(share), to_second(share)
+        moved = to_second(first if c == 0 else pair)
         if c + 1 < chunks:
-            following = to_ring(share)
-            first, second, following = lax.optimization_barrier((first, second, following))
-        else:
-            following = None
-        near = [share, first, second, to_second(first)]
-        far = [to_core(s) for s in near]
-        share = following
+            following = to_ring(share) if c + 2 < chunks else None
+            moved, first, following = together((moved, to_first(share), following))
+        second = jnp.stack([second, moved]) if c == 0 else moved
+        ready = [pair, second, to_core(pair), to_core(second)]
+        if c + 1 < chunks:
+            pair = jnp.stack([share, first])
+            pair, share, sends, *ready = together((pair, following, sends, *ready))
         near_part, far_part, *kept = run_experts(
-            c, chunks, place, near + far, weights, kept, top, rows, slots
+            c, chunks, place, ready, weights, kept, top, rows, slots
         )
+        for i in range(len(sums)):
+            if sums[i].ndim == 3:
+                sums[i] = sums[i] + to_second(sends[i]).astype(jnp.float32)
+                sums[i], sends[i] = sums[i][0], sums[i][1].astype(jnp.bfloat16)
+            elif sends[i] is not None:
+                sums[i], sends[i] = sums[i] + to_first(sends[i]).astype(jnp.float32), None
         mine = near_part.astype(jnp.float32) + to_core(far_part).astype(jnp.float32)
-        mine = mine[:2] + to_second(mine[2:].astype(jnp.bfloat16)).astype(jnp.float32)
-        mine = mine[0] + to_first(mine[1].astype(jnp.bfloat16)).astype(jnp.float32)
-        if c == 0:
-            own = mine
-        else:
-            running = mine if c == 1 else mine + running.astype(jnp.float32)
+        sums.append(mine[:2])
+        sends.append(mine[2:].astype(jnp.bfloat16))
+    for c in range(chunks):
+        if sums[c].ndim == 3:
+            sums[c] = sums[c] + to_second(sends[c]).astype(jnp.float32)
+            sums[c], sends[c] = sums[c][0], sums[c][1].astype(jnp.bfloat16)
+        if sends[c] is not None:
+            sums[c] = sums[c] + to_first(sends[c]).astype(jnp.float32)
+        if c > 0:
+            running = sums[c] if c == 1 else sums[c] + running.astype(jnp.float32)
             running = to_ring(running.astype(jnp.bfloat16))
+    own = sums[0]
     grad_tokens = (own if running is None else own + running.astype(jnp.float32)).astype(jnp.bfloat16)
     rows_x, rows_g, acts, gate_term, up_term = kept
     grad_down = lax.dot_general(acts, rows_g, CONTRACT_FIRST, preferred_element_type=jnp.float32)

time: 182 us -> 167 us (0.918)
  Pallas kernels: 54.6 us -> 31.9 us
  waiting for transfers between devices: 64.4 us -> 77.2 us
  local copies, waits for them, and re-layouts: 15 us -> 10.3 us
  other arithmetic: 3.39 us -> 5.93 us
  starting transfers between devices: 32.3 us -> 30.3 us
    pallas_call x1, Pallas kernels: 17.7 us -> 1.89 us  [pack_share(): pl.pallas_call(pack_kernel, in_specs=[vmem] * 4, out_specs=vmem, out_shap...]
    ppermute x46 -> x35, waiting for transfers between devices: 64.4 us -> 77.2 us  [permute(): return lax.ppermute(value, ('expert', 'etp'), pairs)]
    pallas_call x4, Pallas kernels: 36.9 us -> 30.1 us  [run_experts(): pl.pallas_call(functools.partial(expert_kernel, index, kept is not None,...]
    unnamed x34 -> x26, local copies, waits for them, and re-layouts: 14.6 us -> 9.92 us
    another operation x0 -> x5, other arithmetic: none -> 2.59 us  [the longest x3 1.33 us: gather_body(): pair = jnp.stack([share, first])]
    ppermute x46 -> x35, starting transfers between devices: 32.3 us -> 30.3 us  [permute(): return lax.ppermute(value, ('expert', 'etp'), pairs)]
  transfers between devices with their start and end apart: 46 -> 35, of which waited for: 15 -> 18; matrix products, arithmetic and copies ran while one was open for 7% -> 9% of each run, Pallas kernels for 20% -> 18%
where the time goes in v4:
time: 167 us
  waiting for transfers between devices  77.2 us (46%)
  Pallas kernels  31.9 us (19%)
  starting transfers between devices  30.3 us (18%)
  local copies, waits for them, and re-layouts  10.3 us (6%)
  matrix products  10.1 us (6%)
  other arithmetic  5.93 us (4%)
    ppermute x35, waiting for transfers between devices, permute(): return lax.ppermute(value, ('expert', 'etp'), pairs)  77.2 us
    ppermute x35, starting transfers between devices, permute(): return lax.ppermute(value, ('expert', 'etp'), pairs)  30.3 us
    pallas_call x4, Pallas kernels, run_experts(): pl.pallas_call(functools.partial(expert_kernel, index, kept is not None,...  30.1 us
    unnamed x26, local copies, waits for them, and re-layouts  9.92 us
    dot_general x1, matrix products, gather_body(): lax.dot_general(up_term, rows_x, CONTRACT_FIRST, preferred_element_type=j...  3.38 us
    dot_general x1, matrix products, gather_body(): lax.dot_general(gate_term, rows_x, CONTRACT_FIRST, preferred_element_type...  3.38 us
    dot_general x1, matrix products, gather_body(): lax.dot_general(acts, rows_g, CONTRACT_FIRST, preferred_element_type=jnp....  3.38 us
  transfers between devices with their start and end apart: 35, of which 18 were waited for; matrix products, arithmetic and copies ran while one was open for 9% of the time, Pallas kernels for 18%

profile of v4, /device:TPU:0, one launch (start us, length us, event | category | flops | bytes accessed | tf_op | source)
XLA Modules:
  0.0 166.8 jit_solution(8965900418180473315)
XLA Ops:
  0.6 1.9 %pack.1 = bf16[272,1024]{1,0:T(8,128)(2,1)} custom-call(bf16[128,1024]{1,0:T(8,128)(2,1)} %tokens_ref.1, bf16[128,1024]{1,0:T(8,128)(2,1)} %grads_ref.1, s32[8,128]{1,0:T(8,128)} %bitcast.90, f32[8,128]{1,0:T(8,128)} %bitcast.91), custom_call_target="tpu_custom_call" | custom-call | bytes 1048576 | tf_op jit(solution)/shard_map/pack/pallas_call | solution.py:128
  2.5 3.0 %collective-permute-start = (bf16[272,1024]{1,0:T(8,128)(2,1)}, bf16[272,1024]{1,0:T(8,128)(2,1)S(1)}, u32[]{:S(2)}, u32[]{:S(2)}) collective-permute-start(bf16[272,1024]{1,0:T(8,128)(2,1)} %pack.1), channel_id=1, source_target_pairs={{0,4},{1,5},{2,3},{3,2},{4,0},{5,1},{6,7},{7,6},{8,12},{9,13},{10,... | collective-permute-start | bytes 1671176 | tf_op jit(solution)/shard_map/ppermute | solution.py:288
  5.5 1.5 collective-permute-start.1
  7.0 1.6 collective-permute-start.2
  8.6 10.2 %collective-permute-done = bf16[272,1024]{1,0:T(8,128)(2,1)S(1)} collective-permute-done((bf16[272,1024]{1,0:T(8,128)(2,1)}, bf16[272,1024]{1,0:T(8,128)(2,1)S(1)}, u32[]{:S(2)}, u32[]{:S(2)}) %collective-permute-start) | collective-permute-done | bytes 557088 | tf_op jit(solution)/shard_map/ppermute | solution.py:288
  18.7 3.2 %collective-permute-done.2 = bf16[272,1024]{1,0:T(8,128)(2,1)S(1)} collective-permute-done((bf16[272,1024]{1,0:T(8,128)(2,1)}, bf16[272,1024]{1,0:T(8,128)(2,1)S(1)}, u32[]{:S(2)}, u32[]{:S(2)}) %collective-permute-start.2) | collective-permute-done | bytes 557088 | tf_op jit(solution)/shard_map/ppermute | solution.py:288
  23.8 1.2 pad_maximum_fusion.1.refs_0_
  25.1 10.6 %collective-permute-done.4 = bf16[272,1024]{1,0:T(8,128)(2,1)S(1)} collective-permute-done((bf16[272,1024]{1,0:T(8,128)(2,1)S(1)}, bf16[272,1024]{1,0:T(8,128)(2,1)S(1)}, u32[]{:S(2)}, u32[]{:S(2)}) %collective-permute-start.4) | collective-permute-done | bytes 557088 | tf_op jit(solution)/shard_map/ppermute | solution.py:288
  37.0 1.1 pad_maximum_fusion.refs_0_
  38.2 1.0 copy-done.7
  39.7 1.0 copy-done.9
  40.7 1.5 collective-permute-start.9
  42.3 1.0 collective-permute-start.10
  44.1 1.4 copy-done.2
  45.5 1.2 copy-done.4
  46.8 1.2 copy-done.6
  48.0 1.2 copy-done.8
  49.3 1.2 copy-done.10
  50.5 7.2 %experts.4 = (bf16[4,128,1024]{2,1,0:T(8,128)(2,1)S(1)}, bf16[4,128,1024]{2,1,0:T(8,128)(2,1)S(1)}, bf16[1152,2048]{1,0:T(8,128)(2,1)S(1)}, bf16[1152,2048]{1,0:...) custom-call(s32[3]{0:T(128)S(1)} %pad_add_fusion.place_ref, ...), custom_call_target="tpu_custom_call" | custom-call | flops 3170893824 | bytes 12197888 | tf_op jit(solution)/shard_map/experts/pallas_call | solution.py:251
  58.5 4.0 %collective-permute-done.9.refs_1_ = bf16[2,272,1024]{2,1,0:T(8,128)(2,1)} collective-permute-done((bf16[2,272,1024]{2,1,0:T(8,128)(2,1)}, bf16[2,272,1024]{2,1,0:T(8,128)(2,1)}, u32[]{:S(2)}, u32[]{:S(2)}) %collective-permute-start.9) | collective-permute-done | bytes 1114144 | tf_op jit(solution)/shard_map/ppermute | solution.py:288
  63.7 1.8 %collective-permute-done.13.refs_3_ = bf16[2,272,1024]{2,1,0:T(8,128)(2,1)S(1)} collective-permute-done((bf16[2,272,1024]{2,1,0:T(8,128)(2,1)}, bf16[2,272,1024]{2,1,0:T(8,128)(2,1)S(1)}, u32[]{:S(2)}, u32[]{:S(2)}) %collective-permute-start.13) | collective-permute-done | bytes 1114144 | tf_op jit(solution)/shard_map/ppermute | solution.py:288
  65.5 1.5 collective-permute-start.15
  67.0 1.0 collective-permute-start.16
  68.5 8.3 %experts.5 = (bf16[4,128,1024]{2,1,0:T(8,128)(2,1)S(1)}, bf16[4,128,1024]{2,1,0:T(8,128)(2,1)S(1)}, bf16[1152,2048]{1,0:T(8,128)(2,1)S(1)}, bf16[1152,2048]{1,0:...) custom-call(s32[3]{0:T(128)S(1)} %pad_add_fusion.place_ref, ...), custom_call_target="tpu_custom_call", output_to_operand_aliasing={{2}: (8, {}), {3}: (9, {}), {4}: (10, {}), {5}: (11, {}), {... | custom-call | flops 3170893824 | bytes 12197888 | tf_op jit(solution)/shard_map/experts/pallas_call | solution.py:251
  77.3 5.2 %collective-permute-done.16 = bf16[272,1024]{1,0:T(8,128)(2,1)S(1)} collective-permute-done((bf16[272,1024]{1,0:T(8,128)(2,1)S(1)}, bf16[272,1024]{1,0:T(8,128)(2,1)S(1)}, u32[]{:S(2)}, u32[]{:S(2)}) %collective-permute-start.16) | collective-permute-done | bytes 557088 | tf_op jit(solution)/shard_map/ppermute | solution.py:288
  82.5 4.3 %collective-permute-done.15.refs_1_ = bf16[2,272,1024]{2,1,0:T(8,128)(2,1)S(1)} collective-permute-done((bf16[2,272,1024]{2,1,0:T(8,128)(2,1)S(1)}, bf16[2,272,1024]{2,1,0:T(8,128)(2,1)S(1)}, u32[]{:S(2)}, u32[]{:S(2)}) %collective-permute-start.15) | collective-permute-done | bytes 1114144 | tf_op jit(solution)/shard_map/ppermute | solution.py:288
  86.8 5.6 %collective-permute-done.14 = bf16[2,128,1024]{2,1,0:T(8,128)(2,1)S(1)} collective-permute-done((bf16[2,128,1024]{2,1,0:T(8,128)(2,1)S(1)}, bf16[2,128,1024]{2,1,0:T(8,128)(2,1)S(1)}, u32[]{:S(2)}, u32[]{:S(2)}) %collective-permute-start.14) | collective-permute-done | bytes 524320 | tf_op jit(solution)/shard_map/ppermute | solution.py:288
  93.3 1.6 collective-permute-start.21
  95.4 7.4 %experts.6 = (bf16[4,128,1024]{2,1,0:T(8,128)(2,1)S(1)}, bf16[4,128,1024]{2,1,0:T(8,128)(2,1)S(1)}, bf16[1152,2048]{1,0:T(8,128)(2,1)S(1)}, bf16[1152,2048]{1,0:...) custom-call(s32[3]{0:T(128)S(1)} %pad_add_fusion.place_ref, ...), custom_call_target="tpu_custom_call", output_to_operand_aliasing={{2}: (8, {}), {3}: (9, {}), {4}: (10, {}), {5}: (11, {}), {... | custom-call | flops 3170893824 | bytes 12197888 | tf_op jit(solution)/shard_map/experts/pallas_call | solution.py:251
  103.3 5.5 %collective-permute-done.21.refs_1_ = bf16[2,272,1024]{2,1,0:T(8,128)(2,1)S(1)} collective-permute-done((bf16[2,272,1024]{2,1,0:T(8,128)(2,1)S(1)}, bf16[2,272,1024]{2,1,0:T(8,128)(2,1)S(1)}, u32[]{:S(2)}, u32[]{:S(2)}) %collective-permute-start.21) | collective-permute-done | bytes 1114144 | tf_op jit(solution)/shard_map/ppermute | solution.py:288
  108.8 5.6 %collective-permute-done.30 = bf16[2,128,1024]{2,1,0:T(8,128)(2,1)S(1)} collective-permute-done((bf16[2,128,1024]{2,1,0:T(8,128)(2,1)S(1)}, bf16[2,128,1024]{2,1,0:T(8,128)(2,1)S(1)}, u32[]{:S(2)}, u32[]{:S(2)}) %collective-permute-start.30) | collective-permute-done | bytes 524320 | tf_op jit(solution)/shard_map/ppermute | solution.py:288
  114.6 1.1 collective-permute-start.31
  116.2 1.6 collective-permute-start.28
  117.8 6.1 %collective-permute-done.31 = bf16[128,1024]{1,0:T(8,128)(2,1)S(1)} collective-permute-done((bf16[128,1024]{1,0:T(8,128)(2,1)S(1)}, bf16[128,1024]{1,0:T(8,128)(2,1)S(1)}, u32[]{:S(2)}, u32[]{:S(2)}) %collective-permute-start.31) | collective-permute-done | bytes 262176 | tf_op jit(solution)/shard_map/ppermute | solution.py:288
  123.9 1.9 %collective-permute-start.32 = (bf16[128,1024]{1,0:T(8,128)(2,1)S(1)}, bf16[128,1024]{1,0:T(8,128)(2,1)S(1)}, u32[]{:S(2)}, u32[]{:S(2)}) collective-permute-start(bf16[128,1024]{1,0:T(8,128)(2,1)S(1)} %fusion.4), channel_id=1, source_target_pairs={{0,8},{1,9},{2,10},{3,11},{4,12},{5,13},{6,14},{7,15},{8,24},{9,25... | collective-permute-start | bytes 786440 | tf_op jit(solution)/shard_map/ppermute | solution.py:288
  125.8 7.2 %experts.7 = (bf16[4,128,1024]{2,1,0:T(8,128)(2,1)S(1)}, bf16[4,128,1024]{2,1,0:T(8,128)(2,1)S(1)}, bf16[1152,2048]{1,0:T(8,128)(2,1)S(1)}, bf16[1152,2048]{1,0:...) custom-call(s32[3]{0:T(128)S(1)} %pad_add_fusion.place_ref, ...), custom_call_target="tpu_custom_call", output_to_operand_aliasing={{2}: (8, {}), {3}: (9, {}), {4}: (10, {}), {5}: (11, {}), {... | custom-call | flops 3170893824 | bytes 12197888 | tf_op jit(solution)/shard_map/experts/pallas_call | solution.py:251
  133.3 1.1 collective-permute-start.29
  134.5 0.9 collective-permute-start.20
  135.4 4.3 %collective-permute-done.29 = bf16[128,1024]{1,0:T(8,128)(2,1)S(1)} collective-permute-done((bf16[128,1024]{1,0:T(8,128)(2,1)S(1)}, bf16[128,1024]{1,0:T(8,128)(2,1)S(1)}, u32[]{:S(2)}, u32[]{:S(2)}) %collective-permute-start.29) | collective-permute-done | bytes 262176 | tf_op jit(solution)/shard_map/ppermute | solution.py:288
  139.9 2.4 %collective-permute-start.33 = (bf16[128,1024]{1,0:T(8,128)(2,1)S(1)}, bf16[128,1024]{1,0:T(8,128)(2,1)S(1)}, u32[]{:S(2)}, u32[]{:S(2)}) collective-permute-start(bf16[128,1024]{1,0:T(8,128)(2,1)S(1)} %fusion.7), channel_id=1, source_target_pairs={{0,8},{1,9},{2,10},{3,11},{4,12},{5,13},{6,14},{7,15},{8,24},{9,25... | collective-permute-start | bytes 786440 | tf_op jit(solution)/shard_map/ppermute | solution.py:288
  142.7 1.9 %collective-permute-start.25 = (bf16[2,128,1024]{2,1,0:T(8,128)(2,1)S(1)}, bf16[2,128,1024]{2,1,0:T(8,128)(2,1)S(1)}, u32[]{:S(2)}, u32[]{:S(2)}) collective-permute-start(bf16[2,128,1024]{2,1,0:T(8,128)(2,1)S(1)} %slice.135), channel_id=1, source_target_pairs={{0,1},{1,0},{2,6},{3,7},{4,5},{5,4},{6,2},{7,3},{8,9},{9,8},{10,14... | collective-permute-start | bytes 1572872 | tf_op jit(solution)/shard_map/ppermute | solution.py:288
  144.6 3.4 %fusion.1 = bf16[1,384,2048]{2,1,0:T(8,128)(2,1)} fusion(bf16[1152,384]{1,0:T(8,128)(2,1)S(1)} %get-tuple-element.119, bf16[1152,2048]{1,0:T(8,128)(2,1)S(1)} %get-tuple-element.118), kind=kOutput, calls=%fused_computation.4 | convolution fusion | flops 1812725760 | bytes 7176192 | tf_op jit(solution)/shard_map/dot_general | solution.py:347
  148.0 4.0 %collective-permute-done.25 = bf16[2,128,1024]{2,1,0:T(8,128)(2,1)S(1)} collective-permute-done((bf16[2,128,1024]{2,1,0:T(8,128)(2,1)S(1)}, bf16[2,128,1024]{2,1,0:T(8,128)(2,1)S(1)}, u32[]{:S(2)}, u32[]{:S(2)}) %collective-permute-start.25) | collective-permute-done | bytes 524320 | tf_op jit(solution)/shard_map/ppermute | solution.py:288
  152.2 1.1 collective-permute-start.26
  153.2 3.4 %fusion = bf16[1,384,2048]{2,1,0:T(8,128)(2,1)} fusion(bf16[1152,384]{1,0:T(8,128)(2,1)S(1)} %get-tuple-element.117, bf16[1152,2048]{1,0:T(8,128)(2,1)S(1)} %get-tuple-element.118), kind=kOutput, calls=%fused_computation.3 | convolution fusion | flops 1812725760 | bytes 7176192 | tf_op jit(solution)/shard_map/dot_general | solution.py:346
  156.6 2.0 %collective-permute-done.26 = bf16[128,1024]{1,0:T(8,128)(2,1)S(1)} collective-permute-done((bf16[128,1024]{1,0:T(8,128)(2,1)S(1)}, bf16[128,1024]{1,0:T(8,128)(2,1)S(1)}, u32[]{:S(2)}, u32[]{:S(2)}) %collective-permute-start.26) | collective-permute-done | bytes 262176 | tf_op jit(solution)/shard_map/ppermute | solution.py:288
  158.8 3.4 %fusion.2 = bf16[1,384,2048]{2,1,0:T(8,128)(2,1)} fusion(bf16[1152,384]{1,0:T(8,128)(2,1)S(1)} %get-tuple-element.120, bf16[1152,2048]{1,0:T(8,128)(2,1)S(1)} %get-tuple-element.121), kind=kOutput, calls=%fused_computation.5 | convolution fusion | flops 1812725760 | bytes 7176192 | tf_op jit(solution)/shard_map/dot_general | solution.py:345
  162.2 3.9 %collective-permute-done.34 = bf16[128,1024]{1,0:T(8,128)(2,1)S(1)} collective-permute-done((bf16[128,1024]{1,0:T(8,128)(2,1)S(1)}, bf16[128,1024]{1,0:T(8,128)(2,1)S(1)}, u32[]{:S(2)}, u32[]{:S(2)}) %collective-permute-start.34) | collective-permute-done | bytes 262176 | tf_op jit(solution)/shard_map/ppermute | solution.py:288
  (82 shorter events, 12.5 us)
Async XLA Ops:
  2.5 16.2 %collective-permute-start = (bf16[272,1024]{1,0:T(8,128)(2,1)}, bf16[272,1024]{1,0:T(8,128)(2,1)S(1)}, u32[]{:S(2)}, u32[]{:S(2)}) collective-permute-start(bf16[272,1024]{1,0:T(8,128)(2,1)} %pack.1), channel_id=1, source_target_pairs={{0,4},{1,5},{2,3},{3,2},{4,0},{5,1},{6,7},{7,6},{8,12},{9,13},{10,... | collective-permute-start | bytes 1671176 | tf_op jit(solution)/shard_map/ppermute | solution.py:288
  5.5 13.3 %collective-permute-start.1 = (bf16[272,1024]{1,0:T(8,128)(2,1)}, bf16[272,1024]{1,0:T(8,128)(2,1)S(1)}, u32[]{:S(2)}, u32[]{:S(2)}) collective-permute-start(bf16[272,1024]{1,0:T(8,128)(2,1)} %pack.1), channel_id=1, source_target_pairs={{0,1},{1,0},{2,6},{3,7},{4,5},{5,4},{6,2},{7,3},{8,9},{9,8},{10,14... | collective-permute-start | bytes 1671176 | tf_op jit(solution)/shard_map/ppermute | solution.py:288
  7.0 14.9 %collective-permute-start.2 = (bf16[272,1024]{1,0:T(8,128)(2,1)}, bf16[272,1024]{1,0:T(8,128)(2,1)S(1)}, u32[]{:S(2)}, u32[]{:S(2)}) collective-permute-start(bf16[272,1024]{1,0:T(8,128)(2,1)} %pack.1), channel_id=1, source_target_pairs={{0,8},{1,9},{2,10},{3,11},{4,12},{5,13},{6,14},{7,15},{8,24},{9,25... | collective-permute-start | bytes 1671176 | tf_op jit(solution)/shard_map/ppermute | solution.py:288
  21.9 13.7 %collective-permute-start.4 = (bf16[272,1024]{1,0:T(8,128)(2,1)S(1)}, bf16[272,1024]{1,0:T(8,128)(2,1)S(1)}, u32[]{:S(2)}, u32[]{:S(2)}) collective-permute-start(bf16[272,1024]{1,0:T(8,128)(2,1)S(1)} %collective-permute-done.2), channel_id=1, source_target_pairs={{0,4},{1,5},{2,3},{3,2},{4,0},{5,1},{6,7},{7,6},{8,12},{9,13},{10,... | collective-permute-start | bytes 1671176 | tf_op jit(solution)/shard_map/ppermute | solution.py:288
  22.4 13.5 %collective-permute-start.5 = (bf16[272,1024]{1,0:T(8,128)(2,1)S(1)}, bf16[272,1024]{1,0:T(8,128)(2,1)S(1)}, u32[]{:S(2)}, u32[]{:S(2)}) collective-permute-start(bf16[272,1024]{1,0:T(8,128)(2,1)S(1)} %collective-permute-done.2), channel_id=1, source_target_pairs={{0,8},{1,9},{2,10},{3,11},{4,12},{5,13},{6,14},{7,15},{8,24},{9,25... | collective-permute-start | bytes 1671176 | tf_op jit(solution)/shard_map/ppermute | solution.py:288
  23.3 12.7 %collective-permute-start.3 = (bf16[272,1024]{1,0:T(8,128)(2,1)S(1)}, bf16[272,1024]{1,0:T(8,128)(2,1)S(1)}, u32[]{:S(2)}, u32[]{:S(2)}) collective-permute-start(bf16[272,1024]{1,0:T(8,128)(2,1)S(1)} %collective-permute-done), channel_id=1, source_target_pairs={{0,1},{1,0},{2,6},{3,7},{4,5},{5,4},{6,2},{7,3},{8,9},{9,8},{10,14... | collective-permute-start | bytes 1671176 | tf_op jit(solution)/shard_map/ppermute | solution.py:288
  25.0 13.1 %copy-start.3 = (bf16[2,272,1024]{2,1,0:T(8,128)(2,1)}, bf16[2,272,1024]{2,1,0:T(8,128)(2,1)S(1)}, u32[]{:S(2)}) copy-start(bf16[2,272,1024]{2,1,0:T(8,128)(2,1)S(1)} %pad_maximum_fusion.1.refs_0_) | copy-start | bytes 3342340
  25.0 13.1 %collective-permute-start.6 = (bf16[2,272,1024]{2,1,0:T(8,128)(2,1)S(1)}, bf16[2,272,1024]{2,1,0:T(8,128)(2,1)S(1)}, u32[]{:S(2)}, u32[]{:S(2)}) collective-permute-start(bf16[2,272,1024]{2,1,0:T(8,128)(2,1)S(1)} %pad_maximum_fusion.1.refs_0_), channel_id=1, source_target_pairs={{0,2},{1,3},{2,0},{3,1},{4,6},{5,7},{6,4},{7,5},{8,10},{9,11},{10,... | collective-permute-start | bytes 3342344 | tf_op jit(solution)/shard_map/ppermute | solution.py:288
  36.0 0.8 copy-start.11
  36.8 7.3 %copy-start = (bf16[1,384,2048]{2,1,0:T(8,128)(2,1)S(1)}, bf16[1,384,2048]{2,1,0:T(8,128)(2,1)}, u32[]{:S(2)}) copy-start(bf16[1,384,2048]{2,1,0:T(8,128)(2,1)} %param.11) | copy-start | bytes 4718596
  36.8 7.3 %copy-start.1 = (bf16[1,384,2048]{2,1,0:T(8,128)(2,1)S(1)}, bf16[1,384,2048]{2,1,0:T(8,128)(2,1)}, u32[]{:S(2)}) copy-start(bf16[1,384,2048]{2,1,0:T(8,128)(2,1)} %param.12) | copy-start | bytes 4718596
  36.9 1.4 copy-start.5
  36.9 2.8 %collective-permute-start.7 = (bf16[2,272,1024]{2,1,0:T(8,128)(2,1)S(1)}, bf16[2,272,1024]{2,1,0:T(8,128)(2,1)S(1)}, u32[]{:S(2)}, u32[]{:S(2)}) collective-permute-start(bf16[2,272,1024]{2,1,0:T(8,128)(2,1)S(1)} %pad_maximum_fusion.2.refs_1_), channel_id=1, source_target_pairs={{0,2},{1,3},{2,0},{3,1},{4,6},{5,7},{6,4},{7,5},{8,10},{9,11},{10,... | collective-permute-start | bytes 3342344 | tf_op jit(solution)/shard_map/ppermute | solution.py:288
  38.2 1.0 copy-start.7
  39.7 1.0 copy-start.9
  40.7 21.8 %collective-permute-start.9 = (bf16[2,272,1024]{2,1,0:T(8,128)(2,1)}, bf16[2,272,1024]{2,1,0:T(8,128)(2,1)}, u32[]{:S(2)}, u32[]{:S(2)}) collective-permute-start(bf16[2,272,1024]{2,1,0:T(8,128)(2,1)} %pad_maximum_fusion.refs_0_), channel_id=1, source_target_pairs={{0,1},{1,0},{2,6},{3,7},{4,5},{5,4},{6,2},{7,3},{8,9},{9,8},{10,14... | collective-permute-start | bytes 3342344 | tf_op jit(solution)/shard_map/ppermute | solution.py:288
  42.3 16.0 %collective-permute-start.10 = (bf16[272,1024]{1,0:T(8,128)(2,1)}, bf16[272,1024]{1,0:T(8,128)(2,1)S(1)}, u32[]{:S(2)}, u32[]{:S(2)}) collective-permute-start(bf16[272,1024]{1,0:T(8,128)(2,1)} %copy-done.11), channel_id=1, source_target_pairs={{0,4},{1,5},{2,3},{3,2},{4,0},{5,1},{6,7},{7,6},{8,12},{9,13},{10,... | collective-permute-start | bytes 1671176 | tf_op jit(solution)/shard_map/ppermute | solution.py:288
  43.3 15.2 %collective-permute-start.11 = (bf16[272,1024]{1,0:T(8,128)(2,1)}, bf16[272,1024]{1,0:T(8,128)(2,1)S(1)}, u32[]{:S(2)}, u32[]{:S(2)}) collective-permute-start(bf16[272,1024]{1,0:T(8,128)(2,1)} %copy-done.11), channel_id=1, source_target_pairs={{0,8},{1,9},{2,10},{3,11},{4,12},{5,13},{6,14},{7,15},{8,24},{9,25... | collective-permute-start | bytes 1671176 | tf_op jit(solution)/shard_map/ppermute | solution.py:288
  44.1 1.4 copy-start.2
  45.5 1.2 copy-start.4
  46.8 1.2 copy-start.6
  48.0 1.2 copy-start.8
  49.3 1.2 copy-start.10
  57.7 4.8 %collective-permute-start.8 = (bf16[4,128,1024]{2,1,0:T(8,128)(2,1)S(1)}, bf16[4,128,1024]{2,1,0:T(8,128)(2,1)S(1)}, u32[]{:S(2)}, u32[]{:S(2)}) collective-permute-start(bf16[4,128,1024]{2,1,0:T(8,128)(2,1)S(1)} %get-tuple-element.74), channel_id=1, source_target_pairs={{0,2},{1,3},{2,0},{3,1},{4,6},{5,7},{6,4},{7,5},{8,10},{9,11},{10,... | collective-permute-start | bytes 3145736 | tf_op jit(solution)/shard_map/ppermute | solution.py:288
  57.8 5.9 %collective-permute-start.12 = (bf16[2,272,1024]{2,1,0:T(8,128)(2,1)}, bf16[2,272,1024]{2,1,0:T(8,128)(2,1)S(1)}, u32[]{:S(2)}, u32[]{:S(2)}) collective-permute-start(bf16[2,272,1024]{2,1,0:T(8,128)(2,1)} %pad_maximum_fusion.refs_0_), channel_id=1, source_target_pairs={{0,2},{1,3},{2,0},{3,1},{4,6},{5,7},{6,4},{7,5},{8,10},{9,11},{10,... | collective-permute-start | bytes 3342344 | tf_op jit(solution)/shard_map/ppermute | solution.py:288
  62.5 3.0 %collective-permute-start.13 = (bf16[2,272,1024]{2,1,0:T(8,128)(2,1)}, bf16[2,272,1024]{2,1,0:T(8,128)(2,1)S(1)}, u32[]{:S(2)}, u32[]{:S(2)}) collective-permute-start(bf16[2,272,1024]{2,1,0:T(8,128)(2,1)} %collective-permute-done.9.refs_1_), channel_id=1, source_target_pairs={{0,2},{1,3},{2,0},{3,1},{4,6},{5,7},{6,4},{7,5},{8,10},{9,11},{10,... | collective-permute-start | bytes 3342344 | tf_op jit(solution)/shard_map/ppermute | solution.py:288
  62.5 1.1 copy-start.12
  65.5 21.3 %collective-permute-start.15 = (bf16[2,272,1024]{2,1,0:T(8,128)(2,1)S(1)}, bf16[2,272,1024]{2,1,0:T(8,128)(2,1)S(1)}, u32[]{:S(2)}, u32[]{:S(2)}) collective-permute-start(bf16[2,272,1024]{2,1,0:T(8,128)(2,1)S(1)} %pad_maximum_fusion.3.refs_0_), channel_id=1, source_target_pairs={{0,1},{1,0},{2,6},{3,7},{4,5},{5,4},{6,2},{7,3},{8,9},{9,8},{10,14... | collective-permute-start | bytes 3342344 | tf_op jit(solution)/shard_map/ppermute | solution.py:288
  67.0 15.6 %collective-permute-start.16 = (bf16[272,1024]{1,0:T(8,128)(2,1)S(1)}, bf16[272,1024]{1,0:T(8,128)(2,1)S(1)}, u32[]{:S(2)}, u32[]{:S(2)}) collective-permute-start(bf16[272,1024]{1,0:T(8,128)(2,1)S(1)} %collective-permute-done.11), channel_id=1, source_target_pairs={{0,4},{1,5},{2,3},{3,2},{4,0},{5,1},{6,7},{7,6},{8,12},{9,13},{10,... | collective-permute-start | bytes 1671176 | tf_op jit(solution)/shard_map/ppermute | solution.py:288
  68.0 24.5 %collective-permute-start.14 = (bf16[2,128,1024]{2,1,0:T(8,128)(2,1)S(1)}, bf16[2,128,1024]{2,1,0:T(8,128)(2,1)S(1)}, u32[]{:S(2)}, u32[]{:S(2)}) collective-permute-start(bf16[2,128,1024]{2,1,0:T(8,128)(2,1)S(1)} %slice.137), channel_id=1, source_target_pairs={{0,1},{1,0},{2,6},{3,7},{4,5},{5,4},{6,2},{7,3},{8,9},{9,8},{10,14... | collective-permute-start | bytes 1572872 | tf_op jit(solution)/shard_map/ppermute | solution.py:288
  76.8 15.9 %collective-permute-start.17 = (bf16[4,128,1024]{2,1,0:T(8,128)(2,1)S(1)}, bf16[4,128,1024]{2,1,0:T(8,128)(2,1)S(1)}, u32[]{:S(2)}, u32[]{:S(2)}) collective-permute-start(bf16[4,128,1024]{2,1,0:T(8,128)(2,1)S(1)} %get-tuple-element.94), channel_id=1, source_target_pairs={{0,2},{1,3},{2,0},{3,1},{4,6},{5,7},{6,4},{7,5},{8,10},{9,11},{10,... | collective-permute-start | bytes 3145736 | tf_op jit(solution)/shard_map/ppermute | solution.py:288
  76.8 16.4 %collective-permute-start.18 = (bf16[2,272,1024]{2,1,0:T(8,128)(2,1)S(1)}, bf16[2,272,1024]{2,1,0:T(8,128)(2,1)S(1)}, u32[]{:S(2)}, u32[]{:S(2)}) collective-permute-start(bf16[2,272,1024]{2,1,0:T(8,128)(2,1)S(1)} %pad_maximum_fusion.3.refs_0_), channel_id=1, source_target_pairs={{0,2},{1,3},{2,0},{3,1},{4,6},{5,7},{6,4},{7,5},{8,10},{9,11},{10,... | collective-permute-start | bytes 3342344 | tf_op jit(solution)/shard_map/ppermute | solution.py:288
  86.8 6.5 %collective-permute-start.19 = (bf16[2,272,1024]{2,1,0:T(8,128)(2,1)S(1)}, bf16[2,272,1024]{2,1,0:T(8,128)(2,1)S(1)}, u32[]{:S(2)}, u32[]{:S(2)}) collective-permute-start(bf16[2,272,1024]{2,1,0:T(8,128)(2,1)S(1)} %collective-permute-done.15.refs_1_), channel_id=1, source_target_pairs={{0,2},{1,3},{2,0},{3,1},{4,6},{5,7},{6,4},{7,5},{8,10},{9,11},{10,... | collective-permute-start | bytes 3342344 | tf_op jit(solution)/shard_map/ppermute | solution.py:288
  93.3 15.6 %collective-permute-start.21 = (bf16[2,272,1024]{2,1,0:T(8,128)(2,1)S(1)}, bf16[2,272,1024]{2,1,0:T(8,128)(2,1)S(1)}, u32[]{:S(2)}, u32[]{:S(2)}) collective-permute-start(bf16[2,272,1024]{2,1,0:T(8,128)(2,1)S(1)} %pad_maximum_fusion.4.refs_0_), channel_id=1, source_target_pairs={{0,1},{1,0},{2,6},{3,7},{4,5},{5,4},{6,2},{7,3},{8,9},{9,8},{10,14... | collective-permute-start | bytes 3342344 | tf_op jit(solution)/shard_map/ppermute | solution.py:288
  94.8 19.6 %collective-permute-start.30 = (bf16[2,128,1024]{2,1,0:T(8,128)(2,1)S(1)}, bf16[2,128,1024]{2,1,0:T(8,128)(2,1)S(1)}, u32[]{:S(2)}, u32[]{:S(2)}) collective-permute-start(bf16[2,128,1024]{2,1,0:T(8,128)(2,1)S(1)} %slice.136), channel_id=1, source_target_pairs={{0,1},{1,0},{2,6},{3,7},{4,5},{5,4},{6,2},{7,3},{8,9},{9,8},{10,14... | collective-permute-start | bytes 1572872 | tf_op jit(solution)/shard_map/ppermute | solution.py:288
  102.8 13.0 %collective-permute-start.27 = (bf16[4,128,1024]{2,1,0:T(8,128)(2,1)S(1)}, bf16[4,128,1024]{2,1,0:T(8,128)(2,1)S(1)}, u32[]{:S(2)}, u32[]{:S(2)}) collective-permute-start(bf16[4,128,1024]{2,1,0:T(8,128)(2,1)S(1)} %get-tuple-element.115), channel_id=1, source_target_pairs={{0,2},{1,3},{2,0},{3,1},{4,6},{5,7},{6,4},{7,5},{8,10},{9,11},{10,... | collective-permute-start | bytes 3145736 | tf_op jit(solution)/shard_map/ppermute | solution.py:288
  102.8 23.0 %collective-permute-start.22 = (bf16[2,272,1024]{2,1,0:T(8,128)(2,1)S(1)}, bf16[2,272,1024]{2,1,0:T(8,128)(2,1)S(1)}, u32[]{:S(2)}, u32[]{:S(2)}) collective-permute-start(bf16[2,272,1024]{2,1,0:T(8,128)(2,1)S(1)} %pad_maximum_fusion.4.refs_0_), channel_id=1, source_target_pairs={{0,2},{1,3},{2,0},{3,1},{4,6},{5,7},{6,4},{7,5},{8,10},{9,11},{10,... | collective-permute-start | bytes 3342344 | tf_op jit(solution)/shard_map/ppermute | solution.py:288
  108.8 17.0 %collective-permute-start.23 = (bf16[2,272,1024]{2,1,0:T(8,128)(2,1)S(1)}, bf16[2,272,1024]{2,1,0:T(8,128)(2,1)S(1)}, u32[]{:S(2)}, u32[]{:S(2)}) collective-permute-start(bf16[2,272,1024]{2,1,0:T(8,128)(2,1)S(1)} %collective-permute-done.21.refs_1_), channel_id=1, source_target_pairs={{0,2},{1,3},{2,0},{3,1},{4,6},{5,7},{6,4},{7,5},{8,10},{9,11},{10,... | collective-permute-start | bytes 3342344 | tf_op jit(solution)/shard_map/ppermute | solution.py:288
  114.6 9.2 %collective-permute-start.31 = (bf16[128,1024]{1,0:T(8,128)(2,1)S(1)}, bf16[128,1024]{1,0:T(8,128)(2,1)S(1)}, u32[]{:S(2)}, u32[]{:S(2)}) collective-permute-start(bf16[128,1024]{1,0:T(8,128)(2,1)S(1)} %fusion.17), channel_id=1, source_target_pairs={{0,4},{1,5},{2,3},{3,2},{4,0},{5,1},{6,7},{7,6},{8,12},{9,13},{10,... | collective-permute-start | bytes 786440 | tf_op jit(solution)/shard_map/ppermute | solution.py:288
  116.2 16.9 %collective-permute-start.28 = (bf16[2,128,1024]{2,1,0:T(8,128)(2,1)S(1)}, bf16[2,128,1024]{2,1,0:T(8,128)(2,1)S(1)}, u32[]{:S(2)}, u32[]{:S(2)}) collective-permute-start(bf16[2,128,1024]{2,1,0:T(8,128)(2,1)S(1)} %slice.134), channel_id=1, source_target_pairs={{0,1},{1,0},{2,6},{3,7},{4,5},{5,4},{6,2},{7,3},{8,9},{9,8},{10,14... | collective-permute-start | bytes 1572872 | tf_op jit(solution)/shard_map/ppermute | solution.py:288
  123.9 11.5 %collective-permute-start.32 = (bf16[128,1024]{1,0:T(8,128)(2,1)S(1)}, bf16[128,1024]{1,0:T(8,128)(2,1)S(1)}, u32[]{:S(2)}, u32[]{:S(2)}) collective-permute-start(bf16[128,1024]{1,0:T(8,128)(2,1)S(1)} %fusion.4), channel_id=1, source_target_pairs={{0,8},{1,9},{2,10},{3,11},{4,12},{5,13},{6,14},{7,15},{8,24},{9,25... | collective-permute-start | bytes 786440 | tf_op jit(solution)/shard_map/ppermute | solution.py:288
  133.0 9.2 %collective-permute-start.24 = (bf16[4,128,1024]{2,1,0:T(8,128)(2,1)S(1)}, bf16[4,128,1024]{2,1,0:T(8,128)(2,1)S(1)}, u32[]{:S(2)}, u32[]{:S(2)}) collective-permute-start(bf16[4,128,1024]{2,1,0:T(8,128)(2,1)S(1)} %get-tuple-element.113), channel_id=1, source_target_pairs={{0,2},{1,3},{2,0},{3,1},{4,6},{5,7},{6,4},{7,5},{8,10},{9,11},{10,... | collective-permute-start | bytes 3145736 | tf_op jit(solution)/shard_map/ppermute | solution.py:288
  133.3 6.4 %collective-permute-start.29 = (bf16[128,1024]{1,0:T(8,128)(2,1)S(1)}, bf16[128,1024]{1,0:T(8,128)(2,1)S(1)}, u32[]{:S(2)}, u32[]{:S(2)}) collective-permute-start(bf16[128,1024]{1,0:T(8,128)(2,1)S(1)} %fusion.16), channel_id=1, source_target_pairs={{0,4},{1,5},{2,3},{3,2},{4,0},{5,1},{6,7},{7,6},{8,12},{9,13},{10,... | collective-permute-start | bytes 786440 | tf_op jit(solution)/shard_map/ppermute | solution.py:288
  134.5 27.7 %collective-permute-start.20 = (bf16[128,1024]{1,0:T(8,128)(2,1)S(1)}, bf16[128,1024]{1,0:T(8,128)(2,1)S(1)}, u32[]{:S(2)}, u32[]{:S(2)}) collective-permute-start(bf16[128,1024]{1,0:T(8,128)(2,1)S(1)} %fusion.14), channel_id=1, source_target_pairs={{0,4},{1,5},{2,3},{3,2},{4,0},{5,1},{6,7},{7,6},{8,12},{9,13},{10,... | collective-permute-start | bytes 786440 | tf_op jit(solution)/shard_map/ppermute | solution.py:288
  139.9 16.7 %collective-permute-start.33 = (bf16[128,1024]{1,0:T(8,128)(2,1)S(1)}, bf16[128,1024]{1,0:T(8,128)(2,1)S(1)}, u32[]{:S(2)}, u32[]{:S(2)}) collective-permute-start(bf16[128,1024]{1,0:T(8,128)(2,1)S(1)} %fusion.7), channel_id=1, source_target_pairs={{0,8},{1,9},{2,10},{3,11},{4,12},{5,13},{6,14},{7,15},{8,24},{9,25... | collective-permute-start | bytes 786440 | tf_op jit(solution)/shard_map/ppermute | solution.py:288
  142.7 9.2 %collective-permute-start.25 = (bf16[2,128,1024]{2,1,0:T(8,128)(2,1)S(1)}, bf16[2,128,1024]{2,1,0:T(8,128)(2,1)S(1)}, u32[]{:S(2)}, u32[]{:S(2)}) collective-permute-start(bf16[2,128,1024]{2,1,0:T(8,128)(2,1)S(1)} %slice.135), channel_id=1, source_target_pairs={{0,1},{1,0},{2,6},{3,7},{4,5},{5,4},{6,2},{7,3},{8,9},{9,8},{10,14... | collective-permute-start | bytes 1572872 | tf_op jit(solution)/shard_map/ppermute | solution.py:288
  152.2 6.4 %collective-permute-start.26 = (bf16[128,1024]{1,0:T(8,128)(2,1)S(1)}, bf16[128,1024]{1,0:T(8,128)(2,1)S(1)}, u32[]{:S(2)}, u32[]{:S(2)}) collective-permute-start(bf16[128,1024]{1,0:T(8,128)(2,1)S(1)} %fusion.15), channel_id=1, source_target_pairs={{0,4},{1,5},{2,3},{3,2},{4,0},{5,1},{6,7},{7,6},{8,12},{9,13},{10,... | collective-permute-start | bytes 786440 | tf_op jit(solution)/shard_map/ppermute | solution.py:288
  158.7 7.3 %collective-permute-start.34 = (bf16[128,1024]{1,0:T(8,128)(2,1)S(1)}, bf16[128,1024]{1,0:T(8,128)(2,1)S(1)}, u32[]{:S(2)}, u32[]{:S(2)}) collective-permute-start(bf16[128,1024]{1,0:T(8,128)(2,1)S(1)} %fusion.10), channel_id=1, source_target_pairs={{0,8},{1,9},{2,10},{3,11},{4,12},{5,13},{6,14},{7,15},{8,24},{9,25... | collective-permute-start | bytes 786440 | tf_op jit(solution)/shard_map/ppermute | solution.py:288

commit v5 on v4

--- a/solution.py
+++ b/solution.py
@@ -10,7 +10,7 @@
 CONTRACT_LAST = (((1,), (1,)), ((), ()))
 CONTRACT_FIRST = (((0,), (0,)), ((), ()))
 INFO_ROWS = 16
-VMEM_LIMIT = 24 * 1024 * 1024
+VMEM_LIMIT = 16 * 1024 * 1024
 
 
 def pack_rows(token_rows, grad_rows, token_of, scale, is_live):
@@ -136,9 +136,9 @@
 
 
 def expert_kernel(index, chained, top, rows, place_ref, *refs):
-    pair_refs = refs[:4]
-    wg_ref, wu_ref, wd_ref = refs[4:7]
-    refs = refs[7 + (5 if chained else 0):]
+    shares = refs[:4], refs[4:8]
+    wg_ref, wu_ref, wd_ref = refs[8:11]
+    refs = refs[11 + (5 if chained else 0):]
     near_ref, far_ref = refs[:2]
     kept_refs = refs[2:7]
     rx_ref, rg_ref, act_ref, gt_ref, ut_ref, slot_ref, sems = refs[7:]
@@ -163,13 +163,10 @@
         return core == 1 if p == 0 else core == 0
 
     def gathered(p, h, part):
-        here = pl.ds(part * rows, rows)
-        first, second = pair_refs[2 * p], pair_refs[2 * p + 1]
+        own, first, second, both = [ref[pl.ds(part * rows, rows)] for ref in shares[p]]
         if h == 0:
-            inner = jnp.where(swapped(p), second[0, here], first[1, here])
-            return jnp.concatenate([first[0, here], inner], axis=0)
-        inner = jnp.where(swapped(p), first[1, here], second[0, here])
-        return jnp.concatenate([inner, second[1, here]], axis=0)
+            return jnp.concatenate([own, jnp.where(swapped(p), second, first)], axis=0)
+        return jnp.concatenate([jnp.where(swapped(p), first, second), both], axis=0)
 
     earlier = (
         lax.broadcasted_iota(jnp.int32, (2 * rows, 2 * rows), 0)
@@ -178,10 +175,10 @@
     picks, scales = [], []
     for p in range(2):
         named, weights = [], []
-        for pair_ref, s in ((pair_refs[2 * p], 0), (pair_refs[2 * p + 1], 1)):
+        for share_ref in (shares[p][0], shares[p][3]):
             hits, weight = 0.0, 0.0
             for k in range(top):
-                info = pair_ref[s, pl.ds(2 * rows, INFO_ROWS), k * rows:(k + 1) * rows].astype(jnp.float32)
+                info = share_ref[pl.ds(2 * rows, INFO_ROWS), k * rows:(k + 1) * rows].astype(jnp.float32)
                 hit = info[0:1] == me
                 hits += hit.astype(jnp.float32)
                 weight += jnp.where(hit, info[1:2] + info[2:3] + info[3:4], 0.0)
@@ -239,18 +236,18 @@
         move.wait()
 
 
-def run_experts(index, chunks, place, pairs, weights, kept, top, rows, slots):
-    width = pairs[0].shape[2]
+def run_experts(index, chunks, place, shares, weights, kept, top, rows, slots):
+    width = shares[0].shape[1]
     hidden, features = weights[0].shape
     anywhere = pl.BlockSpec(memory_space=pl.ANY)
     vmem = pl.BlockSpec(memory_space=pltpu.VMEM)
     part = jax.ShapeDtypeStruct((4, rows, width), jnp.bfloat16)
     wide = jax.ShapeDtypeStruct((chunks * slots, features), jnp.bfloat16)
     narrow = jax.ShapeDtypeStruct((chunks * slots, hidden), jnp.bfloat16)
-    first_kept = 1 + len(pairs) + 3
+    first_kept = 1 + len(shares) + 3
     return pl.pallas_call(
         functools.partial(expert_kernel, index, kept is not None, top, rows),
-        in_specs=[pl.BlockSpec(memory_space=pltpu.SMEM)] + [vmem] * 7 + [anywhere] * (0 if kept is None else 5),
+        in_specs=[pl.BlockSpec(memory_space=pltpu.SMEM)] + [vmem] * 11 + [anywhere] * (0 if kept is None else 5),
         out_specs=[vmem] * 2 + [anywhere] * 5,
         out_shape=[part, part, wide, wide, narrow, narrow, narrow],
         scratch_shapes=[pltpu.VMEM((slots, features), jnp.bfloat16)] * 2
@@ -259,12 +256,12 @@
         input_output_aliases={} if kept is None else {first_kept + i: 2 + i for i in range(5)},
         compiler_params=pltpu.CompilerParams(vmem_limit_bytes=VMEM_LIMIT),
         cost_estimate=pl.CostEstimate(
-            flops=2 * slots * features * (hidden * 5 + 2 * rows * 3),
-            bytes_accessed=2 * (4 * pairs[0].size + 3 * hidden * features + slots * (2 * features + 3 * hidden)),
+            flops=4 * slots * features * (hidden * 5 + 2 * rows * 3),
+            bytes_accessed=2 * (8 * shares[0].size + 3 * hidden * features + slots * (2 * features + 3 * hidden)),
             transcendentals=slots * hidden,
         ),
         name="experts",
-    )(place, *pairs, *weights, *(kept or ()))
+    )(place, *shares, *weights, *(kept or ()))
 
 
 def ring_order(length):
@@ -303,37 +300,58 @@
     place = jnp.stack([me, lax.axis_index("etp"), me % 2]).astype(jnp.int32)
     weights = (w_gate[0], w_up[0], w_down[0])
     share = pack_share(tokens, out_grad, routes, combine)
-    together = lax.optimization_barrier
-    kept = None
-    sums, sends, running = [], [], None
-    first, second, following = together((to_first(share), to_second(share), to_ring(share)))
-    pair, share = jnp.stack([share, first]), following
+    def crossed_sums(near_part, far_part, beside=()):
+        mine = near_part.astype(jnp.float32) + to_core(far_part).astype(jnp.float32)
+        mine, send = mine[:2], mine[2:].astype(jnp.bfloat16)
+        send, beside = lax.optimization_barrier((send, beside))
+        mine = mine + to_second(send).astype(jnp.float32)
+        return mine[0], mine[1].astype(jnp.bfloat16), beside
+
+    ring_sends = [("s", 1)] + [(kind, c) for c in range(2, chunks) for kind in ("s", "f")]
+    ring_sends = [key for key in ring_sends if key[1] < chunks]
+    plane_sends = [("f", 0), ("a", 0), ("f", 1), ("b", 0)] + [(kind, c) for c in range(1, chunks) for kind in ("a", "b")]
+    plane_sends = [key for key in plane_sends if key[1] < chunks]
+    have, crossed, fresh = {("s", 0): share}, {}, [("s", 0)]
+    kept, done, parts = None, 0, None
+    sums, sends = [], []
+    while done < chunks:
+        came = {}
+        planned = [key for key in plane_sends if (("f" if key[0] == "b" else "s"), key[1]) in have][:2]
+        for kind, c in planned:
+            source = have["f" if kind == "b" else "s", c]
+            came[kind, c] = to_first(source) if kind == "f" else to_second(source)
+            plane_sends.remove((kind, c))
+        if ring_sends and (ring_sends[0][0], ring_sends[0][1] - 1) in have:
+            kind, c = ring_sends.pop(0)
+            came[kind, c] = to_ring(have[kind, c - 1])
+        swaps = {key: to_core(have[key]) for key in fresh}
+        for i in range(len(sums)):
+            if sends[i] is not None:
+                sums[i], sends[i] = sums[i] + to_first(sends[i]).astype(jnp.float32), None
+        if parts is not None:
+            mine, send, _ = crossed_sums(*parts)
+            sums.append(mine)
+            sends.append(send)
+            parts = None
+        members = [(kind, done) for kind in "sfab"]
+        near = [have[key] for key in members if key in have]
+        far = [crossed.get(key, swaps.get(key) if done + 1 == chunks else None) for key in members]
+        if len(near) == 4 and all(value is not None for value in far):
+            near_part, far_part, *kept = run_experts(
+                done, chunks, place, near + far, weights, kept, top, rows, slots
+            )
+            parts = near_part, far_part
+            done += 1
+        if done < chunks:
+            came, swaps, sends, parts = lax.optimization_barrier((came, swaps, sends, parts))
+        fresh = list(came)
+        have.update(came)
+        crossed.update(swaps)
+    mine, send, sends = crossed_sums(*parts, sends)
+    sums.append(mine)
+    sends.append(send)
+    running = None
     for c in range(chunks):
-        moved = to_second(first if c == 0 else pair)
-        if c + 1 < chunks:
-            following = to_ring(share) if c + 2 < chunks else None
-            moved, first, following = together((moved, to_first(share), following))
-        second = jnp.stack([second, moved]) if c == 0 else moved
-        ready = [pair, second, to_core(pair), to_core(second)]
-        if c + 1 < chunks:
-            pair = jnp.stack([share, first])
-            pair, share, sends, *ready = together((pair, following, sends, *ready))
-        near_part, far_part, *kept = run_experts(
-            c, chunks, place, ready, weights, kept, top, rows, slots
-        )
-        for i in range(len(sums)):
-            if sums[i].ndim == 3:
-                sums[i] = sums[i] + to_second(sends[i]).astype(jnp.float32)
-                sums[i], sends[i] = sums[i][0], sums[i][1].astype(jnp.bfloat16)
-            elif sends[i] is not None:
-                sums[i], sends[i] = sums[i] + to_first(sends[i]).astype(jnp.float32), None
-        mine = near_part.astype(jnp.float32) + to_core(far_part).astype(jnp.float32)
-        sums.append(mine[:2])
-        sends.append(mine[2:].astype(jnp.bfloat16))
-    for c in range(chunks):
-        if sums[c].ndim == 3:
-            sums[c] = sums[c] + to_second(sends[c]).astype(jnp.float32)
-            sums[c], sends[c] = sums[c][0], sums[c][1].astype(jnp.bfloat16)
         if sends[c] is not None:
             sums[c] = sums[c] + to_first(sends[c]).astype(jnp.float32)
         if c > 0:

time: 167 us -> 167 us (level)
  waiting for transfers between devices: 77.2 us -> 69.6 us
  local copies, waits for them, and re-layouts: 10.3 us -> 15.8 us
  starting transfers between devices: 30.3 us -> 34.1 us
  other arithmetic: 5.93 us -> 3.41 us
    ppermute x35 -> x46, waiting for transfers between devices: 77.2 us -> 69.6 us  [permute(): return lax.ppermute(value, ('expert', 'etp'), pairs)]
    unnamed x26 -> x38, local copies, waits for them, and re-layouts: 9.92 us -> 15.4 us
    ppermute x35 -> x46, starting transfers between devices: 30.3 us -> 34.1 us  [permute(): return lax.ppermute(value, ('expert', 'etp'), pairs)]
    another operation x5 -> x0, other arithmetic: 2.59 us -> none  [the longest x3 1.33 us: gather_body(): pair = jnp.stack([share, first])]
  transfers between devices with their start and end apart: 35 -> 46, of which waited for: 18 -> 17; matrix products, arithmetic and copies ran while one was open for 9% -> 8% of each run, Pallas kernels for 18% -> 18%
where the time goes in v5:
time: 167 us
  waiting for transfers between devices  69.6 us (42%)
  starting transfers between devices  34.1 us (20%)
  Pallas kernels  32.4 us (19%)
  local copies, waits for them, and re-layouts  15.8 us (9%)
  matrix products  10.1 us (6%)
  other arithmetic  3.41 us (2%)
    ppermute x46, waiting for transfers between devices, permute(): return lax.ppermute(value, ('expert', 'etp'), pairs)  69.6 us
    ppermute x46, starting transfers between devices, permute(): return lax.ppermute(value, ('expert', 'etp'), pairs)  34.1 us
    pallas_call x4, Pallas kernels, run_experts(): pl.pallas_call(functools.partial(expert_kernel, index, kept is not None,...  30.6 us
    unnamed x38, local copies, waits for them, and re-layouts  15.4 us
    dot_general x1, matrix products, gather_body(): lax.dot_general(acts, rows_g, CONTRACT_FIRST, preferred_element_type=jnp....  3.38 us
    dot_general x1, matrix products, gather_body(): lax.dot_general(up_term, rows_x, CONTRACT_FIRST, preferred_element_type=j...  3.38 us
    dot_general x1, matrix products, gather_body(): lax.dot_general(gate_term, rows_x, CONTRACT_FIRST, preferred_element_type...  3.38 us
  transfers between devices with their start and end apart: 46, of which 17 were waited for; matrix products, arithmetic and copies ran while one was open for 8% of the time, Pallas kernels for 18%

profile of v5, /device:TPU:0, one launch (start us, length us, event | category | flops | bytes accessed | tf_op | source)
XLA Modules:
  0.0 166.5 jit_solution(86605619563589391)
XLA Ops:
  0.6 1.9 %pack.1.refs_0_ = bf16[272,1024]{1,0:T(8,128)(2,1)} custom-call(bf16[128,1024]{1,0:T(8,128)(2,1)} %tokens_ref.1, bf16[128,1024]{1,0:T(8,128)(2,1)} %grads_ref.1, s32[8,128]{1,0:T(8,128)} %bitcast.70, f32[8,128]{1,0:T(8,128)} %bitcast.71), custom_call_target="tpu_custom_call" | custom-call | bytes 1048576 | tf_op jit(solution)/shard_map/pack/pallas_call | solution.py:128
  2.5 2.9 %collective-permute-start = (bf16[272,1024]{1,0:T(8,128)(2,1)}, bf16[272,1024]{1,0:T(8,128)(2,1)S(1)}, u32[]{:S(2)}, u32[]{:S(2)}) collective-permute-start(bf16[272,1024]{1,0:T(8,128)(2,1)} %pack.1.refs_0_), channel_id=1, source_target_pairs={{0,1},{1,0},{2,6},{3,7},{4,5},{5,4},{6,2},{7,3},{8,9},{9,8},{10,14... | collective-permute-start | bytes 1671176 | tf_op jit(solution)/shard_map/ppermute | solution.py:285
  5.5 1.5 collective-permute-start.1
  7.0 1.6 collective-permute-start.2
  8.6 10.1 %collective-permute-done.refs_2_ = bf16[272,1024]{1,0:T(8,128)(2,1)S(1)} collective-permute-done((bf16[272,1024]{1,0:T(8,128)(2,1)}, bf16[272,1024]{1,0:T(8,128)(2,1)S(1)}, u32[]{:S(2)}, u32[]{:S(2)}) %collective-permute-start) | collective-permute-done | bytes 557088 | tf_op jit(solution)/shard_map/ppermute | solution.py:285
  18.7 3.2 %collective-permute-done.2.refs_0_ = bf16[272,1024]{1,0:T(8,128)(2,1)S(1)} collective-permute-done((bf16[272,1024]{1,0:T(8,128)(2,1)}, bf16[272,1024]{1,0:T(8,128)(2,1)S(1)}, u32[]{:S(2)}, u32[]{:S(2)}) %collective-permute-start.2) | collective-permute-done | bytes 557088 | tf_op jit(solution)/shard_map/ppermute | solution.py:285
  23.2 0.9 collective-permute-start.6
  24.7 1.2 collective-permute-start.8
  26.7 10.7 %collective-permute-done.5.refs_1_ = bf16[272,1024]{1,0:T(8,128)(2,1)S(1)} collective-permute-done((bf16[272,1024]{1,0:T(8,128)(2,1)S(1)}, bf16[272,1024]{1,0:T(8,128)(2,1)S(1)}, u32[]{:S(2)}, u32[]{:S(2)}) %collective-permute-start.5) | collective-permute-done | bytes 557088 | tf_op jit(solution)/shard_map/ppermute | solution.py:285
  41.1 1.5 collective-permute-start.12
  43.1 4.6 %collective-permute-done.11.refs_2_ = bf16[272,1024]{1,0:T(8,128)(2,1)S(1)} collective-permute-done((bf16[272,1024]{1,0:T(8,128)(2,1)S(1)}, bf16[272,1024]{1,0:T(8,128)(2,1)S(1)}, u32[]{:S(2)}, u32[]{:S(2)}) %collective-permute-start.11) | collective-permute-done | bytes 557088 | tf_op jit(solution)/shard_map/ppermute | solution.py:285
  47.7 6.1 %collective-permute-done.12.refs_3_ = bf16[272,1024]{1,0:T(8,128)(2,1)} collective-permute-done((bf16[272,1024]{1,0:T(8,128)(2,1)S(1)}, bf16[272,1024]{1,0:T(8,128)(2,1)}, u32[]{:S(2)}, u32[]{:S(2)}) %collective-permute-start.12) | collective-permute-done | bytes 557088 | tf_op jit(solution)/shard_map/ppermute | solution.py:285
  54.4 3.6 %collective-permute-done.13.refs_1_ = bf16[272,1024]{1,0:T(8,128)(2,1)S(1)} collective-permute-done((bf16[272,1024]{1,0:T(8,128)(2,1)S(1)}, bf16[272,1024]{1,0:T(8,128)(2,1)S(1)}, u32[]{:S(2)}, u32[]{:S(2)}) %collective-permute-start.13) | collective-permute-done | bytes 557088 | tf_op jit(solution)/shard_map/ppermute | solution.py:285
  58.0 1.6 collective-permute-start.18
  60.7 2.6 %collective-permute-done.10.refs_2_ = bf16[272,1024]{1,0:T(8,128)(2,1)S(1)} collective-permute-done((bf16[272,1024]{1,0:T(8,128)(2,1)S(1)}, bf16[272,1024]{1,0:T(8,128)(2,1)S(1)}, u32[]{:S(2)}, u32[]{:S(2)}) %collective-permute-start.10) | collective-permute-done | bytes 557088 | tf_op jit(solution)/shard_map/ppermute | solution.py:285
  63.3 1.1 copy-done
  64.3 1.4 copy-done.1
  65.7 1.4 copy-done.3
  67.2 1.4 copy-done.4
  68.6 1.1 copy-done.10
  69.6 1.1 copy-done.12
  70.7 1.1 copy-done.14
  71.7 1.1 copy-done.16
  72.8 1.1 copy-done.18
  73.8 7.9 %experts.4 = (bf16[4,128,1024]{2,1,0:T(8,128)(2,1)S(1)}, bf16[4,128,1024]{2,1,0:T(8,128)(2,1)S(1)}, bf16[1152,2048]{1,0:T(8,128)(2,1)S(1)}, bf16[1152,2048]{1,0:...) custom-call(s32[3]{0:T(128)S(1)} %pad_add_fusion.place_ref, ...), custom_call_target="tpu_custom_call" | custom-call | flops 6341787648 | bytes 12197888 | tf_op jit(solution)/shard_map/experts/pallas_call | solution.py:248
  82.4 2.3 %collective-permute-done.22 = bf16[4,128,1024]{2,1,0:T(8,128)(2,1)S(1)} collective-permute-done((bf16[4,128,1024]{2,1,0:T(8,128)(2,1)S(1)}, bf16[4,128,1024]{2,1,0:T(8,128)(2,1)S(1)}, u32[]{:S(2)}, u32[]{:S(2)}) %collective-permute-start.22) | collective-permute-done | bytes 1048608 | tf_op jit(solution)/shard_map/ppermute | solution.py:285
  85.7 1.8 %collective-permute-start.25 = (bf16[272,1024]{1,0:T(8,128)(2,1)S(1)}, bf16[272,1024]{1,0:T(8,128)(2,1)S(1)}, u32[]{:S(2)}, u32[]{:S(2)}) collective-permute-start(bf16[272,1024]{1,0:T(8,128)(2,1)S(1)} %collective-permute-done.13.refs_1_), channel_id=1, source_target_pairs={{0,8},{1,9},{2,10},{3,11},{4,12},{5,13},{6,14},{7,15},{8,24},{9,25... | collective-permute-start | bytes 1671176 | tf_op jit(solution)/shard_map/ppermute | solution.py:285
  88.6 5.8 %collective-permute-done.23 = bf16[2,128,1024]{2,1,0:T(8,128)(2,1)S(1)} collective-permute-done((bf16[2,128,1024]{2,1,0:T(8,128)(2,1)S(1)}, bf16[2,128,1024]{2,1,0:T(8,128)(2,1)S(1)}, u32[]{:S(2)}, u32[]{:S(2)}) %collective-permute-start.23) | collective-permute-done | bytes 524320 | tf_op jit(solution)/shard_map/ppermute | solution.py:285
  94.4 8.1 %experts.5 = (bf16[4,128,1024]{2,1,0:T(8,128)(2,1)S(1)}, bf16[4,128,1024]{2,1,0:T(8,128)(2,1)S(1)}, bf16[1152,2048]{1,0:T(8,128)(2,1)S(1)}, bf16[1152,2048]{1,0:...) custom-call(s32[3]{0:T(128)S(1)} %pad_add_fusion.place_ref, ...), custom_call_target="tpu_custom_call", output_to_operand_aliasing={{2}: (12, {}), {3}: (13, {}), {4}: (14, {}), {5}: (15, {}),... | custom-call | flops 6341787648 | bytes 12197888 | tf_op jit(solution)/shard_map/experts/pallas_call | solution.py:248
  104.4 1.2 collective-permute-done.33
  106.7 7.2 %experts.6 = (bf16[4,128,1024]{2,1,0:T(8,128)(2,1)S(1)}, bf16[4,128,1024]{2,1,0:T(8,128)(2,1)S(1)}, bf16[1152,2048]{1,0:T(8,128)(2,1)S(1)}, bf16[1152,2048]{1,0:...) custom-call(s32[3]{0:T(128)S(1)} %pad_add_fusion.place_ref, ...), custom_call_target="tpu_custom_call", output_to_operand_aliasing={{2}: (12, {}), {3}: (13, {}), {4}: (14, {}), {5}: (15, {}),... | custom-call | flops 6341787648 | bytes 12197888 | tf_op jit(solution)/shard_map/experts/pallas_call | solution.py:248
  113.9 4.6 %collective-permute-done.34 = bf16[2,128,1024]{2,1,0:T(8,128)(2,1)S(1)} collective-permute-done((bf16[2,128,1024]{2,1,0:T(8,128)(2,1)S(1)}, bf16[2,128,1024]{2,1,0:T(8,128)(2,1)S(1)}, u32[]{:S(2)}, u32[]{:S(2)}) %collective-permute-start.34) | collective-permute-done | bytes 524320 | tf_op jit(solution)/shard_map/ppermute | solution.py:285
  119.3 2.1 %collective-permute-done.37 = bf16[4,128,1024]{2,1,0:T(8,128)(2,1)S(1)} collective-permute-done((bf16[4,128,1024]{2,1,0:T(8,128)(2,1)S(1)}, bf16[4,128,1024]{2,1,0:T(8,128)(2,1)S(1)}, u32[]{:S(2)}, u32[]{:S(2)}) %collective-permute-start.37) | collective-permute-done | bytes 1048608 | tf_op jit(solution)/shard_map/ppermute | solution.py:285
  122.5 7.4 %experts.7 = (bf16[4,128,1024]{2,1,0:T(8,128)(2,1)S(1)}, bf16[4,128,1024]{2,1,0:T(8,128)(2,1)S(1)}, bf16[1152,2048]{1,0:T(8,128)(2,1)S(1)}, bf16[1152,2048]{1,0:...) custom-call(s32[3]{0:T(128)S(1)} %pad_add_fusion.place_ref, ...), custom_call_target="tpu_custom_call", output_to_operand_aliasing={{2}: (12, {}), {3}: (13, {}), {4}: (14, {}), {5}: (15, {}),... | custom-call | flops 6341787648 | bytes 12197888 | tf_op jit(solution)/shard_map/experts/pallas_call | solution.py:248
  130.0 1.3 collective-permute-start.42
  132.1 4.3 %collective-permute-done.42 = bf16[128,1024]{1,0:T(8,128)(2,1)S(1)} collective-permute-done((bf16[128,1024]{1,0:T(8,128)(2,1)S(1)}, bf16[128,1024]{1,0:T(8,128)(2,1)S(1)}, u32[]{:S(2)}, u32[]{:S(2)}) %collective-permute-start.42) | collective-permute-done | bytes 262176 | tf_op jit(solution)/shard_map/ppermute | solution.py:285
  136.5 1.8 %collective-permute-start.43 = (bf16[128,1024]{1,0:T(8,128)(2,1)S(1)}, bf16[128,1024]{1,0:T(8,128)(2,1)S(1)}, u32[]{:S(2)}, u32[]{:S(2)}) collective-permute-start(bf16[128,1024]{1,0:T(8,128)(2,1)S(1)} %fusion.4), channel_id=1, source_target_pairs={{0,8},{1,9},{2,10},{3,11},{4,12},{5,13},{6,14},{7,15},{8,24},{9,25... | collective-permute-start | bytes 786440 | tf_op jit(solution)/shard_map/ppermute | solution.py:285
  139.5 1.5 collective-permute-start.39
  141.0 3.4 %fusion.1 = bf16[1,384,2048]{2,1,0:T(8,128)(2,1)} fusion(bf16[1152,384]{1,0:T(8,128)(2,1)S(1)} %get-tuple-element.137, bf16[1152,2048]{1,0:T(8,128)(2,1)S(1)} %get-tuple-element.136), kind=kOutput, calls=%fused_computation.4 | convolution fusion | flops 1812725760 | bytes 7176192 | tf_op jit(solution)/shard_map/dot_general | solution.py:365
  144.3 0.9 collective-permute-done.43
  145.3 3.1 %collective-permute-done.41 = bf16[128,1024]{1,0:T(8,128)(2,1)S(1)} collective-permute-done((bf16[128,1024]{1,0:T(8,128)(2,1)S(1)}, bf16[128,1024]{1,0:T(8,128)(2,1)S(1)}, u32[]{:S(2)}, u32[]{:S(2)}) %collective-permute-start.41) | collective-permute-done | bytes 262176 | tf_op jit(solution)/shard_map/ppermute | solution.py:285
  148.5 3.1 %collective-permute-start.44 = (bf16[128,1024]{1,0:T(8,128)(2,1)S(1)}, bf16[128,1024]{1,0:T(8,128)(2,1)S(1)}, u32[]{:S(2)}, u32[]{:S(2)}) collective-permute-start(bf16[128,1024]{1,0:T(8,128)(2,1)S(1)} %fusion.7), channel_id=1, source_target_pairs={{0,8},{1,9},{2,10},{3,11},{4,12},{5,13},{6,14},{7,15},{8,24},{9,25... | collective-permute-start | bytes 786440 | tf_op jit(solution)/shard_map/ppermute | solution.py:285
  151.9 1.5 collective-permute-start.40
  153.3 3.4 %fusion = bf16[1,384,2048]{2,1,0:T(8,128)(2,1)} fusion(bf16[1152,384]{1,0:T(8,128)(2,1)S(1)} %get-tuple-element.135, bf16[1152,2048]{1,0:T(8,128)(2,1)S(1)} %get-tuple-element.136), kind=kOutput, calls=%fused_computation.3 | convolution fusion | flops 1812725760 | bytes 7176192 | tf_op jit(solution)/shard_map/dot_general | solution.py:364
  156.7 1.6 collective-permute-done.40
  158.4 1.2 collective-permute-start.45
  159.7 3.4 %fusion.2 = bf16[1,384,2048]{2,1,0:T(8,128)(2,1)} fusion(bf16[1152,384]{1,0:T(8,128)(2,1)S(1)} %get-tuple-element.138, bf16[1152,2048]{1,0:T(8,128)(2,1)S(1)} %get-tuple-element.139), kind=kOutput, calls=%fused_computation.5 | convolution fusion | flops 1812725760 | bytes 7176192 | tf_op jit(solution)/shard_map/dot_general | solution.py:363
  163.0 2.7 %collective-permute-done.45 = bf16[128,1024]{1,0:T(8,128)(2,1)S(1)} collective-permute-done((bf16[128,1024]{1,0:T(8,128)(2,1)S(1)}, bf16[128,1024]{1,0:T(8,128)(2,1)S(1)}, u32[]{:S(2)}, u32[]{:S(2)}) %collective-permute-start.45) | collective-permute-done | bytes 262176 | tf_op jit(solution)/shard_map/ppermute | solution.py:285
  (111 shorter events, 19.3 us)
Async XLA Ops:
  2.5 16.2 %collective-permute-start = (bf16[272,1024]{1,0:T(8,128)(2,1)}, bf16[272,1024]{1,0:T(8,128)(2,1)S(1)}, u32[]{:S(2)}, u32[]{:S(2)}) collective-permute-start(bf16[272,1024]{1,0:T(8,128)(2,1)} %pack.1.refs_0_), channel_id=1, source_target_pairs={{0,1},{1,0},{2,6},{3,7},{4,5},{5,4},{6,2},{7,3},{8,9},{9,8},{10,14... | collective-permute-start | bytes 1671176 | tf_op jit(solution)/shard_map/ppermute | solution.py:285
  5.5 13.2 %collective-permute-start.1 = (bf16[272,1024]{1,0:T(8,128)(2,1)}, bf16[272,1024]{1,0:T(8,128)(2,1)S(1)}, u32[]{:S(2)}, u32[]{:S(2)}) collective-permute-start(bf16[272,1024]{1,0:T(8,128)(2,1)} %pack.1.refs_0_), channel_id=1, source_target_pairs={{0,4},{1,5},{2,3},{3,2},{4,0},{5,1},{6,7},{7,6},{8,12},{9,13},{10,... | collective-permute-start | bytes 1671176 | tf_op jit(solution)/shard_map/ppermute | solution.py:285
  7.0 14.9 %collective-permute-start.2 = (bf16[272,1024]{1,0:T(8,128)(2,1)}, bf16[272,1024]{1,0:T(8,128)(2,1)S(1)}, u32[]{:S(2)}, u32[]{:S(2)}) collective-permute-start(bf16[272,1024]{1,0:T(8,128)(2,1)} %pack.1.refs_0_), channel_id=1, source_target_pairs={{0,8},{1,9},{2,10},{3,11},{4,12},{5,13},{6,14},{7,15},{8,24},{9,25... | collective-permute-start | bytes 1671176 | tf_op jit(solution)/shard_map/ppermute | solution.py:285
  8.6 13.4 %collective-permute-start.3 = (bf16[272,1024]{1,0:T(8,128)(2,1)}, bf16[272,1024]{1,0:T(8,128)(2,1)S(1)}, u32[]{:S(2)}, u32[]{:S(2)}) collective-permute-start(bf16[272,1024]{1,0:T(8,128)(2,1)} %pack.1.refs_0_), channel_id=1, source_target_pairs={{0,2},{1,3},{2,0},{3,1},{4,6},{5,7},{6,4},{7,5},{8,10},{9,11},{10,... | collective-permute-start | bytes 1671176 | tf_op jit(solution)/shard_map/ppermute | solution.py:285
  22.7 14.6 %collective-permute-start.5 = (bf16[272,1024]{1,0:T(8,128)(2,1)S(1)}, bf16[272,1024]{1,0:T(8,128)(2,1)S(1)}, u32[]{:S(2)}, u32[]{:S(2)}) collective-permute-start(bf16[272,1024]{1,0:T(8,128)(2,1)S(1)} %collective-permute-done.2.refs_0_), channel_id=1, source_target_pairs={{0,4},{1,5},{2,3},{3,2},{4,0},{5,1},{6,7},{7,6},{8,12},{9,13},{10,... | collective-permute-start | bytes 1671176 | tf_op jit(solution)/shard_map/ppermute | solution.py:285
  23.2 14.9 %collective-permute-start.6 = (bf16[272,1024]{1,0:T(8,128)(2,1)S(1)}, bf16[272,1024]{1,0:T(8,128)(2,1)S(1)}, u32[]{:S(2)}, u32[]{:S(2)}) collective-permute-start(bf16[272,1024]{1,0:T(8,128)(2,1)S(1)} %collective-permute-done.2.refs_0_), channel_id=1, source_target_pairs={{0,8},{1,9},{2,10},{3,11},{4,12},{5,13},{6,14},{7,15},{8,24},{9,25... | collective-permute-start | bytes 1671176 | tf_op jit(solution)/shard_map/ppermute | solution.py:285
  24.1 14.6 %collective-permute-start.9 = (bf16[272,1024]{1,0:T(8,128)(2,1)S(1)}, bf16[272,1024]{1,0:T(8,128)(2,1)S(1)}, u32[]{:S(2)}, u32[]{:S(2)}) collective-permute-start(bf16[272,1024]{1,0:T(8,128)(2,1)S(1)} %collective-permute-done.2.refs_0_), channel_id=1, source_target_pairs={{0,2},{1,3},{2,0},{3,1},{4,6},{5,7},{6,4},{7,5},{8,10},{9,11},{10,... | collective-permute-start | bytes 1671176 | tf_op jit(solution)/shard_map/ppermute | solution.py:285
  24.1 15.4 %collective-permute-start.4 = (bf16[272,1024]{1,0:T(8,128)(2,1)S(1)}, bf16[272,1024]{1,0:T(8,128)(2,1)}, u32[]{:S(2)}, u32[]{:S(2)}) collective-permute-start(bf16[272,1024]{1,0:T(8,128)(2,1)S(1)} %collective-permute-done.1.refs_1_), channel_id=1, source_target_pairs={{0,1},{1,0},{2,6},{3,7},{4,5},{5,4},{6,2},{7,3},{8,9},{9,8},{10,14... | collective-permute-start | bytes 1671176 | tf_op jit(solution)/shard_map/ppermute | solution.py:285
  24.7 14.8 %collective-permute-start.8 = (bf16[272,1024]{1,0:T(8,128)(2,1)S(1)}, bf16[272,1024]{1,0:T(8,128)(2,1)S(1)}, u32[]{:S(2)}, u32[]{:S(2)}) collective-permute-start(bf16[272,1024]{1,0:T(8,128)(2,1)S(1)} %collective-permute-done.1.refs_1_), channel_id=1, source_target_pairs={{0,2},{1,3},{2,0},{3,1},{4,6},{5,7},{6,4},{7,5},{8,10},{9,11},{10,... | collective-permute-start | bytes 1671176 | tf_op jit(solution)/shard_map/ppermute | solution.py:285
  37.3 3.0 %collective-permute-start.7 = (bf16[272,1024]{1,0:T(8,128)(2,1)S(1)}, bf16[272,1024]{1,0:T(8,128)(2,1)S(1)}, u32[]{:S(2)}, u32[]{:S(2)}) collective-permute-start(bf16[272,1024]{1,0:T(8,128)(2,1)S(1)} %collective-permute-done.refs_2_), channel_id=1, source_target_pairs={{0,2},{1,3},{2,0},{3,1},{4,6},{5,7},{6,4},{7,5},{8,10},{9,11},{10,... | collective-permute-start | bytes 1671176 | tf_op jit(solution)/shard_map/ppermute | solution.py:285
  38.1 9.5 %collective-permute-start.11 = (bf16[272,1024]{1,0:T(8,128)(2,1)S(1)}, bf16[272,1024]{1,0:T(8,128)(2,1)S(1)}, u32[]{:S(2)}, u32[]{:S(2)}) collective-permute-start(bf16[272,1024]{1,0:T(8,128)(2,1)S(1)} %collective-permute-done.2.refs_0_), channel_id=1, source_target_pairs={{0,1},{1,0},{2,6},{3,7},{4,5},{5,4},{6,2},{7,3},{8,9},{9,8},{10,14... | collective-permute-start | bytes 1671176 | tf_op jit(solution)/shard_map/ppermute | solution.py:285
  41.1 12.6 %collective-permute-start.12 = (bf16[272,1024]{1,0:T(8,128)(2,1)S(1)}, bf16[272,1024]{1,0:T(8,128)(2,1)}, u32[]{:S(2)}, u32[]{:S(2)}) collective-permute-start(bf16[272,1024]{1,0:T(8,128)(2,1)S(1)} %collective-permute-done.5.refs_1_), channel_id=1, source_target_pairs={{0,1},{1,0},{2,6},{3,7},{4,5},{5,4},{6,2},{7,3},{8,9},{9,8},{10,14... | collective-permute-start | bytes 1671176 | tf_op jit(solution)/shard_map/ppermute | solution.py:285
  42.6 15.4 %collective-permute-start.13 = (bf16[272,1024]{1,0:T(8,128)(2,1)S(1)}, bf16[272,1024]{1,0:T(8,128)(2,1)S(1)}, u32[]{:S(2)}, u32[]{:S(2)}) collective-permute-start(bf16[272,1024]{1,0:T(8,128)(2,1)S(1)} %collective-permute-done.5.refs_1_), channel_id=1, source_target_pairs={{0,8},{1,9},{2,10},{3,11},{4,12},{5,13},{6,14},{7,15},{8,24},{9,25... | collective-permute-start | bytes 1671176 | tf_op jit(solution)/shard_map/ppermute | solution.py:285
  42.6 17.0 %collective-permute-start.15 = (bf16[272,1024]{1,0:T(8,128)(2,1)S(1)}, bf16[272,1024]{1,0:T(8,128)(2,1)}, u32[]{:S(2)}, u32[]{:S(2)}) collective-permute-start(bf16[272,1024]{1,0:T(8,128)(2,1)S(1)} %collective-permute-done.5.refs_1_), channel_id=1, source_target_pairs={{0,2},{1,3},{2,0},{3,1},{4,6},{5,7},{6,4},{7,5},{8,10},{9,11},{10,... | collective-permute-start | bytes 1671176 | tf_op jit(solution)/shard_map/ppermute | solution.py:285
  42.6 17.0 %collective-permute-start.16 = (bf16[272,1024]{1,0:T(8,128)(2,1)S(1)}, bf16[272,1024]{1,0:T(8,128)(2,1)S(1)}, u32[]{:S(2)}, u32[]{:S(2)}) collective-permute-start(bf16[272,1024]{1,0:T(8,128)(2,1)S(1)} %collective-permute-done.6.refs_0_), channel_id=1, source_target_pairs={{0,2},{1,3},{2,0},{3,1},{4,6},{5,7},{6,4},{7,5},{8,10},{9,11},{10,... | collective-permute-start | bytes 1671176 | tf_op jit(solution)/shard_map/ppermute | solution.py:285
  47.7 11.9 %collective-permute-start.14 = (bf16[272,1024]{1,0:T(8,128)(2,1)}, bf16[272,1024]{1,0:T(8,128)(2,1)}, u32[]{:S(2)}, u32[]{:S(2)}) collective-permute-start(bf16[272,1024]{1,0:T(8,128)(2,1)} %collective-permute-done.4.refs_3_), channel_id=1, source_target_pairs={{0,2},{1,3},{2,0},{3,1},{4,6},{5,7},{6,4},{7,5},{8,10},{9,11},{10,... | collective-permute-start | bytes 1671176 | tf_op jit(solution)/shard_map/ppermute | solution.py:285
  53.7 9.5 %collective-permute-start.10 = (bf16[272,1024]{1,0:T(8,128)(2,1)S(1)}, bf16[272,1024]{1,0:T(8,128)(2,1)S(1)}, u32[]{:S(2)}, u32[]{:S(2)}) collective-permute-start(bf16[272,1024]{1,0:T(8,128)(2,1)S(1)} %collective-permute-done.6.refs_0_), channel_id=1, source_target_pairs={{0,1},{1,0},{2,6},{3,7},{4,5},{5,4},{6,2},{7,3},{8,9},{9,8},{10,14... | collective-permute-start | bytes 1671176 | tf_op jit(solution)/shard_map/ppermute | solution.py:285
  58.0 23.7 %collective-permute-start.18 = (bf16[272,1024]{1,0:T(8,128)(2,1)S(1)}, bf16[272,1024]{1,0:T(8,128)(2,1)S(1)}, u32[]{:S(2)}, u32[]{:S(2)}) collective-permute-start(bf16[272,1024]{1,0:T(8,128)(2,1)S(1)} %collective-permute-done.6.refs_0_), channel_id=1, source_target_pairs={{0,8},{1,9},{2,10},{3,11},{4,12},{5,13},{6,14},{7,15},{8,24},{9,25... | collective-permute-start | bytes 1671176 | tf_op jit(solution)/shard_map/ppermute | solution.py:285
  59.6 22.1 %collective-permute-start.17 = (bf16[272,1024]{1,0:T(8,128)(2,1)S(1)}, bf16[272,1024]{1,0:T(8,128)(2,1)S(1)}, u32[]{:S(2)}, u32[]{:S(2)}) collective-permute-start(bf16[272,1024]{1,0:T(8,128)(2,1)S(1)} %collective-permute-done.13.refs_1_), channel_id=1, source_target_pairs={{0,1},{1,0},{2,6},{3,7},{4,5},{5,4},{6,2},{7,3},{8,9},{9,8},{10,14... | collective-permute-start | bytes 1671176 | tf_op jit(solution)/shard_map/ppermute | solution.py:285
  60.2 21.5 %collective-permute-start.21 = (bf16[272,1024]{1,0:T(8,128)(2,1)S(1)}, bf16[272,1024]{1,0:T(8,128)(2,1)S(1)}, u32[]{:S(2)}, u32[]{:S(2)}) collective-permute-start(bf16[272,1024]{1,0:T(8,128)(2,1)S(1)} %collective-permute-done.13.refs_1_), channel_id=1, source_target_pairs={{0,2},{1,3},{2,0},{3,1},{4,6},{5,7},{6,4},{7,5},{8,10},{9,11},{10,... | collective-permute-start | bytes 1671176 | tf_op jit(solution)/shard_map/ppermute | solution.py:285
  60.2 21.5 %collective-permute-start.19 = (bf16[272,1024]{1,0:T(8,128)(2,1)}, bf16[272,1024]{1,0:T(8,128)(2,1)S(1)}, u32[]{:S(2)}, u32[]{:S(2)}) collective-permute-start(bf16[272,1024]{1,0:T(8,128)(2,1)} %copy-done.7), channel_id=1, source_target_pairs={{0,2},{1,3},{2,0},{3,1},{4,6},{5,7},{6,4},{7,5},{8,10},{9,11},{10,... | collective-permute-start | bytes 1671176 | tf_op jit(solution)/shard_map/ppermute | solution.py:285
  63.3 18.5 %collective-permute-start.20 = (bf16[272,1024]{1,0:T(8,128)(2,1)}, bf16[272,1024]{1,0:T(8,128)(2,1)S(1)}, u32[]{:S(2)}, u32[]{:S(2)}) collective-permute-start(bf16[272,1024]{1,0:T(8,128)(2,1)} %collective-permute-done.12.refs_3_), channel_id=1, source_target_pairs={{0,2},{1,3},{2,0},{3,1},{4,6},{5,7},{6,4},{7,5},{8,10},{9,11},{10,... | collective-permute-start | bytes 1671176 | tf_op jit(solution)/shard_map/ppermute | solution.py:285
  81.8 12.6 %copy-start.2 = (bf16[1,384,2048]{2,1,0:T(8,128)(2,1)S(1)}, bf16[1,384,2048]{2,1,0:T(8,128)(2,1)}, u32[]{:S(2)}) copy-start(bf16[1,384,2048]{2,1,0:T(8,128)(2,1)} %param.11) | copy-start | bytes 4718596
  81.8 12.6 %copy-start.6 = (bf16[272,1024]{1,0:T(8,128)(2,1)S(1)}, bf16[272,1024]{1,0:T(8,128)(2,1)}, u32[]{:S(2)}) copy-start(bf16[272,1024]{1,0:T(8,128)(2,1)} %copy-done.5) | copy-start | bytes 1671172
  81.8 2.9 %collective-permute-start.22 = (bf16[4,128,1024]{2,1,0:T(8,128)(2,1)S(1)}, bf16[4,128,1024]{2,1,0:T(8,128)(2,1)S(1)}, u32[]{:S(2)}, u32[]{:S(2)}) collective-permute-start(bf16[4,128,1024]{2,1,0:T(8,128)(2,1)S(1)} %get-tuple-element.88), channel_id=1, source_target_pairs={{0,2},{1,3},{2,0},{3,1},{4,6},{5,7},{6,4},{7,5},{8,10},{9,11},{10,... | collective-permute-start | bytes 3145736 | tf_op jit(solution)/shard_map/ppermute | solution.py:285
  85.1 9.2 %collective-permute-start.23 = (bf16[2,128,1024]{2,1,0:T(8,128)(2,1)S(1)}, bf16[2,128,1024]{2,1,0:T(8,128)(2,1)S(1)}, u32[]{:S(2)}, u32[]{:S(2)}) collective-permute-start(bf16[2,128,1024]{2,1,0:T(8,128)(2,1)S(1)} %slice.137), channel_id=1, source_target_pairs={{0,1},{1,0},{2,6},{3,7},{4,5},{5,4},{6,2},{7,3},{8,9},{9,8},{10,14... | collective-permute-start | bytes 1572872 | tf_op jit(solution)/shard_map/ppermute | solution.py:285
  85.7 17.0 %collective-permute-start.25 = (bf16[272,1024]{1,0:T(8,128)(2,1)S(1)}, bf16[272,1024]{1,0:T(8,128)(2,1)S(1)}, u32[]{:S(2)}, u32[]{:S(2)}) collective-permute-start(bf16[272,1024]{1,0:T(8,128)(2,1)S(1)} %collective-permute-done.13.refs_1_), channel_id=1, source_target_pairs={{0,8},{1,9},{2,10},{3,11},{4,12},{5,13},{6,14},{7,15},{8,24},{9,25... | collective-permute-start | bytes 1671176 | tf_op jit(solution)/shard_map/ppermute | solution.py:285
  87.5 15.2 %collective-permute-start.24 = (bf16[272,1024]{1,0:T(8,128)(2,1)S(1)}, bf16[272,1024]{1,0:T(8,128)(2,1)S(1)}, u32[]{:S(2)}, u32[]{:S(2)}) collective-permute-start(bf16[272,1024]{1,0:T(8,128)(2,1)S(1)} %collective-permute-done.18.refs_0_), channel_id=1, source_target_pairs={{0,1},{1,0},{2,6},{3,7},{4,5},{5,4},{6,2},{7,3},{8,9},{9,8},{10,14... | collective-permute-start | bytes 1671176 | tf_op jit(solution)/shard_map/ppermute | solution.py:285
  88.1 14.7 %collective-permute-start.28 = (bf16[272,1024]{1,0:T(8,128)(2,1)S(1)}, bf16[272,1024]{1,0:T(8,128)(2,1)S(1)}, u32[]{:S(2)}, u32[]{:S(2)}) collective-permute-start(bf16[272,1024]{1,0:T(8,128)(2,1)S(1)} %collective-permute-done.18.refs_0_), channel_id=1, source_target_pairs={{0,2},{1,3},{2,0},{3,1},{4,6},{5,7},{6,4},{7,5},{8,10},{9,11},{10,... | collective-permute-start | bytes 1671176 | tf_op jit(solution)/shard_map/ppermute | solution.py:285
  88.1 14.7 %collective-permute-start.26 = (bf16[272,1024]{1,0:T(8,128)(2,1)S(1)}, bf16[272,1024]{1,0:T(8,128)(2,1)S(1)}, u32[]{:S(2)}, u32[]{:S(2)}) collective-permute-start(bf16[272,1024]{1,0:T(8,128)(2,1)S(1)} %collective-permute-done.10.refs_2_), channel_id=1, source_target_pairs={{0,2},{1,3},{2,0},{3,1},{4,6},{5,7},{6,4},{7,5},{8,10},{9,11},{10,... | collective-permute-start | bytes 1671176 | tf_op jit(solution)/shard_map/ppermute | solution.py:285
  94.4 8.4 %collective-permute-start.27 = (bf16[272,1024]{1,0:T(8,128)(2,1)S(1)}, bf16[272,1024]{1,0:T(8,128)(2,1)S(1)}, u32[]{:S(2)}, u32[]{:S(2)}) collective-permute-start(bf16[272,1024]{1,0:T(8,128)(2,1)S(1)} %collective-permute-done.17.refs_3_), channel_id=1, source_target_pairs={{0,2},{1,3},{2,0},{3,1},{4,6},{5,7},{6,4},{7,5},{8,10},{9,11},{10,... | collective-permute-start | bytes 1671176 | tf_op jit(solution)/shard_map/ppermute | solution.py:285
  102.8 2.8 %collective-permute-start.33 = (bf16[4,128,1024]{2,1,0:T(8,128)(2,1)S(1)}, bf16[4,128,1024]{2,1,0:T(8,128)(2,1)S(1)}, u32[]{:S(2)}, u32[]{:S(2)}) collective-permute-start(bf16[4,128,1024]{2,1,0:T(8,128)(2,1)S(1)} %get-tuple-element.107), channel_id=1, source_target_pairs={{0,2},{1,3},{2,0},{3,1},{4,6},{5,7},{6,4},{7,5},{8,10},{9,11},{10,... | collective-permute-start | bytes 3145736 | tf_op jit(solution)/shard_map/ppermute | solution.py:285
  103.3 15.4 %collective-permute-start.30 = (bf16[272,1024]{1,0:T(8,128)(2,1)S(1)}, bf16[272,1024]{1,0:T(8,128)(2,1)S(1)}, u32[]{:S(2)}, u32[]{:S(2)}) collective-permute-start(bf16[272,1024]{1,0:T(8,128)(2,1)S(1)} %collective-permute-done.25.refs_1_), channel_id=1, source_target_pairs={{0,1},{1,0},{2,6},{3,7},{4,5},{5,4},{6,2},{7,3},{8,9},{9,8},{10,14... | collective-permute-start | bytes 1671176 | tf_op jit(solution)/shard_map/ppermute | solution.py:285
  103.9 14.9 %collective-permute-start.32 = (bf16[272,1024]{1,0:T(8,128)(2,1)S(1)}, bf16[272,1024]{1,0:T(8,128)(2,1)S(1)}, u32[]{:S(2)}, u32[]{:S(2)}) collective-permute-start(bf16[272,1024]{1,0:T(8,128)(2,1)S(1)} %collective-permute-done.25.refs_1_), channel_id=1, source_target_pairs={{0,2},{1,3},{2,0},{3,1},{4,6},{5,7},{6,4},{7,5},{8,10},{9,11},{10,... | collective-permute-start | bytes 1671176 | tf_op jit(solution)/shard_map/ppermute | solution.py:285
  103.9 14.9 %collective-permute-start.31 = (bf16[272,1024]{1,0:T(8,128)(2,1)S(1)}, bf16[272,1024]{1,0:T(8,128)(2,1)S(1)}, u32[]{:S(2)}, u32[]{:S(2)}) collective-permute-start(bf16[272,1024]{1,0:T(8,128)(2,1)S(1)} %collective-permute-done.24.refs_2_), channel_id=1, source_target_pairs={{0,2},{1,3},{2,0},{3,1},{4,6},{5,7},{6,4},{7,5},{8,10},{9,11},{10,... | collective-permute-start | bytes 1671176 | tf_op jit(solution)/shard_map/ppermute | solution.py:285
  106.1 12.4 %collective-permute-start.34 = (bf16[2,128,1024]{2,1,0:T(8,128)(2,1)S(1)}, bf16[2,128,1024]{2,1,0:T(8,128)(2,1)S(1)}, u32[]{:S(2)}, u32[]{:S(2)}) collective-permute-start(bf16[2,128,1024]{2,1,0:T(8,128)(2,1)S(1)} %slice.136), channel_id=1, source_target_pairs={{0,1},{1,0},{2,6},{3,7},{4,5},{5,4},{6,2},{7,3},{8,9},{9,8},{10,14... | collective-permute-start | bytes 1572872 | tf_op jit(solution)/shard_map/ppermute | solution.py:285
  118.7 2.7 %collective-permute-start.37 = (bf16[4,128,1024]{2,1,0:T(8,128)(2,1)S(1)}, bf16[4,128,1024]{2,1,0:T(8,128)(2,1)S(1)}, u32[]{:S(2)}, u32[]{:S(2)}) collective-permute-start(bf16[4,128,1024]{2,1,0:T(8,128)(2,1)S(1)} %get-tuple-element.131), channel_id=1, source_target_pairs={{0,2},{1,3},{2,0},{3,1},{4,6},{5,7},{6,4},{7,5},{8,10},{9,11},{10,... | collective-permute-start | bytes 3145736 | tf_op jit(solution)/shard_map/ppermute | solution.py:285
  118.8 3.7 %collective-permute-start.35 = (bf16[272,1024]{1,0:T(8,128)(2,1)S(1)}, bf16[272,1024]{1,0:T(8,128)(2,1)S(1)}, u32[]{:S(2)}, u32[]{:S(2)}) collective-permute-start(bf16[272,1024]{1,0:T(8,128)(2,1)S(1)} %collective-permute-done.30.refs_3_), channel_id=1, source_target_pairs={{0,2},{1,3},{2,0},{3,1},{4,6},{5,7},{6,4},{7,5},{8,10},{9,11},{10,... | collective-permute-start | bytes 1671176 | tf_op jit(solution)/shard_map/ppermute | solution.py:285
  121.9 16.4 %collective-permute-start.38 = (bf16[2,128,1024]{2,1,0:T(8,128)(2,1)S(1)}, bf16[2,128,1024]{2,1,0:T(8,128)(2,1)S(1)}, u32[]{:S(2)}, u32[]{:S(2)}) collective-permute-start(bf16[2,128,1024]{2,1,0:T(8,128)(2,1)S(1)} %slice.134), channel_id=1, source_target_pairs={{0,1},{1,0},{2,6},{3,7},{4,5},{5,4},{6,2},{7,3},{8,9},{9,8},{10,14... | collective-permute-start | bytes 1572872 | tf_op jit(solution)/shard_map/ppermute | solution.py:285
  130.0 8.6 %collective-permute-start.36 = (bf16[4,128,1024]{2,1,0:T(8,128)(2,1)S(1)}, bf16[4,128,1024]{2,1,0:T(8,128)(2,1)S(1)}, u32[]{:S(2)}, u32[]{:S(2)}) collective-permute-start(bf16[4,128,1024]{2,1,0:T(8,128)(2,1)S(1)} %get-tuple-element.129), channel_id=1, source_target_pairs={{0,2},{1,3},{2,0},{3,1},{4,6},{5,7},{6,4},{7,5},{8,10},{9,11},{10,... | collective-permute-start | bytes 3145736 | tf_op jit(solution)/shard_map/ppermute | solution.py:285
  130.0 6.4 %collective-permute-start.42 = (bf16[128,1024]{1,0:T(8,128)(2,1)S(1)}, bf16[128,1024]{1,0:T(8,128)(2,1)S(1)}, u32[]{:S(2)}, u32[]{:S(2)}) collective-permute-start(bf16[128,1024]{1,0:T(8,128)(2,1)S(1)} %fusion.15), channel_id=1, source_target_pairs={{0,4},{1,5},{2,3},{3,2},{4,0},{5,1},{6,7},{7,6},{8,12},{9,13},{10,... | collective-permute-start | bytes 786440 | tf_op jit(solution)/shard_map/ppermute | solution.py:285
  131.4 31.7 %collective-permute-start.29 = (bf16[128,1024]{1,0:T(8,128)(2,1)S(1)}, bf16[128,1024]{1,0:T(8,128)(2,1)S(1)}, u32[]{:S(2)}, u32[]{:S(2)}) collective-permute-start(bf16[128,1024]{1,0:T(8,128)(2,1)S(1)} %fusion.14), channel_id=1, source_target_pairs={{0,4},{1,5},{2,3},{3,2},{4,0},{5,1},{6,7},{7,6},{8,12},{9,13},{10,... | collective-permute-start | bytes 786440 | tf_op jit(solution)/shard_map/ppermute | solution.py:285
  136.5 8.7 %collective-permute-start.43 = (bf16[128,1024]{1,0:T(8,128)(2,1)S(1)}, bf16[128,1024]{1,0:T(8,128)(2,1)S(1)}, u32[]{:S(2)}, u32[]{:S(2)}) collective-permute-start(bf16[128,1024]{1,0:T(8,128)(2,1)S(1)} %fusion.4), channel_id=1, source_target_pairs={{0,8},{1,9},{2,10},{3,11},{4,12},{5,13},{6,14},{7,15},{8,24},{9,25... | collective-permute-start | bytes 786440 | tf_op jit(solution)/shard_map/ppermute | solution.py:285
  139.1 9.3 %collective-permute-start.41 = (bf16[128,1024]{1,0:T(8,128)(2,1)S(1)}, bf16[128,1024]{1,0:T(8,128)(2,1)S(1)}, u32[]{:S(2)}, u32[]{:S(2)}) collective-permute-start(bf16[128,1024]{1,0:T(8,128)(2,1)S(1)} %fusion.16), channel_id=1, source_target_pairs={{0,4},{1,5},{2,3},{3,2},{4,0},{5,1},{6,7},{7,6},{8,12},{9,13},{10,... | collective-permute-start | bytes 786440 | tf_op jit(solution)/shard_map/ppermute | solution.py:285
  139.5 12.2 %collective-permute-start.39 = (bf16[2,128,1024]{2,1,0:T(8,128)(2,1)S(1)}, bf16[2,128,1024]{2,1,0:T(8,128)(2,1)S(1)}, u32[]{:S(2)}, u32[]{:S(2)}) collective-permute-start(bf16[2,128,1024]{2,1,0:T(8,128)(2,1)S(1)} %slice.135), channel_id=1, source_target_pairs={{0,1},{1,0},{2,6},{3,7},{4,5},{5,4},{6,2},{7,3},{8,9},{9,8},{10,14... | collective-permute-start | bytes 1572872 | tf_op jit(solution)/shard_map/ppermute | solution.py:285
  148.5 8.2 %collective-permute-start.44 = (bf16[128,1024]{1,0:T(8,128)(2,1)S(1)}, bf16[128,1024]{1,0:T(8,128)(2,1)S(1)}, u32[]{:S(2)}, u32[]{:S(2)}) collective-permute-start(bf16[128,1024]{1,0:T(8,128)(2,1)S(1)} %fusion.7), channel_id=1, source_target_pairs={{0,8},{1,9},{2,10},{3,11},{4,12},{5,13},{6,14},{7,15},{8,24},{9,25... | collective-permute-start | bytes 786440 | tf_op jit(solution)/shard_map/ppermute | solution.py:285
  151.9 6.4 %collective-permute-start.40 = (bf16[128,1024]{1,0:T(8,128)(2,1)S(1)}, bf16[128,1024]{1,0:T(8,128)(2,1)S(1)}, u32[]{:S(2)}, u32[]{:S(2)}) collective-permute-start(bf16[128,1024]{1,0:T(8,128)(2,1)S(1)} %fusion.17), channel_id=1, source_target_pairs={{0,4},{1,5},{2,3},{3,2},{4,0},{5,1},{6,7},{7,6},{8,12},{9,13},{10,... | collective-permute-start | bytes 786440 | tf_op jit(solution)/shard_map/ppermute | solution.py:285
  158.4 7.3 %collective-permute-start.45 = (bf16[128,1024]{1,0:T(8,128)(2,1)S(1)}, bf16[128,1024]{1,0:T(8,128)(2,1)S(1)}, u32[]{:S(2)}, u32[]{:S(2)}) collective-permute-start(bf16[128,1024]{1,0:T(8,128)(2,1)S(1)} %fusion.10), channel_id=1, source_target_pairs={{0,8},{1,9},{2,10},{3,11},{4,12},{5,13},{6,14},{7,15},{8,24},{9,25... | collective-permute-start | bytes 786440 | tf_op jit(solution)/shard_map/ppermute | solution.py:285
  (17 other events, 34.1 us)

commit v6 on v5

--- a/solution.py
+++ b/solution.py
@@ -135,51 +135,45 @@
     )(tokens, out_grad, routes.T, combine.T)
 
 
-def expert_kernel(index, chained, top, rows, place_ref, *refs):
-    shares = refs[:4], refs[4:8]
-    wg_ref, wu_ref, wd_ref = refs[8:11]
-    refs = refs[11 + (5 if chained else 0):]
-    near_ref, far_ref = refs[:2]
-    kept_refs = refs[2:7]
-    rx_ref, rg_ref, act_ref, gt_ref, ut_ref, slot_ref, sems = refs[7:]
-    me = place_ref[0].astype(jnp.float32)
-    own_half = place_ref[1]
-    core = place_ref[2]
-    slots = rx_ref.shape[0]
-    width = near_ref.shape[2]
-    pair_slots = slots // 2
-    kept_moves = [
-        pltpu.make_async_copy(source, target.at[pl.ds(index * slots, slots)], sems.at[i])
-        for i, (source, target) in enumerate(zip((rx_ref, rg_ref, act_ref, gt_ref, ut_ref), kept_refs))
-    ]
-
-    def columns(h):
-        return pl.ds(pl.multiple_of((own_half if h == 0 else 1 - own_half) * width, width), width)
-
-    def slot_rows(p):
-        return slice(p * pair_slots, (p + 1) * pair_slots)
-
-    def swapped(p):
-        return core == 1 if p == 0 else core == 0
-
-    def gathered(p, h, part):
-        own, first, second, both = [ref[pl.ds(part * rows, rows)] for ref in shares[p]]
-        if h == 0:
-            return jnp.concatenate([own, jnp.where(swapped(p), second, first)], axis=0)
-        return jnp.concatenate([jnp.where(swapped(p), first, second), both], axis=0)
-
+def load_kernel(*refs):
+    count = (len(refs) - 1) // 2
+    moves = [pltpu.make_async_copy(refs[i], refs[count + i], refs[-1].at[i]) for i in range(count)]
+    for move in moves:
+        move.start()
+    for move in moves:
+        move.wait()
+
+
+def load_weights(weights):
+    return pl.pallas_call(
+        load_kernel,
+        in_specs=[pl.BlockSpec(memory_space=pltpu.HBM)] * len(weights),
+        out_specs=[pl.BlockSpec(memory_space=pltpu.VMEM)] * len(weights),
+        out_shape=[jax.ShapeDtypeStruct(w.shape, w.dtype) for w in weights],
+        scratch_shapes=[pltpu.SemaphoreType.DMA((len(weights),))],
+        name="load",
+    )(*weights)
+
+
+def pick_kernel(top, rows, place_ref, *refs):
+    shares, (mine_ref, theirs_ref, picks_ref) = refs[:4], refs[4:]
+    me, own_half, core = place_ref[0], place_ref[1], place_ref[2]
+    pair_slots, width = mine_ref.shape[1], shares[0].shape[1]
     earlier = (
         lax.broadcasted_iota(jnp.int32, (2 * rows, 2 * rows), 0)
         < lax.broadcasted_iota(jnp.int32, (2 * rows, 2 * rows), 1)
     ).astype(jnp.bfloat16)
+    infos = [
+        [share_ref[pl.ds(2 * rows, INFO_ROWS), k * rows:(k + 1) * rows].astype(jnp.float32) for k in range(top)]
+        for share_ref in (shares[0], shares[3])
+    ]
     picks, scales = [], []
-    for p in range(2):
+    for expert in (me, me + 1 - 2 * core):
         named, weights = [], []
-        for share_ref in (shares[p][0], shares[p][3]):
+        for block in infos:
             hits, weight = 0.0, 0.0
-            for k in range(top):
-                info = share_ref[pl.ds(2 * rows, INFO_ROWS), k * rows:(k + 1) * rows].astype(jnp.float32)
-                hit = info[0:1] == me
+            for info in block:
+                hit = info[0:1] == expert.astype(jnp.float32)
                 hits += hit.astype(jnp.float32)
                 weight += jnp.where(hit, info[1:2] + info[2:3] + info[3:4], 0.0)
             named.append(hits)
@@ -195,73 +189,143 @@
         chosen = slot_of == lax.broadcasted_iota(jnp.int32, (pair_slots, 2 * rows), 0)
         picks.append(chosen.astype(jnp.bfloat16))
         scales.append(jnp.sum(jnp.where(chosen, weights, 0.0), axis=1, keepdims=True))
-
+    picks = jnp.concatenate(picks, axis=0)
+    scales = jnp.concatenate(scales, axis=0)
+    picks_ref[...] = picks
     for h in range(2):
-        for p in range(2):
-            picked = jnp.dot(picks[p], gathered(p, h, 0), preferred_element_type=jnp.float32)
-            rx_ref[slot_rows(p), columns(h)] = picked.astype(jnp.bfloat16)
-    kept_moves[0].start()
-    for h in range(2):
-        for p in range(2):
-            picked = jnp.dot(picks[p], gathered(p, h, 1), preferred_element_type=jnp.float32)
-            rg_ref[slot_rows(p), columns(h)] = (scales[p] * picked).astype(jnp.bfloat16)
-    kept_moves[1].start()
-    gate = lax.dot_general(rx_ref[...], wg_ref[...], CONTRACT_LAST, preferred_element_type=jnp.float32)
-    up = lax.dot_general(rx_ref[...], wu_ref[...], CONTRACT_LAST, preferred_element_type=jnp.float32)
-    hidden_grad = lax.dot_general(rg_ref[...], wd_ref[...], CONTRACT_LAST, preferred_element_type=jnp.float32)
+        cols = pl.ds(pl.multiple_of((own_half if h == 0 else 1 - own_half) * width, width), width)
+        for part in range(2):
+            own, first, second, both = [ref[pl.ds(part * rows, rows)] for ref in shares]
+            if h == 0:
+                held = jnp.concatenate([own, jnp.where(core == 1, second, first)], axis=0)
+            else:
+                held = jnp.concatenate([jnp.where(core == 1, first, second), both], axis=0)
+            picked = jnp.dot(picks, held, preferred_element_type=jnp.float32)
+            if part == 1:
+                picked = scales * picked
+            picked = picked.astype(jnp.bfloat16)
+            mine_ref[part, :, cols] = picked[:pair_slots]
+            theirs_ref[part, :, cols] = picked[pair_slots:]
+
+
+def expert_kernel(index, chained, mine_ref, theirs_ref, wg_ref, wu_ref, wd_ref, *refs):
+    near_ref, far_ref, *kept_refs = refs[5 if chained else 0:][:7]
+    act_ref, gt_ref, ut_ref, sems = refs[-4:]
+    pair_slots = mine_ref.shape[1]
+    slots = 2 * pair_slots
+
+    def kept_move(source, target, part, count, i):
+        return pltpu.make_async_copy(
+            source, kept_refs[target].at[pl.ds(index * slots + part * pair_slots, count)], sems.at[i]
+        )
+
+    moves = [
+        kept_move(mine_ref.at[0], 0, 0, pair_slots, 0),
+        kept_move(theirs_ref.at[0], 0, 1, pair_slots, 1),
+        kept_move(mine_ref.at[1], 1, 0, pair_slots, 2),
+        kept_move(theirs_ref.at[1], 1, 1, pair_slots, 3),
+        kept_move(act_ref, 2, 0, slots, 4),
+        kept_move(gt_ref, 3, 0, slots, 5),
+        kept_move(ut_ref, 4, 0, slots, 6),
+    ]
+    for move in moves[:4]:
+        move.start()
+    rows_x = jnp.concatenate([mine_ref[0], theirs_ref[0]], axis=0)
+    rows_g = jnp.concatenate([mine_ref[1], theirs_ref[1]], axis=0)
+    gate = lax.dot_general(rows_x, wg_ref[...], CONTRACT_LAST, preferred_element_type=jnp.float32)
+    up = lax.dot_general(rows_x, wu_ref[...], CONTRACT_LAST, preferred_element_type=jnp.float32)
+    hidden_grad = lax.dot_general(rows_g, wd_ref[...], CONTRACT_LAST, preferred_element_type=jnp.float32)
     sigma = 1.0 / (1.0 + jnp.exp(-gate))
     silu = gate * sigma
     act_ref[...] = (silu * up).astype(jnp.bfloat16)
     gt_ref[...] = (hidden_grad * up * sigma * (1.0 + gate * (1.0 - sigma))).astype(jnp.bfloat16)
     ut_ref[...] = (hidden_grad * silu).astype(jnp.bfloat16)
-    for move in kept_moves[2:]:
+    for move in moves[4:]:
         move.start()
-
     slot = jnp.dot(gt_ref[...], wg_ref[...], preferred_element_type=jnp.float32)
     slot += jnp.dot(ut_ref[...], wu_ref[...], preferred_element_type=jnp.float32)
-    slot_ref[...] = slot.astype(jnp.bfloat16)
-    for p, out_ref in enumerate((near_ref, far_ref)):
-        backs = []
-        for h in range(2):
-            back = lax.dot_general(
-                picks[p], slot_ref[slot_rows(p), columns(h)], CONTRACT_FIRST,
-                preferred_element_type=jnp.float32,
-            ).astype(jnp.bfloat16)
-            backs.append(back)
-        out_ref[0] = backs[0][:rows]
-        out_ref[1] = jnp.where(swapped(p), backs[1][:rows], backs[0][rows:])
-        out_ref[2] = jnp.where(swapped(p), backs[0][rows:], backs[1][:rows])
-        out_ref[3] = backs[1][rows:]
-    for move in kept_moves:
+    far_ref[...] = slot[pair_slots:].astype(jnp.bfloat16)
+    near_ref[...] = slot[:pair_slots].astype(jnp.bfloat16)
+    for move in moves:
         move.wait()
 
 
-def run_experts(index, chunks, place, shares, weights, kept, top, rows, slots):
+def place_kernel(place_ref, picks_ref, near_ref, far_ref, keep_ref, send_ref):
+    own_half, core = place_ref[1], place_ref[2]
+    _, rows, width = keep_ref.shape
+    pair_slots = near_ref.shape[0]
+    backs = []
+    for h in range(2):
+        cols = pl.ds(pl.multiple_of((own_half if h == 0 else 1 - own_half) * width, width), width)
+        slot = jnp.concatenate([near_ref[:, cols], far_ref[:, cols]], axis=0)
+        backs.append(lax.dot_general(picks_ref[...], slot, CONTRACT_FIRST, preferred_element_type=jnp.float32))
+    keep_ref[0] = backs[0][:rows]
+    keep_ref[1] = jnp.where(core == 1, backs[1][:rows], backs[0][rows:])
+    send_ref[0] = jnp.where(core == 1, backs[0][rows:], backs[1][:rows]).astype(jnp.bfloat16)
+    send_ref[1] = backs[1][rows:].astype(jnp.bfloat16)
+
+
+def pick_rows(place, shares, top, rows, pair_slots):
     width = shares[0].shape[1]
-    hidden, features = weights[0].shape
-    anywhere = pl.BlockSpec(memory_space=pl.ANY)
     vmem = pl.BlockSpec(memory_space=pltpu.VMEM)
-    part = jax.ShapeDtypeStruct((4, rows, width), jnp.bfloat16)
+    picked = jax.ShapeDtypeStruct((2, pair_slots, 2 * width), jnp.bfloat16)
+    return pl.pallas_call(
+        functools.partial(pick_kernel, top, rows),
+        in_specs=[pl.BlockSpec(memory_space=pltpu.SMEM)] + [vmem] * 4,
+        out_specs=[vmem] * 3,
+        out_shape=[picked, picked, jax.ShapeDtypeStruct((2 * pair_slots, 2 * rows), jnp.bfloat16)],
+        compiler_params=pltpu.CompilerParams(vmem_limit_bytes=VMEM_LIMIT),
+        cost_estimate=pl.CostEstimate(
+            flops=32 * pair_slots * 2 * rows * 2 * width,
+            bytes_accessed=2 * (4 * shares[0].size + 8 * pair_slots * width),
+            transcendentals=0,
+        ),
+        name="pick",
+    )(place, *shares)
+
+
+def run_experts(index, chunks, mine, theirs, weights, kept):
+    _, pair_slots, features = mine.shape
+    hidden = weights[0].shape[0]
+    slots = 2 * pair_slots
+    hbm = pl.BlockSpec(memory_space=pltpu.HBM)
+    vmem = pl.BlockSpec(memory_space=pltpu.VMEM)
+    part = jax.ShapeDtypeStruct((pair_slots, features), jnp.bfloat16)
     wide = jax.ShapeDtypeStruct((chunks * slots, features), jnp.bfloat16)
     narrow = jax.ShapeDtypeStruct((chunks * slots, hidden), jnp.bfloat16)
-    first_kept = 1 + len(shares) + 3
     return pl.pallas_call(
-        functools.partial(expert_kernel, index, kept is not None, top, rows),
-        in_specs=[pl.BlockSpec(memory_space=pltpu.SMEM)] + [vmem] * 11 + [anywhere] * (0 if kept is None else 5),
-        out_specs=[vmem] * 2 + [anywhere] * 5,
+        functools.partial(expert_kernel, index, kept is not None),
+        in_specs=[vmem] * 5 + [hbm] * (0 if kept is None else 5),
+        out_specs=[vmem] * 2 + [hbm] * 5,
         out_shape=[part, part, wide, wide, narrow, narrow, narrow],
-        scratch_shapes=[pltpu.VMEM((slots, features), jnp.bfloat16)] * 2
-        + [pltpu.VMEM((slots, hidden), jnp.bfloat16)] * 3
-        + [pltpu.VMEM((slots, features), jnp.bfloat16), pltpu.SemaphoreType.DMA((5,))],
-        input_output_aliases={} if kept is None else {first_kept + i: 2 + i for i in range(5)},
+        scratch_shapes=[pltpu.VMEM((slots, hidden), jnp.bfloat16)] * 3 + [pltpu.SemaphoreType.DMA((7,))],
+        input_output_aliases={} if kept is None else {5 + i: 2 + i for i in range(5)},
         compiler_params=pltpu.CompilerParams(vmem_limit_bytes=VMEM_LIMIT),
         cost_estimate=pl.CostEstimate(
-            flops=4 * slots * features * (hidden * 5 + 2 * rows * 3),
-            bytes_accessed=2 * (8 * shares[0].size + 3 * hidden * features + slots * (2 * features + 3 * hidden)),
+            flops=20 * slots * features * hidden,
+            bytes_accessed=2 * (3 * hidden * features + slots * (4 * features + 3 * hidden)),
             transcendentals=slots * hidden,
         ),
         name="experts",
-    )(place, *shares, *weights, *(kept or ()))
+    )(mine, theirs, *weights, *(kept or ()))
+
+
+def place_rows(place, picks, near, far, rows, width):
+    vmem = pl.BlockSpec(memory_space=pltpu.VMEM)
+    return pl.pallas_call(
+        place_kernel,
+        in_specs=[pl.BlockSpec(memory_space=pltpu.SMEM)] + [vmem] * 3,
+        out_specs=[vmem] * 2,
+        out_shape=[
+            jax.ShapeDtypeStruct((2, rows, width), jnp.float32),
+            jax.ShapeDtypeStruct((2, rows, width), jnp.bfloat16),
+        ],
+        compiler_params=pltpu.CompilerParams(vmem_limit_bytes=VMEM_LIMIT),
+        cost_estimate=pl.CostEstimate(
+            flops=4 * picks.size * 2 * width, bytes_accessed=4 * near.size + 12 * rows * width, transcendentals=0
+        ),
+        name="place",
+    )(place, picks, near, far)
 
 
 def ring_order(length):
@@ -275,7 +339,7 @@
     top = routes.shape[1]
     per_pair = rows * top // experts
     capacity = per_pair + per_pair // 8
-    slots = 2 * (-(-2 * capacity // 16) * 16)
+    pair_slots = -(-2 * capacity // 16) * 16
     order = ring_order(chunks)
     after = {order[i]: order[(i + 1) % chunks] for i in range(chunks)}
     devices = [(e, h) for e in range(experts) for h in range(2)]
@@ -298,22 +362,23 @@
 
     me = lax.axis_index("expert")
     place = jnp.stack([me, lax.axis_index("etp"), me % 2]).astype(jnp.int32)
-    weights = (w_gate[0], w_up[0], w_down[0])
     share = pack_share(tokens, out_grad, routes, combine)
-    def crossed_sums(near_part, far_part, beside=()):
-        mine = near_part.astype(jnp.float32) + to_core(far_part).astype(jnp.float32)
-        mine, send = mine[:2], mine[2:].astype(jnp.bfloat16)
+    weights = load_weights((w_gate[0], w_up[0], w_down[0]))
+
+    def summed(picks, near, far, beside=()):
+        keep, send = place_rows(place, picks, near, to_core(far), rows, width)
         send, beside = lax.optimization_barrier((send, beside))
-        mine = mine + to_second(send).astype(jnp.float32)
+        mine = keep + to_second(send).astype(jnp.float32)
         return mine[0], mine[1].astype(jnp.bfloat16), beside
 
     ring_sends = [("s", 1)] + [(kind, c) for c in range(2, chunks) for kind in ("s", "f")]
     ring_sends = [key for key in ring_sends if key[1] < chunks]
     plane_sends = [("f", 0), ("a", 0), ("f", 1), ("b", 0)] + [(kind, c) for c in range(1, chunks) for kind in ("a", "b")]
     plane_sends = [key for key in plane_sends if key[1] < chunks]
-    have, crossed, fresh = {("s", 0): share}, {}, [("s", 0)]
-    kept, done, parts = None, 0, None
+    have = {("s", 0): share}
+    kept, parts, picked, done = None, None, None, 0
     sums, sends = [], []
+    next_pick = 0
     while done < chunks:
         came = {}
         planned = [key for key in plane_sends if (("f" if key[0] == "b" else "s"), key[1]) in have][:2]
@@ -324,30 +389,39 @@
         if ring_sends and (ring_sends[0][0], ring_sends[0][1] - 1) in have:
             kind, c = ring_sends.pop(0)
             came[kind, c] = to_ring(have[kind, c - 1])
-        swaps = {key: to_core(have[key]) for key in fresh}
         for i in range(len(sums)):
             if sends[i] is not None:
                 sums[i], sends[i] = sums[i] + to_first(sends[i]).astype(jnp.float32), None
         if parts is not None:
-            mine, send, _ = crossed_sums(*parts)
+            mine, send, _ = summed(*parts)
             sums.append(mine)
             sends.append(send)
             parts = None
-        members = [(kind, done) for kind in "sfab"]
-        near = [have[key] for key in members if key in have]
-        far = [crossed.get(key, swaps.get(key) if done + 1 == chunks else None) for key in members]
-        if len(near) == 4 and all(value is not None for value in far):
-            near_part, far_part, *kept = run_experts(
-                done, chunks, place, near + far, weights, kept, top, rows, slots
-            )
-            parts = near_part, far_part
+        arrived = [have.get((kind, next_pick)) for kind in "sfab"]
+        last = next_pick + 1 == chunks
+        if picked is not None:
+            mine, theirs, picks = picked
+            near, far, *kept = run_experts(done, chunks, mine, theirs, weights, kept)
+            parts = picks, near, far
+            picked = None
             done += 1
+        if all(value is not None for value in arrived) and next_pick < chunks:
+            mine, theirs, picks = pick_rows(place, arrived, top, rows, pair_slots)
+            picked = mine, to_core(theirs), picks
+            next_pick += 1
+            if last:
+                if parts is not None:
+                    mine, send, _ = summed(*parts)
+                    sums.append(mine)
+                    sends.append(send)
+                mine, theirs, picks = picked
+                near, far, *kept = run_experts(done, chunks, mine, theirs, weights, kept)
+                parts = picks, near, far
+                done += 1
         if done < chunks:
-            came, swaps, sends, parts = lax.optimization_barrier((came, swaps, sends, parts))
-        fresh = list(came)
+            came, sends, parts, picked, weights = lax.optimization_barrier((came, sends, parts, picked, weights))
         have.update(came)
-        crossed.update(swaps)
-    mine, send, sends = crossed_sums(*parts, sends)
+    mine, send, sends = summed(*parts, sends)
     sums.append(mine)
     sends.append(send)
     running = None

time: 167 us -> 157 us (0.940)
  local copies, waits for them, and re-layouts: 15.8 us -> 0.14 us
  Pallas kernels: 32.4 us -> 37.7 us
  starting transfers between devices: 34.1 us -> 38.2 us
    unnamed x38 -> x8, local copies, waits for them, and re-layouts: 15.4 us -> 0.01 us
    pallas_call x4 -> x13, Pallas kernels: 30.6 us -> 35.8 us  [the longest x4 19.5 us: run_experts(): pl.pallas_call(functools.partial(expert_kernel, index, kept is not None),...]
    ppermute x46 -> x34, starting transfers between devices: 34.1 us -> 38.2 us  [permute(): return lax.ppermute(value, ('expert', 'etp'), pairs)]
    ppermute x46 -> x34, waiting for transfers between devices: 69.6 us -> 68.2 us  [permute(): return lax.ppermute(value, ('expert', 'etp'), pairs)]
  transfers between devices with their start and end apart: 46 -> 34, of which waited for: 17 -> 16; matrix products, arithmetic and copies ran while one was open for 8% -> 7% of each run, Pallas kernels for 18% -> 19%
where the time goes in v6:
time: 157 us
  waiting for transfers between devices  68.2 us (43%)
  starting transfers between devices  38.2 us (24%)
  Pallas kernels  37.7 us (24%)
  matrix products  10.2 us (6%)
  other arithmetic  1.79 us (1%)
    ppermute x34, waiting for transfers between devices, permute(): return lax.ppermute(value, ('expert', 'etp'), pairs)  68.2 us
    ppermute x34, starting transfers between devices, permute(): return lax.ppermute(value, ('expert', 'etp'), pairs)  38.2 us
    pallas_call x4, Pallas kernels, run_experts(): pl.pallas_call(functools.partial(expert_kernel, index, kept is not None),...  19.5 us
    pallas_call x4, Pallas kernels, pick_rows(): pl.pallas_call(functools.partial(pick_kernel, top, rows), in_specs=[pl.Bl...  6.58 us
    pallas_call x4, Pallas kernels, place_rows(): pl.pallas_call(place_kernel, in_specs=[pl.BlockSpec(memory_space=pltpu.SM...  5.09 us
    pallas_call x1, Pallas kernels, load_weights(): pl.pallas_call(load_kernel, in_specs=[pl.BlockSpec(memory_space=pltpu.HBM...  4.62 us
    dot_general x1, matrix products, gather_body(): lax.dot_general(up_term, rows_x, CONTRACT_FIRST, preferred_element_type=j...  3.41 us
    dot_general x1, matrix products, gather_body(): lax.dot_general(gate_term, rows_x, CONTRACT_FIRST, preferred_element_type...  3.41 us
  transfers between devices with their start and end apart: 34, of which 16 were waited for; matrix products, arithmetic and copies ran while one was open for 7% of the time, Pallas kernels for 19%

profile of v6, /device:TPU:0, one launch (start us, length us, event | category | flops | bytes accessed | tf_op | source)
XLA Modules:
  0.0 157.2 jit_solution(983923684458050360)
XLA Ops:
  0.6 1.9 %pack.1.refs_0_ = bf16[272,1024]{1,0:T(8,128)(2,1)} custom-call(bf16[128,1024]{1,0:T(8,128)(2,1)} %tokens_ref.1, bf16[128,1024]{1,0:T(8,128)(2,1)} %grads_ref.1, s32[8,128]{1,0:T(8,128)} %bitcast.61, f32[8,128]{1,0:T(8,128)} %bitcast.62), custom_call_target="tpu_custom_call" | custom-call | bytes 1048576 | tf_op jit(solution)/shard_map/pack/pallas_call | solution.py:128
  2.5 2.9 %collective-permute-start = (bf16[272,1024]{1,0:T(8,128)(2,1)}, bf16[272,1024]{1,0:T(8,128)(2,1)S(1)}, u32[]{:S(2)}, u32[]{:S(2)}) collective-permute-start(bf16[272,1024]{1,0:T(8,128)(2,1)} %pack.1.refs_0_), channel_id=1, source_target_pairs={{0,1},{1,0},{2,6},{3,7},{4,5},{5,4},{6,2},{7,3},{8,9},{9,8},{10,14... | collective-permute-start | bytes 1671176 | tf_op jit(solution)/shard_map/ppermute | solution.py:349
  5.5 1.5 collective-permute-start.1
  7.0 1.6 %collective-permute-start.2 = (bf16[272,1024]{1,0:T(8,128)(2,1)}, bf16[272,1024]{1,0:T(8,128)(2,1)S(1)}, u32[]{:S(2)}, u32[]{:S(2)}) collective-permute-start(bf16[272,1024]{1,0:T(8,128)(2,1)} %pack.1.refs_0_), channel_id=1, source_target_pairs={{0,8},{1,9},{2,10},{3,11},{4,12},{5,13},{6,14},{7,15},{8,24},{9,25... | collective-permute-start | bytes 1671176 | tf_op jit(solution)/shard_map/ppermute | solution.py:349
  8.6 4.6 %load.1 = (bf16[384,2048]{1,0:T(8,128)(2,1)}, bf16[384,2048]{1,0:T(8,128)(2,1)}, bf16[384,2048]{1,0:T(8,128)(2,1)}) custom-call(bf16[384,2048]{1,0:T(8,128)(2,1)} %bitcast.58, bf16[384,2048]{1,0:T(8,128)(2,1)} %bitcast.59, bf16[384,2048]{1,0:T(8,128)(2,1)} %bitcast.60), custom_call_target="tpu_custom_call" | custom-call | tf_op jit(solution)/shard_map/load/pallas_call | solution.py:148
  13.2 5.5 %collective-permute-done.refs_2_ = bf16[272,1024]{1,0:T(8,128)(2,1)S(1)} collective-permute-done((bf16[272,1024]{1,0:T(8,128)(2,1)}, bf16[272,1024]{1,0:T(8,128)(2,1)S(1)}, u32[]{:S(2)}, u32[]{:S(2)}) %collective-permute-start) | collective-permute-done | bytes 557088 | tf_op jit(solution)/shard_map/ppermute | solution.py:349
  18.7 3.2 %collective-permute-done.2.refs_0_ = bf16[272,1024]{1,0:T(8,128)(2,1)S(1)} collective-permute-done((bf16[272,1024]{1,0:T(8,128)(2,1)}, bf16[272,1024]{1,0:T(8,128)(2,1)S(1)}, u32[]{:S(2)}, u32[]{:S(2)}) %collective-permute-start.2) | collective-permute-done | bytes 557088 | tf_op jit(solution)/shard_map/ppermute | solution.py:349
  23.9 12.9 %collective-permute-done.4.refs_1_ = bf16[272,1024]{1,0:T(8,128)(2,1)S(1)} collective-permute-done((bf16[272,1024]{1,0:T(8,128)(2,1)S(1)}, bf16[272,1024]{1,0:T(8,128)(2,1)S(1)}, u32[]{:S(2)}, u32[]{:S(2)}) %collective-permute-start.4) | collective-permute-done | bytes 557088 | tf_op jit(solution)/shard_map/ppermute | solution.py:349
  36.9 2.0 %pick.4 = (bf16[2,144,2048]{2,1,0:T(8,128)(2,1)S(1)}, bf16[2,144,2048]{2,1,0:T(8,128)(2,1)S(1)}, bf16[288,256]{1,0:T(8,128)(2,1)S(1)}) custom-call(s32[3]{0:T(128)S(1)} %pad_add_fusion.place_ref, bf16[272,1024]{1,0:T(8,128)(2,1)S(1)} %copy-done.3, bf16[272,1024]{1,0:T(8,128)(2,1)S(1)} %collective-permute-done.1.refs_1_, ...), custom_call_target="tpu_custom_call" | custom-call | flops 2415919104 | bytes 4587520 | tf_op jit(solution)/shard_map/pick/pallas_call | solution.py:272
  39.6 1.4 collective-permute-start.8
  41.1 1.3 collective-permute-start.9
  42.3 6.2 %collective-permute-done.7.refs_2_ = bf16[272,1024]{1,0:T(8,128)(2,1)S(1)} collective-permute-done((bf16[272,1024]{1,0:T(8,128)(2,1)S(1)}, bf16[272,1024]{1,0:T(8,128)(2,1)S(1)}, u32[]{:S(2)}, u32[]{:S(2)}) %collective-permute-start.7) | collective-permute-done | bytes 557088 | tf_op jit(solution)/shard_map/ppermute | solution.py:349
  48.6 6.0 %collective-permute-done.8.refs_3_ = bf16[272,1024]{1,0:T(8,128)(2,1)S(1)} collective-permute-done((bf16[272,1024]{1,0:T(8,128)(2,1)S(1)}, bf16[272,1024]{1,0:T(8,128)(2,1)S(1)}, u32[]{:S(2)}, u32[]{:S(2)}) %collective-permute-start.8) | collective-permute-done | bytes 557088 | tf_op jit(solution)/shard_map/ppermute | solution.py:349
  54.5 1.8 %collective-permute-done.9.refs_1_ = bf16[272,1024]{1,0:T(8,128)(2,1)S(1)} collective-permute-done((bf16[272,1024]{1,0:T(8,128)(2,1)S(1)}, bf16[272,1024]{1,0:T(8,128)(2,1)S(1)}, u32[]{:S(2)}, u32[]{:S(2)}) %collective-permute-start.9) | collective-permute-done | bytes 557088 | tf_op jit(solution)/shard_map/ppermute | solution.py:349
  56.4 1.5 pick.5
  59.4 1.0 collective-permute-start.11
  60.4 4.9 %experts.4 = (bf16[144,2048]{1,0:T(8,128)(2,1)S(1)}, bf16[144,2048]{1,0:T(8,128)(2,1)S(1)}, bf16[1152,2048]{1,0:T(8,128)(2,1)S(1)}, bf16[1152,2048]{1,0:T(8,128)...) custom-call(bf16[2,144,2048]{2,1,0:T(8,128)(2,1)S(1)} %get-tuple-element.130., ...), custom_call_target="tpu_custom_call" | custom-call | flops 4529848320 | bytes 10100736 | tf_op jit(solution)/shard_map/experts/pallas_call | solution.py:296
  65.3 8.6 %collective-permute-done.12.refs_0_ = bf16[272,1024]{1,0:T(8,128)(2,1)S(1)} collective-permute-done((bf16[272,1024]{1,0:T(8,128)(2,1)S(1)}, bf16[272,1024]{1,0:T(8,128)(2,1)S(1)}, u32[]{:S(2)}, u32[]{:S(2)}) %collective-permute-start.12) | collective-permute-done | bytes 557088 | tf_op jit(solution)/shard_map/ppermute | solution.py:349
  74.0 1.5 pick.6
  76.1 1.3 place.4
  77.4 1.0 collective-permute-start.15
  78.4 3.4 %collective-permute-start.17 = (bf16[272,1024]{1,0:T(8,128)(2,1)S(1)}, bf16[272,1024]{1,0:T(8,128)(2,1)S(1)}, u32[]{:S(2)}, u32[]{:S(2)}) collective-permute-start(bf16[272,1024]{1,0:T(8,128)(2,1)S(1)} %collective-permute-done.9.refs_1_), channel_id=1, source_target_pairs={{0,8},{1,9},{2,10},{3,11},{4,12},{5,13},{6,14},{7,15},{8,24},{9,25... | collective-permute-start | bytes 1671176 | tf_op jit(solution)/shard_map/ppermute | solution.py:349
  81.7 1.1 collective-permute-start.16
  82.8 4.9 %experts.5 = (bf16[144,2048]{1,0:T(8,128)(2,1)S(1)}, bf16[144,2048]{1,0:T(8,128)(2,1)S(1)}, bf16[1152,2048]{1,0:T(8,128)(2,1)S(1)}, bf16[1152,2048]{1,0:T(8,128)...) custom-call(bf16[2,144,2048]{2,1,0:T(8,128)(2,1)S(1)} %get-tuple-ele, ...), custom_call_target="tpu_custom_call", output_to_operand_aliasing={{2}: (5, {}), {3}: (6, {}), {4}: (7, {}), {5}: (8, {}), {6}... | custom-call | flops 4529848320 | bytes 10100736 | tf_op jit(solution)/shard_map/experts/pallas_call | solution.py:296
  87.9 5.2 %collective-permute-done.17.refs_1_ = bf16[272,1024]{1,0:T(8,128)(2,1)S(1)} collective-permute-done((bf16[272,1024]{1,0:T(8,128)(2,1)S(1)}, bf16[272,1024]{1,0:T(8,128)(2,1)S(1)}, u32[]{:S(2)}, u32[]{:S(2)}) %collective-permute-start.17) | collective-permute-done | bytes 557088 | tf_op jit(solution)/shard_map/ppermute | solution.py:349
  93.2 2.0 %collective-permute-done.21.far_ref = bf16[144,2048]{1,0:T(8,128)(2,1)S(1)} collective-permute-done((bf16[144,2048]{1,0:T(8,128)(2,1)S(1)}, bf16[144,2048]{1,0:T(8,128)(2,1)S(1)}, u32[]{:S(2)}, u32[]{:S(2)}) %collective-permute-start.21) | collective-permute-done | bytes 589856 | tf_op jit(solution)/shard_map/ppermute | solution.py:349
  95.2 1.3 place.5
  97.4 1.1 collective-permute-start.20
  98.5 4.9 %experts.6 = (bf16[144,2048]{1,0:T(8,128)(2,1)S(1)}, bf16[144,2048]{1,0:T(8,128)(2,1)S(1)}, bf16[1152,2048]{1,0:T(8,128)(2,1)S(1)}, bf16[1152,2048]{1,0:T(8,128)...) custom-call(bf16[2,144,2048]{2,1,0:T(8,128)(2,1)S(1)} %get-tuple-ele, ...), custom_call_target="tpu_custom_call", output_to_operand_aliasing={{2}: (5, {}), {3}: (6, {}), {4}: (7, {}), {5}: (8, {}), {6}... | custom-call | flops 4529848320 | bytes 10100736 | tf_op jit(solution)/shard_map/experts/pallas_call | solution.py:296
  103.4 2.3 %collective-permute-done.22 = bf16[2,128,1024]{2,1,0:T(8,128)(2,1)S(1)} collective-permute-done((bf16[2,128,1024]{2,1,0:T(8,128)(2,1)S(1)}, bf16[2,128,1024]{2,1,0:T(8,128)(2,1)S(1)}, u32[]{:S(2)}, u32[]{:S(2)}) %collective-permute-start.22) | collective-permute-done | bytes 524320 | tf_op jit(solution)/shard_map/ppermute | solution.py:349
  105.9 5.8 %collective-permute-done.20.refs_3_ = bf16[272,1024]{1,0:T(8,128)(2,1)S(1)} collective-permute-done((bf16[272,1024]{1,0:T(8,128)(2,1)S(1)}, bf16[272,1024]{1,0:T(8,128)(2,1)S(1)}, u32[]{:S(2)}, u32[]{:S(2)}) %collective-permute-start.20) | collective-permute-done | bytes 557088 | tf_op jit(solution)/shard_map/ppermute | solution.py:349
  111.7 1.5 pick.7
  113.7 1.5 collective-permute-start.19
  115.8 1.2 collective-permute-done.25.far_ref
  116.9 1.3 place.7
  119.2 4.9 %experts.7 = (bf16[144,2048]{1,0:T(8,128)(2,1)S(1)}, bf16[144,2048]{1,0:T(8,128)(2,1)S(1)}, bf16[1152,2048]{1,0:T(8,128)(2,1)S(1)}, bf16[1152,2048]{1,0:T(8,128)...) custom-call(bf16[2,144,2048]{2,1,0:T(8,128)(2,1)S(1)} %get-tuple-ele, ...), custom_call_target="tpu_custom_call", output_to_operand_aliasing={{2}: (5, {}), {3}: (6, {}), {4}: (7, {}), {5}: (8, {}), {6}... | custom-call | flops 4529848320 | bytes 10100736 | tf_op jit(solution)/shard_map/experts/pallas_call | solution.py:296
  124.9 3.0 %collective-permute-start.31 = (bf16[128,1024]{1,0:T(8,128)(2,1)S(1)}, bf16[128,1024]{1,0:T(8,128)(2,1)S(1)}, u32[]{:S(2)}, u32[]{:S(2)}) collective-permute-start(bf16[128,1024]{1,0:T(8,128)(2,1)S(1)} %fusion.4), channel_id=1, source_target_pairs={{0,8},{1,9},{2,10},{3,11},{4,12},{5,13},{6,14},{7,15},{8,24},{9,25... | collective-permute-start | bytes 786440 | tf_op jit(solution)/shard_map/ppermute | solution.py:349
  128.1 1.3 place.6
  129.4 1.3 collective-permute-start.29
  131.7 3.4 %fusion.1 = bf16[1,384,2048]{2,1,0:T(8,128)(2,1)} fusion(bf16[1152,384]{1,0:T(8,128)(2,1)S(1)} %get-tuple-element.213, bf16[1152,2048]{1,0:T(8,128)(2,1)S(1)} %get-tuple-element.212), kind=kOutput, calls=%fused_computation.4 | convolution fusion | flops 1812725760 | bytes 7176192 | tf_op jit(solution)/shard_map/dot_general | solution.py:439
  135.1 3.4 %collective-permute-done.29 = bf16[128,1024]{1,0:T(8,128)(2,1)S(1)} collective-permute-done((bf16[128,1024]{1,0:T(8,128)(2,1)S(1)}, bf16[128,1024]{1,0:T(8,128)(2,1)S(1)}, u32[]{:S(2)}, u32[]{:S(2)}) %collective-permute-start.29) | collective-permute-done | bytes 262176 | tf_op jit(solution)/shard_map/ppermute | solution.py:349
  138.6 2.4 %collective-permute-start.32 = (bf16[128,1024]{1,0:T(8,128)(2,1)S(1)}, bf16[128,1024]{1,0:T(8,128)(2,1)S(1)}, u32[]{:S(2)}, u32[]{:S(2)}) collective-permute-start(bf16[128,1024]{1,0:T(8,128)(2,1)S(1)} %fusion.7), channel_id=1, source_target_pairs={{0,8},{1,9},{2,10},{3,11},{4,12},{5,13},{6,14},{7,15},{8,24},{9,25... | collective-permute-start | bytes 786440 | tf_op jit(solution)/shard_map/ppermute | solution.py:349
  141.2 1.5 collective-permute-start.28
  142.8 3.4 %fusion = bf16[1,384,2048]{2,1,0:T(8,128)(2,1)} fusion(bf16[1152,384]{1,0:T(8,128)(2,1)S(1)} %get-tuple-element.211, bf16[1152,2048]{1,0:T(8,128)(2,1)S(1)} %get-tuple-element.212), kind=kOutput, calls=%fused_computation.3 | convolution fusion | flops 1812725760 | bytes 7176192 | tf_op jit(solution)/shard_map/dot_general | solution.py:438
  146.2 1.5 collective-permute-done.28
  147.8 2.8 %collective-permute-start.33 = (bf16[128,1024]{1,0:T(8,128)(2,1)S(1)}, bf16[128,1024]{1,0:T(8,128)(2,1)S(1)}, u32[]{:S(2)}, u32[]{:S(2)}) collective-permute-start(bf16[128,1024]{1,0:T(8,128)(2,1)S(1)} %fusion.10), channel_id=1, source_target_pairs={{0,8},{1,9},{2,10},{3,11},{4,12},{5,13},{6,14},{7,15},{8,24},{9,25... | collective-permute-start | bytes 786440 | tf_op jit(solution)/shard_map/ppermute | solution.py:349
  150.6 3.4 %fusion.2 = bf16[1,384,2048]{2,1,0:T(8,128)(2,1)} fusion(bf16[1152,384]{1,0:T(8,128)(2,1)S(1)} %get-tuple-element.214, bf16[1152,2048]{1,0:T(8,128)(2,1)S(1)} %get-tuple-element.215), kind=kOutput, calls=%fused_computation.5 | convolution fusion | flops 1812725760 | bytes 7176192 | tf_op jit(solution)/shard_map/dot_general | solution.py:437
  154.0 2.4 %collective-permute-done.33 = bf16[128,1024]{1,0:T(8,128)(2,1)S(1)} collective-permute-done((bf16[128,1024]{1,0:T(8,128)(2,1)S(1)}, bf16[128,1024]{1,0:T(8,128)(2,1)S(1)}, u32[]{:S(2)}, u32[]{:S(2)}) %collective-permute-start.33) | collective-permute-done | bytes 262176 | tf_op jit(solution)/shard_map/ppermute | solution.py:349
  (58 shorter events, 11.5 us)
Async XLA Ops:
  2.5 16.2 %collective-permute-start = (bf16[272,1024]{1,0:T(8,128)(2,1)}, bf16[272,1024]{1,0:T(8,128)(2,1)S(1)}, u32[]{:S(2)}, u32[]{:S(2)}) collective-permute-start(bf16[272,1024]{1,0:T(8,128)(2,1)} %pack.1.refs_0_), channel_id=1, source_target_pairs={{0,1},{1,0},{2,6},{3,7},{4,5},{5,4},{6,2},{7,3},{8,9},{9,8},{10,14... | collective-permute-start | bytes 1671176 | tf_op jit(solution)/shard_map/ppermute | solution.py:349
  5.5 13.2 %collective-permute-start.1 = (bf16[272,1024]{1,0:T(8,128)(2,1)}, bf16[272,1024]{1,0:T(8,128)(2,1)S(1)}, u32[]{:S(2)}, u32[]{:S(2)}) collective-permute-start(bf16[272,1024]{1,0:T(8,128)(2,1)} %pack.1.refs_0_), channel_id=1, source_target_pairs={{0,4},{1,5},{2,3},{3,2},{4,0},{5,1},{6,7},{7,6},{8,12},{9,13},{10,... | collective-permute-start | bytes 1671176 | tf_op jit(solution)/shard_map/ppermute | solution.py:349
  7.0 14.9 %collective-permute-start.2 = (bf16[272,1024]{1,0:T(8,128)(2,1)}, bf16[272,1024]{1,0:T(8,128)(2,1)S(1)}, u32[]{:S(2)}, u32[]{:S(2)}) collective-permute-start(bf16[272,1024]{1,0:T(8,128)(2,1)} %pack.1.refs_0_), channel_id=1, source_target_pairs={{0,8},{1,9},{2,10},{3,11},{4,12},{5,13},{6,14},{7,15},{8,24},{9,25... | collective-permute-start | bytes 1671176 | tf_op jit(solution)/shard_map/ppermute | solution.py:349
  8.6 28.3 %copy-start.3 = (bf16[272,1024]{1,0:T(8,128)(2,1)S(1)}, bf16[272,1024]{1,0:T(8,128)(2,1)}, u32[]{:S(2)}) copy-start(bf16[272,1024]{1,0:T(8,128)(2,1)} %pack.1.refs_0_) | copy-start | bytes 1671172
  21.9 14.9 %collective-permute-start.4 = (bf16[272,1024]{1,0:T(8,128)(2,1)S(1)}, bf16[272,1024]{1,0:T(8,128)(2,1)S(1)}, u32[]{:S(2)}, u32[]{:S(2)}) collective-permute-start(bf16[272,1024]{1,0:T(8,128)(2,1)S(1)} %collective-permute-done.2.refs_0_), channel_id=1, source_target_pairs={{0,4},{1,5},{2,3},{3,2},{4,0},{5,1},{6,7},{7,6},{8,12},{9,13},{10,... | collective-permute-start | bytes 1671176 | tf_op jit(solution)/shard_map/ppermute | solution.py:349
  22.4 14.4 %collective-permute-start.5 = (bf16[272,1024]{1,0:T(8,128)(2,1)S(1)}, bf16[272,1024]{1,0:T(8,128)(2,1)S(1)}, u32[]{:S(2)}, u32[]{:S(2)}) collective-permute-start(bf16[272,1024]{1,0:T(8,128)(2,1)S(1)} %collective-permute-done.2.refs_0_), channel_id=1, source_target_pairs={{0,8},{1,9},{2,10},{3,11},{4,12},{5,13},{6,14},{7,15},{8,24},{9,25... | collective-permute-start | bytes 1671176 | tf_op jit(solution)/shard_map/ppermute | solution.py:349
  23.3 13.6 %collective-permute-start.3 = (bf16[272,1024]{1,0:T(8,128)(2,1)S(1)}, bf16[272,1024]{1,0:T(8,128)(2,1)}, u32[]{:S(2)}, u32[]{:S(2)}) collective-permute-start(bf16[272,1024]{1,0:T(8,128)(2,1)S(1)} %collective-permute-done.1.refs_1_), channel_id=1, source_target_pairs={{0,1},{1,0},{2,6},{3,7},{4,5},{5,4},{6,2},{7,3},{8,9},{9,8},{10,14... | collective-permute-start | bytes 1671176 | tf_op jit(solution)/shard_map/ppermute | solution.py:349
  38.9 17.5 %collective-permute-start.10 = (bf16[2,144,2048]{2,1,0:T(8,128)(2,1)S(1)}, bf16[2,144,2048]{2,1,0:T(8,128)(2,1)S(1)}, u32[]{:S(2)}, u32[]{:S(2)}) collective-permute-start(bf16[2,144,2048]{2,1,0:T(8,128)(2,1)S(1)} %get-tuple-element.123), channel_id=1, source_target_pairs={{0,2},{1,3},{2,0},{3,1},{4,6},{5,7},{6,4},{7,5},{8,10},{9,11},{10,... | collective-permute-start | bytes 3538952 | tf_op jit(solution)/shard_map/ppermute | solution.py:349
  39.0 9.6 %collective-permute-start.7 = (bf16[272,1024]{1,0:T(8,128)(2,1)S(1)}, bf16[272,1024]{1,0:T(8,128)(2,1)S(1)}, u32[]{:S(2)}, u32[]{:S(2)}) collective-permute-start(bf16[272,1024]{1,0:T(8,128)(2,1)S(1)} %collective-permute-done.2.refs_0_), channel_id=1, source_target_pairs={{0,1},{1,0},{2,6},{3,7},{4,5},{5,4},{6,2},{7,3},{8,9},{9,8},{10,14... | collective-permute-start | bytes 1671176 | tf_op jit(solution)/shard_map/ppermute | solution.py:349
  39.6 14.9 %collective-permute-start.8 = (bf16[272,1024]{1,0:T(8,128)(2,1)S(1)}, bf16[272,1024]{1,0:T(8,128)(2,1)S(1)}, u32[]{:S(2)}, u32[]{:S(2)}) collective-permute-start(bf16[272,1024]{1,0:T(8,128)(2,1)S(1)} %collective-permute-done.4.refs_1_), channel_id=1, source_target_pairs={{0,1},{1,0},{2,6},{3,7},{4,5},{5,4},{6,2},{7,3},{8,9},{9,8},{10,14... | collective-permute-start | bytes 1671176 | tf_op jit(solution)/shard_map/ppermute | solution.py:349
  41.1 15.3 %collective-permute-start.9 = (bf16[272,1024]{1,0:T(8,128)(2,1)S(1)}, bf16[272,1024]{1,0:T(8,128)(2,1)S(1)}, u32[]{:S(2)}, u32[]{:S(2)}) collective-permute-start(bf16[272,1024]{1,0:T(8,128)(2,1)S(1)} %collective-permute-done.4.refs_1_), channel_id=1, source_target_pairs={{0,8},{1,9},{2,10},{3,11},{4,12},{5,13},{6,14},{7,15},{8,24},{9,25... | collective-permute-start | bytes 1671176 | tf_op jit(solution)/shard_map/ppermute | solution.py:349
  56.4 4.1 %copy-start = (bf16[384,2048]{1,0:T(8,128)(2,1)S(1)}, bf16[384,2048]{1,0:T(8,128)(2,1)}, u32[]{:S(2)}) copy-start(bf16[384,2048]{1,0:T(8,128)(2,1)} %get-tuple-element.191.wg_ref) | copy-start | bytes 4718596
  56.4 4.1 %copy-start.1 = (bf16[384,2048]{1,0:T(8,128)(2,1)S(1)}, bf16[384,2048]{1,0:T(8,128)(2,1)}, u32[]{:S(2)}) copy-start(bf16[384,2048]{1,0:T(8,128)(2,1)} %get-tuple-element.192.wu_ref) | copy-start | bytes 4718596
  56.4 4.1 %copy-start.2 = (bf16[384,2048]{1,0:T(8,128)(2,1)S(1)}, bf16[384,2048]{1,0:T(8,128)(2,1)}, u32[]{:S(2)}) copy-start(bf16[384,2048]{1,0:T(8,128)(2,1)} %get-tuple-element.193.wd_ref) | copy-start | bytes 4718596
  57.9 16.0 %collective-permute-start.13 = (bf16[2,144,2048]{2,1,0:T(8,128)(2,1)S(1)}, bf16[2,144,2048]{2,1,0:T(8,128)(2,1)S(1)}, u32[]{:S(2)}, u32[]{:S(2)}) collective-permute-start(bf16[2,144,2048]{2,1,0:T(8,128)(2,1)S(1)} %get-tuple-element.140), channel_id=1, source_target_pairs={{0,2},{1,3},{2,0},{3,1},{4,6},{5,7},{6,4},{7,5},{8,10},{9,11},{10,... | collective-permute-start | bytes 3538952 | tf_op jit(solution)/shard_map/ppermute | solution.py:349
  58.0 15.9 %collective-permute-start.12 = (bf16[272,1024]{1,0:T(8,128)(2,1)S(1)}, bf16[272,1024]{1,0:T(8,128)(2,1)S(1)}, u32[]{:S(2)}, u32[]{:S(2)}) collective-permute-start(bf16[272,1024]{1,0:T(8,128)(2,1)S(1)} %collective-permute-done.5.refs_0_), channel_id=1, source_target_pairs={{0,8},{1,9},{2,10},{3,11},{4,12},{5,13},{6,14},{7,15},{8,24},{9,25... | collective-permute-start | bytes 1671176 | tf_op jit(solution)/shard_map/ppermute | solution.py:349
  58.4 15.5 %collective-permute-start.6 = (bf16[272,1024]{1,0:T(8,128)(2,1)S(1)}, bf16[272,1024]{1,0:T(8,128)(2,1)S(1)}, u32[]{:S(2)}, u32[]{:S(2)}) collective-permute-start(bf16[272,1024]{1,0:T(8,128)(2,1)S(1)} %collective-permute-done.5.refs_0_), channel_id=1, source_target_pairs={{0,1},{1,0},{2,6},{3,7},{4,5},{5,4},{6,2},{7,3},{8,9},{9,8},{10,14... | collective-permute-start | bytes 1671176 | tf_op jit(solution)/shard_map/ppermute | solution.py:349
  59.4 14.5 %collective-permute-start.11 = (bf16[272,1024]{1,0:T(8,128)(2,1)S(1)}, bf16[272,1024]{1,0:T(8,128)(2,1)S(1)}, u32[]{:S(2)}, u32[]{:S(2)}) collective-permute-start(bf16[272,1024]{1,0:T(8,128)(2,1)S(1)} %collective-permute-done.9.refs_1_), channel_id=1, source_target_pairs={{0,1},{1,0},{2,6},{3,7},{4,5},{5,4},{6,2},{7,3},{8,9},{9,8},{10,14... | collective-permute-start | bytes 1671176 | tf_op jit(solution)/shard_map/ppermute | solution.py:349
  73.9 2.2 %collective-permute-start.14 = (bf16[144,2048]{1,0:T(8,128)(2,1)S(1)}, bf16[144,2048]{1,0:T(8,128)(2,1)S(1)}, u32[]{:S(2)}, u32[]{:S(2)}) collective-permute-start(bf16[144,2048]{1,0:T(8,128)(2,1)S(1)} %get-tuple-element.144), channel_id=1, source_target_pairs={{0,2},{1,3},{2,0},{3,1},{4,6},{5,7},{6,4},{7,5},{8,10},{9,11},{10,... | collective-permute-start | bytes 1769480 | tf_op jit(solution)/shard_map/ppermute | solution.py:349
  75.5 17.6 %collective-permute-start.18 = (bf16[2,144,2048]{2,1,0:T(8,128)(2,1)S(1)}, bf16[2,144,2048]{2,1,0:T(8,128)(2,1)S(1)}, u32[]{:S(2)}, u32[]{:S(2)}) collective-permute-start(bf16[2,144,2048]{2,1,0:T(8,128)(2,1)S(1)} %get-tuple-element.164), channel_id=1, source_target_pairs={{0,2},{1,3},{2,0},{3,1},{4,6},{5,7},{6,4},{7,5},{8,10},{9,11},{10,... | collective-permute-start | bytes 3538952 | tf_op jit(solution)/shard_map/ppermute | solution.py:349
  77.4 10.3 %collective-permute-start.15 = (bf16[2,128,1024]{2,1,0:T(8,128)(2,1)S(1)}, bf16[2,128,1024]{2,1,0:T(8,128)(2,1)S(1)}, u32[]{:S(2)}, u32[]{:S(2)}) collective-permute-start(bf16[2,128,1024]{2,1,0:T(8,128)(2,1)S(1)} %get-tuple-element.146), channel_id=1, source_target_pairs={{0,1},{1,0},{2,6},{3,7},{4,5},{5,4},{6,2},{7,3},{8,9},{9,8},{10,14... | collective-permute-start | bytes 1572872 | tf_op jit(solution)/shard_map/ppermute | solution.py:349
  78.4 14.8 %collective-permute-start.17 = (bf16[272,1024]{1,0:T(8,128)(2,1)S(1)}, bf16[272,1024]{1,0:T(8,128)(2,1)S(1)}, u32[]{:S(2)}, u32[]{:S(2)}) collective-permute-start(bf16[272,1024]{1,0:T(8,128)(2,1)S(1)} %collective-permute-done.9.refs_1_), channel_id=1, source_target_pairs={{0,8},{1,9},{2,10},{3,11},{4,12},{5,13},{6,14},{7,15},{8,24},{9,25... | collective-permute-start | bytes 1671176 | tf_op jit(solution)/shard_map/ppermute | solution.py:349
  81.7 11.4 %collective-permute-start.16 = (bf16[272,1024]{1,0:T(8,128)(2,1)S(1)}, bf16[272,1024]{1,0:T(8,128)(2,1)S(1)}, u32[]{:S(2)}, u32[]{:S(2)}) collective-permute-start(bf16[272,1024]{1,0:T(8,128)(2,1)S(1)} %collective-permute-done.12.refs_0_), channel_id=1, source_target_pairs={{0,1},{1,0},{2,6},{3,7},{4,5},{5,4},{6,2},{7,3},{8,9},{9,8},{10,14... | collective-permute-start | bytes 1671176 | tf_op jit(solution)/shard_map/ppermute | solution.py:349
  93.1 2.0 %collective-permute-start.21 = (bf16[144,2048]{1,0:T(8,128)(2,1)S(1)}, bf16[144,2048]{1,0:T(8,128)(2,1)S(1)}, u32[]{:S(2)}, u32[]{:S(2)}) collective-permute-start(bf16[144,2048]{1,0:T(8,128)(2,1)S(1)} %get-tuple-element.171), channel_id=1, source_target_pairs={{0,2},{1,3},{2,0},{3,1},{4,6},{5,7},{6,4},{7,5},{8,10},{9,11},{10,... | collective-permute-start | bytes 1769480 | tf_op jit(solution)/shard_map/ppermute | solution.py:349
  96.4 9.2 %collective-permute-start.22 = (bf16[2,128,1024]{2,1,0:T(8,128)(2,1)S(1)}, bf16[2,128,1024]{2,1,0:T(8,128)(2,1)S(1)}, u32[]{:S(2)}, u32[]{:S(2)}) collective-permute-start(bf16[2,128,1024]{2,1,0:T(8,128)(2,1)S(1)} %get-tuple-element.173), channel_id=1, source_target_pairs={{0,1},{1,0},{2,6},{3,7},{4,5},{5,4},{6,2},{7,3},{8,9},{9,8},{10,14... | collective-permute-start | bytes 1572872 | tf_op jit(solution)/shard_map/ppermute | solution.py:349
  97.4 14.2 %collective-permute-start.20 = (bf16[272,1024]{1,0:T(8,128)(2,1)S(1)}, bf16[272,1024]{1,0:T(8,128)(2,1)S(1)}, u32[]{:S(2)}, u32[]{:S(2)}) collective-permute-start(bf16[272,1024]{1,0:T(8,128)(2,1)S(1)} %collective-permute-done.17.refs_1_), channel_id=1, source_target_pairs={{0,1},{1,0},{2,6},{3,7},{4,5},{5,4},{6,2},{7,3},{8,9},{9,8},{10,14... | collective-permute-start | bytes 1671176 | tf_op jit(solution)/shard_map/ppermute | solution.py:349
  113.2 6.0 %collective-permute-start.23 = (bf16[2,144,2048]{2,1,0:T(8,128)(2,1)S(1)}, bf16[2,144,2048]{2,1,0:T(8,128)(2,1)S(1)}, u32[]{:S(2)}, u32[]{:S(2)}) collective-permute-start(bf16[2,144,2048]{2,1,0:T(8,128)(2,1)S(1)} %get-tuple-element.190), channel_id=1, source_target_pairs={{0,2},{1,3},{2,0},{3,1},{4,6},{5,7},{6,4},{7,5},{8,10},{9,11},{10,... | collective-permute-start | bytes 3538952 | tf_op jit(solution)/shard_map/ppermute | solution.py:349
  113.3 3.7 %collective-permute-start.25 = (bf16[144,2048]{1,0:T(8,128)(2,1)S(1)}, bf16[144,2048]{1,0:T(8,128)(2,1)S(1)}, u32[]{:S(2)}, u32[]{:S(2)}) collective-permute-start(bf16[144,2048]{1,0:T(8,128)(2,1)S(1)} %get-tuple-element.205), channel_id=1, source_target_pairs={{0,2},{1,3},{2,0},{3,1},{4,6},{5,7},{6,4},{7,5},{8,10},{9,11},{10,... | collective-permute-start | bytes 1769480 | tf_op jit(solution)/shard_map/ppermute | solution.py:349
  113.7 40.2 %collective-permute-start.19 = (bf16[128,1024]{1,0:T(8,128)(2,1)S(1)}, bf16[128,1024]{1,0:T(8,128)(2,1)S(1)}, u32[]{:S(2)}, u32[]{:S(2)}) collective-permute-start(bf16[128,1024]{1,0:T(8,128)(2,1)S(1)} %fusion.14), channel_id=1, source_target_pairs={{0,4},{1,5},{2,3},{3,2},{4,0},{5,1},{6,7},{7,6},{8,12},{9,13},{10,... | collective-permute-start | bytes 786440 | tf_op jit(solution)/shard_map/ppermute | solution.py:349
  115.2 9.5 %collective-permute-start.30 = (bf16[128,1024]{1,0:T(8,128)(2,1)S(1)}, bf16[128,1024]{1,0:T(8,128)(2,1)S(1)}, u32[]{:S(2)}, u32[]{:S(2)}) collective-permute-start(bf16[128,1024]{1,0:T(8,128)(2,1)S(1)} %fusion.15), channel_id=1, source_target_pairs={{0,4},{1,5},{2,3},{3,2},{4,0},{5,1},{6,7},{7,6},{8,12},{9,13},{10,... | collective-permute-start | bytes 786440 | tf_op jit(solution)/shard_map/ppermute | solution.py:349
  118.2 9.7 %collective-permute-start.26 = (bf16[2,128,1024]{2,1,0:T(8,128)(2,1)S(1)}, bf16[2,128,1024]{2,1,0:T(8,128)(2,1)S(1)}, u32[]{:S(2)}, u32[]{:S(2)}) collective-permute-start(bf16[2,128,1024]{2,1,0:T(8,128)(2,1)S(1)} %get-tuple-element.207), channel_id=1, source_target_pairs={{0,1},{1,0},{2,6},{3,7},{4,5},{5,4},{6,2},{7,3},{8,9},{9,8},{10,14... | collective-permute-start | bytes 1572872 | tf_op jit(solution)/shard_map/ppermute | solution.py:349
  124.1 4.0 %collective-permute-start.24 = (bf16[144,2048]{1,0:T(8,128)(2,1)S(1)}, bf16[144,2048]{1,0:T(8,128)(2,1)S(1)}, u32[]{:S(2)}, u32[]{:S(2)}) collective-permute-start(bf16[144,2048]{1,0:T(8,128)(2,1)S(1)} %get-tuple-element.200), channel_id=1, source_target_pairs={{0,2},{1,3},{2,0},{3,1},{4,6},{5,7},{6,4},{7,5},{8,10},{9,11},{10,... | collective-permute-start | bytes 1769480 | tf_op jit(solution)/shard_map/ppermute | solution.py:349
  124.9 10.2 %collective-permute-start.31 = (bf16[128,1024]{1,0:T(8,128)(2,1)S(1)}, bf16[128,1024]{1,0:T(8,128)(2,1)S(1)}, u32[]{:S(2)}, u32[]{:S(2)}) collective-permute-start(bf16[128,1024]{1,0:T(8,128)(2,1)S(1)} %fusion.4), channel_id=1, source_target_pairs={{0,8},{1,9},{2,10},{3,11},{4,12},{5,13},{6,14},{7,15},{8,24},{9,25... | collective-permute-start | bytes 786440 | tf_op jit(solution)/shard_map/ppermute | solution.py:349
  129.4 9.1 %collective-permute-start.29 = (bf16[128,1024]{1,0:T(8,128)(2,1)S(1)}, bf16[128,1024]{1,0:T(8,128)(2,1)S(1)}, u32[]{:S(2)}, u32[]{:S(2)}) collective-permute-start(bf16[128,1024]{1,0:T(8,128)(2,1)S(1)} %fusion.16), channel_id=1, source_target_pairs={{0,4},{1,5},{2,3},{3,2},{4,0},{5,1},{6,7},{7,6},{8,12},{9,13},{10,... | collective-permute-start | bytes 786440 | tf_op jit(solution)/shard_map/ppermute | solution.py:349
  130.7 10.2 %collective-permute-start.27 = (bf16[2,128,1024]{2,1,0:T(8,128)(2,1)S(1)}, bf16[2,128,1024]{2,1,0:T(8,128)(2,1)S(1)}, u32[]{:S(2)}, u32[]{:S(2)}) collective-permute-start(bf16[2,128,1024]{2,1,0:T(8,128)(2,1)S(1)} %get-tuple-element.208), channel_id=1, source_target_pairs={{0,1},{1,0},{2,6},{3,7},{4,5},{5,4},{6,2},{7,3},{8,9},{9,8},{10,14... | collective-permute-start | bytes 1572872 | tf_op jit(solution)/shard_map/ppermute | solution.py:349
  138.6 7.6 %collective-permute-start.32 = (bf16[128,1024]{1,0:T(8,128)(2,1)S(1)}, bf16[128,1024]{1,0:T(8,128)(2,1)S(1)}, u32[]{:S(2)}, u32[]{:S(2)}) collective-permute-start(bf16[128,1024]{1,0:T(8,128)(2,1)S(1)} %fusion.7), channel_id=1, source_target_pairs={{0,8},{1,9},{2,10},{3,11},{4,12},{5,13},{6,14},{7,15},{8,24},{9,25... | collective-permute-start | bytes 786440 | tf_op jit(solution)/shard_map/ppermute | solution.py:349
  141.2 6.4 %collective-permute-start.28 = (bf16[128,1024]{1,0:T(8,128)(2,1)S(1)}, bf16[128,1024]{1,0:T(8,128)(2,1)S(1)}, u32[]{:S(2)}, u32[]{:S(2)}) collective-permute-start(bf16[128,1024]{1,0:T(8,128)(2,1)S(1)} %fusion.17), channel_id=1, source_target_pairs={{0,4},{1,5},{2,3},{3,2},{4,0},{5,1},{6,7},{7,6},{8,12},{9,13},{10,... | collective-permute-start | bytes 786440 | tf_op jit(solution)/shard_map/ppermute | solution.py:349
  147.8 8.6 %collective-permute-start.33 = (bf16[128,1024]{1,0:T(8,128)(2,1)S(1)}, bf16[128,1024]{1,0:T(8,128)(2,1)S(1)}, u32[]{:S(2)}, u32[]{:S(2)}) collective-permute-start(bf16[128,1024]{1,0:T(8,128)(2,1)S(1)} %fusion.10), channel_id=1, source_target_pairs={{0,8},{1,9},{2,10},{3,11},{4,12},{5,13},{6,14},{7,15},{8,24},{9,25... | collective-permute-start | bytes 786440 | tf_op jit(solution)/shard_map/ppermute | solution.py:349

commit v7 on v6

--- a/solution.py
+++ b/solution.py
@@ -351,6 +351,10 @@
     def to_ring(value):
         return permute(value, lambda e, h: (after[e // 4] * 4 + e % 4, h))
 
+    def to_owner(value, back):
+        owner = {order[i]: order[(i - back) % chunks] for i in range(chunks)}
+        return permute(value, lambda e, h: (owner[e // 4] * 4 + e % 4, h))
+
     def to_core(value):
         return permute(value, lambda e, h: (e ^ 1, h))
 
@@ -365,21 +369,23 @@
     share = pack_share(tokens, out_grad, routes, combine)
     weights = load_weights((w_gate[0], w_up[0], w_down[0]))
 
-    def summed(picks, near, far, beside=()):
-        keep, send = place_rows(place, picks, near, to_core(far), rows, width)
-        send, beside = lax.optimization_barrier((send, beside))
-        mine = keep + to_second(send).astype(jnp.float32)
-        return mine[0], mine[1].astype(jnp.bfloat16), beside
+    def tied(values, mark):
+        return lax.optimization_barrier((values, mark))[0]
+
+    def placed(picks, near, far):
+        return place_rows(place, picks, near, to_core(far), rows, width)
+
+    def added(keep, came):
+        return keep + came.astype(jnp.float32)
 
     ring_sends = [("s", 1)] + [(kind, c) for c in range(2, chunks) for kind in ("s", "f")]
     ring_sends = [key for key in ring_sends if key[1] < chunks]
     plane_sends = [("f", 0), ("a", 0), ("f", 1), ("b", 0)] + [(kind, c) for c in range(1, chunks) for kind in ("a", "b")]
     plane_sends = [key for key in plane_sends if key[1] < chunks]
     have = {("s", 0): share}
-    kept, parts, picked, done = None, None, None, 0
-    sums, sends = [], []
-    next_pick = 0
-    while done < chunks:
+    kept, picked, parts, waiting = None, None, None, None
+    late, done = [], 0
+    while plane_sends:
         came = {}
         planned = [key for key in plane_sends if (("f" if key[0] == "b" else "s"), key[1]) in have][:2]
         for kind, c in planned:
@@ -389,50 +395,39 @@
         if ring_sends and (ring_sends[0][0], ring_sends[0][1] - 1) in have:
             kind, c = ring_sends.pop(0)
             came[kind, c] = to_ring(have[kind, c - 1])
-        for i in range(len(sums)):
-            if sends[i] is not None:
-                sums[i], sends[i] = sums[i] + to_first(sends[i]).astype(jnp.float32), None
-        if parts is not None:
-            mine, send, _ = summed(*parts)
-            sums.append(mine)
-            sends.append(send)
-            parts = None
-        arrived = [have.get((kind, next_pick)) for kind in "sfab"]
-        last = next_pick + 1 == chunks
+        ready, waiting = waiting, placed(*parts) if parts is not None else None
+        if ready is not None:
+            keep, send = ready
+            late.append((keep, to_second(send if waiting is None else tied(send, waiting[1]))))
+        parts = None
         if picked is not None:
             mine, theirs, picks = picked
-            near, far, *kept = run_experts(done, chunks, mine, theirs, weights, kept)
-            parts = picks, near, far
-            picked = None
+            near, far, *kept = run_experts(done, chunks, mine, to_core(theirs), weights, kept)
+            parts, picked = (picks, near, far), None
             done += 1
-        if all(value is not None for value in arrived) and next_pick < chunks:
-            mine, theirs, picks = pick_rows(place, arrived, top, rows, pair_slots)
-            picked = mine, to_core(theirs), picks
-            next_pick += 1
-            if last:
-                if parts is not None:
-                    mine, send, _ = summed(*parts)
-                    sums.append(mine)
-                    sends.append(send)
-                mine, theirs, picks = picked
-                near, far, *kept = run_experts(done, chunks, mine, theirs, weights, kept)
-                parts = picks, near, far
-                done += 1
-        if done < chunks:
-            came, sends, parts, picked, weights = lax.optimization_barrier((came, sends, parts, picked, weights))
+        if plane_sends and all((kind, done) in have for kind in "sfab"):
+            picked = pick_rows(place, [have.pop((kind, done)) for kind in "sfab"], top, rows, pair_slots)
+        came, have, picked, parts, waiting, weights = lax.optimization_barrier(
+            (came, have, picked, parts, waiting, weights)
+        )
         have.update(came)
-    mine, send, sends = summed(*parts, sends)
-    sums.append(mine)
-    sends.append(send)
-    running = None
-    for c in range(chunks):
-        if sends[c] is not None:
-            sums[c] = sums[c] + to_first(sends[c]).astype(jnp.float32)
-        if c > 0:
-            running = sums[c] if c == 1 else sums[c] + running.astype(jnp.float32)
-            running = to_ring(running.astype(jnp.bfloat16))
-    own = sums[0]
-    grad_tokens = (own if running is None else own + running.astype(jnp.float32)).astype(jnp.bfloat16)
+    mine, theirs, picks = pick_rows(place, [have[kind, done] for kind in "sfab"], top, rows, pair_slots)
+    if waiting is not None:
+        keep, send = waiting
+        late.append((keep, to_second(tied(send, theirs))))
+    if parts is not None:
+        keep, send = placed(*tied(parts, theirs))
+        late.append((keep, to_second(send)))
+    near, far, *kept = run_experts(done, chunks, mine, to_core(theirs), weights, kept)
+    keep, send = placed(picks, near, far)
+    late.append((keep, to_second(send)))
+    marks = ([near] * chunks + [send])[-(len(late) - 1):] + [None]
+    grad_tokens = 0.0
+    for c, ((keep, came), mark) in enumerate(zip(late, marks)):
+        pair = added(keep, came if mark is None else tied(came, mark))
+        total = added(pair[0], to_first(pair[1].astype(jnp.bfloat16)))
+        grad_tokens += total if c == 0 else to_owner(total.astype(jnp.bfloat16), c).astype(jnp.float32)
+    grad_tokens = grad_tokens.astype(jnp.bfloat16)
     rows_x, rows_g, acts, gate_term, up_term = kept
     grad_down = lax.dot_general(acts, rows_g, CONTRACT_FIRST, preferred_element_type=jnp.float32)
     grad_gate = lax.dot_general(gate_term, rows_x, CONTRACT_FIRST, preferred_element_type=jnp.float32)

time: 157 us -> 162 us (1.032)
  waiting for transfers between devices: 68.2 us -> 75.3 us
  starting transfers between devices: 38.2 us -> 32.1 us
  local copies, waits for them, and re-layouts: 0.14 us -> 3.87 us
    ppermute x34, waiting for transfers between devices: 68.2 us -> 75.3 us  [permute(): return lax.ppermute(value, ('expert', 'etp'), pairs)]
    ppermute x34, starting transfers between devices: 38.2 us -> 32.1 us  [permute(): return lax.ppermute(value, ('expert', 'etp'), pairs)]
    unnamed x8 -> x16, local copies, waits for them, and re-layouts: 0.01 us -> 3.74 us
  transfers between devices with their start and end apart: 34 -> 34, of which waited for: 16 -> 17; matrix products, arithmetic and copies ran while one was open for 7% -> 7% of each run, Pallas kernels for 19% -> 21%
where the time goes in v7:
time: 162 us
  waiting for transfers between devices  75.3 us (46%)
  Pallas kernels  38.1 us (24%)
  starting transfers between devices  32.1 us (20%)
  matrix products  10.1 us (6%)
  local copies, waits for them, and re-layouts  3.87 us (2%)
  other arithmetic  1.76 us (1%)
    ppermute x34, waiting for transfers between devices, permute(): return lax.ppermute(value, ('expert', 'etp'), pairs)  75.3 us
    ppermute x34, starting transfers between devices, permute(): return lax.ppermute(value, ('expert', 'etp'), pairs)  32.1 us
    pallas_call x4, Pallas kernels, run_experts(): pl.pallas_call(functools.partial(expert_kernel, index, kept is not None),...  19.8 us
    pallas_call x4, Pallas kernels, pick_rows(): pl.pallas_call(functools.partial(pick_kernel, top, rows), in_specs=[pl.Bl...  6.75 us
    pallas_call x4, Pallas kernels, place_rows(): pl.pallas_call(place_kernel, in_specs=[pl.BlockSpec(memory_space=pltpu.SM...  5.08 us
    pallas_call x1, Pallas kernels, load_weights(): pl.pallas_call(load_kernel, in_specs=[pl.BlockSpec(memory_space=pltpu.HBM...  4.62 us
    unnamed x16, local copies, waits for them, and re-layouts  3.74 us
    dot_general x1, matrix products, gather_body(): lax.dot_general(acts, rows_g, CONTRACT_FIRST, preferred_element_type=jnp....  3.38 us
  transfers between devices with their start and end apart: 34, of which 17 were waited for; matrix products, arithmetic and copies ran while one was open for 7% of the time, Pallas kernels for 21%

profile of v7, /device:TPU:0, one launch (start us, length us, event | category | flops | bytes accessed | tf_op | source)
XLA Modules:
  0.0 162.2 jit_solution(15412459880554840156)
XLA Ops:
  0.6 1.9 %pack.1.refs_0_ = bf16[272,1024]{1,0:T(8,128)(2,1)} custom-call(bf16[128,1024]{1,0:T(8,128)(2,1)} %tokens_ref.1, bf16[128,1024]{1,0:T(8,128)(2,1)} %grads_ref.1, s32[8,128]{1,0:T(8,128)} %bitcast.61, f32[8,128]{1,0:T(8,128)} %bitcast.62), custom_call_target="tpu_custom_call" | custom-call | bytes 1048576 | tf_op jit(solution)/shard_map/pack/pallas_call | solution.py:128
  2.5 2.9 %collective-permute-start = (bf16[272,1024]{1,0:T(8,128)(2,1)}, bf16[272,1024]{1,0:T(8,128)(2,1)S(1)}, u32[]{:S(2)}, u32[]{:S(2)}) collective-permute-start(bf16[272,1024]{1,0:T(8,128)(2,1)} %pack.1.refs_0_), channel_id=1, source_target_pairs={{0,1},{1,0},{2,6},{3,7},{4,5},{5,4},{6,2},{7,3},{8,9},{9,8},{10,14... | collective-permute-start | bytes 1671176 | tf_op jit(solution)/shard_map/ppermute | solution.py:349
  5.5 1.5 collective-permute-start.1
  7.0 1.6 collective-permute-start.2
  8.6 4.6 %load.1 = (bf16[384,2048]{1,0:T(8,128)(2,1)}, bf16[384,2048]{1,0:T(8,128)(2,1)}, bf16[384,2048]{1,0:T(8,128)(2,1)}) custom-call(bf16[384,2048]{1,0:T(8,128)(2,1)} %bitcast.58, bf16[384,2048]{1,0:T(8,128)(2,1)} %bitcast.59, bf16[384,2048]{1,0:T(8,128)(2,1)} %bitcast.60), custom_call_target="tpu_custom_call" | custom-call | tf_op jit(solution)/shard_map/load/pallas_call | solution.py:148
  13.2 5.5 %collective-permute-done.refs_2_ = bf16[272,1024]{1,0:T(8,128)(2,1)S(1)} collective-permute-done((bf16[272,1024]{1,0:T(8,128)(2,1)}, bf16[272,1024]{1,0:T(8,128)(2,1)S(1)}, u32[]{:S(2)}, u32[]{:S(2)}) %collective-permute-start) | collective-permute-done | bytes 557088 | tf_op jit(solution)/shard_map/ppermute | solution.py:349
  18.7 3.2 %collective-permute-done.2.refs_0_ = bf16[272,1024]{1,0:T(8,128)(2,1)S(1)} collective-permute-done((bf16[272,1024]{1,0:T(8,128)(2,1)}, bf16[272,1024]{1,0:T(8,128)(2,1)S(1)}, u32[]{:S(2)}, u32[]{:S(2)}) %collective-permute-start.2) | collective-permute-done | bytes 557088 | tf_op jit(solution)/shard_map/ppermute | solution.py:349
  24.7 11.2 %collective-permute-done.3.refs_3_ = bf16[272,1024]{1,0:T(8,128)(2,1)S(1)} collective-permute-done((bf16[272,1024]{1,0:T(8,128)(2,1)S(1)}, bf16[272,1024]{1,0:T(8,128)(2,1)S(1)}, u32[]{:S(2)}, u32[]{:S(2)}) %collective-permute-start.3) | collective-permute-done | bytes 557088 | tf_op jit(solution)/shard_map/ppermute | solution.py:349
  37.3 1.2 collective-permute-start.6
  40.2 1.1 copy-done.5
  41.2 1.1 copy-done.7
  42.3 1.5 pick.4
  43.8 3.1 %collective-permute-done.6.refs_2_ = bf16[272,1024]{1,0:T(8,128)(2,1)} collective-permute-done((bf16[272,1024]{1,0:T(8,128)(2,1)S(1)}, bf16[272,1024]{1,0:T(8,128)(2,1)}, u32[]{:S(2)}, u32[]{:S(2)}) %collective-permute-start.6) | collective-permute-done | bytes 557088 | tf_op jit(solution)/shard_map/ppermute | solution.py:349
  46.9 6.0 %collective-permute-done.7.refs_3_ = bf16[272,1024]{1,0:T(8,128)(2,1)} collective-permute-done((bf16[272,1024]{1,0:T(8,128)(2,1)S(1)}, bf16[272,1024]{1,0:T(8,128)(2,1)}, u32[]{:S(2)}, u32[]{:S(2)}) %collective-permute-start.7) | collective-permute-done | bytes 557088 | tf_op jit(solution)/shard_map/ppermute | solution.py:349
  53.0 1.3 collective-permute-start.9
  55.9 2.2 %pick.5 = (bf16[2,144,2048]{2,1,0:T(8,128)(2,1)S(1)}, bf16[2,144,2048]{2,1,0:T(8,128)(2,1)S(1)}, bf16[288,256]{1,0:T(8,128)(2,1)S(1)}) custom-call(s32[3]{0:T(128)S(1)} %pad_add_fusion.place_ref, bf16[272,1024]{1,0:T(8,128)(2,1)S(1)} %collective-permute-done.2.refs_0_, bf16[272,1024]{1,0:T(8,128)(2,1)S(1)} %collective-permute-done.4.refs_1_, ...), custom_call_target="tpu_custom_call" | custom-call | flops 2415919104 | bytes 4587520 | tf_op jit(solution)/shard_map/pick/pallas_call | solution.py:272
  58.1 4.9 %experts.4 = (bf16[144,2048]{1,0:T(8,128)(2,1)S(1)}, bf16[144,2048]{1,0:T(8,128)(2,1)S(1)}, bf16[1152,2048]{1,0:T(8,128)(2,1)S(1)}, bf16[1152,2048]{1,0:T(8,128)...) custom-call(bf16[2,144,2048]{2,1,0:T(8,128)(2,1)S(1)} %get-tuple-element.165., ...), custom_call_target="tpu_custom_call" | custom-call | flops 4529848320 | bytes 10100736 | tf_op jit(solution)/shard_map/experts/pallas_call | solution.py:296
  63.0 5.6 %collective-permute-done.10.refs_3_ = bf16[272,1024]{1,0:T(8,128)(2,1)S(1)} collective-permute-done((bf16[272,1024]{1,0:T(8,128)(2,1)S(1)}, bf16[272,1024]{1,0:T(8,128)(2,1)S(1)}, u32[]{:S(2)}, u32[]{:S(2)}) %collective-permute-start.10) | collective-permute-done | bytes 557088 | tf_op jit(solution)/shard_map/ppermute | solution.py:349
  68.5 1.8 %collective-permute-done.11.refs_0_ = bf16[272,1024]{1,0:T(8,128)(2,1)S(1)} collective-permute-done((bf16[272,1024]{1,0:T(8,128)(2,1)S(1)}, bf16[272,1024]{1,0:T(8,128)(2,1)S(1)}, u32[]{:S(2)}, u32[]{:S(2)}) %collective-permute-start.11) | collective-permute-done | bytes 557088 | tf_op jit(solution)/shard_map/ppermute | solution.py:349
  70.9 1.0 collective-permute-start.13
  72.7 1.5 pick.6
  74.2 1.3 place.4
  75.5 4.9 %experts.5 = (bf16[144,2048]{1,0:T(8,128)(2,1)S(1)}, bf16[144,2048]{1,0:T(8,128)(2,1)S(1)}, bf16[1152,2048]{1,0:T(8,128)(2,1)S(1)}, bf16[1152,2048]{1,0:T(8,128)...) custom-call(bf16[2,144,2048]{2,1,0:T(8,128)(2,1)S(1)} %get-tuple-ele, ...), custom_call_target="tpu_custom_call", output_to_operand_aliasing={{2}: (5, {}), {3}: (6, {}), {4}: (7, {}), {5}: (8, {}), {6}... | custom-call | flops 4529848320 | bytes 10100736 | tf_op jit(solution)/shard_map/experts/pallas_call | solution.py:296
  80.4 5.9 %collective-permute-done.14.refs_1_ = bf16[272,1024]{1,0:T(8,128)(2,1)S(1)} collective-permute-done((bf16[272,1024]{1,0:T(8,128)(2,1)S(1)}, bf16[272,1024]{1,0:T(8,128)(2,1)S(1)}, u32[]{:S(2)}, u32[]{:S(2)}) %collective-permute-start.14) | collective-permute-done | bytes 557088 | tf_op jit(solution)/shard_map/ppermute | solution.py:349
  86.8 1.2 collective-permute-start.19
  88.1 1.9 %collective-permute-done.17.far_ref = bf16[144,2048]{1,0:T(8,128)(2,1)S(1)} collective-permute-done((bf16[144,2048]{1,0:T(8,128)(2,1)S(1)}, bf16[144,2048]{1,0:T(8,128)(2,1)S(1)}, u32[]{:S(2)}, u32[]{:S(2)}) %collective-permute-start.17) | collective-permute-done | bytes 589856 | tf_op jit(solution)/shard_map/ppermute | solution.py:349
  90.0 1.3 place.5
  91.3 4.9 %experts.6 = (bf16[144,2048]{1,0:T(8,128)(2,1)S(1)}, bf16[144,2048]{1,0:T(8,128)(2,1)S(1)}, bf16[1152,2048]{1,0:T(8,128)(2,1)S(1)}, bf16[1152,2048]{1,0:T(8,128)...) custom-call(bf16[2,144,2048]{2,1,0:T(8,128)(2,1)S(1)} %get-tuple-ele, ...), custom_call_target="tpu_custom_call", output_to_operand_aliasing={{2}: (5, {}), {3}: (6, {}), {4}: (7, {}), {5}: (8, {}), {6}... | custom-call | flops 4529848320 | bytes 10100736 | tf_op jit(solution)/shard_map/experts/pallas_call | solution.py:296
  96.4 1.5 pick.7
  98.5 1.2 collective-permute-start.18
  100.5 1.2 collective-permute-done.26.far_ref
  101.6 1.3 place.6
  102.9 1.3 collective-permute-start.27
  104.2 5.1 %experts.7 = (bf16[144,2048]{1,0:T(8,128)(2,1)S(1)}, bf16[144,2048]{1,0:T(8,128)(2,1)S(1)}, bf16[1152,2048]{1,0:T(8,128)(2,1)S(1)}, bf16[1152,2048]{1,0:T(8,128)...) custom-call(bf16[2,144,2048]{2,1,0:T(8,128)(2,1)S(1)} %get-tuple-ele, ...), custom_call_target="tpu_custom_call", output_to_operand_aliasing={{2}: (5, {}), {3}: (6, {}), {4}: (7, {}), {5}: (8, {}), {6}... | custom-call | flops 4529848320 | bytes 10100736 | tf_op jit(solution)/shard_map/experts/pallas_call | solution.py:296
  109.8 3.5 %collective-permute-done.23 = bf16[2,128,1024]{2,1,0:T(8,128)(2,1)S(1)} collective-permute-done((bf16[2,128,1024]{2,1,0:T(8,128)(2,1)S(1)}, bf16[2,128,1024]{2,1,0:T(8,128)(2,1)S(1)}, u32[]{:S(2)}, u32[]{:S(2)}) %collective-permute-start.23) | collective-permute-done | bytes 524320 | tf_op jit(solution)/shard_map/ppermute | solution.py:349
  113.4 1.8 %collective-permute-start.24 = (bf16[128,1024]{1,0:T(8,128)(2,1)S(1)}, bf16[128,1024]{1,0:T(8,128)(2,1)S(1)}, u32[]{:S(2)}, u32[]{:S(2)}) collective-permute-start(bf16[128,1024]{1,0:T(8,128)(2,1)S(1)} %fusion.15), channel_id=1, source_target_pairs={{0,4},{1,5},{2,3},{3,2},{4,0},{5,1},{6,7},{7,6},{8,12},{9,13},{10,... | collective-permute-start | bytes 786440 | tf_op jit(solution)/shard_map/ppermute | solution.py:349
  115.8 3.4 %fusion = bf16[1,384,2048]{2,1,0:T(8,128)(2,1)} fusion(bf16[1152,384]{1,0:T(8,128)(2,1)S(1)} %get-tuple-element.255, bf16[1152,2048]{1,0:T(8,128)(2,1)S(1)} %get-tuple-element.256), kind=kOutput, calls=%fused_computation.3 | convolution fusion | flops 1812725760 | bytes 7176192 | tf_op jit(solution)/shard_map/dot_general | solution.py:433
  119.2 3.4 %fusion.1 = bf16[1,384,2048]{2,1,0:T(8,128)(2,1)} fusion(bf16[1152,384]{1,0:T(8,128)(2,1)S(1)} %get-tuple-element.257, bf16[1152,2048]{1,0:T(8,128)(2,1)S(1)} %get-tuple-element.256), kind=kOutput, calls=%fused_computation.4 | convolution fusion | flops 1812725760 | bytes 7176192 | tf_op jit(solution)/shard_map/dot_general | solution.py:434
  122.6 1.3 place.7
  123.9 1.3 collective-permute-start.31
  125.4 1.6 collective-permute-start.29
  127.0 8.4 %collective-permute-done.31 = bf16[2,128,1024]{2,1,0:T(8,128)(2,1)S(1)} collective-permute-done((bf16[2,128,1024]{2,1,0:T(8,128)(2,1)S(1)}, bf16[2,128,1024]{2,1,0:T(8,128)(2,1)S(1)}, u32[]{:S(2)}, u32[]{:S(2)}) %collective-permute-start.31) | collective-permute-done | bytes 524320 | tf_op jit(solution)/shard_map/ppermute | solution.py:349
  135.9 1.6 collective-permute-start.25
  137.6 2.2 %collective-permute-start.30 = (bf16[128,1024]{1,0:T(8,128)(2,1)S(1)}, bf16[128,1024]{1,0:T(8,128)(2,1)S(1)}, u32[]{:S(2)}, u32[]{:S(2)}) collective-permute-start(bf16[128,1024]{1,0:T(8,128)(2,1)S(1)} %fusion.6), channel_id=1, source_target_pairs={{0,24},{1,25},{2,26},{3,27},{4,28},{5,29},{6,30},{7,31},{8,16},{9,... | collective-permute-start | bytes 786440 | tf_op jit(solution)/shard_map/ppermute | solution.py:349
  139.8 2.2 %collective-permute-done.32 = bf16[128,1024]{1,0:T(8,128)(2,1)S(1)} collective-permute-done((bf16[128,1024]{1,0:T(8,128)(2,1)S(1)}, bf16[128,1024]{1,0:T(8,128)(2,1)S(1)}, u32[]{:S(2)}, u32[]{:S(2)}) %collective-permute-start.32) | collective-permute-done | bytes 262176 | tf_op jit(solution)/shard_map/ppermute | solution.py:349
  142.9 3.4 %fusion.2 = bf16[1,384,2048]{2,1,0:T(8,128)(2,1)} fusion(bf16[1152,384]{1,0:T(8,128)(2,1)S(1)} %get-tuple-element.258, bf16[1152,2048]{1,0:T(8,128)(2,1)S(1)} %get-tuple-element.259), kind=kOutput, calls=%fused_computation.5 | convolution fusion | flops 1812725760 | bytes 7176192 | tf_op jit(solution)/shard_map/dot_general | solution.py:432
  146.2 6.2 %collective-permute-done.30 = bf16[128,1024]{1,0:T(8,128)(2,1)S(1)} collective-permute-done((bf16[128,1024]{1,0:T(8,128)(2,1)S(1)}, bf16[128,1024]{1,0:T(8,128)(2,1)S(1)}, u32[]{:S(2)}, u32[]{:S(2)}) %collective-permute-start.30) | collective-permute-done | bytes 262176 | tf_op jit(solution)/shard_map/ppermute | solution.py:349
  152.4 8.8 %collective-permute-done.33 = bf16[128,1024]{1,0:T(8,128)(2,1)S(1)} collective-permute-done((bf16[128,1024]{1,0:T(8,128)(2,1)S(1)}, bf16[128,1024]{1,0:T(8,128)(2,1)S(1)}, u32[]{:S(2)}, u32[]{:S(2)}) %collective-permute-start.33) | collective-permute-done | bytes 262176 | tf_op jit(solution)/shard_map/ppermute | solution.py:349
  (66 shorter events, 14.6 us)
Async XLA Ops:
  2.5 16.2 %collective-permute-start = (bf16[272,1024]{1,0:T(8,128)(2,1)}, bf16[272,1024]{1,0:T(8,128)(2,1)S(1)}, u32[]{:S(2)}, u32[]{:S(2)}) collective-permute-start(bf16[272,1024]{1,0:T(8,128)(2,1)} %pack.1.refs_0_), channel_id=1, source_target_pairs={{0,1},{1,0},{2,6},{3,7},{4,5},{5,4},{6,2},{7,3},{8,9},{9,8},{10,14... | collective-permute-start | bytes 1671176 | tf_op jit(solution)/shard_map/ppermute | solution.py:349
  5.5 13.2 %collective-permute-start.1 = (bf16[272,1024]{1,0:T(8,128)(2,1)}, bf16[272,1024]{1,0:T(8,128)(2,1)S(1)}, u32[]{:S(2)}, u32[]{:S(2)}) collective-permute-start(bf16[272,1024]{1,0:T(8,128)(2,1)} %pack.1.refs_0_), channel_id=1, source_target_pairs={{0,4},{1,5},{2,3},{3,2},{4,0},{5,1},{6,7},{7,6},{8,12},{9,13},{10,... | collective-permute-start | bytes 1671176 | tf_op jit(solution)/shard_map/ppermute | solution.py:349
  7.0 14.9 %collective-permute-start.2 = (bf16[272,1024]{1,0:T(8,128)(2,1)}, bf16[272,1024]{1,0:T(8,128)(2,1)S(1)}, u32[]{:S(2)}, u32[]{:S(2)}) collective-permute-start(bf16[272,1024]{1,0:T(8,128)(2,1)} %pack.1.refs_0_), channel_id=1, source_target_pairs={{0,8},{1,9},{2,10},{3,11},{4,12},{5,13},{6,14},{7,15},{8,24},{9,25... | collective-permute-start | bytes 1671176 | tf_op jit(solution)/shard_map/ppermute | solution.py:349
  8.6 31.6 %copy-start.3 = (bf16[272,1024]{1,0:T(8,128)(2,1)S(1)}, bf16[272,1024]{1,0:T(8,128)(2,1)}, u32[]{:S(2)}) copy-start(bf16[272,1024]{1,0:T(8,128)(2,1)} %pack.1.refs_0_) | copy-start | bytes 1671172
  21.9 14.0 %collective-permute-start.3 = (bf16[272,1024]{1,0:T(8,128)(2,1)S(1)}, bf16[272,1024]{1,0:T(8,128)(2,1)S(1)}, u32[]{:S(2)}, u32[]{:S(2)}) collective-permute-start(bf16[272,1024]{1,0:T(8,128)(2,1)S(1)} %collective-permute-done.1.refs_1_), channel_id=1, source_target_pairs={{0,1},{1,0},{2,6},{3,7},{4,5},{5,4},{6,2},{7,3},{8,9},{9,8},{10,14... | collective-permute-start | bytes 1671176 | tf_op jit(solution)/shard_map/ppermute | solution.py:349
  22.5 0.8 copy-start.4
  23.3 13.4 %collective-permute-start.4 = (bf16[272,1024]{1,0:T(8,128)(2,1)S(1)}, bf16[272,1024]{1,0:T(8,128)(2,1)S(1)}, u32[]{:S(2)}, u32[]{:S(2)}) collective-permute-start(bf16[272,1024]{1,0:T(8,128)(2,1)S(1)} %collective-permute-done.2.refs_0_), channel_id=1, source_target_pairs={{0,4},{1,5},{2,3},{3,2},{4,0},{5,1},{6,7},{7,6},{8,12},{9,13},{10,... | collective-permute-start | bytes 1671176 | tf_op jit(solution)/shard_map/ppermute | solution.py:349
  23.8 13.5 %collective-permute-start.5 = (bf16[272,1024]{1,0:T(8,128)(2,1)S(1)}, bf16[272,1024]{1,0:T(8,128)(2,1)S(1)}, u32[]{:S(2)}, u32[]{:S(2)}) collective-permute-start(bf16[272,1024]{1,0:T(8,128)(2,1)S(1)} %collective-permute-done.2.refs_0_), channel_id=1, source_target_pairs={{0,8},{1,9},{2,10},{3,11},{4,12},{5,13},{6,14},{7,15},{8,24},{9,25... | collective-permute-start | bytes 1671176 | tf_op jit(solution)/shard_map/ppermute | solution.py:349
  35.9 0.8 copy-start.6
  37.3 9.6 %collective-permute-start.6 = (bf16[272,1024]{1,0:T(8,128)(2,1)S(1)}, bf16[272,1024]{1,0:T(8,128)(2,1)}, u32[]{:S(2)}, u32[]{:S(2)}) collective-permute-start(bf16[272,1024]{1,0:T(8,128)(2,1)S(1)} %collective-permute-done.2.refs_0_), channel_id=1, source_target_pairs={{0,1},{1,0},{2,6},{3,7},{4,5},{5,4},{6,2},{7,3},{8,9},{9,8},{10,14... | collective-permute-start | bytes 1671176 | tf_op jit(solution)/shard_map/ppermute | solution.py:349
  38.5 14.4 %collective-permute-start.7 = (bf16[272,1024]{1,0:T(8,128)(2,1)S(1)}, bf16[272,1024]{1,0:T(8,128)(2,1)}, u32[]{:S(2)}, u32[]{:S(2)}) collective-permute-start(bf16[272,1024]{1,0:T(8,128)(2,1)S(1)} %collective-permute-done.4.refs_1_), channel_id=1, source_target_pairs={{0,1},{1,0},{2,6},{3,7},{4,5},{5,4},{6,2},{7,3},{8,9},{9,8},{10,14... | collective-permute-start | bytes 1671176 | tf_op jit(solution)/shard_map/ppermute | solution.py:349
  39.3 13.6 %collective-permute-start.8 = (bf16[272,1024]{1,0:T(8,128)(2,1)S(1)}, bf16[272,1024]{1,0:T(8,128)(2,1)S(1)}, u32[]{:S(2)}, u32[]{:S(2)}) collective-permute-start(bf16[272,1024]{1,0:T(8,128)(2,1)S(1)} %collective-permute-done.4.refs_1_), channel_id=1, source_target_pairs={{0,8},{1,9},{2,10},{3,11},{4,12},{5,13},{6,14},{7,15},{8,24},{9,25... | collective-permute-start | bytes 1671176 | tf_op jit(solution)/shard_map/ppermute | solution.py:349
  40.2 1.1 copy-start.5
  41.2 1.1 copy-start.7
  52.9 5.2 %copy-start = (bf16[384,2048]{1,0:T(8,128)(2,1)S(1)}, bf16[384,2048]{1,0:T(8,128)(2,1)}, u32[]{:S(2)}) copy-start(bf16[384,2048]{1,0:T(8,128)(2,1)} %get-tuple-element.228.wg_ref) | copy-start | bytes 4718596
  52.9 5.2 %copy-start.1 = (bf16[384,2048]{1,0:T(8,128)(2,1)S(1)}, bf16[384,2048]{1,0:T(8,128)(2,1)}, u32[]{:S(2)}) copy-start(bf16[384,2048]{1,0:T(8,128)(2,1)} %get-tuple-element.229.wu_ref) | copy-start | bytes 4718596
  52.9 5.2 %copy-start.2 = (bf16[384,2048]{1,0:T(8,128)(2,1)S(1)}, bf16[384,2048]{1,0:T(8,128)(2,1)}, u32[]{:S(2)}) copy-start(bf16[384,2048]{1,0:T(8,128)(2,1)} %get-tuple-element.230.wd_ref) | copy-start | bytes 4718596
  52.9 5.2 %collective-permute-start.12 = (bf16[2,144,2048]{2,1,0:T(8,128)(2,1)S(1)}, bf16[2,144,2048]{2,1,0:T(8,128)(2,1)S(1)}, u32[]{:S(2)}, u32[]{:S(2)}) collective-permute-start(bf16[2,144,2048]{2,1,0:T(8,128)(2,1)S(1)} %get-tuple-element.166), channel_id=1, source_target_pairs={{0,2},{1,3},{2,0},{3,1},{4,6},{5,7},{6,4},{7,5},{8,10},{9,11},{10,... | collective-permute-start | bytes 3538952 | tf_op jit(solution)/shard_map/ppermute | solution.py:349
  53.0 10.0 %collective-permute-start.9 = (bf16[272,1024]{1,0:T(8,128)(2,1)S(1)}, bf16[272,1024]{1,0:T(8,128)(2,1)S(1)}, u32[]{:S(2)}, u32[]{:S(2)}) collective-permute-start(bf16[272,1024]{1,0:T(8,128)(2,1)S(1)} %collective-permute-done.5.refs_0_), channel_id=1, source_target_pairs={{0,1},{1,0},{2,6},{3,7},{4,5},{5,4},{6,2},{7,3},{8,9},{9,8},{10,14... | collective-permute-start | bytes 1671176 | tf_op jit(solution)/shard_map/ppermute | solution.py:349
  54.3 16.1 %collective-permute-start.11 = (bf16[272,1024]{1,0:T(8,128)(2,1)S(1)}, bf16[272,1024]{1,0:T(8,128)(2,1)S(1)}, u32[]{:S(2)}, u32[]{:S(2)}) collective-permute-start(bf16[272,1024]{1,0:T(8,128)(2,1)S(1)} %collective-permute-done.5.refs_0_), channel_id=1, source_target_pairs={{0,8},{1,9},{2,10},{3,11},{4,12},{5,13},{6,14},{7,15},{8,24},{9,25... | collective-permute-start | bytes 1671176 | tf_op jit(solution)/shard_map/ppermute | solution.py:349
  55.0 13.5 %collective-permute-start.10 = (bf16[272,1024]{1,0:T(8,128)(2,1)S(1)}, bf16[272,1024]{1,0:T(8,128)(2,1)S(1)}, u32[]{:S(2)}, u32[]{:S(2)}) collective-permute-start(bf16[272,1024]{1,0:T(8,128)(2,1)S(1)} %collective-permute-done.8.refs_1_), channel_id=1, source_target_pairs={{0,1},{1,0},{2,6},{3,7},{4,5},{5,4},{6,2},{7,3},{8,9},{9,8},{10,14... | collective-permute-start | bytes 1671176 | tf_op jit(solution)/shard_map/ppermute | solution.py:349
  70.4 5.1 %collective-permute-start.15 = (bf16[2,144,2048]{2,1,0:T(8,128)(2,1)S(1)}, bf16[2,144,2048]{2,1,0:T(8,128)(2,1)S(1)}, u32[]{:S(2)}, u32[]{:S(2)}) collective-permute-start(bf16[2,144,2048]{2,1,0:T(8,128)(2,1)S(1)} %get-tuple-element.182), channel_id=1, source_target_pairs={{0,2},{1,3},{2,0},{3,1},{4,6},{5,7},{6,4},{7,5},{8,10},{9,11},{10,... | collective-permute-start | bytes 3538952 | tf_op jit(solution)/shard_map/ppermute | solution.py:349
  70.4 3.8 %collective-permute-start.16 = (bf16[144,2048]{1,0:T(8,128)(2,1)S(1)}, bf16[144,2048]{1,0:T(8,128)(2,1)S(1)}, u32[]{:S(2)}, u32[]{:S(2)}) collective-permute-start(bf16[144,2048]{1,0:T(8,128)(2,1)S(1)} %get-tuple-element.195), channel_id=1, source_target_pairs={{0,2},{1,3},{2,0},{3,1},{4,6},{5,7},{6,4},{7,5},{8,10},{9,11},{10,... | collective-permute-start | bytes 1769480 | tf_op jit(solution)/shard_map/ppermute | solution.py:349
  70.9 9.5 %collective-permute-start.13 = (bf16[272,1024]{1,0:T(8,128)(2,1)S(1)}, bf16[272,1024]{1,0:T(8,128)(2,1)S(1)}, u32[]{:S(2)}, u32[]{:S(2)}) collective-permute-start(bf16[272,1024]{1,0:T(8,128)(2,1)S(1)} %collective-permute-done.11.refs_0_), channel_id=1, source_target_pairs={{0,1},{1,0},{2,6},{3,7},{4,5},{5,4},{6,2},{7,3},{8,9},{9,8},{10,14... | collective-permute-start | bytes 1671176 | tf_op jit(solution)/shard_map/ppermute | solution.py:349
  71.9 14.4 %collective-permute-start.14 = (bf16[272,1024]{1,0:T(8,128)(2,1)S(1)}, bf16[272,1024]{1,0:T(8,128)(2,1)S(1)}, u32[]{:S(2)}, u32[]{:S(2)}) collective-permute-start(bf16[272,1024]{1,0:T(8,128)(2,1)S(1)} %collective-permute-done.8.refs_1_), channel_id=1, source_target_pairs={{0,8},{1,9},{2,10},{3,11},{4,12},{5,13},{6,14},{7,15},{8,24},{9,25... | collective-permute-start | bytes 1671176 | tf_op jit(solution)/shard_map/ppermute | solution.py:349
  86.3 5.0 %collective-permute-start.20 = (bf16[2,144,2048]{2,1,0:T(8,128)(2,1)S(1)}, bf16[2,144,2048]{2,1,0:T(8,128)(2,1)S(1)}, u32[]{:S(2)}, u32[]{:S(2)}) collective-permute-start(bf16[2,144,2048]{2,1,0:T(8,128)(2,1)S(1)} %get-tuple-element.210), channel_id=1, source_target_pairs={{0,2},{1,3},{2,0},{3,1},{4,6},{5,7},{6,4},{7,5},{8,10},{9,11},{10,... | collective-permute-start | bytes 3538952 | tf_op jit(solution)/shard_map/ppermute | solution.py:349
  86.3 3.7 %collective-permute-start.17 = (bf16[144,2048]{1,0:T(8,128)(2,1)S(1)}, bf16[144,2048]{1,0:T(8,128)(2,1)S(1)}, u32[]{:S(2)}, u32[]{:S(2)}) collective-permute-start(bf16[144,2048]{1,0:T(8,128)(2,1)S(1)} %get-tuple-element.202), channel_id=1, source_target_pairs={{0,2},{1,3},{2,0},{3,1},{4,6},{5,7},{6,4},{7,5},{8,10},{9,11},{10,... | collective-permute-start | bytes 1769480 | tf_op jit(solution)/shard_map/ppermute | solution.py:349
  86.8 9.5 %collective-permute-start.19 = (bf16[272,1024]{1,0:T(8,128)(2,1)S(1)}, bf16[272,1024]{1,0:T(8,128)(2,1)S(1)}, u32[]{:S(2)}, u32[]{:S(2)}) collective-permute-start(bf16[272,1024]{1,0:T(8,128)(2,1)S(1)} %collective-permute-done.14.refs_1_), channel_id=1, source_target_pairs={{0,1},{1,0},{2,6},{3,7},{4,5},{5,4},{6,2},{7,3},{8,9},{9,8},{10,14... | collective-permute-start | bytes 1671176 | tf_op jit(solution)/shard_map/ppermute | solution.py:349
  97.9 6.3 %collective-permute-start.21 = (bf16[2,144,2048]{2,1,0:T(8,128)(2,1)S(1)}, bf16[2,144,2048]{2,1,0:T(8,128)(2,1)S(1)}, u32[]{:S(2)}, u32[]{:S(2)}) collective-permute-start(bf16[2,144,2048]{2,1,0:T(8,128)(2,1)S(1)} %get-tuple-element.227), channel_id=1, source_target_pairs={{0,2},{1,3},{2,0},{3,1},{4,6},{5,7},{6,4},{7,5},{8,10},{9,11},{10,... | collective-permute-start | bytes 3538952 | tf_op jit(solution)/shard_map/ppermute | solution.py:349
  98.0 3.7 %collective-permute-start.26 = (bf16[144,2048]{1,0:T(8,128)(2,1)S(1)}, bf16[144,2048]{1,0:T(8,128)(2,1)S(1)}, u32[]{:S(2)}, u32[]{:S(2)}) collective-permute-start(bf16[144,2048]{1,0:T(8,128)(2,1)S(1)} %get-tuple-element.247), channel_id=1, source_target_pairs={{0,2},{1,3},{2,0},{3,1},{4,6},{5,7},{6,4},{7,5},{8,10},{9,11},{10,... | collective-permute-start | bytes 1769480 | tf_op jit(solution)/shard_map/ppermute | solution.py:349
  98.5 10.9 %collective-permute-start.18 = (bf16[2,128,1024]{2,1,0:T(8,128)(2,1)S(1)}, bf16[2,128,1024]{2,1,0:T(8,128)(2,1)S(1)}, u32[]{:S(2)}, u32[]{:S(2)}) collective-permute-start(bf16[2,128,1024]{2,1,0:T(8,128)(2,1)S(1)} %get-tuple-element.204), channel_id=1, source_target_pairs={{0,1},{1,0},{2,6},{3,7},{4,5},{5,4},{6,2},{7,3},{8,9},{9,8},{10,14... | collective-permute-start | bytes 1572872 | tf_op jit(solution)/shard_map/ppermute | solution.py:349
  99.7 13.6 %collective-permute-start.23 = (bf16[2,128,1024]{2,1,0:T(8,128)(2,1)S(1)}, bf16[2,128,1024]{2,1,0:T(8,128)(2,1)S(1)}, u32[]{:S(2)}, u32[]{:S(2)}) collective-permute-start(bf16[2,128,1024]{2,1,0:T(8,128)(2,1)S(1)} %get-tuple-element.240), channel_id=1, source_target_pairs={{0,1},{1,0},{2,6},{3,7},{4,5},{5,4},{6,2},{7,3},{8,9},{9,8},{10,14... | collective-permute-start | bytes 1572872 | tf_op jit(solution)/shard_map/ppermute | solution.py:349
  102.9 22.2 %collective-permute-start.27 = (bf16[2,128,1024]{2,1,0:T(8,128)(2,1)S(1)}, bf16[2,128,1024]{2,1,0:T(8,128)(2,1)S(1)}, u32[]{:S(2)}, u32[]{:S(2)}) collective-permute-start(bf16[2,128,1024]{2,1,0:T(8,128)(2,1)S(1)} %get-tuple-element.249), channel_id=1, source_target_pairs={{0,1},{1,0},{2,6},{3,7},{4,5},{5,4},{6,2},{7,3},{8,9},{9,8},{10,14... | collective-permute-start | bytes 1572872 | tf_op jit(solution)/shard_map/ppermute | solution.py:349
  109.3 13.2 %collective-permute-start.28 = (bf16[144,2048]{1,0:T(8,128)(2,1)S(1)}, bf16[144,2048]{1,0:T(8,128)(2,1)S(1)}, u32[]{:S(2)}, u32[]{:S(2)}) collective-permute-start(bf16[144,2048]{1,0:T(8,128)(2,1)S(1)} %get-tuple-element.251), channel_id=1, source_target_pairs={{0,2},{1,3},{2,0},{3,1},{4,6},{5,7},{6,4},{7,5},{8,10},{9,11},{10,... | collective-permute-start | bytes 1769480 | tf_op jit(solution)/shard_map/ppermute | solution.py:349
  113.4 22.4 %collective-permute-start.24 = (bf16[128,1024]{1,0:T(8,128)(2,1)S(1)}, bf16[128,1024]{1,0:T(8,128)(2,1)S(1)}, u32[]{:S(2)}, u32[]{:S(2)}) collective-permute-start(bf16[128,1024]{1,0:T(8,128)(2,1)S(1)} %fusion.15), channel_id=1, source_target_pairs={{0,4},{1,5},{2,3},{3,2},{4,0},{5,1},{6,7},{7,6},{8,12},{9,13},{10,... | collective-permute-start | bytes 786440 | tf_op jit(solution)/shard_map/ppermute | solution.py:349
  115.5 30.8 %collective-permute-start.22 = (bf16[128,1024]{1,0:T(8,128)(2,1)S(1)}, bf16[128,1024]{1,0:T(8,128)(2,1)S(1)}, u32[]{:S(2)}, u32[]{:S(2)}) collective-permute-start(bf16[128,1024]{1,0:T(8,128)(2,1)S(1)} %fusion.14), channel_id=1, source_target_pairs={{0,4},{1,5},{2,3},{3,2},{4,0},{5,1},{6,7},{7,6},{8,12},{9,13},{10,... | collective-permute-start | bytes 786440 | tf_op jit(solution)/shard_map/ppermute | solution.py:349
  123.9 11.5 %collective-permute-start.31 = (bf16[2,128,1024]{2,1,0:T(8,128)(2,1)S(1)}, bf16[2,128,1024]{2,1,0:T(8,128)(2,1)S(1)}, u32[]{:S(2)}, u32[]{:S(2)}) collective-permute-start(bf16[2,128,1024]{2,1,0:T(8,128)(2,1)S(1)} %get-tuple-element.252), channel_id=1, source_target_pairs={{0,1},{1,0},{2,6},{3,7},{4,5},{5,4},{6,2},{7,3},{8,9},{9,8},{10,14... | collective-permute-start | bytes 1572872 | tf_op jit(solution)/shard_map/ppermute | solution.py:349
  125.4 12.2 %collective-permute-start.29 = (bf16[128,1024]{1,0:T(8,128)(2,1)S(1)}, bf16[128,1024]{1,0:T(8,128)(2,1)S(1)}, u32[]{:S(2)}, u32[]{:S(2)}) collective-permute-start(bf16[128,1024]{1,0:T(8,128)(2,1)S(1)} %fusion.16), channel_id=1, source_target_pairs={{0,4},{1,5},{2,3},{3,2},{4,0},{5,1},{6,7},{7,6},{8,12},{9,13},{10,... | collective-permute-start | bytes 786440 | tf_op jit(solution)/shard_map/ppermute | solution.py:349
  135.5 6.4 %collective-permute-start.32 = (bf16[128,1024]{1,0:T(8,128)(2,1)S(1)}, bf16[128,1024]{1,0:T(8,128)(2,1)S(1)}, u32[]{:S(2)}, u32[]{:S(2)}) collective-permute-start(bf16[128,1024]{1,0:T(8,128)(2,1)S(1)} %fusion.17), channel_id=1, source_target_pairs={{0,4},{1,5},{2,3},{3,2},{4,0},{5,1},{6,7},{7,6},{8,12},{9,13},{10,... | collective-permute-start | bytes 786440 | tf_op jit(solution)/shard_map/ppermute | solution.py:349
  135.9 10.3 %collective-permute-start.25 = (bf16[128,1024]{1,0:T(8,128)(2,1)S(1)}, bf16[128,1024]{1,0:T(8,128)(2,1)S(1)}, u32[]{:S(2)}, u32[]{:S(2)}) collective-permute-start(bf16[128,1024]{1,0:T(8,128)(2,1)S(1)} %fusion.8), channel_id=1, source_target_pairs={{0,16},{1,17},{2,18},{3,19},{4,20},{5,21},{6,22},{7,23},{8,0},{9,1... | collective-permute-start | bytes 786440 | tf_op jit(solution)/shard_map/ppermute | solution.py:349
  137.6 14.8 %collective-permute-start.30 = (bf16[128,1024]{1,0:T(8,128)(2,1)S(1)}, bf16[128,1024]{1,0:T(8,128)(2,1)S(1)}, u32[]{:S(2)}, u32[]{:S(2)}) collective-permute-start(bf16[128,1024]{1,0:T(8,128)(2,1)S(1)} %fusion.6), channel_id=1, source_target_pairs={{0,24},{1,25},{2,26},{3,27},{4,28},{5,29},{6,30},{7,31},{8,16},{9,... | collective-permute-start | bytes 786440 | tf_op jit(solution)/shard_map/ppermute | solution.py:349
  142.0 19.3 %collective-permute-start.33 = (bf16[128,1024]{1,0:T(8,128)(2,1)S(1)}, bf16[128,1024]{1,0:T(8,128)(2,1)S(1)}, u32[]{:S(2)}, u32[]{:S(2)}) collective-permute-start(bf16[128,1024]{1,0:T(8,128)(2,1)S(1)} %fusion.4), channel_id=1, source_target_pairs={{0,8},{1,9},{2,10},{3,11},{4,12},{5,13},{6,14},{7,15},{8,24},{9,25... | collective-permute-start | bytes 786440 | tf_op jit(solution)/shard_map/ppermute | solution.py:349

commit v8 on v7

--- a/solution.py
+++ b/solution.py
@@ -351,10 +351,6 @@
     def to_ring(value):
         return permute(value, lambda e, h: (after[e // 4] * 4 + e % 4, h))
 
-    def to_owner(value, back):
-        owner = {order[i]: order[(i - back) % chunks] for i in range(chunks)}
-        return permute(value, lambda e, h: (owner[e // 4] * 4 + e % 4, h))
-
     def to_core(value):
         return permute(value, lambda e, h: (e ^ 1, h))
 
@@ -421,13 +417,23 @@
     near, far, *kept = run_experts(done, chunks, mine, to_core(theirs), weights, kept)
     keep, send = placed(picks, near, far)
     late.append((keep, to_second(send)))
-    marks = ([near] * chunks + [send])[-(len(late) - 1):] + [None]
-    grad_tokens = 0.0
-    for c, ((keep, came), mark) in enumerate(zip(late, marks)):
-        pair = added(keep, came if mark is None else tied(came, mark))
-        total = added(pair[0], to_first(pair[1].astype(jnp.bfloat16)))
-        grad_tokens += total if c == 0 else to_owner(total.astype(jnp.bfloat16), c).astype(jnp.float32)
-    grad_tokens = grad_tokens.astype(jnp.bfloat16)
+    running = None
+    for c in range(1, chunks):
+        keep, came = late[c]
+        if c + 1 < chunks:
+            came = tied(came, near if c + 2 < chunks else send)
+        pair = added(keep, came)
+        came = to_first(pair[1].astype(jnp.bfloat16))
+        total = added(pair[0], came if c + 1 == chunks else tied(came, send))
+        running = (total if running is None else added(total, running)).astype(jnp.bfloat16)
+        if c + 1 < chunks:
+            running = to_ring(running)
+    keep, came = late[0]
+    pair = added(keep, came if running is None else tied(came, near))
+    came = pair[1].astype(jnp.bfloat16)
+    own = added(pair[0], to_first(came if running is None else tied(came, running)))
+    grad_tokens = (own if running is None else added(own, to_ring(running))).astype(jnp.bfloat16)
+    kept = tied(kept, send)
     rows_x, rows_g, acts, gate_term, up_term = kept
     grad_down = lax.dot_general(acts, rows_g, CONTRACT_FIRST, preferred_element_type=jnp.float32)
     grad_gate = lax.dot_general(gate_term, rows_x, CONTRACT_FIRST, preferred_element_type=jnp.float32)

time: 162 us -> 149 us (0.920)
  waiting for transfers between devices: 75.3 us -> 58.3 us
  starting transfers between devices: 32.1 us -> 35.6 us
    ppermute x34, waiting for transfers between devices: 75.3 us -> 58.3 us  [permute(): return lax.ppermute(value, ('expert', 'etp'), pairs)]
    ppermute x34, starting transfers between devices: 32.1 us -> 35.6 us  [permute(): return lax.ppermute(value, ('expert', 'etp'), pairs)]
  transfers between devices with their start and end apart: 34 -> 34, of which waited for: 17 -> 20; matrix products, arithmetic and copies ran while one was open for 7% -> 8% of each run, Pallas kernels for 21% -> 23%
where the time goes in v8:
time: 149 us
  waiting for transfers between devices  58.3 us (39%)
  Pallas kernels  38.1 us (26%)
  starting transfers between devices  35.6 us (24%)
  matrix products  10.1 us (7%)
  local copies, waits for them, and re-layouts  3.87 us (3%)
  other arithmetic  1.81 us (1%)
    ppermute x34, waiting for transfers between devices, permute(): return lax.ppermute(value, ('expert', 'etp'), pairs)  58.3 us
    ppermute x34, starting transfers between devices, permute(): return lax.ppermute(value, ('expert', 'etp'), pairs)  35.6 us
    pallas_call x4, Pallas kernels, run_experts(): pl.pallas_call(functools.partial(expert_kernel, index, kept is not None),...  19.7 us
    pallas_call x4, Pallas kernels, pick_rows(): pl.pallas_call(functools.partial(pick_kernel, top, rows), in_specs=[pl.Bl...  6.74 us
    pallas_call x4, Pallas kernels, place_rows(): pl.pallas_call(place_kernel, in_specs=[pl.BlockSpec(memory_space=pltpu.SM...  5.09 us
    pallas_call x1, Pallas kernels, load_weights(): pl.pallas_call(load_kernel, in_specs=[pl.BlockSpec(memory_space=pltpu.HBM...  4.62 us
    unnamed x16, local copies, waits for them, and re-layouts  3.74 us
    dot_general x1, matrix products, gather_body(): lax.dot_general(gate_term, rows_x, CONTRACT_FIRST, preferred_element_type...  3.38 us
  transfers between devices with their start and end apart: 34, of which 20 were waited for; matrix products, arithmetic and copies ran while one was open for 8% of the time, Pallas kernels for 23%

profile of v8, /device:TPU:0, one launch (start us, length us, event | category | flops | bytes accessed | tf_op | source)
XLA Modules:
  0.0 148.7 jit_solution(14305083247667153545)
XLA Ops:
  0.6 1.9 %pack.1.refs_0_ = bf16[272,1024]{1,0:T(8,128)(2,1)} custom-call(bf16[128,1024]{1,0:T(8,128)(2,1)} %tokens_ref.1, bf16[128,1024]{1,0:T(8,128)(2,1)} %grads_ref.1, s32[8,128]{1,0:T(8,128)} %bitcast.61, f32[8,128]{1,0:T(8,128)} %bitcast.62), custom_call_target="tpu_custom_call" | custom-call | bytes 1048576 | tf_op jit(solution)/shard_map/pack/pallas_call | solution.py:128
  2.5 2.9 %collective-permute-start = (bf16[272,1024]{1,0:T(8,128)(2,1)}, bf16[272,1024]{1,0:T(8,128)(2,1)S(1)}, u32[]{:S(2)}, u32[]{:S(2)}) collective-permute-start(bf16[272,1024]{1,0:T(8,128)(2,1)} %pack.1.refs_0_), channel_id=1, source_target_pairs={{0,1},{1,0},{2,6},{3,7},{4,5},{5,4},{6,2},{7,3},{8,9},{9,8},{10,14... | collective-permute-start | bytes 1671176 | tf_op jit(solution)/shard_map/ppermute | solution.py:349
  5.5 1.5 %collective-permute-start.1 = (bf16[272,1024]{1,0:T(8,128)(2,1)}, bf16[272,1024]{1,0:T(8,128)(2,1)S(1)}, u32[]{:S(2)}, u32[]{:S(2)}) collective-permute-start(bf16[272,1024]{1,0:T(8,128)(2,1)} %pack.1.refs_0_), channel_id=1, source_target_pairs={{0,4},{1,5},{2,3},{3,2},{4,0},{5,1},{6,7},{7,6},{8,12},{9,13},{10,... | collective-permute-start | bytes 1671176 | tf_op jit(solution)/shard_map/ppermute | solution.py:349
  7.0 1.6 %collective-permute-start.2 = (bf16[272,1024]{1,0:T(8,128)(2,1)}, bf16[272,1024]{1,0:T(8,128)(2,1)S(1)}, u32[]{:S(2)}, u32[]{:S(2)}) collective-permute-start(bf16[272,1024]{1,0:T(8,128)(2,1)} %pack.1.refs_0_), channel_id=1, source_target_pairs={{0,8},{1,9},{2,10},{3,11},{4,12},{5,13},{6,14},{7,15},{8,24},{9,25... | collective-permute-start | bytes 1671176 | tf_op jit(solution)/shard_map/ppermute | solution.py:349
  8.6 4.6 %load.1 = (bf16[384,2048]{1,0:T(8,128)(2,1)}, bf16[384,2048]{1,0:T(8,128)(2,1)}, bf16[384,2048]{1,0:T(8,128)(2,1)}) custom-call(bf16[384,2048]{1,0:T(8,128)(2,1)} %bitcast.58, bf16[384,2048]{1,0:T(8,128)(2,1)} %bitcast.59, bf16[384,2048]{1,0:T(8,128)(2,1)} %bitcast.60), custom_call_target="tpu_custom_call" | custom-call | tf_op jit(solution)/shard_map/load/pallas_call | solution.py:148
  13.2 5.5 %collective-permute-done.refs_2_ = bf16[272,1024]{1,0:T(8,128)(2,1)S(1)} collective-permute-done((bf16[272,1024]{1,0:T(8,128)(2,1)}, bf16[272,1024]{1,0:T(8,128)(2,1)S(1)}, u32[]{:S(2)}, u32[]{:S(2)}) %collective-permute-start) | collective-permute-done | bytes 557088 | tf_op jit(solution)/shard_map/ppermute | solution.py:349
  18.7 3.2 %collective-permute-done.2.refs_0_ = bf16[272,1024]{1,0:T(8,128)(2,1)S(1)} collective-permute-done((bf16[272,1024]{1,0:T(8,128)(2,1)}, bf16[272,1024]{1,0:T(8,128)(2,1)S(1)}, u32[]{:S(2)}, u32[]{:S(2)}) %collective-permute-start.2) | collective-permute-done | bytes 557088 | tf_op jit(solution)/shard_map/ppermute | solution.py:349
  24.7 11.2 %collective-permute-done.3.refs_3_ = bf16[272,1024]{1,0:T(8,128)(2,1)S(1)} collective-permute-done((bf16[272,1024]{1,0:T(8,128)(2,1)S(1)}, bf16[272,1024]{1,0:T(8,128)(2,1)S(1)}, u32[]{:S(2)}, u32[]{:S(2)}) %collective-permute-start.3) | collective-permute-done | bytes 557088 | tf_op jit(solution)/shard_map/ppermute | solution.py:349
  37.3 1.2 collective-permute-start.6
  40.2 1.1 copy-done.5
  41.2 1.1 copy-done.7
  42.3 1.5 %pick.4 = (bf16[2,144,2048]{2,1,0:T(8,128)(2,1)S(1)}, bf16[2,144,2048]{2,1,0:T(8,128)(2,1)S(1)}, bf16[288,256]{1,0:T(8,128)(2,1)S(1)}) custom-call(s32[3]{0:T(128)S(1)} %pad_add_fusion.place_ref, bf16[272,1024]{1,0:T(8,128)(2,1)S(1)} %copy-done.3, bf16[272,1024]{1,0:T(8,128)(2,1)S(1)} %copy-done.5, bf16[272,1024]{1,0:T(8,128)(2,1)S(1)} %collective-permute-done.refs_2_, ...), custom_call_target="tpu_custom_call" | custom-call | flops 2415919104 | bytes 4587520 | tf_op jit(solution)/shard_map/pick/pallas_call | solution.py:272
  43.8 3.1 %collective-permute-done.6.refs_2_ = bf16[272,1024]{1,0:T(8,128)(2,1)} collective-permute-done((bf16[272,1024]{1,0:T(8,128)(2,1)S(1)}, bf16[272,1024]{1,0:T(8,128)(2,1)}, u32[]{:S(2)}, u32[]{:S(2)}) %collective-permute-start.6) | collective-permute-done | bytes 557088 | tf_op jit(solution)/shard_map/ppermute | solution.py:349
  46.9 6.0 %collective-permute-done.7.refs_3_ = bf16[272,1024]{1,0:T(8,128)(2,1)} collective-permute-done((bf16[272,1024]{1,0:T(8,128)(2,1)S(1)}, bf16[272,1024]{1,0:T(8,128)(2,1)}, u32[]{:S(2)}, u32[]{:S(2)}) %collective-permute-start.7) | collective-permute-done | bytes 557088 | tf_op jit(solution)/shard_map/ppermute | solution.py:349
  53.0 1.3 collective-permute-start.9
  55.9 2.2 %pick.5 = (bf16[2,144,2048]{2,1,0:T(8,128)(2,1)S(1)}, bf16[2,144,2048]{2,1,0:T(8,128)(2,1)S(1)}, bf16[288,256]{1,0:T(8,128)(2,1)S(1)}) custom-call(s32[3]{0:T(128)S(1)} %pad_add_fusion.place_ref, bf16[272,1024]{1,0:T(8,128)(2,1)S(1)} %collective-permute-done.2.refs_0_, bf16[272,1024]{1,0:T(8,128)(2,1)S(1)} %collective-permute-done.4.refs_1_, ...), custom_call_target="tpu_custom_call" | custom-call | flops 2415919104 | bytes 4587520 | tf_op jit(solution)/shard_map/pick/pallas_call | solution.py:272
  58.1 4.9 %experts.4 = (bf16[144,2048]{1,0:T(8,128)(2,1)S(1)}, bf16[144,2048]{1,0:T(8,128)(2,1)S(1)}, bf16[1152,2048]{1,0:T(8,128)(2,1)S(1)}, bf16[1152,2048]{1,0:T(8,128)...) custom-call(bf16[2,144,2048]{2,1,0:T(8,128)(2,1)S(1)} %get-tuple-element.173., ...), custom_call_target="tpu_custom_call" | custom-call | flops 4529848320 | bytes 10100736 | tf_op jit(solution)/shard_map/experts/pallas_call | solution.py:296
  63.0 5.6 %collective-permute-done.10.refs_3_ = bf16[272,1024]{1,0:T(8,128)(2,1)S(1)} collective-permute-done((bf16[272,1024]{1,0:T(8,128)(2,1)S(1)}, bf16[272,1024]{1,0:T(8,128)(2,1)S(1)}, u32[]{:S(2)}, u32[]{:S(2)}) %collective-permute-start.10) | collective-permute-done | bytes 557088 | tf_op jit(solution)/shard_map/ppermute | solution.py:349
  68.5 1.8 %collective-permute-done.11.refs_0_ = bf16[272,1024]{1,0:T(8,128)(2,1)S(1)} collective-permute-done((bf16[272,1024]{1,0:T(8,128)(2,1)S(1)}, bf16[272,1024]{1,0:T(8,128)(2,1)S(1)}, u32[]{:S(2)}, u32[]{:S(2)}) %collective-permute-start.11) | collective-permute-done | bytes 557088 | tf_op jit(solution)/shard_map/ppermute | solution.py:349
  72.7 1.5 %pick.6 = (bf16[2,144,2048]{2,1,0:T(8,128)(2,1)S(1)}, bf16[2,144,2048]{2,1,0:T(8,128)(2,1)S(1)}, bf16[288,256]{1,0:T(8,128)(2,1)S(1)}) custom-call(s32[3]{0:T(128)S(1)} %pad_add_fusion.place_ref, bf16[272,1024]{1,0:T(8,128)(2,1)S(1)} %collective-permute-done.5.refs_0_, bf16[272,1024]{1,0:T(8,128)(2,1)S(1)} %collective-permute-done.8.refs_1_, ...), custom_call_target="tpu_custom_call" | custom-call | flops 2415919104 | bytes 4587520 | tf_op jit(solution)/shard_map/pick/pallas_call | solution.py:272
  74.2 1.3 place.4
  75.5 5.1 %experts.5 = (bf16[144,2048]{1,0:T(8,128)(2,1)S(1)}, bf16[144,2048]{1,0:T(8,128)(2,1)S(1)}, bf16[1152,2048]{1,0:T(8,128)(2,1)S(1)}, bf16[1152,2048]{1,0:T(8,128)...) custom-call(bf16[2,144,2048]{2,1,0:T(8,128)(2,1)S(1)} %get-tuple-ele, ...), custom_call_target="tpu_custom_call", output_to_operand_aliasing={{2}: (5, {}), {3}: (6, {}), {4}: (7, {}), {5}: (8, {}), {6}... | custom-call | flops 4529848320 | bytes 10100736 | tf_op jit(solution)/shard_map/experts/pallas_call | solution.py:296
  80.6 5.7 %collective-permute-done.14.refs_1_ = bf16[272,1024]{1,0:T(8,128)(2,1)S(1)} collective-permute-done((bf16[272,1024]{1,0:T(8,128)(2,1)S(1)}, bf16[272,1024]{1,0:T(8,128)(2,1)S(1)}, u32[]{:S(2)}, u32[]{:S(2)}) %collective-permute-start.14) | collective-permute-done | bytes 557088 | tf_op jit(solution)/shard_map/ppermute | solution.py:349
  86.8 1.2 collective-permute-start.19
  88.1 1.9 %collective-permute-done.17.far_ref = bf16[144,2048]{1,0:T(8,128)(2,1)S(1)} collective-permute-done((bf16[144,2048]{1,0:T(8,128)(2,1)S(1)}, bf16[144,2048]{1,0:T(8,128)(2,1)S(1)}, u32[]{:S(2)}, u32[]{:S(2)}) %collective-permute-start.17) | collective-permute-done | bytes 589856 | tf_op jit(solution)/shard_map/ppermute | solution.py:349
  90.0 1.3 place.5
  91.3 4.9 %experts.6 = (bf16[144,2048]{1,0:T(8,128)(2,1)S(1)}, bf16[144,2048]{1,0:T(8,128)(2,1)S(1)}, bf16[1152,2048]{1,0:T(8,128)(2,1)S(1)}, bf16[1152,2048]{1,0:T(8,128)...) custom-call(bf16[2,144,2048]{2,1,0:T(8,128)(2,1)S(1)} %get-tuple-ele, ...), custom_call_target="tpu_custom_call", output_to_operand_aliasing={{2}: (5, {}), {3}: (6, {}), {4}: (7, {}), {5}: (8, {}), {6}... | custom-call | flops 4529848320 | bytes 10100736 | tf_op jit(solution)/shard_map/experts/pallas_call | solution.py:296
  96.4 1.5 %pick.7 = (bf16[2,144,2048]{2,1,0:T(8,128)(2,1)S(1)}, bf16[2,144,2048]{2,1,0:T(8,128)(2,1)S(1)}, bf16[288,256]{1,0:T(8,128)(2,1)S(1)}) custom-call(s32[3]{0:T(128)S(1)} %pad_add_fusion.place_ref, bf16[272,1024]{1,0:T(8,128)(2,1)S(1)} %collective-permute-done.11.refs_0_, bf16[272,1024]{1,0:T(8,128)(2,1)S(1)} %collective-permute-done.14.refs_1_, ...), custom_call_target="tpu_custom_call" | custom-call | flops 2415919104 | bytes 4587520 | tf_op jit(solution)/shard_map/pick/pallas_call | solution.py:272
  98.5 1.2 collective-permute-start.28
  100.5 1.2 collective-permute-done.25.far_ref
  101.7 1.3 place.7
  102.9 1.3 collective-permute-start.26
  104.2 4.9 %experts.7 = (bf16[144,2048]{1,0:T(8,128)(2,1)S(1)}, bf16[144,2048]{1,0:T(8,128)(2,1)S(1)}, bf16[1152,2048]{1,0:T(8,128)(2,1)S(1)}, bf16[1152,2048]{1,0:T(8,128)...) custom-call(bf16[2,144,2048]{2,1,0:T(8,128)(2,1)S(1)} %get-tuple-ele, ...), custom_call_target="tpu_custom_call", output_to_operand_aliasing={{2}: (5, {}), {3}: (6, {}), {4}: (7, {}), {5}: (8, {}), {6}... | custom-call | flops 4529848320 | bytes 10100736 | tf_op jit(solution)/shard_map/experts/pallas_call | solution.py:296
  109.8 3.5 %collective-permute-done.18 = bf16[2,128,1024]{2,1,0:T(8,128)(2,1)S(1)} collective-permute-done((bf16[2,128,1024]{2,1,0:T(8,128)(2,1)S(1)}, bf16[2,128,1024]{2,1,0:T(8,128)(2,1)S(1)}, u32[]{:S(2)}, u32[]{:S(2)}) %collective-permute-start.18) | collective-permute-done | bytes 524320 | tf_op jit(solution)/shard_map/ppermute | solution.py:349
  113.3 1.7 %collective-permute-start.29 = (bf16[128,1024]{1,0:T(8,128)(2,1)S(1)}, bf16[128,1024]{1,0:T(8,128)(2,1)S(1)}, u32[]{:S(2)}, u32[]{:S(2)}) collective-permute-start(bf16[128,1024]{1,0:T(8,128)(2,1)S(1)} %fusion.17), channel_id=1, source_target_pairs={{0,4},{1,5},{2,3},{3,2},{4,0},{5,1},{6,7},{7,6},{8,12},{9,13},{10,... | collective-permute-start | bytes 786440 | tf_op jit(solution)/shard_map/ppermute | solution.py:349
  115.3 1.3 place.6
  116.5 1.1 collective-permute-start.23
  117.6 4.1 %collective-permute-done.26 = bf16[2,128,1024]{2,1,0:T(8,128)(2,1)S(1)} collective-permute-done((bf16[2,128,1024]{2,1,0:T(8,128)(2,1)S(1)}, bf16[2,128,1024]{2,1,0:T(8,128)(2,1)S(1)}, u32[]{:S(2)}, u32[]{:S(2)}) %collective-permute-start.26) | collective-permute-done | bytes 524320 | tf_op jit(solution)/shard_map/ppermute | solution.py:349
  122.6 1.1 collective-permute-start.30
  123.8 1.8 %collective-permute-start.27 = (bf16[128,1024]{1,0:T(8,128)(2,1)S(1)}, bf16[128,1024]{1,0:T(8,128)(2,1)S(1)}, u32[]{:S(2)}, u32[]{:S(2)}) collective-permute-start(bf16[128,1024]{1,0:T(8,128)(2,1)S(1)} %fusion.16), channel_id=1, source_target_pairs={{0,4},{1,5},{2,3},{3,2},{4,0},{5,1},{6,7},{7,6},{8,12},{9,13},{10,... | collective-permute-start | bytes 786440 | tf_op jit(solution)/shard_map/ppermute | solution.py:349
  125.6 3.4 %fusion = bf16[1,384,2048]{2,1,0:T(8,128)(2,1)} fusion(bf16[1152,384]{1,0:T(8,128)(2,1)S(1)} %get-tuple-element.271, bf16[1152,2048]{1,0:T(8,128)(2,1)S(1)} %get-tuple-element.272), kind=kOutput, calls=%fused_computation.3 | convolution fusion | flops 1812725760 | bytes 7176192 | tf_op jit(solution)/shard_map/dot_general | solution.py:439
  129.0 1.3 collective-permute-done.27
  130.4 3.4 %collective-permute-start.31 = (bf16[128,1024]{1,0:T(8,128)(2,1)S(1)}, bf16[128,1024]{1,0:T(8,128)(2,1)S(1)}, u32[]{:S(2)}, u32[]{:S(2)}) collective-permute-start(bf16[128,1024]{1,0:T(8,128)(2,1)S(1)} %fusion.7), channel_id=1, source_target_pairs={{0,8},{1,9},{2,10},{3,11},{4,12},{5,13},{6,14},{7,15},{8,24},{9,25... | collective-permute-start | bytes 786440 | tf_op jit(solution)/shard_map/ppermute | solution.py:349
  134.0 1.8 %collective-permute-start.24 = (bf16[128,1024]{1,0:T(8,128)(2,1)S(1)}, bf16[128,1024]{1,0:T(8,128)(2,1)S(1)}, u32[]{:S(2)}, u32[]{:S(2)}) collective-permute-start(bf16[128,1024]{1,0:T(8,128)(2,1)S(1)} %fusion.15), channel_id=1, source_target_pairs={{0,4},{1,5},{2,3},{3,2},{4,0},{5,1},{6,7},{7,6},{8,12},{9,13},{10,... | collective-permute-start | bytes 786440 | tf_op jit(solution)/shard_map/ppermute | solution.py:349
  135.9 3.4 %fusion.1 = bf16[1,384,2048]{2,1,0:T(8,128)(2,1)} fusion(bf16[1152,384]{1,0:T(8,128)(2,1)S(1)} %get-tuple-element.273, bf16[1152,2048]{1,0:T(8,128)(2,1)S(1)} %get-tuple-element.272), kind=kOutput, calls=%fused_computation.4 | convolution fusion | flops 1812725760 | bytes 7176192 | tf_op jit(solution)/shard_map/dot_general | solution.py:440
  141.5 1.7 %collective-permute-start.32 = (bf16[128,1024]{1,0:T(8,128)(2,1)S(1)}, bf16[128,1024]{1,0:T(8,128)(2,1)S(1)}, u32[]{:S(2)}, u32[]{:S(2)}) collective-permute-start(bf16[128,1024]{1,0:T(8,128)(2,1)S(1)} %fusion.14), channel_id=1, source_target_pairs={{0,4},{1,5},{2,3},{3,2},{4,0},{5,1},{6,7},{7,6},{8,12},{9,13},{10,... | collective-permute-start | bytes 786440 | tf_op jit(solution)/shard_map/ppermute | solution.py:349
  143.3 3.4 %fusion.2 = bf16[1,384,2048]{2,1,0:T(8,128)(2,1)} fusion(bf16[1152,384]{1,0:T(8,128)(2,1)S(1)} %get-tuple-element.274, bf16[1152,2048]{1,0:T(8,128)(2,1)S(1)} %get-tuple-element.275), kind=kOutput, calls=%fused_computation.5 | convolution fusion | flops 1812725760 | bytes 7176192 | tf_op jit(solution)/shard_map/dot_general | solution.py:438
  146.6 1.3 collective-permute-done.33
  (66 shorter events, 17.1 us)
Async XLA Ops:
  2.5 16.2 %collective-permute-start = (bf16[272,1024]{1,0:T(8,128)(2,1)}, bf16[272,1024]{1,0:T(8,128)(2,1)S(1)}, u32[]{:S(2)}, u32[]{:S(2)}) collective-permute-start(bf16[272,1024]{1,0:T(8,128)(2,1)} %pack.1.refs_0_), channel_id=1, source_target_pairs={{0,1},{1,0},{2,6},{3,7},{4,5},{5,4},{6,2},{7,3},{8,9},{9,8},{10,14... | collective-permute-start | bytes 1671176 | tf_op jit(solution)/shard_map/ppermute | solution.py:349
  5.5 13.2 %collective-permute-start.1 = (bf16[272,1024]{1,0:T(8,128)(2,1)}, bf16[272,1024]{1,0:T(8,128)(2,1)S(1)}, u32[]{:S(2)}, u32[]{:S(2)}) collective-permute-start(bf16[272,1024]{1,0:T(8,128)(2,1)} %pack.1.refs_0_), channel_id=1, source_target_pairs={{0,4},{1,5},{2,3},{3,2},{4,0},{5,1},{6,7},{7,6},{8,12},{9,13},{10,... | collective-permute-start | bytes 1671176 | tf_op jit(solution)/shard_map/ppermute | solution.py:349
  7.0 14.9 %collective-permute-start.2 = (bf16[272,1024]{1,0:T(8,128)(2,1)}, bf16[272,1024]{1,0:T(8,128)(2,1)S(1)}, u32[]{:S(2)}, u32[]{:S(2)}) collective-permute-start(bf16[272,1024]{1,0:T(8,128)(2,1)} %pack.1.refs_0_), channel_id=1, source_target_pairs={{0,8},{1,9},{2,10},{3,11},{4,12},{5,13},{6,14},{7,15},{8,24},{9,25... | collective-permute-start | bytes 1671176 | tf_op jit(solution)/shard_map/ppermute | solution.py:349
  8.6 31.6 %copy-start.3 = (bf16[272,1024]{1,0:T(8,128)(2,1)S(1)}, bf16[272,1024]{1,0:T(8,128)(2,1)}, u32[]{:S(2)}) copy-start(bf16[272,1024]{1,0:T(8,128)(2,1)} %pack.1.refs_0_) | copy-start | bytes 1671172
  21.9 14.0 %collective-permute-start.3 = (bf16[272,1024]{1,0:T(8,128)(2,1)S(1)}, bf16[272,1024]{1,0:T(8,128)(2,1)S(1)}, u32[]{:S(2)}, u32[]{:S(2)}) collective-permute-start(bf16[272,1024]{1,0:T(8,128)(2,1)S(1)} %collective-permute-done.1.refs_1_), channel_id=1, source_target_pairs={{0,1},{1,0},{2,6},{3,7},{4,5},{5,4},{6,2},{7,3},{8,9},{9,8},{10,14... | collective-permute-start | bytes 1671176 | tf_op jit(solution)/shard_map/ppermute | solution.py:349
  22.5 0.8 copy-start.4
  23.3 13.4 %collective-permute-start.4 = (bf16[272,1024]{1,0:T(8,128)(2,1)S(1)}, bf16[272,1024]{1,0:T(8,128)(2,1)S(1)}, u32[]{:S(2)}, u32[]{:S(2)}) collective-permute-start(bf16[272,1024]{1,0:T(8,128)(2,1)S(1)} %collective-permute-done.2.refs_0_), channel_id=1, source_target_pairs={{0,4},{1,5},{2,3},{3,2},{4,0},{5,1},{6,7},{7,6},{8,12},{9,13},{10,... | collective-permute-start | bytes 1671176 | tf_op jit(solution)/shard_map/ppermute | solution.py:349
  23.8 13.5 %collective-permute-start.5 = (bf16[272,1024]{1,0:T(8,128)(2,1)S(1)}, bf16[272,1024]{1,0:T(8,128)(2,1)S(1)}, u32[]{:S(2)}, u32[]{:S(2)}) collective-permute-start(bf16[272,1024]{1,0:T(8,128)(2,1)S(1)} %collective-permute-done.2.refs_0_), channel_id=1, source_target_pairs={{0,8},{1,9},{2,10},{3,11},{4,12},{5,13},{6,14},{7,15},{8,24},{9,25... | collective-permute-start | bytes 1671176 | tf_op jit(solution)/shard_map/ppermute | solution.py:349
  35.9 0.8 copy-start.6
  37.3 9.6 %collective-permute-start.6 = (bf16[272,1024]{1,0:T(8,128)(2,1)S(1)}, bf16[272,1024]{1,0:T(8,128)(2,1)}, u32[]{:S(2)}, u32[]{:S(2)}) collective-permute-start(bf16[272,1024]{1,0:T(8,128)(2,1)S(1)} %collective-permute-done.2.refs_0_), channel_id=1, source_target_pairs={{0,1},{1,0},{2,6},{3,7},{4,5},{5,4},{6,2},{7,3},{8,9},{9,8},{10,14... | collective-permute-start | bytes 1671176 | tf_op jit(solution)/shard_map/ppermute | solution.py:349
  38.5 14.4 %collective-permute-start.7 = (bf16[272,1024]{1,0:T(8,128)(2,1)S(1)}, bf16[272,1024]{1,0:T(8,128)(2,1)}, u32[]{:S(2)}, u32[]{:S(2)}) collective-permute-start(bf16[272,1024]{1,0:T(8,128)(2,1)S(1)} %collective-permute-done.4.refs_1_), channel_id=1, source_target_pairs={{0,1},{1,0},{2,6},{3,7},{4,5},{5,4},{6,2},{7,3},{8,9},{9,8},{10,14... | collective-permute-start | bytes 1671176 | tf_op jit(solution)/shard_map/ppermute | solution.py:349
  39.3 13.6 %collective-permute-start.8 = (bf16[272,1024]{1,0:T(8,128)(2,1)S(1)}, bf16[272,1024]{1,0:T(8,128)(2,1)S(1)}, u32[]{:S(2)}, u32[]{:S(2)}) collective-permute-start(bf16[272,1024]{1,0:T(8,128)(2,1)S(1)} %collective-permute-done.4.refs_1_), channel_id=1, source_target_pairs={{0,8},{1,9},{2,10},{3,11},{4,12},{5,13},{6,14},{7,15},{8,24},{9,25... | collective-permute-start | bytes 1671176 | tf_op jit(solution)/shard_map/ppermute | solution.py:349
  40.2 1.1 copy-start.5
  41.2 1.1 copy-start.7
  52.9 5.2 %copy-start = (bf16[384,2048]{1,0:T(8,128)(2,1)S(1)}, bf16[384,2048]{1,0:T(8,128)(2,1)}, u32[]{:S(2)}) copy-start(bf16[384,2048]{1,0:T(8,128)(2,1)} %get-tuple-element.236.wg_ref) | copy-start | bytes 4718596
  52.9 5.2 %copy-start.1 = (bf16[384,2048]{1,0:T(8,128)(2,1)S(1)}, bf16[384,2048]{1,0:T(8,128)(2,1)}, u32[]{:S(2)}) copy-start(bf16[384,2048]{1,0:T(8,128)(2,1)} %get-tuple-element.237.wu_ref) | copy-start | bytes 4718596
  52.9 5.2 %copy-start.2 = (bf16[384,2048]{1,0:T(8,128)(2,1)S(1)}, bf16[384,2048]{1,0:T(8,128)(2,1)}, u32[]{:S(2)}) copy-start(bf16[384,2048]{1,0:T(8,128)(2,1)} %get-tuple-element.238.wd_ref) | copy-start | bytes 4718596
  52.9 5.2 %collective-permute-start.12 = (bf16[2,144,2048]{2,1,0:T(8,128)(2,1)S(1)}, bf16[2,144,2048]{2,1,0:T(8,128)(2,1)S(1)}, u32[]{:S(2)}, u32[]{:S(2)}) collective-permute-start(bf16[2,144,2048]{2,1,0:T(8,128)(2,1)S(1)} %get-tuple-element.174), channel_id=1, source_target_pairs={{0,2},{1,3},{2,0},{3,1},{4,6},{5,7},{6,4},{7,5},{8,10},{9,11},{10,... | collective-permute-start | bytes 3538952 | tf_op jit(solution)/shard_map/ppermute | solution.py:349
  53.0 10.0 %collective-permute-start.9 = (bf16[272,1024]{1,0:T(8,128)(2,1)S(1)}, bf16[272,1024]{1,0:T(8,128)(2,1)S(1)}, u32[]{:S(2)}, u32[]{:S(2)}) collective-permute-start(bf16[272,1024]{1,0:T(8,128)(2,1)S(1)} %collective-permute-done.5.refs_0_), channel_id=1, source_target_pairs={{0,1},{1,0},{2,6},{3,7},{4,5},{5,4},{6,2},{7,3},{8,9},{9,8},{10,14... | collective-permute-start | bytes 1671176 | tf_op jit(solution)/shard_map/ppermute | solution.py:349
  54.3 16.1 %collective-permute-start.11 = (bf16[272,1024]{1,0:T(8,128)(2,1)S(1)}, bf16[272,1024]{1,0:T(8,128)(2,1)S(1)}, u32[]{:S(2)}, u32[]{:S(2)}) collective-permute-start(bf16[272,1024]{1,0:T(8,128)(2,1)S(1)} %collective-permute-done.5.refs_0_), channel_id=1, source_target_pairs={{0,8},{1,9},{2,10},{3,11},{4,12},{5,13},{6,14},{7,15},{8,24},{9,25... | collective-permute-start | bytes 1671176 | tf_op jit(solution)/shard_map/ppermute | solution.py:349
  55.0 13.5 %collective-permute-start.10 = (bf16[272,1024]{1,0:T(8,128)(2,1)S(1)}, bf16[272,1024]{1,0:T(8,128)(2,1)S(1)}, u32[]{:S(2)}, u32[]{:S(2)}) collective-permute-start(bf16[272,1024]{1,0:T(8,128)(2,1)S(1)} %collective-permute-done.8.refs_1_), channel_id=1, source_target_pairs={{0,1},{1,0},{2,6},{3,7},{4,5},{5,4},{6,2},{7,3},{8,9},{9,8},{10,14... | collective-permute-start | bytes 1671176 | tf_op jit(solution)/shard_map/ppermute | solution.py:349
  70.4 5.1 %collective-permute-start.15 = (bf16[2,144,2048]{2,1,0:T(8,128)(2,1)S(1)}, bf16[2,144,2048]{2,1,0:T(8,128)(2,1)S(1)}, u32[]{:S(2)}, u32[]{:S(2)}) collective-permute-start(bf16[2,144,2048]{2,1,0:T(8,128)(2,1)S(1)} %get-tuple-element.190), channel_id=1, source_target_pairs={{0,2},{1,3},{2,0},{3,1},{4,6},{5,7},{6,4},{7,5},{8,10},{9,11},{10,... | collective-permute-start | bytes 3538952 | tf_op jit(solution)/shard_map/ppermute | solution.py:349
  70.4 3.8 %collective-permute-start.16 = (bf16[144,2048]{1,0:T(8,128)(2,1)S(1)}, bf16[144,2048]{1,0:T(8,128)(2,1)S(1)}, u32[]{:S(2)}, u32[]{:S(2)}) collective-permute-start(bf16[144,2048]{1,0:T(8,128)(2,1)S(1)} %get-tuple-element.203), channel_id=1, source_target_pairs={{0,2},{1,3},{2,0},{3,1},{4,6},{5,7},{6,4},{7,5},{8,10},{9,11},{10,... | collective-permute-start | bytes 1769480 | tf_op jit(solution)/shard_map/ppermute | solution.py:349
  70.9 9.7 %collective-permute-start.13 = (bf16[272,1024]{1,0:T(8,128)(2,1)S(1)}, bf16[272,1024]{1,0:T(8,128)(2,1)S(1)}, u32[]{:S(2)}, u32[]{:S(2)}) collective-permute-start(bf16[272,1024]{1,0:T(8,128)(2,1)S(1)} %collective-permute-done.11.refs_0_), channel_id=1, source_target_pairs={{0,1},{1,0},{2,6},{3,7},{4,5},{5,4},{6,2},{7,3},{8,9},{9,8},{10,14... | collective-permute-start | bytes 1671176 | tf_op jit(solution)/shard_map/ppermute | solution.py:349
  71.9 14.4 %collective-permute-start.14 = (bf16[272,1024]{1,0:T(8,128)(2,1)S(1)}, bf16[272,1024]{1,0:T(8,128)(2,1)S(1)}, u32[]{:S(2)}, u32[]{:S(2)}) collective-permute-start(bf16[272,1024]{1,0:T(8,128)(2,1)S(1)} %collective-permute-done.8.refs_1_), channel_id=1, source_target_pairs={{0,8},{1,9},{2,10},{3,11},{4,12},{5,13},{6,14},{7,15},{8,24},{9,25... | collective-permute-start | bytes 1671176 | tf_op jit(solution)/shard_map/ppermute | solution.py:349
  86.3 5.0 %collective-permute-start.20 = (bf16[2,144,2048]{2,1,0:T(8,128)(2,1)S(1)}, bf16[2,144,2048]{2,1,0:T(8,128)(2,1)S(1)}, u32[]{:S(2)}, u32[]{:S(2)}) collective-permute-start(bf16[2,144,2048]{2,1,0:T(8,128)(2,1)S(1)} %get-tuple-element.218), channel_id=1, source_target_pairs={{0,2},{1,3},{2,0},{3,1},{4,6},{5,7},{6,4},{7,5},{8,10},{9,11},{10,... | collective-permute-start | bytes 3538952 | tf_op jit(solution)/shard_map/ppermute | solution.py:349
  86.3 3.7 %collective-permute-start.17 = (bf16[144,2048]{1,0:T(8,128)(2,1)S(1)}, bf16[144,2048]{1,0:T(8,128)(2,1)S(1)}, u32[]{:S(2)}, u32[]{:S(2)}) collective-permute-start(bf16[144,2048]{1,0:T(8,128)(2,1)S(1)} %get-tuple-element.210), channel_id=1, source_target_pairs={{0,2},{1,3},{2,0},{3,1},{4,6},{5,7},{6,4},{7,5},{8,10},{9,11},{10,... | collective-permute-start | bytes 1769480 | tf_op jit(solution)/shard_map/ppermute | solution.py:349
  86.8 9.5 %collective-permute-start.19 = (bf16[272,1024]{1,0:T(8,128)(2,1)S(1)}, bf16[272,1024]{1,0:T(8,128)(2,1)S(1)}, u32[]{:S(2)}, u32[]{:S(2)}) collective-permute-start(bf16[272,1024]{1,0:T(8,128)(2,1)S(1)} %collective-permute-done.14.refs_1_), channel_id=1, source_target_pairs={{0,1},{1,0},{2,6},{3,7},{4,5},{5,4},{6,2},{7,3},{8,9},{9,8},{10,14... | collective-permute-start | bytes 1671176 | tf_op jit(solution)/shard_map/ppermute | solution.py:349
  97.9 6.3 %collective-permute-start.21 = (bf16[2,144,2048]{2,1,0:T(8,128)(2,1)S(1)}, bf16[2,144,2048]{2,1,0:T(8,128)(2,1)S(1)}, u32[]{:S(2)}, u32[]{:S(2)}) collective-permute-start(bf16[2,144,2048]{2,1,0:T(8,128)(2,1)S(1)} %get-tuple-element.235), channel_id=1, source_target_pairs={{0,2},{1,3},{2,0},{3,1},{4,6},{5,7},{6,4},{7,5},{8,10},{9,11},{10,... | collective-permute-start | bytes 3538952 | tf_op jit(solution)/shard_map/ppermute | solution.py:349
  98.0 3.7 %collective-permute-start.25 = (bf16[144,2048]{1,0:T(8,128)(2,1)S(1)}, bf16[144,2048]{1,0:T(8,128)(2,1)S(1)}, u32[]{:S(2)}, u32[]{:S(2)}) collective-permute-start(bf16[144,2048]{1,0:T(8,128)(2,1)S(1)} %get-tuple-element.255), channel_id=1, source_target_pairs={{0,2},{1,3},{2,0},{3,1},{4,6},{5,7},{6,4},{7,5},{8,10},{9,11},{10,... | collective-permute-start | bytes 1769480 | tf_op jit(solution)/shard_map/ppermute | solution.py:349
  98.5 11.1 %collective-permute-start.28 = (bf16[2,128,1024]{2,1,0:T(8,128)(2,1)S(1)}, bf16[2,128,1024]{2,1,0:T(8,128)(2,1)S(1)}, u32[]{:S(2)}, u32[]{:S(2)}) collective-permute-start(bf16[2,128,1024]{2,1,0:T(8,128)(2,1)S(1)} %get-tuple-element.262), channel_id=1, source_target_pairs={{0,1},{1,0},{2,6},{3,7},{4,5},{5,4},{6,2},{7,3},{8,9},{9,8},{10,14... | collective-permute-start | bytes 1572872 | tf_op jit(solution)/shard_map/ppermute | solution.py:349
  99.7 13.6 %collective-permute-start.18 = (bf16[2,128,1024]{2,1,0:T(8,128)(2,1)S(1)}, bf16[2,128,1024]{2,1,0:T(8,128)(2,1)S(1)}, u32[]{:S(2)}, u32[]{:S(2)}) collective-permute-start(bf16[2,128,1024]{2,1,0:T(8,128)(2,1)S(1)} %get-tuple-element.212), channel_id=1, source_target_pairs={{0,1},{1,0},{2,6},{3,7},{4,5},{5,4},{6,2},{7,3},{8,9},{9,8},{10,14... | collective-permute-start | bytes 1572872 | tf_op jit(solution)/shard_map/ppermute | solution.py:349
  102.9 18.8 %collective-permute-start.26 = (bf16[2,128,1024]{2,1,0:T(8,128)(2,1)S(1)}, bf16[2,128,1024]{2,1,0:T(8,128)(2,1)S(1)}, u32[]{:S(2)}, u32[]{:S(2)}) collective-permute-start(bf16[2,128,1024]{2,1,0:T(8,128)(2,1)S(1)} %get-tuple-element.257), channel_id=1, source_target_pairs={{0,1},{1,0},{2,6},{3,7},{4,5},{5,4},{6,2},{7,3},{8,9},{9,8},{10,14... | collective-permute-start | bytes 1572872 | tf_op jit(solution)/shard_map/ppermute | solution.py:349
  109.1 6.1 %collective-permute-start.22 = (bf16[144,2048]{1,0:T(8,128)(2,1)S(1)}, bf16[144,2048]{1,0:T(8,128)(2,1)S(1)}, u32[]{:S(2)}, u32[]{:S(2)}) collective-permute-start(bf16[144,2048]{1,0:T(8,128)(2,1)S(1)} %get-tuple-element.247), channel_id=1, source_target_pairs={{0,2},{1,3},{2,0},{3,1},{4,6},{5,7},{6,4},{7,5},{8,10},{9,11},{10,... | collective-permute-start | bytes 1769480 | tf_op jit(solution)/shard_map/ppermute | solution.py:349
  113.3 9.2 %collective-permute-start.29 = (bf16[128,1024]{1,0:T(8,128)(2,1)S(1)}, bf16[128,1024]{1,0:T(8,128)(2,1)S(1)}, u32[]{:S(2)}, u32[]{:S(2)}) collective-permute-start(bf16[128,1024]{1,0:T(8,128)(2,1)S(1)} %fusion.17), channel_id=1, source_target_pairs={{0,4},{1,5},{2,3},{3,2},{4,0},{5,1},{6,7},{7,6},{8,12},{9,13},{10,... | collective-permute-start | bytes 786440 | tf_op jit(solution)/shard_map/ppermute | solution.py:349
  116.5 17.3 %collective-permute-start.23 = (bf16[2,128,1024]{2,1,0:T(8,128)(2,1)S(1)}, bf16[2,128,1024]{2,1,0:T(8,128)(2,1)S(1)}, u32[]{:S(2)}, u32[]{:S(2)}) collective-permute-start(bf16[2,128,1024]{2,1,0:T(8,128)(2,1)S(1)} %get-tuple-element.249), channel_id=1, source_target_pairs={{0,1},{1,0},{2,6},{3,7},{4,5},{5,4},{6,2},{7,3},{8,9},{9,8},{10,14... | collective-permute-start | bytes 1572872 | tf_op jit(solution)/shard_map/ppermute | solution.py:349
  122.6 7.8 %collective-permute-start.30 = (bf16[128,1024]{1,0:T(8,128)(2,1)S(1)}, bf16[128,1024]{1,0:T(8,128)(2,1)S(1)}, u32[]{:S(2)}, u32[]{:S(2)}) collective-permute-start(bf16[128,1024]{1,0:T(8,128)(2,1)S(1)} %fusion.4), channel_id=1, source_target_pairs={{0,8},{1,9},{2,10},{3,11},{4,12},{5,13},{6,14},{7,15},{8,24},{9,25... | collective-permute-start | bytes 786440 | tf_op jit(solution)/shard_map/ppermute | solution.py:349
  123.8 6.4 %collective-permute-start.27 = (bf16[128,1024]{1,0:T(8,128)(2,1)S(1)}, bf16[128,1024]{1,0:T(8,128)(2,1)S(1)}, u32[]{:S(2)}, u32[]{:S(2)}) collective-permute-start(bf16[128,1024]{1,0:T(8,128)(2,1)S(1)} %fusion.16), channel_id=1, source_target_pairs={{0,4},{1,5},{2,3},{3,2},{4,0},{5,1},{6,7},{7,6},{8,12},{9,13},{10,... | collective-permute-start | bytes 786440 | tf_op jit(solution)/shard_map/ppermute | solution.py:349
  130.4 9.1 %collective-permute-start.31 = (bf16[128,1024]{1,0:T(8,128)(2,1)S(1)}, bf16[128,1024]{1,0:T(8,128)(2,1)S(1)}, u32[]{:S(2)}, u32[]{:S(2)}) collective-permute-start(bf16[128,1024]{1,0:T(8,128)(2,1)S(1)} %fusion.7), channel_id=1, source_target_pairs={{0,8},{1,9},{2,10},{3,11},{4,12},{5,13},{6,14},{7,15},{8,24},{9,25... | collective-permute-start | bytes 786440 | tf_op jit(solution)/shard_map/ppermute | solution.py:349
  134.0 6.4 %collective-permute-start.24 = (bf16[128,1024]{1,0:T(8,128)(2,1)S(1)}, bf16[128,1024]{1,0:T(8,128)(2,1)S(1)}, u32[]{:S(2)}, u32[]{:S(2)}) collective-permute-start(bf16[128,1024]{1,0:T(8,128)(2,1)S(1)} %fusion.15), channel_id=1, source_target_pairs={{0,4},{1,5},{2,3},{3,2},{4,0},{5,1},{6,7},{7,6},{8,12},{9,13},{10,... | collective-permute-start | bytes 786440 | tf_op jit(solution)/shard_map/ppermute | solution.py:349
  140.6 7.3 %collective-permute-start.33 = (bf16[128,1024]{1,0:T(8,128)(2,1)S(1)}, bf16[128,1024]{1,0:T(8,128)(2,1)S(1)}, u32[]{:S(2)}, u32[]{:S(2)}) collective-permute-start(bf16[128,1024]{1,0:T(8,128)(2,1)S(1)} %fusion.10), channel_id=1, source_target_pairs={{0,8},{1,9},{2,10},{3,11},{4,12},{5,13},{6,14},{7,15},{8,24},{9,25... | collective-permute-start | bytes 786440 | tf_op jit(solution)/shard_map/ppermute | solution.py:349
  141.5 6.4 %collective-permute-start.32 = (bf16[128,1024]{1,0:T(8,128)(2,1)S(1)}, bf16[128,1024]{1,0:T(8,128)(2,1)S(1)}, u32[]{:S(2)}, u32[]{:S(2)}) collective-permute-start(bf16[128,1024]{1,0:T(8,128)(2,1)S(1)} %fusion.14), channel_id=1, source_target_pairs={{0,4},{1,5},{2,3},{3,2},{4,0},{5,1},{6,7},{7,6},{8,12},{9,13},{10,... | collective-permute-start | bytes 786440 | tf_op jit(solution)/shard_map/ppermute | solution.py:349

commit v9 on v8

--- a/solution.py
+++ b/solution.py
@@ -130,7 +130,6 @@
         in_specs=[vmem] * 4,
         out_specs=vmem,
         out_shape=jax.ShapeDtypeStruct((2 * rows + INFO_ROWS, width), jnp.bfloat16),
-        cost_estimate=pl.CostEstimate(flops=0, bytes_accessed=8 * rows * width, transcendentals=0),
         name="pack",
     )(tokens, out_grad, routes.T, combine.T)
 
@@ -275,11 +274,6 @@
         out_specs=[vmem] * 3,
         out_shape=[picked, picked, jax.ShapeDtypeStruct((2 * pair_slots, 2 * rows), jnp.bfloat16)],
         compiler_params=pltpu.CompilerParams(vmem_limit_bytes=VMEM_LIMIT),
-        cost_estimate=pl.CostEstimate(
-            flops=32 * pair_slots * 2 * rows * 2 * width,
-            bytes_accessed=2 * (4 * shares[0].size + 8 * pair_slots * width),
-            transcendentals=0,
-        ),
         name="pick",
     )(place, *shares)
 
@@ -301,11 +295,6 @@
         scratch_shapes=[pltpu.VMEM((slots, hidden), jnp.bfloat16)] * 3 + [pltpu.SemaphoreType.DMA((7,))],
         input_output_aliases={} if kept is None else {5 + i: 2 + i for i in range(5)},
         compiler_params=pltpu.CompilerParams(vmem_limit_bytes=VMEM_LIMIT),
-        cost_estimate=pl.CostEstimate(
-            flops=20 * slots * features * hidden,
-            bytes_accessed=2 * (3 * hidden * features + slots * (4 * features + 3 * hidden)),
-            transcendentals=slots * hidden,
-        ),
         name="experts",
     )(mine, theirs, *weights, *(kept or ()))
 
@@ -321,9 +310,6 @@
             jax.ShapeDtypeStruct((2, rows, width), jnp.bfloat16),
         ],
         compiler_params=pltpu.CompilerParams(vmem_limit_bytes=VMEM_LIMIT),
-        cost_estimate=pl.CostEstimate(
-            flops=4 * picks.size * 2 * width, bytes_accessed=4 * near.size + 12 * rows * width, transcendentals=0
-        ),
         name="place",
     )(place, picks, near, far)
 
@@ -374,46 +360,58 @@
     def added(keep, came):
         return keep + came.astype(jnp.float32)
 
-    ring_sends = [("s", 1)] + [(kind, c) for c in range(2, chunks) for kind in ("s", "f")]
+    ring_sends = [("s", 1)] + [(kind, c) for c in range(2, chunks) for kind in ("f", "s")]
+    ring_sends.sort(key=lambda key: key[1] * 2 - (key[0] == "s"))
+    plane_sends = [("f", 0), ("a", 0), ("b", 0), ("f", 1), ("a", 1), ("b", 1)]
+    plane_sends += [(kind, c) for c in range(2, chunks) for kind in ("a", "b")]
     ring_sends = [key for key in ring_sends if key[1] < chunks]
-    plane_sends = [("f", 0), ("a", 0), ("f", 1), ("b", 0)] + [(kind, c) for c in range(1, chunks) for kind in ("a", "b")]
     plane_sends = [key for key in plane_sends if key[1] < chunks]
+
+    def source_of(key, by_ring):
+        kind, c = key
+        return (kind, c - 1) if by_ring else ("f" if kind == "b" else "s", c)
+
     have = {("s", 0): share}
     kept, picked, parts, waiting = None, None, None, None
     late, done = [], 0
     while plane_sends:
         came = {}
-        planned = [key for key in plane_sends if (("f" if key[0] == "b" else "s"), key[1]) in have][:2]
-        for kind, c in planned:
-            source = have["f" if kind == "b" else "s", c]
-            came[kind, c] = to_first(source) if kind == "f" else to_second(source)
-            plane_sends.remove((kind, c))
-        if ring_sends and (ring_sends[0][0], ring_sends[0][1] - 1) in have:
-            kind, c = ring_sends.pop(0)
-            came[kind, c] = to_ring(have[kind, c - 1])
-        ready, waiting = waiting, placed(*parts) if parts is not None else None
-        if ready is not None:
-            keep, send = ready
-            late.append((keep, to_second(send if waiting is None else tied(send, waiting[1]))))
-        parts = None
+        for key in [key for key in plane_sends if source_of(key, False) in have][:2]:
+            value = have[source_of(key, False)]
+            came[key] = to_first(value) if key[0] == "f" else to_second(value)
+            plane_sends.remove(key)
+        for key in [key for key in ring_sends if source_of(key, True) in have][:1]:
+            came[key] = to_ring(have[source_of(key, True)])
+            ring_sends.remove(key)
+        ready, waiting, before = waiting, None, parts
         if picked is not None:
             mine, theirs, picks = picked
             near, far, *kept = run_experts(done, chunks, mine, to_core(theirs), weights, kept)
             parts, picked = (picks, near, far), None
             done += 1
+        else:
+            parts = None
+        if before is not None:
+            waiting = placed(*before)
         if plane_sends and all((kind, done) in have for kind in "sfab"):
-            picked = pick_rows(place, [have.pop((kind, done)) for kind in "sfab"], top, rows, pair_slots)
-        came, have, picked, parts, waiting, weights = lax.optimization_barrier(
-            (came, have, picked, parts, waiting, weights)
+            picked = pick_rows(place, [have[kind, done] for kind in "sfab"], top, rows, pair_slots)
+        if ready is not None:
+            late.append(ready)
+        needed = {key: have[key] for key in have if key[1] >= done}
+        came, have, picked, parts, waiting, late, weights = lax.optimization_barrier(
+            (came, needed, picked, parts, waiting, late, weights)
         )
         have.update(came)
     mine, theirs, picks = pick_rows(place, [have[kind, done] for kind in "sfab"], top, rows, pair_slots)
+    unsent, late = late, []
     if waiting is not None:
         keep, send = waiting
         late.append((keep, to_second(tied(send, theirs))))
+    beside = theirs
     if parts is not None:
-        keep, send = placed(*tied(parts, theirs))
-        late.append((keep, to_second(send)))
+        keep, beside = placed(*tied(parts, theirs))
+        late.append((keep, to_second(beside)))
+    late = [(keep, to_second(tied(send, beside))) for keep, send in unsent] + late
     near, far, *kept = run_experts(done, chunks, mine, to_core(theirs), weights, kept)
     keep, send = placed(picks, near, far)
     late.append((keep, to_second(send)))
@@ -421,15 +419,16 @@
     for c in range(1, chunks):
         keep, came = late[c]
         if c + 1 < chunks:
-            came = tied(came, near if c + 2 < chunks else send)
+            came = tied(came, near if c == 1 else mark)
         pair = added(keep, came)
         came = to_first(pair[1].astype(jnp.bfloat16))
         total = added(pair[0], came if c + 1 == chunks else tied(came, send))
         running = (total if running is None else added(total, running)).astype(jnp.bfloat16)
+        mark = running if c == 1 else mark
         if c + 1 < chunks:
             running = to_ring(running)
     keep, came = late[0]
-    pair = added(keep, came if running is None else tied(came, near))
+    pair = added(keep, came if running is None else tied(came, mark))
     came = pair[1].astype(jnp.bfloat16)
     own = added(pair[0], to_first(came if running is None else tied(came, running)))
     grad_tokens = (own if running is None else added(own, to_ring(running))).astype(jnp.bfloat16)

time: 149 us -> 147 us (0.987)
  starting transfers between devices: 35.6 us -> 32.5 us
    ppermute x34, starting transfers between devices: 35.6 us -> 32.5 us  [permute(): return lax.ppermute(value, ('expert', 'etp'), pairs)]
    unnamed x16 -> x18, local copies, waits for them, and re-layouts: 3.74 us -> 5.16 us
  transfers between devices with their start and end apart: 34 -> 34, of which waited for: 20 -> 18; matrix products, arithmetic and copies ran while one was open for 8% -> 8% of each run, Pallas kernels for 23% -> 24%
where the time goes in v9:
time: 147 us
  waiting for transfers between devices  57.9 us (39%)
  Pallas kernels  38 us (26%)
  starting transfers between devices  32.5 us (22%)
  matrix products  10.1 us (7%)
  local copies, waits for them, and re-layouts  5.29 us (4%)
  other arithmetic  1.82 us (1%)
    ppermute x34, waiting for transfers between devices, permute(): return lax.ppermute(value, ('expert', 'etp'), pairs)  57.9 us
    ppermute x34, starting transfers between devices, permute(): return lax.ppermute(value, ('expert', 'etp'), pairs)  32.5 us
    pallas_call x4, Pallas kernels, run_experts(): pl.pallas_call(functools.partial(expert_kernel, index, kept is not None),...  19.7 us
    pallas_call x4, Pallas kernels, pick_rows(): pl.pallas_call(functools.partial(pick_kernel, top, rows), in_specs=[pl.Bl...  6.71 us
    unnamed x18, local copies, waits for them, and re-layouts  5.16 us
    pallas_call x4, Pallas kernels, place_rows(): pl.pallas_call(place_kernel, in_specs=[pl.BlockSpec(memory_space=pltpu.SM...  5.08 us
    pallas_call x1, Pallas kernels, load_weights(): pl.pallas_call(load_kernel, in_specs=[pl.BlockSpec(memory_space=pltpu.HBM...  4.62 us
    dot_general x1, matrix products, gather_body(): lax.dot_general(gate_term, rows_x, CONTRACT_FIRST, preferred_element_type...  3.38 us
  transfers between devices with their start and end apart: 34, of which 18 were waited for; matrix products, arithmetic and copies ran while one was open for 8% of the time, Pallas kernels for 24%

profile of v9, /device:TPU:0, one launch (start us, length us, event | category | flops | bytes accessed | tf_op | source)
XLA Modules:
  0.0 146.6 jit_solution(17481684088220096903)
XLA Ops:
  0.6 1.9 %pack.1.refs_0_ = bf16[272,1024]{1,0:T(8,128)(2,1)} custom-call(bf16[128,1024]{1,0:T(8,128)(2,1)} %tokens_ref.1, bf16[128,1024]{1,0:T(8,128)(2,1)} %grads_ref.1, s32[8,128]{1,0:T(8,128)} %bitcast.61, f32[8,128]{1,0:T(8,128)} %bitcast.62), custom_call_target="tpu_custom_call" | custom-call | tf_op jit(solution)/shard_map/pack/pallas_call | solution.py:128
  2.5 3.0 %collective-permute-start.2 = (bf16[272,1024]{1,0:T(8,128)(2,1)}, bf16[272,1024]{1,0:T(8,128)(2,1)S(1)}, u32[]{:S(2)}, u32[]{:S(2)}) collective-permute-start(bf16[272,1024]{1,0:T(8,128)(2,1)} %pack.1.refs_0_), channel_id=1, source_target_pairs={{0,8},{1,9},{2,10},{3,11},{4,12},{5,13},{6,14},{7,15},{8,24},{9,25... | collective-permute-start | bytes 1671176 | tf_op jit(solution)/shard_map/ppermute | solution.py:335
  5.5 1.5 %collective-permute-start.1 = (bf16[272,1024]{1,0:T(8,128)(2,1)}, bf16[272,1024]{1,0:T(8,128)(2,1)S(1)}, u32[]{:S(2)}, u32[]{:S(2)}) collective-permute-start(bf16[272,1024]{1,0:T(8,128)(2,1)} %pack.1.refs_0_), channel_id=1, source_target_pairs={{0,4},{1,5},{2,3},{3,2},{4,0},{5,1},{6,7},{7,6},{8,12},{9,13},{10,... | collective-permute-start | bytes 1671176 | tf_op jit(solution)/shard_map/ppermute | solution.py:335
  7.1 1.5 %collective-permute-start = (bf16[272,1024]{1,0:T(8,128)(2,1)}, bf16[272,1024]{1,0:T(8,128)(2,1)S(1)}, u32[]{:S(2)}, u32[]{:S(2)}) collective-permute-start(bf16[272,1024]{1,0:T(8,128)(2,1)} %pack.1.refs_0_), channel_id=1, source_target_pairs={{0,1},{1,0},{2,6},{3,7},{4,5},{5,4},{6,2},{7,3},{8,9},{9,8},{10,14... | collective-permute-start | bytes 1671176 | tf_op jit(solution)/shard_map/ppermute | solution.py:335
  8.6 4.6 %load.1 = (bf16[384,2048]{1,0:T(8,128)(2,1)}, bf16[384,2048]{1,0:T(8,128)(2,1)}, bf16[384,2048]{1,0:T(8,128)(2,1)}) custom-call(bf16[384,2048]{1,0:T(8,128)(2,1)} %bitcast.58, bf16[384,2048]{1,0:T(8,128)(2,1)} %bitcast.59, bf16[384,2048]{1,0:T(8,128)(2,1)} %bitcast.60), custom_call_target="tpu_custom_call" | custom-call | tf_op jit(solution)/shard_map/load/pallas_call | solution.py:147
  13.2 6.2 %collective-permute-done.2.refs_0_ = bf16[272,1024]{1,0:T(8,128)(2,1)S(1)} collective-permute-done((bf16[272,1024]{1,0:T(8,128)(2,1)}, bf16[272,1024]{1,0:T(8,128)(2,1)S(1)}, u32[]{:S(2)}, u32[]{:S(2)}) %collective-permute-start.2) | collective-permute-done | bytes 557088 | tf_op jit(solution)/shard_map/ppermute | solution.py:335
  19.4 1.7 %collective-permute-done.1.refs_1_ = bf16[272,1024]{1,0:T(8,128)(2,1)S(1)} collective-permute-done((bf16[272,1024]{1,0:T(8,128)(2,1)}, bf16[272,1024]{1,0:T(8,128)(2,1)S(1)}, u32[]{:S(2)}, u32[]{:S(2)}) %collective-permute-start.1) | collective-permute-done | bytes 557088 | tf_op jit(solution)/shard_map/ppermute | solution.py:335
  22.4 2.6 %collective-permute-start.5 = (bf16[272,1024]{1,0:T(8,128)(2,1)S(1)}, bf16[272,1024]{1,0:T(8,128)(2,1)S(1)}, u32[]{:S(2)}, u32[]{:S(2)}) collective-permute-start(bf16[272,1024]{1,0:T(8,128)(2,1)S(1)} %collective-permute-done.2.refs_0_), channel_id=1, source_target_pairs={{0,8},{1,9},{2,10},{3,11},{4,12},{5,13},{6,14},{7,15},{8,24},{9,25... | collective-permute-start | bytes 1671176 | tf_op jit(solution)/shard_map/ppermute | solution.py:335
  25.0 1.5 %collective-permute-start.4 = (bf16[272,1024]{1,0:T(8,128)(2,1)S(1)}, bf16[272,1024]{1,0:T(8,128)(2,1)S(1)}, u32[]{:S(2)}, u32[]{:S(2)}) collective-permute-start(bf16[272,1024]{1,0:T(8,128)(2,1)S(1)} %collective-permute-done.2.refs_0_), channel_id=1, source_target_pairs={{0,4},{1,5},{2,3},{3,2},{4,0},{5,1},{6,7},{7,6},{8,12},{9,13},{10,... | collective-permute-start | bytes 1671176 | tf_op jit(solution)/shard_map/ppermute | solution.py:335
  26.5 8.3 %collective-permute-done.3.refs_3_ = bf16[272,1024]{1,0:T(8,128)(2,1)S(1)} collective-permute-done((bf16[272,1024]{1,0:T(8,128)(2,1)S(1)}, bf16[272,1024]{1,0:T(8,128)(2,1)S(1)}, u32[]{:S(2)}, u32[]{:S(2)}) %collective-permute-start.3) | collective-permute-done | bytes 557088 | tf_op jit(solution)/shard_map/ppermute | solution.py:335
  35.6 2.8 %collective-permute-done.5.refs_0_ = bf16[272,1024]{1,0:T(8,128)(2,1)S(1)} collective-permute-done((bf16[272,1024]{1,0:T(8,128)(2,1)S(1)}, bf16[272,1024]{1,0:T(8,128)(2,1)S(1)}, u32[]{:S(2)}, u32[]{:S(2)}) %collective-permute-start.5) | collective-permute-done | bytes 557088 | tf_op jit(solution)/shard_map/ppermute | solution.py:335
  38.5 2.8 %collective-permute-start.8 = (bf16[272,1024]{1,0:T(8,128)(2,1)S(1)}, bf16[272,1024]{1,0:T(8,128)(2,1)S(1)}, u32[]{:S(2)}, u32[]{:S(2)}) collective-permute-start(bf16[272,1024]{1,0:T(8,128)(2,1)S(1)} %collective-permute-done.4.refs_1_), channel_id=1, source_target_pairs={{0,8},{1,9},{2,10},{3,11},{4,12},{5,13},{6,14},{7,15},{8,24},{9,25... | collective-permute-start | bytes 1671176 | tf_op jit(solution)/shard_map/ppermute | solution.py:335
  41.2 1.2 collective-permute-start.7
  42.6 1.1 copy-done.6
  43.6 1.1 copy-done.8
  44.7 1.5 %pick.4 = (bf16[2,144,2048]{2,1,0:T(8,128)(2,1)S(1)}, bf16[2,144,2048]{2,1,0:T(8,128)(2,1)S(1)}, bf16[288,256]{1,0:T(8,128)(2,1)S(1)}) custom-call(s32[3]{0:T(128)S(1)} %pad_add_fusion.place_ref, bf16[272,1024]{1,0:T(8,128)(2,1)S(1)} %copy-done.4, bf16[272,1024]{1,0:T(8,128)(2,1)S(1)} %collective-permute-done.1.refs_1_, bf16[272,1024]{1,0:T(8,128)(2,1)S(1)} %copy-done.6, ...), custom_call_target="tpu_custom_call" | custom-call | tf_op jit(solution)/shard_map/pick/pallas_call | solution.py:271
  46.2 1.9 %collective-permute-done.6.refs_2_ = bf16[272,1024]{1,0:T(8,128)(2,1)} collective-permute-done((bf16[272,1024]{1,0:T(8,128)(2,1)S(1)}, bf16[272,1024]{1,0:T(8,128)(2,1)}, u32[]{:S(2)}, u32[]{:S(2)}) %collective-permute-start.6) | collective-permute-done | bytes 557088 | tf_op jit(solution)/shard_map/ppermute | solution.py:335
  48.1 6.1 %collective-permute-done.8.refs_1_ = bf16[272,1024]{1,0:T(8,128)(2,1)S(1)} collective-permute-done((bf16[272,1024]{1,0:T(8,128)(2,1)S(1)}, bf16[272,1024]{1,0:T(8,128)(2,1)S(1)}, u32[]{:S(2)}, u32[]{:S(2)}) %collective-permute-start.8) | collective-permute-done | bytes 557088 | tf_op jit(solution)/shard_map/ppermute | solution.py:335
  54.4 2.4 %collective-permute-start.11 = (bf16[272,1024]{1,0:T(8,128)(2,1)S(1)}, bf16[272,1024]{1,0:T(8,128)(2,1)S(1)}, u32[]{:S(2)}, u32[]{:S(2)}) collective-permute-start(bf16[272,1024]{1,0:T(8,128)(2,1)S(1)} %collective-permute-done.5.refs_0_), channel_id=1, source_target_pairs={{0,8},{1,9},{2,10},{3,11},{4,12},{5,13},{6,14},{7,15},{8,24},{9,25... | collective-permute-start | bytes 1671176 | tf_op jit(solution)/shard_map/ppermute | solution.py:335
  56.8 1.2 collective-permute-start.9
  58.1 2.2 %pick.5 = (bf16[2,144,2048]{2,1,0:T(8,128)(2,1)S(1)}, bf16[2,144,2048]{2,1,0:T(8,128)(2,1)S(1)}, bf16[288,256]{1,0:T(8,128)(2,1)S(1)}) custom-call(s32[3]{0:T(128)S(1)} %pad_add_fusion.place_ref, bf16[272,1024]{1,0:T(8,128)(2,1)S(1)} %collective-permute-done.2.refs_0_, bf16[272,1024]{1,0:T(8,128)(2,1)S(1)} %collective-permute-done.4.refs_1_, ...), custom_call_target="tpu_custom_call" | custom-call | tf_op jit(solution)/shard_map/pick/pallas_call | solution.py:271
  60.3 1.4 copy-done.2
  61.7 4.8 %experts.4 = (bf16[144,2048]{1,0:T(8,128)(2,1)S(1)}, bf16[144,2048]{1,0:T(8,128)(2,1)S(1)}, bf16[1152,2048]{1,0:T(8,128)(2,1)S(1)}, bf16[1152,2048]{1,0:T(8,128)...) custom-call(bf16[2,144,2048]{2,1,0:T(8,128)(2,1)S(1)} %get-tuple-element.175., ...), custom_call_target="tpu_custom_call" | custom-call | tf_op jit(solution)/shard_map/experts/pallas_call | solution.py:290
  66.6 4.1 %collective-permute-done.11.refs_0_ = bf16[272,1024]{1,0:T(8,128)(2,1)S(1)} collective-permute-done((bf16[272,1024]{1,0:T(8,128)(2,1)S(1)}, bf16[272,1024]{1,0:T(8,128)(2,1)S(1)}, u32[]{:S(2)}, u32[]{:S(2)}) %collective-permute-start.11) | collective-permute-done | bytes 557088 | tf_op jit(solution)/shard_map/ppermute | solution.py:335
  71.4 1.5 collective-permute-start.14
  72.9 1.5 %pick.6 = (bf16[2,144,2048]{2,1,0:T(8,128)(2,1)S(1)}, bf16[2,144,2048]{2,1,0:T(8,128)(2,1)S(1)}, bf16[288,256]{1,0:T(8,128)(2,1)S(1)}) custom-call(s32[3]{0:T(128)S(1)} %pad_add_fusion.place_ref, bf16[272,1024]{1,0:T(8,128)(2,1)S(1)} %collective-permute-done.5.refs_0_, bf16[272,1024]{1,0:T(8,128)(2,1)S(1)} %collective-permute-done.8.refs_1_, ...), custom_call_target="tpu_custom_call" | custom-call | tf_op jit(solution)/shard_map/pick/pallas_call | solution.py:271
  74.4 1.3 place.4
  75.7 5.1 %experts.5 = (bf16[144,2048]{1,0:T(8,128)(2,1)S(1)}, bf16[144,2048]{1,0:T(8,128)(2,1)S(1)}, bf16[1152,2048]{1,0:T(8,128)(2,1)S(1)}, bf16[1152,2048]{1,0:T(8,128)...) custom-call(bf16[2,144,2048]{2,1,0:T(8,128)(2,1)S(1)} %get-tuple-ele, ...), custom_call_target="tpu_custom_call", output_to_operand_aliasing={{2}: (5, {}), {3}: (6, {}), {4}: (7, {}), {5}: (8, {}), {6}... | custom-call | tf_op jit(solution)/shard_map/experts/pallas_call | solution.py:290
  80.8 6.9 %collective-permute-done.14.refs_1_ = bf16[272,1024]{1,0:T(8,128)(2,1)S(1)} collective-permute-done((bf16[272,1024]{1,0:T(8,128)(2,1)S(1)}, bf16[272,1024]{1,0:T(8,128)(2,1)S(1)}, u32[]{:S(2)}, u32[]{:S(2)}) %collective-permute-start.14) | collective-permute-done | bytes 557088 | tf_op jit(solution)/shard_map/ppermute | solution.py:335
  88.4 3.0 %collective-permute-done.19.far_ref = bf16[144,2048]{1,0:T(8,128)(2,1)S(1)} collective-permute-done((bf16[144,2048]{1,0:T(8,128)(2,1)S(1)}, bf16[144,2048]{1,0:T(8,128)(2,1)S(1)}, u32[]{:S(2)}, u32[]{:S(2)}) %collective-permute-start.19) | collective-permute-done | bytes 589856 | tf_op jit(solution)/shard_map/ppermute | solution.py:335
  91.3 1.3 place.5
  92.6 4.9 %experts.6 = (bf16[144,2048]{1,0:T(8,128)(2,1)S(1)}, bf16[144,2048]{1,0:T(8,128)(2,1)S(1)}, bf16[1152,2048]{1,0:T(8,128)(2,1)S(1)}, bf16[1152,2048]{1,0:T(8,128)...) custom-call(bf16[2,144,2048]{2,1,0:T(8,128)(2,1)S(1)} %get-tuple-ele, ...), custom_call_target="tpu_custom_call", output_to_operand_aliasing={{2}: (5, {}), {3}: (6, {}), {4}: (7, {}), {5}: (8, {}), {6}... | custom-call | tf_op jit(solution)/shard_map/experts/pallas_call | solution.py:290
  97.7 1.5 %pick.7 = (bf16[2,144,2048]{2,1,0:T(8,128)(2,1)S(1)}, bf16[2,144,2048]{2,1,0:T(8,128)(2,1)S(1)}, bf16[288,256]{1,0:T(8,128)(2,1)S(1)}) custom-call(s32[3]{0:T(128)S(1)} %pad_add_fusion.place_ref, bf16[272,1024]{1,0:T(8,128)(2,1)S(1)} %collective-permute-done.11.refs_0_, bf16[272,1024]{1,0:T(8,128)(2,1)S(1)} %collective-permute-done.14.refs_1_, ...), custom_call_target="tpu_custom_call" | custom-call | tf_op jit(solution)/shard_map/pick/pallas_call | solution.py:271
  100.0 3.0 %collective-permute-done.20.far_ref = bf16[144,2048]{1,0:T(8,128)(2,1)S(1)} collective-permute-done((bf16[144,2048]{1,0:T(8,128)(2,1)S(1)}, bf16[144,2048]{1,0:T(8,128)(2,1)S(1)}, u32[]{:S(2)}, u32[]{:S(2)}) %collective-permute-start.20) | collective-permute-done | bytes 589856 | tf_op jit(solution)/shard_map/ppermute | solution.py:335
  103.0 1.3 place.6
  104.5 4.9 %experts.7 = (bf16[144,2048]{1,0:T(8,128)(2,1)S(1)}, bf16[144,2048]{1,0:T(8,128)(2,1)S(1)}, bf16[1152,2048]{1,0:T(8,128)(2,1)S(1)}, bf16[1152,2048]{1,0:T(8,128)...) custom-call(bf16[2,144,2048]{2,1,0:T(8,128)(2,1)S(1)} %get-tuple-ele, ...), custom_call_target="tpu_custom_call", output_to_operand_aliasing={{2}: (5, {}), {3}: (6, {}), {4}: (7, {}), {5}: (8, {}), {6}... | custom-call | tf_op jit(solution)/shard_map/experts/pallas_call | solution.py:290
  110.2 1.3 collective-permute-start.24
  112.4 1.3 place.7
  113.7 1.1 collective-permute-start.26
  114.8 4.0 %collective-permute-done.24 = bf16[128,1024]{1,0:T(8,128)(2,1)S(1)} collective-permute-done((bf16[128,1024]{1,0:T(8,128)(2,1)S(1)}, bf16[128,1024]{1,0:T(8,128)(2,1)S(1)}, u32[]{:S(2)}, u32[]{:S(2)}) %collective-permute-start.24) | collective-permute-done | bytes 262176 | tf_op jit(solution)/shard_map/ppermute | solution.py:335
  118.9 1.0 collective-permute-start.30
  121.1 3.4 %fusion = bf16[1,384,2048]{2,1,0:T(8,128)(2,1)} fusion(bf16[1152,384]{1,0:T(8,128)(2,1)S(1)} %get-tuple-element.275, bf16[1152,2048]{1,0:T(8,128)(2,1)S(1)} %get-tuple-element.276), kind=kOutput, calls=%fused_computation.3 | convolution fusion | flops 1812725760 | bytes 7176192 | tf_op jit(solution)/shard_map/dot_general | solution.py:438
  124.4 3.4 %fusion.1 = bf16[1,384,2048]{2,1,0:T(8,128)(2,1)} fusion(bf16[1152,384]{1,0:T(8,128)(2,1)S(1)} %get-tuple-element.277, bf16[1152,2048]{1,0:T(8,128)(2,1)S(1)} %get-tuple-element.276), kind=kOutput, calls=%fused_computation.4 | convolution fusion | flops 1812725760 | bytes 7176192 | tf_op jit(solution)/shard_map/dot_general | solution.py:439
  127.8 1.6 %collective-permute-done.29 = bf16[128,1024]{1,0:T(8,128)(2,1)S(1)} collective-permute-done((bf16[128,1024]{1,0:T(8,128)(2,1)S(1)}, bf16[128,1024]{1,0:T(8,128)(2,1)S(1)}, u32[]{:S(2)}, u32[]{:S(2)}) %collective-permute-start.29) | collective-permute-done | bytes 262176 | tf_op jit(solution)/shard_map/ppermute | solution.py:335
  129.5 1.7 %collective-permute-start.31 = (bf16[128,1024]{1,0:T(8,128)(2,1)S(1)}, bf16[128,1024]{1,0:T(8,128)(2,1)S(1)}, u32[]{:S(2)}, u32[]{:S(2)}) collective-permute-start(bf16[128,1024]{1,0:T(8,128)(2,1)S(1)} %fusion.5), channel_id=1, source_target_pairs={{0,8},{1,9},{2,10},{3,11},{4,12},{5,13},{6,14},{7,15},{8,24},{9,25... | collective-permute-start | bytes 786440 | tf_op jit(solution)/shard_map/ppermute | solution.py:335
  132.8 4.5 %collective-permute-done.31 = bf16[128,1024]{1,0:T(8,128)(2,1)S(1)} collective-permute-done((bf16[128,1024]{1,0:T(8,128)(2,1)S(1)}, bf16[128,1024]{1,0:T(8,128)(2,1)S(1)}, u32[]{:S(2)}, u32[]{:S(2)}) %collective-permute-start.31) | collective-permute-done | bytes 262176 | tf_op jit(solution)/shard_map/ppermute | solution.py:335
  139.8 3.4 %fusion.2 = bf16[1,384,2048]{2,1,0:T(8,128)(2,1)} fusion(bf16[1152,384]{1,0:T(8,128)(2,1)S(1)} %get-tuple-element.278, bf16[1152,2048]{1,0:T(8,128)(2,1)S(1)} %get-tuple-element.279), kind=kOutput, calls=%fused_computation.5 | convolution fusion | flops 1812725760 | bytes 7176192 | tf_op jit(solution)/shard_map/dot_general | solution.py:437
  143.1 2.5 %collective-permute-done.32 = bf16[128,1024]{1,0:T(8,128)(2,1)S(1)} collective-permute-done((bf16[128,1024]{1,0:T(8,128)(2,1)S(1)}, bf16[128,1024]{1,0:T(8,128)(2,1)S(1)}, u32[]{:S(2)}, u32[]{:S(2)}) %collective-permute-start.32) | collective-permute-done | bytes 262176 | tf_op jit(solution)/shard_map/ppermute | solution.py:335
  (68 shorter events, 13.2 us)
Async XLA Ops:
  2.5 16.9 %collective-permute-start.2 = (bf16[272,1024]{1,0:T(8,128)(2,1)}, bf16[272,1024]{1,0:T(8,128)(2,1)S(1)}, u32[]{:S(2)}, u32[]{:S(2)}) collective-permute-start(bf16[272,1024]{1,0:T(8,128)(2,1)} %pack.1.refs_0_), channel_id=1, source_target_pairs={{0,8},{1,9},{2,10},{3,11},{4,12},{5,13},{6,14},{7,15},{8,24},{9,25... | collective-permute-start | bytes 1671176 | tf_op jit(solution)/shard_map/ppermute | solution.py:335
  5.5 15.5 %collective-permute-start.1 = (bf16[272,1024]{1,0:T(8,128)(2,1)}, bf16[272,1024]{1,0:T(8,128)(2,1)S(1)}, u32[]{:S(2)}, u32[]{:S(2)}) collective-permute-start(bf16[272,1024]{1,0:T(8,128)(2,1)} %pack.1.refs_0_), channel_id=1, source_target_pairs={{0,4},{1,5},{2,3},{3,2},{4,0},{5,1},{6,7},{7,6},{8,12},{9,13},{10,... | collective-permute-start | bytes 1671176 | tf_op jit(solution)/shard_map/ppermute | solution.py:335
  7.1 14.0 %collective-permute-start = (bf16[272,1024]{1,0:T(8,128)(2,1)}, bf16[272,1024]{1,0:T(8,128)(2,1)S(1)}, u32[]{:S(2)}, u32[]{:S(2)}) collective-permute-start(bf16[272,1024]{1,0:T(8,128)(2,1)} %pack.1.refs_0_), channel_id=1, source_target_pairs={{0,1},{1,0},{2,6},{3,7},{4,5},{5,4},{6,2},{7,3},{8,9},{9,8},{10,14... | collective-permute-start | bytes 1671176 | tf_op jit(solution)/shard_map/ppermute | solution.py:335
  8.6 34.0 %copy-start.4 = (bf16[272,1024]{1,0:T(8,128)(2,1)S(1)}, bf16[272,1024]{1,0:T(8,128)(2,1)}, u32[]{:S(2)}) copy-start(bf16[272,1024]{1,0:T(8,128)(2,1)} %pack.1.refs_0_) | copy-start | bytes 1671172
  21.1 0.8 copy-start.5
  21.9 12.9 %collective-permute-start.3 = (bf16[272,1024]{1,0:T(8,128)(2,1)S(1)}, bf16[272,1024]{1,0:T(8,128)(2,1)S(1)}, u32[]{:S(2)}, u32[]{:S(2)}) collective-permute-start(bf16[272,1024]{1,0:T(8,128)(2,1)S(1)} %collective-permute-done.1.refs_1_), channel_id=1, source_target_pairs={{0,1},{1,0},{2,6},{3,7},{4,5},{5,4},{6,2},{7,3},{8,9},{9,8},{10,14... | collective-permute-start | bytes 1671176 | tf_op jit(solution)/shard_map/ppermute | solution.py:335
  22.4 16.0 %collective-permute-start.5 = (bf16[272,1024]{1,0:T(8,128)(2,1)S(1)}, bf16[272,1024]{1,0:T(8,128)(2,1)S(1)}, u32[]{:S(2)}, u32[]{:S(2)}) collective-permute-start(bf16[272,1024]{1,0:T(8,128)(2,1)S(1)} %collective-permute-done.2.refs_0_), channel_id=1, source_target_pairs={{0,8},{1,9},{2,10},{3,11},{4,12},{5,13},{6,14},{7,15},{8,24},{9,25... | collective-permute-start | bytes 1671176 | tf_op jit(solution)/shard_map/ppermute | solution.py:335
  25.0 13.5 %collective-permute-start.4 = (bf16[272,1024]{1,0:T(8,128)(2,1)S(1)}, bf16[272,1024]{1,0:T(8,128)(2,1)S(1)}, u32[]{:S(2)}, u32[]{:S(2)}) collective-permute-start(bf16[272,1024]{1,0:T(8,128)(2,1)S(1)} %collective-permute-done.2.refs_0_), channel_id=1, source_target_pairs={{0,4},{1,5},{2,3},{3,2},{4,0},{5,1},{6,7},{7,6},{8,12},{9,13},{10,... | collective-permute-start | bytes 1671176 | tf_op jit(solution)/shard_map/ppermute | solution.py:335
  34.8 0.8 copy-start.7
  38.5 9.6 %collective-permute-start.6 = (bf16[272,1024]{1,0:T(8,128)(2,1)S(1)}, bf16[272,1024]{1,0:T(8,128)(2,1)}, u32[]{:S(2)}, u32[]{:S(2)}) collective-permute-start(bf16[272,1024]{1,0:T(8,128)(2,1)S(1)} %collective-permute-done.2.refs_0_), channel_id=1, source_target_pairs={{0,1},{1,0},{2,6},{3,7},{4,5},{5,4},{6,2},{7,3},{8,9},{9,8},{10,14... | collective-permute-start | bytes 1671176 | tf_op jit(solution)/shard_map/ppermute | solution.py:335
  38.5 15.7 %collective-permute-start.8 = (bf16[272,1024]{1,0:T(8,128)(2,1)S(1)}, bf16[272,1024]{1,0:T(8,128)(2,1)S(1)}, u32[]{:S(2)}, u32[]{:S(2)}) collective-permute-start(bf16[272,1024]{1,0:T(8,128)(2,1)S(1)} %collective-permute-done.4.refs_1_), channel_id=1, source_target_pairs={{0,8},{1,9},{2,10},{3,11},{4,12},{5,13},{6,14},{7,15},{8,24},{9,25... | collective-permute-start | bytes 1671176 | tf_op jit(solution)/shard_map/ppermute | solution.py:335
  41.2 12.9 %collective-permute-start.7 = (bf16[272,1024]{1,0:T(8,128)(2,1)S(1)}, bf16[272,1024]{1,0:T(8,128)(2,1)}, u32[]{:S(2)}, u32[]{:S(2)}) collective-permute-start(bf16[272,1024]{1,0:T(8,128)(2,1)S(1)} %collective-permute-done.4.refs_1_), channel_id=1, source_target_pairs={{0,1},{1,0},{2,6},{3,7},{4,5},{5,4},{6,2},{7,3},{8,9},{9,8},{10,14... | collective-permute-start | bytes 1671176 | tf_op jit(solution)/shard_map/ppermute | solution.py:335
  42.6 1.1 copy-start.6
  43.6 1.1 copy-start.8
  44.7 15.6 %copy-start.1 = (bf16[384,2048]{1,0:T(8,128)(2,1)S(1)}, bf16[384,2048]{1,0:T(8,128)(2,1)}, u32[]{:S(2)}) copy-start(bf16[384,2048]{1,0:T(8,128)(2,1)} %get-tuple-element.251.wu_ref) | copy-start | bytes 4718596
  46.2 14.1 %copy-start = (bf16[384,2048]{1,0:T(8,128)(2,1)S(1)}, bf16[384,2048]{1,0:T(8,128)(2,1)}, u32[]{:S(2)}) copy-start(bf16[384,2048]{1,0:T(8,128)(2,1)} %get-tuple-element.250.wg_ref) | copy-start | bytes 4718596
  54.2 6.1 %collective-permute-start.12 = (bf16[2,144,2048]{2,1,0:T(8,128)(2,1)S(1)}, bf16[2,144,2048]{2,1,0:T(8,128)(2,1)S(1)}, u32[]{:S(2)}, u32[]{:S(2)}) collective-permute-start(bf16[2,144,2048]{2,1,0:T(8,128)(2,1)S(1)} %get-tuple-element.176), channel_id=1, source_target_pairs={{0,2},{1,3},{2,0},{3,1},{4,6},{5,7},{6,4},{7,5},{8,10},{9,11},{10,... | collective-permute-start | bytes 3538952 | tf_op jit(solution)/shard_map/ppermute | solution.py:335
  54.2 12.4 %collective-permute-start.10 = (bf16[272,1024]{1,0:T(8,128)(2,1)S(1)}, bf16[272,1024]{1,0:T(8,128)(2,1)S(1)}, u32[]{:S(2)}, u32[]{:S(2)}) collective-permute-start(bf16[272,1024]{1,0:T(8,128)(2,1)S(1)} %collective-permute-done.8.refs_1_), channel_id=1, source_target_pairs={{0,1},{1,0},{2,6},{3,7},{4,5},{5,4},{6,2},{7,3},{8,9},{9,8},{10,14... | collective-permute-start | bytes 1671176 | tf_op jit(solution)/shard_map/ppermute | solution.py:335
  54.4 16.2 %collective-permute-start.11 = (bf16[272,1024]{1,0:T(8,128)(2,1)S(1)}, bf16[272,1024]{1,0:T(8,128)(2,1)S(1)}, u32[]{:S(2)}, u32[]{:S(2)}) collective-permute-start(bf16[272,1024]{1,0:T(8,128)(2,1)S(1)} %collective-permute-done.5.refs_0_), channel_id=1, source_target_pairs={{0,8},{1,9},{2,10},{3,11},{4,12},{5,13},{6,14},{7,15},{8,24},{9,25... | collective-permute-start | bytes 1671176 | tf_op jit(solution)/shard_map/ppermute | solution.py:335
  56.8 13.8 %collective-permute-start.9 = (bf16[272,1024]{1,0:T(8,128)(2,1)S(1)}, bf16[272,1024]{1,0:T(8,128)(2,1)S(1)}, u32[]{:S(2)}, u32[]{:S(2)}) collective-permute-start(bf16[272,1024]{1,0:T(8,128)(2,1)S(1)} %collective-permute-done.5.refs_0_), channel_id=1, source_target_pairs={{0,1},{1,0},{2,6},{3,7},{4,5},{5,4},{6,2},{7,3},{8,9},{9,8},{10,14... | collective-permute-start | bytes 1671176 | tf_op jit(solution)/shard_map/ppermute | solution.py:335
  60.3 1.4 copy-start.2
  70.6 5.0 %copy-start.3 = (bf16[384,2048]{1,0:T(8,128)(2,1)S(1)}, bf16[384,2048]{1,0:T(8,128)(2,1)}, u32[]{:S(2)}) copy-start(bf16[384,2048]{1,0:T(8,128)(2,1)} %get-tuple-element.252.wd_ref) | copy-start | bytes 4718596
  70.6 5.0 %collective-permute-start.15 = (bf16[2,144,2048]{2,1,0:T(8,128)(2,1)S(1)}, bf16[2,144,2048]{2,1,0:T(8,128)(2,1)S(1)}, u32[]{:S(2)}, u32[]{:S(2)}) collective-permute-start(bf16[2,144,2048]{2,1,0:T(8,128)(2,1)S(1)} %get-tuple-element.192), channel_id=1, source_target_pairs={{0,2},{1,3},{2,0},{3,1},{4,6},{5,7},{6,4},{7,5},{8,10},{9,11},{10,... | collective-permute-start | bytes 3538952 | tf_op jit(solution)/shard_map/ppermute | solution.py:335
  70.8 3.6 %collective-permute-start.16 = (bf16[144,2048]{1,0:T(8,128)(2,1)S(1)}, bf16[144,2048]{1,0:T(8,128)(2,1)S(1)}, u32[]{:S(2)}, u32[]{:S(2)}) collective-permute-start(bf16[144,2048]{1,0:T(8,128)(2,1)S(1)} %get-tuple-element.205), channel_id=1, source_target_pairs={{0,2},{1,3},{2,0},{3,1},{4,6},{5,7},{6,4},{7,5},{8,10},{9,11},{10,... | collective-permute-start | bytes 1769480 | tf_op jit(solution)/shard_map/ppermute | solution.py:335
  71.2 9.6 %collective-permute-start.13 = (bf16[272,1024]{1,0:T(8,128)(2,1)S(1)}, bf16[272,1024]{1,0:T(8,128)(2,1)S(1)}, u32[]{:S(2)}, u32[]{:S(2)}) collective-permute-start(bf16[272,1024]{1,0:T(8,128)(2,1)S(1)} %collective-permute-done.11.refs_0_), channel_id=1, source_target_pairs={{0,1},{1,0},{2,6},{3,7},{4,5},{5,4},{6,2},{7,3},{8,9},{9,8},{10,14... | collective-permute-start | bytes 1671176 | tf_op jit(solution)/shard_map/ppermute | solution.py:335
  71.4 16.2 %collective-permute-start.14 = (bf16[272,1024]{1,0:T(8,128)(2,1)S(1)}, bf16[272,1024]{1,0:T(8,128)(2,1)S(1)}, u32[]{:S(2)}, u32[]{:S(2)}) collective-permute-start(bf16[272,1024]{1,0:T(8,128)(2,1)S(1)} %collective-permute-done.8.refs_1_), channel_id=1, source_target_pairs={{0,8},{1,9},{2,10},{3,11},{4,12},{5,13},{6,14},{7,15},{8,24},{9,25... | collective-permute-start | bytes 1671176 | tf_op jit(solution)/shard_map/ppermute | solution.py:335
  87.6 5.0 %collective-permute-start.18 = (bf16[2,144,2048]{2,1,0:T(8,128)(2,1)S(1)}, bf16[2,144,2048]{2,1,0:T(8,128)(2,1)S(1)}, u32[]{:S(2)}, u32[]{:S(2)}) collective-permute-start(bf16[2,144,2048]{2,1,0:T(8,128)(2,1)S(1)} %get-tuple-element.213), channel_id=1, source_target_pairs={{0,2},{1,3},{2,0},{3,1},{4,6},{5,7},{6,4},{7,5},{8,10},{9,11},{10,... | collective-permute-start | bytes 3538952 | tf_op jit(solution)/shard_map/ppermute | solution.py:335
  87.6 3.7 %collective-permute-start.19 = (bf16[144,2048]{1,0:T(8,128)(2,1)S(1)}, bf16[144,2048]{1,0:T(8,128)(2,1)S(1)}, u32[]{:S(2)}, u32[]{:S(2)}) collective-permute-start(bf16[144,2048]{1,0:T(8,128)(2,1)S(1)} %get-tuple-element.226), channel_id=1, source_target_pairs={{0,2},{1,3},{2,0},{3,1},{4,6},{5,7},{6,4},{7,5},{8,10},{9,11},{10,... | collective-permute-start | bytes 1769480 | tf_op jit(solution)/shard_map/ppermute | solution.py:335
  88.2 9.5 %collective-permute-start.17 = (bf16[272,1024]{1,0:T(8,128)(2,1)S(1)}, bf16[272,1024]{1,0:T(8,128)(2,1)S(1)}, u32[]{:S(2)}, u32[]{:S(2)}) collective-permute-start(bf16[272,1024]{1,0:T(8,128)(2,1)S(1)} %collective-permute-done.14.refs_1_), channel_id=1, source_target_pairs={{0,1},{1,0},{2,6},{3,7},{4,5},{5,4},{6,2},{7,3},{8,9},{9,8},{10,14... | collective-permute-start | bytes 1671176 | tf_op jit(solution)/shard_map/ppermute | solution.py:335
  99.2 5.3 %collective-permute-start.23 = (bf16[2,144,2048]{2,1,0:T(8,128)(2,1)S(1)}, bf16[2,144,2048]{2,1,0:T(8,128)(2,1)S(1)}, u32[]{:S(2)}, u32[]{:S(2)}) collective-permute-start(bf16[2,144,2048]{2,1,0:T(8,128)(2,1)S(1)} %get-tuple-element.240), channel_id=1, source_target_pairs={{0,2},{1,3},{2,0},{3,1},{4,6},{5,7},{6,4},{7,5},{8,10},{9,11},{10,... | collective-permute-start | bytes 3538952 | tf_op jit(solution)/shard_map/ppermute | solution.py:335
  99.3 3.7 %collective-permute-start.20 = (bf16[144,2048]{1,0:T(8,128)(2,1)S(1)}, bf16[144,2048]{1,0:T(8,128)(2,1)S(1)}, u32[]{:S(2)}, u32[]{:S(2)}) collective-permute-start(bf16[144,2048]{1,0:T(8,128)(2,1)S(1)} %get-tuple-element.243), channel_id=1, source_target_pairs={{0,2},{1,3},{2,0},{3,1},{4,6},{5,7},{6,4},{7,5},{8,10},{9,11},{10,... | collective-permute-start | bytes 1769480 | tf_op jit(solution)/shard_map/ppermute | solution.py:335
  99.8 9.6 %collective-permute-start.22 = (bf16[2,128,1024]{2,1,0:T(8,128)(2,1)S(1)}, bf16[2,128,1024]{2,1,0:T(8,128)(2,1)S(1)}, u32[]{:S(2)}, u32[]{:S(2)}) collective-permute-start(bf16[2,128,1024]{2,1,0:T(8,128)(2,1)S(1)} %get-tuple-element.248), channel_id=1, source_target_pairs={{0,1},{1,0},{2,6},{3,7},{4,5},{5,4},{6,2},{7,3},{8,9},{9,8},{10,14... | collective-permute-start | bytes 1572872 | tf_op jit(solution)/shard_map/ppermute | solution.py:335
  104.2 15.7 %collective-permute-start.28 = (bf16[2,128,1024]{2,1,0:T(8,128)(2,1)S(1)}, bf16[2,128,1024]{2,1,0:T(8,128)(2,1)S(1)}, u32[]{:S(2)}, u32[]{:S(2)}) collective-permute-start(bf16[2,128,1024]{2,1,0:T(8,128)(2,1)S(1)} %get-tuple-element.244), channel_id=1, source_target_pairs={{0,1},{1,0},{2,6},{3,7},{4,5},{5,4},{6,2},{7,3},{8,9},{9,8},{10,14... | collective-permute-start | bytes 1572872 | tf_op jit(solution)/shard_map/ppermute | solution.py:335
  109.4 3.0 %collective-permute-start.25 = (bf16[144,2048]{1,0:T(8,128)(2,1)S(1)}, bf16[144,2048]{1,0:T(8,128)(2,1)S(1)}, u32[]{:S(2)}, u32[]{:S(2)}) collective-permute-start(bf16[144,2048]{1,0:T(8,128)(2,1)S(1)} %get-tuple-element.261), channel_id=1, source_target_pairs={{0,2},{1,3},{2,0},{3,1},{4,6},{5,7},{6,4},{7,5},{8,10},{9,11},{10,... | collective-permute-start | bytes 1769480 | tf_op jit(solution)/shard_map/ppermute | solution.py:335
  110.2 8.7 %collective-permute-start.24 = (bf16[128,1024]{1,0:T(8,128)(2,1)S(1)}, bf16[128,1024]{1,0:T(8,128)(2,1)S(1)}, u32[]{:S(2)}, u32[]{:S(2)}) collective-permute-start(bf16[128,1024]{1,0:T(8,128)(2,1)S(1)} %fusion.14), channel_id=1, source_target_pairs={{0,4},{1,5},{2,3},{3,2},{4,0},{5,1},{6,7},{7,6},{8,12},{9,13},{10,... | collective-permute-start | bytes 786440 | tf_op jit(solution)/shard_map/ppermute | solution.py:335
  111.5 16.4 %collective-permute-start.21 = (bf16[2,128,1024]{2,1,0:T(8,128)(2,1)S(1)}, bf16[2,128,1024]{2,1,0:T(8,128)(2,1)S(1)}, u32[]{:S(2)}, u32[]{:S(2)}) collective-permute-start(bf16[2,128,1024]{2,1,0:T(8,128)(2,1)S(1)} %get-tuple-element.245), channel_id=1, source_target_pairs={{0,1},{1,0},{2,6},{3,7},{4,5},{5,4},{6,2},{7,3},{8,9},{9,8},{10,14... | collective-permute-start | bytes 1572872 | tf_op jit(solution)/shard_map/ppermute | solution.py:335
  113.7 17.7 %collective-permute-start.26 = (bf16[2,128,1024]{2,1,0:T(8,128)(2,1)S(1)}, bf16[2,128,1024]{2,1,0:T(8,128)(2,1)S(1)}, u32[]{:S(2)}, u32[]{:S(2)}) collective-permute-start(bf16[2,128,1024]{2,1,0:T(8,128)(2,1)S(1)} %get-tuple-element.262), channel_id=1, source_target_pairs={{0,1},{1,0},{2,6},{3,7},{4,5},{5,4},{6,2},{7,3},{8,9},{9,8},{10,14... | collective-permute-start | bytes 1572872 | tf_op jit(solution)/shard_map/ppermute | solution.py:335
  118.9 10.5 %collective-permute-start.30 = (bf16[128,1024]{1,0:T(8,128)(2,1)S(1)}, bf16[128,1024]{1,0:T(8,128)(2,1)S(1)}, u32[]{:S(2)}, u32[]{:S(2)}) collective-permute-start(bf16[128,1024]{1,0:T(8,128)(2,1)S(1)} %fusion.13), channel_id=1, source_target_pairs={{0,8},{1,9},{2,10},{3,11},{4,12},{5,13},{6,14},{7,15},{8,24},{9,25... | collective-permute-start | bytes 786440 | tf_op jit(solution)/shard_map/ppermute | solution.py:335
  120.1 9.3 %collective-permute-start.29 = (bf16[128,1024]{1,0:T(8,128)(2,1)S(1)}, bf16[128,1024]{1,0:T(8,128)(2,1)S(1)}, u32[]{:S(2)}, u32[]{:S(2)}) collective-permute-start(bf16[128,1024]{1,0:T(8,128)(2,1)S(1)} %fusion.17), channel_id=1, source_target_pairs={{0,4},{1,5},{2,3},{3,2},{4,0},{5,1},{6,7},{7,6},{8,12},{9,13},{10,... | collective-permute-start | bytes 786440 | tf_op jit(solution)/shard_map/ppermute | solution.py:335
  129.5 7.7 %collective-permute-start.31 = (bf16[128,1024]{1,0:T(8,128)(2,1)S(1)}, bf16[128,1024]{1,0:T(8,128)(2,1)S(1)}, u32[]{:S(2)}, u32[]{:S(2)}) collective-permute-start(bf16[128,1024]{1,0:T(8,128)(2,1)S(1)} %fusion.5), channel_id=1, source_target_pairs={{0,8},{1,9},{2,10},{3,11},{4,12},{5,13},{6,14},{7,15},{8,24},{9,25... | collective-permute-start | bytes 786440 | tf_op jit(solution)/shard_map/ppermute | solution.py:335
  131.7 6.4 %collective-permute-start.27 = (bf16[128,1024]{1,0:T(8,128)(2,1)S(1)}, bf16[128,1024]{1,0:T(8,128)(2,1)S(1)}, u32[]{:S(2)}, u32[]{:S(2)}) collective-permute-start(bf16[128,1024]{1,0:T(8,128)(2,1)S(1)} %fusion.16), channel_id=1, source_target_pairs={{0,4},{1,5},{2,3},{3,2},{4,0},{5,1},{6,7},{7,6},{8,12},{9,13},{10,... | collective-permute-start | bytes 786440 | tf_op jit(solution)/shard_map/ppermute | solution.py:335
  138.2 7.6 %collective-permute-start.33 = (bf16[128,1024]{1,0:T(8,128)(2,1)S(1)}, bf16[128,1024]{1,0:T(8,128)(2,1)S(1)}, u32[]{:S(2)}, u32[]{:S(2)}) collective-permute-start(bf16[128,1024]{1,0:T(8,128)(2,1)S(1)} %fusion.8), channel_id=1, source_target_pairs={{0,8},{1,9},{2,10},{3,11},{4,12},{5,13},{6,14},{7,15},{8,24},{9,25... | collective-permute-start | bytes 786440 | tf_op jit(solution)/shard_map/ppermute | solution.py:335
  139.2 6.4 %collective-permute-start.32 = (bf16[128,1024]{1,0:T(8,128)(2,1)S(1)}, bf16[128,1024]{1,0:T(8,128)(2,1)S(1)}, u32[]{:S(2)}, u32[]{:S(2)}) collective-permute-start(bf16[128,1024]{1,0:T(8,128)(2,1)S(1)} %fusion.15), channel_id=1, source_target_pairs={{0,4},{1,5},{2,3},{3,2},{4,0},{5,1},{6,7},{7,6},{8,12},{9,13},{10,... | collective-permute-start | bytes 786440 | tf_op jit(solution)/shard_map/ppermute | solution.py:335

commit v10 on v9

--- a/solution.py
+++ b/solution.py
@@ -383,35 +383,37 @@
         for key in [key for key in ring_sends if source_of(key, True) in have][:1]:
             came[key] = to_ring(have[source_of(key, True)])
             ring_sends.remove(key)
-        ready, waiting, before = waiting, None, parts
+        ready, waiting = waiting, placed(*parts) if parts is not None else None
+        parts = None
         if picked is not None:
             mine, theirs, picks = picked
             near, far, *kept = run_experts(done, chunks, mine, to_core(theirs), weights, kept)
             parts, picked = (picks, near, far), None
             done += 1
-        else:
-            parts = None
-        if before is not None:
-            waiting = placed(*before)
         if plane_sends and all((kind, done) in have for kind in "sfab"):
             picked = pick_rows(place, [have[kind, done] for kind in "sfab"], top, rows, pair_slots)
+            if done == 0:
+                mine, theirs, picks = picked
+                near, far, *kept = run_experts(done, chunks, mine, to_core(theirs), weights, kept)
+                parts, picked = (picks, near, far), None
+                done += 1
         if ready is not None:
-            late.append(ready)
+            keep, send = ready
+            late.append((keep, to_second(send)))
         needed = {key: have[key] for key in have if key[1] >= done}
-        came, have, picked, parts, waiting, late, weights = lax.optimization_barrier(
-            (came, needed, picked, parts, waiting, late, weights)
+        order_of = sorted(came, key=lambda key: key[0] != "s")
+        values, have, picked, parts, waiting, late, weights = lax.optimization_barrier(
+            ([came[key] for key in order_of], needed, picked, parts, waiting, late, weights)
         )
+        came = dict(zip(order_of, values))
         have.update(came)
     mine, theirs, picks = pick_rows(place, [have[kind, done] for kind in "sfab"], top, rows, pair_slots)
-    unsent, late = late, []
     if waiting is not None:
         keep, send = waiting
         late.append((keep, to_second(tied(send, theirs))))
-    beside = theirs
     if parts is not None:
-        keep, beside = placed(*tied(parts, theirs))
-        late.append((keep, to_second(beside)))
-    late = [(keep, to_second(tied(send, beside))) for keep, send in unsent] + late
+        keep, send = placed(*tied(parts, theirs))
+        late.append((keep, to_second(send)))
     near, far, *kept = run_experts(done, chunks, mine, to_core(theirs), weights, kept)
     keep, send = placed(picks, near, far)
     late.append((keep, to_second(send)))

time: 147 us -> 149 us (1.014)
    unnamed x18 -> x16, local copies, waits for them, and re-layouts: 5.16 us -> 4.7 us
  transfers between devices with their start and end apart: 34 -> 34, of which waited for: 18 -> 19; matrix products, arithmetic and copies ran while one was open for 8% -> 8% of each run, Pallas kernels for 24% -> 22%
where the time goes in v10:
time: 149 us
  waiting for transfers between devices  59.2 us (40%)
  Pallas kernels  38.5 us (26%)
  starting transfers between devices  33.4 us (22%)
  matrix products  10.2 us (7%)
  local copies, waits for them, and re-layouts  4.83 us (3%)
  other arithmetic  1.71 us (1%)
    ppermute x34, waiting for transfers between devices, permute(): return lax.ppermute(value, ('expert', 'etp'), pairs)  59.2 us
    ppermute x34, starting transfers between devices, permute(): return lax.ppermute(value, ('expert', 'etp'), pairs)  33.4 us
    pallas_call x4, Pallas kernels, run_experts(): pl.pallas_call(functools.partial(expert_kernel, index, kept is not None),...  19.7 us
    pallas_call x4, Pallas kernels, pick_rows(): pl.pallas_call(functools.partial(pick_kernel, top, rows), in_specs=[pl.Bl...  7.24 us
    pallas_call x4, Pallas kernels, place_rows(): pl.pallas_call(place_kernel, in_specs=[pl.BlockSpec(memory_space=pltpu.SM...  5.08 us
    unnamed x16, local copies, waits for them, and re-layouts  4.7 us
    pallas_call x1, Pallas kernels, load_weights(): pl.pallas_call(load_kernel, in_specs=[pl.BlockSpec(memory_space=pltpu.HBM...  4.62 us
    dot_general x1, matrix products, gather_body(): lax.dot_general(gate_term, rows_x, CONTRACT_FIRST, preferred_element_type...  3.42 us
  transfers between devices with their start and end apart: 34, of which 19 were waited for; matrix products, arithmetic and copies ran while one was open for 8% of the time, Pallas kernels for 22%

profile of v10, /device:TPU:0, one launch (start us, length us, event | category | flops | bytes accessed | tf_op | source)
XLA Modules:
  0.0 148.9 jit_solution(13343379859390711730)
XLA Ops:
  0.6 1.9 %pack.1.refs_0_ = bf16[272,1024]{1,0:T(8,128)(2,1)} custom-call(bf16[128,1024]{1,0:T(8,128)(2,1)} %tokens_ref.1, bf16[128,1024]{1,0:T(8,128)(2,1)} %grads_ref.1, s32[8,128]{1,0:T(8,128)} %bitcast.61, f32[8,128]{1,0:T(8,128)} %bitcast.62), custom_call_target="tpu_custom_call" | custom-call | tf_op jit(solution)/shard_map/pack/pallas_call | solution.py:128
  2.5 2.9 %collective-permute-start.2 = (bf16[272,1024]{1,0:T(8,128)(2,1)}, bf16[272,1024]{1,0:T(8,128)(2,1)S(1)}, u32[]{:S(2)}, u32[]{:S(2)}) collective-permute-start(bf16[272,1024]{1,0:T(8,128)(2,1)} %pack.1.refs_0_), channel_id=1, source_target_pairs={{0,1},{1,0},{2,6},{3,7},{4,5},{5,4},{6,2},{7,3},{8,9},{9,8},{10,14... | collective-permute-start | bytes 1671176 | tf_op jit(solution)/shard_map/ppermute | solution.py:335
  5.5 1.5 %collective-permute-start.1 = (bf16[272,1024]{1,0:T(8,128)(2,1)}, bf16[272,1024]{1,0:T(8,128)(2,1)}, u32[]{:S(2)}, u32[]{:S(2)}) collective-permute-start(bf16[272,1024]{1,0:T(8,128)(2,1)} %pack.1.refs_0_), channel_id=1, source_target_pairs={{0,4},{1,5},{2,3},{3,2},{4,0},{5,1},{6,7},{7,6},{8,12},{9,13},{10,... | collective-permute-start | bytes 1671176 | tf_op jit(solution)/shard_map/ppermute | solution.py:335
  7.0 1.6 %collective-permute-start = (bf16[272,1024]{1,0:T(8,128)(2,1)}, bf16[272,1024]{1,0:T(8,128)(2,1)S(1)}, u32[]{:S(2)}, u32[]{:S(2)}) collective-permute-start(bf16[272,1024]{1,0:T(8,128)(2,1)} %pack.1.refs_0_), channel_id=1, source_target_pairs={{0,8},{1,9},{2,10},{3,11},{4,12},{5,13},{6,14},{7,15},{8,24},{9,25... | collective-permute-start | bytes 1671176 | tf_op jit(solution)/shard_map/ppermute | solution.py:335
  8.6 4.6 %load.1 = (bf16[384,2048]{1,0:T(8,128)(2,1)}, bf16[384,2048]{1,0:T(8,128)(2,1)}, bf16[384,2048]{1,0:T(8,128)(2,1)}) custom-call(bf16[384,2048]{1,0:T(8,128)(2,1)} %bitcast.58, bf16[384,2048]{1,0:T(8,128)(2,1)} %bitcast.59, bf16[384,2048]{1,0:T(8,128)(2,1)} %bitcast.60), custom_call_target="tpu_custom_call" | custom-call | tf_op jit(solution)/shard_map/load/pallas_call | solution.py:147
  13.2 5.5 %collective-permute-done.2.refs_2_ = bf16[272,1024]{1,0:T(8,128)(2,1)S(1)} collective-permute-done((bf16[272,1024]{1,0:T(8,128)(2,1)}, bf16[272,1024]{1,0:T(8,128)(2,1)S(1)}, u32[]{:S(2)}, u32[]{:S(2)}) %collective-permute-start.2) | collective-permute-done | bytes 557088 | tf_op jit(solution)/shard_map/ppermute | solution.py:335
  19.5 2.4 %collective-permute-done.refs_0_ = bf16[272,1024]{1,0:T(8,128)(2,1)S(1)} collective-permute-done((bf16[272,1024]{1,0:T(8,128)(2,1)}, bf16[272,1024]{1,0:T(8,128)(2,1)S(1)}, u32[]{:S(2)}, u32[]{:S(2)}) %collective-permute-start) | collective-permute-done | bytes 557088 | tf_op jit(solution)/shard_map/ppermute | solution.py:335
  22.9 1.3 collective-permute-start.3
  24.3 10.9 %collective-permute-done.4.refs_3_ = bf16[272,1024]{1,0:T(8,128)(2,1)} collective-permute-done((bf16[272,1024]{1,0:T(8,128)(2,1)}, bf16[272,1024]{1,0:T(8,128)(2,1)}, u32[]{:S(2)}, u32[]{:S(2)}) %collective-permute-start.4) | collective-permute-done | bytes 557088 | tf_op jit(solution)/shard_map/ppermute | solution.py:335
  35.2 1.3 collective-permute-done.3.refs_0_
  37.5 2.2 %pick.4 = (bf16[2,144,2048]{2,1,0:T(8,128)(2,1)S(1)}, bf16[2,144,2048]{2,1,0:T(8,128)(2,1)S(1)}, bf16[288,256]{1,0:T(8,128)(2,1)S(1)}) custom-call(s32[3]{0:T(128)S(1)} %pad_add_fusion.place_ref, bf16[272,1024]{1,0:T(8,128)(2,1)S(1)} %copy-done.5, bf16[272,1024]{1,0:T(8,128)(2,1)} %collective-permute-done.1.refs_1_, bf16[272,1024]{1,0:T(8,128)(2,1)S(1)} %copy-done.7, ...), custom_call_target="tpu_custom_call" | custom-call | tf_op jit(solution)/shard_map/pick/pallas_call | solution.py:271
  39.8 1.3 collective-permute-start.6
  42.7 1.4 copy-done.1
  44.1 1.4 copy-done.3
  45.5 4.8 %experts.4 = (bf16[144,2048]{1,0:T(8,128)(2,1)S(1)}, bf16[144,2048]{1,0:T(8,128)(2,1)S(1)}, bf16[1152,2048]{1,0:T(8,128)(2,1)S(1)}, bf16[1152,2048]{1,0:T(8,128)...) custom-call(bf16[2,144,2048]{2,1,0:T(8,128)(2,1)S(1)} %get-tuple-element.158., ...), custom_call_target="tpu_custom_call" | custom-call | tf_op jit(solution)/shard_map/experts/pallas_call | solution.py:290
  50.4 7.0 %collective-permute-done.8.refs_1_ = bf16[272,1024]{1,0:T(8,128)(2,1)S(1)} collective-permute-done((bf16[272,1024]{1,0:T(8,128)(2,1)}, bf16[272,1024]{1,0:T(8,128)(2,1)S(1)}, u32[]{:S(2)}, u32[]{:S(2)}) %collective-permute-start.8) | collective-permute-done | bytes 557088 | tf_op jit(solution)/shard_map/ppermute | solution.py:335
  60.3 2.0 %pick.5 = (bf16[2,144,2048]{2,1,0:T(8,128)(2,1)S(1)}, bf16[2,144,2048]{2,1,0:T(8,128)(2,1)S(1)}, bf16[288,256]{1,0:T(8,128)(2,1)S(1)}) custom-call(s32[3]{0:T(128)S(1)} %pad_add_fusion.place_ref, bf16[272,1024]{1,0:T(8,128)(2,1)S(1)} %collective-permute-done.refs_0_, bf16[272,1024]{1,0:T(8,128)(2,1)} %collective-permute-done.5.refs_1_, ...), custom_call_target="tpu_custom_call" | custom-call | tf_op jit(solution)/shard_map/pick/pallas_call | solution.py:271
  62.4 1.3 place.4
  63.7 3.3 %collective-permute-done.12.refs_3_ = bf16[272,1024]{1,0:T(8,128)(2,1)S(1)} collective-permute-done((bf16[272,1024]{1,0:T(8,128)(2,1)S(1)}, bf16[272,1024]{1,0:T(8,128)(2,1)S(1)}, u32[]{:S(2)}, u32[]{:S(2)}) %collective-permute-start.12) | collective-permute-done | bytes 557088 | tf_op jit(solution)/shard_map/ppermute | solution.py:335
  66.9 6.0 %collective-permute-done.11.refs_2_ = bf16[272,1024]{1,0:T(8,128)(2,1)S(1)} collective-permute-done((bf16[272,1024]{1,0:T(8,128)(2,1)S(1)}, bf16[272,1024]{1,0:T(8,128)(2,1)S(1)}, u32[]{:S(2)}, u32[]{:S(2)}) %collective-permute-start.11) | collective-permute-done | bytes 557088 | tf_op jit(solution)/shard_map/ppermute | solution.py:335
  72.9 1.9 %collective-permute-done.10.refs_0_ = bf16[272,1024]{1,0:T(8,128)(2,1)S(1)} collective-permute-done((bf16[272,1024]{1,0:T(8,128)(2,1)S(1)}, bf16[272,1024]{1,0:T(8,128)(2,1)S(1)}, u32[]{:S(2)}, u32[]{:S(2)}) %collective-permute-start.10) | collective-permute-done | bytes 557088 | tf_op jit(solution)/shard_map/ppermute | solution.py:335
  77.6 1.5 %pick.6 = (bf16[2,144,2048]{2,1,0:T(8,128)(2,1)S(1)}, bf16[2,144,2048]{2,1,0:T(8,128)(2,1)S(1)}, bf16[288,256]{1,0:T(8,128)(2,1)S(1)}) custom-call(s32[3]{0:T(128)S(1)} %pad_add_fusion.place_ref, bf16[272,1024]{1,0:T(8,128)(2,1)S(1)} %collective-permute-done.3.refs_0_, bf16[272,1024]{1,0:T(8,128)(2,1)S(1)} %collective-permute-done.8.refs_1_, ...), custom_call_target="tpu_custom_call" | custom-call | tf_op jit(solution)/shard_map/pick/pallas_call | solution.py:271
  79.2 5.1 %experts.5 = (bf16[144,2048]{1,0:T(8,128)(2,1)S(1)}, bf16[144,2048]{1,0:T(8,128)(2,1)S(1)}, bf16[1152,2048]{1,0:T(8,128)(2,1)S(1)}, bf16[1152,2048]{1,0:T(8,128)...) custom-call(bf16[2,144,2048]{2,1,0:T(8,128)(2,1)S(1)} %get-tuple-ele, ...), custom_call_target="tpu_custom_call", output_to_operand_aliasing={{2}: (5, {}), {3}: (6, {}), {4}: (7, {}), {5}: (8, {}), {6}... | custom-call | tf_op jit(solution)/shard_map/experts/pallas_call | solution.py:290
  84.2 5.7 %collective-permute-done.17 = bf16[2,128,1024]{2,1,0:T(8,128)(2,1)S(1)} collective-permute-done((bf16[2,128,1024]{2,1,0:T(8,128)(2,1)S(1)}, bf16[2,128,1024]{2,1,0:T(8,128)(2,1)S(1)}, u32[]{:S(2)}, u32[]{:S(2)}) %collective-permute-start.17) | collective-permute-done | bytes 524320 | tf_op jit(solution)/shard_map/ppermute | solution.py:335
  91.3 1.2 collective-permute-start.18
  92.5 2.0 %collective-permute-done.20.far_ref = bf16[144,2048]{1,0:T(8,128)(2,1)S(1)} collective-permute-done((bf16[144,2048]{1,0:T(8,128)(2,1)S(1)}, bf16[144,2048]{1,0:T(8,128)(2,1)S(1)}, u32[]{:S(2)}, u32[]{:S(2)}) %collective-permute-start.20) | collective-permute-done | bytes 589856 | tf_op jit(solution)/shard_map/ppermute | solution.py:335
  94.5 1.3 place.5
  95.8 4.9 %experts.6 = (bf16[144,2048]{1,0:T(8,128)(2,1)S(1)}, bf16[144,2048]{1,0:T(8,128)(2,1)S(1)}, bf16[1152,2048]{1,0:T(8,128)(2,1)S(1)}, bf16[1152,2048]{1,0:T(8,128)...) custom-call(bf16[2,144,2048]{2,1,0:T(8,128)(2,1)S(1)} %get-tuple-ele, ...), custom_call_target="tpu_custom_call", output_to_operand_aliasing={{2}: (5, {}), {3}: (6, {}), {4}: (7, {}), {5}: (8, {}), {6}... | custom-call | tf_op jit(solution)/shard_map/experts/pallas_call | solution.py:290
  100.8 1.5 %pick.7 = (bf16[2,144,2048]{2,1,0:T(8,128)(2,1)S(1)}, bf16[2,144,2048]{2,1,0:T(8,128)(2,1)S(1)}, bf16[288,256]{1,0:T(8,128)(2,1)S(1)}) custom-call(s32[3]{0:T(128)S(1)} %pad_add_fusion.place_ref, bf16[272,1024]{1,0:T(8,128)(2,1)S(1)} %collective-permute-done.10.refs_0_, bf16[272,1024]{1,0:T(8,128)(2,1)S(1)} %collective-permute-done.15.refs_1_, ...), custom_call_target="tpu_custom_call" | custom-call | tf_op jit(solution)/shard_map/pick/pallas_call | solution.py:271
  102.9 1.2 collective-permute-start.21
  104.1 2.0 %collective-permute-done.27.far_ref = bf16[144,2048]{1,0:T(8,128)(2,1)S(1)} collective-permute-done((bf16[144,2048]{1,0:T(8,128)(2,1)S(1)}, bf16[144,2048]{1,0:T(8,128)(2,1)S(1)}, u32[]{:S(2)}, u32[]{:S(2)}) %collective-permute-start.27) | collective-permute-done | bytes 589856 | tf_op jit(solution)/shard_map/ppermute | solution.py:335
  106.1 1.3 place.7
  107.4 1.3 collective-permute-start.28
  108.7 4.9 %experts.7 = (bf16[144,2048]{1,0:T(8,128)(2,1)S(1)}, bf16[144,2048]{1,0:T(8,128)(2,1)S(1)}, bf16[1152,2048]{1,0:T(8,128)(2,1)S(1)}, bf16[1152,2048]{1,0:T(8,128)...) custom-call(bf16[2,144,2048]{2,1,0:T(8,128)(2,1)S(1)} %get-tuple-ele, ...), custom_call_target="tpu_custom_call", output_to_operand_aliasing={{2}: (5, {}), {3}: (6, {}), {4}: (7, {}), {5}: (8, {}), {6}... | custom-call | tf_op jit(solution)/shard_map/experts/pallas_call | solution.py:290
  114.2 1.2 collective-permute-start.23
  115.6 1.3 place.6
  116.9 1.1 collective-permute-start.25
  118.0 3.2 %collective-permute-done.23 = bf16[128,1024]{1,0:T(8,128)(2,1)S(1)} collective-permute-done((bf16[128,1024]{1,0:T(8,128)(2,1)S(1)}, bf16[128,1024]{1,0:T(8,128)(2,1)S(1)}, u32[]{:S(2)}, u32[]{:S(2)}) %collective-permute-start.23) | collective-permute-done | bytes 262176 | tf_op jit(solution)/shard_map/ppermute | solution.py:335
  122.5 1.1 collective-permute-start.29
  123.6 3.4 %fusion = bf16[1,384,2048]{2,1,0:T(8,128)(2,1)} fusion(bf16[1152,384]{1,0:T(8,128)(2,1)S(1)} %get-tuple-element.271, bf16[1152,2048]{1,0:T(8,128)(2,1)S(1)} %get-tuple-element.272), kind=kOutput, calls=%fused_computation.3 | convolution fusion | flops 1812725760 | bytes 7176192 | tf_op jit(solution)/shard_map/dot_general | solution.py:440
  127.0 3.4 %fusion.1 = bf16[1,384,2048]{2,1,0:T(8,128)(2,1)} fusion(bf16[1152,384]{1,0:T(8,128)(2,1)S(1)} %get-tuple-element.273, bf16[1152,2048]{1,0:T(8,128)(2,1)S(1)} %get-tuple-element.272), kind=kOutput, calls=%fused_computation.4 | convolution fusion | flops 1812725760 | bytes 7176192 | tf_op jit(solution)/shard_map/dot_general | solution.py:441
  130.6 3.4 %collective-permute-start.31 = (bf16[128,1024]{1,0:T(8,128)(2,1)S(1)}, bf16[128,1024]{1,0:T(8,128)(2,1)S(1)}, u32[]{:S(2)}, u32[]{:S(2)}) collective-permute-start(bf16[128,1024]{1,0:T(8,128)(2,1)S(1)} %fusion.5), channel_id=1, source_target_pairs={{0,8},{1,9},{2,10},{3,11},{4,12},{5,13},{6,14},{7,15},{8,24},{9,25... | collective-permute-start | bytes 786440 | tf_op jit(solution)/shard_map/ppermute | solution.py:335
  134.2 1.1 collective-permute-start.26
  135.5 3.4 %collective-permute-done.31 = bf16[128,1024]{1,0:T(8,128)(2,1)S(1)} collective-permute-done((bf16[128,1024]{1,0:T(8,128)(2,1)S(1)}, bf16[128,1024]{1,0:T(8,128)(2,1)S(1)}, u32[]{:S(2)}, u32[]{:S(2)}) %collective-permute-start.31) | collective-permute-done | bytes 262176 | tf_op jit(solution)/shard_map/ppermute | solution.py:335
  138.9 1.8 %collective-permute-done.26 = bf16[128,1024]{1,0:T(8,128)(2,1)S(1)} collective-permute-done((bf16[128,1024]{1,0:T(8,128)(2,1)S(1)}, bf16[128,1024]{1,0:T(8,128)(2,1)S(1)}, u32[]{:S(2)}, u32[]{:S(2)}) %collective-permute-start.26) | collective-permute-done | bytes 262176 | tf_op jit(solution)/shard_map/ppermute | solution.py:335
  141.5 1.5 %collective-permute-start.32 = (bf16[128,1024]{1,0:T(8,128)(2,1)S(1)}, bf16[128,1024]{1,0:T(8,128)(2,1)S(1)}, u32[]{:S(2)}, u32[]{:S(2)}) collective-permute-start(bf16[128,1024]{1,0:T(8,128)(2,1)S(1)} %fusion.15), channel_id=1, source_target_pairs={{0,4},{1,5},{2,3},{3,2},{4,0},{5,1},{6,7},{7,6},{8,12},{9,13},{10,... | collective-permute-start | bytes 786440 | tf_op jit(solution)/shard_map/ppermute | solution.py:335
  143.1 3.4 %fusion.2 = bf16[1,384,2048]{2,1,0:T(8,128)(2,1)} fusion(bf16[1152,384]{1,0:T(8,128)(2,1)S(1)} %get-tuple-element.274, bf16[1152,2048]{1,0:T(8,128)(2,1)S(1)} %get-tuple-element.275), kind=kOutput, calls=%fused_computation.5 | convolution fusion | flops 1812725760 | bytes 7176192 | tf_op jit(solution)/shard_map/dot_general | solution.py:439
  146.5 1.4 collective-permute-done.32
  (66 shorter events, 16.8 us)
Async XLA Ops:
  2.5 16.2 %collective-permute-start.2 = (bf16[272,1024]{1,0:T(8,128)(2,1)}, bf16[272,1024]{1,0:T(8,128)(2,1)S(1)}, u32[]{:S(2)}, u32[]{:S(2)}) collective-permute-start(bf16[272,1024]{1,0:T(8,128)(2,1)} %pack.1.refs_0_), channel_id=1, source_target_pairs={{0,1},{1,0},{2,6},{3,7},{4,5},{5,4},{6,2},{7,3},{8,9},{9,8},{10,14... | collective-permute-start | bytes 1671176 | tf_op jit(solution)/shard_map/ppermute | solution.py:335
  5.5 14.0 %collective-permute-start.1 = (bf16[272,1024]{1,0:T(8,128)(2,1)}, bf16[272,1024]{1,0:T(8,128)(2,1)}, u32[]{:S(2)}, u32[]{:S(2)}) collective-permute-start(bf16[272,1024]{1,0:T(8,128)(2,1)} %pack.1.refs_0_), channel_id=1, source_target_pairs={{0,4},{1,5},{2,3},{3,2},{4,0},{5,1},{6,7},{7,6},{8,12},{9,13},{10,... | collective-permute-start | bytes 1671176 | tf_op jit(solution)/shard_map/ppermute | solution.py:335
  7.0 14.9 %collective-permute-start = (bf16[272,1024]{1,0:T(8,128)(2,1)}, bf16[272,1024]{1,0:T(8,128)(2,1)S(1)}, u32[]{:S(2)}, u32[]{:S(2)}) collective-permute-start(bf16[272,1024]{1,0:T(8,128)(2,1)} %pack.1.refs_0_), channel_id=1, source_target_pairs={{0,8},{1,9},{2,10},{3,11},{4,12},{5,13},{6,14},{7,15},{8,24},{9,25... | collective-permute-start | bytes 1671176 | tf_op jit(solution)/shard_map/ppermute | solution.py:335
  8.6 27.9 %copy-start.5 = (bf16[272,1024]{1,0:T(8,128)(2,1)S(1)}, bf16[272,1024]{1,0:T(8,128)(2,1)}, u32[]{:S(2)}) copy-start(bf16[272,1024]{1,0:T(8,128)(2,1)} %pack.1.refs_0_) | copy-start | bytes 1671172
  13.2 29.5 %copy-start = (bf16[384,2048]{1,0:T(8,128)(2,1)S(1)}, bf16[384,2048]{1,0:T(8,128)(2,1)}, u32[]{:S(2)}) copy-start(bf16[384,2048]{1,0:T(8,128)(2,1)} %get-tuple-element.239.wg_ref) | copy-start | bytes 4718596
  18.7 0.8 copy-start.6
  21.9 13.2 %collective-permute-start.4 = (bf16[272,1024]{1,0:T(8,128)(2,1)}, bf16[272,1024]{1,0:T(8,128)(2,1)}, u32[]{:S(2)}, u32[]{:S(2)}) collective-permute-start(bf16[272,1024]{1,0:T(8,128)(2,1)} %collective-permute-done.1.refs_1_), channel_id=1, source_target_pairs={{0,1},{1,0},{2,6},{3,7},{4,5},{5,4},{6,2},{7,3},{8,9},{9,8},{10,14... | collective-permute-start | bytes 1671176 | tf_op jit(solution)/shard_map/ppermute | solution.py:335
  22.5 12.7 %collective-permute-start.5 = (bf16[272,1024]{1,0:T(8,128)(2,1)S(1)}, bf16[272,1024]{1,0:T(8,128)(2,1)}, u32[]{:S(2)}, u32[]{:S(2)}) collective-permute-start(bf16[272,1024]{1,0:T(8,128)(2,1)S(1)} %collective-permute-done.refs_0_), channel_id=1, source_target_pairs={{0,4},{1,5},{2,3},{3,2},{4,0},{5,1},{6,7},{7,6},{8,12},{9,13},{10,... | collective-permute-start | bytes 1671176 | tf_op jit(solution)/shard_map/ppermute | solution.py:335
  22.9 13.5 %collective-permute-start.3 = (bf16[272,1024]{1,0:T(8,128)(2,1)S(1)}, bf16[272,1024]{1,0:T(8,128)(2,1)S(1)}, u32[]{:S(2)}, u32[]{:S(2)}) collective-permute-start(bf16[272,1024]{1,0:T(8,128)(2,1)S(1)} %collective-permute-done.refs_0_), channel_id=1, source_target_pairs={{0,8},{1,9},{2,10},{3,11},{4,12},{5,13},{6,14},{7,15},{8,24},{9,25... | collective-permute-start | bytes 1671176 | tf_op jit(solution)/shard_map/ppermute | solution.py:335
  36.5 1.1 copy-start.7
  39.7 3.0 %collective-permute-start.9 = (bf16[2,144,2048]{2,1,0:T(8,128)(2,1)S(1)}, bf16[2,144,2048]{2,1,0:T(8,128)(2,1)S(1)}, u32[]{:S(2)}, u32[]{:S(2)}) collective-permute-start(bf16[2,144,2048]{2,1,0:T(8,128)(2,1)S(1)} %get-tuple-element.159), channel_id=1, source_target_pairs={{0,2},{1,3},{2,0},{3,1},{4,6},{5,7},{6,4},{7,5},{8,10},{9,11},{10,... | collective-permute-start | bytes 3538952 | tf_op jit(solution)/shard_map/ppermute | solution.py:335
  39.8 10.6 %collective-permute-start.6 = (bf16[272,1024]{1,0:T(8,128)(2,1)S(1)}, bf16[272,1024]{1,0:T(8,128)(2,1)S(1)}, u32[]{:S(2)}, u32[]{:S(2)}) collective-permute-start(bf16[272,1024]{1,0:T(8,128)(2,1)S(1)} %collective-permute-done.refs_0_), channel_id=1, source_target_pairs={{0,1},{1,0},{2,6},{3,7},{4,5},{5,4},{6,2},{7,3},{8,9},{9,8},{10,14... | collective-permute-start | bytes 1671176 | tf_op jit(solution)/shard_map/ppermute | solution.py:335
  41.1 16.3 %collective-permute-start.8 = (bf16[272,1024]{1,0:T(8,128)(2,1)}, bf16[272,1024]{1,0:T(8,128)(2,1)S(1)}, u32[]{:S(2)}, u32[]{:S(2)}) collective-permute-start(bf16[272,1024]{1,0:T(8,128)(2,1)} %collective-permute-done.5.refs_1_), channel_id=1, source_target_pairs={{0,8},{1,9},{2,10},{3,11},{4,12},{5,13},{6,14},{7,15},{8,24},{9,25... | collective-permute-start | bytes 1671176 | tf_op jit(solution)/shard_map/ppermute | solution.py:335
  41.9 15.6 %collective-permute-start.7 = (bf16[272,1024]{1,0:T(8,128)(2,1)}, bf16[272,1024]{1,0:T(8,128)(2,1)S(1)}, u32[]{:S(2)}, u32[]{:S(2)}) collective-permute-start(bf16[272,1024]{1,0:T(8,128)(2,1)} %collective-permute-done.5.refs_1_), channel_id=1, source_target_pairs={{0,1},{1,0},{2,6},{3,7},{4,5},{5,4},{6,2},{7,3},{8,9},{9,8},{10,14... | collective-permute-start | bytes 1671176 | tf_op jit(solution)/shard_map/ppermute | solution.py:335
  42.7 1.4 copy-start.1
  44.1 1.4 copy-start.3
  57.4 5.0 %collective-permute-start.13 = (bf16[144,2048]{1,0:T(8,128)(2,1)S(1)}, bf16[144,2048]{1,0:T(8,128)(2,1)S(1)}, u32[]{:S(2)}, u32[]{:S(2)}) collective-permute-start(bf16[144,2048]{1,0:T(8,128)(2,1)S(1)} %get-tuple-element.176), channel_id=1, source_target_pairs={{0,2},{1,3},{2,0},{3,1},{4,6},{5,7},{6,4},{7,5},{8,10},{9,11},{10,... | collective-permute-start | bytes 1769480 | tf_op jit(solution)/shard_map/ppermute | solution.py:335
  57.4 9.5 %collective-permute-start.12 = (bf16[272,1024]{1,0:T(8,128)(2,1)S(1)}, bf16[272,1024]{1,0:T(8,128)(2,1)S(1)}, u32[]{:S(2)}, u32[]{:S(2)}) collective-permute-start(bf16[272,1024]{1,0:T(8,128)(2,1)S(1)} %collective-permute-done.8.refs_1_), channel_id=1, source_target_pairs={{0,1},{1,0},{2,6},{3,7},{4,5},{5,4},{6,2},{7,3},{8,9},{9,8},{10,14... | collective-permute-start | bytes 1671176 | tf_op jit(solution)/shard_map/ppermute | solution.py:335
  58.5 14.5 %collective-permute-start.11 = (bf16[272,1024]{1,0:T(8,128)(2,1)S(1)}, bf16[272,1024]{1,0:T(8,128)(2,1)S(1)}, u32[]{:S(2)}, u32[]{:S(2)}) collective-permute-start(bf16[272,1024]{1,0:T(8,128)(2,1)S(1)} %collective-permute-done.3.refs_0_), channel_id=1, source_target_pairs={{0,1},{1,0},{2,6},{3,7},{4,5},{5,4},{6,2},{7,3},{8,9},{9,8},{10,14... | collective-permute-start | bytes 1671176 | tf_op jit(solution)/shard_map/ppermute | solution.py:335
  59.4 15.4 %collective-permute-start.10 = (bf16[272,1024]{1,0:T(8,128)(2,1)S(1)}, bf16[272,1024]{1,0:T(8,128)(2,1)S(1)}, u32[]{:S(2)}, u32[]{:S(2)}) collective-permute-start(bf16[272,1024]{1,0:T(8,128)(2,1)S(1)} %collective-permute-done.3.refs_0_), channel_id=1, source_target_pairs={{0,8},{1,9},{2,10},{3,11},{4,12},{5,13},{6,14},{7,15},{8,24},{9,25... | collective-permute-start | bytes 1671176 | tf_op jit(solution)/shard_map/ppermute | solution.py:335
  62.4 16.8 %copy-start.2 = (bf16[384,2048]{1,0:T(8,128)(2,1)S(1)}, bf16[384,2048]{1,0:T(8,128)(2,1)}, u32[]{:S(2)}) copy-start(bf16[384,2048]{1,0:T(8,128)(2,1)} %get-tuple-element.240.wu_ref) | copy-start | bytes 4718596
  62.4 16.8 %copy-start.4 = (bf16[384,2048]{1,0:T(8,128)(2,1)S(1)}, bf16[384,2048]{1,0:T(8,128)(2,1)}, u32[]{:S(2)}) copy-start(bf16[384,2048]{1,0:T(8,128)(2,1)} %get-tuple-element.241.wd_ref) | copy-start | bytes 4718596
  74.8 4.3 %collective-permute-start.16 = (bf16[2,144,2048]{2,1,0:T(8,128)(2,1)S(1)}, bf16[2,144,2048]{2,1,0:T(8,128)(2,1)S(1)}, u32[]{:S(2)}, u32[]{:S(2)}) collective-permute-start(bf16[2,144,2048]{2,1,0:T(8,128)(2,1)S(1)} %get-tuple-element.192), channel_id=1, source_target_pairs={{0,2},{1,3},{2,0},{3,1},{4,6},{5,7},{6,4},{7,5},{8,10},{9,11},{10,... | collective-permute-start | bytes 3538952 | tf_op jit(solution)/shard_map/ppermute | solution.py:335
  74.8 15.2 %collective-permute-start.14 = (bf16[272,1024]{1,0:T(8,128)(2,1)S(1)}, bf16[272,1024]{1,0:T(8,128)(2,1)S(1)}, u32[]{:S(2)}, u32[]{:S(2)}) collective-permute-start(bf16[272,1024]{1,0:T(8,128)(2,1)S(1)} %collective-permute-done.10.refs_0_), channel_id=1, source_target_pairs={{0,1},{1,0},{2,6},{3,7},{4,5},{5,4},{6,2},{7,3},{8,9},{9,8},{10,14... | collective-permute-start | bytes 1671176 | tf_op jit(solution)/shard_map/ppermute | solution.py:335
  75.8 15.0 %collective-permute-start.15 = (bf16[272,1024]{1,0:T(8,128)(2,1)S(1)}, bf16[272,1024]{1,0:T(8,128)(2,1)S(1)}, u32[]{:S(2)}, u32[]{:S(2)}) collective-permute-start(bf16[272,1024]{1,0:T(8,128)(2,1)S(1)} %collective-permute-done.8.refs_1_), channel_id=1, source_target_pairs={{0,8},{1,9},{2,10},{3,11},{4,12},{5,13},{6,14},{7,15},{8,24},{9,25... | collective-permute-start | bytes 1671176 | tf_op jit(solution)/shard_map/ppermute | solution.py:335
  76.6 13.4 %collective-permute-start.17 = (bf16[2,128,1024]{2,1,0:T(8,128)(2,1)S(1)}, bf16[2,128,1024]{2,1,0:T(8,128)(2,1)S(1)}, u32[]{:S(2)}, u32[]{:S(2)}) collective-permute-start(bf16[2,128,1024]{2,1,0:T(8,128)(2,1)S(1)} %get-tuple-element.204), channel_id=1, source_target_pairs={{0,1},{1,0},{2,6},{3,7},{4,5},{5,4},{6,2},{7,3},{8,9},{9,8},{10,14... | collective-permute-start | bytes 1572872 | tf_op jit(solution)/shard_map/ppermute | solution.py:335
  90.8 5.0 %collective-permute-start.19 = (bf16[2,144,2048]{2,1,0:T(8,128)(2,1)S(1)}, bf16[2,144,2048]{2,1,0:T(8,128)(2,1)S(1)}, u32[]{:S(2)}, u32[]{:S(2)}) collective-permute-start(bf16[2,144,2048]{2,1,0:T(8,128)(2,1)S(1)} %get-tuple-element.210), channel_id=1, source_target_pairs={{0,2},{1,3},{2,0},{3,1},{4,6},{5,7},{6,4},{7,5},{8,10},{9,11},{10,... | collective-permute-start | bytes 3538952 | tf_op jit(solution)/shard_map/ppermute | solution.py:335
  90.8 3.7 %collective-permute-start.20 = (bf16[144,2048]{1,0:T(8,128)(2,1)S(1)}, bf16[144,2048]{1,0:T(8,128)(2,1)S(1)}, u32[]{:S(2)}, u32[]{:S(2)}) collective-permute-start(bf16[144,2048]{1,0:T(8,128)(2,1)S(1)} %get-tuple-element.223), channel_id=1, source_target_pairs={{0,2},{1,3},{2,0},{3,1},{4,6},{5,7},{6,4},{7,5},{8,10},{9,11},{10,... | collective-permute-start | bytes 1769480 | tf_op jit(solution)/shard_map/ppermute | solution.py:335
  91.3 9.5 %collective-permute-start.18 = (bf16[272,1024]{1,0:T(8,128)(2,1)S(1)}, bf16[272,1024]{1,0:T(8,128)(2,1)S(1)}, u32[]{:S(2)}, u32[]{:S(2)}) collective-permute-start(bf16[272,1024]{1,0:T(8,128)(2,1)S(1)} %collective-permute-done.15.refs_1_), channel_id=1, source_target_pairs={{0,1},{1,0},{2,6},{3,7},{4,5},{5,4},{6,2},{7,3},{8,9},{9,8},{10,14... | collective-permute-start | bytes 1671176 | tf_op jit(solution)/shard_map/ppermute | solution.py:335
  102.4 6.3 %collective-permute-start.22 = (bf16[2,144,2048]{2,1,0:T(8,128)(2,1)S(1)}, bf16[2,144,2048]{2,1,0:T(8,128)(2,1)S(1)}, u32[]{:S(2)}, u32[]{:S(2)}) collective-permute-start(bf16[2,144,2048]{2,1,0:T(8,128)(2,1)S(1)} %get-tuple-element.236), channel_id=1, source_target_pairs={{0,2},{1,3},{2,0},{3,1},{4,6},{5,7},{6,4},{7,5},{8,10},{9,11},{10,... | collective-permute-start | bytes 3538952 | tf_op jit(solution)/shard_map/ppermute | solution.py:335
  102.4 3.7 %collective-permute-start.27 = (bf16[144,2048]{1,0:T(8,128)(2,1)S(1)}, bf16[144,2048]{1,0:T(8,128)(2,1)S(1)}, u32[]{:S(2)}, u32[]{:S(2)}) collective-permute-start(bf16[144,2048]{1,0:T(8,128)(2,1)S(1)} %get-tuple-element.260), channel_id=1, source_target_pairs={{0,2},{1,3},{2,0},{3,1},{4,6},{5,7},{6,4},{7,5},{8,10},{9,11},{10,... | collective-permute-start | bytes 1769480 | tf_op jit(solution)/shard_map/ppermute | solution.py:335
  102.9 10.6 %collective-permute-start.21 = (bf16[2,128,1024]{2,1,0:T(8,128)(2,1)S(1)}, bf16[2,128,1024]{2,1,0:T(8,128)(2,1)S(1)}, u32[]{:S(2)}, u32[]{:S(2)}) collective-permute-start(bf16[2,128,1024]{2,1,0:T(8,128)(2,1)S(1)} %get-tuple-element.237), channel_id=1, source_target_pairs={{0,1},{1,0},{2,6},{3,7},{4,5},{5,4},{6,2},{7,3},{8,9},{9,8},{10,14... | collective-permute-start | bytes 1572872 | tf_op jit(solution)/shard_map/ppermute | solution.py:335
  107.4 14.9 %collective-permute-start.28 = (bf16[2,128,1024]{2,1,0:T(8,128)(2,1)S(1)}, bf16[2,128,1024]{2,1,0:T(8,128)(2,1)S(1)}, u32[]{:S(2)}, u32[]{:S(2)}) collective-permute-start(bf16[2,128,1024]{2,1,0:T(8,128)(2,1)S(1)} %get-tuple-element.262), channel_id=1, source_target_pairs={{0,1},{1,0},{2,6},{3,7},{4,5},{5,4},{6,2},{7,3},{8,9},{9,8},{10,14... | collective-permute-start | bytes 1572872 | tf_op jit(solution)/shard_map/ppermute | solution.py:335
  113.6 2.1 %collective-permute-start.24 = (bf16[144,2048]{1,0:T(8,128)(2,1)S(1)}, bf16[144,2048]{1,0:T(8,128)(2,1)S(1)}, u32[]{:S(2)}, u32[]{:S(2)}) collective-permute-start(bf16[144,2048]{1,0:T(8,128)(2,1)S(1)} %get-tuple-element.250), channel_id=1, source_target_pairs={{0,2},{1,3},{2,0},{3,1},{4,6},{5,7},{6,4},{7,5},{8,10},{9,11},{10,... | collective-permute-start | bytes 1769480 | tf_op jit(solution)/shard_map/ppermute | solution.py:335
  114.2 7.0 %collective-permute-start.23 = (bf16[128,1024]{1,0:T(8,128)(2,1)S(1)}, bf16[128,1024]{1,0:T(8,128)(2,1)S(1)}, u32[]{:S(2)}, u32[]{:S(2)}) collective-permute-start(bf16[128,1024]{1,0:T(8,128)(2,1)S(1)} %fusion.14), channel_id=1, source_target_pairs={{0,4},{1,5},{2,3},{3,2},{4,0},{5,1},{6,7},{7,6},{8,12},{9,13},{10,... | collective-permute-start | bytes 786440 | tf_op jit(solution)/shard_map/ppermute | solution.py:335
  116.9 17.1 %collective-permute-start.25 = (bf16[2,128,1024]{2,1,0:T(8,128)(2,1)S(1)}, bf16[2,128,1024]{2,1,0:T(8,128)(2,1)S(1)}, u32[]{:S(2)}, u32[]{:S(2)}) collective-permute-start(bf16[2,128,1024]{2,1,0:T(8,128)(2,1)S(1)} %get-tuple-element.251), channel_id=1, source_target_pairs={{0,1},{1,0},{2,6},{3,7},{4,5},{5,4},{6,2},{7,3},{8,9},{9,8},{10,14... | collective-permute-start | bytes 1572872 | tf_op jit(solution)/shard_map/ppermute | solution.py:335
  121.3 9.2 %collective-permute-start.30 = (bf16[128,1024]{1,0:T(8,128)(2,1)S(1)}, bf16[128,1024]{1,0:T(8,128)(2,1)S(1)}, u32[]{:S(2)}, u32[]{:S(2)}) collective-permute-start(bf16[128,1024]{1,0:T(8,128)(2,1)S(1)} %fusion.13), channel_id=1, source_target_pairs={{0,8},{1,9},{2,10},{3,11},{4,12},{5,13},{6,14},{7,15},{8,24},{9,25... | collective-permute-start | bytes 786440 | tf_op jit(solution)/shard_map/ppermute | solution.py:335
  122.5 7.9 %collective-permute-start.29 = (bf16[128,1024]{1,0:T(8,128)(2,1)S(1)}, bf16[128,1024]{1,0:T(8,128)(2,1)S(1)}, u32[]{:S(2)}, u32[]{:S(2)}) collective-permute-start(bf16[128,1024]{1,0:T(8,128)(2,1)S(1)} %fusion.17), channel_id=1, source_target_pairs={{0,4},{1,5},{2,3},{3,2},{4,0},{5,1},{6,7},{7,6},{8,12},{9,13},{10,... | collective-permute-start | bytes 786440 | tf_op jit(solution)/shard_map/ppermute | solution.py:335
  130.6 8.3 %collective-permute-start.31 = (bf16[128,1024]{1,0:T(8,128)(2,1)S(1)}, bf16[128,1024]{1,0:T(8,128)(2,1)S(1)}, u32[]{:S(2)}, u32[]{:S(2)}) collective-permute-start(bf16[128,1024]{1,0:T(8,128)(2,1)S(1)} %fusion.5), channel_id=1, source_target_pairs={{0,8},{1,9},{2,10},{3,11},{4,12},{5,13},{6,14},{7,15},{8,24},{9,25... | collective-permute-start | bytes 786440 | tf_op jit(solution)/shard_map/ppermute | solution.py:335
  134.2 6.4 %collective-permute-start.26 = (bf16[128,1024]{1,0:T(8,128)(2,1)S(1)}, bf16[128,1024]{1,0:T(8,128)(2,1)S(1)}, u32[]{:S(2)}, u32[]{:S(2)}) collective-permute-start(bf16[128,1024]{1,0:T(8,128)(2,1)S(1)} %fusion.16), channel_id=1, source_target_pairs={{0,4},{1,5},{2,3},{3,2},{4,0},{5,1},{6,7},{7,6},{8,12},{9,13},{10,... | collective-permute-start | bytes 786440 | tf_op jit(solution)/shard_map/ppermute | solution.py:335
  140.8 7.3 %collective-permute-start.33 = (bf16[128,1024]{1,0:T(8,128)(2,1)S(1)}, bf16[128,1024]{1,0:T(8,128)(2,1)S(1)}, u32[]{:S(2)}, u32[]{:S(2)}) collective-permute-start(bf16[128,1024]{1,0:T(8,128)(2,1)S(1)} %fusion.8), channel_id=1, source_target_pairs={{0,8},{1,9},{2,10},{3,11},{4,12},{5,13},{6,14},{7,15},{8,24},{9,25... | collective-permute-start | bytes 786440 | tf_op jit(solution)/shard_map/ppermute | solution.py:335
  141.5 6.4 %collective-permute-start.32 = (bf16[128,1024]{1,0:T(8,128)(2,1)S(1)}, bf16[128,1024]{1,0:T(8,128)(2,1)S(1)}, u32[]{:S(2)}, u32[]{:S(2)}) collective-permute-start(bf16[128,1024]{1,0:T(8,128)(2,1)S(1)} %fusion.15), channel_id=1, source_target_pairs={{0,4},{1,5},{2,3},{3,2},{4,0},{5,1},{6,7},{7,6},{8,12},{9,13},{10,... | collective-permute-start | bytes 786440 | tf_op jit(solution)/shard_map/ppermute | solution.py:335

commit v11 on v9

--- a/solution.py
+++ b/solution.py
@@ -398,42 +398,44 @@
         if ready is not None:
             late.append(ready)
         needed = {key: have[key] for key in have if key[1] >= done}
-        came, have, picked, parts, waiting, late, weights = lax.optimization_barrier(
-            (came, needed, picked, parts, waiting, late, weights)
+        listed = sorted(came, reverse=True)
+        values, have, picked, parts, waiting, late, weights = lax.optimization_barrier(
+            ([came[key] for key in listed], needed, picked, parts, waiting, late, weights)
         )
+        came = dict(zip(listed, values))
         have.update(came)
     mine, theirs, picks = pick_rows(place, [have[kind, done] for kind in "sfab"], top, rows, pair_slots)
     unsent, late = late, []
     if waiting is not None:
         keep, send = waiting
         late.append((keep, to_second(tied(send, theirs))))
-    beside = theirs
     if parts is not None:
-        keep, beside = placed(*tied(parts, theirs))
-        late.append((keep, to_second(beside)))
-    late = [(keep, to_second(tied(send, beside))) for keep, send in unsent] + late
+        keep, send = placed(*tied(parts, theirs))
+        late.append((keep, to_second(send)))
     near, far, *kept = run_experts(done, chunks, mine, to_core(theirs), weights, kept)
     keep, send = placed(picks, near, far)
     late.append((keep, to_second(send)))
+    late = [(keep, to_second(tied(first, send))) for keep, first in unsent] + late
+    marks = [send] * (chunks + 2)
     running = None
     for c in range(1, chunks):
         keep, came = late[c]
         if c + 1 < chunks:
-            came = tied(came, near if c == 1 else mark)
+            came = tied(came, near if c == 1 else marks[0])
         pair = added(keep, came)
         came = to_first(pair[1].astype(jnp.bfloat16))
         total = added(pair[0], came if c + 1 == chunks else tied(came, send))
         running = (total if running is None else added(total, running)).astype(jnp.bfloat16)
-        mark = running if c == 1 else mark
+        marks[min(c - 1, 2)] = running
         if c + 1 < chunks:
             running = to_ring(running)
     keep, came = late[0]
-    pair = added(keep, came if running is None else tied(came, mark))
+    pair = added(keep, came)
     came = pair[1].astype(jnp.bfloat16)
     own = added(pair[0], to_first(came if running is None else tied(came, running)))
     grad_tokens = (own if running is None else added(own, to_ring(running))).astype(jnp.bfloat16)
-    kept = tied(kept, send)
     rows_x, rows_g, acts, gate_term, up_term = kept
+    acts, gate_term, up_term = tied(acts, marks[0]), tied(gate_term, marks[1]), tied(up_term, marks[2])
     grad_down = lax.dot_general(acts, rows_g, CONTRACT_FIRST, preferred_element_type=jnp.float32)
     grad_gate = lax.dot_general(gate_term, rows_x, CONTRACT_FIRST, preferred_element_type=jnp.float32)
     grad_up = lax.dot_general(up_term, rows_x, CONTRACT_FIRST, preferred_element_type=jnp.float32)

time: 147 us -> 150 us (1.020)
  waiting for transfers between devices: 57.9 us -> 62.7 us
  starting transfers between devices: 32.5 us -> 31 us
    ppermute x34, waiting for transfers between devices: 57.9 us -> 62.7 us  [permute(): return lax.ppermute(value, ('expert', 'etp'), pairs)]
    ppermute x34, starting transfers between devices: 32.5 us -> 31 us  [permute(): return lax.ppermute(value, ('expert', 'etp'), pairs)]
  transfers between devices with their start and end apart: 34 -> 34, of which waited for: 18 -> 18; matrix products, arithmetic and copies ran while one was open for 8% -> 7% of each run, Pallas kernels for 24% -> 23%
where the time goes in v11:
time: 150 us
  waiting for transfers between devices  62.7 us (42%)
  Pallas kernels  38 us (25%)
  starting transfers between devices  31 us (21%)
  matrix products  10.1 us (7%)
  local copies, waits for them, and re-layouts  5.29 us (4%)
  other arithmetic  1.81 us (1%)
    ppermute x34, waiting for transfers between devices, permute(): return lax.ppermute(value, ('expert', 'etp'), pairs)  62.7 us
    ppermute x34, starting transfers between devices, permute(): return lax.ppermute(value, ('expert', 'etp'), pairs)  31 us
    pallas_call x4, Pallas kernels, run_experts(): pl.pallas_call(functools.partial(expert_kernel, index, kept is not None),...  19.7 us
    pallas_call x4, Pallas kernels, pick_rows(): pl.pallas_call(functools.partial(pick_kernel, top, rows), in_specs=[pl.Bl...  6.7 us
    unnamed x18, local copies, waits for them, and re-layouts  5.16 us
    pallas_call x4, Pallas kernels, place_rows(): pl.pallas_call(place_kernel, in_specs=[pl.BlockSpec(memory_space=pltpu.SM...  5.08 us
    pallas_call x1, Pallas kernels, load_weights(): pl.pallas_call(load_kernel, in_specs=[pl.BlockSpec(memory_space=pltpu.HBM...  4.62 us
    dot_general x1, matrix products, gather_body(): lax.dot_general(acts, rows_g, CONTRACT_FIRST, preferred_element_type=jnp....  3.38 us
  transfers between devices with their start and end apart: 34, of which 18 were waited for; matrix products, arithmetic and copies ran while one was open for 7% of the time, Pallas kernels for 23%

profile of v11, /device:TPU:0, one launch (start us, length us, event | category | flops | bytes accessed | tf_op | source)
XLA Modules:
  0.0 149.9 jit_solution(11276979681503293897)
XLA Ops:
  0.6 1.9 %pack.1.refs_0_ = bf16[272,1024]{1,0:T(8,128)(2,1)} custom-call(bf16[128,1024]{1,0:T(8,128)(2,1)} %tokens_ref.1, bf16[128,1024]{1,0:T(8,128)(2,1)} %grads_ref.1, s32[8,128]{1,0:T(8,128)} %bitcast.61, f32[8,128]{1,0:T(8,128)} %bitcast.62), custom_call_target="tpu_custom_call" | custom-call | tf_op jit(solution)/shard_map/pack/pallas_call | solution.py:128
  2.5 2.9 %collective-permute-start.2 = (bf16[272,1024]{1,0:T(8,128)(2,1)}, bf16[272,1024]{1,0:T(8,128)(2,1)S(1)}, u32[]{:S(2)}, u32[]{:S(2)}) collective-permute-start(bf16[272,1024]{1,0:T(8,128)(2,1)} %pack.1.refs_0_), channel_id=1, source_target_pairs={{0,1},{1,0},{2,6},{3,7},{4,5},{5,4},{6,2},{7,3},{8,9},{9,8},{10,14... | collective-permute-start | bytes 1671176 | tf_op jit(solution)/shard_map/ppermute | solution.py:335
  5.5 1.5 %collective-permute-start.1 = (bf16[272,1024]{1,0:T(8,128)(2,1)}, bf16[272,1024]{1,0:T(8,128)(2,1)S(1)}, u32[]{:S(2)}, u32[]{:S(2)}) collective-permute-start(bf16[272,1024]{1,0:T(8,128)(2,1)} %pack.1.refs_0_), channel_id=1, source_target_pairs={{0,4},{1,5},{2,3},{3,2},{4,0},{5,1},{6,7},{7,6},{8,12},{9,13},{10,... | collective-permute-start | bytes 1671176 | tf_op jit(solution)/shard_map/ppermute | solution.py:335
  7.0 1.6 %collective-permute-start = (bf16[272,1024]{1,0:T(8,128)(2,1)}, bf16[272,1024]{1,0:T(8,128)(2,1)S(1)}, u32[]{:S(2)}, u32[]{:S(2)}) collective-permute-start(bf16[272,1024]{1,0:T(8,128)(2,1)} %pack.1.refs_0_), channel_id=1, source_target_pairs={{0,8},{1,9},{2,10},{3,11},{4,12},{5,13},{6,14},{7,15},{8,24},{9,25... | collective-permute-start | bytes 1671176 | tf_op jit(solution)/shard_map/ppermute | solution.py:335
  8.6 4.6 %load.1 = (bf16[384,2048]{1,0:T(8,128)(2,1)}, bf16[384,2048]{1,0:T(8,128)(2,1)}, bf16[384,2048]{1,0:T(8,128)(2,1)}) custom-call(bf16[384,2048]{1,0:T(8,128)(2,1)} %bitcast.58, bf16[384,2048]{1,0:T(8,128)(2,1)} %bitcast.59, bf16[384,2048]{1,0:T(8,128)(2,1)} %bitcast.60), custom_call_target="tpu_custom_call" | custom-call | tf_op jit(solution)/shard_map/load/pallas_call | solution.py:147
  13.2 5.5 %collective-permute-done.2.refs_2_ = bf16[272,1024]{1,0:T(8,128)(2,1)S(1)} collective-permute-done((bf16[272,1024]{1,0:T(8,128)(2,1)}, bf16[272,1024]{1,0:T(8,128)(2,1)S(1)}, u32[]{:S(2)}, u32[]{:S(2)}) %collective-permute-start.2) | collective-permute-done | bytes 557088 | tf_op jit(solution)/shard_map/ppermute | solution.py:335
  18.7 3.2 %collective-permute-done.refs_0_ = bf16[272,1024]{1,0:T(8,128)(2,1)S(1)} collective-permute-done((bf16[272,1024]{1,0:T(8,128)(2,1)}, bf16[272,1024]{1,0:T(8,128)(2,1)S(1)}, u32[]{:S(2)}, u32[]{:S(2)}) %collective-permute-start) | collective-permute-done | bytes 557088 | tf_op jit(solution)/shard_map/ppermute | solution.py:335
  24.7 11.2 %collective-permute-done.5.refs_3_ = bf16[272,1024]{1,0:T(8,128)(2,1)S(1)} collective-permute-done((bf16[272,1024]{1,0:T(8,128)(2,1)S(1)}, bf16[272,1024]{1,0:T(8,128)(2,1)S(1)}, u32[]{:S(2)}, u32[]{:S(2)}) %collective-permute-start.5) | collective-permute-done | bytes 557088 | tf_op jit(solution)/shard_map/ppermute | solution.py:335
  37.3 1.2 collective-permute-start.8
  40.2 1.1 copy-done.6
  41.2 1.1 copy-done.8
  42.3 1.5 %pick.4 = (bf16[2,144,2048]{2,1,0:T(8,128)(2,1)S(1)}, bf16[2,144,2048]{2,1,0:T(8,128)(2,1)S(1)}, bf16[288,256]{1,0:T(8,128)(2,1)S(1)}) custom-call(s32[3]{0:T(128)S(1)} %pad_add_fusion.place_ref, bf16[272,1024]{1,0:T(8,128)(2,1)S(1)} %copy-done.4, bf16[272,1024]{1,0:T(8,128)(2,1)S(1)} %copy-done.6, bf16[272,1024]{1,0:T(8,128)(2,1)S(1)} %collective-permute-done.2.refs_2_, ...), custom_call_target="tpu_custom_call" | custom-call | tf_op jit(solution)/shard_map/pick/pallas_call | solution.py:271
  43.8 3.1 %collective-permute-done.8.refs_2_ = bf16[272,1024]{1,0:T(8,128)(2,1)} collective-permute-done((bf16[272,1024]{1,0:T(8,128)(2,1)S(1)}, bf16[272,1024]{1,0:T(8,128)(2,1)}, u32[]{:S(2)}, u32[]{:S(2)}) %collective-permute-start.8) | collective-permute-done | bytes 557088 | tf_op jit(solution)/shard_map/ppermute | solution.py:335
  46.9 6.0 %collective-permute-done.7.refs_3_ = bf16[272,1024]{1,0:T(8,128)(2,1)} collective-permute-done((bf16[272,1024]{1,0:T(8,128)(2,1)S(1)}, bf16[272,1024]{1,0:T(8,128)(2,1)}, u32[]{:S(2)}, u32[]{:S(2)}) %collective-permute-start.7) | collective-permute-done | bytes 557088 | tf_op jit(solution)/shard_map/ppermute | solution.py:335
  52.9 1.2 collective-permute-start.10
  55.7 2.2 %pick.5 = (bf16[2,144,2048]{2,1,0:T(8,128)(2,1)S(1)}, bf16[2,144,2048]{2,1,0:T(8,128)(2,1)S(1)}, bf16[288,256]{1,0:T(8,128)(2,1)S(1)}) custom-call(s32[3]{0:T(128)S(1)} %pad_add_fusion.place_ref, bf16[272,1024]{1,0:T(8,128)(2,1)S(1)} %collective-permute-done.refs_0_, bf16[272,1024]{1,0:T(8,128)(2,1)S(1)} %collective-permute-done.4.refs_1_, ...), custom_call_target="tpu_custom_call" | custom-call | tf_op jit(solution)/shard_map/pick/pallas_call | solution.py:271
  57.9 1.4 copy-done.2
  59.3 4.8 %experts.4 = (bf16[144,2048]{1,0:T(8,128)(2,1)S(1)}, bf16[144,2048]{1,0:T(8,128)(2,1)S(1)}, bf16[1152,2048]{1,0:T(8,128)(2,1)S(1)}, bf16[1152,2048]{1,0:T(8,128)...) custom-call(bf16[2,144,2048]{2,1,0:T(8,128)(2,1)S(1)} %get-tuple-element.172., ...), custom_call_target="tpu_custom_call" | custom-call | tf_op jit(solution)/shard_map/experts/pallas_call | solution.py:290
  64.2 4.2 %collective-permute-done.11.refs_2_ = bf16[272,1024]{1,0:T(8,128)(2,1)S(1)} collective-permute-done((bf16[272,1024]{1,0:T(8,128)(2,1)S(1)}, bf16[272,1024]{1,0:T(8,128)(2,1)S(1)}, u32[]{:S(2)}, u32[]{:S(2)}) %collective-permute-start.11) | collective-permute-done | bytes 557088 | tf_op jit(solution)/shard_map/ppermute | solution.py:335
  68.4 1.9 %collective-permute-done.9.refs_0_ = bf16[272,1024]{1,0:T(8,128)(2,1)S(1)} collective-permute-done((bf16[272,1024]{1,0:T(8,128)(2,1)S(1)}, bf16[272,1024]{1,0:T(8,128)(2,1)S(1)}, u32[]{:S(2)}, u32[]{:S(2)}) %collective-permute-start.9) | collective-permute-done | bytes 557088 | tf_op jit(solution)/shard_map/ppermute | solution.py:335
  70.8 1.2 collective-permute-start.14
  72.8 1.5 %pick.6 = (bf16[2,144,2048]{2,1,0:T(8,128)(2,1)S(1)}, bf16[2,144,2048]{2,1,0:T(8,128)(2,1)S(1)}, bf16[288,256]{1,0:T(8,128)(2,1)S(1)}) custom-call(s32[3]{0:T(128)S(1)} %pad_add_fusion.place_ref, bf16[272,1024]{1,0:T(8,128)(2,1)S(1)} %collective-permute-done.3.refs_0_, bf16[272,1024]{1,0:T(8,128)(2,1)S(1)} %collective-permute-done.6.refs_1_, ...), custom_call_target="tpu_custom_call" | custom-call | tf_op jit(solution)/shard_map/pick/pallas_call | solution.py:271
  74.3 1.3 place.4
  75.6 5.1 %experts.5 = (bf16[144,2048]{1,0:T(8,128)(2,1)S(1)}, bf16[144,2048]{1,0:T(8,128)(2,1)S(1)}, bf16[1152,2048]{1,0:T(8,128)(2,1)S(1)}, bf16[1152,2048]{1,0:T(8,128)...) custom-call(bf16[2,144,2048]{2,1,0:T(8,128)(2,1)S(1)} %get-tuple-ele, ...), custom_call_target="tpu_custom_call", output_to_operand_aliasing={{2}: (5, {}), {3}: (6, {}), {4}: (7, {}), {5}: (8, {}), {6}... | custom-call | tf_op jit(solution)/shard_map/experts/pallas_call | solution.py:290
  80.7 7.0 %collective-permute-done.13.refs_1_ = bf16[272,1024]{1,0:T(8,128)(2,1)S(1)} collective-permute-done((bf16[272,1024]{1,0:T(8,128)(2,1)S(1)}, bf16[272,1024]{1,0:T(8,128)(2,1)S(1)}, u32[]{:S(2)}, u32[]{:S(2)}) %collective-permute-start.13) | collective-permute-done | bytes 557088 | tf_op jit(solution)/shard_map/ppermute | solution.py:335
  88.2 1.0 collective-permute-start.17
  89.2 2.1 %collective-permute-done.19.far_ref = bf16[144,2048]{1,0:T(8,128)(2,1)S(1)} collective-permute-done((bf16[144,2048]{1,0:T(8,128)(2,1)S(1)}, bf16[144,2048]{1,0:T(8,128)(2,1)S(1)}, u32[]{:S(2)}, u32[]{:S(2)}) %collective-permute-start.19) | collective-permute-done | bytes 589856 | tf_op jit(solution)/shard_map/ppermute | solution.py:335
  91.4 1.3 place.5
  92.7 4.9 %experts.6 = (bf16[144,2048]{1,0:T(8,128)(2,1)S(1)}, bf16[144,2048]{1,0:T(8,128)(2,1)S(1)}, bf16[1152,2048]{1,0:T(8,128)(2,1)S(1)}, bf16[1152,2048]{1,0:T(8,128)...) custom-call(bf16[2,144,2048]{2,1,0:T(8,128)(2,1)S(1)} %get-tuple-ele, ...), custom_call_target="tpu_custom_call", output_to_operand_aliasing={{2}: (5, {}), {3}: (6, {}), {4}: (7, {}), {5}: (8, {}), {6}... | custom-call | tf_op jit(solution)/shard_map/experts/pallas_call | solution.py:290
  97.7 1.5 %pick.7 = (bf16[2,144,2048]{2,1,0:T(8,128)(2,1)S(1)}, bf16[2,144,2048]{2,1,0:T(8,128)(2,1)S(1)}, bf16[288,256]{1,0:T(8,128)(2,1)S(1)}) custom-call(s32[3]{0:T(128)S(1)} %pad_add_fusion.place_ref, bf16[272,1024]{1,0:T(8,128)(2,1)S(1)} %collective-permute-done.9.refs_0_, bf16[272,1024]{1,0:T(8,128)(2,1)S(1)} %collective-permute-done.13.refs_1_, ...), custom_call_target="tpu_custom_call" | custom-call | tf_op jit(solution)/shard_map/pick/pallas_call | solution.py:271
  99.8 1.0 collective-permute-start.27
  100.9 2.2 %collective-permute-done.25.far_ref = bf16[144,2048]{1,0:T(8,128)(2,1)S(1)} collective-permute-done((bf16[144,2048]{1,0:T(8,128)(2,1)S(1)}, bf16[144,2048]{1,0:T(8,128)(2,1)S(1)}, u32[]{:S(2)}, u32[]{:S(2)}) %collective-permute-start.25) | collective-permute-done | bytes 589856 | tf_op jit(solution)/shard_map/ppermute | solution.py:335
  103.0 1.3 place.7
  104.3 1.1 collective-permute-start.26
  105.4 4.9 %experts.7 = (bf16[144,2048]{1,0:T(8,128)(2,1)S(1)}, bf16[144,2048]{1,0:T(8,128)(2,1)S(1)}, bf16[1152,2048]{1,0:T(8,128)(2,1)S(1)}, bf16[1152,2048]{1,0:T(8,128)...) custom-call(bf16[2,144,2048]{2,1,0:T(8,128)(2,1)S(1)} %get-tuple-ele, ...), custom_call_target="tpu_custom_call", output_to_operand_aliasing={{2}: (5, {}), {3}: (6, {}), {4}: (7, {}), {5}: (8, {}), {6}... | custom-call | tf_op jit(solution)/shard_map/experts/pallas_call | solution.py:290
  112.4 1.3 place.6
  113.6 1.1 collective-permute-start.23
  114.7 2.9 %collective-permute-done.28 = bf16[128,1024]{1,0:T(8,128)(2,1)S(1)} collective-permute-done((bf16[128,1024]{1,0:T(8,128)(2,1)S(1)}, bf16[128,1024]{1,0:T(8,128)(2,1)S(1)}, u32[]{:S(2)}, u32[]{:S(2)}) %collective-permute-start.28) | collective-permute-done | bytes 262176 | tf_op jit(solution)/shard_map/ppermute | solution.py:335
  117.6 1.1 collective-permute-start.30
  118.9 1.0 collective-permute-start.29
  120.9 3.4 %fusion.2 = bf16[1,384,2048]{2,1,0:T(8,128)(2,1)} fusion(bf16[1152,384]{1,0:T(8,128)(2,1)S(1)} %get-tuple-element.272, bf16[1152,2048]{1,0:T(8,128)(2,1)S(1)} %get-tuple-element.273), kind=kOutput, calls=%fused_computation.5 | convolution fusion | flops 1812725760 | bytes 7176192 | tf_op jit(solution)/shard_map/dot_general | solution.py:439
  124.3 3.9 %collective-permute-done.29 = bf16[128,1024]{1,0:T(8,128)(2,1)S(1)} collective-permute-done((bf16[128,1024]{1,0:T(8,128)(2,1)S(1)}, bf16[128,1024]{1,0:T(8,128)(2,1)S(1)}, u32[]{:S(2)}, u32[]{:S(2)}) %collective-permute-start.29) | collective-permute-done | bytes 262176 | tf_op jit(solution)/shard_map/ppermute | solution.py:335
  128.3 3.3 %collective-permute-start.31 = (bf16[128,1024]{1,0:T(8,128)(2,1)S(1)}, bf16[128,1024]{1,0:T(8,128)(2,1)S(1)}, u32[]{:S(2)}, u32[]{:S(2)}) collective-permute-start(bf16[128,1024]{1,0:T(8,128)(2,1)S(1)} %fusion.5), channel_id=1, source_target_pairs={{0,8},{1,9},{2,10},{3,11},{4,12},{5,13},{6,14},{7,15},{8,24},{9,25... | collective-permute-start | bytes 786440 | tf_op jit(solution)/shard_map/ppermute | solution.py:335
  131.6 3.4 %fusion = bf16[1,384,2048]{2,1,0:T(8,128)(2,1)} fusion(bf16[1152,384]{1,0:T(8,128)(2,1)S(1)} %get-tuple-element.267, bf16[1152,2048]{1,0:T(8,128)(2,1)S(1)} %get-tuple-element.268), kind=kOutput, calls=%fused_computation.3 | convolution fusion | flops 1812725760 | bytes 7176192 | tf_op jit(solution)/shard_map/dot_general | solution.py:440
  135.2 1.1 collective-permute-start.24
  136.5 5.1 %collective-permute-done.24 = bf16[128,1024]{1,0:T(8,128)(2,1)S(1)} collective-permute-done((bf16[128,1024]{1,0:T(8,128)(2,1)S(1)}, bf16[128,1024]{1,0:T(8,128)(2,1)S(1)}, u32[]{:S(2)}, u32[]{:S(2)}) %collective-permute-start.24) | collective-permute-done | bytes 262176 | tf_op jit(solution)/shard_map/ppermute | solution.py:335
  142.9 3.4 %fusion.1 = bf16[1,384,2048]{2,1,0:T(8,128)(2,1)} fusion(bf16[1152,384]{1,0:T(8,128)(2,1)S(1)} %get-tuple-element.270, bf16[1152,2048]{1,0:T(8,128)(2,1)S(1)} %get-tuple-element.268), kind=kOutput, calls=%fused_computation.4 | convolution fusion | flops 1812725760 | bytes 7176192 | tf_op jit(solution)/shard_map/dot_general | solution.py:441
  146.3 2.0 %collective-permute-done.32 = bf16[128,1024]{1,0:T(8,128)(2,1)S(1)} collective-permute-done((bf16[128,1024]{1,0:T(8,128)(2,1)S(1)}, bf16[128,1024]{1,0:T(8,128)(2,1)S(1)}, u32[]{:S(2)}, u32[]{:S(2)}) %collective-permute-start.32) | collective-permute-done | bytes 262176 | tf_op jit(solution)/shard_map/ppermute | solution.py:335
  (68 shorter events, 16.5 us)
Async XLA Ops:
  2.5 16.2 %collective-permute-start.2 = (bf16[272,1024]{1,0:T(8,128)(2,1)}, bf16[272,1024]{1,0:T(8,128)(2,1)S(1)}, u32[]{:S(2)}, u32[]{:S(2)}) collective-permute-start(bf16[272,1024]{1,0:T(8,128)(2,1)} %pack.1.refs_0_), channel_id=1, source_target_pairs={{0,1},{1,0},{2,6},{3,7},{4,5},{5,4},{6,2},{7,3},{8,9},{9,8},{10,14... | collective-permute-start | bytes 1671176 | tf_op jit(solution)/shard_map/ppermute | solution.py:335
  5.5 13.2 %collective-permute-start.1 = (bf16[272,1024]{1,0:T(8,128)(2,1)}, bf16[272,1024]{1,0:T(8,128)(2,1)S(1)}, u32[]{:S(2)}, u32[]{:S(2)}) collective-permute-start(bf16[272,1024]{1,0:T(8,128)(2,1)} %pack.1.refs_0_), channel_id=1, source_target_pairs={{0,4},{1,5},{2,3},{3,2},{4,0},{5,1},{6,7},{7,6},{8,12},{9,13},{10,... | collective-permute-start | bytes 1671176 | tf_op jit(solution)/shard_map/ppermute | solution.py:335
  7.0 14.9 %collective-permute-start = (bf16[272,1024]{1,0:T(8,128)(2,1)}, bf16[272,1024]{1,0:T(8,128)(2,1)S(1)}, u32[]{:S(2)}, u32[]{:S(2)}) collective-permute-start(bf16[272,1024]{1,0:T(8,128)(2,1)} %pack.1.refs_0_), channel_id=1, source_target_pairs={{0,8},{1,9},{2,10},{3,11},{4,12},{5,13},{6,14},{7,15},{8,24},{9,25... | collective-permute-start | bytes 1671176 | tf_op jit(solution)/shard_map/ppermute | solution.py:335
  8.6 31.6 %copy-start.4 = (bf16[272,1024]{1,0:T(8,128)(2,1)S(1)}, bf16[272,1024]{1,0:T(8,128)(2,1)}, u32[]{:S(2)}) copy-start(bf16[272,1024]{1,0:T(8,128)(2,1)} %pack.1.refs_0_) | copy-start | bytes 1671172
  21.9 13.9 %collective-permute-start.5 = (bf16[272,1024]{1,0:T(8,128)(2,1)S(1)}, bf16[272,1024]{1,0:T(8,128)(2,1)S(1)}, u32[]{:S(2)}, u32[]{:S(2)}) collective-permute-start(bf16[272,1024]{1,0:T(8,128)(2,1)S(1)} %collective-permute-done.1.refs_1_), channel_id=1, source_target_pairs={{0,1},{1,0},{2,6},{3,7},{4,5},{5,4},{6,2},{7,3},{8,9},{9,8},{10,14... | collective-permute-start | bytes 1671176 | tf_op jit(solution)/shard_map/ppermute | solution.py:335
  22.5 0.8 copy-start.5
  23.3 13.4 %collective-permute-start.4 = (bf16[272,1024]{1,0:T(8,128)(2,1)S(1)}, bf16[272,1024]{1,0:T(8,128)(2,1)S(1)}, u32[]{:S(2)}, u32[]{:S(2)}) collective-permute-start(bf16[272,1024]{1,0:T(8,128)(2,1)S(1)} %collective-permute-done.refs_0_), channel_id=1, source_target_pairs={{0,4},{1,5},{2,3},{3,2},{4,0},{5,1},{6,7},{7,6},{8,12},{9,13},{10,... | collective-permute-start | bytes 1671176 | tf_op jit(solution)/shard_map/ppermute | solution.py:335
  23.7 13.5 %collective-permute-start.3 = (bf16[272,1024]{1,0:T(8,128)(2,1)S(1)}, bf16[272,1024]{1,0:T(8,128)(2,1)S(1)}, u32[]{:S(2)}, u32[]{:S(2)}) collective-permute-start(bf16[272,1024]{1,0:T(8,128)(2,1)S(1)} %collective-permute-done.refs_0_), channel_id=1, source_target_pairs={{0,8},{1,9},{2,10},{3,11},{4,12},{5,13},{6,14},{7,15},{8,24},{9,25... | collective-permute-start | bytes 1671176 | tf_op jit(solution)/shard_map/ppermute | solution.py:335
  35.9 0.8 copy-start.7
  37.3 9.6 %collective-permute-start.8 = (bf16[272,1024]{1,0:T(8,128)(2,1)S(1)}, bf16[272,1024]{1,0:T(8,128)(2,1)}, u32[]{:S(2)}, u32[]{:S(2)}) collective-permute-start(bf16[272,1024]{1,0:T(8,128)(2,1)S(1)} %collective-permute-done.refs_0_), channel_id=1, source_target_pairs={{0,1},{1,0},{2,6},{3,7},{4,5},{5,4},{6,2},{7,3},{8,9},{9,8},{10,14... | collective-permute-start | bytes 1671176 | tf_op jit(solution)/shard_map/ppermute | solution.py:335
  38.5 14.4 %collective-permute-start.7 = (bf16[272,1024]{1,0:T(8,128)(2,1)S(1)}, bf16[272,1024]{1,0:T(8,128)(2,1)}, u32[]{:S(2)}, u32[]{:S(2)}) collective-permute-start(bf16[272,1024]{1,0:T(8,128)(2,1)S(1)} %collective-permute-done.4.refs_1_), channel_id=1, source_target_pairs={{0,1},{1,0},{2,6},{3,7},{4,5},{5,4},{6,2},{7,3},{8,9},{9,8},{10,14... | collective-permute-start | bytes 1671176 | tf_op jit(solution)/shard_map/ppermute | solution.py:335
  39.3 13.6 %collective-permute-start.6 = (bf16[272,1024]{1,0:T(8,128)(2,1)S(1)}, bf16[272,1024]{1,0:T(8,128)(2,1)S(1)}, u32[]{:S(2)}, u32[]{:S(2)}) collective-permute-start(bf16[272,1024]{1,0:T(8,128)(2,1)S(1)} %collective-permute-done.4.refs_1_), channel_id=1, source_target_pairs={{0,8},{1,9},{2,10},{3,11},{4,12},{5,13},{6,14},{7,15},{8,24},{9,25... | collective-permute-start | bytes 1671176 | tf_op jit(solution)/shard_map/ppermute | solution.py:335
  40.2 1.1 copy-start.6
  41.2 1.1 copy-start.8
  42.3 15.6 %copy-start.1 = (bf16[384,2048]{1,0:T(8,128)(2,1)S(1)}, bf16[384,2048]{1,0:T(8,128)(2,1)}, u32[]{:S(2)}) copy-start(bf16[384,2048]{1,0:T(8,128)(2,1)} %get-tuple-element.238.wu_ref) | copy-start | bytes 4718596
  43.8 14.1 %copy-start = (bf16[384,2048]{1,0:T(8,128)(2,1)S(1)}, bf16[384,2048]{1,0:T(8,128)(2,1)}, u32[]{:S(2)}) copy-start(bf16[384,2048]{1,0:T(8,128)(2,1)} %get-tuple-element.237.wg_ref) | copy-start | bytes 4718596
  52.9 5.0 %collective-permute-start.12 = (bf16[2,144,2048]{2,1,0:T(8,128)(2,1)S(1)}, bf16[2,144,2048]{2,1,0:T(8,128)(2,1)S(1)}, u32[]{:S(2)}, u32[]{:S(2)}) collective-permute-start(bf16[2,144,2048]{2,1,0:T(8,128)(2,1)S(1)} %get-tuple-element.173), channel_id=1, source_target_pairs={{0,2},{1,3},{2,0},{3,1},{4,6},{5,7},{6,4},{7,5},{8,10},{9,11},{10,... | collective-permute-start | bytes 3538952 | tf_op jit(solution)/shard_map/ppermute | solution.py:335
  52.9 11.3 %collective-permute-start.10 = (bf16[272,1024]{1,0:T(8,128)(2,1)S(1)}, bf16[272,1024]{1,0:T(8,128)(2,1)S(1)}, u32[]{:S(2)}, u32[]{:S(2)}) collective-permute-start(bf16[272,1024]{1,0:T(8,128)(2,1)S(1)} %collective-permute-done.6.refs_1_), channel_id=1, source_target_pairs={{0,1},{1,0},{2,6},{3,7},{4,5},{5,4},{6,2},{7,3},{8,9},{9,8},{10,14... | collective-permute-start | bytes 1671176 | tf_op jit(solution)/shard_map/ppermute | solution.py:335
  54.1 14.3 %collective-permute-start.11 = (bf16[272,1024]{1,0:T(8,128)(2,1)S(1)}, bf16[272,1024]{1,0:T(8,128)(2,1)S(1)}, u32[]{:S(2)}, u32[]{:S(2)}) collective-permute-start(bf16[272,1024]{1,0:T(8,128)(2,1)S(1)} %collective-permute-done.3.refs_0_), channel_id=1, source_target_pairs={{0,1},{1,0},{2,6},{3,7},{4,5},{5,4},{6,2},{7,3},{8,9},{9,8},{10,14... | collective-permute-start | bytes 1671176 | tf_op jit(solution)/shard_map/ppermute | solution.py:335
  54.9 15.4 %collective-permute-start.9 = (bf16[272,1024]{1,0:T(8,128)(2,1)S(1)}, bf16[272,1024]{1,0:T(8,128)(2,1)S(1)}, u32[]{:S(2)}, u32[]{:S(2)}) collective-permute-start(bf16[272,1024]{1,0:T(8,128)(2,1)S(1)} %collective-permute-done.3.refs_0_), channel_id=1, source_target_pairs={{0,8},{1,9},{2,10},{3,11},{4,12},{5,13},{6,14},{7,15},{8,24},{9,25... | collective-permute-start | bytes 1671176 | tf_op jit(solution)/shard_map/ppermute | solution.py:335
  57.9 1.4 copy-start.2
  70.3 5.3 %copy-start.3 = (bf16[384,2048]{1,0:T(8,128)(2,1)S(1)}, bf16[384,2048]{1,0:T(8,128)(2,1)}, u32[]{:S(2)}) copy-start(bf16[384,2048]{1,0:T(8,128)(2,1)} %get-tuple-element.239.wd_ref) | copy-start | bytes 4718596
  70.3 5.3 %collective-permute-start.15 = (bf16[2,144,2048]{2,1,0:T(8,128)(2,1)S(1)}, bf16[2,144,2048]{2,1,0:T(8,128)(2,1)S(1)}, u32[]{:S(2)}, u32[]{:S(2)}) collective-permute-start(bf16[2,144,2048]{2,1,0:T(8,128)(2,1)S(1)} %get-tuple-element.189), channel_id=1, source_target_pairs={{0,2},{1,3},{2,0},{3,1},{4,6},{5,7},{6,4},{7,5},{8,10},{9,11},{10,... | collective-permute-start | bytes 3538952 | tf_op jit(solution)/shard_map/ppermute | solution.py:335
  70.3 4.0 %collective-permute-start.16 = (bf16[144,2048]{1,0:T(8,128)(2,1)S(1)}, bf16[144,2048]{1,0:T(8,128)(2,1)S(1)}, u32[]{:S(2)}, u32[]{:S(2)}) collective-permute-start(bf16[144,2048]{1,0:T(8,128)(2,1)S(1)} %get-tuple-element.202), channel_id=1, source_target_pairs={{0,2},{1,3},{2,0},{3,1},{4,6},{5,7},{6,4},{7,5},{8,10},{9,11},{10,... | collective-permute-start | bytes 1769480 | tf_op jit(solution)/shard_map/ppermute | solution.py:335
  70.8 9.9 %collective-permute-start.14 = (bf16[272,1024]{1,0:T(8,128)(2,1)S(1)}, bf16[272,1024]{1,0:T(8,128)(2,1)S(1)}, u32[]{:S(2)}, u32[]{:S(2)}) collective-permute-start(bf16[272,1024]{1,0:T(8,128)(2,1)S(1)} %collective-permute-done.9.refs_0_), channel_id=1, source_target_pairs={{0,1},{1,0},{2,6},{3,7},{4,5},{5,4},{6,2},{7,3},{8,9},{9,8},{10,14... | collective-permute-start | bytes 1671176 | tf_op jit(solution)/shard_map/ppermute | solution.py:335
  72.0 15.7 %collective-permute-start.13 = (bf16[272,1024]{1,0:T(8,128)(2,1)S(1)}, bf16[272,1024]{1,0:T(8,128)(2,1)S(1)}, u32[]{:S(2)}, u32[]{:S(2)}) collective-permute-start(bf16[272,1024]{1,0:T(8,128)(2,1)S(1)} %collective-permute-done.6.refs_1_), channel_id=1, source_target_pairs={{0,8},{1,9},{2,10},{3,11},{4,12},{5,13},{6,14},{7,15},{8,24},{9,25... | collective-permute-start | bytes 1671176 | tf_op jit(solution)/shard_map/ppermute | solution.py:335
  87.7 5.0 %collective-permute-start.18 = (bf16[2,144,2048]{2,1,0:T(8,128)(2,1)S(1)}, bf16[2,144,2048]{2,1,0:T(8,128)(2,1)S(1)}, u32[]{:S(2)}, u32[]{:S(2)}) collective-permute-start(bf16[2,144,2048]{2,1,0:T(8,128)(2,1)S(1)} %get-tuple-element.210), channel_id=1, source_target_pairs={{0,2},{1,3},{2,0},{3,1},{4,6},{5,7},{6,4},{7,5},{8,10},{9,11},{10,... | collective-permute-start | bytes 3538952 | tf_op jit(solution)/shard_map/ppermute | solution.py:335
  87.7 3.7 %collective-permute-start.19 = (bf16[144,2048]{1,0:T(8,128)(2,1)S(1)}, bf16[144,2048]{1,0:T(8,128)(2,1)S(1)}, u32[]{:S(2)}, u32[]{:S(2)}) collective-permute-start(bf16[144,2048]{1,0:T(8,128)(2,1)S(1)} %get-tuple-element.223), channel_id=1, source_target_pairs={{0,2},{1,3},{2,0},{3,1},{4,6},{5,7},{6,4},{7,5},{8,10},{9,11},{10,... | collective-permute-start | bytes 1769480 | tf_op jit(solution)/shard_map/ppermute | solution.py:335
  88.2 9.5 %collective-permute-start.17 = (bf16[272,1024]{1,0:T(8,128)(2,1)S(1)}, bf16[272,1024]{1,0:T(8,128)(2,1)S(1)}, u32[]{:S(2)}, u32[]{:S(2)}) collective-permute-start(bf16[272,1024]{1,0:T(8,128)(2,1)S(1)} %collective-permute-done.13.refs_1_), channel_id=1, source_target_pairs={{0,1},{1,0},{2,6},{3,7},{4,5},{5,4},{6,2},{7,3},{8,9},{9,8},{10,14... | collective-permute-start | bytes 1671176 | tf_op jit(solution)/shard_map/ppermute | solution.py:335
  99.3 6.1 %collective-permute-start.20 = (bf16[2,144,2048]{2,1,0:T(8,128)(2,1)S(1)}, bf16[2,144,2048]{2,1,0:T(8,128)(2,1)S(1)}, u32[]{:S(2)}, u32[]{:S(2)}) collective-permute-start(bf16[2,144,2048]{2,1,0:T(8,128)(2,1)S(1)} %get-tuple-element.236), channel_id=1, source_target_pairs={{0,2},{1,3},{2,0},{3,1},{4,6},{5,7},{6,4},{7,5},{8,10},{9,11},{10,... | collective-permute-start | bytes 3538952 | tf_op jit(solution)/shard_map/ppermute | solution.py:335
  99.3 3.7 %collective-permute-start.25 = (bf16[144,2048]{1,0:T(8,128)(2,1)S(1)}, bf16[144,2048]{1,0:T(8,128)(2,1)S(1)}, u32[]{:S(2)}, u32[]{:S(2)}) collective-permute-start(bf16[144,2048]{1,0:T(8,128)(2,1)S(1)} %get-tuple-element.255), channel_id=1, source_target_pairs={{0,2},{1,3},{2,0},{3,1},{4,6},{5,7},{6,4},{7,5},{8,10},{9,11},{10,... | collective-permute-start | bytes 1769480 | tf_op jit(solution)/shard_map/ppermute | solution.py:335
  99.8 10.4 %collective-permute-start.27 = (bf16[2,128,1024]{2,1,0:T(8,128)(2,1)S(1)}, bf16[2,128,1024]{2,1,0:T(8,128)(2,1)S(1)}, u32[]{:S(2)}, u32[]{:S(2)}) collective-permute-start(bf16[2,128,1024]{2,1,0:T(8,128)(2,1)S(1)} %get-tuple-element.260), channel_id=1, source_target_pairs={{0,1},{1,0},{2,6},{3,7},{4,5},{5,4},{6,2},{7,3},{8,9},{9,8},{10,14... | collective-permute-start | bytes 1572872 | tf_op jit(solution)/shard_map/ppermute | solution.py:335
  104.3 14.4 %collective-permute-start.26 = (bf16[2,128,1024]{2,1,0:T(8,128)(2,1)S(1)}, bf16[2,128,1024]{2,1,0:T(8,128)(2,1)S(1)}, u32[]{:S(2)}, u32[]{:S(2)}) collective-permute-start(bf16[2,128,1024]{2,1,0:T(8,128)(2,1)S(1)} %get-tuple-element.257), channel_id=1, source_target_pairs={{0,1},{1,0},{2,6},{3,7},{4,5},{5,4},{6,2},{7,3},{8,9},{9,8},{10,14... | collective-permute-start | bytes 1572872 | tf_op jit(solution)/shard_map/ppermute | solution.py:335
  110.3 2.1 %collective-permute-start.21 = (bf16[144,2048]{1,0:T(8,128)(2,1)S(1)}, bf16[144,2048]{1,0:T(8,128)(2,1)S(1)}, u32[]{:S(2)}, u32[]{:S(2)}) collective-permute-start(bf16[144,2048]{1,0:T(8,128)(2,1)S(1)} %get-tuple-element.246), channel_id=1, source_target_pairs={{0,2},{1,3},{2,0},{3,1},{4,6},{5,7},{6,4},{7,5},{8,10},{9,11},{10,... | collective-permute-start | bytes 1769480 | tf_op jit(solution)/shard_map/ppermute | solution.py:335
  110.6 7.0 %collective-permute-start.28 = (bf16[128,1024]{1,0:T(8,128)(2,1)S(1)}, bf16[128,1024]{1,0:T(8,128)(2,1)S(1)}, u32[]{:S(2)}, u32[]{:S(2)}) collective-permute-start(bf16[128,1024]{1,0:T(8,128)(2,1)S(1)} %fusion.16), channel_id=1, source_target_pairs={{0,4},{1,5},{2,3},{3,2},{4,0},{5,1},{6,7},{7,6},{8,12},{9,13},{10,... | collective-permute-start | bytes 786440 | tf_op jit(solution)/shard_map/ppermute | solution.py:335
  113.6 21.3 %collective-permute-start.23 = (bf16[2,128,1024]{2,1,0:T(8,128)(2,1)S(1)}, bf16[2,128,1024]{2,1,0:T(8,128)(2,1)S(1)}, u32[]{:S(2)}, u32[]{:S(2)}) collective-permute-start(bf16[2,128,1024]{2,1,0:T(8,128)(2,1)S(1)} %get-tuple-element.247), channel_id=1, source_target_pairs={{0,1},{1,0},{2,6},{3,7},{4,5},{5,4},{6,2},{7,3},{8,9},{9,8},{10,14... | collective-permute-start | bytes 1572872 | tf_op jit(solution)/shard_map/ppermute | solution.py:335
  117.6 10.6 %collective-permute-start.30 = (bf16[128,1024]{1,0:T(8,128)(2,1)S(1)}, bf16[128,1024]{1,0:T(8,128)(2,1)S(1)}, u32[]{:S(2)}, u32[]{:S(2)}) collective-permute-start(bf16[128,1024]{1,0:T(8,128)(2,1)S(1)} %fusion.7), channel_id=1, source_target_pairs={{0,8},{1,9},{2,10},{3,11},{4,12},{5,13},{6,14},{7,15},{8,24},{9,25... | collective-permute-start | bytes 786440 | tf_op jit(solution)/shard_map/ppermute | solution.py:335
  118.9 9.3 %collective-permute-start.29 = (bf16[128,1024]{1,0:T(8,128)(2,1)S(1)}, bf16[128,1024]{1,0:T(8,128)(2,1)S(1)}, u32[]{:S(2)}, u32[]{:S(2)}) collective-permute-start(bf16[128,1024]{1,0:T(8,128)(2,1)S(1)} %fusion.17), channel_id=1, source_target_pairs={{0,4},{1,5},{2,3},{3,2},{4,0},{5,1},{6,7},{7,6},{8,12},{9,13},{10,... | collective-permute-start | bytes 786440 | tf_op jit(solution)/shard_map/ppermute | solution.py:335
  119.9 16.4 %collective-permute-start.22 = (bf16[2,128,1024]{2,1,0:T(8,128)(2,1)S(1)}, bf16[2,128,1024]{2,1,0:T(8,128)(2,1)S(1)}, u32[]{:S(2)}, u32[]{:S(2)}) collective-permute-start(bf16[2,128,1024]{2,1,0:T(8,128)(2,1)S(1)} %get-tuple-element.248), channel_id=1, source_target_pairs={{0,1},{1,0},{2,6},{3,7},{4,5},{5,4},{6,2},{7,3},{8,9},{9,8},{10,14... | collective-permute-start | bytes 1572872 | tf_op jit(solution)/shard_map/ppermute | solution.py:335
  128.3 8.2 %collective-permute-start.31 = (bf16[128,1024]{1,0:T(8,128)(2,1)S(1)}, bf16[128,1024]{1,0:T(8,128)(2,1)S(1)}, u32[]{:S(2)}, u32[]{:S(2)}) collective-permute-start(bf16[128,1024]{1,0:T(8,128)(2,1)S(1)} %fusion.5), channel_id=1, source_target_pairs={{0,8},{1,9},{2,10},{3,11},{4,12},{5,13},{6,14},{7,15},{8,24},{9,25... | collective-permute-start | bytes 786440 | tf_op jit(solution)/shard_map/ppermute | solution.py:335
  135.2 6.4 %collective-permute-start.24 = (bf16[128,1024]{1,0:T(8,128)(2,1)S(1)}, bf16[128,1024]{1,0:T(8,128)(2,1)S(1)}, u32[]{:S(2)}, u32[]{:S(2)}) collective-permute-start(bf16[128,1024]{1,0:T(8,128)(2,1)S(1)} %fusion.15), channel_id=1, source_target_pairs={{0,4},{1,5},{2,3},{3,2},{4,0},{5,1},{6,7},{7,6},{8,12},{9,13},{10,... | collective-permute-start | bytes 786440 | tf_op jit(solution)/shard_map/ppermute | solution.py:335
  141.7 7.3 %collective-permute-start.33 = (bf16[128,1024]{1,0:T(8,128)(2,1)S(1)}, bf16[128,1024]{1,0:T(8,128)(2,1)S(1)}, u32[]{:S(2)}, u32[]{:S(2)}) collective-permute-start(bf16[128,1024]{1,0:T(8,128)(2,1)S(1)} %fusion.10), channel_id=1, source_target_pairs={{0,8},{1,9},{2,10},{3,11},{4,12},{5,13},{6,14},{7,15},{8,24},{9,25... | collective-permute-start | bytes 786440 | tf_op jit(solution)/shard_map/ppermute | solution.py:335
  142.0 6.4 %collective-permute-start.32 = (bf16[128,1024]{1,0:T(8,128)(2,1)S(1)}, bf16[128,1024]{1,0:T(8,128)(2,1)S(1)}, u32[]{:S(2)}, u32[]{:S(2)}) collective-permute-start(bf16[128,1024]{1,0:T(8,128)(2,1)S(1)} %fusion.14), channel_id=1, source_target_pairs={{0,4},{1,5},{2,3},{3,2},{4,0},{5,1},{6,7},{7,6},{8,12},{9,13},{10,... | collective-permute-start | bytes 786440 | tf_op jit(solution)/shard_map/ppermute | solution.py:335

commit v12 on v11

--- a/solution.py
+++ b/solution.py
@@ -10,7 +10,7 @@
 CONTRACT_LAST = (((1,), (1,)), ((), ()))
 CONTRACT_FIRST = (((0,), (0,)), ((), ()))
 INFO_ROWS = 16
-VMEM_LIMIT = 16 * 1024 * 1024
+VMEM_LIMIT = 8 * 1024 * 1024
 
 
 def pack_rows(token_rows, grad_rows, token_of, scale, is_live):
@@ -130,28 +130,9 @@
         in_specs=[vmem] * 4,
         out_specs=vmem,
         out_shape=jax.ShapeDtypeStruct((2 * rows + INFO_ROWS, width), jnp.bfloat16),
+        compiler_params=pltpu.CompilerParams(vmem_limit_bytes=VMEM_LIMIT),
         name="pack",
     )(tokens, out_grad, routes.T, combine.T)
-
-
-def load_kernel(*refs):
-    count = (len(refs) - 1) // 2
-    moves = [pltpu.make_async_copy(refs[i], refs[count + i], refs[-1].at[i]) for i in range(count)]
-    for move in moves:
-        move.start()
-    for move in moves:
-        move.wait()
-
-
-def load_weights(weights):
-    return pl.pallas_call(
-        load_kernel,
-        in_specs=[pl.BlockSpec(memory_space=pltpu.HBM)] * len(weights),
-        out_specs=[pl.BlockSpec(memory_space=pltpu.VMEM)] * len(weights),
-        out_shape=[jax.ShapeDtypeStruct(w.shape, w.dtype) for w in weights],
-        scratch_shapes=[pltpu.SemaphoreType.DMA((len(weights),))],
-        name="load",
-    )(*weights)
 
 
 def pick_kernel(top, rows, place_ref, *refs):
@@ -349,7 +330,7 @@
     me = lax.axis_index("expert")
     place = jnp.stack([me, lax.axis_index("etp"), me % 2]).astype(jnp.int32)
     share = pack_share(tokens, out_grad, routes, combine)
-    weights = load_weights((w_gate[0], w_up[0], w_down[0]))
+    weights = (w_gate[0], w_up[0], w_down[0])
 
     def tied(values, mark):
         return lax.optimization_barrier((values, mark))[0]
@@ -398,35 +379,49 @@
         if ready is not None:
             late.append(ready)
         needed = {key: have[key] for key in have if key[1] >= done}
-        listed = sorted(came, reverse=True)
-        values, have, picked, parts, waiting, late, weights = lax.optimization_barrier(
-            ([came[key] for key in listed], needed, picked, parts, waiting, late, weights)
-        )
+        listed = sorted(came)
+        held = (needed, picked, parts, waiting if plane_sends else None, late)
+        values, (have, picked, parts, held, late) = lax.optimization_barrier(([came[key] for key in listed], held))
+        waiting = held if plane_sends else waiting
         came = dict(zip(listed, values))
         have.update(came)
     mine, theirs, picks = pick_rows(place, [have[kind, done] for kind in "sfab"], top, rows, pair_slots)
-    unsent, late = late, []
+    unsent, late, early = late, [], None
     if waiting is not None:
         keep, send = waiting
-        late.append((keep, to_second(tied(send, theirs))))
+        came, parts = lax.optimization_barrier((to_second(send), parts))
+        late.append((keep, came))
     if parts is not None:
         keep, send = placed(*tied(parts, theirs))
         late.append((keep, to_second(send)))
+        mine = tied(mine, send)
     near, far, *kept = run_experts(done, chunks, mine, to_core(theirs), weights, kept)
+    if len(unsent) == 1 and late:
+        pair = added(*late[0])
+        came, near, far = lax.optimization_barrier((to_first(pair[1].astype(jnp.bfloat16)), near, far))
+        early = added(pair[0], came)
+        if len(late) > 1:
+            keep, came = late[1]
+            came, near = lax.optimization_barrier((came, near))
+            late[1] = keep, came
     keep, send = placed(picks, near, far)
     late.append((keep, to_second(send)))
     late = [(keep, to_second(tied(first, send))) for keep, first in unsent] + late
     marks = [send] * (chunks + 2)
     running = None
     for c in range(1, chunks):
-        keep, came = late[c]
-        if c + 1 < chunks:
-            came = tied(came, near if c == 1 else marks[0])
-        pair = added(keep, came)
-        came = to_first(pair[1].astype(jnp.bfloat16))
-        total = added(pair[0], came if c + 1 == chunks else tied(came, send))
+        if c == 1 and early is not None:
+            total = early
+        else:
+            keep, came = late[c]
+            if c + 1 < chunks:
+                came = tied(came, near if c == 1 else send)
+            pair = added(keep, came)
+            came = to_first(pair[1].astype(jnp.bfloat16))
+            total = added(pair[0], came if c + 1 == chunks else tied(came, send))
         running = (total if running is None else added(total, running)).astype(jnp.bfloat16)
-        marks[min(c - 1, 2)] = running
+        if c > 1:
+            marks[min(c - 1, 2)] = running
         if c + 1 < chunks:
             running = to_ring(running)
     keep, came = late[0]

time: 150 us -> 151 us (level)
  waiting for transfers between devices: 62.7 us -> 68.9 us
  Pallas kernels: 38 us -> 31.9 us
  local copies, waits for them, and re-layouts: 5.29 us -> 8.98 us
  starting transfers between devices: 31 us -> 27.9 us
    ppermute x34, waiting for transfers between devices: 62.7 us -> 68.9 us  [permute(): return lax.ppermute(value, ('expert', 'etp'), pairs)]
    pallas_call x1 -> x0, Pallas kernels: 4.62 us -> none  [load_weights(): pl.pallas_call(load_kernel, in_specs=[pl.BlockSpec(memory_space=pltpu.HBM...]
    unnamed x18 -> x26, local copies, waits for them, and re-layouts: 5.16 us -> 8.85 us
    ppermute x34, starting transfers between devices: 31 us -> 27.9 us  [permute(): return lax.ppermute(value, ('expert', 'etp'), pairs)]
    pallas_call x1, Pallas kernels: 1.89 us -> 0.05 us  [pack_share(): pl.pallas_call(pack_kernel, in_specs=[vmem] * 4, out_specs=vmem, out_shap...]
  transfers between devices with their start and end apart: 34 -> 34, of which waited for: 18 -> 17; matrix products, arithmetic and copies ran while one was open for 7% -> 7% of each run, Pallas kernels for 23% -> 21%
where the time goes in v12:
time: 151 us
  waiting for transfers between devices  68.9 us (46%)
  Pallas kernels  31.9 us (21%)
  starting transfers between devices  27.9 us (18%)
  matrix products  10.2 us (7%)
  local copies, waits for them, and re-layouts  8.98 us (6%)
  other arithmetic  1.82 us (1%)
    ppermute x34, waiting for transfers between devices, permute(): return lax.ppermute(value, ('expert', 'etp'), pairs)  68.9 us
    ppermute x34, starting transfers between devices, permute(): return lax.ppermute(value, ('expert', 'etp'), pairs)  27.9 us
    pallas_call x4, Pallas kernels, run_experts(): pl.pallas_call(functools.partial(expert_kernel, index, kept is not None),...  19.7 us
    unnamed x26, local copies, waits for them, and re-layouts  8.85 us
    pallas_call x4, Pallas kernels, pick_rows(): pl.pallas_call(functools.partial(pick_kernel, top, rows), in_specs=[pl.Bl...  7.09 us
    pallas_call x4, Pallas kernels, place_rows(): pl.pallas_call(place_kernel, in_specs=[pl.BlockSpec(memory_space=pltpu.SM...  5.08 us
    dot_general x1, matrix products, gather_body(): lax.dot_general(gate_term, rows_x, CONTRACT_FIRST, preferred_element_type...  3.4 us
    dot_general x1, matrix products, gather_body(): lax.dot_general(up_term, rows_x, CONTRACT_FIRST, preferred_element_type=j...  3.4 us
  transfers between devices with their start and end apart: 34, of which 17 were waited for; matrix products, arithmetic and copies ran while one was open for 7% of the time, Pallas kernels for 21%

profile of v12, /device:TPU:0, one launch (start us, length us, event | category | flops | bytes accessed | tf_op | source)
XLA Modules:
  0.0 150.6 jit_solution(15997691269757958262)
XLA Ops:
  0.6 0.9 copy-done.9
  1.6 0.9 copy-done.10
  4.0 3.0 %collective-permute-start = (bf16[272,1024]{1,0:T(8,128)(2,1)S(1)}, bf16[272,1024]{1,0:T(8,128)(2,1)S(1)}, u32[]{:S(2)}, u32[]{:S(2)}) collective-permute-start(bf16[272,1024]{1,0:T(8,128)(2,1)S(1)} %pack.1.refs_0_), channel_id=1, source_target_pairs={{0,1},{1,0},{2,6},{3,7},{4,5},{5,4},{6,2},{7,3},{8,9},{9,8},{10,14... | collective-permute-start | bytes 1671176 | tf_op jit(solution)/shard_map/ppermute | solution.py:316
  7.0 1.5 %collective-permute-start.1 = (bf16[272,1024]{1,0:T(8,128)(2,1)S(1)}, bf16[272,1024]{1,0:T(8,128)(2,1)S(1)}, u32[]{:S(2)}, u32[]{:S(2)}) collective-permute-start(bf16[272,1024]{1,0:T(8,128)(2,1)S(1)} %pack.1.refs_0_), channel_id=1, source_target_pairs={{0,4},{1,5},{2,3},{3,2},{4,0},{5,1},{6,7},{7,6},{8,12},{9,13},{10,... | collective-permute-start | bytes 1671176 | tf_op jit(solution)/shard_map/ppermute | solution.py:316
  8.5 1.6 %collective-permute-start.2 = (bf16[272,1024]{1,0:T(8,128)(2,1)S(1)}, bf16[272,1024]{1,0:T(8,128)(2,1)}, u32[]{:S(2)}, u32[]{:S(2)}) collective-permute-start(bf16[272,1024]{1,0:T(8,128)(2,1)S(1)} %pack.1.refs_0_), channel_id=1, source_target_pairs={{0,8},{1,9},{2,10},{3,11},{4,12},{5,13},{6,14},{7,15},{8,24},{9,25... | collective-permute-start | bytes 1671176 | tf_op jit(solution)/shard_map/ppermute | solution.py:316
  10.1 9.8 %collective-permute-done.refs_2_ = bf16[272,1024]{1,0:T(8,128)(2,1)S(1)} collective-permute-done((bf16[272,1024]{1,0:T(8,128)(2,1)S(1)}, bf16[272,1024]{1,0:T(8,128)(2,1)S(1)}, u32[]{:S(2)}, u32[]{:S(2)}) %collective-permute-start) | collective-permute-done | bytes 557088 | tf_op jit(solution)/shard_map/ppermute | solution.py:316
  20.7 2.6 %collective-permute-done.2.refs_0_ = bf16[272,1024]{1,0:T(8,128)(2,1)} collective-permute-done((bf16[272,1024]{1,0:T(8,128)(2,1)S(1)}, bf16[272,1024]{1,0:T(8,128)(2,1)}, u32[]{:S(2)}, u32[]{:S(2)}) %collective-permute-start.2) | collective-permute-done | bytes 557088 | tf_op jit(solution)/shard_map/ppermute | solution.py:316
  24.5 1.0 collective-permute-start.3
  26.3 12.1 %collective-permute-done.4.refs_1_ = bf16[272,1024]{1,0:T(8,128)(2,1)} collective-permute-done((bf16[272,1024]{1,0:T(8,128)(2,1)}, bf16[272,1024]{1,0:T(8,128)(2,1)}, u32[]{:S(2)}, u32[]{:S(2)}) %collective-permute-start.4) | collective-permute-done | bytes 557088 | tf_op jit(solution)/shard_map/ppermute | solution.py:316
  39.8 0.9 collective-permute-start.8
  40.7 1.0 collective-permute-start.6
  41.9 1.1 copy-done.4
  42.9 1.1 copy-done.6
  44.0 1.1 copy-done.8
  45.0 1.5 %pick.4 = (bf16[2,144,2048]{2,1,0:T(8,128)(2,1)S(1)}, bf16[2,144,2048]{2,1,0:T(8,128)(2,1)S(1)}, bf16[288,256]{1,0:T(8,128)(2,1)S(1)}) custom-call(s32[3]{0:T(128)S(1)} %pad_add_fusion.place_ref, bf16[272,1024]{1,0:T(8,128)(2,1)S(1)} %pack.1.refs_0_, bf16[272,1024]{1,0:T(8,128)(2,1)S(1)} %copy-done.6, bf16[272,1024]{1,0:T(8,128)(2,1)S(1)} %copy-done.4, ...), custom_call_target="tpu_custom_call" | custom-call | tf_op jit(solution)/shard_map/pick/pallas_call | solution.py:252
  46.6 2.5 %collective-permute-done.7.refs_3_ = bf16[272,1024]{1,0:T(8,128)(2,1)} collective-permute-done((bf16[272,1024]{1,0:T(8,128)(2,1)}, bf16[272,1024]{1,0:T(8,128)(2,1)}, u32[]{:S(2)}, u32[]{:S(2)}) %collective-permute-start.7) | collective-permute-done | bytes 557088 | tf_op jit(solution)/shard_map/ppermute | solution.py:316
  49.0 5.2 %collective-permute-done.8.refs_1_ = bf16[272,1024]{1,0:T(8,128)(2,1)S(1)} collective-permute-done((bf16[272,1024]{1,0:T(8,128)(2,1)}, bf16[272,1024]{1,0:T(8,128)(2,1)S(1)}, u32[]{:S(2)}, u32[]{:S(2)}) %collective-permute-start.8) | collective-permute-done | bytes 557088 | tf_op jit(solution)/shard_map/ppermute | solution.py:316
  55.7 0.9 collective-permute-start.11
  56.6 1.0 collective-permute-start.9
  57.6 2.5 %pick.5 = (bf16[2,144,2048]{2,1,0:T(8,128)(2,1)S(1)}, bf16[2,144,2048]{2,1,0:T(8,128)(2,1)S(1)}, bf16[288,256]{1,0:T(8,128)(2,1)S(1)}) custom-call(s32[3]{0:T(128)S(1)} %pad_add_fusion.place_ref, bf16[272,1024]{1,0:T(8,128)(2,1)} %collective-permute-done.2.refs_0_, bf16[272,1024]{1,0:T(8,128)(2,1)} %collective-permute-done.4.refs_1_, ...), custom_call_target="tpu_custom_call" | custom-call | tf_op jit(solution)/shard_map/pick/pallas_call | solution.py:252
  60.2 4.9 %experts.4 = (bf16[144,2048]{1,0:T(8,128)(2,1)S(1)}, bf16[144,2048]{1,0:T(8,128)(2,1)S(1)}, bf16[1152,2048]{1,0:T(8,128)(2,1)S(1)}, bf16[1152,2048]{1,0:T(8,128)...) custom-call(bf16[2,144,2048]{2,1,0:T(8,128)(2,1)S(1)} %get-tuple-element.147., ...), custom_call_target="tpu_custom_call" | custom-call | tf_op jit(solution)/shard_map/experts/pallas_call | solution.py:271
  65.1 6.6 %collective-permute-done.11.refs_0_ = bf16[272,1024]{1,0:T(8,128)(2,1)S(1)} collective-permute-done((bf16[272,1024]{1,0:T(8,128)(2,1)S(1)}, bf16[272,1024]{1,0:T(8,128)(2,1)S(1)}, u32[]{:S(2)}, u32[]{:S(2)}) %collective-permute-start.11) | collective-permute-done | bytes 557088 | tf_op jit(solution)/shard_map/ppermute | solution.py:316
  73.1 1.5 %pick.6 = (bf16[2,144,2048]{2,1,0:T(8,128)(2,1)S(1)}, bf16[2,144,2048]{2,1,0:T(8,128)(2,1)S(1)}, bf16[288,256]{1,0:T(8,128)(2,1)S(1)}) custom-call(s32[3]{0:T(128)S(1)} %pad_add_fusion.place_ref, bf16[272,1024]{1,0:T(8,128)(2,1)S(1)} %collective-permute-done.5.refs_0_, bf16[272,1024]{1,0:T(8,128)(2,1)S(1)} %collective-permute-done.8.refs_1_, ...), custom_call_target="tpu_custom_call" | custom-call | tf_op jit(solution)/shard_map/pick/pallas_call | solution.py:252
  75.3 1.3 place.4
  76.6 5.1 %experts.5 = (bf16[144,2048]{1,0:T(8,128)(2,1)S(1)}, bf16[144,2048]{1,0:T(8,128)(2,1)S(1)}, bf16[1152,2048]{1,0:T(8,128)(2,1)S(1)}, bf16[1152,2048]{1,0:T(8,128)...) custom-call(bf16[2,144,2048]{2,1,0:T(8,128)(2,1)S(1)} %get-tuple-ele, ...), custom_call_target="tpu_custom_call", output_to_operand_aliasing={{2}: (5, {}), {3}: (6, {}), {4}: (7, {}), {5}: (8, {}), {6}... | custom-call | tf_op jit(solution)/shard_map/experts/pallas_call | solution.py:271
  81.7 6.7 %collective-permute-done.14.refs_1_ = bf16[272,1024]{1,0:T(8,128)(2,1)S(1)} collective-permute-done((bf16[272,1024]{1,0:T(8,128)(2,1)S(1)}, bf16[272,1024]{1,0:T(8,128)(2,1)S(1)}, u32[]{:S(2)}, u32[]{:S(2)}) %collective-permute-start.14) | collective-permute-done | bytes 557088 | tf_op jit(solution)/shard_map/ppermute | solution.py:316
  89.5 2.5 %collective-permute-done.19.far_ref = bf16[144,2048]{1,0:T(8,128)(2,1)S(1)} collective-permute-done((bf16[144,2048]{1,0:T(8,128)(2,1)S(1)}, bf16[144,2048]{1,0:T(8,128)(2,1)S(1)}, u32[]{:S(2)}, u32[]{:S(2)}) %collective-permute-start.19) | collective-permute-done | bytes 589856 | tf_op jit(solution)/shard_map/ppermute | solution.py:316
  92.0 1.3 place.5
  94.1 4.9 %experts.6 = (bf16[144,2048]{1,0:T(8,128)(2,1)S(1)}, bf16[144,2048]{1,0:T(8,128)(2,1)S(1)}, bf16[1152,2048]{1,0:T(8,128)(2,1)S(1)}, bf16[1152,2048]{1,0:T(8,128)...) custom-call(bf16[2,144,2048]{2,1,0:T(8,128)(2,1)S(1)} %get-tuple-ele, ...), custom_call_target="tpu_custom_call", output_to_operand_aliasing={{2}: (5, {}), {3}: (6, {}), {4}: (7, {}), {5}: (8, {}), {6}... | custom-call | tf_op jit(solution)/shard_map/experts/pallas_call | solution.py:271
  99.0 1.5 %pick.7 = (bf16[2,144,2048]{2,1,0:T(8,128)(2,1)S(1)}, bf16[2,144,2048]{2,1,0:T(8,128)(2,1)S(1)}, bf16[288,256]{1,0:T(8,128)(2,1)S(1)}) custom-call(s32[3]{0:T(128)S(1)} %pad_add_fusion.place_ref, bf16[272,1024]{1,0:T(8,128)(2,1)S(1)} %collective-permute-done.11.refs_0_, bf16[272,1024]{1,0:T(8,128)(2,1)S(1)} %collective-permute-done.14.refs_1_, ...), custom_call_target="tpu_custom_call" | custom-call | tf_op jit(solution)/shard_map/pick/pallas_call | solution.py:252
  100.7 3.3 %collective-permute-done.20 = bf16[2,128,1024]{2,1,0:T(8,128)(2,1)S(1)} collective-permute-done((bf16[2,128,1024]{2,1,0:T(8,128)(2,1)S(1)}, bf16[2,128,1024]{2,1,0:T(8,128)(2,1)S(1)}, u32[]{:S(2)}, u32[]{:S(2)}) %collective-permute-start.20) | collective-permute-done | bytes 524320 | tf_op jit(solution)/shard_map/ppermute | solution.py:316
  104.2 1.0 collective-permute-start.23
  106.0 1.3 place.6
  108.0 4.9 %experts.7 = (bf16[144,2048]{1,0:T(8,128)(2,1)S(1)}, bf16[144,2048]{1,0:T(8,128)(2,1)S(1)}, bf16[1152,2048]{1,0:T(8,128)(2,1)S(1)}, bf16[1152,2048]{1,0:T(8,128)...) custom-call(bf16[2,144,2048]{2,1,0:T(8,128)(2,1)S(1)} %get-tuple-ele, ...), custom_call_target="tpu_custom_call", output_to_operand_aliasing={{2}: (5, {}), {3}: (6, {}), {4}: (7, {}), {5}: (8, {}), {6}... | custom-call | tf_op jit(solution)/shard_map/experts/pallas_call | solution.py:271
  113.2 3.4 %collective-permute-done.22 = bf16[2,128,1024]{2,1,0:T(8,128)(2,1)S(1)} collective-permute-done((bf16[2,128,1024]{2,1,0:T(8,128)(2,1)S(1)}, bf16[2,128,1024]{2,1,0:T(8,128)(2,1)S(1)}, u32[]{:S(2)}, u32[]{:S(2)}) %collective-permute-start.22) | collective-permute-done | bytes 524320 | tf_op jit(solution)/shard_map/ppermute | solution.py:316
  117.4 1.3 place.7
  119.5 0.9 collective-permute-start.29
  120.4 1.1 collective-permute-start.26
  121.5 3.4 %fusion.2 = bf16[1,384,2048]{2,1,0:T(8,128)(2,1)} fusion(bf16[1152,384]{1,0:T(8,128)(2,1)S(1)} %get-tuple-element.240, bf16[1152,2048]{1,0:T(8,128)(2,1)S(1)} %get-tuple-element.241), kind=kOutput, calls=%fused_computation.5 | convolution fusion | flops 1812725760 | bytes 7176192 | tf_op jit(solution)/shard_map/dot_general | solution.py:434
  124.9 3.9 %collective-permute-done.29 = bf16[128,1024]{1,0:T(8,128)(2,1)S(1)} collective-permute-done((bf16[128,1024]{1,0:T(8,128)(2,1)S(1)}, bf16[128,1024]{1,0:T(8,128)(2,1)S(1)}, u32[]{:S(2)}, u32[]{:S(2)}) %collective-permute-start.29) | collective-permute-done | bytes 262176 | tf_op jit(solution)/shard_map/ppermute | solution.py:316
  128.9 3.4 %collective-permute-start.31 = (bf16[128,1024]{1,0:T(8,128)(2,1)S(1)}, bf16[128,1024]{1,0:T(8,128)(2,1)S(1)}, u32[]{:S(2)}, u32[]{:S(2)}) collective-permute-start(bf16[128,1024]{1,0:T(8,128)(2,1)S(1)} %fusion.7), channel_id=1, source_target_pairs={{0,8},{1,9},{2,10},{3,11},{4,12},{5,13},{6,14},{7,15},{8,24},{9,25... | collective-permute-start | bytes 786440 | tf_op jit(solution)/shard_map/ppermute | solution.py:316
  132.3 3.4 %fusion = bf16[1,384,2048]{2,1,0:T(8,128)(2,1)} fusion(bf16[1152,384]{1,0:T(8,128)(2,1)S(1)} %get-tuple-element.235, bf16[1152,2048]{1,0:T(8,128)(2,1)S(1)} %get-tuple-element.236), kind=kOutput, calls=%fused_computation.3 | convolution fusion | flops 1812725760 | bytes 7176192 | tf_op jit(solution)/shard_map/dot_general | solution.py:435
  136.0 0.9 collective-permute-start.28
  137.2 5.2 %collective-permute-done.28 = bf16[128,1024]{1,0:T(8,128)(2,1)S(1)} collective-permute-done((bf16[128,1024]{1,0:T(8,128)(2,1)S(1)}, bf16[128,1024]{1,0:T(8,128)(2,1)S(1)}, u32[]{:S(2)}, u32[]{:S(2)}) %collective-permute-start.28) | collective-permute-done | bytes 262176 | tf_op jit(solution)/shard_map/ppermute | solution.py:316
  142.6 0.9 collective-permute-start.32
  143.5 3.4 %fusion.1 = bf16[1,384,2048]{2,1,0:T(8,128)(2,1)} fusion(bf16[1152,384]{1,0:T(8,128)(2,1)S(1)} %get-tuple-element.238, bf16[1152,2048]{1,0:T(8,128)(2,1)S(1)} %get-tuple-element.236), kind=kOutput, calls=%fused_computation.4 | convolution fusion | flops 1812725760 | bytes 7176192 | tf_op jit(solution)/shard_map/dot_general | solution.py:436
  146.9 2.1 %collective-permute-done.32 = bf16[128,1024]{1,0:T(8,128)(2,1)S(1)} collective-permute-done((bf16[128,1024]{1,0:T(8,128)(2,1)S(1)}, bf16[128,1024]{1,0:T(8,128)(2,1)S(1)}, u32[]{:S(2)}, u32[]{:S(2)}) %collective-permute-start.32) | collective-permute-done | bytes 262176 | tf_op jit(solution)/shard_map/ppermute | solution.py:316
  149.0 0.8 collective-permute-done.33
  (75 shorter events, 16.6 us)
Async XLA Ops:
  0.6 1.0 copy-start.9
  1.6 0.9 copy-start.10
  2.5 0.7 copy-start.11
  3.2 0.7 copy-start.12
  3.9 56.2 %copy-start.2 = (bf16[1,384,2048]{2,1,0:T(8,128)(2,1)S(1)}, bf16[1,384,2048]{2,1,0:T(8,128)(2,1)}, u32[]{:S(2)}) copy-start(bf16[1,384,2048]{2,1,0:T(8,128)(2,1)} %param.13) | copy-start | bytes 4718596
  4.0 15.9 %collective-permute-start = (bf16[272,1024]{1,0:T(8,128)(2,1)S(1)}, bf16[272,1024]{1,0:T(8,128)(2,1)S(1)}, u32[]{:S(2)}, u32[]{:S(2)}) collective-permute-start(bf16[272,1024]{1,0:T(8,128)(2,1)S(1)} %pack.1.refs_0_), channel_id=1, source_target_pairs={{0,1},{1,0},{2,6},{3,7},{4,5},{5,4},{6,2},{7,3},{8,9},{9,8},{10,14... | collective-permute-start | bytes 1671176 | tf_op jit(solution)/shard_map/ppermute | solution.py:316
  7.0 13.7 %collective-permute-start.1 = (bf16[272,1024]{1,0:T(8,128)(2,1)S(1)}, bf16[272,1024]{1,0:T(8,128)(2,1)S(1)}, u32[]{:S(2)}, u32[]{:S(2)}) collective-permute-start(bf16[272,1024]{1,0:T(8,128)(2,1)S(1)} %pack.1.refs_0_), channel_id=1, source_target_pairs={{0,4},{1,5},{2,3},{3,2},{4,0},{5,1},{6,7},{7,6},{8,12},{9,13},{10,... | collective-permute-start | bytes 1671176 | tf_op jit(solution)/shard_map/ppermute | solution.py:316
  8.5 14.8 %collective-permute-start.2 = (bf16[272,1024]{1,0:T(8,128)(2,1)S(1)}, bf16[272,1024]{1,0:T(8,128)(2,1)}, u32[]{:S(2)}, u32[]{:S(2)}) collective-permute-start(bf16[272,1024]{1,0:T(8,128)(2,1)S(1)} %pack.1.refs_0_), channel_id=1, source_target_pairs={{0,8},{1,9},{2,10},{3,11},{4,12},{5,13},{6,14},{7,15},{8,24},{9,25... | collective-permute-start | bytes 1671176 | tf_op jit(solution)/shard_map/ppermute | solution.py:316
  19.9 0.8 copy-start.3
  23.3 15.1 %collective-permute-start.4 = (bf16[272,1024]{1,0:T(8,128)(2,1)}, bf16[272,1024]{1,0:T(8,128)(2,1)}, u32[]{:S(2)}, u32[]{:S(2)}) collective-permute-start(bf16[272,1024]{1,0:T(8,128)(2,1)} %collective-permute-done.2.refs_0_), channel_id=1, source_target_pairs={{0,4},{1,5},{2,3},{3,2},{4,0},{5,1},{6,7},{7,6},{8,12},{9,13},{10,... | collective-permute-start | bytes 1671176 | tf_op jit(solution)/shard_map/ppermute | solution.py:316
  23.8 14.6 %collective-permute-start.5 = (bf16[272,1024]{1,0:T(8,128)(2,1)}, bf16[272,1024]{1,0:T(8,128)(2,1)S(1)}, u32[]{:S(2)}, u32[]{:S(2)}) collective-permute-start(bf16[272,1024]{1,0:T(8,128)(2,1)} %collective-permute-done.2.refs_0_), channel_id=1, source_target_pairs={{0,8},{1,9},{2,10},{3,11},{4,12},{5,13},{6,14},{7,15},{8,24},{9,25... | collective-permute-start | bytes 1671176 | tf_op jit(solution)/shard_map/ppermute | solution.py:316
  24.5 13.9 %collective-permute-start.3 = (bf16[272,1024]{1,0:T(8,128)(2,1)S(1)}, bf16[272,1024]{1,0:T(8,128)(2,1)S(1)}, u32[]{:S(2)}, u32[]{:S(2)}) collective-permute-start(bf16[272,1024]{1,0:T(8,128)(2,1)S(1)} %collective-permute-done.1.refs_1_), channel_id=1, source_target_pairs={{0,1},{1,0},{2,6},{3,7},{4,5},{5,4},{6,2},{7,3},{8,9},{9,8},{10,14... | collective-permute-start | bytes 1671176 | tf_op jit(solution)/shard_map/ppermute | solution.py:316
  25.5 0.8 copy-start.5
  38.4 0.8 copy-start.7
  39.2 9.8 %collective-permute-start.7 = (bf16[272,1024]{1,0:T(8,128)(2,1)}, bf16[272,1024]{1,0:T(8,128)(2,1)}, u32[]{:S(2)}, u32[]{:S(2)}) collective-permute-start(bf16[272,1024]{1,0:T(8,128)(2,1)} %collective-permute-done.4.refs_1_), channel_id=1, source_target_pairs={{0,1},{1,0},{2,6},{3,7},{4,5},{5,4},{6,2},{7,3},{8,9},{9,8},{10,14... | collective-permute-start | bytes 1671176 | tf_op jit(solution)/shard_map/ppermute | solution.py:316
  39.8 14.4 %collective-permute-start.8 = (bf16[272,1024]{1,0:T(8,128)(2,1)}, bf16[272,1024]{1,0:T(8,128)(2,1)S(1)}, u32[]{:S(2)}, u32[]{:S(2)}) collective-permute-start(bf16[272,1024]{1,0:T(8,128)(2,1)} %collective-permute-done.4.refs_1_), channel_id=1, source_target_pairs={{0,8},{1,9},{2,10},{3,11},{4,12},{5,13},{6,14},{7,15},{8,24},{9,25... | collective-permute-start | bytes 1671176 | tf_op jit(solution)/shard_map/ppermute | solution.py:316
  40.7 14.3 %collective-permute-start.6 = (bf16[272,1024]{1,0:T(8,128)(2,1)}, bf16[272,1024]{1,0:T(8,128)(2,1)}, u32[]{:S(2)}, u32[]{:S(2)}) collective-permute-start(bf16[272,1024]{1,0:T(8,128)(2,1)} %collective-permute-done.2.refs_0_), channel_id=1, source_target_pairs={{0,1},{1,0},{2,6},{3,7},{4,5},{5,4},{6,2},{7,3},{8,9},{9,8},{10,14... | collective-permute-start | bytes 1671176 | tf_op jit(solution)/shard_map/ppermute | solution.py:316
  41.9 1.1 copy-start.4
  42.9 1.1 copy-start.6
  44.0 1.1 copy-start.8
  45.0 15.1 %copy-start.1 = (bf16[1,384,2048]{2,1,0:T(8,128)(2,1)S(1)}, bf16[1,384,2048]{2,1,0:T(8,128)(2,1)}, u32[]{:S(2)}) copy-start(bf16[1,384,2048]{2,1,0:T(8,128)(2,1)} %param.12) | copy-start | bytes 4718596
  46.5 13.6 %copy-start = (bf16[1,384,2048]{2,1,0:T(8,128)(2,1)S(1)}, bf16[1,384,2048]{2,1,0:T(8,128)(2,1)}, u32[]{:S(2)}) copy-start(bf16[1,384,2048]{2,1,0:T(8,128)(2,1)} %param.11) | copy-start | bytes 4718596
  55.0 5.1 %collective-permute-start.12 = (bf16[2,144,2048]{2,1,0:T(8,128)(2,1)S(1)}, bf16[2,144,2048]{2,1,0:T(8,128)(2,1)S(1)}, u32[]{:S(2)}, u32[]{:S(2)}) collective-permute-start(bf16[2,144,2048]{2,1,0:T(8,128)(2,1)S(1)} %get-tuple-element.148), channel_id=1, source_target_pairs={{0,2},{1,3},{2,0},{3,1},{4,6},{5,7},{6,4},{7,5},{8,10},{9,11},{10,... | collective-permute-start | bytes 3538952 | tf_op jit(solution)/shard_map/ppermute | solution.py:316
  55.0 10.1 %collective-permute-start.10 = (bf16[272,1024]{1,0:T(8,128)(2,1)S(1)}, bf16[272,1024]{1,0:T(8,128)(2,1)S(1)}, u32[]{:S(2)}, u32[]{:S(2)}) collective-permute-start(bf16[272,1024]{1,0:T(8,128)(2,1)S(1)} %collective-permute-done.8.refs_1_), channel_id=1, source_target_pairs={{0,1},{1,0},{2,6},{3,7},{4,5},{5,4},{6,2},{7,3},{8,9},{9,8},{10,14... | collective-permute-start | bytes 1671176 | tf_op jit(solution)/shard_map/ppermute | solution.py:316
  55.7 16.0 %collective-permute-start.11 = (bf16[272,1024]{1,0:T(8,128)(2,1)S(1)}, bf16[272,1024]{1,0:T(8,128)(2,1)S(1)}, u32[]{:S(2)}, u32[]{:S(2)}) collective-permute-start(bf16[272,1024]{1,0:T(8,128)(2,1)S(1)} %collective-permute-done.5.refs_0_), channel_id=1, source_target_pairs={{0,8},{1,9},{2,10},{3,11},{4,12},{5,13},{6,14},{7,15},{8,24},{9,25... | collective-permute-start | bytes 1671176 | tf_op jit(solution)/shard_map/ppermute | solution.py:316
  56.6 15.1 %collective-permute-start.9 = (bf16[272,1024]{1,0:T(8,128)(2,1)S(1)}, bf16[272,1024]{1,0:T(8,128)(2,1)S(1)}, u32[]{:S(2)}, u32[]{:S(2)}) collective-permute-start(bf16[272,1024]{1,0:T(8,128)(2,1)S(1)} %collective-permute-done.5.refs_0_), channel_id=1, source_target_pairs={{0,1},{1,0},{2,6},{3,7},{4,5},{5,4},{6,2},{7,3},{8,9},{9,8},{10,14... | collective-permute-start | bytes 1671176 | tf_op jit(solution)/shard_map/ppermute | solution.py:316
  71.6 5.0 %collective-permute-start.15 = (bf16[2,144,2048]{2,1,0:T(8,128)(2,1)S(1)}, bf16[2,144,2048]{2,1,0:T(8,128)(2,1)S(1)}, u32[]{:S(2)}, u32[]{:S(2)}) collective-permute-start(bf16[2,144,2048]{2,1,0:T(8,128)(2,1)S(1)} %get-tuple-element.161), channel_id=1, source_target_pairs={{0,2},{1,3},{2,0},{3,1},{4,6},{5,7},{6,4},{7,5},{8,10},{9,11},{10,... | collective-permute-start | bytes 3538952 | tf_op jit(solution)/shard_map/ppermute | solution.py:316
  71.6 3.7 %collective-permute-start.16 = (bf16[144,2048]{1,0:T(8,128)(2,1)S(1)}, bf16[144,2048]{1,0:T(8,128)(2,1)S(1)}, u32[]{:S(2)}, u32[]{:S(2)}) collective-permute-start(bf16[144,2048]{1,0:T(8,128)(2,1)S(1)} %get-tuple-element.171), channel_id=1, source_target_pairs={{0,2},{1,3},{2,0},{3,1},{4,6},{5,7},{6,4},{7,5},{8,10},{9,11},{10,... | collective-permute-start | bytes 1769480 | tf_op jit(solution)/shard_map/ppermute | solution.py:316
  72.1 9.6 %collective-permute-start.13 = (bf16[272,1024]{1,0:T(8,128)(2,1)S(1)}, bf16[272,1024]{1,0:T(8,128)(2,1)S(1)}, u32[]{:S(2)}, u32[]{:S(2)}) collective-permute-start(bf16[272,1024]{1,0:T(8,128)(2,1)S(1)} %collective-permute-done.11.refs_0_), channel_id=1, source_target_pairs={{0,1},{1,0},{2,6},{3,7},{4,5},{5,4},{6,2},{7,3},{8,9},{9,8},{10,14... | collective-permute-start | bytes 1671176 | tf_op jit(solution)/shard_map/ppermute | solution.py:316
  72.7 15.7 %collective-permute-start.14 = (bf16[272,1024]{1,0:T(8,128)(2,1)S(1)}, bf16[272,1024]{1,0:T(8,128)(2,1)S(1)}, u32[]{:S(2)}, u32[]{:S(2)}) collective-permute-start(bf16[272,1024]{1,0:T(8,128)(2,1)S(1)} %collective-permute-done.8.refs_1_), channel_id=1, source_target_pairs={{0,8},{1,9},{2,10},{3,11},{4,12},{5,13},{6,14},{7,15},{8,24},{9,25... | collective-permute-start | bytes 1671176 | tf_op jit(solution)/shard_map/ppermute | solution.py:316
  88.3 5.7 %collective-permute-start.18 = (bf16[2,144,2048]{2,1,0:T(8,128)(2,1)S(1)}, bf16[2,144,2048]{2,1,0:T(8,128)(2,1)S(1)}, u32[]{:S(2)}, u32[]{:S(2)}) collective-permute-start(bf16[2,144,2048]{2,1,0:T(8,128)(2,1)S(1)} %get-tuple-element.179), channel_id=1, source_target_pairs={{0,2},{1,3},{2,0},{3,1},{4,6},{5,7},{6,4},{7,5},{8,10},{9,11},{10,... | collective-permute-start | bytes 3538952 | tf_op jit(solution)/shard_map/ppermute | solution.py:316
  88.4 3.7 %collective-permute-start.19 = (bf16[144,2048]{1,0:T(8,128)(2,1)S(1)}, bf16[144,2048]{1,0:T(8,128)(2,1)S(1)}, u32[]{:S(2)}, u32[]{:S(2)}) collective-permute-start(bf16[144,2048]{1,0:T(8,128)(2,1)S(1)} %get-tuple-element.198), channel_id=1, source_target_pairs={{0,2},{1,3},{2,0},{3,1},{4,6},{5,7},{6,4},{7,5},{8,10},{9,11},{10,... | collective-permute-start | bytes 1769480 | tf_op jit(solution)/shard_map/ppermute | solution.py:316
  88.9 10.1 %collective-permute-start.17 = (bf16[272,1024]{1,0:T(8,128)(2,1)S(1)}, bf16[272,1024]{1,0:T(8,128)(2,1)S(1)}, u32[]{:S(2)}, u32[]{:S(2)}) collective-permute-start(bf16[272,1024]{1,0:T(8,128)(2,1)S(1)} %collective-permute-done.14.refs_1_), channel_id=1, source_target_pairs={{0,1},{1,0},{2,6},{3,7},{4,5},{5,4},{6,2},{7,3},{8,9},{9,8},{10,14... | collective-permute-start | bytes 1671176 | tf_op jit(solution)/shard_map/ppermute | solution.py:316
  93.3 10.7 %collective-permute-start.20 = (bf16[2,128,1024]{2,1,0:T(8,128)(2,1)S(1)}, bf16[2,128,1024]{2,1,0:T(8,128)(2,1)S(1)}, u32[]{:S(2)}, u32[]{:S(2)}) collective-permute-start(bf16[2,128,1024]{2,1,0:T(8,128)(2,1)S(1)} %get-tuple-element.199), channel_id=1, source_target_pairs={{0,1},{1,0},{2,6},{3,7},{4,5},{5,4},{6,2},{7,3},{8,9},{9,8},{10,14... | collective-permute-start | bytes 1572872 | tf_op jit(solution)/shard_map/ppermute | solution.py:316
  100.5 7.5 %collective-permute-start.24 = (bf16[2,144,2048]{2,1,0:T(8,128)(2,1)S(1)}, bf16[2,144,2048]{2,1,0:T(8,128)(2,1)S(1)}, u32[]{:S(2)}, u32[]{:S(2)}) collective-permute-start(bf16[2,144,2048]{2,1,0:T(8,128)(2,1)S(1)} %get-tuple-element.206), channel_id=1, source_target_pairs={{0,2},{1,3},{2,0},{3,1},{4,6},{5,7},{6,4},{7,5},{8,10},{9,11},{10,... | collective-permute-start | bytes 3538952 | tf_op jit(solution)/shard_map/ppermute | solution.py:316
  104.0 2.0 %collective-permute-start.21 = (bf16[144,2048]{1,0:T(8,128)(2,1)S(1)}, bf16[144,2048]{1,0:T(8,128)(2,1)S(1)}, u32[]{:S(2)}, u32[]{:S(2)}) collective-permute-start(bf16[144,2048]{1,0:T(8,128)(2,1)S(1)} %get-tuple-element.209), channel_id=1, source_target_pairs={{0,2},{1,3},{2,0},{3,1},{4,6},{5,7},{6,4},{7,5},{8,10},{9,11},{10,... | collective-permute-start | bytes 1769480 | tf_op jit(solution)/shard_map/ppermute | solution.py:316
  104.2 8.7 %collective-permute-start.23 = (bf16[128,1024]{1,0:T(8,128)(2,1)S(1)}, bf16[128,1024]{1,0:T(8,128)(2,1)S(1)}, u32[]{:S(2)}, u32[]{:S(2)}) collective-permute-start(bf16[128,1024]{1,0:T(8,128)(2,1)S(1)} %fusion.14), channel_id=1, source_target_pairs={{0,4},{1,5},{2,3},{3,2},{4,0},{5,1},{6,7},{7,6},{8,12},{9,13},{10,... | collective-permute-start | bytes 786440 | tf_op jit(solution)/shard_map/ppermute | solution.py:316
  107.3 9.2 %collective-permute-start.22 = (bf16[2,128,1024]{2,1,0:T(8,128)(2,1)S(1)}, bf16[2,128,1024]{2,1,0:T(8,128)(2,1)S(1)}, u32[]{:S(2)}, u32[]{:S(2)}) collective-permute-start(bf16[2,128,1024]{2,1,0:T(8,128)(2,1)S(1)} %get-tuple-element.210), channel_id=1, source_target_pairs={{0,1},{1,0},{2,6},{3,7},{4,5},{5,4},{6,2},{7,3},{8,9},{9,8},{10,14... | collective-permute-start | bytes 1572872 | tf_op jit(solution)/shard_map/ppermute | solution.py:316
  112.9 4.4 %collective-permute-start.25 = (bf16[144,2048]{1,0:T(8,128)(2,1)S(1)}, bf16[144,2048]{1,0:T(8,128)(2,1)S(1)}, u32[]{:S(2)}, u32[]{:S(2)}) collective-permute-start(bf16[144,2048]{1,0:T(8,128)(2,1)S(1)} %get-tuple-element.224), channel_id=1, source_target_pairs={{0,2},{1,3},{2,0},{3,1},{4,6},{5,7},{6,4},{7,5},{8,10},{9,11},{10,... | collective-permute-start | bytes 1769480 | tf_op jit(solution)/shard_map/ppermute | solution.py:316
  116.6 12.2 %collective-permute-start.30 = (bf16[128,1024]{1,0:T(8,128)(2,1)S(1)}, bf16[128,1024]{1,0:T(8,128)(2,1)S(1)}, u32[]{:S(2)}, u32[]{:S(2)}) collective-permute-start(bf16[128,1024]{1,0:T(8,128)(2,1)S(1)} %fusion.4), channel_id=1, source_target_pairs={{0,8},{1,9},{2,10},{3,11},{4,12},{5,13},{6,14},{7,15},{8,24},{9,25... | collective-permute-start | bytes 786440 | tf_op jit(solution)/shard_map/ppermute | solution.py:316
  118.6 17.1 %collective-permute-start.27 = (bf16[2,128,1024]{2,1,0:T(8,128)(2,1)S(1)}, bf16[2,128,1024]{2,1,0:T(8,128)(2,1)S(1)}, u32[]{:S(2)}, u32[]{:S(2)}) collective-permute-start(bf16[2,128,1024]{2,1,0:T(8,128)(2,1)S(1)} %get-tuple-element.225), channel_id=1, source_target_pairs={{0,1},{1,0},{2,6},{3,7},{4,5},{5,4},{6,2},{7,3},{8,9},{9,8},{10,14... | collective-permute-start | bytes 1572872 | tf_op jit(solution)/shard_map/ppermute | solution.py:316
  119.5 9.3 %collective-permute-start.29 = (bf16[128,1024]{1,0:T(8,128)(2,1)S(1)}, bf16[128,1024]{1,0:T(8,128)(2,1)S(1)}, u32[]{:S(2)}, u32[]{:S(2)}) collective-permute-start(bf16[128,1024]{1,0:T(8,128)(2,1)S(1)} %fusion.17), channel_id=1, source_target_pairs={{0,4},{1,5},{2,3},{3,2},{4,0},{5,1},{6,7},{7,6},{8,12},{9,13},{10,... | collective-permute-start | bytes 786440 | tf_op jit(solution)/shard_map/ppermute | solution.py:316
  120.4 16.5 %collective-permute-start.26 = (bf16[2,128,1024]{2,1,0:T(8,128)(2,1)S(1)}, bf16[2,128,1024]{2,1,0:T(8,128)(2,1)S(1)}, u32[]{:S(2)}, u32[]{:S(2)}) collective-permute-start(bf16[2,128,1024]{2,1,0:T(8,128)(2,1)S(1)} %get-tuple-element.226), channel_id=1, source_target_pairs={{0,1},{1,0},{2,6},{3,7},{4,5},{5,4},{6,2},{7,3},{8,9},{9,8},{10,14... | collective-permute-start | bytes 1572872 | tf_op jit(solution)/shard_map/ppermute | solution.py:316
  128.9 8.3 %collective-permute-start.31 = (bf16[128,1024]{1,0:T(8,128)(2,1)S(1)}, bf16[128,1024]{1,0:T(8,128)(2,1)S(1)}, u32[]{:S(2)}, u32[]{:S(2)}) collective-permute-start(bf16[128,1024]{1,0:T(8,128)(2,1)S(1)} %fusion.7), channel_id=1, source_target_pairs={{0,8},{1,9},{2,10},{3,11},{4,12},{5,13},{6,14},{7,15},{8,24},{9,25... | collective-permute-start | bytes 786440 | tf_op jit(solution)/shard_map/ppermute | solution.py:316
  136.0 6.4 %collective-permute-start.28 = (bf16[128,1024]{1,0:T(8,128)(2,1)S(1)}, bf16[128,1024]{1,0:T(8,128)(2,1)S(1)}, u32[]{:S(2)}, u32[]{:S(2)}) collective-permute-start(bf16[128,1024]{1,0:T(8,128)(2,1)S(1)} %fusion.16), channel_id=1, source_target_pairs={{0,4},{1,5},{2,3},{3,2},{4,0},{5,1},{6,7},{7,6},{8,12},{9,13},{10,... | collective-permute-start | bytes 786440 | tf_op jit(solution)/shard_map/ppermute | solution.py:316
  142.5 7.3 %collective-permute-start.33 = (bf16[128,1024]{1,0:T(8,128)(2,1)S(1)}, bf16[128,1024]{1,0:T(8,128)(2,1)S(1)}, u32[]{:S(2)}, u32[]{:S(2)}) collective-permute-start(bf16[128,1024]{1,0:T(8,128)(2,1)S(1)} %fusion.10), channel_id=1, source_target_pairs={{0,8},{1,9},{2,10},{3,11},{4,12},{5,13},{6,14},{7,15},{8,24},{9,25... | collective-permute-start | bytes 786440 | tf_op jit(solution)/shard_map/ppermute | solution.py:316
  142.6 6.4 %collective-permute-start.32 = (bf16[128,1024]{1,0:T(8,128)(2,1)S(1)}, bf16[128,1024]{1,0:T(8,128)(2,1)S(1)}, u32[]{:S(2)}, u32[]{:S(2)}) collective-permute-start(bf16[128,1024]{1,0:T(8,128)(2,1)S(1)} %fusion.15), channel_id=1, source_target_pairs={{0,4},{1,5},{2,3},{3,2},{4,0},{5,1},{6,7},{7,6},{8,12},{9,13},{10,... | collective-permute-start | bytes 786440 | tf_op jit(solution)/shard_map/ppermute | solution.py:316

commit v13 on v11

--- a/solution.py
+++ b/solution.py
@@ -132,26 +132,6 @@
         out_shape=jax.ShapeDtypeStruct((2 * rows + INFO_ROWS, width), jnp.bfloat16),
         name="pack",
     )(tokens, out_grad, routes.T, combine.T)
-
-
-def load_kernel(*refs):
-    count = (len(refs) - 1) // 2
-    moves = [pltpu.make_async_copy(refs[i], refs[count + i], refs[-1].at[i]) for i in range(count)]
-    for move in moves:
-        move.start()
-    for move in moves:
-        move.wait()
-
-
-def load_weights(weights):
-    return pl.pallas_call(
-        load_kernel,
-        in_specs=[pl.BlockSpec(memory_space=pltpu.HBM)] * len(weights),
-        out_specs=[pl.BlockSpec(memory_space=pltpu.VMEM)] * len(weights),
-        out_shape=[jax.ShapeDtypeStruct(w.shape, w.dtype) for w in weights],
-        scratch_shapes=[pltpu.SemaphoreType.DMA((len(weights),))],
-        name="load",
-    )(*weights)
 
 
 def pick_kernel(top, rows, place_ref, *refs):
@@ -349,7 +329,7 @@
     me = lax.axis_index("expert")
     place = jnp.stack([me, lax.axis_index("etp"), me % 2]).astype(jnp.int32)
     share = pack_share(tokens, out_grad, routes, combine)
-    weights = load_weights((w_gate[0], w_up[0], w_down[0]))
+    weights = (w_gate[0], w_up[0], w_down[0])
 
     def tied(values, mark):
         return lax.optimization_barrier((values, mark))[0]
@@ -360,77 +340,79 @@
     def added(keep, came):
         return keep + came.astype(jnp.float32)
 
-    ring_sends = [("s", 1)] + [(kind, c) for c in range(2, chunks) for kind in ("f", "s")]
-    ring_sends.sort(key=lambda key: key[1] * 2 - (key[0] == "s"))
-    plane_sends = [("f", 0), ("a", 0), ("b", 0), ("f", 1), ("a", 1), ("b", 1)]
-    plane_sends += [(kind, c) for c in range(2, chunks) for kind in ("a", "b")]
-    ring_sends = [key for key in ring_sends if key[1] < chunks]
-    plane_sends = [key for key in plane_sends if key[1] < chunks]
-
-    def source_of(key, by_ring):
-        kind, c = key
-        return (kind, c - 1) if by_ring else ("f" if kind == "b" else "s", c)
-
+    waves = [
+        ([("f", 0), ("a", 0)], ("s", 1)),
+        ([("b", 0), ("f", 1)], ("s", 2)),
+        ([("a", 1), ("b", 1), ("a", 2)], ("s", 3)),
+        ([("a", 3), ("f", 3)], ("f", 2)),
+        ([("b", 2), ("b", 3)], None),
+    ]
     have = {("s", 0): share}
-    kept, picked, parts, waiting = None, None, None, None
-    late, done = [], 0
-    while plane_sends:
+    kept, picked, parts = None, None, None
+    late, last, done = [], [], 0
+    for plane, ring in waves:
         came = {}
-        for key in [key for key in plane_sends if source_of(key, False) in have][:2]:
-            value = have[source_of(key, False)]
-            came[key] = to_first(value) if key[0] == "f" else to_second(value)
-            plane_sends.remove(key)
-        for key in [key for key in ring_sends if source_of(key, True) in have][:1]:
-            came[key] = to_ring(have[source_of(key, True)])
-            ring_sends.remove(key)
-        ready, waiting, before = waiting, None, parts
+        for kind, c in plane:
+            if c < chunks:
+                value = have["f" if kind == "b" else "s", c]
+                came[kind, c] = to_first(value) if kind == "f" else to_second(value)
+        if ring is not None and ring[1] < chunks:
+            came[ring] = to_ring(have[ring[0], ring[1] - 1])
+        before, parts = parts, None
         if picked is not None:
             mine, theirs, picks = picked
             near, far, *kept = run_experts(done, chunks, mine, to_core(theirs), weights, kept)
             parts, picked = (picks, near, far), None
             done += 1
-        else:
-            parts = None
-        if before is not None:
-            waiting = placed(*before)
-        if plane_sends and all((kind, done) in have for kind in "sfab"):
+        if ring is None:
+            have.update(came)
+            break
+        if all((kind, done) in have for kind in "sfab") and done + 1 < chunks:
             picked = pick_rows(place, [have[kind, done] for kind in "sfab"], top, rows, pair_slots)
-        if ready is not None:
-            late.append(ready)
-        needed = {key: have[key] for key in have if key[1] >= done}
-        listed = sorted(came, reverse=True)
-        values, have, picked, parts, waiting, late, weights = lax.optimization_barrier(
-            ([came[key] for key in listed], needed, picked, parts, waiting, late, weights)
+        listed = sorted(came, reverse=False)
+        values, picked, parts, weights = lax.optimization_barrier(
+            ([came[key] for key in listed], picked, parts, weights)
         )
-        came = dict(zip(listed, values))
-        have.update(came)
-    mine, theirs, picks = pick_rows(place, [have[kind, done] for kind in "sfab"], top, rows, pair_slots)
-    unsent, late = late, []
-    if waiting is not None:
-        keep, send = waiting
-        late.append((keep, to_second(tied(send, theirs))))
+        have.update(zip(listed, values))
+    mark = []
+    if before is not None:
+        keep, send = placed(*before)
+        late.append((keep, to_second(send)))
+        mark.append(send)
     if parts is not None:
-        keep, send = placed(*tied(parts, theirs))
+        mark.append(parts[1])
+    while done < chunks:
+        shares = tied([have[kind, done] for kind in "sfab"], mark)
+        mine, theirs, picks = pick_rows(place, shares, top, rows, pair_slots)
+        if parts is not None:
+            keep, send = placed(*parts)
+            late.append((keep, to_second(send)))
+            mine, parts = tied(mine, send), None
+        near, far, *kept = run_experts(done, chunks, mine, to_core(theirs), weights, kept)
+        last.append((picks, near, far))
+        done += 1
+    nears = [near for _, near, _ in last]
+    near, send = nears[-1], nears[0]
+    for picks, first, far in last:
+        keep, send = placed(picks, tied(first, send), far)
         late.append((keep, to_second(send)))
-    near, far, *kept = run_experts(done, chunks, mine, to_core(theirs), weights, kept)
-    keep, send = placed(picks, near, far)
-    late.append((keep, to_second(send)))
-    late = [(keep, to_second(tied(first, send))) for keep, first in unsent] + late
+    ties = [nears[0], send]
     marks = [send] * (chunks + 2)
     running = None
     for c in range(1, chunks):
         keep, came = late[c]
         if c + 1 < chunks:
-            came = tied(came, near if c == 1 else marks[0])
+            came = tied(came, ties[c - 1])
         pair = added(keep, came)
         came = to_first(pair[1].astype(jnp.bfloat16))
-        total = added(pair[0], came if c + 1 == chunks else tied(came, send))
+        total = added(pair[0], tied(came, send) if c == 1 else came)
         running = (total if running is None else added(total, running)).astype(jnp.bfloat16)
-        marks[min(c - 1, 2)] = running
+        if c > 1:
+            marks[min(c - 1, 2)] = running
         if c + 1 < chunks:
             running = to_ring(running)
     keep, came = late[0]
-    pair = added(keep, came)
+    pair = added(keep, tied(came, send))
     came = pair[1].astype(jnp.bfloat16)
     own = added(pair[0], to_first(came if running is None else tied(came, running)))
     grad_tokens = (own if running is None else added(own, to_ring(running))).astype(jnp.bfloat16)
@@ -453,7 +435,7 @@
     def body(tokens, out_grad, routes, combine, w_gate, w_up, w_down):
         rows, width = tokens.shape
         top = routes.shape[1]
-        gathers = top * 4 >= experts and experts % 4 == 0 and mesh.shape["etp"] == 2
+        gathers = top * 4 >= experts and experts % 4 == 0 and experts <= 16 and mesh.shape["etp"] == 2
         run = gather_body if gathers and top * rows <= width else exchange_body
         return run(tokens, out_grad, routes, combine, w_gate, w_up, w_down)
 

time: 150 us -> 145 us (0.967)
  waiting for transfers between devices: 62.7 us -> 58.2 us
  Pallas kernels: 38 us -> 34.1 us
  starting transfers between devices: 31 us -> 32.6 us
    pallas_call x1 -> x0, Pallas kernels: 4.62 us -> none  [load_weights(): pl.pallas_call(load_kernel, in_specs=[pl.BlockSpec(memory_space=pltpu.HBM...]
    ppermute x34, waiting for transfers between devices: 62.7 us -> 58.2 us  [permute(): return lax.ppermute(value, ('expert', 'etp'), pairs)]
    ppermute x34, starting transfers between devices: 31 us -> 32.6 us  [permute(): return lax.ppermute(value, ('expert', 'etp'), pairs)]
    unnamed x18 -> x20, local copies, waits for them, and re-layouts: 5.16 us -> 6.63 us
  transfers between devices with their start and end apart: 34 -> 34, of which waited for: 18 -> 17; matrix products, arithmetic and copies ran while one was open for 7% -> 8% of each run, Pallas kernels for 23% -> 22%
where the time goes in v13:
time: 145 us
  waiting for transfers between devices  58.2 us (40%)
  Pallas kernels  34.1 us (24%)
  starting transfers between devices  32.6 us (22%)
  matrix products  10.2 us (7%)
  local copies, waits for them, and re-layouts  6.76 us (5%)
  other arithmetic  1.85 us (1%)
    ppermute x34, waiting for transfers between devices, permute(): return lax.ppermute(value, ('expert', 'etp'), pairs)  58.2 us
    ppermute x34, starting transfers between devices, permute(): return lax.ppermute(value, ('expert', 'etp'), pairs)  32.6 us
    pallas_call x4, Pallas kernels, run_experts(): pl.pallas_call(functools.partial(expert_kernel, index, kept is not None),...  19.9 us
    pallas_call x4, Pallas kernels, pick_rows(): pl.pallas_call(functools.partial(pick_kernel, top, rows), in_specs=[pl.Bl...  7.05 us
    unnamed x20, local copies, waits for them, and re-layouts  6.63 us
    pallas_call x4, Pallas kernels, place_rows(): pl.pallas_call(place_kernel, in_specs=[pl.BlockSpec(memory_space=pltpu.SM...  5.08 us
    dot_general x1, matrix products, gather_body(): lax.dot_general(acts, rows_g, CONTRACT_FIRST, preferred_element_type=jnp....  3.4 us
    dot_general x1, matrix products, gather_body(): lax.dot_general(up_term, rows_x, CONTRACT_FIRST, preferred_element_type=j...  3.38 us
  transfers between devices with their start and end apart: 34, of which 17 were waited for; matrix products, arithmetic and copies ran while one was open for 8% of the time, Pallas kernels for 22%

profile of v13, /device:TPU:0, one launch (start us, length us, event | category | flops | bytes accessed | tf_op | source)
XLA Modules:
  0.0 144.6 jit_solution(17287838226898686694)
XLA Ops:
  0.6 2.0 %pack.1.refs_0_ = bf16[272,1024]{1,0:T(8,128)(2,1)} custom-call(bf16[128,1024]{1,0:T(8,128)(2,1)} %tokens_ref.1, bf16[128,1024]{1,0:T(8,128)(2,1)} %grads_ref.1, s32[8,128]{1,0:T(8,128)} %bitcast.70, f32[8,128]{1,0:T(8,128)} %bitcast.71), custom_call_target="tpu_custom_call" | custom-call | tf_op jit(solution)/shard_map/pack/pallas_call | solution.py:128
  2.6 2.9 %collective-permute-start = (bf16[272,1024]{1,0:T(8,128)(2,1)}, bf16[272,1024]{1,0:T(8,128)(2,1)S(1)}, u32[]{:S(2)}, u32[]{:S(2)}) collective-permute-start(bf16[272,1024]{1,0:T(8,128)(2,1)} %pack.1.refs_0_), channel_id=1, source_target_pairs={{0,1},{1,0},{2,6},{3,7},{4,5},{5,4},{6,2},{7,3},{8,9},{9,8},{10,14... | collective-permute-start | bytes 1671176 | tf_op jit(solution)/shard_map/ppermute | solution.py:315
  5.6 1.5 %collective-permute-start.1 = (bf16[272,1024]{1,0:T(8,128)(2,1)}, bf16[272,1024]{1,0:T(8,128)(2,1)S(1)}, u32[]{:S(2)}, u32[]{:S(2)}) collective-permute-start(bf16[272,1024]{1,0:T(8,128)(2,1)} %pack.1.refs_0_), channel_id=1, source_target_pairs={{0,4},{1,5},{2,3},{3,2},{4,0},{5,1},{6,7},{7,6},{8,12},{9,13},{10,... | collective-permute-start | bytes 1671176 | tf_op jit(solution)/shard_map/ppermute | solution.py:315
  7.1 1.6 %collective-permute-start.2 = (bf16[272,1024]{1,0:T(8,128)(2,1)}, bf16[272,1024]{1,0:T(8,128)(2,1)}, u32[]{:S(2)}, u32[]{:S(2)}) collective-permute-start(bf16[272,1024]{1,0:T(8,128)(2,1)} %pack.1.refs_0_), channel_id=1, source_target_pairs={{0,8},{1,9},{2,10},{3,11},{4,12},{5,13},{6,14},{7,15},{8,24},{9,25... | collective-permute-start | bytes 1671176 | tf_op jit(solution)/shard_map/ppermute | solution.py:315
  8.7 10.1 %collective-permute-done.refs_2_ = bf16[272,1024]{1,0:T(8,128)(2,1)S(1)} collective-permute-done((bf16[272,1024]{1,0:T(8,128)(2,1)}, bf16[272,1024]{1,0:T(8,128)(2,1)S(1)}, u32[]{:S(2)}, u32[]{:S(2)}) %collective-permute-start) | collective-permute-done | bytes 557088 | tf_op jit(solution)/shard_map/ppermute | solution.py:315
  19.6 2.5 %collective-permute-done.2.refs_0_ = bf16[272,1024]{1,0:T(8,128)(2,1)} collective-permute-done((bf16[272,1024]{1,0:T(8,128)(2,1)}, bf16[272,1024]{1,0:T(8,128)(2,1)}, u32[]{:S(2)}, u32[]{:S(2)}) %collective-permute-start.2) | collective-permute-done | bytes 557088 | tf_op jit(solution)/shard_map/ppermute | solution.py:315
  25.1 1.1 collective-permute-start.3
  26.2 11.7 %collective-permute-done.5.refs_1_ = bf16[272,1024]{1,0:T(8,128)(2,1)} collective-permute-done((bf16[272,1024]{1,0:T(8,128)(2,1)}, bf16[272,1024]{1,0:T(8,128)(2,1)}, u32[]{:S(2)}, u32[]{:S(2)}) %collective-permute-start.5) | collective-permute-done | bytes 557088 | tf_op jit(solution)/shard_map/ppermute | solution.py:315
  39.3 1.5 %collective-permute-start.8 = (bf16[272,1024]{1,0:T(8,128)(2,1)}, bf16[272,1024]{1,0:T(8,128)(2,1)}, u32[]{:S(2)}, u32[]{:S(2)}) collective-permute-start(bf16[272,1024]{1,0:T(8,128)(2,1)} %collective-permute-done.5.refs_1_), channel_id=1, source_target_pairs={{0,1},{1,0},{2,6},{3,7},{4,5},{5,4},{6,2},{7,3},{8,9},{9,8},{10,14... | collective-permute-start | bytes 1671176 | tf_op jit(solution)/shard_map/ppermute | solution.py:315
  40.9 1.1 copy-done.3
  41.9 1.1 copy-done.5
  43.0 1.1 copy-done.7
  44.0 1.1 copy-done.9
  45.1 1.5 %pick.4 = (bf16[2,144,2048]{2,1,0:T(8,128)(2,1)S(1)}, bf16[2,144,2048]{2,1,0:T(8,128)(2,1)S(1)}, bf16[288,256]{1,0:T(8,128)(2,1)S(1)}) custom-call(s32[3]{0:T(128)S(1)} %pad_add_fusion.place_ref, bf16[272,1024]{1,0:T(8,128)(2,1)S(1)} %copy-done.3, bf16[272,1024]{1,0:T(8,128)(2,1)S(1)} %copy-done.7, bf16[272,1024]{1,0:T(8,128)(2,1)S(1)} %copy-done.5, ...), custom_call_target="tpu_custom_call" | custom-call | tf_op jit(solution)/shard_map/pick/pallas_call | solution.py:251
  46.6 1.7 %collective-permute-done.7.refs_2_ = bf16[272,1024]{1,0:T(8,128)(2,1)S(1)} collective-permute-done((bf16[272,1024]{1,0:T(8,128)(2,1)S(1)}, bf16[272,1024]{1,0:T(8,128)(2,1)S(1)}, u32[]{:S(2)}, u32[]{:S(2)}) %collective-permute-start.7) | collective-permute-done | bytes 557088 | tf_op jit(solution)/shard_map/ppermute | solution.py:315
  48.3 6.1 %collective-permute-done.8.refs_3_ = bf16[272,1024]{1,0:T(8,128)(2,1)} collective-permute-done((bf16[272,1024]{1,0:T(8,128)(2,1)}, bf16[272,1024]{1,0:T(8,128)(2,1)}, u32[]{:S(2)}, u32[]{:S(2)}) %collective-permute-start.8) | collective-permute-done | bytes 557088 | tf_op jit(solution)/shard_map/ppermute | solution.py:315
  54.9 1.6 %collective-permute-start.11 = (bf16[272,1024]{1,0:T(8,128)(2,1)}, bf16[272,1024]{1,0:T(8,128)(2,1)S(1)}, u32[]{:S(2)}, u32[]{:S(2)}) collective-permute-start(bf16[272,1024]{1,0:T(8,128)(2,1)} %collective-permute-done.5.refs_1_), channel_id=1, source_target_pairs={{0,8},{1,9},{2,10},{3,11},{4,12},{5,13},{6,14},{7,15},{8,24},{9,25... | collective-permute-start | bytes 1671176 | tf_op jit(solution)/shard_map/ppermute | solution.py:315
  57.8 2.5 %pick.5 = (bf16[2,144,2048]{2,1,0:T(8,128)(2,1)S(1)}, bf16[2,144,2048]{2,1,0:T(8,128)(2,1)S(1)}, bf16[288,256]{1,0:T(8,128)(2,1)S(1)}) custom-call(s32[3]{0:T(128)S(1)} %pad_add_fusion.place_ref, bf16[272,1024]{1,0:T(8,128)(2,1)} %collective-permute-done.2.refs_0_, bf16[272,1024]{1,0:T(8,128)(2,1)} %collective-permute-done.5.refs_1_, ...), custom_call_target="tpu_custom_call" | custom-call | tf_op jit(solution)/shard_map/pick/pallas_call | solution.py:251
  60.4 5.0 %experts.4 = (bf16[144,2048]{1,0:T(8,128)(2,1)S(1)}, bf16[144,2048]{1,0:T(8,128)(2,1)S(1)}, bf16[1152,2048]{1,0:T(8,128)(2,1)S(1)}, bf16[1152,2048]{1,0:T(8,128)...) custom-call(bf16[2,144,2048]{2,1,0:T(8,128)(2,1)S(1)} %get-tuple-element.127., ...), custom_call_target="tpu_custom_call" | custom-call | tf_op jit(solution)/shard_map/experts/pallas_call | solution.py:270
  65.5 5.1 %collective-permute-done.11.refs_1_ = bf16[272,1024]{1,0:T(8,128)(2,1)S(1)} collective-permute-done((bf16[272,1024]{1,0:T(8,128)(2,1)}, bf16[272,1024]{1,0:T(8,128)(2,1)S(1)}, u32[]{:S(2)}, u32[]{:S(2)}) %collective-permute-start.11) | collective-permute-done | bytes 557088 | tf_op jit(solution)/shard_map/ppermute | solution.py:315
  72.3 1.1 collective-permute-start.16
  73.5 1.2 collective-permute-done.14.far_ref
  74.6 1.3 place.4
  75.9 4.9 %experts.5 = (bf16[144,2048]{1,0:T(8,128)(2,1)S(1)}, bf16[144,2048]{1,0:T(8,128)(2,1)S(1)}, bf16[1152,2048]{1,0:T(8,128)(2,1)S(1)}, bf16[1152,2048]{1,0:T(8,128)...) custom-call(bf16[2,144,2048]{2,1,0:T(8,128)(2,1)S(1)} %get-tuple-ele, ...), custom_call_target="tpu_custom_call", output_to_operand_aliasing={{2}: (5, {}), {3}: (6, {}), {4}: (7, {}), {5}: (8, {}), {6}... | custom-call | tf_op jit(solution)/shard_map/experts/pallas_call | solution.py:270
  81.0 1.5 %pick.7 = (bf16[2,144,2048]{2,1,0:T(8,128)(2,1)S(1)}, bf16[2,144,2048]{2,1,0:T(8,128)(2,1)S(1)}, bf16[288,256]{1,0:T(8,128)(2,1)S(1)}) custom-call(s32[3]{0:T(128)S(1)} %pad_add_fusion.place_ref, bf16[272,1024]{1,0:T(8,128)(2,1)S(1)} %collective-permute-done.6.refs_0_, bf16[272,1024]{1,0:T(8,128)(2,1)S(1)} %collective-permute-done.11.refs_1_, ...), custom_call_target="tpu_custom_call" | custom-call | tf_op jit(solution)/shard_map/pick/pallas_call | solution.py:251
  82.6 4.4 %collective-permute-done.16.refs_3_ = bf16[272,1024]{1,0:T(8,128)(2,1)S(1)} collective-permute-done((bf16[272,1024]{1,0:T(8,128)(2,1)S(1)}, bf16[272,1024]{1,0:T(8,128)(2,1)S(1)}, u32[]{:S(2)}, u32[]{:S(2)}) %collective-permute-start.16) | collective-permute-done | bytes 557088 | tf_op jit(solution)/shard_map/ppermute | solution.py:315
  87.0 1.5 %pick.6 = (bf16[2,144,2048]{2,1,0:T(8,128)(2,1)S(1)}, bf16[2,144,2048]{2,1,0:T(8,128)(2,1)S(1)}, bf16[288,256]{1,0:T(8,128)(2,1)S(1)}) custom-call(s32[3]{0:T(128)S(1)} %pad_add_fusion.place_ref, bf16[272,1024]{1,0:T(8,128)(2,1)S(1)} %collective-permute-done.9.refs_0_, bf16[272,1024]{1,0:T(8,128)(2,1)S(1)} %collective-permute-done.12.refs_1_, ...), custom_call_target="tpu_custom_call" | custom-call | tf_op jit(solution)/shard_map/pick/pallas_call | solution.py:251
  89.1 3.2 %collective-permute-done.20.far_ref = bf16[144,2048]{1,0:T(8,128)(2,1)S(1)} collective-permute-done((bf16[144,2048]{1,0:T(8,128)(2,1)S(1)}, bf16[144,2048]{1,0:T(8,128)(2,1)S(1)}, u32[]{:S(2)}, u32[]{:S(2)}) %collective-permute-start.20) | collective-permute-done | bytes 589856 | tf_op jit(solution)/shard_map/ppermute | solution.py:315
  92.2 1.3 place.5
  93.5 0.9 collective-permute-start.28
  94.5 1.2 collective-permute-start.15
  95.6 4.9 %experts.6 = (bf16[144,2048]{1,0:T(8,128)(2,1)S(1)}, bf16[144,2048]{1,0:T(8,128)(2,1)S(1)}, bf16[1152,2048]{1,0:T(8,128)(2,1)S(1)}, bf16[1152,2048]{1,0:T(8,128)...) custom-call(bf16[2,144,2048]{2,1,0:T(8,128)(2,1)S(1)} %get-tuple-ele, ...), custom_call_target="tpu_custom_call", output_to_operand_aliasing={{2}: (5, {}), {3}: (6, {}), {4}: (7, {}), {5}: (8, {}), {6}... | custom-call | tf_op jit(solution)/shard_map/experts/pallas_call | solution.py:270
  100.6 5.1 %experts.7 = (bf16[144,2048]{1,0:T(8,128)(2,1)S(1)}, bf16[144,2048]{1,0:T(8,128)(2,1)S(1)}, bf16[1152,2048]{1,0:T(8,128)(2,1)S(1)}, bf16[1152,2048]{1,0:T(8,128)...) custom-call(bf16[2,144,2048]{2,1,0:T(8,128)(2,1)S(1)} %get-tuple-ele, ...), custom_call_target="tpu_custom_call", output_to_operand_aliasing={{2}: (5, {}), {3}: (6, {}), {4}: (7, {}), {5}: (8, {}), {6}... | custom-call | tf_op jit(solution)/shard_map/experts/pallas_call | solution.py:270
  106.5 1.6 %collective-permute-start.29 = (bf16[128,1024]{1,0:T(8,128)(2,1)S(1)}, bf16[128,1024]{1,0:T(8,128)(2,1)S(1)}, u32[]{:S(2)}, u32[]{:S(2)}) collective-permute-start(bf16[128,1024]{1,0:T(8,128)(2,1)S(1)} %fusion.17), channel_id=1, source_target_pairs={{0,4},{1,5},{2,3},{3,2},{4,0},{5,1},{6,7},{7,6},{8,12},{9,13},{10,... | collective-permute-start | bytes 786440 | tf_op jit(solution)/shard_map/ppermute | solution.py:315
  108.1 1.3 place.6
  110.1 1.3 place.7
  111.4 1.4 collective-permute-start.24
  112.8 1.9 %collective-permute-done.29 = bf16[128,1024]{1,0:T(8,128)(2,1)S(1)} collective-permute-done((bf16[128,1024]{1,0:T(8,128)(2,1)S(1)}, bf16[128,1024]{1,0:T(8,128)(2,1)S(1)}, u32[]{:S(2)}, u32[]{:S(2)}) %collective-permute-start.29) | collective-permute-done | bytes 262176 | tf_op jit(solution)/shard_map/ppermute | solution.py:315
  114.8 3.1 %collective-permute-start.30 = (bf16[128,1024]{1,0:T(8,128)(2,1)S(1)}, bf16[128,1024]{1,0:T(8,128)(2,1)S(1)}, u32[]{:S(2)}, u32[]{:S(2)}) collective-permute-start(bf16[128,1024]{1,0:T(8,128)(2,1)S(1)} %fusion.4), channel_id=1, source_target_pairs={{0,8},{1,9},{2,10},{3,11},{4,12},{5,13},{6,14},{7,15},{8,24},{9,25... | collective-permute-start | bytes 786440 | tf_op jit(solution)/shard_map/ppermute | solution.py:315
  118.1 3.4 %fusion.2 = bf16[1,384,2048]{2,1,0:T(8,128)(2,1)} fusion(bf16[1152,384]{1,0:T(8,128)(2,1)S(1)} %get-tuple-element.204, bf16[1152,2048]{1,0:T(8,128)(2,1)S(1)} %get-tuple-element.205), kind=kOutput, calls=%fused_computation.5 | convolution fusion | flops 1812725760 | bytes 7176192 | tf_op jit(solution)/shard_map/dot_general | solution.py:421
  122.4 4.4 %collective-permute-done.24 = bf16[2,128,1024]{2,1,0:T(8,128)(2,1)S(1)} collective-permute-done((bf16[2,128,1024]{2,1,0:T(8,128)(2,1)S(1)}, bf16[2,128,1024]{2,1,0:T(8,128)(2,1)S(1)}, u32[]{:S(2)}, u32[]{:S(2)}) %collective-permute-start.24) | collective-permute-done | bytes 524320 | tf_op jit(solution)/shard_map/ppermute | solution.py:315
  127.2 1.0 collective-permute-done.27
  128.3 2.0 %collective-permute-start.31 = (bf16[128,1024]{1,0:T(8,128)(2,1)S(1)}, bf16[128,1024]{1,0:T(8,128)(2,1)S(1)}, u32[]{:S(2)}, u32[]{:S(2)}) collective-permute-start(bf16[128,1024]{1,0:T(8,128)(2,1)S(1)} %fusion.7), channel_id=1, source_target_pairs={{0,8},{1,9},{2,10},{3,11},{4,12},{5,13},{6,14},{7,15},{8,24},{9,25... | collective-permute-start | bytes 786440 | tf_op jit(solution)/shard_map/ppermute | solution.py:315
  130.3 3.4 %fusion = bf16[1,384,2048]{2,1,0:T(8,128)(2,1)} fusion(bf16[1152,384]{1,0:T(8,128)(2,1)S(1)} %get-tuple-element.199, bf16[1152,2048]{1,0:T(8,128)(2,1)S(1)} %get-tuple-element.200), kind=kOutput, calls=%fused_computation.3 | convolution fusion | flops 1812725760 | bytes 7176192 | tf_op jit(solution)/shard_map/dot_general | solution.py:422
  133.7 2.7 %collective-permute-done.31 = bf16[128,1024]{1,0:T(8,128)(2,1)S(1)} collective-permute-done((bf16[128,1024]{1,0:T(8,128)(2,1)S(1)}, bf16[128,1024]{1,0:T(8,128)(2,1)S(1)}, u32[]{:S(2)}, u32[]{:S(2)}) %collective-permute-start.31) | collective-permute-done | bytes 262176 | tf_op jit(solution)/shard_map/ppermute | solution.py:315
  137.4 1.4 collective-permute-start.32
  138.8 3.4 %fusion.1 = bf16[1,384,2048]{2,1,0:T(8,128)(2,1)} fusion(bf16[1152,384]{1,0:T(8,128)(2,1)S(1)} %get-tuple-element.202, bf16[1152,2048]{1,0:T(8,128)(2,1)S(1)} %get-tuple-element.200), kind=kOutput, calls=%fused_computation.4 | convolution fusion | flops 1812725760 | bytes 7176192 | tf_op jit(solution)/shard_map/dot_general | solution.py:423
  142.2 1.6 %collective-permute-done.32 = bf16[128,1024]{1,0:T(8,128)(2,1)S(1)} collective-permute-done((bf16[128,1024]{1,0:T(8,128)(2,1)S(1)}, bf16[128,1024]{1,0:T(8,128)(2,1)S(1)}, u32[]{:S(2)}, u32[]{:S(2)}) %collective-permute-start.32) | collective-permute-done | bytes 262176 | tf_op jit(solution)/shard_map/ppermute | solution.py:315
  (69 shorter events, 14.7 us)
Async XLA Ops:
  0.6 59.8 %copy-start.2 = (bf16[1,384,2048]{2,1,0:T(8,128)(2,1)S(1)}, bf16[1,384,2048]{2,1,0:T(8,128)(2,1)}, u32[]{:S(2)}) copy-start(bf16[1,384,2048]{2,1,0:T(8,128)(2,1)} %param.13) | copy-start | bytes 4718596
  2.6 16.2 %collective-permute-start = (bf16[272,1024]{1,0:T(8,128)(2,1)}, bf16[272,1024]{1,0:T(8,128)(2,1)S(1)}, u32[]{:S(2)}, u32[]{:S(2)}) collective-permute-start(bf16[272,1024]{1,0:T(8,128)(2,1)} %pack.1.refs_0_), channel_id=1, source_target_pairs={{0,1},{1,0},{2,6},{3,7},{4,5},{5,4},{6,2},{7,3},{8,9},{9,8},{10,14... | collective-permute-start | bytes 1671176 | tf_op jit(solution)/shard_map/ppermute | solution.py:315
  5.6 14.0 %collective-permute-start.1 = (bf16[272,1024]{1,0:T(8,128)(2,1)}, bf16[272,1024]{1,0:T(8,128)(2,1)S(1)}, u32[]{:S(2)}, u32[]{:S(2)}) collective-permute-start(bf16[272,1024]{1,0:T(8,128)(2,1)} %pack.1.refs_0_), channel_id=1, source_target_pairs={{0,4},{1,5},{2,3},{3,2},{4,0},{5,1},{6,7},{7,6},{8,12},{9,13},{10,... | collective-permute-start | bytes 1671176 | tf_op jit(solution)/shard_map/ppermute | solution.py:315
  7.1 15.0 %collective-permute-start.2 = (bf16[272,1024]{1,0:T(8,128)(2,1)}, bf16[272,1024]{1,0:T(8,128)(2,1)}, u32[]{:S(2)}, u32[]{:S(2)}) collective-permute-start(bf16[272,1024]{1,0:T(8,128)(2,1)} %pack.1.refs_0_), channel_id=1, source_target_pairs={{0,8},{1,9},{2,10},{3,11},{4,12},{5,13},{6,14},{7,15},{8,24},{9,25... | collective-permute-start | bytes 1671176 | tf_op jit(solution)/shard_map/ppermute | solution.py:315
  18.8 0.8 copy-start.4
  22.1 15.8 %collective-permute-start.5 = (bf16[272,1024]{1,0:T(8,128)(2,1)}, bf16[272,1024]{1,0:T(8,128)(2,1)}, u32[]{:S(2)}, u32[]{:S(2)}) collective-permute-start(bf16[272,1024]{1,0:T(8,128)(2,1)} %collective-permute-done.2.refs_0_), channel_id=1, source_target_pairs={{0,4},{1,5},{2,3},{3,2},{4,0},{5,1},{6,7},{7,6},{8,12},{9,13},{10,... | collective-permute-start | bytes 1671176 | tf_op jit(solution)/shard_map/ppermute | solution.py:315
  22.7 15.3 %collective-permute-start.6 = (bf16[272,1024]{1,0:T(8,128)(2,1)}, bf16[272,1024]{1,0:T(8,128)(2,1)S(1)}, u32[]{:S(2)}, u32[]{:S(2)}) collective-permute-start(bf16[272,1024]{1,0:T(8,128)(2,1)} %collective-permute-done.2.refs_0_), channel_id=1, source_target_pairs={{0,8},{1,9},{2,10},{3,11},{4,12},{5,13},{6,14},{7,15},{8,24},{9,25... | collective-permute-start | bytes 1671176 | tf_op jit(solution)/shard_map/ppermute | solution.py:315
  23.4 14.6 %collective-permute-start.4 = (bf16[272,1024]{1,0:T(8,128)(2,1)S(1)}, bf16[272,1024]{1,0:T(8,128)(2,1)S(1)}, u32[]{:S(2)}, u32[]{:S(2)}) collective-permute-start(bf16[272,1024]{1,0:T(8,128)(2,1)S(1)} %collective-permute-done.1.refs_1_), channel_id=1, source_target_pairs={{0,1},{1,0},{2,6},{3,7},{4,5},{5,4},{6,2},{7,3},{8,9},{9,8},{10,14... | collective-permute-start | bytes 1671176 | tf_op jit(solution)/shard_map/ppermute | solution.py:315
  24.3 0.8 copy-start.6
  25.1 21.5 %collective-permute-start.3 = (bf16[272,1024]{1,0:T(8,128)(2,1)}, bf16[272,1024]{1,0:T(8,128)(2,1)}, u32[]{:S(2)}, u32[]{:S(2)}) collective-permute-start(bf16[272,1024]{1,0:T(8,128)(2,1)} %collective-permute-done.2.refs_0_), channel_id=1, source_target_pairs={{0,1},{1,0},{2,6},{3,7},{4,5},{5,4},{6,2},{7,3},{8,9},{9,8},{10,14... | collective-permute-start | bytes 1671176 | tf_op jit(solution)/shard_map/ppermute | solution.py:315
  38.0 0.8 copy-start.8
  38.8 9.5 %collective-permute-start.7 = (bf16[272,1024]{1,0:T(8,128)(2,1)S(1)}, bf16[272,1024]{1,0:T(8,128)(2,1)S(1)}, u32[]{:S(2)}, u32[]{:S(2)}) collective-permute-start(bf16[272,1024]{1,0:T(8,128)(2,1)S(1)} %collective-permute-done.6.refs_0_), channel_id=1, source_target_pairs={{0,1},{1,0},{2,6},{3,7},{4,5},{5,4},{6,2},{7,3},{8,9},{9,8},{10,14... | collective-permute-start | bytes 1671176 | tf_op jit(solution)/shard_map/ppermute | solution.py:315
  39.3 15.1 %collective-permute-start.8 = (bf16[272,1024]{1,0:T(8,128)(2,1)}, bf16[272,1024]{1,0:T(8,128)(2,1)}, u32[]{:S(2)}, u32[]{:S(2)}) collective-permute-start(bf16[272,1024]{1,0:T(8,128)(2,1)} %collective-permute-done.5.refs_1_), channel_id=1, source_target_pairs={{0,1},{1,0},{2,6},{3,7},{4,5},{5,4},{6,2},{7,3},{8,9},{9,8},{10,14... | collective-permute-start | bytes 1671176 | tf_op jit(solution)/shard_map/ppermute | solution.py:315
  40.8 13.6 %collective-permute-start.9 = (bf16[272,1024]{1,0:T(8,128)(2,1)S(1)}, bf16[272,1024]{1,0:T(8,128)(2,1)S(1)}, u32[]{:S(2)}, u32[]{:S(2)}) collective-permute-start(bf16[272,1024]{1,0:T(8,128)(2,1)S(1)} %collective-permute-done.6.refs_0_), channel_id=1, source_target_pairs={{0,8},{1,9},{2,10},{3,11},{4,12},{5,13},{6,14},{7,15},{8,24},{9,25... | collective-permute-start | bytes 1671176 | tf_op jit(solution)/shard_map/ppermute | solution.py:315
  40.9 1.1 copy-start.3
  41.9 1.1 copy-start.5
  43.0 1.1 copy-start.7
  44.0 1.1 copy-start.9
  45.1 15.3 %copy-start.1 = (bf16[1,384,2048]{2,1,0:T(8,128)(2,1)S(1)}, bf16[1,384,2048]{2,1,0:T(8,128)(2,1)}, u32[]{:S(2)}) copy-start(bf16[1,384,2048]{2,1,0:T(8,128)(2,1)} %param.12) | copy-start | bytes 4718596
  46.6 13.8 %copy-start = (bf16[1,384,2048]{2,1,0:T(8,128)(2,1)S(1)}, bf16[1,384,2048]{2,1,0:T(8,128)(2,1)}, u32[]{:S(2)}) copy-start(bf16[1,384,2048]{2,1,0:T(8,128)(2,1)} %param.11) | copy-start | bytes 4718596
  54.4 6.0 %collective-permute-start.13 = (bf16[2,144,2048]{2,1,0:T(8,128)(2,1)S(1)}, bf16[2,144,2048]{2,1,0:T(8,128)(2,1)S(1)}, u32[]{:S(2)}, u32[]{:S(2)}) collective-permute-start(bf16[2,144,2048]{2,1,0:T(8,128)(2,1)S(1)} %get-tuple-element.128), channel_id=1, source_target_pairs={{0,2},{1,3},{2,0},{3,1},{4,6},{5,7},{6,4},{7,5},{8,10},{9,11},{10,... | collective-permute-start | bytes 3538952 | tf_op jit(solution)/shard_map/ppermute | solution.py:315
  54.9 15.6 %collective-permute-start.11 = (bf16[272,1024]{1,0:T(8,128)(2,1)}, bf16[272,1024]{1,0:T(8,128)(2,1)S(1)}, u32[]{:S(2)}, u32[]{:S(2)}) collective-permute-start(bf16[272,1024]{1,0:T(8,128)(2,1)} %collective-permute-done.5.refs_1_), channel_id=1, source_target_pairs={{0,8},{1,9},{2,10},{3,11},{4,12},{5,13},{6,14},{7,15},{8,24},{9,25... | collective-permute-start | bytes 1671176 | tf_op jit(solution)/shard_map/ppermute | solution.py:315
  56.5 14.5 %collective-permute-start.10 = (bf16[272,1024]{1,0:T(8,128)(2,1)S(1)}, bf16[272,1024]{1,0:T(8,128)(2,1)S(1)}, u32[]{:S(2)}, u32[]{:S(2)}) collective-permute-start(bf16[272,1024]{1,0:T(8,128)(2,1)S(1)} %collective-permute-done.9.refs_0_), channel_id=1, source_target_pairs={{0,1},{1,0},{2,6},{3,7},{4,5},{5,4},{6,2},{7,3},{8,9},{9,8},{10,14... | collective-permute-start | bytes 1671176 | tf_op jit(solution)/shard_map/ppermute | solution.py:315
  57.1 13.8 %collective-permute-start.12 = (bf16[272,1024]{1,0:T(8,128)(2,1)S(1)}, bf16[272,1024]{1,0:T(8,128)(2,1)S(1)}, u32[]{:S(2)}, u32[]{:S(2)}) collective-permute-start(bf16[272,1024]{1,0:T(8,128)(2,1)S(1)} %collective-permute-done.9.refs_0_), channel_id=1, source_target_pairs={{0,4},{1,5},{2,3},{3,2},{4,0},{5,1},{6,7},{7,6},{8,12},{9,13},{10,... | collective-permute-start | bytes 1671176 | tf_op jit(solution)/shard_map/ppermute | solution.py:315
  70.9 5.0 %collective-permute-start.17 = (bf16[2,144,2048]{2,1,0:T(8,128)(2,1)S(1)}, bf16[2,144,2048]{2,1,0:T(8,128)(2,1)S(1)}, u32[]{:S(2)}, u32[]{:S(2)}) collective-permute-start(bf16[2,144,2048]{2,1,0:T(8,128)(2,1)S(1)} %get-tuple-element.142), channel_id=1, source_target_pairs={{0,2},{1,3},{2,0},{3,1},{4,6},{5,7},{6,4},{7,5},{8,10},{9,11},{10,... | collective-permute-start | bytes 3538952 | tf_op jit(solution)/shard_map/ppermute | solution.py:315
  70.9 3.7 %collective-permute-start.14 = (bf16[144,2048]{1,0:T(8,128)(2,1)S(1)}, bf16[144,2048]{1,0:T(8,128)(2,1)S(1)}, u32[]{:S(2)}, u32[]{:S(2)}) collective-permute-start(bf16[144,2048]{1,0:T(8,128)(2,1)S(1)} %get-tuple-element.136), channel_id=1, source_target_pairs={{0,2},{1,3},{2,0},{3,1},{4,6},{5,7},{6,4},{7,5},{8,10},{9,11},{10,... | collective-permute-start | bytes 1769480 | tf_op jit(solution)/shard_map/ppermute | solution.py:315
  71.5 9.5 %collective-permute-start.19 = (bf16[272,1024]{1,0:T(8,128)(2,1)S(1)}, bf16[272,1024]{1,0:T(8,128)(2,1)S(1)}, u32[]{:S(2)}, u32[]{:S(2)}) collective-permute-start(bf16[272,1024]{1,0:T(8,128)(2,1)S(1)} %collective-permute-done.11.refs_1_), channel_id=1, source_target_pairs={{0,1},{1,0},{2,6},{3,7},{4,5},{5,4},{6,2},{7,3},{8,9},{9,8},{10,14... | collective-permute-start | bytes 1671176 | tf_op jit(solution)/shard_map/ppermute | solution.py:315
  72.3 14.6 %collective-permute-start.16 = (bf16[272,1024]{1,0:T(8,128)(2,1)S(1)}, bf16[272,1024]{1,0:T(8,128)(2,1)S(1)}, u32[]{:S(2)}, u32[]{:S(2)}) collective-permute-start(bf16[272,1024]{1,0:T(8,128)(2,1)S(1)} %collective-permute-done.12.refs_1_), channel_id=1, source_target_pairs={{0,1},{1,0},{2,6},{3,7},{4,5},{5,4},{6,2},{7,3},{8,9},{9,8},{10,14... | collective-permute-start | bytes 1671176 | tf_op jit(solution)/shard_map/ppermute | solution.py:315
  82.5 13.1 %collective-permute-start.21 = (bf16[2,144,2048]{2,1,0:T(8,128)(2,1)S(1)}, bf16[2,144,2048]{2,1,0:T(8,128)(2,1)S(1)}, u32[]{:S(2)}, u32[]{:S(2)}) collective-permute-start(bf16[2,144,2048]{2,1,0:T(8,128)(2,1)S(1)} %get-tuple-element.170), channel_id=1, source_target_pairs={{0,2},{1,3},{2,0},{3,1},{4,6},{5,7},{6,4},{7,5},{8,10},{9,11},{10,... | collective-permute-start | bytes 3538952 | tf_op jit(solution)/shard_map/ppermute | solution.py:315
  88.5 12.1 %collective-permute-start.18 = (bf16[2,144,2048]{2,1,0:T(8,128)(2,1)S(1)}, bf16[2,144,2048]{2,1,0:T(8,128)(2,1)S(1)}, u32[]{:S(2)}, u32[]{:S(2)}) collective-permute-start(bf16[2,144,2048]{2,1,0:T(8,128)(2,1)S(1)} %get-tuple-element.158), channel_id=1, source_target_pairs={{0,2},{1,3},{2,0},{3,1},{4,6},{5,7},{6,4},{7,5},{8,10},{9,11},{10,... | collective-permute-start | bytes 3538952 | tf_op jit(solution)/shard_map/ppermute | solution.py:315
  88.6 3.7 %collective-permute-start.20 = (bf16[144,2048]{1,0:T(8,128)(2,1)S(1)}, bf16[144,2048]{1,0:T(8,128)(2,1)S(1)}, u32[]{:S(2)}, u32[]{:S(2)}) collective-permute-start(bf16[144,2048]{1,0:T(8,128)(2,1)S(1)} %get-tuple-element.167), channel_id=1, source_target_pairs={{0,2},{1,3},{2,0},{3,1},{4,6},{5,7},{6,4},{7,5},{8,10},{9,11},{10,... | collective-permute-start | bytes 1769480 | tf_op jit(solution)/shard_map/ppermute | solution.py:315
  93.5 12.8 %collective-permute-start.28 = (bf16[2,128,1024]{2,1,0:T(8,128)(2,1)S(1)}, bf16[2,128,1024]{2,1,0:T(8,128)(2,1)S(1)}, u32[]{:S(2)}, u32[]{:S(2)}) collective-permute-start(bf16[2,128,1024]{2,1,0:T(8,128)(2,1)S(1)} %get-tuple-element.168), channel_id=1, source_target_pairs={{0,1},{1,0},{2,6},{3,7},{4,5},{5,4},{6,2},{7,3},{8,9},{9,8},{10,14... | collective-permute-start | bytes 1572872 | tf_op jit(solution)/shard_map/ppermute | solution.py:315
  94.5 23.4 %collective-permute-start.15 = (bf16[2,128,1024]{2,1,0:T(8,128)(2,1)S(1)}, bf16[2,128,1024]{2,1,0:T(8,128)(2,1)S(1)}, u32[]{:S(2)}, u32[]{:S(2)}) collective-permute-start(bf16[2,128,1024]{2,1,0:T(8,128)(2,1)S(1)} %get-tuple-element.138), channel_id=1, source_target_pairs={{0,1},{1,0},{2,6},{3,7},{4,5},{5,4},{6,2},{7,3},{8,9},{9,8},{10,14... | collective-permute-start | bytes 1572872 | tf_op jit(solution)/shard_map/ppermute | solution.py:315
  100.5 7.6 %collective-permute-start.22 = (bf16[144,2048]{1,0:T(8,128)(2,1)S(1)}, bf16[144,2048]{1,0:T(8,128)(2,1)S(1)}, u32[]{:S(2)}, u32[]{:S(2)}) collective-permute-start(bf16[144,2048]{1,0:T(8,128)(2,1)S(1)} %get-tuple-element.185), channel_id=1, source_target_pairs={{0,2},{1,3},{2,0},{3,1},{4,6},{5,7},{6,4},{7,5},{8,10},{9,11},{10,... | collective-permute-start | bytes 1769480 | tf_op jit(solution)/shard_map/ppermute | solution.py:315
  105.7 4.4 %collective-permute-start.23 = (bf16[144,2048]{1,0:T(8,128)(2,1)S(1)}, bf16[144,2048]{1,0:T(8,128)(2,1)S(1)}, u32[]{:S(2)}, u32[]{:S(2)}) collective-permute-start(bf16[144,2048]{1,0:T(8,128)(2,1)S(1)} %get-tuple-element.188), channel_id=1, source_target_pairs={{0,2},{1,3},{2,0},{3,1},{4,6},{5,7},{6,4},{7,5},{8,10},{9,11},{10,... | collective-permute-start | bytes 1769480 | tf_op jit(solution)/shard_map/ppermute | solution.py:315
  106.5 8.3 %collective-permute-start.29 = (bf16[128,1024]{1,0:T(8,128)(2,1)S(1)}, bf16[128,1024]{1,0:T(8,128)(2,1)S(1)}, u32[]{:S(2)}, u32[]{:S(2)}) collective-permute-start(bf16[128,1024]{1,0:T(8,128)(2,1)S(1)} %fusion.17), channel_id=1, source_target_pairs={{0,4},{1,5},{2,3},{3,2},{4,0},{5,1},{6,7},{7,6},{8,12},{9,13},{10,... | collective-permute-start | bytes 786440 | tf_op jit(solution)/shard_map/ppermute | solution.py:315
  109.4 12.2 %collective-permute-start.26 = (bf16[2,128,1024]{2,1,0:T(8,128)(2,1)S(1)}, bf16[2,128,1024]{2,1,0:T(8,128)(2,1)S(1)}, u32[]{:S(2)}, u32[]{:S(2)}) collective-permute-start(bf16[2,128,1024]{2,1,0:T(8,128)(2,1)S(1)} %get-tuple-element.186), channel_id=1, source_target_pairs={{0,1},{1,0},{2,6},{3,7},{4,5},{5,4},{6,2},{7,3},{8,9},{9,8},{10,14... | collective-permute-start | bytes 1572872 | tf_op jit(solution)/shard_map/ppermute | solution.py:315
  111.4 15.5 %collective-permute-start.24 = (bf16[2,128,1024]{2,1,0:T(8,128)(2,1)S(1)}, bf16[2,128,1024]{2,1,0:T(8,128)(2,1)S(1)}, u32[]{:S(2)}, u32[]{:S(2)}) collective-permute-start(bf16[2,128,1024]{2,1,0:T(8,128)(2,1)S(1)} %get-tuple-element.189), channel_id=1, source_target_pairs={{0,1},{1,0},{2,6},{3,7},{4,5},{5,4},{6,2},{7,3},{8,9},{9,8},{10,14... | collective-permute-start | bytes 1572872 | tf_op jit(solution)/shard_map/ppermute | solution.py:315
  114.8 12.3 %collective-permute-start.30 = (bf16[128,1024]{1,0:T(8,128)(2,1)S(1)}, bf16[128,1024]{1,0:T(8,128)(2,1)S(1)}, u32[]{:S(2)}, u32[]{:S(2)}) collective-permute-start(bf16[128,1024]{1,0:T(8,128)(2,1)S(1)} %fusion.4), channel_id=1, source_target_pairs={{0,8},{1,9},{2,10},{3,11},{4,12},{5,13},{6,14},{7,15},{8,24},{9,25... | collective-permute-start | bytes 786440 | tf_op jit(solution)/shard_map/ppermute | solution.py:315
  121.8 6.4 %collective-permute-start.27 = (bf16[128,1024]{1,0:T(8,128)(2,1)S(1)}, bf16[128,1024]{1,0:T(8,128)(2,1)S(1)}, u32[]{:S(2)}, u32[]{:S(2)}) collective-permute-start(bf16[128,1024]{1,0:T(8,128)(2,1)S(1)} %fusion.16), channel_id=1, source_target_pairs={{0,4},{1,5},{2,3},{3,2},{4,0},{5,1},{6,7},{7,6},{8,12},{9,13},{10,... | collective-permute-start | bytes 786440 | tf_op jit(solution)/shard_map/ppermute | solution.py:315
  127.1 6.7 %collective-permute-start.25 = (bf16[128,1024]{1,0:T(8,128)(2,1)S(1)}, bf16[128,1024]{1,0:T(8,128)(2,1)S(1)}, u32[]{:S(2)}, u32[]{:S(2)}) collective-permute-start(bf16[128,1024]{1,0:T(8,128)(2,1)S(1)} %fusion.15), channel_id=1, source_target_pairs={{0,4},{1,5},{2,3},{3,2},{4,0},{5,1},{6,7},{7,6},{8,12},{9,13},{10,... | collective-permute-start | bytes 786440 | tf_op jit(solution)/shard_map/ppermute | solution.py:315
  128.3 8.1 %collective-permute-start.31 = (bf16[128,1024]{1,0:T(8,128)(2,1)S(1)}, bf16[128,1024]{1,0:T(8,128)(2,1)S(1)}, u32[]{:S(2)}, u32[]{:S(2)}) collective-permute-start(bf16[128,1024]{1,0:T(8,128)(2,1)S(1)} %fusion.7), channel_id=1, source_target_pairs={{0,8},{1,9},{2,10},{3,11},{4,12},{5,13},{6,14},{7,15},{8,24},{9,25... | collective-permute-start | bytes 786440 | tf_op jit(solution)/shard_map/ppermute | solution.py:315
  136.5 7.3 %collective-permute-start.33 = (bf16[128,1024]{1,0:T(8,128)(2,1)S(1)}, bf16[128,1024]{1,0:T(8,128)(2,1)S(1)}, u32[]{:S(2)}, u32[]{:S(2)}) collective-permute-start(bf16[128,1024]{1,0:T(8,128)(2,1)S(1)} %fusion.10), channel_id=1, source_target_pairs={{0,8},{1,9},{2,10},{3,11},{4,12},{5,13},{6,14},{7,15},{8,24},{9,25... | collective-permute-start | bytes 786440 | tf_op jit(solution)/shard_map/ppermute | solution.py:315
  137.4 6.4 %collective-permute-start.32 = (bf16[128,1024]{1,0:T(8,128)(2,1)S(1)}, bf16[128,1024]{1,0:T(8,128)(2,1)S(1)}, u32[]{:S(2)}, u32[]{:S(2)}) collective-permute-start(bf16[128,1024]{1,0:T(8,128)(2,1)S(1)} %fusion.14), channel_id=1, source_target_pairs={{0,4},{1,5},{2,3},{3,2},{4,0},{5,1},{6,7},{7,6},{8,12},{9,13},{10,... | collective-permute-start | bytes 786440 | tf_op jit(solution)/shard_map/ppermute | solution.py:315

commit v14 on v13

--- a/solution.py
+++ b/solution.py
@@ -381,15 +381,24 @@
         mark.append(send)
     if parts is not None:
         mark.append(parts[1])
+    crossed = None
+    if parts is not None:
+        picks, near, far = parts
+        crossed = to_core(far)
     while done < chunks:
         shares = tied([have[kind, done] for kind in "sfab"], mark)
-        mine, theirs, picks = pick_rows(place, shares, top, rows, pair_slots)
-        if parts is not None:
-            keep, send = placed(*parts)
-            late.append((keep, to_second(send)))
-            mine, parts = tied(mine, send), None
+        rows_of = pick_rows(place, shares, top, rows, pair_slots)
+        last.append(rows_of)
+        mark = [crossed]
+        done += 1
+    if crossed is not None:
+        keep, send = place_rows(place, picks, near, crossed, rows, width)
+        late.append((keep, to_second(send)))
+    done -= len(last)
+    for i, (mine, theirs, picks) in enumerate(last):
+        mine = tied(mine, send) if i == 0 else mine
         near, far, *kept = run_experts(done, chunks, mine, to_core(theirs), weights, kept)
-        last.append((picks, near, far))
+        last[i] = picks, near, far
         done += 1
     nears = [near for _, near, _ in last]
     near, send = nears[-1], nears[0]
@@ -401,12 +410,12 @@
     running = None
     for c in range(1, chunks):
         keep, came = late[c]
-        if c + 1 < chunks:
-            came = tied(came, ties[c - 1])
+        came = tied(came, ties[c - 1] if c + 1 < chunks else previous)
         pair = added(keep, came)
         came = to_first(pair[1].astype(jnp.bfloat16))
         total = added(pair[0], tied(came, send) if c == 1 else came)
         running = (total if running is None else added(total, running)).astype(jnp.bfloat16)
+        previous = running
         if c > 1:
             marks[min(c - 1, 2)] = running
         if c + 1 < chunks:

time: 145 us -> 150 us (1.034)
  waiting for transfers between devices: 58.2 us -> 62.5 us
    ppermute x34, waiting for transfers between devices: 58.2 us -> 62.5 us  [permute(): return lax.ppermute(value, ('expert', 'etp'), pairs)]
  transfers between devices with their start and end apart: 34 -> 34, of which waited for: 17 -> 15; matrix products, arithmetic and copies ran while one was open for 8% -> 7% of each run, Pallas kernels for 22% -> 21%
where the time goes in v14:
time: 150 us
  waiting for transfers between devices  62.5 us (42%)
  Pallas kernels  34.1 us (23%)
  starting transfers between devices  33.7 us (22%)
  matrix products  10.2 us (7%)
  local copies, waits for them, and re-layouts  6.76 us (5%)
  other arithmetic  1.78 us (1%)
    ppermute x34, waiting for transfers between devices, permute(): return lax.ppermute(value, ('expert', 'etp'), pairs)  62.5 us
    ppermute x34, starting transfers between devices, permute(): return lax.ppermute(value, ('expert', 'etp'), pairs)  33.7 us
    pallas_call x4, Pallas kernels, run_experts(): pl.pallas_call(functools.partial(expert_kernel, index, kept is not None),...  19.9 us
    pallas_call x4, Pallas kernels, pick_rows(): pl.pallas_call(functools.partial(pick_kernel, top, rows), in_specs=[pl.Bl...  7.05 us
    unnamed x20, local copies, waits for them, and re-layouts  6.63 us
    pallas_call x4, Pallas kernels, place_rows(): pl.pallas_call(place_kernel, in_specs=[pl.BlockSpec(memory_space=pltpu.SM...  5.09 us
    dot_general x1, matrix products, gather_body(): lax.dot_general(acts, rows_g, CONTRACT_FIRST, preferred_element_type=jnp....  3.4 us
    dot_general x1, matrix products, gather_body(): lax.dot_general(gate_term, rows_x, CONTRACT_FIRST, preferred_element_type...  3.38 us
  transfers between devices with their start and end apart: 34, of which 15 were waited for; matrix products, arithmetic and copies ran while one was open for 7% of the time, Pallas kernels for 21%

profile of v14, /device:TPU:0, one launch (start us, length us, event | category | flops | bytes accessed | tf_op | source)
XLA Modules:
  0.0 149.9 jit_solution(11993893239979501600)
XLA Ops:
  0.6 2.0 %pack.1.refs_0_ = bf16[272,1024]{1,0:T(8,128)(2,1)} custom-call(bf16[128,1024]{1,0:T(8,128)(2,1)} %tokens_ref.1, bf16[128,1024]{1,0:T(8,128)(2,1)} %grads_ref.1, s32[8,128]{1,0:T(8,128)} %bitcast.70, f32[8,128]{1,0:T(8,128)} %bitcast.71), custom_call_target="tpu_custom_call" | custom-call | tf_op jit(solution)/shard_map/pack/pallas_call | solution.py:128
  2.6 2.9 %collective-permute-start = (bf16[272,1024]{1,0:T(8,128)(2,1)}, bf16[272,1024]{1,0:T(8,128)(2,1)S(1)}, u32[]{:S(2)}, u32[]{:S(2)}) collective-permute-start(bf16[272,1024]{1,0:T(8,128)(2,1)} %pack.1.refs_0_), channel_id=1, source_target_pairs={{0,1},{1,0},{2,6},{3,7},{4,5},{5,4},{6,2},{7,3},{8,9},{9,8},{10,14... | collective-permute-start | bytes 1671176 | tf_op jit(solution)/shard_map/ppermute | solution.py:315
  5.6 1.5 %collective-permute-start.1 = (bf16[272,1024]{1,0:T(8,128)(2,1)}, bf16[272,1024]{1,0:T(8,128)(2,1)S(1)}, u32[]{:S(2)}, u32[]{:S(2)}) collective-permute-start(bf16[272,1024]{1,0:T(8,128)(2,1)} %pack.1.refs_0_), channel_id=1, source_target_pairs={{0,4},{1,5},{2,3},{3,2},{4,0},{5,1},{6,7},{7,6},{8,12},{9,13},{10,... | collective-permute-start | bytes 1671176 | tf_op jit(solution)/shard_map/ppermute | solution.py:315
  7.1 1.6 %collective-permute-start.2 = (bf16[272,1024]{1,0:T(8,128)(2,1)}, bf16[272,1024]{1,0:T(8,128)(2,1)}, u32[]{:S(2)}, u32[]{:S(2)}) collective-permute-start(bf16[272,1024]{1,0:T(8,128)(2,1)} %pack.1.refs_0_), channel_id=1, source_target_pairs={{0,8},{1,9},{2,10},{3,11},{4,12},{5,13},{6,14},{7,15},{8,24},{9,25... | collective-permute-start | bytes 1671176 | tf_op jit(solution)/shard_map/ppermute | solution.py:315
  8.7 10.1 %collective-permute-done.refs_2_ = bf16[272,1024]{1,0:T(8,128)(2,1)S(1)} collective-permute-done((bf16[272,1024]{1,0:T(8,128)(2,1)}, bf16[272,1024]{1,0:T(8,128)(2,1)S(1)}, u32[]{:S(2)}, u32[]{:S(2)}) %collective-permute-start) | collective-permute-done | bytes 557088 | tf_op jit(solution)/shard_map/ppermute | solution.py:315
  19.6 2.5 %collective-permute-done.2.refs_0_ = bf16[272,1024]{1,0:T(8,128)(2,1)} collective-permute-done((bf16[272,1024]{1,0:T(8,128)(2,1)}, bf16[272,1024]{1,0:T(8,128)(2,1)}, u32[]{:S(2)}, u32[]{:S(2)}) %collective-permute-start.2) | collective-permute-done | bytes 557088 | tf_op jit(solution)/shard_map/ppermute | solution.py:315
  23.4 0.9 collective-permute-start.4
  25.1 1.1 collective-permute-start.3
  26.2 11.7 %collective-permute-done.5.refs_1_ = bf16[272,1024]{1,0:T(8,128)(2,1)} collective-permute-done((bf16[272,1024]{1,0:T(8,128)(2,1)}, bf16[272,1024]{1,0:T(8,128)(2,1)}, u32[]{:S(2)}, u32[]{:S(2)}) %collective-permute-start.5) | collective-permute-done | bytes 557088 | tf_op jit(solution)/shard_map/ppermute | solution.py:315
  39.3 1.5 collective-permute-start.8
  40.9 1.1 copy-done.3
  41.9 1.1 copy-done.5
  43.0 1.1 copy-done.7
  44.0 1.1 copy-done.9
  45.1 1.5 %pick.4 = (bf16[2,144,2048]{2,1,0:T(8,128)(2,1)S(1)}, bf16[2,144,2048]{2,1,0:T(8,128)(2,1)S(1)}, bf16[288,256]{1,0:T(8,128)(2,1)S(1)}) custom-call(s32[3]{0:T(128)S(1)} %pad_add_fusion.place_ref, bf16[272,1024]{1,0:T(8,128)(2,1)S(1)} %copy-done.3, bf16[272,1024]{1,0:T(8,128)(2,1)S(1)} %copy-done.7, bf16[272,1024]{1,0:T(8,128)(2,1)S(1)} %copy-done.5, ...), custom_call_target="tpu_custom_call" | custom-call | tf_op jit(solution)/shard_map/pick/pallas_call | solution.py:251
  46.6 1.7 %collective-permute-done.7.refs_2_ = bf16[272,1024]{1,0:T(8,128)(2,1)S(1)} collective-permute-done((bf16[272,1024]{1,0:T(8,128)(2,1)S(1)}, bf16[272,1024]{1,0:T(8,128)(2,1)S(1)}, u32[]{:S(2)}, u32[]{:S(2)}) %collective-permute-start.7) | collective-permute-done | bytes 557088 | tf_op jit(solution)/shard_map/ppermute | solution.py:315
  48.3 6.1 %collective-permute-done.8.refs_3_ = bf16[272,1024]{1,0:T(8,128)(2,1)} collective-permute-done((bf16[272,1024]{1,0:T(8,128)(2,1)}, bf16[272,1024]{1,0:T(8,128)(2,1)}, u32[]{:S(2)}, u32[]{:S(2)}) %collective-permute-start.8) | collective-permute-done | bytes 557088 | tf_op jit(solution)/shard_map/ppermute | solution.py:315
  54.9 1.6 %collective-permute-start.11 = (bf16[272,1024]{1,0:T(8,128)(2,1)}, bf16[272,1024]{1,0:T(8,128)(2,1)S(1)}, u32[]{:S(2)}, u32[]{:S(2)}) collective-permute-start(bf16[272,1024]{1,0:T(8,128)(2,1)} %collective-permute-done.5.refs_1_), channel_id=1, source_target_pairs={{0,8},{1,9},{2,10},{3,11},{4,12},{5,13},{6,14},{7,15},{8,24},{9,25... | collective-permute-start | bytes 1671176 | tf_op jit(solution)/shard_map/ppermute | solution.py:315
  57.8 2.5 %pick.5 = (bf16[2,144,2048]{2,1,0:T(8,128)(2,1)S(1)}, bf16[2,144,2048]{2,1,0:T(8,128)(2,1)S(1)}, bf16[288,256]{1,0:T(8,128)(2,1)S(1)}) custom-call(s32[3]{0:T(128)S(1)} %pad_add_fusion.place_ref, bf16[272,1024]{1,0:T(8,128)(2,1)} %collective-permute-done.2.refs_0_, bf16[272,1024]{1,0:T(8,128)(2,1)} %collective-permute-done.5.refs_1_, ...), custom_call_target="tpu_custom_call" | custom-call | tf_op jit(solution)/shard_map/pick/pallas_call | solution.py:251
  60.4 5.0 %experts.4 = (bf16[144,2048]{1,0:T(8,128)(2,1)S(1)}, bf16[144,2048]{1,0:T(8,128)(2,1)S(1)}, bf16[1152,2048]{1,0:T(8,128)(2,1)S(1)}, bf16[1152,2048]{1,0:T(8,128)...) custom-call(bf16[2,144,2048]{2,1,0:T(8,128)(2,1)S(1)} %get-tuple-element.128., ...), custom_call_target="tpu_custom_call" | custom-call | tf_op jit(solution)/shard_map/experts/pallas_call | solution.py:270
  65.5 5.1 %collective-permute-done.11.refs_1_ = bf16[272,1024]{1,0:T(8,128)(2,1)S(1)} collective-permute-done((bf16[272,1024]{1,0:T(8,128)(2,1)}, bf16[272,1024]{1,0:T(8,128)(2,1)S(1)}, u32[]{:S(2)}, u32[]{:S(2)}) %collective-permute-start.11) | collective-permute-done | bytes 557088 | tf_op jit(solution)/shard_map/ppermute | solution.py:315
  72.3 1.5 collective-permute-done.17.theirs_ref
  73.8 4.9 %experts.5 = (bf16[144,2048]{1,0:T(8,128)(2,1)S(1)}, bf16[144,2048]{1,0:T(8,128)(2,1)S(1)}, bf16[1152,2048]{1,0:T(8,128)(2,1)S(1)}, bf16[1152,2048]{1,0:T(8,128)...) custom-call(bf16[2,144,2048]{2,1,0:T(8,128)(2,1)S(1)} %get-tuple-ele, ...), custom_call_target="tpu_custom_call", output_to_operand_aliasing={{2}: (5, {}), {3}: (6, {}), {4}: (7, {}), {5}: (8, {}), {6}... | custom-call | tf_op jit(solution)/shard_map/experts/pallas_call | solution.py:270
  79.8 1.3 place.4
  81.1 1.5 %pick.7 = (bf16[2,144,2048]{2,1,0:T(8,128)(2,1)S(1)}, bf16[2,144,2048]{2,1,0:T(8,128)(2,1)S(1)}, bf16[288,256]{1,0:T(8,128)(2,1)S(1)}) custom-call(s32[3]{0:T(128)S(1)} %pad_add_fusion.place_ref, bf16[272,1024]{1,0:T(8,128)(2,1)S(1)} %collective-permute-done.6.refs_0_, bf16[272,1024]{1,0:T(8,128)(2,1)S(1)} %collective-permute-done.11.refs_1_, ...), custom_call_target="tpu_custom_call" | custom-call | tf_op jit(solution)/shard_map/pick/pallas_call | solution.py:251
  83.4 5.0 %collective-permute-done.16.refs_3_ = bf16[272,1024]{1,0:T(8,128)(2,1)S(1)} collective-permute-done((bf16[272,1024]{1,0:T(8,128)(2,1)S(1)}, bf16[272,1024]{1,0:T(8,128)(2,1)S(1)}, u32[]{:S(2)}, u32[]{:S(2)}) %collective-permute-start.16) | collective-permute-done | bytes 557088 | tf_op jit(solution)/shard_map/ppermute | solution.py:315
  88.4 1.5 %pick.6 = (bf16[2,144,2048]{2,1,0:T(8,128)(2,1)S(1)}, bf16[2,144,2048]{2,1,0:T(8,128)(2,1)S(1)}, bf16[288,256]{1,0:T(8,128)(2,1)S(1)}) custom-call(s32[3]{0:T(128)S(1)} %pad_add_fusion.place_ref, bf16[272,1024]{1,0:T(8,128)(2,1)S(1)} %collective-permute-done.9.refs_0_, bf16[272,1024]{1,0:T(8,128)(2,1)S(1)} %collective-permute-done.12.refs_1_, ...), custom_call_target="tpu_custom_call" | custom-call | tf_op jit(solution)/shard_map/pick/pallas_call | solution.py:251
  90.0 1.3 place.5
  91.3 0.9 collective-permute-start.27
  92.2 4.9 %experts.6 = (bf16[144,2048]{1,0:T(8,128)(2,1)S(1)}, bf16[144,2048]{1,0:T(8,128)(2,1)S(1)}, bf16[1152,2048]{1,0:T(8,128)(2,1)S(1)}, bf16[1152,2048]{1,0:T(8,128)...) custom-call(bf16[2,144,2048]{2,1,0:T(8,128)(2,1)S(1)} %get-tuple-ele, ...), custom_call_target="tpu_custom_call", output_to_operand_aliasing={{2}: (5, {}), {3}: (6, {}), {4}: (7, {}), {5}: (8, {}), {6}... | custom-call | tf_op jit(solution)/shard_map/experts/pallas_call | solution.py:270
  97.1 0.9 collective-permute-start.22
  98.1 2.5 %collective-permute-done.27 = bf16[2,128,1024]{2,1,0:T(8,128)(2,1)S(1)} collective-permute-done((bf16[2,128,1024]{2,1,0:T(8,128)(2,1)S(1)}, bf16[2,128,1024]{2,1,0:T(8,128)(2,1)S(1)}, u32[]{:S(2)}, u32[]{:S(2)}) %collective-permute-start.27) | collective-permute-done | bytes 524320 | tf_op jit(solution)/shard_map/ppermute | solution.py:315
  100.6 5.1 %experts.7 = (bf16[144,2048]{1,0:T(8,128)(2,1)S(1)}, bf16[144,2048]{1,0:T(8,128)(2,1)S(1)}, bf16[1152,2048]{1,0:T(8,128)(2,1)S(1)}, bf16[1152,2048]{1,0:T(8,128)...) custom-call(bf16[2,144,2048]{2,1,0:T(8,128)(2,1)S(1)} %get-tuple-ele, ...), custom_call_target="tpu_custom_call", output_to_operand_aliasing={{2}: (5, {}), {3}: (6, {}), {4}: (7, {}), {5}: (8, {}), {6}... | custom-call | tf_op jit(solution)/shard_map/experts/pallas_call | solution.py:270
  105.9 1.3 place.6
  107.2 0.9 collective-permute-start.25
  108.2 1.4 collective-permute-start.28
  109.5 1.4 collective-permute-start.15
  110.9 1.3 place.7
  112.9 4.6 %collective-permute-done.28 = bf16[128,1024]{1,0:T(8,128)(2,1)S(1)} collective-permute-done((bf16[128,1024]{1,0:T(8,128)(2,1)S(1)}, bf16[128,1024]{1,0:T(8,128)(2,1)S(1)}, u32[]{:S(2)}, u32[]{:S(2)}) %collective-permute-start.28) | collective-permute-done | bytes 262176 | tf_op jit(solution)/shard_map/ppermute | solution.py:315
  117.5 2.3 %collective-permute-start.29 = (bf16[128,1024]{1,0:T(8,128)(2,1)S(1)}, bf16[128,1024]{1,0:T(8,128)(2,1)S(1)}, u32[]{:S(2)}, u32[]{:S(2)}) collective-permute-start(bf16[128,1024]{1,0:T(8,128)(2,1)S(1)} %fusion.7), channel_id=1, source_target_pairs={{0,8},{1,9},{2,10},{3,11},{4,12},{5,13},{6,14},{7,15},{8,24},{9,25... | collective-permute-start | bytes 786440 | tf_op jit(solution)/shard_map/ppermute | solution.py:315
  120.9 6.8 %collective-permute-done.15 = bf16[2,128,1024]{2,1,0:T(8,128)(2,1)S(1)} collective-permute-done((bf16[2,128,1024]{2,1,0:T(8,128)(2,1)S(1)}, bf16[2,128,1024]{2,1,0:T(8,128)(2,1)S(1)}, u32[]{:S(2)}, u32[]{:S(2)}) %collective-permute-start.15) | collective-permute-done | bytes 524320 | tf_op jit(solution)/shard_map/ppermute | solution.py:315
  127.7 3.4 %fusion.2 = bf16[1,384,2048]{2,1,0:T(8,128)(2,1)} fusion(bf16[1152,384]{1,0:T(8,128)(2,1)S(1)} %get-tuple-element.206, bf16[1152,2048]{1,0:T(8,128)(2,1)S(1)} %get-tuple-element.207), kind=kOutput, calls=%fused_computation.5 | convolution fusion | flops 1812725760 | bytes 7176192 | tf_op jit(solution)/shard_map/dot_general | solution.py:430
  131.4 2.7 %collective-permute-start.31 = (bf16[128,1024]{1,0:T(8,128)(2,1)S(1)}, bf16[128,1024]{1,0:T(8,128)(2,1)S(1)}, u32[]{:S(2)}, u32[]{:S(2)}) collective-permute-start(bf16[128,1024]{1,0:T(8,128)(2,1)S(1)} %fusion.10), channel_id=1, source_target_pairs={{0,8},{1,9},{2,10},{3,11},{4,12},{5,13},{6,14},{7,15},{8,24},{9,25... | collective-permute-start | bytes 786440 | tf_op jit(solution)/shard_map/ppermute | solution.py:315
  135.1 3.4 %fusion = bf16[1,384,2048]{2,1,0:T(8,128)(2,1)} fusion(bf16[1152,384]{1,0:T(8,128)(2,1)S(1)} %get-tuple-element.201, bf16[1152,2048]{1,0:T(8,128)(2,1)S(1)} %get-tuple-element.202), kind=kOutput, calls=%fused_computation.3 | convolution fusion | flops 1812725760 | bytes 7176192 | tf_op jit(solution)/shard_map/dot_general | solution.py:431
  138.8 2.0 %collective-permute-done.30 = bf16[128,1024]{1,0:T(8,128)(2,1)S(1)} collective-permute-done((bf16[128,1024]{1,0:T(8,128)(2,1)S(1)}, bf16[128,1024]{1,0:T(8,128)(2,1)S(1)}, u32[]{:S(2)}, u32[]{:S(2)}) %collective-permute-start.30) | collective-permute-done | bytes 262176 | tf_op jit(solution)/shard_map/ppermute | solution.py:315
  140.9 1.8 %collective-permute-start.33 = (bf16[128,1024]{1,0:T(8,128)(2,1)S(1)}, bf16[128,1024]{1,0:T(8,128)(2,1)S(1)}, u32[]{:S(2)}, u32[]{:S(2)}) collective-permute-start(bf16[128,1024]{1,0:T(8,128)(2,1)S(1)} %fusion.5), channel_id=1, source_target_pairs={{0,8},{1,9},{2,10},{3,11},{4,12},{5,13},{6,14},{7,15},{8,24},{9,25... | collective-permute-start | bytes 786440 | tf_op jit(solution)/shard_map/ppermute | solution.py:315
  143.5 3.4 %fusion.1 = bf16[1,384,2048]{2,1,0:T(8,128)(2,1)} fusion(bf16[1152,384]{1,0:T(8,128)(2,1)S(1)} %get-tuple-element.204, bf16[1152,2048]{1,0:T(8,128)(2,1)S(1)} %get-tuple-element.202), kind=kOutput, calls=%fused_computation.4 | convolution fusion | flops 1812725760 | bytes 7176192 | tf_op jit(solution)/shard_map/dot_general | solution.py:432
  146.8 2.3 %collective-permute-done.32 = bf16[128,1024]{1,0:T(8,128)(2,1)S(1)} collective-permute-done((bf16[128,1024]{1,0:T(8,128)(2,1)S(1)}, bf16[128,1024]{1,0:T(8,128)(2,1)S(1)}, u32[]{:S(2)}, u32[]{:S(2)}) %collective-permute-start.32) | collective-permute-done | bytes 262176 | tf_op jit(solution)/shard_map/ppermute | solution.py:315
  (69 shorter events, 15.2 us)
Async XLA Ops:
  0.6 59.8 %copy-start.2 = (bf16[1,384,2048]{2,1,0:T(8,128)(2,1)S(1)}, bf16[1,384,2048]{2,1,0:T(8,128)(2,1)}, u32[]{:S(2)}) copy-start(bf16[1,384,2048]{2,1,0:T(8,128)(2,1)} %param.13) | copy-start | bytes 4718596
  2.6 16.2 %collective-permute-start = (bf16[272,1024]{1,0:T(8,128)(2,1)}, bf16[272,1024]{1,0:T(8,128)(2,1)S(1)}, u32[]{:S(2)}, u32[]{:S(2)}) collective-permute-start(bf16[272,1024]{1,0:T(8,128)(2,1)} %pack.1.refs_0_), channel_id=1, source_target_pairs={{0,1},{1,0},{2,6},{3,7},{4,5},{5,4},{6,2},{7,3},{8,9},{9,8},{10,14... | collective-permute-start | bytes 1671176 | tf_op jit(solution)/shard_map/ppermute | solution.py:315
  5.6 14.0 %collective-permute-start.1 = (bf16[272,1024]{1,0:T(8,128)(2,1)}, bf16[272,1024]{1,0:T(8,128)(2,1)S(1)}, u32[]{:S(2)}, u32[]{:S(2)}) collective-permute-start(bf16[272,1024]{1,0:T(8,128)(2,1)} %pack.1.refs_0_), channel_id=1, source_target_pairs={{0,4},{1,5},{2,3},{3,2},{4,0},{5,1},{6,7},{7,6},{8,12},{9,13},{10,... | collective-permute-start | bytes 1671176 | tf_op jit(solution)/shard_map/ppermute | solution.py:315
  7.1 15.0 %collective-permute-start.2 = (bf16[272,1024]{1,0:T(8,128)(2,1)}, bf16[272,1024]{1,0:T(8,128)(2,1)}, u32[]{:S(2)}, u32[]{:S(2)}) collective-permute-start(bf16[272,1024]{1,0:T(8,128)(2,1)} %pack.1.refs_0_), channel_id=1, source_target_pairs={{0,8},{1,9},{2,10},{3,11},{4,12},{5,13},{6,14},{7,15},{8,24},{9,25... | collective-permute-start | bytes 1671176 | tf_op jit(solution)/shard_map/ppermute | solution.py:315
  18.8 0.8 copy-start.4
  22.1 15.8 %collective-permute-start.5 = (bf16[272,1024]{1,0:T(8,128)(2,1)}, bf16[272,1024]{1,0:T(8,128)(2,1)}, u32[]{:S(2)}, u32[]{:S(2)}) collective-permute-start(bf16[272,1024]{1,0:T(8,128)(2,1)} %collective-permute-done.2.refs_0_), channel_id=1, source_target_pairs={{0,4},{1,5},{2,3},{3,2},{4,0},{5,1},{6,7},{7,6},{8,12},{9,13},{10,... | collective-permute-start | bytes 1671176 | tf_op jit(solution)/shard_map/ppermute | solution.py:315
  22.7 15.3 %collective-permute-start.6 = (bf16[272,1024]{1,0:T(8,128)(2,1)}, bf16[272,1024]{1,0:T(8,128)(2,1)S(1)}, u32[]{:S(2)}, u32[]{:S(2)}) collective-permute-start(bf16[272,1024]{1,0:T(8,128)(2,1)} %collective-permute-done.2.refs_0_), channel_id=1, source_target_pairs={{0,8},{1,9},{2,10},{3,11},{4,12},{5,13},{6,14},{7,15},{8,24},{9,25... | collective-permute-start | bytes 1671176 | tf_op jit(solution)/shard_map/ppermute | solution.py:315
  23.4 14.6 %collective-permute-start.4 = (bf16[272,1024]{1,0:T(8,128)(2,1)S(1)}, bf16[272,1024]{1,0:T(8,128)(2,1)S(1)}, u32[]{:S(2)}, u32[]{:S(2)}) collective-permute-start(bf16[272,1024]{1,0:T(8,128)(2,1)S(1)} %collective-permute-done.1.refs_1_), channel_id=1, source_target_pairs={{0,1},{1,0},{2,6},{3,7},{4,5},{5,4},{6,2},{7,3},{8,9},{9,8},{10,14... | collective-permute-start | bytes 1671176 | tf_op jit(solution)/shard_map/ppermute | solution.py:315
  24.3 0.8 copy-start.6
  25.1 21.5 %collective-permute-start.3 = (bf16[272,1024]{1,0:T(8,128)(2,1)}, bf16[272,1024]{1,0:T(8,128)(2,1)}, u32[]{:S(2)}, u32[]{:S(2)}) collective-permute-start(bf16[272,1024]{1,0:T(8,128)(2,1)} %collective-permute-done.2.refs_0_), channel_id=1, source_target_pairs={{0,1},{1,0},{2,6},{3,7},{4,5},{5,4},{6,2},{7,3},{8,9},{9,8},{10,14... | collective-permute-start | bytes 1671176 | tf_op jit(solution)/shard_map/ppermute | solution.py:315
  38.0 0.8 copy-start.8
  38.8 9.5 %collective-permute-start.7 = (bf16[272,1024]{1,0:T(8,128)(2,1)S(1)}, bf16[272,1024]{1,0:T(8,128)(2,1)S(1)}, u32[]{:S(2)}, u32[]{:S(2)}) collective-permute-start(bf16[272,1024]{1,0:T(8,128)(2,1)S(1)} %collective-permute-done.6.refs_0_), channel_id=1, source_target_pairs={{0,1},{1,0},{2,6},{3,7},{4,5},{5,4},{6,2},{7,3},{8,9},{9,8},{10,14... | collective-permute-start | bytes 1671176 | tf_op jit(solution)/shard_map/ppermute | solution.py:315
  39.3 15.1 %collective-permute-start.8 = (bf16[272,1024]{1,0:T(8,128)(2,1)}, bf16[272,1024]{1,0:T(8,128)(2,1)}, u32[]{:S(2)}, u32[]{:S(2)}) collective-permute-start(bf16[272,1024]{1,0:T(8,128)(2,1)} %collective-permute-done.5.refs_1_), channel_id=1, source_target_pairs={{0,1},{1,0},{2,6},{3,7},{4,5},{5,4},{6,2},{7,3},{8,9},{9,8},{10,14... | collective-permute-start | bytes 1671176 | tf_op jit(solution)/shard_map/ppermute | solution.py:315
  40.8 13.6 %collective-permute-start.9 = (bf16[272,1024]{1,0:T(8,128)(2,1)S(1)}, bf16[272,1024]{1,0:T(8,128)(2,1)S(1)}, u32[]{:S(2)}, u32[]{:S(2)}) collective-permute-start(bf16[272,1024]{1,0:T(8,128)(2,1)S(1)} %collective-permute-done.6.refs_0_), channel_id=1, source_target_pairs={{0,8},{1,9},{2,10},{3,11},{4,12},{5,13},{6,14},{7,15},{8,24},{9,25... | collective-permute-start | bytes 1671176 | tf_op jit(solution)/shard_map/ppermute | solution.py:315
  40.9 1.1 copy-start.3
  41.9 1.1 copy-start.5
  43.0 1.1 copy-start.7
  44.0 1.1 copy-start.9
  45.1 15.3 %copy-start.1 = (bf16[1,384,2048]{2,1,0:T(8,128)(2,1)S(1)}, bf16[1,384,2048]{2,1,0:T(8,128)(2,1)}, u32[]{:S(2)}) copy-start(bf16[1,384,2048]{2,1,0:T(8,128)(2,1)} %param.12) | copy-start | bytes 4718596
  46.6 13.8 %copy-start = (bf16[1,384,2048]{2,1,0:T(8,128)(2,1)S(1)}, bf16[1,384,2048]{2,1,0:T(8,128)(2,1)}, u32[]{:S(2)}) copy-start(bf16[1,384,2048]{2,1,0:T(8,128)(2,1)} %param.11) | copy-start | bytes 4718596
  54.4 6.0 %collective-permute-start.13 = (bf16[2,144,2048]{2,1,0:T(8,128)(2,1)S(1)}, bf16[2,144,2048]{2,1,0:T(8,128)(2,1)S(1)}, u32[]{:S(2)}, u32[]{:S(2)}) collective-permute-start(bf16[2,144,2048]{2,1,0:T(8,128)(2,1)S(1)} %get-tuple-element.129), channel_id=1, source_target_pairs={{0,2},{1,3},{2,0},{3,1},{4,6},{5,7},{6,4},{7,5},{8,10},{9,11},{10,... | collective-permute-start | bytes 3538952 | tf_op jit(solution)/shard_map/ppermute | solution.py:315
  54.9 15.6 %collective-permute-start.11 = (bf16[272,1024]{1,0:T(8,128)(2,1)}, bf16[272,1024]{1,0:T(8,128)(2,1)S(1)}, u32[]{:S(2)}, u32[]{:S(2)}) collective-permute-start(bf16[272,1024]{1,0:T(8,128)(2,1)} %collective-permute-done.5.refs_1_), channel_id=1, source_target_pairs={{0,8},{1,9},{2,10},{3,11},{4,12},{5,13},{6,14},{7,15},{8,24},{9,25... | collective-permute-start | bytes 1671176 | tf_op jit(solution)/shard_map/ppermute | solution.py:315
  56.5 14.5 %collective-permute-start.10 = (bf16[272,1024]{1,0:T(8,128)(2,1)S(1)}, bf16[272,1024]{1,0:T(8,128)(2,1)S(1)}, u32[]{:S(2)}, u32[]{:S(2)}) collective-permute-start(bf16[272,1024]{1,0:T(8,128)(2,1)S(1)} %collective-permute-done.9.refs_0_), channel_id=1, source_target_pairs={{0,1},{1,0},{2,6},{3,7},{4,5},{5,4},{6,2},{7,3},{8,9},{9,8},{10,14... | collective-permute-start | bytes 1671176 | tf_op jit(solution)/shard_map/ppermute | solution.py:315
  57.1 13.8 %collective-permute-start.12 = (bf16[272,1024]{1,0:T(8,128)(2,1)S(1)}, bf16[272,1024]{1,0:T(8,128)(2,1)S(1)}, u32[]{:S(2)}, u32[]{:S(2)}) collective-permute-start(bf16[272,1024]{1,0:T(8,128)(2,1)S(1)} %collective-permute-done.9.refs_0_), channel_id=1, source_target_pairs={{0,4},{1,5},{2,3},{3,2},{4,0},{5,1},{6,7},{7,6},{8,12},{9,13},{10,... | collective-permute-start | bytes 1671176 | tf_op jit(solution)/shard_map/ppermute | solution.py:315
  70.9 2.8 %collective-permute-start.17 = (bf16[2,144,2048]{2,1,0:T(8,128)(2,1)S(1)}, bf16[2,144,2048]{2,1,0:T(8,128)(2,1)S(1)}, u32[]{:S(2)}, u32[]{:S(2)}) collective-permute-start(bf16[2,144,2048]{2,1,0:T(8,128)(2,1)S(1)} %get-tuple-element.143), channel_id=1, source_target_pairs={{0,2},{1,3},{2,0},{3,1},{4,6},{5,7},{6,4},{7,5},{8,10},{9,11},{10,... | collective-permute-start | bytes 3538952 | tf_op jit(solution)/shard_map/ppermute | solution.py:315
  70.9 8.8 %collective-permute-start.14 = (bf16[144,2048]{1,0:T(8,128)(2,1)S(1)}, bf16[144,2048]{1,0:T(8,128)(2,1)S(1)}, u32[]{:S(2)}, u32[]{:S(2)}) collective-permute-start(bf16[144,2048]{1,0:T(8,128)(2,1)S(1)} %get-tuple-element.137), channel_id=1, source_target_pairs={{0,2},{1,3},{2,0},{3,1},{4,6},{5,7},{6,4},{7,5},{8,10},{9,11},{10,... | collective-permute-start | bytes 1769480 | tf_op jit(solution)/shard_map/ppermute | solution.py:315
  71.5 9.6 %collective-permute-start.20 = (bf16[272,1024]{1,0:T(8,128)(2,1)S(1)}, bf16[272,1024]{1,0:T(8,128)(2,1)S(1)}, u32[]{:S(2)}, u32[]{:S(2)}) collective-permute-start(bf16[272,1024]{1,0:T(8,128)(2,1)S(1)} %collective-permute-done.11.refs_1_), channel_id=1, source_target_pairs={{0,1},{1,0},{2,6},{3,7},{4,5},{5,4},{6,2},{7,3},{8,9},{9,8},{10,14... | collective-permute-start | bytes 1671176 | tf_op jit(solution)/shard_map/ppermute | solution.py:315
  78.7 9.7 %collective-permute-start.18 = (bf16[144,2048]{1,0:T(8,128)(2,1)S(1)}, bf16[144,2048]{1,0:T(8,128)(2,1)S(1)}, u32[]{:S(2)}, u32[]{:S(2)}) collective-permute-start(bf16[144,2048]{1,0:T(8,128)(2,1)S(1)} %get-tuple-element.152), channel_id=1, source_target_pairs={{0,2},{1,3},{2,0},{3,1},{4,6},{5,7},{6,4},{7,5},{8,10},{9,11},{10,... | collective-permute-start | bytes 1769480 | tf_op jit(solution)/shard_map/ppermute | solution.py:315
  78.9 9.5 %collective-permute-start.16 = (bf16[272,1024]{1,0:T(8,128)(2,1)S(1)}, bf16[272,1024]{1,0:T(8,128)(2,1)S(1)}, u32[]{:S(2)}, u32[]{:S(2)}) collective-permute-start(bf16[272,1024]{1,0:T(8,128)(2,1)S(1)} %collective-permute-done.12.refs_1_), channel_id=1, source_target_pairs={{0,1},{1,0},{2,6},{3,7},{4,5},{5,4},{6,2},{7,3},{8,9},{9,8},{10,14... | collective-permute-start | bytes 1671176 | tf_op jit(solution)/shard_map/ppermute | solution.py:315
  82.6 9.7 %collective-permute-start.21 = (bf16[2,144,2048]{2,1,0:T(8,128)(2,1)S(1)}, bf16[2,144,2048]{2,1,0:T(8,128)(2,1)S(1)}, u32[]{:S(2)}, u32[]{:S(2)}) collective-permute-start(bf16[2,144,2048]{2,1,0:T(8,128)(2,1)S(1)} %get-tuple-element.171), channel_id=1, source_target_pairs={{0,2},{1,3},{2,0},{3,1},{4,6},{5,7},{6,4},{7,5},{8,10},{9,11},{10,... | collective-permute-start | bytes 3538952 | tf_op jit(solution)/shard_map/ppermute | solution.py:315
  89.9 10.6 %collective-permute-start.19 = (bf16[2,144,2048]{2,1,0:T(8,128)(2,1)S(1)}, bf16[2,144,2048]{2,1,0:T(8,128)(2,1)S(1)}, u32[]{:S(2)}, u32[]{:S(2)}) collective-permute-start(bf16[2,144,2048]{2,1,0:T(8,128)(2,1)S(1)} %get-tuple-element.159), channel_id=1, source_target_pairs={{0,2},{1,3},{2,0},{3,1},{4,6},{5,7},{6,4},{7,5},{8,10},{9,11},{10,... | collective-permute-start | bytes 3538952 | tf_op jit(solution)/shard_map/ppermute | solution.py:315
  91.3 9.2 %collective-permute-start.27 = (bf16[2,128,1024]{2,1,0:T(8,128)(2,1)S(1)}, bf16[2,128,1024]{2,1,0:T(8,128)(2,1)S(1)}, u32[]{:S(2)}, u32[]{:S(2)}) collective-permute-start(bf16[2,128,1024]{2,1,0:T(8,128)(2,1)S(1)} %get-tuple-element.169), channel_id=1, source_target_pairs={{0,1},{1,0},{2,6},{3,7},{4,5},{5,4},{6,2},{7,3},{8,9},{9,8},{10,14... | collective-permute-start | bytes 1572872 | tf_op jit(solution)/shard_map/ppermute | solution.py:315
  97.1 8.8 %collective-permute-start.22 = (bf16[144,2048]{1,0:T(8,128)(2,1)S(1)}, bf16[144,2048]{1,0:T(8,128)(2,1)S(1)}, u32[]{:S(2)}, u32[]{:S(2)}) collective-permute-start(bf16[144,2048]{1,0:T(8,128)(2,1)S(1)} %get-tuple-element.186), channel_id=1, source_target_pairs={{0,2},{1,3},{2,0},{3,1},{4,6},{5,7},{6,4},{7,5},{8,10},{9,11},{10,... | collective-permute-start | bytes 1769480 | tf_op jit(solution)/shard_map/ppermute | solution.py:315
  105.7 5.2 %collective-permute-start.23 = (bf16[144,2048]{1,0:T(8,128)(2,1)S(1)}, bf16[144,2048]{1,0:T(8,128)(2,1)S(1)}, u32[]{:S(2)}, u32[]{:S(2)}) collective-permute-start(bf16[144,2048]{1,0:T(8,128)(2,1)S(1)} %get-tuple-element.189), channel_id=1, source_target_pairs={{0,2},{1,3},{2,0},{3,1},{4,6},{5,7},{6,4},{7,5},{8,10},{9,11},{10,... | collective-permute-start | bytes 1769480 | tf_op jit(solution)/shard_map/ppermute | solution.py:315
  107.2 12.6 %collective-permute-start.25 = (bf16[2,128,1024]{2,1,0:T(8,128)(2,1)S(1)}, bf16[2,128,1024]{2,1,0:T(8,128)(2,1)S(1)}, u32[]{:S(2)}, u32[]{:S(2)}) collective-permute-start(bf16[2,128,1024]{2,1,0:T(8,128)(2,1)S(1)} %get-tuple-element.187), channel_id=1, source_target_pairs={{0,1},{1,0},{2,6},{3,7},{4,5},{5,4},{6,2},{7,3},{8,9},{9,8},{10,14... | collective-permute-start | bytes 1572872 | tf_op jit(solution)/shard_map/ppermute | solution.py:315
  108.2 9.3 %collective-permute-start.28 = (bf16[128,1024]{1,0:T(8,128)(2,1)S(1)}, bf16[128,1024]{1,0:T(8,128)(2,1)S(1)}, u32[]{:S(2)}, u32[]{:S(2)}) collective-permute-start(bf16[128,1024]{1,0:T(8,128)(2,1)S(1)} %fusion.16), channel_id=1, source_target_pairs={{0,4},{1,5},{2,3},{3,2},{4,0},{5,1},{6,7},{7,6},{8,12},{9,13},{10,... | collective-permute-start | bytes 786440 | tf_op jit(solution)/shard_map/ppermute | solution.py:315
  109.5 18.1 %collective-permute-start.15 = (bf16[2,128,1024]{2,1,0:T(8,128)(2,1)S(1)}, bf16[2,128,1024]{2,1,0:T(8,128)(2,1)S(1)}, u32[]{:S(2)}, u32[]{:S(2)}) collective-permute-start(bf16[2,128,1024]{2,1,0:T(8,128)(2,1)S(1)} %get-tuple-element.139), channel_id=1, source_target_pairs={{0,1},{1,0},{2,6},{3,7},{4,5},{5,4},{6,2},{7,3},{8,9},{9,8},{10,14... | collective-permute-start | bytes 1572872 | tf_op jit(solution)/shard_map/ppermute | solution.py:315
  112.2 21.9 %collective-permute-start.24 = (bf16[2,128,1024]{2,1,0:T(8,128)(2,1)S(1)}, bf16[2,128,1024]{2,1,0:T(8,128)(2,1)S(1)}, u32[]{:S(2)}, u32[]{:S(2)}) collective-permute-start(bf16[2,128,1024]{2,1,0:T(8,128)(2,1)S(1)} %get-tuple-element.190), channel_id=1, source_target_pairs={{0,1},{1,0},{2,6},{3,7},{4,5},{5,4},{6,2},{7,3},{8,9},{9,8},{10,14... | collective-permute-start | bytes 1572872 | tf_op jit(solution)/shard_map/ppermute | solution.py:315
  117.5 13.8 %collective-permute-start.29 = (bf16[128,1024]{1,0:T(8,128)(2,1)S(1)}, bf16[128,1024]{1,0:T(8,128)(2,1)S(1)}, u32[]{:S(2)}, u32[]{:S(2)}) collective-permute-start(bf16[128,1024]{1,0:T(8,128)(2,1)S(1)} %fusion.7), channel_id=1, source_target_pairs={{0,8},{1,9},{2,10},{3,11},{4,12},{5,13},{6,14},{7,15},{8,24},{9,25... | collective-permute-start | bytes 786440 | tf_op jit(solution)/shard_map/ppermute | solution.py:315
  120.0 11.3 %collective-permute-start.26 = (bf16[128,1024]{1,0:T(8,128)(2,1)S(1)}, bf16[128,1024]{1,0:T(8,128)(2,1)S(1)}, u32[]{:S(2)}, u32[]{:S(2)}) collective-permute-start(bf16[128,1024]{1,0:T(8,128)(2,1)S(1)} %fusion.15), channel_id=1, source_target_pairs={{0,4},{1,5},{2,3},{3,2},{4,0},{5,1},{6,7},{7,6},{8,12},{9,13},{10,... | collective-permute-start | bytes 786440 | tf_op jit(solution)/shard_map/ppermute | solution.py:315
  131.4 7.3 %collective-permute-start.31 = (bf16[128,1024]{1,0:T(8,128)(2,1)S(1)}, bf16[128,1024]{1,0:T(8,128)(2,1)S(1)}, u32[]{:S(2)}, u32[]{:S(2)}) collective-permute-start(bf16[128,1024]{1,0:T(8,128)(2,1)S(1)} %fusion.10), channel_id=1, source_target_pairs={{0,8},{1,9},{2,10},{3,11},{4,12},{5,13},{6,14},{7,15},{8,24},{9,25... | collective-permute-start | bytes 786440 | tf_op jit(solution)/shard_map/ppermute | solution.py:315
  134.4 6.4 %collective-permute-start.30 = (bf16[128,1024]{1,0:T(8,128)(2,1)S(1)}, bf16[128,1024]{1,0:T(8,128)(2,1)S(1)}, u32[]{:S(2)}, u32[]{:S(2)}) collective-permute-start(bf16[128,1024]{1,0:T(8,128)(2,1)S(1)} %fusion.17), channel_id=1, source_target_pairs={{0,4},{1,5},{2,3},{3,2},{4,0},{5,1},{6,7},{7,6},{8,12},{9,13},{10,... | collective-permute-start | bytes 786440 | tf_op jit(solution)/shard_map/ppermute | solution.py:315
  140.9 8.2 %collective-permute-start.33 = (bf16[128,1024]{1,0:T(8,128)(2,1)S(1)}, bf16[128,1024]{1,0:T(8,128)(2,1)S(1)}, u32[]{:S(2)}, u32[]{:S(2)}) collective-permute-start(bf16[128,1024]{1,0:T(8,128)(2,1)S(1)} %fusion.5), channel_id=1, source_target_pairs={{0,8},{1,9},{2,10},{3,11},{4,12},{5,13},{6,14},{7,15},{8,24},{9,25... | collective-permute-start | bytes 786440 | tf_op jit(solution)/shard_map/ppermute | solution.py:315
  142.7 6.4 %collective-permute-start.32 = (bf16[128,1024]{1,0:T(8,128)(2,1)S(1)}, bf16[128,1024]{1,0:T(8,128)(2,1)S(1)}, u32[]{:S(2)}, u32[]{:S(2)}) collective-permute-start(bf16[128,1024]{1,0:T(8,128)(2,1)S(1)} %fusion.14), channel_id=1, source_target_pairs={{0,4},{1,5},{2,3},{3,2},{4,0},{5,1},{6,7},{7,6},{8,12},{9,13},{10,... | collective-permute-start | bytes 786440 | tf_op jit(solution)/shard_map/ppermute | solution.py:315

commit v15 on v14

--- a/solution.py
+++ b/solution.py
@@ -421,7 +421,7 @@
         if c + 1 < chunks:
             running = to_ring(running)
     keep, came = late[0]
-    pair = added(keep, tied(came, send))
+    pair = added(keep, tied(came, near))
     came = pair[1].astype(jnp.bfloat16)
     own = added(pair[0], to_first(came if running is None else tied(came, running)))
     grad_tokens = (own if running is None else added(own, to_ring(running))).astype(jnp.bfloat16)

time: 150 us -> 146 us (0.973)
  waiting for transfers between devices: 62.5 us -> 57.1 us
    ppermute x34, waiting for transfers between devices: 62.5 us -> 57.1 us  [permute(): return lax.ppermute(value, ('expert', 'etp'), pairs)]
  transfers between devices with their start and end apart: 34 -> 34, of which waited for: 15 -> 17; matrix products, arithmetic and copies ran while one was open for 7% -> 8% of each run, Pallas kernels for 21% -> 22%
where the time goes in v15:
time: 146 us; the launch traced here: 145 us
  waiting for transfers between devices  57.1 us (39%)
  starting transfers between devices  34.4 us (24%)
  Pallas kernels  34.1 us (23%)
  matrix products  10.2 us (7%)
  local copies, waits for them, and re-layouts  6.76 us (5%)
  other arithmetic  1.81 us (1%)
    ppermute x34, waiting for transfers between devices, permute(): return lax.ppermute(value, ('expert', 'etp'), pairs)  57.1 us
    ppermute x34, starting transfers between devices, permute(): return lax.ppermute(value, ('expert', 'etp'), pairs)  34.4 us
    pallas_call x4, Pallas kernels, run_experts(): pl.pallas_call(functools.partial(expert_kernel, index, kept is not None),...  19.9 us
    pallas_call x4, Pallas kernels, pick_rows(): pl.pallas_call(functools.partial(pick_kernel, top, rows), in_specs=[pl.Bl...  7.05 us
    unnamed x20, local copies, waits for them, and re-layouts  6.63 us
    pallas_call x4, Pallas kernels, place_rows(): pl.pallas_call(place_kernel, in_specs=[pl.BlockSpec(memory_space=pltpu.SM...  5.09 us
    dot_general x1, matrix products, gather_body(): lax.dot_general(acts, rows_g, CONTRACT_FIRST, preferred_element_type=jnp....  3.4 us
    dot_general x1, matrix products, gather_body(): lax.dot_general(up_term, rows_x, CONTRACT_FIRST, preferred_element_type=j...  3.38 us
  transfers between devices with their start and end apart: 34, of which 17 were waited for; matrix products, arithmetic and copies ran while one was open for 8% of the time, Pallas kernels for 22%

profile of v15, /device:TPU:0, one launch (start us, length us, event | category | flops | bytes accessed | tf_op | source)
XLA Modules:
  0.0 145.2 jit_solution(17642859185347179981)
XLA Ops:
  0.6 2.0 %pack.1.refs_0_ = bf16[272,1024]{1,0:T(8,128)(2,1)} custom-call(bf16[128,1024]{1,0:T(8,128)(2,1)} %tokens_ref.1, bf16[128,1024]{1,0:T(8,128)(2,1)} %grads_ref.1, s32[8,128]{1,0:T(8,128)} %bitcast.70, f32[8,128]{1,0:T(8,128)} %bitcast.71), custom_call_target="tpu_custom_call" | custom-call | tf_op jit(solution)/shard_map/pack/pallas_call | solution.py:128
  2.6 2.9 %collective-permute-start = (bf16[272,1024]{1,0:T(8,128)(2,1)}, bf16[272,1024]{1,0:T(8,128)(2,1)S(1)}, u32[]{:S(2)}, u32[]{:S(2)}) collective-permute-start(bf16[272,1024]{1,0:T(8,128)(2,1)} %pack.1.refs_0_), channel_id=1, source_target_pairs={{0,1},{1,0},{2,6},{3,7},{4,5},{5,4},{6,2},{7,3},{8,9},{9,8},{10,14... | collective-permute-start | bytes 1671176 | tf_op jit(solution)/shard_map/ppermute | solution.py:315
  5.6 1.5 %collective-permute-start.1 = (bf16[272,1024]{1,0:T(8,128)(2,1)}, bf16[272,1024]{1,0:T(8,128)(2,1)S(1)}, u32[]{:S(2)}, u32[]{:S(2)}) collective-permute-start(bf16[272,1024]{1,0:T(8,128)(2,1)} %pack.1.refs_0_), channel_id=1, source_target_pairs={{0,4},{1,5},{2,3},{3,2},{4,0},{5,1},{6,7},{7,6},{8,12},{9,13},{10,... | collective-permute-start | bytes 1671176 | tf_op jit(solution)/shard_map/ppermute | solution.py:315
  7.1 1.6 %collective-permute-start.2 = (bf16[272,1024]{1,0:T(8,128)(2,1)}, bf16[272,1024]{1,0:T(8,128)(2,1)}, u32[]{:S(2)}, u32[]{:S(2)}) collective-permute-start(bf16[272,1024]{1,0:T(8,128)(2,1)} %pack.1.refs_0_), channel_id=1, source_target_pairs={{0,8},{1,9},{2,10},{3,11},{4,12},{5,13},{6,14},{7,15},{8,24},{9,25... | collective-permute-start | bytes 1671176 | tf_op jit(solution)/shard_map/ppermute | solution.py:315
  8.7 10.1 %collective-permute-done.refs_2_ = bf16[272,1024]{1,0:T(8,128)(2,1)S(1)} collective-permute-done((bf16[272,1024]{1,0:T(8,128)(2,1)}, bf16[272,1024]{1,0:T(8,128)(2,1)S(1)}, u32[]{:S(2)}, u32[]{:S(2)}) %collective-permute-start) | collective-permute-done | bytes 557088 | tf_op jit(solution)/shard_map/ppermute | solution.py:315
  19.6 2.5 %collective-permute-done.2.refs_0_ = bf16[272,1024]{1,0:T(8,128)(2,1)} collective-permute-done((bf16[272,1024]{1,0:T(8,128)(2,1)}, bf16[272,1024]{1,0:T(8,128)(2,1)}, u32[]{:S(2)}, u32[]{:S(2)}) %collective-permute-start.2) | collective-permute-done | bytes 557088 | tf_op jit(solution)/shard_map/ppermute | solution.py:315
  25.1 1.1 collective-permute-start.3
  26.2 11.7 %collective-permute-done.5.refs_1_ = bf16[272,1024]{1,0:T(8,128)(2,1)} collective-permute-done((bf16[272,1024]{1,0:T(8,128)(2,1)}, bf16[272,1024]{1,0:T(8,128)(2,1)}, u32[]{:S(2)}, u32[]{:S(2)}) %collective-permute-start.5) | collective-permute-done | bytes 557088 | tf_op jit(solution)/shard_map/ppermute | solution.py:315
  39.3 1.5 %collective-permute-start.8 = (bf16[272,1024]{1,0:T(8,128)(2,1)}, bf16[272,1024]{1,0:T(8,128)(2,1)}, u32[]{:S(2)}, u32[]{:S(2)}) collective-permute-start(bf16[272,1024]{1,0:T(8,128)(2,1)} %collective-permute-done.5.refs_1_), channel_id=1, source_target_pairs={{0,1},{1,0},{2,6},{3,7},{4,5},{5,4},{6,2},{7,3},{8,9},{9,8},{10,14... | collective-permute-start | bytes 1671176 | tf_op jit(solution)/shard_map/ppermute | solution.py:315
  40.9 1.1 copy-done.3
  41.9 1.1 copy-done.5
  43.0 1.1 copy-done.7
  44.0 1.1 copy-done.9
  45.1 1.5 %pick.4 = (bf16[2,144,2048]{2,1,0:T(8,128)(2,1)S(1)}, bf16[2,144,2048]{2,1,0:T(8,128)(2,1)S(1)}, bf16[288,256]{1,0:T(8,128)(2,1)S(1)}) custom-call(s32[3]{0:T(128)S(1)} %pad_add_fusion.place_ref, bf16[272,1024]{1,0:T(8,128)(2,1)S(1)} %copy-done.3, bf16[272,1024]{1,0:T(8,128)(2,1)S(1)} %copy-done.7, bf16[272,1024]{1,0:T(8,128)(2,1)S(1)} %copy-done.5, ...), custom_call_target="tpu_custom_call" | custom-call | tf_op jit(solution)/shard_map/pick/pallas_call | solution.py:251
  46.6 1.7 %collective-permute-done.7.refs_2_ = bf16[272,1024]{1,0:T(8,128)(2,1)S(1)} collective-permute-done((bf16[272,1024]{1,0:T(8,128)(2,1)S(1)}, bf16[272,1024]{1,0:T(8,128)(2,1)S(1)}, u32[]{:S(2)}, u32[]{:S(2)}) %collective-permute-start.7) | collective-permute-done | bytes 557088 | tf_op jit(solution)/shard_map/ppermute | solution.py:315
  48.3 6.1 %collective-permute-done.8.refs_3_ = bf16[272,1024]{1,0:T(8,128)(2,1)} collective-permute-done((bf16[272,1024]{1,0:T(8,128)(2,1)}, bf16[272,1024]{1,0:T(8,128)(2,1)}, u32[]{:S(2)}, u32[]{:S(2)}) %collective-permute-start.8) | collective-permute-done | bytes 557088 | tf_op jit(solution)/shard_map/ppermute | solution.py:315
  54.9 1.6 %collective-permute-start.11 = (bf16[272,1024]{1,0:T(8,128)(2,1)}, bf16[272,1024]{1,0:T(8,128)(2,1)S(1)}, u32[]{:S(2)}, u32[]{:S(2)}) collective-permute-start(bf16[272,1024]{1,0:T(8,128)(2,1)} %collective-permute-done.5.refs_1_), channel_id=1, source_target_pairs={{0,8},{1,9},{2,10},{3,11},{4,12},{5,13},{6,14},{7,15},{8,24},{9,25... | collective-permute-start | bytes 1671176 | tf_op jit(solution)/shard_map/ppermute | solution.py:315
  57.8 2.5 %pick.5 = (bf16[2,144,2048]{2,1,0:T(8,128)(2,1)S(1)}, bf16[2,144,2048]{2,1,0:T(8,128)(2,1)S(1)}, bf16[288,256]{1,0:T(8,128)(2,1)S(1)}) custom-call(s32[3]{0:T(128)S(1)} %pad_add_fusion.place_ref, bf16[272,1024]{1,0:T(8,128)(2,1)} %collective-permute-done.2.refs_0_, bf16[272,1024]{1,0:T(8,128)(2,1)} %collective-permute-done.5.refs_1_, ...), custom_call_target="tpu_custom_call" | custom-call | tf_op jit(solution)/shard_map/pick/pallas_call | solution.py:251
  60.4 5.0 %experts.4 = (bf16[144,2048]{1,0:T(8,128)(2,1)S(1)}, bf16[144,2048]{1,0:T(8,128)(2,1)S(1)}, bf16[1152,2048]{1,0:T(8,128)(2,1)S(1)}, bf16[1152,2048]{1,0:T(8,128)...) custom-call(bf16[2,144,2048]{2,1,0:T(8,128)(2,1)S(1)} %get-tuple-element.128., ...), custom_call_target="tpu_custom_call" | custom-call | tf_op jit(solution)/shard_map/experts/pallas_call | solution.py:270
  65.5 5.1 %collective-permute-done.11.refs_1_ = bf16[272,1024]{1,0:T(8,128)(2,1)S(1)} collective-permute-done((bf16[272,1024]{1,0:T(8,128)(2,1)}, bf16[272,1024]{1,0:T(8,128)(2,1)S(1)}, u32[]{:S(2)}, u32[]{:S(2)}) %collective-permute-start.11) | collective-permute-done | bytes 557088 | tf_op jit(solution)/shard_map/ppermute | solution.py:315
  72.3 1.5 %collective-permute-done.17.theirs_ref = bf16[2,144,2048]{2,1,0:T(8,128)(2,1)S(1)} collective-permute-done((bf16[2,144,2048]{2,1,0:T(8,128)(2,1)S(1)}, bf16[2,144,2048]{2,1,0:T(8,128)(2,1)S(1)}, u32[]{:S(2)}, u32[]{:S(2)}) %collective-permute-start.17) | collective-permute-done | bytes 1179680 | tf_op jit(solution)/shard_map/ppermute | solution.py:315
  73.8 4.9 %experts.5 = (bf16[144,2048]{1,0:T(8,128)(2,1)S(1)}, bf16[144,2048]{1,0:T(8,128)(2,1)S(1)}, bf16[1152,2048]{1,0:T(8,128)(2,1)S(1)}, bf16[1152,2048]{1,0:T(8,128)...) custom-call(bf16[2,144,2048]{2,1,0:T(8,128)(2,1)S(1)} %get-tuple-ele, ...), custom_call_target="tpu_custom_call", output_to_operand_aliasing={{2}: (5, {}), {3}: (6, {}), {4}: (7, {}), {5}: (8, {}), {6}... | custom-call | tf_op jit(solution)/shard_map/experts/pallas_call | solution.py:270
  79.8 1.3 place.4
  81.1 1.5 %pick.7 = (bf16[2,144,2048]{2,1,0:T(8,128)(2,1)S(1)}, bf16[2,144,2048]{2,1,0:T(8,128)(2,1)S(1)}, bf16[288,256]{1,0:T(8,128)(2,1)S(1)}) custom-call(s32[3]{0:T(128)S(1)} %pad_add_fusion.place_ref, bf16[272,1024]{1,0:T(8,128)(2,1)S(1)} %collective-permute-done.6.refs_0_, bf16[272,1024]{1,0:T(8,128)(2,1)S(1)} %collective-permute-done.11.refs_1_, ...), custom_call_target="tpu_custom_call" | custom-call | tf_op jit(solution)/shard_map/pick/pallas_call | solution.py:251
  83.4 5.0 %collective-permute-done.16.refs_3_ = bf16[272,1024]{1,0:T(8,128)(2,1)S(1)} collective-permute-done((bf16[272,1024]{1,0:T(8,128)(2,1)S(1)}, bf16[272,1024]{1,0:T(8,128)(2,1)S(1)}, u32[]{:S(2)}, u32[]{:S(2)}) %collective-permute-start.16) | collective-permute-done | bytes 557088 | tf_op jit(solution)/shard_map/ppermute | solution.py:315
  88.4 1.5 %pick.6 = (bf16[2,144,2048]{2,1,0:T(8,128)(2,1)S(1)}, bf16[2,144,2048]{2,1,0:T(8,128)(2,1)S(1)}, bf16[288,256]{1,0:T(8,128)(2,1)S(1)}) custom-call(s32[3]{0:T(128)S(1)} %pad_add_fusion.place_ref, bf16[272,1024]{1,0:T(8,128)(2,1)S(1)} %collective-permute-done.9.refs_0_, bf16[272,1024]{1,0:T(8,128)(2,1)S(1)} %collective-permute-done.12.refs_1_, ...), custom_call_target="tpu_custom_call" | custom-call | tf_op jit(solution)/shard_map/pick/pallas_call | solution.py:251
  90.0 1.3 place.5
  91.3 0.9 collective-permute-start.27
  92.2 4.9 %experts.6 = (bf16[144,2048]{1,0:T(8,128)(2,1)S(1)}, bf16[144,2048]{1,0:T(8,128)(2,1)S(1)}, bf16[1152,2048]{1,0:T(8,128)(2,1)S(1)}, bf16[1152,2048]{1,0:T(8,128)...) custom-call(bf16[2,144,2048]{2,1,0:T(8,128)(2,1)S(1)} %get-tuple-ele, ...), custom_call_target="tpu_custom_call", output_to_operand_aliasing={{2}: (5, {}), {3}: (6, {}), {4}: (7, {}), {5}: (8, {}), {6}... | custom-call | tf_op jit(solution)/shard_map/experts/pallas_call | solution.py:270
  98.7 1.8 %collective-permute-done.27 = bf16[2,128,1024]{2,1,0:T(8,128)(2,1)S(1)} collective-permute-done((bf16[2,128,1024]{2,1,0:T(8,128)(2,1)S(1)}, bf16[2,128,1024]{2,1,0:T(8,128)(2,1)S(1)}, u32[]{:S(2)}, u32[]{:S(2)}) %collective-permute-start.27) | collective-permute-done | bytes 524320 | tf_op jit(solution)/shard_map/ppermute | solution.py:315
  100.7 5.1 %experts.7 = (bf16[144,2048]{1,0:T(8,128)(2,1)S(1)}, bf16[144,2048]{1,0:T(8,128)(2,1)S(1)}, bf16[1152,2048]{1,0:T(8,128)(2,1)S(1)}, bf16[1152,2048]{1,0:T(8,128)...) custom-call(bf16[2,144,2048]{2,1,0:T(8,128)(2,1)S(1)} %get-tuple-ele, ...), custom_call_target="tpu_custom_call", output_to_operand_aliasing={{2}: (5, {}), {3}: (6, {}), {4}: (7, {}), {5}: (8, {}), {6}... | custom-call | tf_op jit(solution)/shard_map/experts/pallas_call | solution.py:270
  106.0 1.6 %collective-permute-start.28 = (bf16[128,1024]{1,0:T(8,128)(2,1)S(1)}, bf16[128,1024]{1,0:T(8,128)(2,1)S(1)}, u32[]{:S(2)}, u32[]{:S(2)}) collective-permute-start(bf16[128,1024]{1,0:T(8,128)(2,1)S(1)} %fusion.16), channel_id=1, source_target_pairs={{0,4},{1,5},{2,3},{3,2},{4,0},{5,1},{6,7},{7,6},{8,12},{9,13},{10,... | collective-permute-start | bytes 786440 | tf_op jit(solution)/shard_map/ppermute | solution.py:315
  107.6 1.3 place.6
  109.8 1.3 place.7
  111.1 1.4 collective-permute-start.24
  112.5 1.2 collective-permute-done.28
  113.7 3.1 %collective-permute-start.29 = (bf16[128,1024]{1,0:T(8,128)(2,1)S(1)}, bf16[128,1024]{1,0:T(8,128)(2,1)S(1)}, u32[]{:S(2)}, u32[]{:S(2)}) collective-permute-start(bf16[128,1024]{1,0:T(8,128)(2,1)S(1)} %fusion.7), channel_id=1, source_target_pairs={{0,8},{1,9},{2,10},{3,11},{4,12},{5,13},{6,14},{7,15},{8,24},{9,25... | collective-permute-start | bytes 786440 | tf_op jit(solution)/shard_map/ppermute | solution.py:315
  116.8 1.3 collective-permute-done.25
  118.3 1.1 collective-permute-start.26
  119.4 3.4 %fusion.2 = bf16[1,384,2048]{2,1,0:T(8,128)(2,1)} fusion(bf16[1152,384]{1,0:T(8,128)(2,1)S(1)} %get-tuple-element.206, bf16[1152,2048]{1,0:T(8,128)(2,1)S(1)} %get-tuple-element.207), kind=kOutput, calls=%fused_computation.5 | convolution fusion | flops 1812725760 | bytes 7176192 | tf_op jit(solution)/shard_map/dot_general | solution.py:430
  122.8 3.7 %collective-permute-done.26 = bf16[128,1024]{1,0:T(8,128)(2,1)S(1)} collective-permute-done((bf16[128,1024]{1,0:T(8,128)(2,1)S(1)}, bf16[128,1024]{1,0:T(8,128)(2,1)S(1)}, u32[]{:S(2)}, u32[]{:S(2)}) %collective-permute-start.26) | collective-permute-done | bytes 262176 | tf_op jit(solution)/shard_map/ppermute | solution.py:315
  126.6 2.7 %collective-permute-start.31 = (bf16[128,1024]{1,0:T(8,128)(2,1)S(1)}, bf16[128,1024]{1,0:T(8,128)(2,1)S(1)}, u32[]{:S(2)}, u32[]{:S(2)}) collective-permute-start(bf16[128,1024]{1,0:T(8,128)(2,1)S(1)} %fusion.10), channel_id=1, source_target_pairs={{0,8},{1,9},{2,10},{3,11},{4,12},{5,13},{6,14},{7,15},{8,24},{9,25... | collective-permute-start | bytes 786440 | tf_op jit(solution)/shard_map/ppermute | solution.py:315
  130.3 3.4 %fusion = bf16[1,384,2048]{2,1,0:T(8,128)(2,1)} fusion(bf16[1152,384]{1,0:T(8,128)(2,1)S(1)} %get-tuple-element.201, bf16[1152,2048]{1,0:T(8,128)(2,1)S(1)} %get-tuple-element.202), kind=kOutput, calls=%fused_computation.3 | convolution fusion | flops 1812725760 | bytes 7176192 | tf_op jit(solution)/shard_map/dot_general | solution.py:431
  133.6 2.2 %collective-permute-done.31 = bf16[128,1024]{1,0:T(8,128)(2,1)S(1)} collective-permute-done((bf16[128,1024]{1,0:T(8,128)(2,1)S(1)}, bf16[128,1024]{1,0:T(8,128)(2,1)S(1)}, u32[]{:S(2)}, u32[]{:S(2)}) %collective-permute-start.31) | collective-permute-done | bytes 262176 | tf_op jit(solution)/shard_map/ppermute | solution.py:315
  136.0 1.2 collective-permute-start.33
  137.3 1.0 collective-permute-start.32
  138.3 3.4 %fusion.1 = bf16[1,384,2048]{2,1,0:T(8,128)(2,1)} fusion(bf16[1152,384]{1,0:T(8,128)(2,1)S(1)} %get-tuple-element.204, bf16[1152,2048]{1,0:T(8,128)(2,1)S(1)} %get-tuple-element.202), kind=kOutput, calls=%fused_computation.4 | convolution fusion | flops 1812725760 | bytes 7176192 | tf_op jit(solution)/shard_map/dot_general | solution.py:432
  141.7 2.0 %collective-permute-done.32 = bf16[128,1024]{1,0:T(8,128)(2,1)S(1)} collective-permute-done((bf16[128,1024]{1,0:T(8,128)(2,1)S(1)}, bf16[128,1024]{1,0:T(8,128)(2,1)S(1)}, u32[]{:S(2)}, u32[]{:S(2)}) %collective-permute-start.32) | collective-permute-done | bytes 262176 | tf_op jit(solution)/shard_map/ppermute | solution.py:315
  (69 shorter events, 16.8 us)
Async XLA Ops:
  0.6 59.8 %copy-start.2 = (bf16[1,384,2048]{2,1,0:T(8,128)(2,1)S(1)}, bf16[1,384,2048]{2,1,0:T(8,128)(2,1)}, u32[]{:S(2)}) copy-start(bf16[1,384,2048]{2,1,0:T(8,128)(2,1)} %param.13) | copy-start | bytes 4718596
  2.6 16.2 %collective-permute-start = (bf16[272,1024]{1,0:T(8,128)(2,1)}, bf16[272,1024]{1,0:T(8,128)(2,1)S(1)}, u32[]{:S(2)}, u32[]{:S(2)}) collective-permute-start(bf16[272,1024]{1,0:T(8,128)(2,1)} %pack.1.refs_0_), channel_id=1, source_target_pairs={{0,1},{1,0},{2,6},{3,7},{4,5},{5,4},{6,2},{7,3},{8,9},{9,8},{10,14... | collective-permute-start | bytes 1671176 | tf_op jit(solution)/shard_map/ppermute | solution.py:315
  5.6 14.0 %collective-permute-start.1 = (bf16[272,1024]{1,0:T(8,128)(2,1)}, bf16[272,1024]{1,0:T(8,128)(2,1)S(1)}, u32[]{:S(2)}, u32[]{:S(2)}) collective-permute-start(bf16[272,1024]{1,0:T(8,128)(2,1)} %pack.1.refs_0_), channel_id=1, source_target_pairs={{0,4},{1,5},{2,3},{3,2},{4,0},{5,1},{6,7},{7,6},{8,12},{9,13},{10,... | collective-permute-start | bytes 1671176 | tf_op jit(solution)/shard_map/ppermute | solution.py:315
  7.1 15.0 %collective-permute-start.2 = (bf16[272,1024]{1,0:T(8,128)(2,1)}, bf16[272,1024]{1,0:T(8,128)(2,1)}, u32[]{:S(2)}, u32[]{:S(2)}) collective-permute-start(bf16[272,1024]{1,0:T(8,128)(2,1)} %pack.1.refs_0_), channel_id=1, source_target_pairs={{0,8},{1,9},{2,10},{3,11},{4,12},{5,13},{6,14},{7,15},{8,24},{9,25... | collective-permute-start | bytes 1671176 | tf_op jit(solution)/shard_map/ppermute | solution.py:315
  18.8 0.8 copy-start.4
  22.1 15.8 %collective-permute-start.5 = (bf16[272,1024]{1,0:T(8,128)(2,1)}, bf16[272,1024]{1,0:T(8,128)(2,1)}, u32[]{:S(2)}, u32[]{:S(2)}) collective-permute-start(bf16[272,1024]{1,0:T(8,128)(2,1)} %collective-permute-done.2.refs_0_), channel_id=1, source_target_pairs={{0,4},{1,5},{2,3},{3,2},{4,0},{5,1},{6,7},{7,6},{8,12},{9,13},{10,... | collective-permute-start | bytes 1671176 | tf_op jit(solution)/shard_map/ppermute | solution.py:315
  22.7 15.3 %collective-permute-start.6 = (bf16[272,1024]{1,0:T(8,128)(2,1)}, bf16[272,1024]{1,0:T(8,128)(2,1)S(1)}, u32[]{:S(2)}, u32[]{:S(2)}) collective-permute-start(bf16[272,1024]{1,0:T(8,128)(2,1)} %collective-permute-done.2.refs_0_), channel_id=1, source_target_pairs={{0,8},{1,9},{2,10},{3,11},{4,12},{5,13},{6,14},{7,15},{8,24},{9,25... | collective-permute-start | bytes 1671176 | tf_op jit(solution)/shard_map/ppermute | solution.py:315
  23.4 14.6 %collective-permute-start.4 = (bf16[272,1024]{1,0:T(8,128)(2,1)S(1)}, bf16[272,1024]{1,0:T(8,128)(2,1)S(1)}, u32[]{:S(2)}, u32[]{:S(2)}) collective-permute-start(bf16[272,1024]{1,0:T(8,128)(2,1)S(1)} %collective-permute-done.1.refs_1_), channel_id=1, source_target_pairs={{0,1},{1,0},{2,6},{3,7},{4,5},{5,4},{6,2},{7,3},{8,9},{9,8},{10,14... | collective-permute-start | bytes 1671176 | tf_op jit(solution)/shard_map/ppermute | solution.py:315
  24.3 0.8 copy-start.6
  25.1 21.5 %collective-permute-start.3 = (bf16[272,1024]{1,0:T(8,128)(2,1)}, bf16[272,1024]{1,0:T(8,128)(2,1)}, u32[]{:S(2)}, u32[]{:S(2)}) collective-permute-start(bf16[272,1024]{1,0:T(8,128)(2,1)} %collective-permute-done.2.refs_0_), channel_id=1, source_target_pairs={{0,1},{1,0},{2,6},{3,7},{4,5},{5,4},{6,2},{7,3},{8,9},{9,8},{10,14... | collective-permute-start | bytes 1671176 | tf_op jit(solution)/shard_map/ppermute | solution.py:315
  38.0 0.8 copy-start.8
  38.8 9.5 %collective-permute-start.7 = (bf16[272,1024]{1,0:T(8,128)(2,1)S(1)}, bf16[272,1024]{1,0:T(8,128)(2,1)S(1)}, u32[]{:S(2)}, u32[]{:S(2)}) collective-permute-start(bf16[272,1024]{1,0:T(8,128)(2,1)S(1)} %collective-permute-done.6.refs_0_), channel_id=1, source_target_pairs={{0,1},{1,0},{2,6},{3,7},{4,5},{5,4},{6,2},{7,3},{8,9},{9,8},{10,14... | collective-permute-start | bytes 1671176 | tf_op jit(solution)/shard_map/ppermute | solution.py:315
  39.3 15.1 %collective-permute-start.8 = (bf16[272,1024]{1,0:T(8,128)(2,1)}, bf16[272,1024]{1,0:T(8,128)(2,1)}, u32[]{:S(2)}, u32[]{:S(2)}) collective-permute-start(bf16[272,1024]{1,0:T(8,128)(2,1)} %collective-permute-done.5.refs_1_), channel_id=1, source_target_pairs={{0,1},{1,0},{2,6},{3,7},{4,5},{5,4},{6,2},{7,3},{8,9},{9,8},{10,14... | collective-permute-start | bytes 1671176 | tf_op jit(solution)/shard_map/ppermute | solution.py:315
  40.8 13.6 %collective-permute-start.9 = (bf16[272,1024]{1,0:T(8,128)(2,1)S(1)}, bf16[272,1024]{1,0:T(8,128)(2,1)S(1)}, u32[]{:S(2)}, u32[]{:S(2)}) collective-permute-start(bf16[272,1024]{1,0:T(8,128)(2,1)S(1)} %collective-permute-done.6.refs_0_), channel_id=1, source_target_pairs={{0,8},{1,9},{2,10},{3,11},{4,12},{5,13},{6,14},{7,15},{8,24},{9,25... | collective-permute-start | bytes 1671176 | tf_op jit(solution)/shard_map/ppermute | solution.py:315
  40.9 1.1 copy-start.3
  41.9 1.1 copy-start.5
  43.0 1.1 copy-start.7
  44.0 1.1 copy-start.9
  45.1 15.3 %copy-start.1 = (bf16[1,384,2048]{2,1,0:T(8,128)(2,1)S(1)}, bf16[1,384,2048]{2,1,0:T(8,128)(2,1)}, u32[]{:S(2)}) copy-start(bf16[1,384,2048]{2,1,0:T(8,128)(2,1)} %param.12) | copy-start | bytes 4718596
  46.6 13.8 %copy-start = (bf16[1,384,2048]{2,1,0:T(8,128)(2,1)S(1)}, bf16[1,384,2048]{2,1,0:T(8,128)(2,1)}, u32[]{:S(2)}) copy-start(bf16[1,384,2048]{2,1,0:T(8,128)(2,1)} %param.11) | copy-start | bytes 4718596
  54.4 6.0 %collective-permute-start.13 = (bf16[2,144,2048]{2,1,0:T(8,128)(2,1)S(1)}, bf16[2,144,2048]{2,1,0:T(8,128)(2,1)S(1)}, u32[]{:S(2)}, u32[]{:S(2)}) collective-permute-start(bf16[2,144,2048]{2,1,0:T(8,128)(2,1)S(1)} %get-tuple-element.129), channel_id=1, source_target_pairs={{0,2},{1,3},{2,0},{3,1},{4,6},{5,7},{6,4},{7,5},{8,10},{9,11},{10,... | collective-permute-start | bytes 3538952 | tf_op jit(solution)/shard_map/ppermute | solution.py:315
  54.9 15.6 %collective-permute-start.11 = (bf16[272,1024]{1,0:T(8,128)(2,1)}, bf16[272,1024]{1,0:T(8,128)(2,1)S(1)}, u32[]{:S(2)}, u32[]{:S(2)}) collective-permute-start(bf16[272,1024]{1,0:T(8,128)(2,1)} %collective-permute-done.5.refs_1_), channel_id=1, source_target_pairs={{0,8},{1,9},{2,10},{3,11},{4,12},{5,13},{6,14},{7,15},{8,24},{9,25... | collective-permute-start | bytes 1671176 | tf_op jit(solution)/shard_map/ppermute | solution.py:315
  56.5 14.5 %collective-permute-start.10 = (bf16[272,1024]{1,0:T(8,128)(2,1)S(1)}, bf16[272,1024]{1,0:T(8,128)(2,1)S(1)}, u32[]{:S(2)}, u32[]{:S(2)}) collective-permute-start(bf16[272,1024]{1,0:T(8,128)(2,1)S(1)} %collective-permute-done.9.refs_0_), channel_id=1, source_target_pairs={{0,1},{1,0},{2,6},{3,7},{4,5},{5,4},{6,2},{7,3},{8,9},{9,8},{10,14... | collective-permute-start | bytes 1671176 | tf_op jit(solution)/shard_map/ppermute | solution.py:315
  57.1 13.8 %collective-permute-start.12 = (bf16[272,1024]{1,0:T(8,128)(2,1)S(1)}, bf16[272,1024]{1,0:T(8,128)(2,1)S(1)}, u32[]{:S(2)}, u32[]{:S(2)}) collective-permute-start(bf16[272,1024]{1,0:T(8,128)(2,1)S(1)} %collective-permute-done.9.refs_0_), channel_id=1, source_target_pairs={{0,4},{1,5},{2,3},{3,2},{4,0},{5,1},{6,7},{7,6},{8,12},{9,13},{10,... | collective-permute-start | bytes 1671176 | tf_op jit(solution)/shard_map/ppermute | solution.py:315
  70.9 2.8 %collective-permute-start.17 = (bf16[2,144,2048]{2,1,0:T(8,128)(2,1)S(1)}, bf16[2,144,2048]{2,1,0:T(8,128)(2,1)S(1)}, u32[]{:S(2)}, u32[]{:S(2)}) collective-permute-start(bf16[2,144,2048]{2,1,0:T(8,128)(2,1)S(1)} %get-tuple-element.143), channel_id=1, source_target_pairs={{0,2},{1,3},{2,0},{3,1},{4,6},{5,7},{6,4},{7,5},{8,10},{9,11},{10,... | collective-permute-start | bytes 3538952 | tf_op jit(solution)/shard_map/ppermute | solution.py:315
  70.9 8.8 %collective-permute-start.14 = (bf16[144,2048]{1,0:T(8,128)(2,1)S(1)}, bf16[144,2048]{1,0:T(8,128)(2,1)S(1)}, u32[]{:S(2)}, u32[]{:S(2)}) collective-permute-start(bf16[144,2048]{1,0:T(8,128)(2,1)S(1)} %get-tuple-element.137), channel_id=1, source_target_pairs={{0,2},{1,3},{2,0},{3,1},{4,6},{5,7},{6,4},{7,5},{8,10},{9,11},{10,... | collective-permute-start | bytes 1769480 | tf_op jit(solution)/shard_map/ppermute | solution.py:315
  71.5 9.6 %collective-permute-start.20 = (bf16[272,1024]{1,0:T(8,128)(2,1)S(1)}, bf16[272,1024]{1,0:T(8,128)(2,1)S(1)}, u32[]{:S(2)}, u32[]{:S(2)}) collective-permute-start(bf16[272,1024]{1,0:T(8,128)(2,1)S(1)} %collective-permute-done.11.refs_1_), channel_id=1, source_target_pairs={{0,1},{1,0},{2,6},{3,7},{4,5},{5,4},{6,2},{7,3},{8,9},{9,8},{10,14... | collective-permute-start | bytes 1671176 | tf_op jit(solution)/shard_map/ppermute | solution.py:315
  78.7 9.7 %collective-permute-start.18 = (bf16[144,2048]{1,0:T(8,128)(2,1)S(1)}, bf16[144,2048]{1,0:T(8,128)(2,1)S(1)}, u32[]{:S(2)}, u32[]{:S(2)}) collective-permute-start(bf16[144,2048]{1,0:T(8,128)(2,1)S(1)} %get-tuple-element.152), channel_id=1, source_target_pairs={{0,2},{1,3},{2,0},{3,1},{4,6},{5,7},{6,4},{7,5},{8,10},{9,11},{10,... | collective-permute-start | bytes 1769480 | tf_op jit(solution)/shard_map/ppermute | solution.py:315
  78.9 9.5 %collective-permute-start.16 = (bf16[272,1024]{1,0:T(8,128)(2,1)S(1)}, bf16[272,1024]{1,0:T(8,128)(2,1)S(1)}, u32[]{:S(2)}, u32[]{:S(2)}) collective-permute-start(bf16[272,1024]{1,0:T(8,128)(2,1)S(1)} %collective-permute-done.12.refs_1_), channel_id=1, source_target_pairs={{0,1},{1,0},{2,6},{3,7},{4,5},{5,4},{6,2},{7,3},{8,9},{9,8},{10,14... | collective-permute-start | bytes 1671176 | tf_op jit(solution)/shard_map/ppermute | solution.py:315
  82.6 9.7 %collective-permute-start.21 = (bf16[2,144,2048]{2,1,0:T(8,128)(2,1)S(1)}, bf16[2,144,2048]{2,1,0:T(8,128)(2,1)S(1)}, u32[]{:S(2)}, u32[]{:S(2)}) collective-permute-start(bf16[2,144,2048]{2,1,0:T(8,128)(2,1)S(1)} %get-tuple-element.170), channel_id=1, source_target_pairs={{0,2},{1,3},{2,0},{3,1},{4,6},{5,7},{6,4},{7,5},{8,10},{9,11},{10,... | collective-permute-start | bytes 3538952 | tf_op jit(solution)/shard_map/ppermute | solution.py:315
  89.9 10.8 %collective-permute-start.19 = (bf16[2,144,2048]{2,1,0:T(8,128)(2,1)S(1)}, bf16[2,144,2048]{2,1,0:T(8,128)(2,1)S(1)}, u32[]{:S(2)}, u32[]{:S(2)}) collective-permute-start(bf16[2,144,2048]{2,1,0:T(8,128)(2,1)S(1)} %get-tuple-element.158), channel_id=1, source_target_pairs={{0,2},{1,3},{2,0},{3,1},{4,6},{5,7},{6,4},{7,5},{8,10},{9,11},{10,... | collective-permute-start | bytes 3538952 | tf_op jit(solution)/shard_map/ppermute | solution.py:315
  91.3 9.2 %collective-permute-start.27 = (bf16[2,128,1024]{2,1,0:T(8,128)(2,1)S(1)}, bf16[2,128,1024]{2,1,0:T(8,128)(2,1)S(1)}, u32[]{:S(2)}, u32[]{:S(2)}) collective-permute-start(bf16[2,128,1024]{2,1,0:T(8,128)(2,1)S(1)} %get-tuple-element.168), channel_id=1, source_target_pairs={{0,1},{1,0},{2,6},{3,7},{4,5},{5,4},{6,2},{7,3},{8,9},{9,8},{10,14... | collective-permute-start | bytes 1572872 | tf_op jit(solution)/shard_map/ppermute | solution.py:315
  97.1 10.4 %collective-permute-start.22 = (bf16[144,2048]{1,0:T(8,128)(2,1)S(1)}, bf16[144,2048]{1,0:T(8,128)(2,1)S(1)}, u32[]{:S(2)}, u32[]{:S(2)}) collective-permute-start(bf16[144,2048]{1,0:T(8,128)(2,1)S(1)} %get-tuple-element.187), channel_id=1, source_target_pairs={{0,2},{1,3},{2,0},{3,1},{4,6},{5,7},{6,4},{7,5},{8,10},{9,11},{10,... | collective-permute-start | bytes 1769480 | tf_op jit(solution)/shard_map/ppermute | solution.py:315
  98.1 11.5 %collective-permute-start.15 = (bf16[2,128,1024]{2,1,0:T(8,128)(2,1)S(1)}, bf16[2,128,1024]{2,1,0:T(8,128)(2,1)S(1)}, u32[]{:S(2)}, u32[]{:S(2)}) collective-permute-start(bf16[2,128,1024]{2,1,0:T(8,128)(2,1)S(1)} %get-tuple-element.139), channel_id=1, source_target_pairs={{0,1},{1,0},{2,6},{3,7},{4,5},{5,4},{6,2},{7,3},{8,9},{9,8},{10,14... | collective-permute-start | bytes 1572872 | tf_op jit(solution)/shard_map/ppermute | solution.py:315
  105.9 4.0 %collective-permute-start.23 = (bf16[144,2048]{1,0:T(8,128)(2,1)S(1)}, bf16[144,2048]{1,0:T(8,128)(2,1)S(1)}, u32[]{:S(2)}, u32[]{:S(2)}) collective-permute-start(bf16[144,2048]{1,0:T(8,128)(2,1)S(1)} %get-tuple-element.190), channel_id=1, source_target_pairs={{0,2},{1,3},{2,0},{3,1},{4,6},{5,7},{6,4},{7,5},{8,10},{9,11},{10,... | collective-permute-start | bytes 1769480 | tf_op jit(solution)/shard_map/ppermute | solution.py:315
  106.0 7.7 %collective-permute-start.28 = (bf16[128,1024]{1,0:T(8,128)(2,1)S(1)}, bf16[128,1024]{1,0:T(8,128)(2,1)S(1)}, u32[]{:S(2)}, u32[]{:S(2)}) collective-permute-start(bf16[128,1024]{1,0:T(8,128)(2,1)S(1)} %fusion.16), channel_id=1, source_target_pairs={{0,4},{1,5},{2,3},{3,2},{4,0},{5,1},{6,7},{7,6},{8,12},{9,13},{10,... | collective-permute-start | bytes 786440 | tf_op jit(solution)/shard_map/ppermute | solution.py:315
  108.8 9.2 %collective-permute-start.25 = (bf16[2,128,1024]{2,1,0:T(8,128)(2,1)S(1)}, bf16[2,128,1024]{2,1,0:T(8,128)(2,1)S(1)}, u32[]{:S(2)}, u32[]{:S(2)}) collective-permute-start(bf16[2,128,1024]{2,1,0:T(8,128)(2,1)S(1)} %get-tuple-element.188), channel_id=1, source_target_pairs={{0,1},{1,0},{2,6},{3,7},{4,5},{5,4},{6,2},{7,3},{8,9},{9,8},{10,14... | collective-permute-start | bytes 1572872 | tf_op jit(solution)/shard_map/ppermute | solution.py:315
  111.1 18.1 %collective-permute-start.24 = (bf16[2,128,1024]{2,1,0:T(8,128)(2,1)S(1)}, bf16[2,128,1024]{2,1,0:T(8,128)(2,1)S(1)}, u32[]{:S(2)}, u32[]{:S(2)}) collective-permute-start(bf16[2,128,1024]{2,1,0:T(8,128)(2,1)S(1)} %get-tuple-element.192), channel_id=1, source_target_pairs={{0,1},{1,0},{2,6},{3,7},{4,5},{5,4},{6,2},{7,3},{8,9},{9,8},{10,14... | collective-permute-start | bytes 1572872 | tf_op jit(solution)/shard_map/ppermute | solution.py:315
  113.7 9.0 %collective-permute-start.29 = (bf16[128,1024]{1,0:T(8,128)(2,1)S(1)}, bf16[128,1024]{1,0:T(8,128)(2,1)S(1)}, u32[]{:S(2)}, u32[]{:S(2)}) collective-permute-start(bf16[128,1024]{1,0:T(8,128)(2,1)S(1)} %fusion.7), channel_id=1, source_target_pairs={{0,8},{1,9},{2,10},{3,11},{4,12},{5,13},{6,14},{7,15},{8,24},{9,25... | collective-permute-start | bytes 786440 | tf_op jit(solution)/shard_map/ppermute | solution.py:315
  118.3 8.2 %collective-permute-start.26 = (bf16[128,1024]{1,0:T(8,128)(2,1)S(1)}, bf16[128,1024]{1,0:T(8,128)(2,1)S(1)}, u32[]{:S(2)}, u32[]{:S(2)}) collective-permute-start(bf16[128,1024]{1,0:T(8,128)(2,1)S(1)} %fusion.15), channel_id=1, source_target_pairs={{0,4},{1,5},{2,3},{3,2},{4,0},{5,1},{6,7},{7,6},{8,12},{9,13},{10,... | collective-permute-start | bytes 786440 | tf_op jit(solution)/shard_map/ppermute | solution.py:315
  126.6 9.3 %collective-permute-start.31 = (bf16[128,1024]{1,0:T(8,128)(2,1)S(1)}, bf16[128,1024]{1,0:T(8,128)(2,1)S(1)}, u32[]{:S(2)}, u32[]{:S(2)}) collective-permute-start(bf16[128,1024]{1,0:T(8,128)(2,1)S(1)} %fusion.10), channel_id=1, source_target_pairs={{0,8},{1,9},{2,10},{3,11},{4,12},{5,13},{6,14},{7,15},{8,24},{9,25... | collective-permute-start | bytes 786440 | tf_op jit(solution)/shard_map/ppermute | solution.py:315
  129.5 6.4 %collective-permute-start.30 = (bf16[128,1024]{1,0:T(8,128)(2,1)S(1)}, bf16[128,1024]{1,0:T(8,128)(2,1)S(1)}, u32[]{:S(2)}, u32[]{:S(2)}) collective-permute-start(bf16[128,1024]{1,0:T(8,128)(2,1)S(1)} %fusion.17), channel_id=1, source_target_pairs={{0,4},{1,5},{2,3},{3,2},{4,0},{5,1},{6,7},{7,6},{8,12},{9,13},{10,... | collective-permute-start | bytes 786440 | tf_op jit(solution)/shard_map/ppermute | solution.py:315
  136.0 8.4 %collective-permute-start.33 = (bf16[128,1024]{1,0:T(8,128)(2,1)S(1)}, bf16[128,1024]{1,0:T(8,128)(2,1)S(1)}, u32[]{:S(2)}, u32[]{:S(2)}) collective-permute-start(bf16[128,1024]{1,0:T(8,128)(2,1)S(1)} %fusion.5), channel_id=1, source_target_pairs={{0,8},{1,9},{2,10},{3,11},{4,12},{5,13},{6,14},{7,15},{8,24},{9,25... | collective-permute-start | bytes 786440 | tf_op jit(solution)/shard_map/ppermute | solution.py:315
  137.3 6.4 %collective-permute-start.32 = (bf16[128,1024]{1,0:T(8,128)(2,1)S(1)}, bf16[128,1024]{1,0:T(8,128)(2,1)S(1)}, u32[]{:S(2)}, u32[]{:S(2)}) collective-permute-start(bf16[128,1024]{1,0:T(8,128)(2,1)S(1)} %fusion.14), channel_id=1, source_target_pairs={{0,4},{1,5},{2,3},{3,2},{4,0},{5,1},{6,7},{7,6},{8,12},{9,13},{10,... | collective-permute-start | bytes 786440 | tf_op jit(solution)/shard_map/ppermute | solution.py:315

commit v16 on v15

--- a/solution.py
+++ b/solution.py
@@ -386,34 +386,44 @@
         picks, near, far = parts
         crossed = to_core(far)
     while done < chunks:
-        shares = tied([have[kind, done] for kind in "sfab"], mark)
+        shares = tied([have[kind, done] for kind in "sfab"], [mark, list(came.values())])
         rows_of = pick_rows(place, shares, top, rows, pair_slots)
         last.append(rows_of)
-        mark = [crossed]
+        mark = []
         done += 1
     if crossed is not None:
         keep, send = place_rows(place, picks, near, crossed, rows, width)
         late.append((keep, to_second(send)))
     done -= len(last)
+    early = None
     for i, (mine, theirs, picks) in enumerate(last):
         mine = tied(mine, send) if i == 0 else mine
         near, far, *kept = run_experts(done, chunks, mine, to_core(theirs), weights, kept)
         last[i] = picks, near, far
         done += 1
+        if i == 0 and len(late) > 1:
+            keep, came = late[1]
+            pair = added(keep, tied(came, near))
+            early = pair[0], to_first(pair[1].astype(jnp.bfloat16))
     nears = [near for _, near, _ in last]
     near, send = nears[-1], nears[0]
-    for picks, first, far in last:
+    if early is not None:
+        came, near = lax.optimization_barrier((early[1], near))
+        early = added(early[0], came)
+        nears[-1] = near
+    for (picks, _, far), first in zip(last, nears):
         keep, send = placed(picks, tied(first, send), far)
         late.append((keep, to_second(send)))
     ties = [nears[0], send]
     marks = [send] * (chunks + 2)
     running = None
     for c in range(1, chunks):
-        keep, came = late[c]
-        came = tied(came, ties[c - 1] if c + 1 < chunks else previous)
-        pair = added(keep, came)
-        came = to_first(pair[1].astype(jnp.bfloat16))
-        total = added(pair[0], tied(came, send) if c == 1 else came)
+        if c == 1 and early is not None:
+            total = early
+        else:
+            keep, came = late[c]
+            pair = added(keep, tied(came, ties[c - 1] if c + 1 < chunks else previous))
+            total = added(pair[0], to_first(pair[1].astype(jnp.bfloat16)))
         running = (total if running is None else added(total, running)).astype(jnp.bfloat16)
         previous = running
         if c > 1:

time: 146 us -> 152 us (1.041)
  waiting for transfers between devices: 57.1 us -> 67.1 us
  starting transfers between devices: 34.4 us -> 30.9 us
    ppermute x34, waiting for transfers between devices: 57.1 us -> 67.1 us  [permute(): return lax.ppermute(value, ('expert', 'etp'), pairs)]
    ppermute x34, starting transfers between devices: 34.4 us -> 30.9 us  [permute(): return lax.ppermute(value, ('expert', 'etp'), pairs)]
  transfers between devices with their start and end apart: 34 -> 34, of which waited for: 17 -> 19; matrix products, arithmetic and copies ran while one was open for 8% -> 7% of each run, Pallas kernels for 22% -> 20%
where the time goes in v16:
time: 152 us
  waiting for transfers between devices  67.1 us (44%)
  Pallas kernels  33.9 us (22%)
  starting transfers between devices  30.9 us (20%)
  matrix products  10.2 us (7%)
  local copies, waits for them, and re-layouts  6.76 us (4%)
  other arithmetic  1.76 us (1%)
    ppermute x34, waiting for transfers between devices, permute(): return lax.ppermute(value, ('expert', 'etp'), pairs)  67.1 us
    ppermute x34, starting transfers between devices, permute(): return lax.ppermute(value, ('expert', 'etp'), pairs)  30.9 us
    pallas_call x4, Pallas kernels, run_experts(): pl.pallas_call(functools.partial(expert_kernel, index, kept is not None),...  19.7 us
    pallas_call x4, Pallas kernels, pick_rows(): pl.pallas_call(functools.partial(pick_kernel, top, rows), in_specs=[pl.Bl...  7.04 us
    unnamed x20, local copies, waits for them, and re-layouts  6.63 us
    pallas_call x4, Pallas kernels, place_rows(): pl.pallas_call(place_kernel, in_specs=[pl.BlockSpec(memory_space=pltpu.SM...  5.08 us
    dot_general x1, matrix products, gather_body(): lax.dot_general(acts, rows_g, CONTRACT_FIRST, preferred_element_type=jnp....  3.4 us
    dot_general x1, matrix products, gather_body(): lax.dot_general(gate_term, rows_x, CONTRACT_FIRST, preferred_element_type...  3.38 us
  transfers between devices with their start and end apart: 34, of which 19 were waited for; matrix products, arithmetic and copies ran while one was open for 7% of the time, Pallas kernels for 20%

profile of v16, /device:TPU:0, one launch (start us, length us, event | category | flops | bytes accessed | tf_op | source)
XLA Modules:
  0.0 151.5 jit_solution(6998464986309790157)
XLA Ops:
  0.6 2.0 %pack.1.refs_0_ = bf16[272,1024]{1,0:T(8,128)(2,1)} custom-call(bf16[128,1024]{1,0:T(8,128)(2,1)} %tokens_ref.1, bf16[128,1024]{1,0:T(8,128)(2,1)} %grads_ref.1, s32[8,128]{1,0:T(8,128)} %bitcast.70, f32[8,128]{1,0:T(8,128)} %bitcast.71), custom_call_target="tpu_custom_call" | custom-call | tf_op jit(solution)/shard_map/pack/pallas_call | solution.py:128
  2.6 2.9 %collective-permute-start = (bf16[272,1024]{1,0:T(8,128)(2,1)}, bf16[272,1024]{1,0:T(8,128)(2,1)S(1)}, u32[]{:S(2)}, u32[]{:S(2)}) collective-permute-start(bf16[272,1024]{1,0:T(8,128)(2,1)} %pack.1.refs_0_), channel_id=1, source_target_pairs={{0,1},{1,0},{2,6},{3,7},{4,5},{5,4},{6,2},{7,3},{8,9},{9,8},{10,14... | collective-permute-start | bytes 1671176 | tf_op jit(solution)/shard_map/ppermute | solution.py:315
  5.6 1.5 %collective-permute-start.1 = (bf16[272,1024]{1,0:T(8,128)(2,1)}, bf16[272,1024]{1,0:T(8,128)(2,1)S(1)}, u32[]{:S(2)}, u32[]{:S(2)}) collective-permute-start(bf16[272,1024]{1,0:T(8,128)(2,1)} %pack.1.refs_0_), channel_id=1, source_target_pairs={{0,4},{1,5},{2,3},{3,2},{4,0},{5,1},{6,7},{7,6},{8,12},{9,13},{10,... | collective-permute-start | bytes 1671176 | tf_op jit(solution)/shard_map/ppermute | solution.py:315
  7.1 1.6 %collective-permute-start.2 = (bf16[272,1024]{1,0:T(8,128)(2,1)}, bf16[272,1024]{1,0:T(8,128)(2,1)}, u32[]{:S(2)}, u32[]{:S(2)}) collective-permute-start(bf16[272,1024]{1,0:T(8,128)(2,1)} %pack.1.refs_0_), channel_id=1, source_target_pairs={{0,8},{1,9},{2,10},{3,11},{4,12},{5,13},{6,14},{7,15},{8,24},{9,25... | collective-permute-start | bytes 1671176 | tf_op jit(solution)/shard_map/ppermute | solution.py:315
  8.7 10.1 %collective-permute-done.refs_2_ = bf16[272,1024]{1,0:T(8,128)(2,1)S(1)} collective-permute-done((bf16[272,1024]{1,0:T(8,128)(2,1)}, bf16[272,1024]{1,0:T(8,128)(2,1)S(1)}, u32[]{:S(2)}, u32[]{:S(2)}) %collective-permute-start) | collective-permute-done | bytes 557088 | tf_op jit(solution)/shard_map/ppermute | solution.py:315
  19.6 2.5 %collective-permute-done.2.refs_0_ = bf16[272,1024]{1,0:T(8,128)(2,1)} collective-permute-done((bf16[272,1024]{1,0:T(8,128)(2,1)}, bf16[272,1024]{1,0:T(8,128)(2,1)}, u32[]{:S(2)}, u32[]{:S(2)}) %collective-permute-start.2) | collective-permute-done | bytes 557088 | tf_op jit(solution)/shard_map/ppermute | solution.py:315
  24.0 1.1 collective-permute-start.6
  25.1 1.1 collective-permute-start.3
  26.2 10.0 %collective-permute-done.4.refs_3_ = bf16[272,1024]{1,0:T(8,128)(2,1)S(1)} collective-permute-done((bf16[272,1024]{1,0:T(8,128)(2,1)S(1)}, bf16[272,1024]{1,0:T(8,128)(2,1)S(1)}, u32[]{:S(2)}, u32[]{:S(2)}) %collective-permute-start.4) | collective-permute-done | bytes 557088 | tf_op jit(solution)/shard_map/ppermute | solution.py:315
  37.1 2.3 %collective-permute-done.5.refs_1_ = bf16[272,1024]{1,0:T(8,128)(2,1)} collective-permute-done((bf16[272,1024]{1,0:T(8,128)(2,1)}, bf16[272,1024]{1,0:T(8,128)(2,1)}, u32[]{:S(2)}, u32[]{:S(2)}) %collective-permute-start.5) | collective-permute-done | bytes 557088 | tf_op jit(solution)/shard_map/ppermute | solution.py:315
  39.4 1.5 collective-permute-start.7
  42.4 1.1 copy-done.3
  43.4 1.1 copy-done.5
  44.5 1.1 copy-done.7
  45.5 1.1 copy-done.9
  46.6 1.5 pick.4
  48.9 6.1 %collective-permute-done.8.refs_3_ = bf16[272,1024]{1,0:T(8,128)(2,1)} collective-permute-done((bf16[272,1024]{1,0:T(8,128)(2,1)}, bf16[272,1024]{1,0:T(8,128)(2,1)}, u32[]{:S(2)}, u32[]{:S(2)}) %collective-permute-start.8) | collective-permute-done | bytes 557088 | tf_op jit(solution)/shard_map/ppermute | solution.py:315
  55.0 0.9 collective-permute-start.11
  55.9 1.4 collective-permute-start.10
  57.8 2.5 %pick.5 = (bf16[2,144,2048]{2,1,0:T(8,128)(2,1)S(1)}, bf16[2,144,2048]{2,1,0:T(8,128)(2,1)S(1)}, bf16[288,256]{1,0:T(8,128)(2,1)S(1)}) custom-call(s32[3]{0:T(128)S(1)} %pad_add_fusion.place_ref, bf16[272,1024]{1,0:T(8,128)(2,1)} %collective-permute-done.2.refs_0_, bf16[272,1024]{1,0:T(8,128)(2,1)} %collective-permute-done.5.refs_1_, ...), custom_call_target="tpu_custom_call" | custom-call | tf_op jit(solution)/shard_map/pick/pallas_call | solution.py:251
  60.4 4.9 %experts.4 = (bf16[144,2048]{1,0:T(8,128)(2,1)S(1)}, bf16[144,2048]{1,0:T(8,128)(2,1)S(1)}, bf16[1152,2048]{1,0:T(8,128)(2,1)S(1)}, bf16[1152,2048]{1,0:T(8,128)...) custom-call(bf16[2,144,2048]{2,1,0:T(8,128)(2,1)S(1)} %get-tuple-element.129., ...), custom_call_target="tpu_custom_call" | custom-call | tf_op jit(solution)/shard_map/experts/pallas_call | solution.py:270
  65.2 5.9 %collective-permute-done.11.refs_1_ = bf16[272,1024]{1,0:T(8,128)(2,1)S(1)} collective-permute-done((bf16[272,1024]{1,0:T(8,128)(2,1)}, bf16[272,1024]{1,0:T(8,128)(2,1)S(1)}, u32[]{:S(2)}, u32[]{:S(2)}) %collective-permute-start.11) | collective-permute-done | bytes 557088 | tf_op jit(solution)/shard_map/ppermute | solution.py:315
  71.9 1.3 collective-permute-start.19
  73.9 1.2 collective-permute-done.14.far_ref
  75.1 1.3 place.4
  76.3 4.9 %experts.5 = (bf16[144,2048]{1,0:T(8,128)(2,1)S(1)}, bf16[144,2048]{1,0:T(8,128)(2,1)S(1)}, bf16[1152,2048]{1,0:T(8,128)(2,1)S(1)}, bf16[1152,2048]{1,0:T(8,128)...) custom-call(bf16[2,144,2048]{2,1,0:T(8,128)(2,1)S(1)} %get-tuple-ele, ...), custom_call_target="tpu_custom_call", output_to_operand_aliasing={{2}: (5, {}), {3}: (6, {}), {4}: (7, {}), {5}: (8, {}), {6}... | custom-call | tf_op jit(solution)/shard_map/experts/pallas_call | solution.py:270
  81.4 6.0 %collective-permute-done.20.refs_3_ = bf16[272,1024]{1,0:T(8,128)(2,1)S(1)} collective-permute-done((bf16[272,1024]{1,0:T(8,128)(2,1)S(1)}, bf16[272,1024]{1,0:T(8,128)(2,1)S(1)}, u32[]{:S(2)}, u32[]{:S(2)}) %collective-permute-start.20) | collective-permute-done | bytes 557088 | tf_op jit(solution)/shard_map/ppermute | solution.py:315
  87.4 1.5 pick.6
  89.5 3.2 %collective-permute-done.17.far_ref = bf16[144,2048]{1,0:T(8,128)(2,1)S(1)} collective-permute-done((bf16[144,2048]{1,0:T(8,128)(2,1)S(1)}, bf16[144,2048]{1,0:T(8,128)(2,1)S(1)}, u32[]{:S(2)}, u32[]{:S(2)}) %collective-permute-start.17) | collective-permute-done | bytes 589856 | tf_op jit(solution)/shard_map/ppermute | solution.py:315
  92.6 1.3 place.5
  93.9 1.3 collective-permute-start.18
  95.3 1.5 pick.7
  97.7 5.1 %experts.6 = (bf16[144,2048]{1,0:T(8,128)(2,1)S(1)}, bf16[144,2048]{1,0:T(8,128)(2,1)S(1)}, bf16[1152,2048]{1,0:T(8,128)(2,1)S(1)}, bf16[1152,2048]{1,0:T(8,128)...) custom-call(bf16[2,144,2048]{2,1,0:T(8,128)(2,1)S(1)} %get-tuple-ele, ...), custom_call_target="tpu_custom_call", output_to_operand_aliasing={{2}: (5, {}), {3}: (6, {}), {4}: (7, {}), {5}: (8, {}), {6}... | custom-call | tf_op jit(solution)/shard_map/experts/pallas_call | solution.py:270
  103.4 1.1 collective-permute-start.22
  104.5 4.9 %experts.7 = (bf16[144,2048]{1,0:T(8,128)(2,1)S(1)}, bf16[144,2048]{1,0:T(8,128)(2,1)S(1)}, bf16[1152,2048]{1,0:T(8,128)(2,1)S(1)}, bf16[1152,2048]{1,0:T(8,128)...) custom-call(bf16[2,144,2048]{2,1,0:T(8,128)(2,1)S(1)} %get-tuple-ele, ...), custom_call_target="tpu_custom_call", output_to_operand_aliasing={{2}: (5, {}), {3}: (6, {}), {4}: (7, {}), {5}: (8, {}), {6}... | custom-call | tf_op jit(solution)/shard_map/experts/pallas_call | solution.py:270
  111.0 3.1 %collective-permute-start.29 = (bf16[128,1024]{1,0:T(8,128)(2,1)S(1)}, bf16[128,1024]{1,0:T(8,128)(2,1)S(1)}, u32[]{:S(2)}, u32[]{:S(2)}) collective-permute-start(bf16[128,1024]{1,0:T(8,128)(2,1)S(1)} %fusion.7), channel_id=1, source_target_pairs={{0,8},{1,9},{2,10},{3,11},{4,12},{5,13},{6,14},{7,15},{8,24},{9,25... | collective-permute-start | bytes 786440 | tf_op jit(solution)/shard_map/ppermute | solution.py:315
  114.1 1.3 place.6
  115.3 1.3 collective-permute-start.27
  116.8 1.3 place.7
  119.0 5.6 %collective-permute-done.27 = bf16[2,128,1024]{2,1,0:T(8,128)(2,1)S(1)} collective-permute-done((bf16[2,128,1024]{2,1,0:T(8,128)(2,1)S(1)}, bf16[2,128,1024]{2,1,0:T(8,128)(2,1)S(1)}, u32[]{:S(2)}, u32[]{:S(2)}) %collective-permute-start.27) | collective-permute-done | bytes 524320 | tf_op jit(solution)/shard_map/ppermute | solution.py:315
  124.8 0.9 collective-permute-start.28
  125.7 3.4 %fusion.2 = bf16[1,384,2048]{2,1,0:T(8,128)(2,1)} fusion(bf16[1152,384]{1,0:T(8,128)(2,1)S(1)} %get-tuple-element.208, bf16[1152,2048]{1,0:T(8,128)(2,1)S(1)} %get-tuple-element.209), kind=kOutput, calls=%fused_computation.5 | convolution fusion | flops 1812725760 | bytes 7176192 | tf_op jit(solution)/shard_map/dot_general | solution.py:440
  129.1 3.3 %collective-permute-done.28 = bf16[128,1024]{1,0:T(8,128)(2,1)S(1)} collective-permute-done((bf16[128,1024]{1,0:T(8,128)(2,1)S(1)}, bf16[128,1024]{1,0:T(8,128)(2,1)S(1)}, u32[]{:S(2)}, u32[]{:S(2)}) %collective-permute-start.28) | collective-permute-done | bytes 262176 | tf_op jit(solution)/shard_map/ppermute | solution.py:315
  134.5 3.4 %fusion = bf16[1,384,2048]{2,1,0:T(8,128)(2,1)} fusion(bf16[1152,384]{1,0:T(8,128)(2,1)S(1)} %get-tuple-element.203, bf16[1152,2048]{1,0:T(8,128)(2,1)S(1)} %get-tuple-element.204), kind=kOutput, calls=%fused_computation.3 | convolution fusion | flops 1812725760 | bytes 7176192 | tf_op jit(solution)/shard_map/dot_general | solution.py:441
  137.9 4.1 %collective-permute-done.31 = bf16[128,1024]{1,0:T(8,128)(2,1)S(1)} collective-permute-done((bf16[128,1024]{1,0:T(8,128)(2,1)S(1)}, bf16[128,1024]{1,0:T(8,128)(2,1)S(1)}, u32[]{:S(2)}, u32[]{:S(2)}) %collective-permute-start.31) | collective-permute-done | bytes 262176 | tf_op jit(solution)/shard_map/ppermute | solution.py:315
  142.1 0.9 collective-permute-start.32
  143.0 3.4 %fusion.1 = bf16[1,384,2048]{2,1,0:T(8,128)(2,1)} fusion(bf16[1152,384]{1,0:T(8,128)(2,1)S(1)} %get-tuple-element.206, bf16[1152,2048]{1,0:T(8,128)(2,1)S(1)} %get-tuple-element.204), kind=kOutput, calls=%fused_computation.4 | convolution fusion | flops 1812725760 | bytes 7176192 | tf_op jit(solution)/shard_map/dot_general | solution.py:442
  146.4 4.3 %collective-permute-done.33 = bf16[128,1024]{1,0:T(8,128)(2,1)S(1)} collective-permute-done((bf16[128,1024]{1,0:T(8,128)(2,1)S(1)}, bf16[128,1024]{1,0:T(8,128)(2,1)S(1)}, u32[]{:S(2)}, u32[]{:S(2)}) %collective-permute-start.33) | collective-permute-done | bytes 262176 | tf_op jit(solution)/shard_map/ppermute | solution.py:315
  (69 shorter events, 15.9 us)
Async XLA Ops:
  0.6 59.7 %copy-start.2 = (bf16[1,384,2048]{2,1,0:T(8,128)(2,1)S(1)}, bf16[1,384,2048]{2,1,0:T(8,128)(2,1)}, u32[]{:S(2)}) copy-start(bf16[1,384,2048]{2,1,0:T(8,128)(2,1)} %param.13) | copy-start | bytes 4718596
  2.6 16.2 %collective-permute-start = (bf16[272,1024]{1,0:T(8,128)(2,1)}, bf16[272,1024]{1,0:T(8,128)(2,1)S(1)}, u32[]{:S(2)}, u32[]{:S(2)}) collective-permute-start(bf16[272,1024]{1,0:T(8,128)(2,1)} %pack.1.refs_0_), channel_id=1, source_target_pairs={{0,1},{1,0},{2,6},{3,7},{4,5},{5,4},{6,2},{7,3},{8,9},{9,8},{10,14... | collective-permute-start | bytes 1671176 | tf_op jit(solution)/shard_map/ppermute | solution.py:315
  5.6 14.0 %collective-permute-start.1 = (bf16[272,1024]{1,0:T(8,128)(2,1)}, bf16[272,1024]{1,0:T(8,128)(2,1)S(1)}, u32[]{:S(2)}, u32[]{:S(2)}) collective-permute-start(bf16[272,1024]{1,0:T(8,128)(2,1)} %pack.1.refs_0_), channel_id=1, source_target_pairs={{0,4},{1,5},{2,3},{3,2},{4,0},{5,1},{6,7},{7,6},{8,12},{9,13},{10,... | collective-permute-start | bytes 1671176 | tf_op jit(solution)/shard_map/ppermute | solution.py:315
  7.1 15.0 %collective-permute-start.2 = (bf16[272,1024]{1,0:T(8,128)(2,1)}, bf16[272,1024]{1,0:T(8,128)(2,1)}, u32[]{:S(2)}, u32[]{:S(2)}) collective-permute-start(bf16[272,1024]{1,0:T(8,128)(2,1)} %pack.1.refs_0_), channel_id=1, source_target_pairs={{0,8},{1,9},{2,10},{3,11},{4,12},{5,13},{6,14},{7,15},{8,24},{9,25... | collective-permute-start | bytes 1671176 | tf_op jit(solution)/shard_map/ppermute | solution.py:315
  18.8 0.8 copy-start.4
  22.1 14.1 %collective-permute-start.4 = (bf16[272,1024]{1,0:T(8,128)(2,1)S(1)}, bf16[272,1024]{1,0:T(8,128)(2,1)S(1)}, u32[]{:S(2)}, u32[]{:S(2)}) collective-permute-start(bf16[272,1024]{1,0:T(8,128)(2,1)S(1)} %collective-permute-done.1.refs_1_), channel_id=1, source_target_pairs={{0,1},{1,0},{2,6},{3,7},{4,5},{5,4},{6,2},{7,3},{8,9},{9,8},{10,14... | collective-permute-start | bytes 1671176 | tf_op jit(solution)/shard_map/ppermute | solution.py:315
  22.7 0.8 copy-start.6
  23.5 15.9 %collective-permute-start.5 = (bf16[272,1024]{1,0:T(8,128)(2,1)}, bf16[272,1024]{1,0:T(8,128)(2,1)}, u32[]{:S(2)}, u32[]{:S(2)}) collective-permute-start(bf16[272,1024]{1,0:T(8,128)(2,1)} %collective-permute-done.2.refs_0_), channel_id=1, source_target_pairs={{0,4},{1,5},{2,3},{3,2},{4,0},{5,1},{6,7},{7,6},{8,12},{9,13},{10,... | collective-permute-start | bytes 1671176 | tf_op jit(solution)/shard_map/ppermute | solution.py:315
  24.0 15.4 %collective-permute-start.6 = (bf16[272,1024]{1,0:T(8,128)(2,1)}, bf16[272,1024]{1,0:T(8,128)(2,1)S(1)}, u32[]{:S(2)}, u32[]{:S(2)}) collective-permute-start(bf16[272,1024]{1,0:T(8,128)(2,1)} %collective-permute-done.2.refs_0_), channel_id=1, source_target_pairs={{0,8},{1,9},{2,10},{3,11},{4,12},{5,13},{6,14},{7,15},{8,24},{9,25... | collective-permute-start | bytes 1671176 | tf_op jit(solution)/shard_map/ppermute | solution.py:315
  25.1 23.0 %collective-permute-start.3 = (bf16[272,1024]{1,0:T(8,128)(2,1)}, bf16[272,1024]{1,0:T(8,128)(2,1)}, u32[]{:S(2)}, u32[]{:S(2)}) collective-permute-start(bf16[272,1024]{1,0:T(8,128)(2,1)} %collective-permute-done.2.refs_0_), channel_id=1, source_target_pairs={{0,1},{1,0},{2,6},{3,7},{4,5},{5,4},{6,2},{7,3},{8,9},{9,8},{10,14... | collective-permute-start | bytes 1671176 | tf_op jit(solution)/shard_map/ppermute | solution.py:315
  36.3 0.8 copy-start.8
  39.4 9.5 %collective-permute-start.7 = (bf16[272,1024]{1,0:T(8,128)(2,1)S(1)}, bf16[272,1024]{1,0:T(8,128)(2,1)S(1)}, u32[]{:S(2)}, u32[]{:S(2)}) collective-permute-start(bf16[272,1024]{1,0:T(8,128)(2,1)S(1)} %collective-permute-done.6.refs_0_), channel_id=1, source_target_pairs={{0,1},{1,0},{2,6},{3,7},{4,5},{5,4},{6,2},{7,3},{8,9},{9,8},{10,14... | collective-permute-start | bytes 1671176 | tf_op jit(solution)/shard_map/ppermute | solution.py:315
  40.9 14.1 %collective-permute-start.8 = (bf16[272,1024]{1,0:T(8,128)(2,1)}, bf16[272,1024]{1,0:T(8,128)(2,1)}, u32[]{:S(2)}, u32[]{:S(2)}) collective-permute-start(bf16[272,1024]{1,0:T(8,128)(2,1)} %collective-permute-done.5.refs_1_), channel_id=1, source_target_pairs={{0,1},{1,0},{2,6},{3,7},{4,5},{5,4},{6,2},{7,3},{8,9},{9,8},{10,14... | collective-permute-start | bytes 1671176 | tf_op jit(solution)/shard_map/ppermute | solution.py:315
  41.4 13.6 %collective-permute-start.9 = (bf16[272,1024]{1,0:T(8,128)(2,1)S(1)}, bf16[272,1024]{1,0:T(8,128)(2,1)S(1)}, u32[]{:S(2)}, u32[]{:S(2)}) collective-permute-start(bf16[272,1024]{1,0:T(8,128)(2,1)S(1)} %collective-permute-done.6.refs_0_), channel_id=1, source_target_pairs={{0,8},{1,9},{2,10},{3,11},{4,12},{5,13},{6,14},{7,15},{8,24},{9,25... | collective-permute-start | bytes 1671176 | tf_op jit(solution)/shard_map/ppermute | solution.py:315
  42.4 1.1 copy-start.3
  43.4 1.1 copy-start.5
  44.5 1.1 copy-start.7
  45.5 1.1 copy-start.9
  46.6 13.8 %copy-start.1 = (bf16[1,384,2048]{2,1,0:T(8,128)(2,1)S(1)}, bf16[1,384,2048]{2,1,0:T(8,128)(2,1)}, u32[]{:S(2)}) copy-start(bf16[1,384,2048]{2,1,0:T(8,128)(2,1)} %param.12) | copy-start | bytes 4718596
  48.1 12.3 %copy-start = (bf16[1,384,2048]{2,1,0:T(8,128)(2,1)S(1)}, bf16[1,384,2048]{2,1,0:T(8,128)(2,1)}, u32[]{:S(2)}) copy-start(bf16[1,384,2048]{2,1,0:T(8,128)(2,1)} %param.11) | copy-start | bytes 4718596
  55.0 5.4 %collective-permute-start.13 = (bf16[2,144,2048]{2,1,0:T(8,128)(2,1)S(1)}, bf16[2,144,2048]{2,1,0:T(8,128)(2,1)S(1)}, u32[]{:S(2)}, u32[]{:S(2)}) collective-permute-start(bf16[2,144,2048]{2,1,0:T(8,128)(2,1)S(1)} %get-tuple-element.130), channel_id=1, source_target_pairs={{0,2},{1,3},{2,0},{3,1},{4,6},{5,7},{6,4},{7,5},{8,10},{9,11},{10,... | collective-permute-start | bytes 3538952 | tf_op jit(solution)/shard_map/ppermute | solution.py:315
  55.0 16.1 %collective-permute-start.11 = (bf16[272,1024]{1,0:T(8,128)(2,1)}, bf16[272,1024]{1,0:T(8,128)(2,1)S(1)}, u32[]{:S(2)}, u32[]{:S(2)}) collective-permute-start(bf16[272,1024]{1,0:T(8,128)(2,1)} %collective-permute-done.5.refs_1_), channel_id=1, source_target_pairs={{0,8},{1,9},{2,10},{3,11},{4,12},{5,13},{6,14},{7,15},{8,24},{9,25... | collective-permute-start | bytes 1671176 | tf_op jit(solution)/shard_map/ppermute | solution.py:315
  55.9 15.5 %collective-permute-start.10 = (bf16[272,1024]{1,0:T(8,128)(2,1)S(1)}, bf16[272,1024]{1,0:T(8,128)(2,1)S(1)}, u32[]{:S(2)}, u32[]{:S(2)}) collective-permute-start(bf16[272,1024]{1,0:T(8,128)(2,1)S(1)} %collective-permute-done.9.refs_0_), channel_id=1, source_target_pairs={{0,1},{1,0},{2,6},{3,7},{4,5},{5,4},{6,2},{7,3},{8,9},{9,8},{10,14... | collective-permute-start | bytes 1671176 | tf_op jit(solution)/shard_map/ppermute | solution.py:315
  57.2 14.1 %collective-permute-start.12 = (bf16[272,1024]{1,0:T(8,128)(2,1)S(1)}, bf16[272,1024]{1,0:T(8,128)(2,1)S(1)}, u32[]{:S(2)}, u32[]{:S(2)}) collective-permute-start(bf16[272,1024]{1,0:T(8,128)(2,1)S(1)} %collective-permute-done.9.refs_0_), channel_id=1, source_target_pairs={{0,4},{1,5},{2,3},{3,2},{4,0},{5,1},{6,7},{7,6},{8,12},{9,13},{10,... | collective-permute-start | bytes 1671176 | tf_op jit(solution)/shard_map/ppermute | solution.py:315
  71.4 5.0 %collective-permute-start.16 = (bf16[2,144,2048]{2,1,0:T(8,128)(2,1)S(1)}, bf16[2,144,2048]{2,1,0:T(8,128)(2,1)S(1)}, u32[]{:S(2)}, u32[]{:S(2)}) collective-permute-start(bf16[2,144,2048]{2,1,0:T(8,128)(2,1)S(1)} %get-tuple-element.143), channel_id=1, source_target_pairs={{0,2},{1,3},{2,0},{3,1},{4,6},{5,7},{6,4},{7,5},{8,10},{9,11},{10,... | collective-permute-start | bytes 3538952 | tf_op jit(solution)/shard_map/ppermute | solution.py:315
  71.5 3.6 %collective-permute-start.14 = (bf16[144,2048]{1,0:T(8,128)(2,1)S(1)}, bf16[144,2048]{1,0:T(8,128)(2,1)S(1)}, u32[]{:S(2)}, u32[]{:S(2)}) collective-permute-start(bf16[144,2048]{1,0:T(8,128)(2,1)S(1)} %get-tuple-element.138), channel_id=1, source_target_pairs={{0,2},{1,3},{2,0},{3,1},{4,6},{5,7},{6,4},{7,5},{8,10},{9,11},{10,... | collective-permute-start | bytes 1769480 | tf_op jit(solution)/shard_map/ppermute | solution.py:315
  71.9 9.5 %collective-permute-start.19 = (bf16[272,1024]{1,0:T(8,128)(2,1)S(1)}, bf16[272,1024]{1,0:T(8,128)(2,1)S(1)}, u32[]{:S(2)}, u32[]{:S(2)}) collective-permute-start(bf16[272,1024]{1,0:T(8,128)(2,1)S(1)} %collective-permute-done.11.refs_1_), channel_id=1, source_target_pairs={{0,1},{1,0},{2,6},{3,7},{4,5},{5,4},{6,2},{7,3},{8,9},{9,8},{10,14... | collective-permute-start | bytes 1671176 | tf_op jit(solution)/shard_map/ppermute | solution.py:315
  73.1 14.2 %collective-permute-start.20 = (bf16[272,1024]{1,0:T(8,128)(2,1)S(1)}, bf16[272,1024]{1,0:T(8,128)(2,1)S(1)}, u32[]{:S(2)}, u32[]{:S(2)}) collective-permute-start(bf16[272,1024]{1,0:T(8,128)(2,1)S(1)} %collective-permute-done.12.refs_1_), channel_id=1, source_target_pairs={{0,1},{1,0},{2,6},{3,7},{4,5},{5,4},{6,2},{7,3},{8,9},{9,8},{10,14... | collective-permute-start | bytes 1671176 | tf_op jit(solution)/shard_map/ppermute | solution.py:315
  88.9 8.8 %collective-permute-start.21 = (bf16[2,144,2048]{2,1,0:T(8,128)(2,1)S(1)}, bf16[2,144,2048]{2,1,0:T(8,128)(2,1)S(1)}, u32[]{:S(2)}, u32[]{:S(2)}) collective-permute-start(bf16[2,144,2048]{2,1,0:T(8,128)(2,1)S(1)} %get-tuple-element.165), channel_id=1, source_target_pairs={{0,2},{1,3},{2,0},{3,1},{4,6},{5,7},{6,4},{7,5},{8,10},{9,11},{10,... | collective-permute-start | bytes 3538952 | tf_op jit(solution)/shard_map/ppermute | solution.py:315
  89.0 3.7 %collective-permute-start.17 = (bf16[144,2048]{1,0:T(8,128)(2,1)S(1)}, bf16[144,2048]{1,0:T(8,128)(2,1)S(1)}, u32[]{:S(2)}, u32[]{:S(2)}) collective-permute-start(bf16[144,2048]{1,0:T(8,128)(2,1)S(1)} %get-tuple-element.153), channel_id=1, source_target_pairs={{0,2},{1,3},{2,0},{3,1},{4,6},{5,7},{6,4},{7,5},{8,10},{9,11},{10,... | collective-permute-start | bytes 1769480 | tf_op jit(solution)/shard_map/ppermute | solution.py:315
  93.9 9.2 %collective-permute-start.18 = (bf16[2,128,1024]{2,1,0:T(8,128)(2,1)S(1)}, bf16[2,128,1024]{2,1,0:T(8,128)(2,1)S(1)}, u32[]{:S(2)}, u32[]{:S(2)}) collective-permute-start(bf16[2,128,1024]{2,1,0:T(8,128)(2,1)S(1)} %get-tuple-element.155), channel_id=1, source_target_pairs={{0,1},{1,0},{2,6},{3,7},{4,5},{5,4},{6,2},{7,3},{8,9},{9,8},{10,14... | collective-permute-start | bytes 1572872 | tf_op jit(solution)/shard_map/ppermute | solution.py:315
  96.8 7.7 %collective-permute-start.23 = (bf16[2,144,2048]{2,1,0:T(8,128)(2,1)S(1)}, bf16[2,144,2048]{2,1,0:T(8,128)(2,1)S(1)}, u32[]{:S(2)}, u32[]{:S(2)}) collective-permute-start(bf16[2,144,2048]{2,1,0:T(8,128)(2,1)S(1)} %get-tuple-element.179), channel_id=1, source_target_pairs={{0,2},{1,3},{2,0},{3,1},{4,6},{5,7},{6,4},{7,5},{8,10},{9,11},{10,... | collective-permute-start | bytes 3538952 | tf_op jit(solution)/shard_map/ppermute | solution.py:315
  96.8 14.1 %collective-permute-start.15 = (bf16[2,128,1024]{2,1,0:T(8,128)(2,1)S(1)}, bf16[2,128,1024]{2,1,0:T(8,128)(2,1)S(1)}, u32[]{:S(2)}, u32[]{:S(2)}) collective-permute-start(bf16[2,128,1024]{2,1,0:T(8,128)(2,1)S(1)} %get-tuple-element.140), channel_id=1, source_target_pairs={{0,1},{1,0},{2,6},{3,7},{4,5},{5,4},{6,2},{7,3},{8,9},{9,8},{10,14... | collective-permute-start | bytes 1572872 | tf_op jit(solution)/shard_map/ppermute | solution.py:315
  103.2 10.9 %collective-permute-start.24 = (bf16[144,2048]{1,0:T(8,128)(2,1)S(1)}, bf16[144,2048]{1,0:T(8,128)(2,1)S(1)}, u32[]{:S(2)}, u32[]{:S(2)}) collective-permute-start(bf16[144,2048]{1,0:T(8,128)(2,1)S(1)} %get-tuple-element.191), channel_id=1, source_target_pairs={{0,2},{1,3},{2,0},{3,1},{4,6},{5,7},{6,4},{7,5},{8,10},{9,11},{10,... | collective-permute-start | bytes 1769480 | tf_op jit(solution)/shard_map/ppermute | solution.py:315
  103.4 7.4 %collective-permute-start.22 = (bf16[128,1024]{1,0:T(8,128)(2,1)S(1)}, bf16[128,1024]{1,0:T(8,128)(2,1)S(1)}, u32[]{:S(2)}, u32[]{:S(2)}) collective-permute-start(bf16[128,1024]{1,0:T(8,128)(2,1)S(1)} %fusion.14), channel_id=1, source_target_pairs={{0,4},{1,5},{2,3},{3,2},{4,0},{5,1},{6,7},{7,6},{8,12},{9,13},{10,... | collective-permute-start | bytes 786440 | tf_op jit(solution)/shard_map/ppermute | solution.py:315
  109.4 7.3 %collective-permute-start.25 = (bf16[144,2048]{1,0:T(8,128)(2,1)S(1)}, bf16[144,2048]{1,0:T(8,128)(2,1)S(1)}, u32[]{:S(2)}, u32[]{:S(2)}) collective-permute-start(bf16[144,2048]{1,0:T(8,128)(2,1)S(1)} %get-tuple-element.194), channel_id=1, source_target_pairs={{0,2},{1,3},{2,0},{3,1},{4,6},{5,7},{6,4},{7,5},{8,10},{9,11},{10,... | collective-permute-start | bytes 1769480 | tf_op jit(solution)/shard_map/ppermute | solution.py:315
  111.0 18.1 %collective-permute-start.29 = (bf16[128,1024]{1,0:T(8,128)(2,1)S(1)}, bf16[128,1024]{1,0:T(8,128)(2,1)S(1)}, u32[]{:S(2)}, u32[]{:S(2)}) collective-permute-start(bf16[128,1024]{1,0:T(8,128)(2,1)S(1)} %fusion.7), channel_id=1, source_target_pairs={{0,8},{1,9},{2,10},{3,11},{4,12},{5,13},{6,14},{7,15},{8,24},{9,25... | collective-permute-start | bytes 786440 | tf_op jit(solution)/shard_map/ppermute | solution.py:315
  115.3 9.2 %collective-permute-start.27 = (bf16[2,128,1024]{2,1,0:T(8,128)(2,1)S(1)}, bf16[2,128,1024]{2,1,0:T(8,128)(2,1)S(1)}, u32[]{:S(2)}, u32[]{:S(2)}) collective-permute-start(bf16[2,128,1024]{2,1,0:T(8,128)(2,1)S(1)} %get-tuple-element.192), channel_id=1, source_target_pairs={{0,1},{1,0},{2,6},{3,7},{4,5},{5,4},{6,2},{7,3},{8,9},{9,8},{10,14... | collective-permute-start | bytes 1572872 | tf_op jit(solution)/shard_map/ppermute | solution.py:315
  118.1 15.3 %collective-permute-start.26 = (bf16[2,128,1024]{2,1,0:T(8,128)(2,1)S(1)}, bf16[2,128,1024]{2,1,0:T(8,128)(2,1)S(1)}, u32[]{:S(2)}, u32[]{:S(2)}) collective-permute-start(bf16[2,128,1024]{2,1,0:T(8,128)(2,1)S(1)} %get-tuple-element.196), channel_id=1, source_target_pairs={{0,1},{1,0},{2,6},{3,7},{4,5},{5,4},{6,2},{7,3},{8,9},{9,8},{10,14... | collective-permute-start | bytes 1572872 | tf_op jit(solution)/shard_map/ppermute | solution.py:315
  124.8 7.6 %collective-permute-start.28 = (bf16[128,1024]{1,0:T(8,128)(2,1)S(1)}, bf16[128,1024]{1,0:T(8,128)(2,1)S(1)}, u32[]{:S(2)}, u32[]{:S(2)}) collective-permute-start(bf16[128,1024]{1,0:T(8,128)(2,1)S(1)} %fusion.16), channel_id=1, source_target_pairs={{0,4},{1,5},{2,3},{3,2},{4,0},{5,1},{6,7},{7,6},{8,12},{9,13},{10,... | collective-permute-start | bytes 786440 | tf_op jit(solution)/shard_map/ppermute | solution.py:315
  132.5 9.5 %collective-permute-start.31 = (bf16[128,1024]{1,0:T(8,128)(2,1)S(1)}, bf16[128,1024]{1,0:T(8,128)(2,1)S(1)}, u32[]{:S(2)}, u32[]{:S(2)}) collective-permute-start(bf16[128,1024]{1,0:T(8,128)(2,1)S(1)} %fusion.10), channel_id=1, source_target_pairs={{0,8},{1,9},{2,10},{3,11},{4,12},{5,13},{6,14},{7,15},{8,24},{9,25... | collective-permute-start | bytes 786440 | tf_op jit(solution)/shard_map/ppermute | solution.py:315
  133.6 8.4 %collective-permute-start.30 = (bf16[128,1024]{1,0:T(8,128)(2,1)S(1)}, bf16[128,1024]{1,0:T(8,128)(2,1)S(1)}, u32[]{:S(2)}, u32[]{:S(2)}) collective-permute-start(bf16[128,1024]{1,0:T(8,128)(2,1)S(1)} %fusion.17), channel_id=1, source_target_pairs={{0,4},{1,5},{2,3},{3,2},{4,0},{5,1},{6,7},{7,6},{8,12},{9,13},{10,... | collective-permute-start | bytes 786440 | tf_op jit(solution)/shard_map/ppermute | solution.py:315
  142.1 8.7 %collective-permute-start.33 = (bf16[128,1024]{1,0:T(8,128)(2,1)S(1)}, bf16[128,1024]{1,0:T(8,128)(2,1)S(1)}, u32[]{:S(2)}, u32[]{:S(2)}) collective-permute-start(bf16[128,1024]{1,0:T(8,128)(2,1)S(1)} %fusion.5), channel_id=1, source_target_pairs={{0,8},{1,9},{2,10},{3,11},{4,12},{5,13},{6,14},{7,15},{8,24},{9,25... | collective-permute-start | bytes 786440 | tf_op jit(solution)/shard_map/ppermute | solution.py:315
  142.1 8.6 %collective-permute-start.32 = (bf16[128,1024]{1,0:T(8,128)(2,1)S(1)}, bf16[128,1024]{1,0:T(8,128)(2,1)S(1)}, u32[]{:S(2)}, u32[]{:S(2)}) collective-permute-start(bf16[128,1024]{1,0:T(8,128)(2,1)S(1)} %fusion.15), channel_id=1, source_target_pairs={{0,4},{1,5},{2,3},{3,2},{4,0},{5,1},{6,7},{7,6},{8,12},{9,13},{10,... | collective-permute-start | bytes 786440 | tf_op jit(solution)/shard_map/ppermute | solution.py:315

commit v17 on v13

--- a/solution.py
+++ b/solution.py
@@ -349,7 +349,7 @@
     ]
     have = {("s", 0): share}
     kept, picked, parts = None, None, None
-    late, last, done = [], [], 0
+    late, done = [], 0
     for plane, ring in waves:
         came = {}
         for kind, c in plane:
@@ -387,32 +387,28 @@
         if parts is not None:
             keep, send = placed(*parts)
             late.append((keep, to_second(send)))
-            mine, parts = tied(mine, send), None
+            mine = tied(mine, send)
         near, far, *kept = run_experts(done, chunks, mine, to_core(theirs), weights, kept)
-        last.append((picks, near, far))
+        parts, mark = (picks, near, far), [near]
         done += 1
-    nears = [near for _, near, _ in last]
-    near, send = nears[-1], nears[0]
-    for picks, first, far in last:
-        keep, send = placed(picks, tied(first, send), far)
-        late.append((keep, to_second(send)))
-    ties = [nears[0], send]
+    keep, send = placed(*parts)
+    late.append((keep, to_second(send)))
     marks = [send] * (chunks + 2)
-    running = None
+    running, previous = None, send
     for c in range(1, chunks):
         keep, came = late[c]
-        if c + 1 < chunks:
-            came = tied(came, ties[c - 1])
+        came = tied(came, near if c == 1 else send if c + 1 < chunks else previous)
         pair = added(keep, came)
         came = to_first(pair[1].astype(jnp.bfloat16))
-        total = added(pair[0], tied(came, send) if c == 1 else came)
+        total = added(pair[0], tied(came, send) if c + 2 < chunks else came)
         running = (total if running is None else added(total, running)).astype(jnp.bfloat16)
+        previous = running
         if c > 1:
             marks[min(c - 1, 2)] = running
         if c + 1 < chunks:
             running = to_ring(running)
     keep, came = late[0]
-    pair = added(keep, tied(came, send))
+    pair = added(keep, tied(came, near))
     came = pair[1].astype(jnp.bfloat16)
     own = added(pair[0], to_first(came if running is None else tied(came, running)))
     grad_tokens = (own if running is None else added(own, to_ring(running))).astype(jnp.bfloat16)

time: 145 us -> 145 us (level)
  transfers between devices with their start and end apart: 34 -> 34, of which waited for: 17 -> 19; matrix products, arithmetic and copies ran while one was open for 8% -> 8% of each run, Pallas kernels for 22% -> 20%
where the time goes in v17:
time: 145 us
  waiting for transfers between devices  58.7 us (40%)
  Pallas kernels  33.8 us (23%)
  starting transfers between devices  32.5 us (22%)
  matrix products  10.2 us (7%)
  local copies, waits for them, and re-layouts  6.76 us (5%)
  other arithmetic  1.71 us (1%)
    ppermute x34, waiting for transfers between devices, permute(): return lax.ppermute(value, ('expert', 'etp'), pairs)  58.7 us
    ppermute x34, starting transfers between devices, permute(): return lax.ppermute(value, ('expert', 'etp'), pairs)  32.5 us
    pallas_call x4, Pallas kernels, run_experts(): pl.pallas_call(functools.partial(expert_kernel, index, kept is not None),...  19.7 us
    pallas_call x4, Pallas kernels, pick_rows(): pl.pallas_call(functools.partial(pick_kernel, top, rows), in_specs=[pl.Bl...  7.05 us
    unnamed x20, local copies, waits for them, and re-layouts  6.63 us
    pallas_call x4, Pallas kernels, place_rows(): pl.pallas_call(place_kernel, in_specs=[pl.BlockSpec(memory_space=pltpu.SM...  5.08 us
    dot_general x1, matrix products, gather_body(): lax.dot_general(gate_term, rows_x, CONTRACT_FIRST, preferred_element_type...  3.41 us
    dot_general x1, matrix products, gather_body(): lax.dot_general(up_term, rows_x, CONTRACT_FIRST, preferred_element_type=j...  3.41 us
  transfers between devices with their start and end apart: 34, of which 19 were waited for; matrix products, arithmetic and copies ran while one was open for 8% of the time, Pallas kernels for 20%

profile of v17, /device:TPU:0, one launch (start us, length us, event | category | flops | bytes accessed | tf_op | source)
XLA Modules:
  0.0 144.8 jit_solution(9221749152226087981)
XLA Ops:
  0.6 2.0 %pack.1.refs_0_ = bf16[272,1024]{1,0:T(8,128)(2,1)} custom-call(bf16[128,1024]{1,0:T(8,128)(2,1)} %tokens_ref.1, bf16[128,1024]{1,0:T(8,128)(2,1)} %grads_ref.1, s32[8,128]{1,0:T(8,128)} %bitcast.70, f32[8,128]{1,0:T(8,128)} %bitcast.71), custom_call_target="tpu_custom_call" | custom-call | tf_op jit(solution)/shard_map/pack/pallas_call | solution.py:128
  2.6 2.9 %collective-permute-start = (bf16[272,1024]{1,0:T(8,128)(2,1)}, bf16[272,1024]{1,0:T(8,128)(2,1)S(1)}, u32[]{:S(2)}, u32[]{:S(2)}) collective-permute-start(bf16[272,1024]{1,0:T(8,128)(2,1)} %pack.1.refs_0_), channel_id=1, source_target_pairs={{0,1},{1,0},{2,6},{3,7},{4,5},{5,4},{6,2},{7,3},{8,9},{9,8},{10,14... | collective-permute-start | bytes 1671176 | tf_op jit(solution)/shard_map/ppermute | solution.py:315
  5.6 1.5 %collective-permute-start.1 = (bf16[272,1024]{1,0:T(8,128)(2,1)}, bf16[272,1024]{1,0:T(8,128)(2,1)S(1)}, u32[]{:S(2)}, u32[]{:S(2)}) collective-permute-start(bf16[272,1024]{1,0:T(8,128)(2,1)} %pack.1.refs_0_), channel_id=1, source_target_pairs={{0,4},{1,5},{2,3},{3,2},{4,0},{5,1},{6,7},{7,6},{8,12},{9,13},{10,... | collective-permute-start | bytes 1671176 | tf_op jit(solution)/shard_map/ppermute | solution.py:315
  7.1 1.6 %collective-permute-start.2 = (bf16[272,1024]{1,0:T(8,128)(2,1)}, bf16[272,1024]{1,0:T(8,128)(2,1)}, u32[]{:S(2)}, u32[]{:S(2)}) collective-permute-start(bf16[272,1024]{1,0:T(8,128)(2,1)} %pack.1.refs_0_), channel_id=1, source_target_pairs={{0,8},{1,9},{2,10},{3,11},{4,12},{5,13},{6,14},{7,15},{8,24},{9,25... | collective-permute-start | bytes 1671176 | tf_op jit(solution)/shard_map/ppermute | solution.py:315
  8.7 10.1 %collective-permute-done.refs_2_ = bf16[272,1024]{1,0:T(8,128)(2,1)S(1)} collective-permute-done((bf16[272,1024]{1,0:T(8,128)(2,1)}, bf16[272,1024]{1,0:T(8,128)(2,1)S(1)}, u32[]{:S(2)}, u32[]{:S(2)}) %collective-permute-start) | collective-permute-done | bytes 557088 | tf_op jit(solution)/shard_map/ppermute | solution.py:315
  19.6 2.5 %collective-permute-done.2.refs_0_ = bf16[272,1024]{1,0:T(8,128)(2,1)} collective-permute-done((bf16[272,1024]{1,0:T(8,128)(2,1)}, bf16[272,1024]{1,0:T(8,128)(2,1)}, u32[]{:S(2)}, u32[]{:S(2)}) %collective-permute-start.2) | collective-permute-done | bytes 557088 | tf_op jit(solution)/shard_map/ppermute | solution.py:315
  25.1 1.1 collective-permute-start.3
  26.2 11.7 %collective-permute-done.5.refs_1_ = bf16[272,1024]{1,0:T(8,128)(2,1)} collective-permute-done((bf16[272,1024]{1,0:T(8,128)(2,1)}, bf16[272,1024]{1,0:T(8,128)(2,1)}, u32[]{:S(2)}, u32[]{:S(2)}) %collective-permute-start.5) | collective-permute-done | bytes 557088 | tf_op jit(solution)/shard_map/ppermute | solution.py:315
  39.3 1.5 %collective-permute-start.8 = (bf16[272,1024]{1,0:T(8,128)(2,1)}, bf16[272,1024]{1,0:T(8,128)(2,1)}, u32[]{:S(2)}, u32[]{:S(2)}) collective-permute-start(bf16[272,1024]{1,0:T(8,128)(2,1)} %collective-permute-done.5.refs_1_), channel_id=1, source_target_pairs={{0,1},{1,0},{2,6},{3,7},{4,5},{5,4},{6,2},{7,3},{8,9},{9,8},{10,14... | collective-permute-start | bytes 1671176 | tf_op jit(solution)/shard_map/ppermute | solution.py:315
  40.9 1.1 copy-done.3
  41.9 1.1 copy-done.5
  43.0 1.1 copy-done.7
  44.0 1.1 copy-done.9
  45.1 1.5 %pick.4 = (bf16[2,144,2048]{2,1,0:T(8,128)(2,1)S(1)}, bf16[2,144,2048]{2,1,0:T(8,128)(2,1)S(1)}, bf16[288,256]{1,0:T(8,128)(2,1)S(1)}) custom-call(s32[3]{0:T(128)S(1)} %pad_add_fusion.place_ref, bf16[272,1024]{1,0:T(8,128)(2,1)S(1)} %copy-done.3, bf16[272,1024]{1,0:T(8,128)(2,1)S(1)} %copy-done.7, bf16[272,1024]{1,0:T(8,128)(2,1)S(1)} %copy-done.5, ...), custom_call_target="tpu_custom_call" | custom-call | tf_op jit(solution)/shard_map/pick/pallas_call | solution.py:251
  46.6 1.7 %collective-permute-done.7.refs_2_ = bf16[272,1024]{1,0:T(8,128)(2,1)S(1)} collective-permute-done((bf16[272,1024]{1,0:T(8,128)(2,1)S(1)}, bf16[272,1024]{1,0:T(8,128)(2,1)S(1)}, u32[]{:S(2)}, u32[]{:S(2)}) %collective-permute-start.7) | collective-permute-done | bytes 557088 | tf_op jit(solution)/shard_map/ppermute | solution.py:315
  48.3 6.1 %collective-permute-done.8.refs_3_ = bf16[272,1024]{1,0:T(8,128)(2,1)} collective-permute-done((bf16[272,1024]{1,0:T(8,128)(2,1)}, bf16[272,1024]{1,0:T(8,128)(2,1)}, u32[]{:S(2)}, u32[]{:S(2)}) %collective-permute-start.8) | collective-permute-done | bytes 557088 | tf_op jit(solution)/shard_map/ppermute | solution.py:315
  54.9 1.6 %collective-permute-start.11 = (bf16[272,1024]{1,0:T(8,128)(2,1)}, bf16[272,1024]{1,0:T(8,128)(2,1)S(1)}, u32[]{:S(2)}, u32[]{:S(2)}) collective-permute-start(bf16[272,1024]{1,0:T(8,128)(2,1)} %collective-permute-done.5.refs_1_), channel_id=1, source_target_pairs={{0,8},{1,9},{2,10},{3,11},{4,12},{5,13},{6,14},{7,15},{8,24},{9,25... | collective-permute-start | bytes 1671176 | tf_op jit(solution)/shard_map/ppermute | solution.py:315
  57.8 2.5 %pick.5 = (bf16[2,144,2048]{2,1,0:T(8,128)(2,1)S(1)}, bf16[2,144,2048]{2,1,0:T(8,128)(2,1)S(1)}, bf16[288,256]{1,0:T(8,128)(2,1)S(1)}) custom-call(s32[3]{0:T(128)S(1)} %pad_add_fusion.place_ref, bf16[272,1024]{1,0:T(8,128)(2,1)} %collective-permute-done.2.refs_0_, bf16[272,1024]{1,0:T(8,128)(2,1)} %collective-permute-done.5.refs_1_, ...), custom_call_target="tpu_custom_call" | custom-call | tf_op jit(solution)/shard_map/pick/pallas_call | solution.py:251
  60.4 4.9 %experts.4 = (bf16[144,2048]{1,0:T(8,128)(2,1)S(1)}, bf16[144,2048]{1,0:T(8,128)(2,1)S(1)}, bf16[1152,2048]{1,0:T(8,128)(2,1)S(1)}, bf16[1152,2048]{1,0:T(8,128)...) custom-call(bf16[2,144,2048]{2,1,0:T(8,128)(2,1)S(1)} %get-tuple-element.127., ...), custom_call_target="tpu_custom_call" | custom-call | tf_op jit(solution)/shard_map/experts/pallas_call | solution.py:270
  65.3 5.3 %collective-permute-done.11.refs_1_ = bf16[272,1024]{1,0:T(8,128)(2,1)S(1)} collective-permute-done((bf16[272,1024]{1,0:T(8,128)(2,1)}, bf16[272,1024]{1,0:T(8,128)(2,1)S(1)}, u32[]{:S(2)}, u32[]{:S(2)}) %collective-permute-start.11) | collective-permute-done | bytes 557088 | tf_op jit(solution)/shard_map/ppermute | solution.py:315
  72.3 2.3 %collective-permute-done.14.far_ref = bf16[144,2048]{1,0:T(8,128)(2,1)S(1)} collective-permute-done((bf16[144,2048]{1,0:T(8,128)(2,1)S(1)}, bf16[144,2048]{1,0:T(8,128)(2,1)S(1)}, u32[]{:S(2)}, u32[]{:S(2)}) %collective-permute-start.14) | collective-permute-done | bytes 589856 | tf_op jit(solution)/shard_map/ppermute | solution.py:315
  74.6 1.3 place.4
  75.9 4.9 %experts.5 = (bf16[144,2048]{1,0:T(8,128)(2,1)S(1)}, bf16[144,2048]{1,0:T(8,128)(2,1)S(1)}, bf16[1152,2048]{1,0:T(8,128)(2,1)S(1)}, bf16[1152,2048]{1,0:T(8,128)...) custom-call(bf16[2,144,2048]{2,1,0:T(8,128)(2,1)S(1)} %get-tuple-ele, ...), custom_call_target="tpu_custom_call", output_to_operand_aliasing={{2}: (5, {}), {3}: (6, {}), {4}: (7, {}), {5}: (8, {}), {6}... | custom-call | tf_op jit(solution)/shard_map/experts/pallas_call | solution.py:270
  81.0 1.5 %pick.6 = (bf16[2,144,2048]{2,1,0:T(8,128)(2,1)S(1)}, bf16[2,144,2048]{2,1,0:T(8,128)(2,1)S(1)}, bf16[288,256]{1,0:T(8,128)(2,1)S(1)}) custom-call(s32[3]{0:T(128)S(1)} %pad_add_fusion.place_ref, bf16[272,1024]{1,0:T(8,128)(2,1)S(1)} %collective-permute-done.6.refs_0_, bf16[272,1024]{1,0:T(8,128)(2,1)S(1)} %collective-permute-done.11.refs_1_, ...), custom_call_target="tpu_custom_call" | custom-call | tf_op jit(solution)/shard_map/pick/pallas_call | solution.py:251
  84.0 2.3 %collective-permute-done.19.far_ref = bf16[144,2048]{1,0:T(8,128)(2,1)S(1)} collective-permute-done((bf16[144,2048]{1,0:T(8,128)(2,1)S(1)}, bf16[144,2048]{1,0:T(8,128)(2,1)S(1)}, u32[]{:S(2)}, u32[]{:S(2)}) %collective-permute-start.19) | collective-permute-done | bytes 589856 | tf_op jit(solution)/shard_map/ppermute | solution.py:315
  86.3 1.3 place.5
  87.6 5.1 %experts.6 = (bf16[144,2048]{1,0:T(8,128)(2,1)S(1)}, bf16[144,2048]{1,0:T(8,128)(2,1)S(1)}, bf16[1152,2048]{1,0:T(8,128)(2,1)S(1)}, bf16[1152,2048]{1,0:T(8,128)...) custom-call(bf16[2,144,2048]{2,1,0:T(8,128)(2,1)S(1)} %get-tuple-ele, ...), custom_call_target="tpu_custom_call", output_to_operand_aliasing={{2}: (5, {}), {3}: (6, {}), {4}: (7, {}), {5}: (8, {}), {6}... | custom-call | tf_op jit(solution)/shard_map/experts/pallas_call | solution.py:270
  92.7 1.5 %pick.7 = (bf16[2,144,2048]{2,1,0:T(8,128)(2,1)S(1)}, bf16[2,144,2048]{2,1,0:T(8,128)(2,1)S(1)}, bf16[288,256]{1,0:T(8,128)(2,1)S(1)}) custom-call(s32[3]{0:T(128)S(1)} %pad_add_fusion.place_ref, bf16[272,1024]{1,0:T(8,128)(2,1)S(1)} %collective-permute-done.9.refs_0_, bf16[272,1024]{1,0:T(8,128)(2,1)S(1)} %collective-permute-done.12.refs_1_, ...), custom_call_target="tpu_custom_call" | custom-call | tf_op jit(solution)/shard_map/pick/pallas_call | solution.py:251
  95.6 1.1 collective-permute-start.15
  96.8 1.2 collective-permute-done.21.far_ref
  97.9 1.3 place.6
  99.2 0.9 collective-permute-start.25
  100.2 4.9 %experts.7 = (bf16[144,2048]{1,0:T(8,128)(2,1)S(1)}, bf16[144,2048]{1,0:T(8,128)(2,1)S(1)}, bf16[1152,2048]{1,0:T(8,128)(2,1)S(1)}, bf16[1152,2048]{1,0:T(8,128)...) custom-call(bf16[2,144,2048]{2,1,0:T(8,128)(2,1)S(1)} %get-tuple-ele, ...), custom_call_target="tpu_custom_call", output_to_operand_aliasing={{2}: (5, {}), {3}: (6, {}), {4}: (7, {}), {5}: (8, {}), {6}... | custom-call | tf_op jit(solution)/shard_map/experts/pallas_call | solution.py:270
  105.8 0.9 collective-permute-start.28
  106.7 3.9 %collective-permute-done.15 = bf16[2,128,1024]{2,1,0:T(8,128)(2,1)S(1)} collective-permute-done((bf16[2,128,1024]{2,1,0:T(8,128)(2,1)S(1)}, bf16[2,128,1024]{2,1,0:T(8,128)(2,1)S(1)}, u32[]{:S(2)}, u32[]{:S(2)}) %collective-permute-start.15) | collective-permute-done | bytes 524320 | tf_op jit(solution)/shard_map/ppermute | solution.py:315
  110.7 1.3 place.7
  112.7 2.4 %collective-permute-done.28 = bf16[128,1024]{1,0:T(8,128)(2,1)S(1)} collective-permute-done((bf16[128,1024]{1,0:T(8,128)(2,1)S(1)}, bf16[128,1024]{1,0:T(8,128)(2,1)S(1)}, u32[]{:S(2)}, u32[]{:S(2)}) %collective-permute-start.28) | collective-permute-done | bytes 262176 | tf_op jit(solution)/shard_map/ppermute | solution.py:315
  115.2 1.9 %collective-permute-start.29 = (bf16[128,1024]{1,0:T(8,128)(2,1)S(1)}, bf16[128,1024]{1,0:T(8,128)(2,1)S(1)}, u32[]{:S(2)}, u32[]{:S(2)}) collective-permute-start(bf16[128,1024]{1,0:T(8,128)(2,1)S(1)} %fusion.7), channel_id=1, source_target_pairs={{0,8},{1,9},{2,10},{3,11},{4,12},{5,13},{6,14},{7,15},{8,24},{9,25... | collective-permute-start | bytes 786440 | tf_op jit(solution)/shard_map/ppermute | solution.py:315
  117.0 0.9 collective-permute-done.25
  118.2 1.6 %collective-permute-start.26 = (bf16[128,1024]{1,0:T(8,128)(2,1)S(1)}, bf16[128,1024]{1,0:T(8,128)(2,1)S(1)}, u32[]{:S(2)}, u32[]{:S(2)}) collective-permute-start(bf16[128,1024]{1,0:T(8,128)(2,1)S(1)} %fusion.15), channel_id=1, source_target_pairs={{0,4},{1,5},{2,3},{3,2},{4,0},{5,1},{6,7},{7,6},{8,12},{9,13},{10,... | collective-permute-start | bytes 786440 | tf_op jit(solution)/shard_map/ppermute | solution.py:315
  119.8 3.4 %fusion.2 = bf16[1,384,2048]{2,1,0:T(8,128)(2,1)} fusion(bf16[1152,384]{1,0:T(8,128)(2,1)S(1)} %get-tuple-element.204, bf16[1152,2048]{1,0:T(8,128)(2,1)S(1)} %get-tuple-element.205), kind=kOutput, calls=%fused_computation.5 | convolution fusion | flops 1812725760 | bytes 7176192 | tf_op jit(solution)/shard_map/dot_general | solution.py:417
  123.5 2.1 %collective-permute-done.26 = bf16[128,1024]{1,0:T(8,128)(2,1)S(1)} collective-permute-done((bf16[128,1024]{1,0:T(8,128)(2,1)S(1)}, bf16[128,1024]{1,0:T(8,128)(2,1)S(1)}, u32[]{:S(2)}, u32[]{:S(2)}) %collective-permute-start.26) | collective-permute-done | bytes 262176 | tf_op jit(solution)/shard_map/ppermute | solution.py:315
  125.7 2.7 %collective-permute-start.31 = (bf16[128,1024]{1,0:T(8,128)(2,1)S(1)}, bf16[128,1024]{1,0:T(8,128)(2,1)S(1)}, u32[]{:S(2)}, u32[]{:S(2)}) collective-permute-start(bf16[128,1024]{1,0:T(8,128)(2,1)S(1)} %fusion.10), channel_id=1, source_target_pairs={{0,8},{1,9},{2,10},{3,11},{4,12},{5,13},{6,14},{7,15},{8,24},{9,25... | collective-permute-start | bytes 786440 | tf_op jit(solution)/shard_map/ppermute | solution.py:315
  129.3 3.4 %fusion = bf16[1,384,2048]{2,1,0:T(8,128)(2,1)} fusion(bf16[1152,384]{1,0:T(8,128)(2,1)S(1)} %get-tuple-element.199, bf16[1152,2048]{1,0:T(8,128)(2,1)S(1)} %get-tuple-element.200), kind=kOutput, calls=%fused_computation.3 | convolution fusion | flops 1812725760 | bytes 7176192 | tf_op jit(solution)/shard_map/dot_general | solution.py:418
  132.7 2.5 %collective-permute-done.31 = bf16[128,1024]{1,0:T(8,128)(2,1)S(1)} collective-permute-done((bf16[128,1024]{1,0:T(8,128)(2,1)S(1)}, bf16[128,1024]{1,0:T(8,128)(2,1)S(1)}, u32[]{:S(2)}, u32[]{:S(2)}) %collective-permute-start.31) | collective-permute-done | bytes 262176 | tf_op jit(solution)/shard_map/ppermute | solution.py:315
  135.3 1.8 %collective-permute-start.33 = (bf16[128,1024]{1,0:T(8,128)(2,1)S(1)}, bf16[128,1024]{1,0:T(8,128)(2,1)S(1)}, u32[]{:S(2)}, u32[]{:S(2)}) collective-permute-start(bf16[128,1024]{1,0:T(8,128)(2,1)S(1)} %fusion.5), channel_id=1, source_target_pairs={{0,8},{1,9},{2,10},{3,11},{4,12},{5,13},{6,14},{7,15},{8,24},{9,25... | collective-permute-start | bytes 786440 | tf_op jit(solution)/shard_map/ppermute | solution.py:315
  137.7 3.4 %fusion.1 = bf16[1,384,2048]{2,1,0:T(8,128)(2,1)} fusion(bf16[1152,384]{1,0:T(8,128)(2,1)S(1)} %get-tuple-element.202, bf16[1152,2048]{1,0:T(8,128)(2,1)S(1)} %get-tuple-element.200), kind=kOutput, calls=%fused_computation.4 | convolution fusion | flops 1812725760 | bytes 7176192 | tf_op jit(solution)/shard_map/dot_general | solution.py:419
  141.1 2.4 %collective-permute-done.32 = bf16[128,1024]{1,0:T(8,128)(2,1)S(1)} collective-permute-done((bf16[128,1024]{1,0:T(8,128)(2,1)S(1)}, bf16[128,1024]{1,0:T(8,128)(2,1)S(1)}, u32[]{:S(2)}, u32[]{:S(2)}) %collective-permute-start.32) | collective-permute-done | bytes 262176 | tf_op jit(solution)/shard_map/ppermute | solution.py:315
  (69 shorter events, 17.1 us)
Async XLA Ops:
  0.6 59.8 %copy-start.2 = (bf16[1,384,2048]{2,1,0:T(8,128)(2,1)S(1)}, bf16[1,384,2048]{2,1,0:T(8,128)(2,1)}, u32[]{:S(2)}) copy-start(bf16[1,384,2048]{2,1,0:T(8,128)(2,1)} %param.13) | copy-start | bytes 4718596
  2.6 16.2 %collective-permute-start = (bf16[272,1024]{1,0:T(8,128)(2,1)}, bf16[272,1024]{1,0:T(8,128)(2,1)S(1)}, u32[]{:S(2)}, u32[]{:S(2)}) collective-permute-start(bf16[272,1024]{1,0:T(8,128)(2,1)} %pack.1.refs_0_), channel_id=1, source_target_pairs={{0,1},{1,0},{2,6},{3,7},{4,5},{5,4},{6,2},{7,3},{8,9},{9,8},{10,14... | collective-permute-start | bytes 1671176 | tf_op jit(solution)/shard_map/ppermute | solution.py:315
  5.6 14.0 %collective-permute-start.1 = (bf16[272,1024]{1,0:T(8,128)(2,1)}, bf16[272,1024]{1,0:T(8,128)(2,1)S(1)}, u32[]{:S(2)}, u32[]{:S(2)}) collective-permute-start(bf16[272,1024]{1,0:T(8,128)(2,1)} %pack.1.refs_0_), channel_id=1, source_target_pairs={{0,4},{1,5},{2,3},{3,2},{4,0},{5,1},{6,7},{7,6},{8,12},{9,13},{10,... | collective-permute-start | bytes 1671176 | tf_op jit(solution)/shard_map/ppermute | solution.py:315
  7.1 15.0 %collective-permute-start.2 = (bf16[272,1024]{1,0:T(8,128)(2,1)}, bf16[272,1024]{1,0:T(8,128)(2,1)}, u32[]{:S(2)}, u32[]{:S(2)}) collective-permute-start(bf16[272,1024]{1,0:T(8,128)(2,1)} %pack.1.refs_0_), channel_id=1, source_target_pairs={{0,8},{1,9},{2,10},{3,11},{4,12},{5,13},{6,14},{7,15},{8,24},{9,25... | collective-permute-start | bytes 1671176 | tf_op jit(solution)/shard_map/ppermute | solution.py:315
  18.8 0.8 copy-start.4
  22.1 15.8 %collective-permute-start.5 = (bf16[272,1024]{1,0:T(8,128)(2,1)}, bf16[272,1024]{1,0:T(8,128)(2,1)}, u32[]{:S(2)}, u32[]{:S(2)}) collective-permute-start(bf16[272,1024]{1,0:T(8,128)(2,1)} %collective-permute-done.2.refs_0_), channel_id=1, source_target_pairs={{0,4},{1,5},{2,3},{3,2},{4,0},{5,1},{6,7},{7,6},{8,12},{9,13},{10,... | collective-permute-start | bytes 1671176 | tf_op jit(solution)/shard_map/ppermute | solution.py:315
  22.7 15.3 %collective-permute-start.6 = (bf16[272,1024]{1,0:T(8,128)(2,1)}, bf16[272,1024]{1,0:T(8,128)(2,1)S(1)}, u32[]{:S(2)}, u32[]{:S(2)}) collective-permute-start(bf16[272,1024]{1,0:T(8,128)(2,1)} %collective-permute-done.2.refs_0_), channel_id=1, source_target_pairs={{0,8},{1,9},{2,10},{3,11},{4,12},{5,13},{6,14},{7,15},{8,24},{9,25... | collective-permute-start | bytes 1671176 | tf_op jit(solution)/shard_map/ppermute | solution.py:315
  23.4 14.6 %collective-permute-start.4 = (bf16[272,1024]{1,0:T(8,128)(2,1)S(1)}, bf16[272,1024]{1,0:T(8,128)(2,1)S(1)}, u32[]{:S(2)}, u32[]{:S(2)}) collective-permute-start(bf16[272,1024]{1,0:T(8,128)(2,1)S(1)} %collective-permute-done.1.refs_1_), channel_id=1, source_target_pairs={{0,1},{1,0},{2,6},{3,7},{4,5},{5,4},{6,2},{7,3},{8,9},{9,8},{10,14... | collective-permute-start | bytes 1671176 | tf_op jit(solution)/shard_map/ppermute | solution.py:315
  24.3 0.8 copy-start.6
  25.1 21.5 %collective-permute-start.3 = (bf16[272,1024]{1,0:T(8,128)(2,1)}, bf16[272,1024]{1,0:T(8,128)(2,1)}, u32[]{:S(2)}, u32[]{:S(2)}) collective-permute-start(bf16[272,1024]{1,0:T(8,128)(2,1)} %collective-permute-done.2.refs_0_), channel_id=1, source_target_pairs={{0,1},{1,0},{2,6},{3,7},{4,5},{5,4},{6,2},{7,3},{8,9},{9,8},{10,14... | collective-permute-start | bytes 1671176 | tf_op jit(solution)/shard_map/ppermute | solution.py:315
  38.0 0.8 copy-start.8
  38.8 9.5 %collective-permute-start.7 = (bf16[272,1024]{1,0:T(8,128)(2,1)S(1)}, bf16[272,1024]{1,0:T(8,128)(2,1)S(1)}, u32[]{:S(2)}, u32[]{:S(2)}) collective-permute-start(bf16[272,1024]{1,0:T(8,128)(2,1)S(1)} %collective-permute-done.6.refs_0_), channel_id=1, source_target_pairs={{0,1},{1,0},{2,6},{3,7},{4,5},{5,4},{6,2},{7,3},{8,9},{9,8},{10,14... | collective-permute-start | bytes 1671176 | tf_op jit(solution)/shard_map/ppermute | solution.py:315
  39.3 15.1 %collective-permute-start.8 = (bf16[272,1024]{1,0:T(8,128)(2,1)}, bf16[272,1024]{1,0:T(8,128)(2,1)}, u32[]{:S(2)}, u32[]{:S(2)}) collective-permute-start(bf16[272,1024]{1,0:T(8,128)(2,1)} %collective-permute-done.5.refs_1_), channel_id=1, source_target_pairs={{0,1},{1,0},{2,6},{3,7},{4,5},{5,4},{6,2},{7,3},{8,9},{9,8},{10,14... | collective-permute-start | bytes 1671176 | tf_op jit(solution)/shard_map/ppermute | solution.py:315
  40.8 13.6 %collective-permute-start.9 = (bf16[272,1024]{1,0:T(8,128)(2,1)S(1)}, bf16[272,1024]{1,0:T(8,128)(2,1)S(1)}, u32[]{:S(2)}, u32[]{:S(2)}) collective-permute-start(bf16[272,1024]{1,0:T(8,128)(2,1)S(1)} %collective-permute-done.6.refs_0_), channel_id=1, source_target_pairs={{0,8},{1,9},{2,10},{3,11},{4,12},{5,13},{6,14},{7,15},{8,24},{9,25... | collective-permute-start | bytes 1671176 | tf_op jit(solution)/shard_map/ppermute | solution.py:315
  40.9 1.1 copy-start.3
  41.9 1.1 copy-start.5
  43.0 1.1 copy-start.7
  44.0 1.1 copy-start.9
  45.1 15.3 %copy-start.1 = (bf16[1,384,2048]{2,1,0:T(8,128)(2,1)S(1)}, bf16[1,384,2048]{2,1,0:T(8,128)(2,1)}, u32[]{:S(2)}) copy-start(bf16[1,384,2048]{2,1,0:T(8,128)(2,1)} %param.12) | copy-start | bytes 4718596
  46.6 13.8 %copy-start = (bf16[1,384,2048]{2,1,0:T(8,128)(2,1)S(1)}, bf16[1,384,2048]{2,1,0:T(8,128)(2,1)}, u32[]{:S(2)}) copy-start(bf16[1,384,2048]{2,1,0:T(8,128)(2,1)} %param.11) | copy-start | bytes 4718596
  54.4 6.0 %collective-permute-start.13 = (bf16[2,144,2048]{2,1,0:T(8,128)(2,1)S(1)}, bf16[2,144,2048]{2,1,0:T(8,128)(2,1)S(1)}, u32[]{:S(2)}, u32[]{:S(2)}) collective-permute-start(bf16[2,144,2048]{2,1,0:T(8,128)(2,1)S(1)} %get-tuple-element.128), channel_id=1, source_target_pairs={{0,2},{1,3},{2,0},{3,1},{4,6},{5,7},{6,4},{7,5},{8,10},{9,11},{10,... | collective-permute-start | bytes 3538952 | tf_op jit(solution)/shard_map/ppermute | solution.py:315
  54.9 15.6 %collective-permute-start.11 = (bf16[272,1024]{1,0:T(8,128)(2,1)}, bf16[272,1024]{1,0:T(8,128)(2,1)S(1)}, u32[]{:S(2)}, u32[]{:S(2)}) collective-permute-start(bf16[272,1024]{1,0:T(8,128)(2,1)} %collective-permute-done.5.refs_1_), channel_id=1, source_target_pairs={{0,8},{1,9},{2,10},{3,11},{4,12},{5,13},{6,14},{7,15},{8,24},{9,25... | collective-permute-start | bytes 1671176 | tf_op jit(solution)/shard_map/ppermute | solution.py:315
  56.5 14.5 %collective-permute-start.10 = (bf16[272,1024]{1,0:T(8,128)(2,1)S(1)}, bf16[272,1024]{1,0:T(8,128)(2,1)S(1)}, u32[]{:S(2)}, u32[]{:S(2)}) collective-permute-start(bf16[272,1024]{1,0:T(8,128)(2,1)S(1)} %collective-permute-done.9.refs_0_), channel_id=1, source_target_pairs={{0,1},{1,0},{2,6},{3,7},{4,5},{5,4},{6,2},{7,3},{8,9},{9,8},{10,14... | collective-permute-start | bytes 1671176 | tf_op jit(solution)/shard_map/ppermute | solution.py:315
  57.1 13.8 %collective-permute-start.12 = (bf16[272,1024]{1,0:T(8,128)(2,1)S(1)}, bf16[272,1024]{1,0:T(8,128)(2,1)S(1)}, u32[]{:S(2)}, u32[]{:S(2)}) collective-permute-start(bf16[272,1024]{1,0:T(8,128)(2,1)S(1)} %collective-permute-done.9.refs_0_), channel_id=1, source_target_pairs={{0,4},{1,5},{2,3},{3,2},{4,0},{5,1},{6,7},{7,6},{8,12},{9,13},{10,... | collective-permute-start | bytes 1671176 | tf_op jit(solution)/shard_map/ppermute | solution.py:315
  70.9 5.0 %collective-permute-start.18 = (bf16[2,144,2048]{2,1,0:T(8,128)(2,1)S(1)}, bf16[2,144,2048]{2,1,0:T(8,128)(2,1)S(1)}, u32[]{:S(2)}, u32[]{:S(2)}) collective-permute-start(bf16[2,144,2048]{2,1,0:T(8,128)(2,1)S(1)} %get-tuple-element.144), channel_id=1, source_target_pairs={{0,2},{1,3},{2,0},{3,1},{4,6},{5,7},{6,4},{7,5},{8,10},{9,11},{10,... | collective-permute-start | bytes 3538952 | tf_op jit(solution)/shard_map/ppermute | solution.py:315
  70.9 3.7 %collective-permute-start.14 = (bf16[144,2048]{1,0:T(8,128)(2,1)S(1)}, bf16[144,2048]{1,0:T(8,128)(2,1)S(1)}, u32[]{:S(2)}, u32[]{:S(2)}) collective-permute-start(bf16[144,2048]{1,0:T(8,128)(2,1)S(1)} %get-tuple-element.136), channel_id=1, source_target_pairs={{0,2},{1,3},{2,0},{3,1},{4,6},{5,7},{6,4},{7,5},{8,10},{9,11},{10,... | collective-permute-start | bytes 1769480 | tf_op jit(solution)/shard_map/ppermute | solution.py:315
  71.5 9.5 %collective-permute-start.17 = (bf16[272,1024]{1,0:T(8,128)(2,1)S(1)}, bf16[272,1024]{1,0:T(8,128)(2,1)S(1)}, u32[]{:S(2)}, u32[]{:S(2)}) collective-permute-start(bf16[272,1024]{1,0:T(8,128)(2,1)S(1)} %collective-permute-done.11.refs_1_), channel_id=1, source_target_pairs={{0,1},{1,0},{2,6},{3,7},{4,5},{5,4},{6,2},{7,3},{8,9},{9,8},{10,14... | collective-permute-start | bytes 1671176 | tf_op jit(solution)/shard_map/ppermute | solution.py:315
  82.5 5.0 %collective-permute-start.20 = (bf16[2,144,2048]{2,1,0:T(8,128)(2,1)S(1)}, bf16[2,144,2048]{2,1,0:T(8,128)(2,1)S(1)}, u32[]{:S(2)}, u32[]{:S(2)}) collective-permute-start(bf16[2,144,2048]{2,1,0:T(8,128)(2,1)S(1)} %get-tuple-element.163), channel_id=1, source_target_pairs={{0,2},{1,3},{2,0},{3,1},{4,6},{5,7},{6,4},{7,5},{8,10},{9,11},{10,... | collective-permute-start | bytes 3538952 | tf_op jit(solution)/shard_map/ppermute | solution.py:315
  82.6 3.7 %collective-permute-start.19 = (bf16[144,2048]{1,0:T(8,128)(2,1)S(1)}, bf16[144,2048]{1,0:T(8,128)(2,1)S(1)}, u32[]{:S(2)}, u32[]{:S(2)}) collective-permute-start(bf16[144,2048]{1,0:T(8,128)(2,1)S(1)} %get-tuple-element.160), channel_id=1, source_target_pairs={{0,2},{1,3},{2,0},{3,1},{4,6},{5,7},{6,4},{7,5},{8,10},{9,11},{10,... | collective-permute-start | bytes 1769480 | tf_op jit(solution)/shard_map/ppermute | solution.py:315
  83.1 9.6 %collective-permute-start.16 = (bf16[272,1024]{1,0:T(8,128)(2,1)S(1)}, bf16[272,1024]{1,0:T(8,128)(2,1)S(1)}, u32[]{:S(2)}, u32[]{:S(2)}) collective-permute-start(bf16[272,1024]{1,0:T(8,128)(2,1)S(1)} %collective-permute-done.12.refs_1_), channel_id=1, source_target_pairs={{0,1},{1,0},{2,6},{3,7},{4,5},{5,4},{6,2},{7,3},{8,9},{9,8},{10,14... | collective-permute-start | bytes 1671176 | tf_op jit(solution)/shard_map/ppermute | solution.py:315
  94.2 6.0 %collective-permute-start.22 = (bf16[2,144,2048]{2,1,0:T(8,128)(2,1)S(1)}, bf16[2,144,2048]{2,1,0:T(8,128)(2,1)S(1)}, u32[]{:S(2)}, u32[]{:S(2)}) collective-permute-start(bf16[2,144,2048]{2,1,0:T(8,128)(2,1)S(1)} %get-tuple-element.179), channel_id=1, source_target_pairs={{0,2},{1,3},{2,0},{3,1},{4,6},{5,7},{6,4},{7,5},{8,10},{9,11},{10,... | collective-permute-start | bytes 3538952 | tf_op jit(solution)/shard_map/ppermute | solution.py:315
  94.4 3.6 %collective-permute-start.21 = (bf16[144,2048]{1,0:T(8,128)(2,1)S(1)}, bf16[144,2048]{1,0:T(8,128)(2,1)S(1)}, u32[]{:S(2)}, u32[]{:S(2)}) collective-permute-start(bf16[144,2048]{1,0:T(8,128)(2,1)S(1)} %get-tuple-element.176), channel_id=1, source_target_pairs={{0,2},{1,3},{2,0},{3,1},{4,6},{5,7},{6,4},{7,5},{8,10},{9,11},{10,... | collective-permute-start | bytes 1769480 | tf_op jit(solution)/shard_map/ppermute | solution.py:315
  94.7 10.9 %collective-permute-start.27 = (bf16[2,128,1024]{2,1,0:T(8,128)(2,1)S(1)}, bf16[2,128,1024]{2,1,0:T(8,128)(2,1)S(1)}, u32[]{:S(2)}, u32[]{:S(2)}) collective-permute-start(bf16[2,128,1024]{2,1,0:T(8,128)(2,1)S(1)} %get-tuple-element.161), channel_id=1, source_target_pairs={{0,1},{1,0},{2,6},{3,7},{4,5},{5,4},{6,2},{7,3},{8,9},{9,8},{10,14... | collective-permute-start | bytes 1572872 | tf_op jit(solution)/shard_map/ppermute | solution.py:315
  95.6 14.9 %collective-permute-start.15 = (bf16[2,128,1024]{2,1,0:T(8,128)(2,1)S(1)}, bf16[2,128,1024]{2,1,0:T(8,128)(2,1)S(1)}, u32[]{:S(2)}, u32[]{:S(2)}) collective-permute-start(bf16[2,128,1024]{2,1,0:T(8,128)(2,1)S(1)} %get-tuple-element.138), channel_id=1, source_target_pairs={{0,1},{1,0},{2,6},{3,7},{4,5},{5,4},{6,2},{7,3},{8,9},{9,8},{10,14... | collective-permute-start | bytes 1572872 | tf_op jit(solution)/shard_map/ppermute | solution.py:315
  99.2 18.8 %collective-permute-start.25 = (bf16[2,128,1024]{2,1,0:T(8,128)(2,1)S(1)}, bf16[2,128,1024]{2,1,0:T(8,128)(2,1)S(1)}, u32[]{:S(2)}, u32[]{:S(2)}) collective-permute-start(bf16[2,128,1024]{2,1,0:T(8,128)(2,1)S(1)} %get-tuple-element.177), channel_id=1, source_target_pairs={{0,1},{1,0},{2,6},{3,7},{4,5},{5,4},{6,2},{7,3},{8,9},{9,8},{10,14... | collective-permute-start | bytes 1572872 | tf_op jit(solution)/shard_map/ppermute | solution.py:315
  105.1 5.7 %collective-permute-start.23 = (bf16[144,2048]{1,0:T(8,128)(2,1)S(1)}, bf16[144,2048]{1,0:T(8,128)(2,1)S(1)}, u32[]{:S(2)}, u32[]{:S(2)}) collective-permute-start(bf16[144,2048]{1,0:T(8,128)(2,1)S(1)} %get-tuple-element.188), channel_id=1, source_target_pairs={{0,2},{1,3},{2,0},{3,1},{4,6},{5,7},{6,4},{7,5},{8,10},{9,11},{10,... | collective-permute-start | bytes 1769480 | tf_op jit(solution)/shard_map/ppermute | solution.py:315
  105.8 9.3 %collective-permute-start.28 = (bf16[128,1024]{1,0:T(8,128)(2,1)S(1)}, bf16[128,1024]{1,0:T(8,128)(2,1)S(1)}, u32[]{:S(2)}, u32[]{:S(2)}) collective-permute-start(bf16[128,1024]{1,0:T(8,128)(2,1)S(1)} %fusion.16), channel_id=1, source_target_pairs={{0,4},{1,5},{2,3},{3,2},{4,0},{5,1},{6,7},{7,6},{8,12},{9,13},{10,... | collective-permute-start | bytes 786440 | tf_op jit(solution)/shard_map/ppermute | solution.py:315
  112.0 16.3 %collective-permute-start.24 = (bf16[2,128,1024]{2,1,0:T(8,128)(2,1)S(1)}, bf16[2,128,1024]{2,1,0:T(8,128)(2,1)S(1)}, u32[]{:S(2)}, u32[]{:S(2)}) collective-permute-start(bf16[2,128,1024]{2,1,0:T(8,128)(2,1)S(1)} %get-tuple-element.190), channel_id=1, source_target_pairs={{0,1},{1,0},{2,6},{3,7},{4,5},{5,4},{6,2},{7,3},{8,9},{9,8},{10,14... | collective-permute-start | bytes 1572872 | tf_op jit(solution)/shard_map/ppermute | solution.py:315
  115.2 8.3 %collective-permute-start.29 = (bf16[128,1024]{1,0:T(8,128)(2,1)S(1)}, bf16[128,1024]{1,0:T(8,128)(2,1)S(1)}, u32[]{:S(2)}, u32[]{:S(2)}) collective-permute-start(bf16[128,1024]{1,0:T(8,128)(2,1)S(1)} %fusion.7), channel_id=1, source_target_pairs={{0,8},{1,9},{2,10},{3,11},{4,12},{5,13},{6,14},{7,15},{8,24},{9,25... | collective-permute-start | bytes 786440 | tf_op jit(solution)/shard_map/ppermute | solution.py:315
  118.2 7.4 %collective-permute-start.26 = (bf16[128,1024]{1,0:T(8,128)(2,1)S(1)}, bf16[128,1024]{1,0:T(8,128)(2,1)S(1)}, u32[]{:S(2)}, u32[]{:S(2)}) collective-permute-start(bf16[128,1024]{1,0:T(8,128)(2,1)S(1)} %fusion.15), channel_id=1, source_target_pairs={{0,4},{1,5},{2,3},{3,2},{4,0},{5,1},{6,7},{7,6},{8,12},{9,13},{10,... | collective-permute-start | bytes 786440 | tf_op jit(solution)/shard_map/ppermute | solution.py:315
  125.7 9.5 %collective-permute-start.31 = (bf16[128,1024]{1,0:T(8,128)(2,1)S(1)}, bf16[128,1024]{1,0:T(8,128)(2,1)S(1)}, u32[]{:S(2)}, u32[]{:S(2)}) collective-permute-start(bf16[128,1024]{1,0:T(8,128)(2,1)S(1)} %fusion.10), channel_id=1, source_target_pairs={{0,8},{1,9},{2,10},{3,11},{4,12},{5,13},{6,14},{7,15},{8,24},{9,25... | collective-permute-start | bytes 786440 | tf_op jit(solution)/shard_map/ppermute | solution.py:315
  128.6 6.6 %collective-permute-start.30 = (bf16[128,1024]{1,0:T(8,128)(2,1)S(1)}, bf16[128,1024]{1,0:T(8,128)(2,1)S(1)}, u32[]{:S(2)}, u32[]{:S(2)}) collective-permute-start(bf16[128,1024]{1,0:T(8,128)(2,1)S(1)} %fusion.17), channel_id=1, source_target_pairs={{0,4},{1,5},{2,3},{3,2},{4,0},{5,1},{6,7},{7,6},{8,12},{9,13},{10,... | collective-permute-start | bytes 786440 | tf_op jit(solution)/shard_map/ppermute | solution.py:315
  135.3 8.7 %collective-permute-start.33 = (bf16[128,1024]{1,0:T(8,128)(2,1)S(1)}, bf16[128,1024]{1,0:T(8,128)(2,1)S(1)}, u32[]{:S(2)}, u32[]{:S(2)}) collective-permute-start(bf16[128,1024]{1,0:T(8,128)(2,1)S(1)} %fusion.5), channel_id=1, source_target_pairs={{0,8},{1,9},{2,10},{3,11},{4,12},{5,13},{6,14},{7,15},{8,24},{9,25... | collective-permute-start | bytes 786440 | tf_op jit(solution)/shard_map/ppermute | solution.py:315
  137.1 6.4 %collective-permute-start.32 = (bf16[128,1024]{1,0:T(8,128)(2,1)S(1)}, bf16[128,1024]{1,0:T(8,128)(2,1)S(1)}, u32[]{:S(2)}, u32[]{:S(2)}) collective-permute-start(bf16[128,1024]{1,0:T(8,128)(2,1)S(1)} %fusion.14), channel_id=1, source_target_pairs={{0,4},{1,5},{2,3},{3,2},{4,0},{5,1},{6,7},{7,6},{8,12},{9,13},{10,... | collective-permute-start | bytes 786440 | tf_op jit(solution)/shard_map/ppermute | solution.py:315

commit v18 on v17

--- a/solution.py
+++ b/solution.py
@@ -375,10 +375,10 @@
         )
         have.update(zip(listed, values))
     mark = []
+    first_out = None
     if before is not None:
-        keep, send = placed(*before)
-        late.append((keep, to_second(send)))
-        mark.append(send)
+        first_out = placed(*before)
+        mark.append(first_out[1])
     if parts is not None:
         mark.append(parts[1])
     while done < chunks:
@@ -393,6 +393,8 @@
         done += 1
     keep, send = placed(*parts)
     late.append((keep, to_second(send)))
+    if first_out is not None:
+        late.insert(0, (first_out[0], to_second(tied(first_out[1], send))))
     marks = [send] * (chunks + 2)
     running, previous = None, send
     for c in range(1, chunks):
@@ -408,7 +410,7 @@
         if c + 1 < chunks:
             running = to_ring(running)
     keep, came = late[0]
-    pair = added(keep, tied(came, near))
+    pair = added(keep, came)
     came = pair[1].astype(jnp.bfloat16)
     own = added(pair[0], to_first(came if running is None else tied(came, running)))
     grad_tokens = (own if running is None else added(own, to_ring(running))).astype(jnp.bfloat16)

time: 145 us -> 145 us (level)
  starting transfers between devices: 32.5 us -> 30.6 us
  waiting for transfers between devices: 58.7 us -> 60.3 us
    ppermute x34, starting transfers between devices: 32.5 us -> 30.6 us  [permute(): return lax.ppermute(value, ('expert', 'etp'), pairs)]
    ppermute x34, waiting for transfers between devices: 58.7 us -> 60.3 us  [permute(): return lax.ppermute(value, ('expert', 'etp'), pairs)]
where the time goes in v18:
time: 145 us
  waiting for transfers between devices  60.3 us (42%)
  Pallas kernels  33.8 us (23%)
  starting transfers between devices  30.6 us (21%)
  matrix products  10.2 us (7%)
  local copies, waits for them, and re-layouts  6.76 us (5%)
  other arithmetic  1.78 us (1%)
    ppermute x34, waiting for transfers between devices, permute(): return lax.ppermute(value, ('expert', 'etp'), pairs)  60.3 us
    ppermute x34, starting transfers between devices, permute(): return lax.ppermute(value, ('expert', 'etp'), pairs)  30.6 us
    pallas_call x4, Pallas kernels, run_experts(): pl.pallas_call(functools.partial(expert_kernel, index, kept is not None),...  19.7 us
    pallas_call x4, Pallas kernels, pick_rows(): pl.pallas_call(functools.partial(pick_kernel, top, rows), in_specs=[pl.Bl...  7.05 us
    unnamed x20, local copies, waits for them, and re-layouts  6.63 us
    pallas_call x4, Pallas kernels, place_rows(): pl.pallas_call(place_kernel, in_specs=[pl.BlockSpec(memory_space=pltpu.SM...  5.08 us
    dot_general x1, matrix products, gather_body(): lax.dot_general(acts, rows_g, CONTRACT_FIRST, preferred_element_type=jnp....  3.42 us
    dot_general x1, matrix products, gather_body(): lax.dot_general(up_term, rows_x, CONTRACT_FIRST, preferred_element_type=j...  3.42 us
  transfers between devices with their start and end apart: 34, of which 19 were waited for; matrix products, arithmetic and copies ran while one was open for 8% of the time, Pallas kernels for 20%

profile of v18, /device:TPU:0, one launch (start us, length us, event | category | flops | bytes accessed | tf_op | source)
XLA Modules:
  0.0 144.5 jit_solution(1343043154655043550)
XLA Ops:
  0.6 2.0 %pack.1.refs_0_ = bf16[272,1024]{1,0:T(8,128)(2,1)} custom-call(bf16[128,1024]{1,0:T(8,128)(2,1)} %tokens_ref.1, bf16[128,1024]{1,0:T(8,128)(2,1)} %grads_ref.1, s32[8,128]{1,0:T(8,128)} %bitcast.70, f32[8,128]{1,0:T(8,128)} %bitcast.71), custom_call_target="tpu_custom_call" | custom-call | tf_op jit(solution)/shard_map/pack/pallas_call | solution.py:128
  2.6 2.9 %collective-permute-start = (bf16[272,1024]{1,0:T(8,128)(2,1)}, bf16[272,1024]{1,0:T(8,128)(2,1)S(1)}, u32[]{:S(2)}, u32[]{:S(2)}) collective-permute-start(bf16[272,1024]{1,0:T(8,128)(2,1)} %pack.1.refs_0_), channel_id=1, source_target_pairs={{0,1},{1,0},{2,6},{3,7},{4,5},{5,4},{6,2},{7,3},{8,9},{9,8},{10,14... | collective-permute-start | bytes 1671176 | tf_op jit(solution)/shard_map/ppermute | solution.py:315
  5.6 1.5 %collective-permute-start.1 = (bf16[272,1024]{1,0:T(8,128)(2,1)}, bf16[272,1024]{1,0:T(8,128)(2,1)S(1)}, u32[]{:S(2)}, u32[]{:S(2)}) collective-permute-start(bf16[272,1024]{1,0:T(8,128)(2,1)} %pack.1.refs_0_), channel_id=1, source_target_pairs={{0,4},{1,5},{2,3},{3,2},{4,0},{5,1},{6,7},{7,6},{8,12},{9,13},{10,... | collective-permute-start | bytes 1671176 | tf_op jit(solution)/shard_map/ppermute | solution.py:315
  7.1 1.6 %collective-permute-start.2 = (bf16[272,1024]{1,0:T(8,128)(2,1)}, bf16[272,1024]{1,0:T(8,128)(2,1)}, u32[]{:S(2)}, u32[]{:S(2)}) collective-permute-start(bf16[272,1024]{1,0:T(8,128)(2,1)} %pack.1.refs_0_), channel_id=1, source_target_pairs={{0,8},{1,9},{2,10},{3,11},{4,12},{5,13},{6,14},{7,15},{8,24},{9,25... | collective-permute-start | bytes 1671176 | tf_op jit(solution)/shard_map/ppermute | solution.py:315
  8.7 10.1 %collective-permute-done.refs_2_ = bf16[272,1024]{1,0:T(8,128)(2,1)S(1)} collective-permute-done((bf16[272,1024]{1,0:T(8,128)(2,1)}, bf16[272,1024]{1,0:T(8,128)(2,1)S(1)}, u32[]{:S(2)}, u32[]{:S(2)}) %collective-permute-start) | collective-permute-done | bytes 557088 | tf_op jit(solution)/shard_map/ppermute | solution.py:315
  19.6 2.5 %collective-permute-done.2.refs_0_ = bf16[272,1024]{1,0:T(8,128)(2,1)} collective-permute-done((bf16[272,1024]{1,0:T(8,128)(2,1)}, bf16[272,1024]{1,0:T(8,128)(2,1)}, u32[]{:S(2)}, u32[]{:S(2)}) %collective-permute-start.2) | collective-permute-done | bytes 557088 | tf_op jit(solution)/shard_map/ppermute | solution.py:315
  25.1 1.1 collective-permute-start.3
  26.2 11.7 %collective-permute-done.5.refs_1_ = bf16[272,1024]{1,0:T(8,128)(2,1)} collective-permute-done((bf16[272,1024]{1,0:T(8,128)(2,1)}, bf16[272,1024]{1,0:T(8,128)(2,1)}, u32[]{:S(2)}, u32[]{:S(2)}) %collective-permute-start.5) | collective-permute-done | bytes 557088 | tf_op jit(solution)/shard_map/ppermute | solution.py:315
  39.3 1.5 %collective-permute-start.8 = (bf16[272,1024]{1,0:T(8,128)(2,1)}, bf16[272,1024]{1,0:T(8,128)(2,1)}, u32[]{:S(2)}, u32[]{:S(2)}) collective-permute-start(bf16[272,1024]{1,0:T(8,128)(2,1)} %collective-permute-done.5.refs_1_), channel_id=1, source_target_pairs={{0,1},{1,0},{2,6},{3,7},{4,5},{5,4},{6,2},{7,3},{8,9},{9,8},{10,14... | collective-permute-start | bytes 1671176 | tf_op jit(solution)/shard_map/ppermute | solution.py:315
  40.9 1.1 copy-done.3
  41.9 1.1 copy-done.5
  43.0 1.1 copy-done.7
  44.0 1.1 copy-done.9
  45.1 1.5 %pick.4 = (bf16[2,144,2048]{2,1,0:T(8,128)(2,1)S(1)}, bf16[2,144,2048]{2,1,0:T(8,128)(2,1)S(1)}, bf16[288,256]{1,0:T(8,128)(2,1)S(1)}) custom-call(s32[3]{0:T(128)S(1)} %pad_add_fusion.place_ref, bf16[272,1024]{1,0:T(8,128)(2,1)S(1)} %copy-done.3, bf16[272,1024]{1,0:T(8,128)(2,1)S(1)} %copy-done.7, bf16[272,1024]{1,0:T(8,128)(2,1)S(1)} %copy-done.5, ...), custom_call_target="tpu_custom_call" | custom-call | tf_op jit(solution)/shard_map/pick/pallas_call | solution.py:251
  46.6 1.7 %collective-permute-done.7.refs_2_ = bf16[272,1024]{1,0:T(8,128)(2,1)S(1)} collective-permute-done((bf16[272,1024]{1,0:T(8,128)(2,1)S(1)}, bf16[272,1024]{1,0:T(8,128)(2,1)S(1)}, u32[]{:S(2)}, u32[]{:S(2)}) %collective-permute-start.7) | collective-permute-done | bytes 557088 | tf_op jit(solution)/shard_map/ppermute | solution.py:315
  48.3 6.1 %collective-permute-done.8.refs_3_ = bf16[272,1024]{1,0:T(8,128)(2,1)} collective-permute-done((bf16[272,1024]{1,0:T(8,128)(2,1)}, bf16[272,1024]{1,0:T(8,128)(2,1)}, u32[]{:S(2)}, u32[]{:S(2)}) %collective-permute-start.8) | collective-permute-done | bytes 557088 | tf_op jit(solution)/shard_map/ppermute | solution.py:315
  54.9 1.6 %collective-permute-start.11 = (bf16[272,1024]{1,0:T(8,128)(2,1)}, bf16[272,1024]{1,0:T(8,128)(2,1)S(1)}, u32[]{:S(2)}, u32[]{:S(2)}) collective-permute-start(bf16[272,1024]{1,0:T(8,128)(2,1)} %collective-permute-done.5.refs_1_), channel_id=1, source_target_pairs={{0,8},{1,9},{2,10},{3,11},{4,12},{5,13},{6,14},{7,15},{8,24},{9,25... | collective-permute-start | bytes 1671176 | tf_op jit(solution)/shard_map/ppermute | solution.py:315
  57.8 2.5 %pick.5 = (bf16[2,144,2048]{2,1,0:T(8,128)(2,1)S(1)}, bf16[2,144,2048]{2,1,0:T(8,128)(2,1)S(1)}, bf16[288,256]{1,0:T(8,128)(2,1)S(1)}) custom-call(s32[3]{0:T(128)S(1)} %pad_add_fusion.place_ref, bf16[272,1024]{1,0:T(8,128)(2,1)} %collective-permute-done.2.refs_0_, bf16[272,1024]{1,0:T(8,128)(2,1)} %collective-permute-done.5.refs_1_, ...), custom_call_target="tpu_custom_call" | custom-call | tf_op jit(solution)/shard_map/pick/pallas_call | solution.py:251
  60.4 4.9 %experts.4 = (bf16[144,2048]{1,0:T(8,128)(2,1)S(1)}, bf16[144,2048]{1,0:T(8,128)(2,1)S(1)}, bf16[1152,2048]{1,0:T(8,128)(2,1)S(1)}, bf16[1152,2048]{1,0:T(8,128)...) custom-call(bf16[2,144,2048]{2,1,0:T(8,128)(2,1)S(1)} %get-tuple-element.127., ...), custom_call_target="tpu_custom_call" | custom-call | tf_op jit(solution)/shard_map/experts/pallas_call | solution.py:270
  65.3 5.3 %collective-permute-done.11.refs_1_ = bf16[272,1024]{1,0:T(8,128)(2,1)S(1)} collective-permute-done((bf16[272,1024]{1,0:T(8,128)(2,1)}, bf16[272,1024]{1,0:T(8,128)(2,1)S(1)}, u32[]{:S(2)}, u32[]{:S(2)}) %collective-permute-start.11) | collective-permute-done | bytes 557088 | tf_op jit(solution)/shard_map/ppermute | solution.py:315
  72.3 2.3 %collective-permute-done.14.far_ref = bf16[144,2048]{1,0:T(8,128)(2,1)S(1)} collective-permute-done((bf16[144,2048]{1,0:T(8,128)(2,1)S(1)}, bf16[144,2048]{1,0:T(8,128)(2,1)S(1)}, u32[]{:S(2)}, u32[]{:S(2)}) %collective-permute-start.14) | collective-permute-done | bytes 589856 | tf_op jit(solution)/shard_map/ppermute | solution.py:315
  74.6 1.3 place.4
  75.9 4.9 %experts.5 = (bf16[144,2048]{1,0:T(8,128)(2,1)S(1)}, bf16[144,2048]{1,0:T(8,128)(2,1)S(1)}, bf16[1152,2048]{1,0:T(8,128)(2,1)S(1)}, bf16[1152,2048]{1,0:T(8,128)...) custom-call(bf16[2,144,2048]{2,1,0:T(8,128)(2,1)S(1)} %get-tuple-ele, ...), custom_call_target="tpu_custom_call", output_to_operand_aliasing={{2}: (5, {}), {3}: (6, {}), {4}: (7, {}), {5}: (8, {}), {6}... | custom-call | tf_op jit(solution)/shard_map/experts/pallas_call | solution.py:270
  81.0 1.5 %pick.6 = (bf16[2,144,2048]{2,1,0:T(8,128)(2,1)S(1)}, bf16[2,144,2048]{2,1,0:T(8,128)(2,1)S(1)}, bf16[288,256]{1,0:T(8,128)(2,1)S(1)}) custom-call(s32[3]{0:T(128)S(1)} %pad_add_fusion.place_ref, bf16[272,1024]{1,0:T(8,128)(2,1)S(1)} %collective-permute-done.6.refs_0_, bf16[272,1024]{1,0:T(8,128)(2,1)S(1)} %collective-permute-done.11.refs_1_, ...), custom_call_target="tpu_custom_call" | custom-call | tf_op jit(solution)/shard_map/pick/pallas_call | solution.py:251
  84.0 2.3 %collective-permute-done.18.far_ref = bf16[144,2048]{1,0:T(8,128)(2,1)S(1)} collective-permute-done((bf16[144,2048]{1,0:T(8,128)(2,1)S(1)}, bf16[144,2048]{1,0:T(8,128)(2,1)S(1)}, u32[]{:S(2)}, u32[]{:S(2)}) %collective-permute-start.18) | collective-permute-done | bytes 589856 | tf_op jit(solution)/shard_map/ppermute | solution.py:315
  86.3 1.3 place.5
  87.6 5.1 %experts.6 = (bf16[144,2048]{1,0:T(8,128)(2,1)S(1)}, bf16[144,2048]{1,0:T(8,128)(2,1)S(1)}, bf16[1152,2048]{1,0:T(8,128)(2,1)S(1)}, bf16[1152,2048]{1,0:T(8,128)...) custom-call(bf16[2,144,2048]{2,1,0:T(8,128)(2,1)S(1)} %get-tuple-ele, ...), custom_call_target="tpu_custom_call", output_to_operand_aliasing={{2}: (5, {}), {3}: (6, {}), {4}: (7, {}), {5}: (8, {}), {6}... | custom-call | tf_op jit(solution)/shard_map/experts/pallas_call | solution.py:270
  92.7 1.5 %pick.7 = (bf16[2,144,2048]{2,1,0:T(8,128)(2,1)S(1)}, bf16[2,144,2048]{2,1,0:T(8,128)(2,1)S(1)}, bf16[288,256]{1,0:T(8,128)(2,1)S(1)}) custom-call(s32[3]{0:T(128)S(1)} %pad_add_fusion.place_ref, bf16[272,1024]{1,0:T(8,128)(2,1)S(1)} %collective-permute-done.9.refs_0_, bf16[272,1024]{1,0:T(8,128)(2,1)S(1)} %collective-permute-done.12.refs_1_, ...), custom_call_target="tpu_custom_call" | custom-call | tf_op jit(solution)/shard_map/pick/pallas_call | solution.py:251
  94.7 0.9 collective-permute-start.27
  95.6 2.3 %collective-permute-done.20.far_ref = bf16[144,2048]{1,0:T(8,128)(2,1)S(1)} collective-permute-done((bf16[144,2048]{1,0:T(8,128)(2,1)S(1)}, bf16[144,2048]{1,0:T(8,128)(2,1)S(1)}, u32[]{:S(2)}, u32[]{:S(2)}) %collective-permute-start.20) | collective-permute-done | bytes 589856 | tf_op jit(solution)/shard_map/ppermute | solution.py:315
  97.9 1.3 place.6
  99.2 0.9 collective-permute-start.25
  100.2 4.9 %experts.7 = (bf16[144,2048]{1,0:T(8,128)(2,1)S(1)}, bf16[144,2048]{1,0:T(8,128)(2,1)S(1)}, bf16[1152,2048]{1,0:T(8,128)(2,1)S(1)}, bf16[1152,2048]{1,0:T(8,128)...) custom-call(bf16[2,144,2048]{2,1,0:T(8,128)(2,1)S(1)} %get-tuple-ele, ...), custom_call_target="tpu_custom_call", output_to_operand_aliasing={{2}: (5, {}), {3}: (6, {}), {4}: (7, {}), {5}: (8, {}), {6}... | custom-call | tf_op jit(solution)/shard_map/experts/pallas_call | solution.py:270
  105.8 0.9 collective-permute-start.28
  107.2 1.3 place.7
  108.5 1.1 collective-permute-start.24
  109.6 3.3 %collective-permute-done.28 = bf16[128,1024]{1,0:T(8,128)(2,1)S(1)} collective-permute-done((bf16[128,1024]{1,0:T(8,128)(2,1)S(1)}, bf16[128,1024]{1,0:T(8,128)(2,1)S(1)}, u32[]{:S(2)}, u32[]{:S(2)}) %collective-permute-start.28) | collective-permute-done | bytes 262176 | tf_op jit(solution)/shard_map/ppermute | solution.py:315
  113.0 1.9 %collective-permute-start.29 = (bf16[128,1024]{1,0:T(8,128)(2,1)S(1)}, bf16[128,1024]{1,0:T(8,128)(2,1)S(1)}, u32[]{:S(2)}, u32[]{:S(2)}) collective-permute-start(bf16[128,1024]{1,0:T(8,128)(2,1)S(1)} %fusion.7), channel_id=1, source_target_pairs={{0,8},{1,9},{2,10},{3,11},{4,12},{5,13},{6,14},{7,15},{8,24},{9,25... | collective-permute-start | bytes 786440 | tf_op jit(solution)/shard_map/ppermute | solution.py:315
  115.1 1.4 collective-permute-start.26
  117.1 3.4 %fusion.2 = bf16[1,384,2048]{2,1,0:T(8,128)(2,1)} fusion(bf16[1152,384]{1,0:T(8,128)(2,1)S(1)} %get-tuple-element.204, bf16[1152,2048]{1,0:T(8,128)(2,1)S(1)} %get-tuple-element.205), kind=kOutput, calls=%fused_computation.5 | convolution fusion | flops 1812725760 | bytes 7176192 | tf_op jit(solution)/shard_map/dot_general | solution.py:419
  120.5 1.3 collective-permute-done.29
  121.8 2.5 %collective-permute-done.26 = bf16[128,1024]{1,0:T(8,128)(2,1)S(1)} collective-permute-done((bf16[128,1024]{1,0:T(8,128)(2,1)S(1)}, bf16[128,1024]{1,0:T(8,128)(2,1)S(1)}, u32[]{:S(2)}, u32[]{:S(2)}) %collective-permute-start.26) | collective-permute-done | bytes 262176 | tf_op jit(solution)/shard_map/ppermute | solution.py:315
  124.4 1.3 collective-permute-start.31
  125.7 3.4 %fusion = bf16[1,384,2048]{2,1,0:T(8,128)(2,1)} fusion(bf16[1152,384]{1,0:T(8,128)(2,1)S(1)} %get-tuple-element.199, bf16[1152,2048]{1,0:T(8,128)(2,1)S(1)} %get-tuple-element.200), kind=kOutput, calls=%fused_computation.3 | convolution fusion | flops 1812725760 | bytes 7176192 | tf_op jit(solution)/shard_map/dot_general | solution.py:420
  129.3 1.4 collective-permute-start.30
  131.8 4.0 %collective-permute-done.30 = bf16[128,1024]{1,0:T(8,128)(2,1)S(1)} collective-permute-done((bf16[128,1024]{1,0:T(8,128)(2,1)S(1)}, bf16[128,1024]{1,0:T(8,128)(2,1)S(1)}, u32[]{:S(2)}, u32[]{:S(2)}) %collective-permute-start.30) | collective-permute-done | bytes 262176 | tf_op jit(solution)/shard_map/ppermute | solution.py:315
  137.3 3.4 %fusion.1 = bf16[1,384,2048]{2,1,0:T(8,128)(2,1)} fusion(bf16[1152,384]{1,0:T(8,128)(2,1)S(1)} %get-tuple-element.202, bf16[1152,2048]{1,0:T(8,128)(2,1)S(1)} %get-tuple-element.200), kind=kOutput, calls=%fused_computation.4 | convolution fusion | flops 1812725760 | bytes 7176192 | tf_op jit(solution)/shard_map/dot_general | solution.py:421
  140.8 2.1 %collective-permute-done.32 = bf16[128,1024]{1,0:T(8,128)(2,1)S(1)} collective-permute-done((bf16[128,1024]{1,0:T(8,128)(2,1)S(1)}, bf16[128,1024]{1,0:T(8,128)(2,1)S(1)}, u32[]{:S(2)}, u32[]{:S(2)}) %collective-permute-start.32) | collective-permute-done | bytes 262176 | tf_op jit(solution)/shard_map/ppermute | solution.py:315
  (69 shorter events, 17.8 us)
Async XLA Ops:
  0.6 59.8 %copy-start.2 = (bf16[1,384,2048]{2,1,0:T(8,128)(2,1)S(1)}, bf16[1,384,2048]{2,1,0:T(8,128)(2,1)}, u32[]{:S(2)}) copy-start(bf16[1,384,2048]{2,1,0:T(8,128)(2,1)} %param.13) | copy-start | bytes 4718596
  2.6 16.2 %collective-permute-start = (bf16[272,1024]{1,0:T(8,128)(2,1)}, bf16[272,1024]{1,0:T(8,128)(2,1)S(1)}, u32[]{:S(2)}, u32[]{:S(2)}) collective-permute-start(bf16[272,1024]{1,0:T(8,128)(2,1)} %pack.1.refs_0_), channel_id=1, source_target_pairs={{0,1},{1,0},{2,6},{3,7},{4,5},{5,4},{6,2},{7,3},{8,9},{9,8},{10,14... | collective-permute-start | bytes 1671176 | tf_op jit(solution)/shard_map/ppermute | solution.py:315
  5.6 14.0 %collective-permute-start.1 = (bf16[272,1024]{1,0:T(8,128)(2,1)}, bf16[272,1024]{1,0:T(8,128)(2,1)S(1)}, u32[]{:S(2)}, u32[]{:S(2)}) collective-permute-start(bf16[272,1024]{1,0:T(8,128)(2,1)} %pack.1.refs_0_), channel_id=1, source_target_pairs={{0,4},{1,5},{2,3},{3,2},{4,0},{5,1},{6,7},{7,6},{8,12},{9,13},{10,... | collective-permute-start | bytes 1671176 | tf_op jit(solution)/shard_map/ppermute | solution.py:315
  7.1 15.0 %collective-permute-start.2 = (bf16[272,1024]{1,0:T(8,128)(2,1)}, bf16[272,1024]{1,0:T(8,128)(2,1)}, u32[]{:S(2)}, u32[]{:S(2)}) collective-permute-start(bf16[272,1024]{1,0:T(8,128)(2,1)} %pack.1.refs_0_), channel_id=1, source_target_pairs={{0,8},{1,9},{2,10},{3,11},{4,12},{5,13},{6,14},{7,15},{8,24},{9,25... | collective-permute-start | bytes 1671176 | tf_op jit(solution)/shard_map/ppermute | solution.py:315
  18.8 0.8 copy-start.4
  22.1 15.8 %collective-permute-start.5 = (bf16[272,1024]{1,0:T(8,128)(2,1)}, bf16[272,1024]{1,0:T(8,128)(2,1)}, u32[]{:S(2)}, u32[]{:S(2)}) collective-permute-start(bf16[272,1024]{1,0:T(8,128)(2,1)} %collective-permute-done.2.refs_0_), channel_id=1, source_target_pairs={{0,4},{1,5},{2,3},{3,2},{4,0},{5,1},{6,7},{7,6},{8,12},{9,13},{10,... | collective-permute-start | bytes 1671176 | tf_op jit(solution)/shard_map/ppermute | solution.py:315
  22.7 15.3 %collective-permute-start.6 = (bf16[272,1024]{1,0:T(8,128)(2,1)}, bf16[272,1024]{1,0:T(8,128)(2,1)S(1)}, u32[]{:S(2)}, u32[]{:S(2)}) collective-permute-start(bf16[272,1024]{1,0:T(8,128)(2,1)} %collective-permute-done.2.refs_0_), channel_id=1, source_target_pairs={{0,8},{1,9},{2,10},{3,11},{4,12},{5,13},{6,14},{7,15},{8,24},{9,25... | collective-permute-start | bytes 1671176 | tf_op jit(solution)/shard_map/ppermute | solution.py:315
  23.4 14.6 %collective-permute-start.4 = (bf16[272,1024]{1,0:T(8,128)(2,1)S(1)}, bf16[272,1024]{1,0:T(8,128)(2,1)S(1)}, u32[]{:S(2)}, u32[]{:S(2)}) collective-permute-start(bf16[272,1024]{1,0:T(8,128)(2,1)S(1)} %collective-permute-done.1.refs_1_), channel_id=1, source_target_pairs={{0,1},{1,0},{2,6},{3,7},{4,5},{5,4},{6,2},{7,3},{8,9},{9,8},{10,14... | collective-permute-start | bytes 1671176 | tf_op jit(solution)/shard_map/ppermute | solution.py:315
  24.3 0.8 copy-start.6
  25.1 21.5 %collective-permute-start.3 = (bf16[272,1024]{1,0:T(8,128)(2,1)}, bf16[272,1024]{1,0:T(8,128)(2,1)}, u32[]{:S(2)}, u32[]{:S(2)}) collective-permute-start(bf16[272,1024]{1,0:T(8,128)(2,1)} %collective-permute-done.2.refs_0_), channel_id=1, source_target_pairs={{0,1},{1,0},{2,6},{3,7},{4,5},{5,4},{6,2},{7,3},{8,9},{9,8},{10,14... | collective-permute-start | bytes 1671176 | tf_op jit(solution)/shard_map/ppermute | solution.py:315
  38.0 0.8 copy-start.8
  38.8 9.5 %collective-permute-start.7 = (bf16[272,1024]{1,0:T(8,128)(2,1)S(1)}, bf16[272,1024]{1,0:T(8,128)(2,1)S(1)}, u32[]{:S(2)}, u32[]{:S(2)}) collective-permute-start(bf16[272,1024]{1,0:T(8,128)(2,1)S(1)} %collective-permute-done.6.refs_0_), channel_id=1, source_target_pairs={{0,1},{1,0},{2,6},{3,7},{4,5},{5,4},{6,2},{7,3},{8,9},{9,8},{10,14... | collective-permute-start | bytes 1671176 | tf_op jit(solution)/shard_map/ppermute | solution.py:315
  39.3 15.1 %collective-permute-start.8 = (bf16[272,1024]{1,0:T(8,128)(2,1)}, bf16[272,1024]{1,0:T(8,128)(2,1)}, u32[]{:S(2)}, u32[]{:S(2)}) collective-permute-start(bf16[272,1024]{1,0:T(8,128)(2,1)} %collective-permute-done.5.refs_1_), channel_id=1, source_target_pairs={{0,1},{1,0},{2,6},{3,7},{4,5},{5,4},{6,2},{7,3},{8,9},{9,8},{10,14... | collective-permute-start | bytes 1671176 | tf_op jit(solution)/shard_map/ppermute | solution.py:315
  40.8 13.6 %collective-permute-start.9 = (bf16[272,1024]{1,0:T(8,128)(2,1)S(1)}, bf16[272,1024]{1,0:T(8,128)(2,1)S(1)}, u32[]{:S(2)}, u32[]{:S(2)}) collective-permute-start(bf16[272,1024]{1,0:T(8,128)(2,1)S(1)} %collective-permute-done.6.refs_0_), channel_id=1, source_target_pairs={{0,8},{1,9},{2,10},{3,11},{4,12},{5,13},{6,14},{7,15},{8,24},{9,25... | collective-permute-start | bytes 1671176 | tf_op jit(solution)/shard_map/ppermute | solution.py:315
  40.9 1.1 copy-start.3
  41.9 1.1 copy-start.5
  43.0 1.1 copy-start.7
  44.0 1.1 copy-start.9
  45.1 15.3 %copy-start.1 = (bf16[1,384,2048]{2,1,0:T(8,128)(2,1)S(1)}, bf16[1,384,2048]{2,1,0:T(8,128)(2,1)}, u32[]{:S(2)}) copy-start(bf16[1,384,2048]{2,1,0:T(8,128)(2,1)} %param.12) | copy-start | bytes 4718596
  46.6 13.8 %copy-start = (bf16[1,384,2048]{2,1,0:T(8,128)(2,1)S(1)}, bf16[1,384,2048]{2,1,0:T(8,128)(2,1)}, u32[]{:S(2)}) copy-start(bf16[1,384,2048]{2,1,0:T(8,128)(2,1)} %param.11) | copy-start | bytes 4718596
  54.4 6.0 %collective-permute-start.13 = (bf16[2,144,2048]{2,1,0:T(8,128)(2,1)S(1)}, bf16[2,144,2048]{2,1,0:T(8,128)(2,1)S(1)}, u32[]{:S(2)}, u32[]{:S(2)}) collective-permute-start(bf16[2,144,2048]{2,1,0:T(8,128)(2,1)S(1)} %get-tuple-element.128), channel_id=1, source_target_pairs={{0,2},{1,3},{2,0},{3,1},{4,6},{5,7},{6,4},{7,5},{8,10},{9,11},{10,... | collective-permute-start | bytes 3538952 | tf_op jit(solution)/shard_map/ppermute | solution.py:315
  54.9 15.6 %collective-permute-start.11 = (bf16[272,1024]{1,0:T(8,128)(2,1)}, bf16[272,1024]{1,0:T(8,128)(2,1)S(1)}, u32[]{:S(2)}, u32[]{:S(2)}) collective-permute-start(bf16[272,1024]{1,0:T(8,128)(2,1)} %collective-permute-done.5.refs_1_), channel_id=1, source_target_pairs={{0,8},{1,9},{2,10},{3,11},{4,12},{5,13},{6,14},{7,15},{8,24},{9,25... | collective-permute-start | bytes 1671176 | tf_op jit(solution)/shard_map/ppermute | solution.py:315
  56.5 14.5 %collective-permute-start.10 = (bf16[272,1024]{1,0:T(8,128)(2,1)S(1)}, bf16[272,1024]{1,0:T(8,128)(2,1)S(1)}, u32[]{:S(2)}, u32[]{:S(2)}) collective-permute-start(bf16[272,1024]{1,0:T(8,128)(2,1)S(1)} %collective-permute-done.9.refs_0_), channel_id=1, source_target_pairs={{0,1},{1,0},{2,6},{3,7},{4,5},{5,4},{6,2},{7,3},{8,9},{9,8},{10,14... | collective-permute-start | bytes 1671176 | tf_op jit(solution)/shard_map/ppermute | solution.py:315
  57.1 13.8 %collective-permute-start.12 = (bf16[272,1024]{1,0:T(8,128)(2,1)S(1)}, bf16[272,1024]{1,0:T(8,128)(2,1)S(1)}, u32[]{:S(2)}, u32[]{:S(2)}) collective-permute-start(bf16[272,1024]{1,0:T(8,128)(2,1)S(1)} %collective-permute-done.9.refs_0_), channel_id=1, source_target_pairs={{0,4},{1,5},{2,3},{3,2},{4,0},{5,1},{6,7},{7,6},{8,12},{9,13},{10,... | collective-permute-start | bytes 1671176 | tf_op jit(solution)/shard_map/ppermute | solution.py:315
  70.9 5.0 %collective-permute-start.17 = (bf16[2,144,2048]{2,1,0:T(8,128)(2,1)S(1)}, bf16[2,144,2048]{2,1,0:T(8,128)(2,1)S(1)}, u32[]{:S(2)}, u32[]{:S(2)}) collective-permute-start(bf16[2,144,2048]{2,1,0:T(8,128)(2,1)S(1)} %get-tuple-element.144), channel_id=1, source_target_pairs={{0,2},{1,3},{2,0},{3,1},{4,6},{5,7},{6,4},{7,5},{8,10},{9,11},{10,... | collective-permute-start | bytes 3538952 | tf_op jit(solution)/shard_map/ppermute | solution.py:315
  70.9 3.7 %collective-permute-start.14 = (bf16[144,2048]{1,0:T(8,128)(2,1)S(1)}, bf16[144,2048]{1,0:T(8,128)(2,1)S(1)}, u32[]{:S(2)}, u32[]{:S(2)}) collective-permute-start(bf16[144,2048]{1,0:T(8,128)(2,1)S(1)} %get-tuple-element.136), channel_id=1, source_target_pairs={{0,2},{1,3},{2,0},{3,1},{4,6},{5,7},{6,4},{7,5},{8,10},{9,11},{10,... | collective-permute-start | bytes 1769480 | tf_op jit(solution)/shard_map/ppermute | solution.py:315
  71.5 9.5 %collective-permute-start.16 = (bf16[272,1024]{1,0:T(8,128)(2,1)S(1)}, bf16[272,1024]{1,0:T(8,128)(2,1)S(1)}, u32[]{:S(2)}, u32[]{:S(2)}) collective-permute-start(bf16[272,1024]{1,0:T(8,128)(2,1)S(1)} %collective-permute-done.11.refs_1_), channel_id=1, source_target_pairs={{0,1},{1,0},{2,6},{3,7},{4,5},{5,4},{6,2},{7,3},{8,9},{9,8},{10,14... | collective-permute-start | bytes 1671176 | tf_op jit(solution)/shard_map/ppermute | solution.py:315
  82.5 5.0 %collective-permute-start.19 = (bf16[2,144,2048]{2,1,0:T(8,128)(2,1)S(1)}, bf16[2,144,2048]{2,1,0:T(8,128)(2,1)S(1)}, u32[]{:S(2)}, u32[]{:S(2)}) collective-permute-start(bf16[2,144,2048]{2,1,0:T(8,128)(2,1)S(1)} %get-tuple-element.163), channel_id=1, source_target_pairs={{0,2},{1,3},{2,0},{3,1},{4,6},{5,7},{6,4},{7,5},{8,10},{9,11},{10,... | collective-permute-start | bytes 3538952 | tf_op jit(solution)/shard_map/ppermute | solution.py:315
  82.6 3.7 %collective-permute-start.18 = (bf16[144,2048]{1,0:T(8,128)(2,1)S(1)}, bf16[144,2048]{1,0:T(8,128)(2,1)S(1)}, u32[]{:S(2)}, u32[]{:S(2)}) collective-permute-start(bf16[144,2048]{1,0:T(8,128)(2,1)S(1)} %get-tuple-element.160), channel_id=1, source_target_pairs={{0,2},{1,3},{2,0},{3,1},{4,6},{5,7},{6,4},{7,5},{8,10},{9,11},{10,... | collective-permute-start | bytes 1769480 | tf_op jit(solution)/shard_map/ppermute | solution.py:315
  83.1 9.6 %collective-permute-start.15 = (bf16[272,1024]{1,0:T(8,128)(2,1)S(1)}, bf16[272,1024]{1,0:T(8,128)(2,1)S(1)}, u32[]{:S(2)}, u32[]{:S(2)}) collective-permute-start(bf16[272,1024]{1,0:T(8,128)(2,1)S(1)} %collective-permute-done.12.refs_1_), channel_id=1, source_target_pairs={{0,1},{1,0},{2,6},{3,7},{4,5},{5,4},{6,2},{7,3},{8,9},{9,8},{10,14... | collective-permute-start | bytes 1671176 | tf_op jit(solution)/shard_map/ppermute | solution.py:315
  94.2 6.0 %collective-permute-start.21 = (bf16[2,144,2048]{2,1,0:T(8,128)(2,1)S(1)}, bf16[2,144,2048]{2,1,0:T(8,128)(2,1)S(1)}, u32[]{:S(2)}, u32[]{:S(2)}) collective-permute-start(bf16[2,144,2048]{2,1,0:T(8,128)(2,1)S(1)} %get-tuple-element.180), channel_id=1, source_target_pairs={{0,2},{1,3},{2,0},{3,1},{4,6},{5,7},{6,4},{7,5},{8,10},{9,11},{10,... | collective-permute-start | bytes 3538952 | tf_op jit(solution)/shard_map/ppermute | solution.py:315
  94.4 3.6 %collective-permute-start.20 = (bf16[144,2048]{1,0:T(8,128)(2,1)S(1)}, bf16[144,2048]{1,0:T(8,128)(2,1)S(1)}, u32[]{:S(2)}, u32[]{:S(2)}) collective-permute-start(bf16[144,2048]{1,0:T(8,128)(2,1)S(1)} %get-tuple-element.177), channel_id=1, source_target_pairs={{0,2},{1,3},{2,0},{3,1},{4,6},{5,7},{6,4},{7,5},{8,10},{9,11},{10,... | collective-permute-start | bytes 1769480 | tf_op jit(solution)/shard_map/ppermute | solution.py:315
  94.7 10.9 %collective-permute-start.27 = (bf16[2,128,1024]{2,1,0:T(8,128)(2,1)S(1)}, bf16[2,128,1024]{2,1,0:T(8,128)(2,1)S(1)}, u32[]{:S(2)}, u32[]{:S(2)}) collective-permute-start(bf16[2,128,1024]{2,1,0:T(8,128)(2,1)S(1)} %get-tuple-element.161), channel_id=1, source_target_pairs={{0,1},{1,0},{2,6},{3,7},{4,5},{5,4},{6,2},{7,3},{8,9},{9,8},{10,14... | collective-permute-start | bytes 1572872 | tf_op jit(solution)/shard_map/ppermute | solution.py:315
  99.2 15.7 %collective-permute-start.25 = (bf16[2,128,1024]{2,1,0:T(8,128)(2,1)S(1)}, bf16[2,128,1024]{2,1,0:T(8,128)(2,1)S(1)}, u32[]{:S(2)}, u32[]{:S(2)}) collective-permute-start(bf16[2,128,1024]{2,1,0:T(8,128)(2,1)S(1)} %get-tuple-element.178), channel_id=1, source_target_pairs={{0,1},{1,0},{2,6},{3,7},{4,5},{5,4},{6,2},{7,3},{8,9},{9,8},{10,14... | collective-permute-start | bytes 1572872 | tf_op jit(solution)/shard_map/ppermute | solution.py:315
  105.1 2.2 %collective-permute-start.22 = (bf16[144,2048]{1,0:T(8,128)(2,1)S(1)}, bf16[144,2048]{1,0:T(8,128)(2,1)S(1)}, u32[]{:S(2)}, u32[]{:S(2)}) collective-permute-start(bf16[144,2048]{1,0:T(8,128)(2,1)S(1)} %get-tuple-element.187), channel_id=1, source_target_pairs={{0,2},{1,3},{2,0},{3,1},{4,6},{5,7},{6,4},{7,5},{8,10},{9,11},{10,... | collective-permute-start | bytes 1769480 | tf_op jit(solution)/shard_map/ppermute | solution.py:315
  105.8 7.1 %collective-permute-start.28 = (bf16[128,1024]{1,0:T(8,128)(2,1)S(1)}, bf16[128,1024]{1,0:T(8,128)(2,1)S(1)}, u32[]{:S(2)}, u32[]{:S(2)}) collective-permute-start(bf16[128,1024]{1,0:T(8,128)(2,1)S(1)} %fusion.16), channel_id=1, source_target_pairs={{0,4},{1,5},{2,3},{3,2},{4,0},{5,1},{6,7},{7,6},{8,12},{9,13},{10,... | collective-permute-start | bytes 786440 | tf_op jit(solution)/shard_map/ppermute | solution.py:315
  108.5 20.6 %collective-permute-start.24 = (bf16[2,128,1024]{2,1,0:T(8,128)(2,1)S(1)}, bf16[2,128,1024]{2,1,0:T(8,128)(2,1)S(1)}, u32[]{:S(2)}, u32[]{:S(2)}) collective-permute-start(bf16[2,128,1024]{2,1,0:T(8,128)(2,1)S(1)} %get-tuple-element.188), channel_id=1, source_target_pairs={{0,1},{1,0},{2,6},{3,7},{4,5},{5,4},{6,2},{7,3},{8,9},{9,8},{10,14... | collective-permute-start | bytes 1572872 | tf_op jit(solution)/shard_map/ppermute | solution.py:315
  113.0 8.8 %collective-permute-start.29 = (bf16[128,1024]{1,0:T(8,128)(2,1)S(1)}, bf16[128,1024]{1,0:T(8,128)(2,1)S(1)}, u32[]{:S(2)}, u32[]{:S(2)}) collective-permute-start(bf16[128,1024]{1,0:T(8,128)(2,1)S(1)} %fusion.7), channel_id=1, source_target_pairs={{0,8},{1,9},{2,10},{3,11},{4,12},{5,13},{6,14},{7,15},{8,24},{9,25... | collective-permute-start | bytes 786440 | tf_op jit(solution)/shard_map/ppermute | solution.py:315
  115.1 9.2 %collective-permute-start.26 = (bf16[128,1024]{1,0:T(8,128)(2,1)S(1)}, bf16[128,1024]{1,0:T(8,128)(2,1)S(1)}, u32[]{:S(2)}, u32[]{:S(2)}) collective-permute-start(bf16[128,1024]{1,0:T(8,128)(2,1)S(1)} %fusion.15), channel_id=1, source_target_pairs={{0,4},{1,5},{2,3},{3,2},{4,0},{5,1},{6,7},{7,6},{8,12},{9,13},{10,... | collective-permute-start | bytes 786440 | tf_op jit(solution)/shard_map/ppermute | solution.py:315
  116.5 14.3 %collective-permute-start.23 = (bf16[2,128,1024]{2,1,0:T(8,128)(2,1)S(1)}, bf16[2,128,1024]{2,1,0:T(8,128)(2,1)S(1)}, u32[]{:S(2)}, u32[]{:S(2)}) collective-permute-start(bf16[2,128,1024]{2,1,0:T(8,128)(2,1)S(1)} %get-tuple-element.189), channel_id=1, source_target_pairs={{0,1},{1,0},{2,6},{3,7},{4,5},{5,4},{6,2},{7,3},{8,9},{9,8},{10,14... | collective-permute-start | bytes 1572872 | tf_op jit(solution)/shard_map/ppermute | solution.py:315
  124.4 7.3 %collective-permute-start.31 = (bf16[128,1024]{1,0:T(8,128)(2,1)S(1)}, bf16[128,1024]{1,0:T(8,128)(2,1)S(1)}, u32[]{:S(2)}, u32[]{:S(2)}) collective-permute-start(bf16[128,1024]{1,0:T(8,128)(2,1)S(1)} %fusion.10), channel_id=1, source_target_pairs={{0,8},{1,9},{2,10},{3,11},{4,12},{5,13},{6,14},{7,15},{8,24},{9,25... | collective-permute-start | bytes 786440 | tf_op jit(solution)/shard_map/ppermute | solution.py:315
  129.3 6.4 %collective-permute-start.30 = (bf16[128,1024]{1,0:T(8,128)(2,1)S(1)}, bf16[128,1024]{1,0:T(8,128)(2,1)S(1)}, u32[]{:S(2)}, u32[]{:S(2)}) collective-permute-start(bf16[128,1024]{1,0:T(8,128)(2,1)S(1)} %fusion.17), channel_id=1, source_target_pairs={{0,4},{1,5},{2,3},{3,2},{4,0},{5,1},{6,7},{7,6},{8,12},{9,13},{10,... | collective-permute-start | bytes 786440 | tf_op jit(solution)/shard_map/ppermute | solution.py:315
  135.9 7.9 %collective-permute-start.33 = (bf16[128,1024]{1,0:T(8,128)(2,1)S(1)}, bf16[128,1024]{1,0:T(8,128)(2,1)S(1)}, u32[]{:S(2)}, u32[]{:S(2)}) collective-permute-start(bf16[128,1024]{1,0:T(8,128)(2,1)S(1)} %fusion.5), channel_id=1, source_target_pairs={{0,8},{1,9},{2,10},{3,11},{4,12},{5,13},{6,14},{7,15},{8,24},{9,25... | collective-permute-start | bytes 786440 | tf_op jit(solution)/shard_map/ppermute | solution.py:315
  136.5 6.4 %collective-permute-start.32 = (bf16[128,1024]{1,0:T(8,128)(2,1)S(1)}, bf16[128,1024]{1,0:T(8,128)(2,1)S(1)}, u32[]{:S(2)}, u32[]{:S(2)}) collective-permute-start(bf16[128,1024]{1,0:T(8,128)(2,1)S(1)} %fusion.14), channel_id=1, source_target_pairs={{0,4},{1,5},{2,3},{3,2},{4,0},{5,1},{6,7},{7,6},{8,12},{9,13},{10,... | collective-permute-start | bytes 786440 | tf_op jit(solution)/shard_map/ppermute | solution.py:315

commit v19 on v18

--- a/solution.py
+++ b/solution.py
@@ -401,12 +401,13 @@
         keep, came = late[c]
         came = tied(came, near if c == 1 else send if c + 1 < chunks else previous)
         pair = added(keep, came)
-        came = to_first(pair[1].astype(jnp.bfloat16))
+        leaving = pair[1].astype(jnp.bfloat16)
+        came = to_first(leaving)
         total = added(pair[0], tied(came, send) if c + 2 < chunks else came)
         running = (total if running is None else added(total, running)).astype(jnp.bfloat16)
         previous = running
-        if c > 1:
-            marks[min(c - 1, 2)] = running
+        if c > 1 and c + 1 == chunks:
+            marks[1], marks[2] = leaving, running
         if c + 1 < chunks:
             running = to_ring(running)
     keep, came = late[0]

time: 145 us -> 141 us (0.972)
  waiting for transfers between devices: 60.3 us -> 56.9 us
    ppermute x34, waiting for transfers between devices: 60.3 us -> 56.9 us  [permute(): return lax.ppermute(value, ('expert', 'etp'), pairs)]
where the time goes in v19:
time: 141 us
  waiting for transfers between devices  56.9 us (40%)
  Pallas kernels  33.8 us (24%)
  starting transfers between devices  30.6 us (22%)
  matrix products  10.2 us (7%)
  local copies, waits for them, and re-layouts  6.76 us (5%)
  other arithmetic  1.78 us (1%)
    ppermute x34, waiting for transfers between devices, permute(): return lax.ppermute(value, ('expert', 'etp'), pairs)  56.9 us
    ppermute x34, starting transfers between devices, permute(): return lax.ppermute(value, ('expert', 'etp'), pairs)  30.6 us
    pallas_call x4, Pallas kernels, run_experts(): pl.pallas_call(functools.partial(expert_kernel, index, kept is not None),...  19.7 us
    pallas_call x4, Pallas kernels, pick_rows(): pl.pallas_call(functools.partial(pick_kernel, top, rows), in_specs=[pl.Bl...  7.05 us
    unnamed x20, local copies, waits for them, and re-layouts  6.63 us
    pallas_call x4, Pallas kernels, place_rows(): pl.pallas_call(place_kernel, in_specs=[pl.BlockSpec(memory_space=pltpu.SM...  5.08 us
    dot_general x1, matrix products, gather_body(): lax.dot_general(acts, rows_g, CONTRACT_FIRST, preferred_element_type=jnp....  3.42 us
    dot_general x1, matrix products, gather_body(): lax.dot_general(up_term, rows_x, CONTRACT_FIRST, preferred_element_type=j...  3.41 us
  transfers between devices with their start and end apart: 34, of which 19 were waited for; matrix products, arithmetic and copies ran while one was open for 8% of the time, Pallas kernels for 20%

profile of v19, /device:TPU:0, one launch (start us, length us, event | category | flops | bytes accessed | tf_op | source)
XLA Modules:
  0.0 141.1 jit_solution(9645242382825695142)
XLA Ops:
  0.6 2.0 %pack.1.refs_0_ = bf16[272,1024]{1,0:T(8,128)(2,1)} custom-call(bf16[128,1024]{1,0:T(8,128)(2,1)} %tokens_ref.1, bf16[128,1024]{1,0:T(8,128)(2,1)} %grads_ref.1, s32[8,128]{1,0:T(8,128)} %bitcast.70, f32[8,128]{1,0:T(8,128)} %bitcast.71), custom_call_target="tpu_custom_call" | custom-call | tf_op jit(solution)/shard_map/pack/pallas_call | solution.py:128
  2.6 2.9 %collective-permute-start = (bf16[272,1024]{1,0:T(8,128)(2,1)}, bf16[272,1024]{1,0:T(8,128)(2,1)S(1)}, u32[]{:S(2)}, u32[]{:S(2)}) collective-permute-start(bf16[272,1024]{1,0:T(8,128)(2,1)} %pack.1.refs_0_), channel_id=1, source_target_pairs={{0,1},{1,0},{2,6},{3,7},{4,5},{5,4},{6,2},{7,3},{8,9},{9,8},{10,14... | collective-permute-start | bytes 1671176 | tf_op jit(solution)/shard_map/ppermute | solution.py:315
  5.6 1.5 %collective-permute-start.1 = (bf16[272,1024]{1,0:T(8,128)(2,1)}, bf16[272,1024]{1,0:T(8,128)(2,1)S(1)}, u32[]{:S(2)}, u32[]{:S(2)}) collective-permute-start(bf16[272,1024]{1,0:T(8,128)(2,1)} %pack.1.refs_0_), channel_id=1, source_target_pairs={{0,4},{1,5},{2,3},{3,2},{4,0},{5,1},{6,7},{7,6},{8,12},{9,13},{10,... | collective-permute-start | bytes 1671176 | tf_op jit(solution)/shard_map/ppermute | solution.py:315
  7.1 1.6 %collective-permute-start.2 = (bf16[272,1024]{1,0:T(8,128)(2,1)}, bf16[272,1024]{1,0:T(8,128)(2,1)}, u32[]{:S(2)}, u32[]{:S(2)}) collective-permute-start(bf16[272,1024]{1,0:T(8,128)(2,1)} %pack.1.refs_0_), channel_id=1, source_target_pairs={{0,8},{1,9},{2,10},{3,11},{4,12},{5,13},{6,14},{7,15},{8,24},{9,25... | collective-permute-start | bytes 1671176 | tf_op jit(solution)/shard_map/ppermute | solution.py:315
  8.7 10.1 %collective-permute-done.refs_2_ = bf16[272,1024]{1,0:T(8,128)(2,1)S(1)} collective-permute-done((bf16[272,1024]{1,0:T(8,128)(2,1)}, bf16[272,1024]{1,0:T(8,128)(2,1)S(1)}, u32[]{:S(2)}, u32[]{:S(2)}) %collective-permute-start) | collective-permute-done | bytes 557088 | tf_op jit(solution)/shard_map/ppermute | solution.py:315
  19.6 2.5 %collective-permute-done.2.refs_0_ = bf16[272,1024]{1,0:T(8,128)(2,1)} collective-permute-done((bf16[272,1024]{1,0:T(8,128)(2,1)}, bf16[272,1024]{1,0:T(8,128)(2,1)}, u32[]{:S(2)}, u32[]{:S(2)}) %collective-permute-start.2) | collective-permute-done | bytes 557088 | tf_op jit(solution)/shard_map/ppermute | solution.py:315
  25.1 1.1 collective-permute-start.3
  26.2 11.7 %collective-permute-done.5.refs_1_ = bf16[272,1024]{1,0:T(8,128)(2,1)} collective-permute-done((bf16[272,1024]{1,0:T(8,128)(2,1)}, bf16[272,1024]{1,0:T(8,128)(2,1)}, u32[]{:S(2)}, u32[]{:S(2)}) %collective-permute-start.5) | collective-permute-done | bytes 557088 | tf_op jit(solution)/shard_map/ppermute | solution.py:315
  39.3 1.5 %collective-permute-start.8 = (bf16[272,1024]{1,0:T(8,128)(2,1)}, bf16[272,1024]{1,0:T(8,128)(2,1)}, u32[]{:S(2)}, u32[]{:S(2)}) collective-permute-start(bf16[272,1024]{1,0:T(8,128)(2,1)} %collective-permute-done.5.refs_1_), channel_id=1, source_target_pairs={{0,1},{1,0},{2,6},{3,7},{4,5},{5,4},{6,2},{7,3},{8,9},{9,8},{10,14... | collective-permute-start | bytes 1671176 | tf_op jit(solution)/shard_map/ppermute | solution.py:315
  40.9 1.1 copy-done.3
  41.9 1.1 copy-done.5
  43.0 1.1 copy-done.7
  44.0 1.1 copy-done.9
  45.1 1.5 %pick.4 = (bf16[2,144,2048]{2,1,0:T(8,128)(2,1)S(1)}, bf16[2,144,2048]{2,1,0:T(8,128)(2,1)S(1)}, bf16[288,256]{1,0:T(8,128)(2,1)S(1)}) custom-call(s32[3]{0:T(128)S(1)} %pad_add_fusion.place_ref, bf16[272,1024]{1,0:T(8,128)(2,1)S(1)} %copy-done.3, bf16[272,1024]{1,0:T(8,128)(2,1)S(1)} %copy-done.7, bf16[272,1024]{1,0:T(8,128)(2,1)S(1)} %copy-done.5, ...), custom_call_target="tpu_custom_call" | custom-call | tf_op jit(solution)/shard_map/pick/pallas_call | solution.py:251
  46.6 1.7 %collective-permute-done.7.refs_2_ = bf16[272,1024]{1,0:T(8,128)(2,1)S(1)} collective-permute-done((bf16[272,1024]{1,0:T(8,128)(2,1)S(1)}, bf16[272,1024]{1,0:T(8,128)(2,1)S(1)}, u32[]{:S(2)}, u32[]{:S(2)}) %collective-permute-start.7) | collective-permute-done | bytes 557088 | tf_op jit(solution)/shard_map/ppermute | solution.py:315
  48.3 6.1 %collective-permute-done.8.refs_3_ = bf16[272,1024]{1,0:T(8,128)(2,1)} collective-permute-done((bf16[272,1024]{1,0:T(8,128)(2,1)}, bf16[272,1024]{1,0:T(8,128)(2,1)}, u32[]{:S(2)}, u32[]{:S(2)}) %collective-permute-start.8) | collective-permute-done | bytes 557088 | tf_op jit(solution)/shard_map/ppermute | solution.py:315
  54.9 1.6 %collective-permute-start.11 = (bf16[272,1024]{1,0:T(8,128)(2,1)}, bf16[272,1024]{1,0:T(8,128)(2,1)S(1)}, u32[]{:S(2)}, u32[]{:S(2)}) collective-permute-start(bf16[272,1024]{1,0:T(8,128)(2,1)} %collective-permute-done.5.refs_1_), channel_id=1, source_target_pairs={{0,8},{1,9},{2,10},{3,11},{4,12},{5,13},{6,14},{7,15},{8,24},{9,25... | collective-permute-start | bytes 1671176 | tf_op jit(solution)/shard_map/ppermute | solution.py:315
  57.8 2.5 %pick.5 = (bf16[2,144,2048]{2,1,0:T(8,128)(2,1)S(1)}, bf16[2,144,2048]{2,1,0:T(8,128)(2,1)S(1)}, bf16[288,256]{1,0:T(8,128)(2,1)S(1)}) custom-call(s32[3]{0:T(128)S(1)} %pad_add_fusion.place_ref, bf16[272,1024]{1,0:T(8,128)(2,1)} %collective-permute-done.2.refs_0_, bf16[272,1024]{1,0:T(8,128)(2,1)} %collective-permute-done.5.refs_1_, ...), custom_call_target="tpu_custom_call" | custom-call | tf_op jit(solution)/shard_map/pick/pallas_call | solution.py:251
  60.4 4.9 %experts.4 = (bf16[144,2048]{1,0:T(8,128)(2,1)S(1)}, bf16[144,2048]{1,0:T(8,128)(2,1)S(1)}, bf16[1152,2048]{1,0:T(8,128)(2,1)S(1)}, bf16[1152,2048]{1,0:T(8,128)...) custom-call(bf16[2,144,2048]{2,1,0:T(8,128)(2,1)S(1)} %get-tuple-element.127., ...), custom_call_target="tpu_custom_call" | custom-call | tf_op jit(solution)/shard_map/experts/pallas_call | solution.py:270
  65.3 5.3 %collective-permute-done.11.refs_1_ = bf16[272,1024]{1,0:T(8,128)(2,1)S(1)} collective-permute-done((bf16[272,1024]{1,0:T(8,128)(2,1)}, bf16[272,1024]{1,0:T(8,128)(2,1)S(1)}, u32[]{:S(2)}, u32[]{:S(2)}) %collective-permute-start.11) | collective-permute-done | bytes 557088 | tf_op jit(solution)/shard_map/ppermute | solution.py:315
  72.3 2.3 %collective-permute-done.14.far_ref = bf16[144,2048]{1,0:T(8,128)(2,1)S(1)} collective-permute-done((bf16[144,2048]{1,0:T(8,128)(2,1)S(1)}, bf16[144,2048]{1,0:T(8,128)(2,1)S(1)}, u32[]{:S(2)}, u32[]{:S(2)}) %collective-permute-start.14) | collective-permute-done | bytes 589856 | tf_op jit(solution)/shard_map/ppermute | solution.py:315
  74.6 1.3 place.4
  75.9 4.9 %experts.5 = (bf16[144,2048]{1,0:T(8,128)(2,1)S(1)}, bf16[144,2048]{1,0:T(8,128)(2,1)S(1)}, bf16[1152,2048]{1,0:T(8,128)(2,1)S(1)}, bf16[1152,2048]{1,0:T(8,128)...) custom-call(bf16[2,144,2048]{2,1,0:T(8,128)(2,1)S(1)} %get-tuple-ele, ...), custom_call_target="tpu_custom_call", output_to_operand_aliasing={{2}: (5, {}), {3}: (6, {}), {4}: (7, {}), {5}: (8, {}), {6}... | custom-call | tf_op jit(solution)/shard_map/experts/pallas_call | solution.py:270
  81.0 1.5 %pick.6 = (bf16[2,144,2048]{2,1,0:T(8,128)(2,1)S(1)}, bf16[2,144,2048]{2,1,0:T(8,128)(2,1)S(1)}, bf16[288,256]{1,0:T(8,128)(2,1)S(1)}) custom-call(s32[3]{0:T(128)S(1)} %pad_add_fusion.place_ref, bf16[272,1024]{1,0:T(8,128)(2,1)S(1)} %collective-permute-done.6.refs_0_, bf16[272,1024]{1,0:T(8,128)(2,1)S(1)} %collective-permute-done.11.refs_1_, ...), custom_call_target="tpu_custom_call" | custom-call | tf_op jit(solution)/shard_map/pick/pallas_call | solution.py:251
  84.0 2.3 %collective-permute-done.18.far_ref = bf16[144,2048]{1,0:T(8,128)(2,1)S(1)} collective-permute-done((bf16[144,2048]{1,0:T(8,128)(2,1)S(1)}, bf16[144,2048]{1,0:T(8,128)(2,1)S(1)}, u32[]{:S(2)}, u32[]{:S(2)}) %collective-permute-start.18) | collective-permute-done | bytes 589856 | tf_op jit(solution)/shard_map/ppermute | solution.py:315
  86.3 1.3 place.5
  87.6 5.1 %experts.6 = (bf16[144,2048]{1,0:T(8,128)(2,1)S(1)}, bf16[144,2048]{1,0:T(8,128)(2,1)S(1)}, bf16[1152,2048]{1,0:T(8,128)(2,1)S(1)}, bf16[1152,2048]{1,0:T(8,128)...) custom-call(bf16[2,144,2048]{2,1,0:T(8,128)(2,1)S(1)} %get-tuple-ele, ...), custom_call_target="tpu_custom_call", output_to_operand_aliasing={{2}: (5, {}), {3}: (6, {}), {4}: (7, {}), {5}: (8, {}), {6}... | custom-call | tf_op jit(solution)/shard_map/experts/pallas_call | solution.py:270
  92.7 1.5 %pick.7 = (bf16[2,144,2048]{2,1,0:T(8,128)(2,1)S(1)}, bf16[2,144,2048]{2,1,0:T(8,128)(2,1)S(1)}, bf16[288,256]{1,0:T(8,128)(2,1)S(1)}) custom-call(s32[3]{0:T(128)S(1)} %pad_add_fusion.place_ref, bf16[272,1024]{1,0:T(8,128)(2,1)S(1)} %collective-permute-done.9.refs_0_, bf16[272,1024]{1,0:T(8,128)(2,1)S(1)} %collective-permute-done.12.refs_1_, ...), custom_call_target="tpu_custom_call" | custom-call | tf_op jit(solution)/shard_map/pick/pallas_call | solution.py:251
  94.7 0.9 collective-permute-start.27
  95.6 2.3 %collective-permute-done.20.far_ref = bf16[144,2048]{1,0:T(8,128)(2,1)S(1)} collective-permute-done((bf16[144,2048]{1,0:T(8,128)(2,1)S(1)}, bf16[144,2048]{1,0:T(8,128)(2,1)S(1)}, u32[]{:S(2)}, u32[]{:S(2)}) %collective-permute-start.20) | collective-permute-done | bytes 589856 | tf_op jit(solution)/shard_map/ppermute | solution.py:315
  97.9 1.3 place.6
  99.2 0.9 collective-permute-start.25
  100.2 4.9 %experts.7 = (bf16[144,2048]{1,0:T(8,128)(2,1)S(1)}, bf16[144,2048]{1,0:T(8,128)(2,1)S(1)}, bf16[1152,2048]{1,0:T(8,128)(2,1)S(1)}, bf16[1152,2048]{1,0:T(8,128)...) custom-call(bf16[2,144,2048]{2,1,0:T(8,128)(2,1)S(1)} %get-tuple-ele, ...), custom_call_target="tpu_custom_call", output_to_operand_aliasing={{2}: (5, {}), {3}: (6, {}), {4}: (7, {}), {5}: (8, {}), {6}... | custom-call | tf_op jit(solution)/shard_map/experts/pallas_call | solution.py:270
  105.8 0.9 collective-permute-start.28
  107.2 1.3 place.7
  108.5 1.1 collective-permute-start.24
  109.6 3.3 %collective-permute-done.28 = bf16[128,1024]{1,0:T(8,128)(2,1)S(1)} collective-permute-done((bf16[128,1024]{1,0:T(8,128)(2,1)S(1)}, bf16[128,1024]{1,0:T(8,128)(2,1)S(1)}, u32[]{:S(2)}, u32[]{:S(2)}) %collective-permute-start.28) | collective-permute-done | bytes 262176 | tf_op jit(solution)/shard_map/ppermute | solution.py:315
  113.0 1.9 %collective-permute-start.29 = (bf16[128,1024]{1,0:T(8,128)(2,1)S(1)}, bf16[128,1024]{1,0:T(8,128)(2,1)S(1)}, u32[]{:S(2)}, u32[]{:S(2)}) collective-permute-start(bf16[128,1024]{1,0:T(8,128)(2,1)S(1)} %fusion.7), channel_id=1, source_target_pairs={{0,8},{1,9},{2,10},{3,11},{4,12},{5,13},{6,14},{7,15},{8,24},{9,25... | collective-permute-start | bytes 786440 | tf_op jit(solution)/shard_map/ppermute | solution.py:315
  115.1 1.4 collective-permute-start.26
  117.1 3.4 %fusion.2 = bf16[1,384,2048]{2,1,0:T(8,128)(2,1)} fusion(bf16[1152,384]{1,0:T(8,128)(2,1)S(1)} %get-tuple-element.204, bf16[1152,2048]{1,0:T(8,128)(2,1)S(1)} %get-tuple-element.205), kind=kOutput, calls=%fused_computation.5 | convolution fusion | flops 1812725760 | bytes 7176192 | tf_op jit(solution)/shard_map/dot_general | solution.py:420
  120.5 1.3 collective-permute-done.29
  121.8 2.5 %collective-permute-done.26 = bf16[128,1024]{1,0:T(8,128)(2,1)S(1)} collective-permute-done((bf16[128,1024]{1,0:T(8,128)(2,1)S(1)}, bf16[128,1024]{1,0:T(8,128)(2,1)S(1)}, u32[]{:S(2)}, u32[]{:S(2)}) %collective-permute-start.26) | collective-permute-done | bytes 262176 | tf_op jit(solution)/shard_map/ppermute | solution.py:315
  124.4 1.3 collective-permute-start.31
  125.9 1.4 collective-permute-start.30
  127.3 3.4 %fusion = bf16[1,384,2048]{2,1,0:T(8,128)(2,1)} fusion(bf16[1152,384]{1,0:T(8,128)(2,1)S(1)} %get-tuple-element.199, bf16[1152,2048]{1,0:T(8,128)(2,1)S(1)} %get-tuple-element.200), kind=kOutput, calls=%fused_computation.3 | convolution fusion | flops 1812725760 | bytes 7176192 | tf_op jit(solution)/shard_map/dot_general | solution.py:421
  132.5 1.4 %collective-permute-start.33 = (bf16[128,1024]{1,0:T(8,128)(2,1)S(1)}, bf16[128,1024]{1,0:T(8,128)(2,1)S(1)}, u32[]{:S(2)}, u32[]{:S(2)}) collective-permute-start(bf16[128,1024]{1,0:T(8,128)(2,1)S(1)} %fusion.5), channel_id=1, source_target_pairs={{0,8},{1,9},{2,10},{3,11},{4,12},{5,13},{6,14},{7,15},{8,24},{9,25... | collective-permute-start | bytes 786440 | tf_op jit(solution)/shard_map/ppermute | solution.py:315
  133.9 3.4 %fusion.1 = bf16[1,384,2048]{2,1,0:T(8,128)(2,1)} fusion(bf16[1152,384]{1,0:T(8,128)(2,1)S(1)} %get-tuple-element.202, bf16[1152,2048]{1,0:T(8,128)(2,1)S(1)} %get-tuple-element.200), kind=kOutput, calls=%fused_computation.4 | convolution fusion | flops 1812725760 | bytes 7176192 | tf_op jit(solution)/shard_map/dot_general | solution.py:422
  137.3 2.9 %collective-permute-done.32 = bf16[128,1024]{1,0:T(8,128)(2,1)S(1)} collective-permute-done((bf16[128,1024]{1,0:T(8,128)(2,1)S(1)}, bf16[128,1024]{1,0:T(8,128)(2,1)S(1)}, u32[]{:S(2)}, u32[]{:S(2)}) %collective-permute-start.32) | collective-permute-done | bytes 262176 | tf_op jit(solution)/shard_map/ppermute | solution.py:315
  (69 shorter events, 16.2 us)
Async XLA Ops:
  0.6 59.8 %copy-start.2 = (bf16[1,384,2048]{2,1,0:T(8,128)(2,1)S(1)}, bf16[1,384,2048]{2,1,0:T(8,128)(2,1)}, u32[]{:S(2)}) copy-start(bf16[1,384,2048]{2,1,0:T(8,128)(2,1)} %param.13) | copy-start | bytes 4718596
  2.6 16.2 %collective-permute-start = (bf16[272,1024]{1,0:T(8,128)(2,1)}, bf16[272,1024]{1,0:T(8,128)(2,1)S(1)}, u32[]{:S(2)}, u32[]{:S(2)}) collective-permute-start(bf16[272,1024]{1,0:T(8,128)(2,1)} %pack.1.refs_0_), channel_id=1, source_target_pairs={{0,1},{1,0},{2,6},{3,7},{4,5},{5,4},{6,2},{7,3},{8,9},{9,8},{10,14... | collective-permute-start | bytes 1671176 | tf_op jit(solution)/shard_map/ppermute | solution.py:315
  5.6 14.0 %collective-permute-start.1 = (bf16[272,1024]{1,0:T(8,128)(2,1)}, bf16[272,1024]{1,0:T(8,128)(2,1)S(1)}, u32[]{:S(2)}, u32[]{:S(2)}) collective-permute-start(bf16[272,1024]{1,0:T(8,128)(2,1)} %pack.1.refs_0_), channel_id=1, source_target_pairs={{0,4},{1,5},{2,3},{3,2},{4,0},{5,1},{6,7},{7,6},{8,12},{9,13},{10,... | collective-permute-start | bytes 1671176 | tf_op jit(solution)/shard_map/ppermute | solution.py:315
  7.1 15.0 %collective-permute-start.2 = (bf16[272,1024]{1,0:T(8,128)(2,1)}, bf16[272,1024]{1,0:T(8,128)(2,1)}, u32[]{:S(2)}, u32[]{:S(2)}) collective-permute-start(bf16[272,1024]{1,0:T(8,128)(2,1)} %pack.1.refs_0_), channel_id=1, source_target_pairs={{0,8},{1,9},{2,10},{3,11},{4,12},{5,13},{6,14},{7,15},{8,24},{9,25... | collective-permute-start | bytes 1671176 | tf_op jit(solution)/shard_map/ppermute | solution.py:315
  18.8 0.8 copy-start.4
  22.1 15.8 %collective-permute-start.5 = (bf16[272,1024]{1,0:T(8,128)(2,1)}, bf16[272,1024]{1,0:T(8,128)(2,1)}, u32[]{:S(2)}, u32[]{:S(2)}) collective-permute-start(bf16[272,1024]{1,0:T(8,128)(2,1)} %collective-permute-done.2.refs_0_), channel_id=1, source_target_pairs={{0,4},{1,5},{2,3},{3,2},{4,0},{5,1},{6,7},{7,6},{8,12},{9,13},{10,... | collective-permute-start | bytes 1671176 | tf_op jit(solution)/shard_map/ppermute | solution.py:315
  22.7 15.3 %collective-permute-start.6 = (bf16[272,1024]{1,0:T(8,128)(2,1)}, bf16[272,1024]{1,0:T(8,128)(2,1)S(1)}, u32[]{:S(2)}, u32[]{:S(2)}) collective-permute-start(bf16[272,1024]{1,0:T(8,128)(2,1)} %collective-permute-done.2.refs_0_), channel_id=1, source_target_pairs={{0,8},{1,9},{2,10},{3,11},{4,12},{5,13},{6,14},{7,15},{8,24},{9,25... | collective-permute-start | bytes 1671176 | tf_op jit(solution)/shard_map/ppermute | solution.py:315
  23.4 14.6 %collective-permute-start.4 = (bf16[272,1024]{1,0:T(8,128)(2,1)S(1)}, bf16[272,1024]{1,0:T(8,128)(2,1)S(1)}, u32[]{:S(2)}, u32[]{:S(2)}) collective-permute-start(bf16[272,1024]{1,0:T(8,128)(2,1)S(1)} %collective-permute-done.1.refs_1_), channel_id=1, source_target_pairs={{0,1},{1,0},{2,6},{3,7},{4,5},{5,4},{6,2},{7,3},{8,9},{9,8},{10,14... | collective-permute-start | bytes 1671176 | tf_op jit(solution)/shard_map/ppermute | solution.py:315
  24.3 0.8 copy-start.6
  25.1 21.5 %collective-permute-start.3 = (bf16[272,1024]{1,0:T(8,128)(2,1)}, bf16[272,1024]{1,0:T(8,128)(2,1)}, u32[]{:S(2)}, u32[]{:S(2)}) collective-permute-start(bf16[272,1024]{1,0:T(8,128)(2,1)} %collective-permute-done.2.refs_0_), channel_id=1, source_target_pairs={{0,1},{1,0},{2,6},{3,7},{4,5},{5,4},{6,2},{7,3},{8,9},{9,8},{10,14... | collective-permute-start | bytes 1671176 | tf_op jit(solution)/shard_map/ppermute | solution.py:315
  38.0 0.8 copy-start.8
  38.8 9.5 %collective-permute-start.7 = (bf16[272,1024]{1,0:T(8,128)(2,1)S(1)}, bf16[272,1024]{1,0:T(8,128)(2,1)S(1)}, u32[]{:S(2)}, u32[]{:S(2)}) collective-permute-start(bf16[272,1024]{1,0:T(8,128)(2,1)S(1)} %collective-permute-done.6.refs_0_), channel_id=1, source_target_pairs={{0,1},{1,0},{2,6},{3,7},{4,5},{5,4},{6,2},{7,3},{8,9},{9,8},{10,14... | collective-permute-start | bytes 1671176 | tf_op jit(solution)/shard_map/ppermute | solution.py:315
  39.3 15.1 %collective-permute-start.8 = (bf16[272,1024]{1,0:T(8,128)(2,1)}, bf16[272,1024]{1,0:T(8,128)(2,1)}, u32[]{:S(2)}, u32[]{:S(2)}) collective-permute-start(bf16[272,1024]{1,0:T(8,128)(2,1)} %collective-permute-done.5.refs_1_), channel_id=1, source_target_pairs={{0,1},{1,0},{2,6},{3,7},{4,5},{5,4},{6,2},{7,3},{8,9},{9,8},{10,14... | collective-permute-start | bytes 1671176 | tf_op jit(solution)/shard_map/ppermute | solution.py:315
  40.8 13.6 %collective-permute-start.9 = (bf16[272,1024]{1,0:T(8,128)(2,1)S(1)}, bf16[272,1024]{1,0:T(8,128)(2,1)S(1)}, u32[]{:S(2)}, u32[]{:S(2)}) collective-permute-start(bf16[272,1024]{1,0:T(8,128)(2,1)S(1)} %collective-permute-done.6.refs_0_), channel_id=1, source_target_pairs={{0,8},{1,9},{2,10},{3,11},{4,12},{5,13},{6,14},{7,15},{8,24},{9,25... | collective-permute-start | bytes 1671176 | tf_op jit(solution)/shard_map/ppermute | solution.py:315
  40.9 1.1 copy-start.3
  41.9 1.1 copy-start.5
  43.0 1.1 copy-start.7
  44.0 1.1 copy-start.9
  45.1 15.3 %copy-start.1 = (bf16[1,384,2048]{2,1,0:T(8,128)(2,1)S(1)}, bf16[1,384,2048]{2,1,0:T(8,128)(2,1)}, u32[]{:S(2)}) copy-start(bf16[1,384,2048]{2,1,0:T(8,128)(2,1)} %param.12) | copy-start | bytes 4718596
  46.6 13.8 %copy-start = (bf16[1,384,2048]{2,1,0:T(8,128)(2,1)S(1)}, bf16[1,384,2048]{2,1,0:T(8,128)(2,1)}, u32[]{:S(2)}) copy-start(bf16[1,384,2048]{2,1,0:T(8,128)(2,1)} %param.11) | copy-start | bytes 4718596
  54.4 6.0 %collective-permute-start.13 = (bf16[2,144,2048]{2,1,0:T(8,128)(2,1)S(1)}, bf16[2,144,2048]{2,1,0:T(8,128)(2,1)S(1)}, u32[]{:S(2)}, u32[]{:S(2)}) collective-permute-start(bf16[2,144,2048]{2,1,0:T(8,128)(2,1)S(1)} %get-tuple-element.128), channel_id=1, source_target_pairs={{0,2},{1,3},{2,0},{3,1},{4,6},{5,7},{6,4},{7,5},{8,10},{9,11},{10,... | collective-permute-start | bytes 3538952 | tf_op jit(solution)/shard_map/ppermute | solution.py:315
  54.9 15.6 %collective-permute-start.11 = (bf16[272,1024]{1,0:T(8,128)(2,1)}, bf16[272,1024]{1,0:T(8,128)(2,1)S(1)}, u32[]{:S(2)}, u32[]{:S(2)}) collective-permute-start(bf16[272,1024]{1,0:T(8,128)(2,1)} %collective-permute-done.5.refs_1_), channel_id=1, source_target_pairs={{0,8},{1,9},{2,10},{3,11},{4,12},{5,13},{6,14},{7,15},{8,24},{9,25... | collective-permute-start | bytes 1671176 | tf_op jit(solution)/shard_map/ppermute | solution.py:315
  56.5 14.5 %collective-permute-start.10 = (bf16[272,1024]{1,0:T(8,128)(2,1)S(1)}, bf16[272,1024]{1,0:T(8,128)(2,1)S(1)}, u32[]{:S(2)}, u32[]{:S(2)}) collective-permute-start(bf16[272,1024]{1,0:T(8,128)(2,1)S(1)} %collective-permute-done.9.refs_0_), channel_id=1, source_target_pairs={{0,1},{1,0},{2,6},{3,7},{4,5},{5,4},{6,2},{7,3},{8,9},{9,8},{10,14... | collective-permute-start | bytes 1671176 | tf_op jit(solution)/shard_map/ppermute | solution.py:315
  57.1 13.8 %collective-permute-start.12 = (bf16[272,1024]{1,0:T(8,128)(2,1)S(1)}, bf16[272,1024]{1,0:T(8,128)(2,1)S(1)}, u32[]{:S(2)}, u32[]{:S(2)}) collective-permute-start(bf16[272,1024]{1,0:T(8,128)(2,1)S(1)} %collective-permute-done.9.refs_0_), channel_id=1, source_target_pairs={{0,4},{1,5},{2,3},{3,2},{4,0},{5,1},{6,7},{7,6},{8,12},{9,13},{10,... | collective-permute-start | bytes 1671176 | tf_op jit(solution)/shard_map/ppermute | solution.py:315
  70.9 5.0 %collective-permute-start.17 = (bf16[2,144,2048]{2,1,0:T(8,128)(2,1)S(1)}, bf16[2,144,2048]{2,1,0:T(8,128)(2,1)S(1)}, u32[]{:S(2)}, u32[]{:S(2)}) collective-permute-start(bf16[2,144,2048]{2,1,0:T(8,128)(2,1)S(1)} %get-tuple-element.144), channel_id=1, source_target_pairs={{0,2},{1,3},{2,0},{3,1},{4,6},{5,7},{6,4},{7,5},{8,10},{9,11},{10,... | collective-permute-start | bytes 3538952 | tf_op jit(solution)/shard_map/ppermute | solution.py:315
  70.9 3.7 %collective-permute-start.14 = (bf16[144,2048]{1,0:T(8,128)(2,1)S(1)}, bf16[144,2048]{1,0:T(8,128)(2,1)S(1)}, u32[]{:S(2)}, u32[]{:S(2)}) collective-permute-start(bf16[144,2048]{1,0:T(8,128)(2,1)S(1)} %get-tuple-element.136), channel_id=1, source_target_pairs={{0,2},{1,3},{2,0},{3,1},{4,6},{5,7},{6,4},{7,5},{8,10},{9,11},{10,... | collective-permute-start | bytes 1769480 | tf_op jit(solution)/shard_map/ppermute | solution.py:315
  71.5 9.5 %collective-permute-start.16 = (bf16[272,1024]{1,0:T(8,128)(2,1)S(1)}, bf16[272,1024]{1,0:T(8,128)(2,1)S(1)}, u32[]{:S(2)}, u32[]{:S(2)}) collective-permute-start(bf16[272,1024]{1,0:T(8,128)(2,1)S(1)} %collective-permute-done.11.refs_1_), channel_id=1, source_target_pairs={{0,1},{1,0},{2,6},{3,7},{4,5},{5,4},{6,2},{7,3},{8,9},{9,8},{10,14... | collective-permute-start | bytes 1671176 | tf_op jit(solution)/shard_map/ppermute | solution.py:315
  82.5 5.0 %collective-permute-start.19 = (bf16[2,144,2048]{2,1,0:T(8,128)(2,1)S(1)}, bf16[2,144,2048]{2,1,0:T(8,128)(2,1)S(1)}, u32[]{:S(2)}, u32[]{:S(2)}) collective-permute-start(bf16[2,144,2048]{2,1,0:T(8,128)(2,1)S(1)} %get-tuple-element.163), channel_id=1, source_target_pairs={{0,2},{1,3},{2,0},{3,1},{4,6},{5,7},{6,4},{7,5},{8,10},{9,11},{10,... | collective-permute-start | bytes 3538952 | tf_op jit(solution)/shard_map/ppermute | solution.py:315
  82.6 3.7 %collective-permute-start.18 = (bf16[144,2048]{1,0:T(8,128)(2,1)S(1)}, bf16[144,2048]{1,0:T(8,128)(2,1)S(1)}, u32[]{:S(2)}, u32[]{:S(2)}) collective-permute-start(bf16[144,2048]{1,0:T(8,128)(2,1)S(1)} %get-tuple-element.160), channel_id=1, source_target_pairs={{0,2},{1,3},{2,0},{3,1},{4,6},{5,7},{6,4},{7,5},{8,10},{9,11},{10,... | collective-permute-start | bytes 1769480 | tf_op jit(solution)/shard_map/ppermute | solution.py:315
  83.1 9.6 %collective-permute-start.15 = (bf16[272,1024]{1,0:T(8,128)(2,1)S(1)}, bf16[272,1024]{1,0:T(8,128)(2,1)S(1)}, u32[]{:S(2)}, u32[]{:S(2)}) collective-permute-start(bf16[272,1024]{1,0:T(8,128)(2,1)S(1)} %collective-permute-done.12.refs_1_), channel_id=1, source_target_pairs={{0,1},{1,0},{2,6},{3,7},{4,5},{5,4},{6,2},{7,3},{8,9},{9,8},{10,14... | collective-permute-start | bytes 1671176 | tf_op jit(solution)/shard_map/ppermute | solution.py:315
  94.2 6.0 %collective-permute-start.21 = (bf16[2,144,2048]{2,1,0:T(8,128)(2,1)S(1)}, bf16[2,144,2048]{2,1,0:T(8,128)(2,1)S(1)}, u32[]{:S(2)}, u32[]{:S(2)}) collective-permute-start(bf16[2,144,2048]{2,1,0:T(8,128)(2,1)S(1)} %get-tuple-element.180), channel_id=1, source_target_pairs={{0,2},{1,3},{2,0},{3,1},{4,6},{5,7},{6,4},{7,5},{8,10},{9,11},{10,... | collective-permute-start | bytes 3538952 | tf_op jit(solution)/shard_map/ppermute | solution.py:315
  94.4 3.6 %collective-permute-start.20 = (bf16[144,2048]{1,0:T(8,128)(2,1)S(1)}, bf16[144,2048]{1,0:T(8,128)(2,1)S(1)}, u32[]{:S(2)}, u32[]{:S(2)}) collective-permute-start(bf16[144,2048]{1,0:T(8,128)(2,1)S(1)} %get-tuple-element.177), channel_id=1, source_target_pairs={{0,2},{1,3},{2,0},{3,1},{4,6},{5,7},{6,4},{7,5},{8,10},{9,11},{10,... | collective-permute-start | bytes 1769480 | tf_op jit(solution)/shard_map/ppermute | solution.py:315
  94.7 10.9 %collective-permute-start.27 = (bf16[2,128,1024]{2,1,0:T(8,128)(2,1)S(1)}, bf16[2,128,1024]{2,1,0:T(8,128)(2,1)S(1)}, u32[]{:S(2)}, u32[]{:S(2)}) collective-permute-start(bf16[2,128,1024]{2,1,0:T(8,128)(2,1)S(1)} %get-tuple-element.161), channel_id=1, source_target_pairs={{0,1},{1,0},{2,6},{3,7},{4,5},{5,4},{6,2},{7,3},{8,9},{9,8},{10,14... | collective-permute-start | bytes 1572872 | tf_op jit(solution)/shard_map/ppermute | solution.py:315
  99.2 15.7 %collective-permute-start.25 = (bf16[2,128,1024]{2,1,0:T(8,128)(2,1)S(1)}, bf16[2,128,1024]{2,1,0:T(8,128)(2,1)S(1)}, u32[]{:S(2)}, u32[]{:S(2)}) collective-permute-start(bf16[2,128,1024]{2,1,0:T(8,128)(2,1)S(1)} %get-tuple-element.178), channel_id=1, source_target_pairs={{0,1},{1,0},{2,6},{3,7},{4,5},{5,4},{6,2},{7,3},{8,9},{9,8},{10,14... | collective-permute-start | bytes 1572872 | tf_op jit(solution)/shard_map/ppermute | solution.py:315
  105.1 2.2 %collective-permute-start.22 = (bf16[144,2048]{1,0:T(8,128)(2,1)S(1)}, bf16[144,2048]{1,0:T(8,128)(2,1)S(1)}, u32[]{:S(2)}, u32[]{:S(2)}) collective-permute-start(bf16[144,2048]{1,0:T(8,128)(2,1)S(1)} %get-tuple-element.187), channel_id=1, source_target_pairs={{0,2},{1,3},{2,0},{3,1},{4,6},{5,7},{6,4},{7,5},{8,10},{9,11},{10,... | collective-permute-start | bytes 1769480 | tf_op jit(solution)/shard_map/ppermute | solution.py:315
  105.8 7.1 %collective-permute-start.28 = (bf16[128,1024]{1,0:T(8,128)(2,1)S(1)}, bf16[128,1024]{1,0:T(8,128)(2,1)S(1)}, u32[]{:S(2)}, u32[]{:S(2)}) collective-permute-start(bf16[128,1024]{1,0:T(8,128)(2,1)S(1)} %fusion.16), channel_id=1, source_target_pairs={{0,4},{1,5},{2,3},{3,2},{4,0},{5,1},{6,7},{7,6},{8,12},{9,13},{10,... | collective-permute-start | bytes 786440 | tf_op jit(solution)/shard_map/ppermute | solution.py:315
  108.5 17.2 %collective-permute-start.24 = (bf16[2,128,1024]{2,1,0:T(8,128)(2,1)S(1)}, bf16[2,128,1024]{2,1,0:T(8,128)(2,1)S(1)}, u32[]{:S(2)}, u32[]{:S(2)}) collective-permute-start(bf16[2,128,1024]{2,1,0:T(8,128)(2,1)S(1)} %get-tuple-element.188), channel_id=1, source_target_pairs={{0,1},{1,0},{2,6},{3,7},{4,5},{5,4},{6,2},{7,3},{8,9},{9,8},{10,14... | collective-permute-start | bytes 1572872 | tf_op jit(solution)/shard_map/ppermute | solution.py:315
  113.0 8.8 %collective-permute-start.29 = (bf16[128,1024]{1,0:T(8,128)(2,1)S(1)}, bf16[128,1024]{1,0:T(8,128)(2,1)S(1)}, u32[]{:S(2)}, u32[]{:S(2)}) collective-permute-start(bf16[128,1024]{1,0:T(8,128)(2,1)S(1)} %fusion.7), channel_id=1, source_target_pairs={{0,8},{1,9},{2,10},{3,11},{4,12},{5,13},{6,14},{7,15},{8,24},{9,25... | collective-permute-start | bytes 786440 | tf_op jit(solution)/shard_map/ppermute | solution.py:315
  115.1 9.2 %collective-permute-start.26 = (bf16[128,1024]{1,0:T(8,128)(2,1)S(1)}, bf16[128,1024]{1,0:T(8,128)(2,1)S(1)}, u32[]{:S(2)}, u32[]{:S(2)}) collective-permute-start(bf16[128,1024]{1,0:T(8,128)(2,1)S(1)} %fusion.15), channel_id=1, source_target_pairs={{0,4},{1,5},{2,3},{3,2},{4,0},{5,1},{6,7},{7,6},{8,12},{9,13},{10,... | collective-permute-start | bytes 786440 | tf_op jit(solution)/shard_map/ppermute | solution.py:315
  116.5 14.3 %collective-permute-start.23 = (bf16[2,128,1024]{2,1,0:T(8,128)(2,1)S(1)}, bf16[2,128,1024]{2,1,0:T(8,128)(2,1)S(1)}, u32[]{:S(2)}, u32[]{:S(2)}) collective-permute-start(bf16[2,128,1024]{2,1,0:T(8,128)(2,1)S(1)} %get-tuple-element.189), channel_id=1, source_target_pairs={{0,1},{1,0},{2,6},{3,7},{4,5},{5,4},{6,2},{7,3},{8,9},{9,8},{10,14... | collective-permute-start | bytes 1572872 | tf_op jit(solution)/shard_map/ppermute | solution.py:315
  124.4 7.3 %collective-permute-start.31 = (bf16[128,1024]{1,0:T(8,128)(2,1)S(1)}, bf16[128,1024]{1,0:T(8,128)(2,1)S(1)}, u32[]{:S(2)}, u32[]{:S(2)}) collective-permute-start(bf16[128,1024]{1,0:T(8,128)(2,1)S(1)} %fusion.10), channel_id=1, source_target_pairs={{0,8},{1,9},{2,10},{3,11},{4,12},{5,13},{6,14},{7,15},{8,24},{9,25... | collective-permute-start | bytes 786440 | tf_op jit(solution)/shard_map/ppermute | solution.py:315
  125.9 6.4 %collective-permute-start.30 = (bf16[128,1024]{1,0:T(8,128)(2,1)S(1)}, bf16[128,1024]{1,0:T(8,128)(2,1)S(1)}, u32[]{:S(2)}, u32[]{:S(2)}) collective-permute-start(bf16[128,1024]{1,0:T(8,128)(2,1)S(1)} %fusion.17), channel_id=1, source_target_pairs={{0,4},{1,5},{2,3},{3,2},{4,0},{5,1},{6,7},{7,6},{8,12},{9,13},{10,... | collective-permute-start | bytes 786440 | tf_op jit(solution)/shard_map/ppermute | solution.py:315
  132.5 7.9 %collective-permute-start.33 = (bf16[128,1024]{1,0:T(8,128)(2,1)S(1)}, bf16[128,1024]{1,0:T(8,128)(2,1)S(1)}, u32[]{:S(2)}, u32[]{:S(2)}) collective-permute-start(bf16[128,1024]{1,0:T(8,128)(2,1)S(1)} %fusion.5), channel_id=1, source_target_pairs={{0,8},{1,9},{2,10},{3,11},{4,12},{5,13},{6,14},{7,15},{8,24},{9,25... | collective-permute-start | bytes 786440 | tf_op jit(solution)/shard_map/ppermute | solution.py:315
  133.9 6.4 %collective-permute-start.32 = (bf16[128,1024]{1,0:T(8,128)(2,1)S(1)}, bf16[128,1024]{1,0:T(8,128)(2,1)S(1)}, u32[]{:S(2)}, u32[]{:S(2)}) collective-permute-start(bf16[128,1024]{1,0:T(8,128)(2,1)S(1)} %fusion.14), channel_id=1, source_target_pairs={{0,4},{1,5},{2,3},{3,2},{4,0},{5,1},{6,7},{7,6},{8,12},{9,13},{10,... | collective-permute-start | bytes 786440 | tf_op jit(solution)/shard_map/ppermute | solution.py:315
